TPU v7x, 32 devices: a whole 2x2x4 slice. The times are simulated.
32 devices in a mesh: bpar: 2 (over y), tgt: 4 (over z), prj: 2 (over x), rep: 2 (over core).
Axes of the slice: x: 2, y: 2, z: 4, core: 2. Of those that a mesh axis runs over, the one named last changes fastest.
Arguments:
- tgt_basis: bfloat16 [2, 4096, 512], P(None, 'tgt', 'rep'), may hold values from -6 to 6
- proj_basis: bfloat16 [2, 8, 512, 512], P(None, None, 'prj', 'rep'), may hold values from -0.00390625 to 0.00390625
- quad_weight: float32 [1024], P(('bpar', 'rep')), parts along dimension 0, may hold values from 0.3 to 3
- tgt_energy: float32 [4096], P(('tgt', 'prj', 'rep')), may hold values from -1 to 1
- proj_energy: float32 [8, 512], P(('tgt', 'rep'), 'prj'), may hold values from -1 to 1
- pair_flags: int32 [8, 2], P('bpar'), parts along dimension 0, may hold values 0 or 1
- tile_counts: int32 [8, 2], P('bpar'), parts along dimension 0, may hold values from 1 to 4
- tgt_amp: float32 [8192, 128], P(('bpar', 'tgt', 'prj', 'rep')), parts along dimension 0, may hold values from -6 to 6
- proj_amp: float32 [16, 512, 128], P(('bpar', 'tgt', 'rep'), 'prj'), parts along dimension 0, may hold values from -6 to 6
Outputs:
- new_tgt_amp: float32 [8192, 128], P(('bpar', 'tgt', 'prj', 'rep')), parts along dimension 0
- new_proj_amp: float32 [16, 512, 128], P(('bpar', 'tgt', 'rep'), 'prj'), parts along dimension 0
There are 2 independent parts, one for each index of `bpar`. A program takes and returns all parts, laid end to end along the dimension named above; an argument that names none is the same for every part. Nothing has to cross between parts.
All inputs are finite; a program needn't handle non-finite values.
Results may differ from a plain program's by a relative error of at most 0.02.
Values may be sent and summed in bfloat16 or wider, within the bound.
No kernel may reach another device: no remote copies, remote signals or barrier semaphores. Data moves between devices by JAX's collectives and lax.ppermute only.
A program may use at most 64 MiB of HBM per device.

v0:
```python
import jax
import jax.numpy as jnp
from jax import lax
from jax.sharding import PartitionSpec as P

time_step = 0.4


def rotate(energy, state_now, coupled):
    half_cols = state_now.shape[-1] // 2
    summed = energy[..., None] * state_now + coupled
    return jnp.concatenate([summed[..., half_cols:], -summed[..., :half_cols]], axis=-1)


def turned(amplitude):
    half_cols = amplitude.shape[-1] // 2
    return jnp.concatenate([amplitude[..., half_cols:], -amplitude[..., :half_cols]], axis=-1)


def conj_project(basis_real, basis_imag, amplitude):
    contract = (((0,), (0,)), ((), ()))
    first_part = lax.dot_general(
        basis_real, amplitude, contract, preferred_element_type=jnp.float32
    )
    second = lax.dot_general(
        basis_imag, turned(amplitude), contract, preferred_element_type=jnp.float32
    )
    return first_part + second


def expand(basis_real, basis_imag, projected):
    first_part = jnp.dot(basis_real, projected, preferred_element_type=jnp.float32)
    second = jnp.dot(basis_imag, turned(projected), preferred_element_type=jnp.float32)
    return first_part - second


def shards(
    tgt_basis,
    proj_basis,
    quad_weight,
    tgt_energy,
    proj_energy,
    pair_flags,
    tile_counts,
    tgt_amp,
    proj_amp,
):
    rep_index = lax.axis_index("rep")
    tgt_index = lax.axis_index("tgt")
    prj_index = lax.axis_index("prj")
    pair_flag = pair_flags[tgt_index, prj_index]
    pair_tiles = tile_counts[tgt_index, prj_index]
    tile_width = quad_weight.shape[0] // 2
    lower_tiles = (
        tgt_basis[..., :tile_width],
        proj_basis[..., :tile_width],
        quad_weight[:tile_width],
    )
    upper_tiles = (
        tgt_basis[..., tile_width:],
        proj_basis[..., tile_width:],
        quad_weight[tile_width:],
    )
    first_tiles = list(lower_tiles)
    second_tiles = list(upper_tiles)
    tile_ids = (2 * rep_index, 2 * rep_index + 1)
    slot_list = []
    for tile_id, tile_set in zip(tile_ids, (first_tiles, second_tiles)):
        is_live = jnp.logical_and(pair_flag > 0, tile_id < pair_tiles)
        slot_list.append((is_live, tile_set[0], tile_set[1], tile_set[2]))

    def coupled_rates(tgt_state, proj_state):
        tgt_send = tgt_state.astype(jnp.bfloat16)
        proj_send = proj_state.astype(jnp.bfloat16)
        two_cols = tgt_state.shape[-1]
        group_rows = proj_state.shape[1]
        zero_block = jnp.zeros((tile_width, two_cols), jnp.float32)
        shard_rows = lax.all_gather(tgt_send, ("prj", "rep"), axis=0, tiled=True)
        row_count = shard_rows.shape[0]
        updated = []
        for add_slot_index in range(2):
            is_live, tgt_tile = (slot_list[add_slot_index][0], slot_list[add_slot_index][1])
            basis_real = tgt_tile[0]
            basis_imag = tgt_tile[1]
            term = lax.cond(
                is_live,
                lambda: conj_project(basis_real, basis_imag, shard_rows),
                lambda: zero_block,
            )
            updated.append(term)
        tgt_raw = (updated[0], updated[1])
        target_coefficient = [
            (slot_list[slot_index][3][:, None] * tgt_raw[slot_index]).astype(jnp.bfloat16)
            for slot_index in range(2)
        ]

        def add_projectile(shard_rows):
            row_count = shard_rows.shape[0]
            flat_rows = shard_rows.reshape(row_count * group_rows, two_cols)
            updated = []
            for slot_index in range(2):
                is_live, proj_tile = (slot_list[slot_index][0], slot_list[slot_index][2])
                basis_real = proj_tile[0].reshape(row_count * group_rows, tile_width)
                basis_imag = proj_tile[1].reshape(row_count * group_rows, tile_width)
                term = lax.cond(
                    is_live,
                    lambda: conj_project(basis_real, basis_imag, flat_rows),
                    lambda: zero_block,
                )
                updated.append(term)
            return (updated[0], updated[1])

        proj_raw = add_projectile(lax.all_gather(proj_send, ("tgt", "rep"), axis=0, tiled=True))
        projectile_coefficient = [
            (slot_list[slot_index][3][:, None] * proj_raw[slot_index]).astype(jnp.bfloat16)
            for slot_index in range(2)
        ]
        row_count = proj_state.shape[0] * lax.axis_size(("tgt", "rep"))
        zero_terms = jnp.zeros((row_count, group_rows, two_cols), jnp.float32)
        summed = zero_terms
        for slot_index in range(2):
            is_live, proj_tile = (slot_list[slot_index][0], slot_list[slot_index][2])
            projectile_basis_real = proj_tile[0].reshape(row_count * group_rows, tile_width)
            projectile_basis_imag = proj_tile[1].reshape(row_count * group_rows, tile_width)
            coef_now = target_coefficient[slot_index]
            term = lax.cond(
                is_live,
                lambda: expand(projectile_basis_real, projectile_basis_imag, coef_now).reshape(
                    row_count, group_rows, two_cols
                ),
                lambda: zero_terms,
            )
            summed = summed + term
        proj_coupled = lax.psum_scatter(
            summed.astype(jnp.bfloat16), ("tgt", "rep"), scatter_dimension=0, tiled=True
        ).astype(jnp.float32)
        target_zero_terms = jnp.zeros(
            (tgt_state.shape[0] * lax.axis_size(("prj", "rep")), two_cols), jnp.float32
        )
        summed = target_zero_terms
        for slot_index in range(2):
            is_live, tgt_tile = (slot_list[slot_index][0], slot_list[slot_index][1])
            target_basis_real = tgt_tile[0]
            target_basis_imag = tgt_tile[1]
            target_coef_now = projectile_coefficient[slot_index]
            term = lax.cond(
                is_live,
                lambda: expand(target_basis_real, target_basis_imag, target_coef_now),
                lambda: target_zero_terms,
            )
            summed = summed + term
        tgt_coupled = lax.psum_scatter(
            summed.astype(jnp.bfloat16), ("prj", "rep"), scatter_dimension=0, tiled=True
        ).astype(jnp.float32)
        return (
            rotate(tgt_energy, tgt_state, tgt_coupled),
            rotate(proj_energy, proj_state, proj_coupled),
        )

    tgt_rate, proj_rate = coupled_rates(tgt_amp, proj_amp)
    tgt_half = tgt_amp + 0.5 * time_step * tgt_rate
    proj_half = proj_amp + 0.5 * time_step * proj_rate
    tgt_rate, proj_rate = coupled_rates(tgt_half, proj_half)
    return (tgt_amp + time_step * tgt_rate, proj_amp + time_step * proj_rate)


def solution(mesh):
    in_specs = (
        P(None, "tgt", "rep"),
        P(None, None, "prj", "rep"),
        P(("bpar", "rep")),
        P(("tgt", "prj", "rep")),
        P(("tgt", "rep"), "prj"),
        P("bpar", None),
        P("bpar", None),
        P(("bpar", "tgt", "prj", "rep"), None),
        P(("bpar", "tgt", "rep"), "prj", None),
    )
    out_specs = (P(("bpar", "tgt", "prj", "rep"), None), P(("bpar", "tgt", "rep"), "prj", None))
    return jax.shard_map(shards, mesh=mesh, in_specs=in_specs, out_specs=out_specs, check_vma=False)
```

profile of v0, /device:TPU:0, one launch (start us, length us, event | category | flops | bytes accessed | tf_op | source)
XLA Modules:
  0.0 208.0 jit_solution(11372533353395268817)
XLA Ops:
  11.2 2.1 %slice_bitcast_fusion = (bf16[1024,128]{1,0:T(8,128)(2,1)S(1)}, bf16[1024,128]{1,0:T(8,128)(2,1)}, bf16[1024,128]{1,0:T(8,128)(2,1)S(1)}, bf16[1024,128]{1,0:T(8,128)(2,1)S(1)}) fusion(bf16[2,1024,256]{2,1,0:T(8,128)(2,1)} %param.41), kind=kLoop, calls=%fused_computation.116 | loop fusion | bytes 2097152 | tf_op jit(solution)/shard_map/squeeze | solution.py:144
  14.6 16.6 %all_gather.12 = bf16[8,256,128]{2,1,0:T(8,128)(2,1)S(1)} all-gather(bf16[1,256,128]{2,1,0:T(8,128)(2,1)S(1)} %convert_element_type.81), channel_id=1, replica_groups=mesh['bpar'=2,'tgt'=4,'prj'=2,'rep'=2] {'tgt','rep'}, dimensions={0}, use_global_device_ids=true | all-gather | bytes 589824 | tf_op jit(solution)/shard_map/all_gather | solution.py:113
  31.2 1.7 conditional.16
  32.9 1.5 multiply_convert_fusion.7
  34.4 3.9 %conditional.17 = (f32[1024,128]{1,0:T(8,128)}) conditional(s32[]{:T(128)} %convert_element_type.80, () %tuple.104, (bf16[1024,128]{1,0:T(8,128)(2,1)S(1)}, bf16[128,128]{1,0:T(8,128)(2,1)}, bf16[1024,128]{1,0:T(8,128)(2,1)}) %tuple.107), branch_computations={%region_2.0_spmd, %region_3.0_spmd} | conditional | flops 67313664 | bytes 2228232 | solution.py:146
  36.3 2.0 fusion.5
  39.0 1.6 multiply_convert_fusion.6
  41.4 1.8 add_convert_fusion.3
  43.3 24.4 %reduce-scatter.5.cloned.1.call-done = bf16[256,128]{1,0:T(8,128)(2,1)} async-done(((bf16[1024,128]{1,0:T(8,128)(2,1)}), bf16[256,128]{1,0:T(8,128)(2,1)}) %reduce-scatter.5.cloned.1.call-update) | async-done | bytes 65552 | tf_op jit(solution)/shard_map/reduce_scatter | solution.py:152
  70.1 5.8 %all_gather.13 = bf16[1024,128]{1,0:T(8,128)(2,1)S(1)} all-gather(bf16[256,128]{1,0:T(8,128)(2,1)S(1)} %get-tuple-element.239), channel_id=1, replica_groups=mesh['bpar'=2,'tgt'=4,'prj'=2,'rep'=2] {'prj','rep'}, dimensions={0}, use_global_device_ids=true | all-gather | bytes 327680 | tf_op jit(solution)/shard_map/all_gather | solution.py:78
  75.9 5.9 %all_gather.15 = bf16[1024,128]{1,0:T(8,128)(2,1)S(1)} all-gather(bf16[256,128]{1,0:T(8,128)(2,1)S(1)} %get-tuple-element.238), channel_id=1, replica_groups=mesh['bpar'=2,'tgt'=4,'prj'=2,'rep'=2] {'prj','rep'}, dimensions={0}, use_global_device_ids=true | all-gather | bytes 327680 | tf_op jit(solution)/shard_map/all_gather | solution.py:78
  83.0 1.7 conditional.20
  85.3 2.3 %conditional.28 = (f32[128,128]{1,0:T(8,128)}) conditional(s32[]{:T(128)} %convert_element_type.80, () %tuple.129, (bf16[1024,128]{1,0:T(8,128)(2,1)S(1)}, bf16[1024,128]{1,0:T(8,128)(2,1)S(1)}, bf16[1024,128]{1,0:T(8,128)(2,1)}) %tuple.130), branch_computations={%region_27.0_spmd, %region_28.0_spmd} | conditional | flops 67715072 | bytes 1769480 | solution.py:85
  85.7 1.9 fusion.60
  88.7 1.8 conditional.21
  91.6 2.4 %add_convert_fusion.1 = bf16[8,256,128]{2,1,0:T(8,128)(2,1)} fusion(f32[8,256,128]{2,1,0:T(8,128)} %get-tuple-element.259, f32[8,256,128]{2,1,0:T(8,128)} %get-tuple-element.261), kind=kLoop, calls=%fused_computation.113 | loop fusion | flops 524288 | bytes 2621440 | tf_op jit(solution)/shard_map/convert_element_type | solution.py:135
  94.1 1.8 conditional.29
  96.9 2.4 %add_convert_fusion = bf16[8,256,128]{2,1,0:T(8,128)(2,1)} fusion(f32[8,256,128]{2,1,0:T(8,128)} %get-tuple-element.267, f32[8,256,128]{2,1,0:T(8,128)} %get-tuple-element.269), kind=kLoop, calls=%fused_computation.112 | loop fusion | flops 524288 | bytes 2621440 | tf_op jit(solution)/shard_map/convert_element_type | solution.py:135
  99.4 27.9 %reduce-scatter.7.cloned.1.call-done = bf16[1,256,128]{2,1,0:T(8,128)(2,1)} async-done(((bf16[8,256,128]{2,1,0:T(8,128)(2,1)}), bf16[1,256,128]{2,1,0:T(8,128)(2,1)}) %reduce-scatter.7.cloned.1.call-update) | async-done | bytes 65552 | tf_op jit(solution)/shard_map/reduce_scatter | solution.py:134
  128.4 30.4 %reduce-scatter.11.cloned.1.call-done = bf16[1,256,128]{2,1,0:T(8,128)(2,1)} async-done(((bf16[8,256,128]{2,1,0:T(8,128)(2,1)}), bf16[1,256,128]{2,1,0:T(8,128)(2,1)}) %reduce-scatter.11.cloned.1.call-update) | async-done | bytes 65552 | tf_op jit(solution)/shard_map/reduce_scatter | solution.py:134
  158.7 1.6 convert_add_fusion
  160.4 15.0 %all_gather.14 = bf16[8,256,128]{2,1,0:T(8,128)(2,1)S(1)} all-gather(bf16[1,256,128]{2,1,0:T(8,128)(2,1)S(1)} %get-tuple-element.235), channel_id=1, replica_groups=mesh['bpar'=2,'tgt'=4,'prj'=2,'rep'=2] {'tgt','rep'}, dimensions={0}, use_global_device_ids=true | all-gather | bytes 589824 | tf_op jit(solution)/shard_map/all_gather | solution.py:113
  175.4 1.7 conditional.24
  181.4 18.3 %reduce-scatter.9.cloned.1.call-done = bf16[256,128]{1,0:T(8,128)(2,1)} async-done(((bf16[1024,128]{1,0:T(8,128)(2,1)}), bf16[256,128]{1,0:T(8,128)(2,1)}) %reduce-scatter.9.cloned.1.call-update) | async-done | bytes 65552 | tf_op jit(solution)/shard_map/reduce_scatter | solution.py:152
  (94 shorter events, 35.7 us)
Async XLA Ops:
  7.2 60.6 %reduce-scatter.5.cloned.1.call-start = ((), (), s32[]{:S(2)}) async-start(), calls=%async_computation.4 | async-start | bytes 327680 | tf_op jit(solution)/shard_map/reduce_scatter | solution.py:152
  11.1 2.1 %copy-start.1 = (bf16[2,8,256,256]{3,2,1,0:T(8,128)(2,1)S(1)}, bf16[2,8,256,256]{3,2,1,0:T(8,128)(2,1)}, u32[]{:S(2)}) copy-start(bf16[2,8,256,256]{3,2,1,0:T(8,128)(2,1)} %param.42) | copy-start | bytes 6291460
  13.3 1.3 copy-start.3
  13.3 17.9 %copy-start.13 = (f32[256]{0:T(256)S(1)}, f32[256]{0:T(256)}, u32[]{:S(2)}) copy-start(f32[256]{0:T(256)} %param.43) | copy-start | bytes 3076
  39.0 2.4 %copy-start.2 = (f32[1024,128]{1,0:T(8,128)S(1)}, f32[1024,128]{1,0:T(8,128)}, u32[]{:S(2)}) copy-start(f32[1024,128]{1,0:T(8,128)} %get-tuple-element.255) | copy-start | bytes 1572868
  40.6 27.1 %copy-start.12 = (f32[256]{0:T(256)S(1)}, f32[256]{0:T(256)}, u32[]{:S(2)}) copy-start(f32[256]{0:T(256)} %param.44) | copy-start | bytes 3076
  43.3 84.0 %reduce-scatter.7.cloned.1.call-start = ((), (), s32[]{:S(2)}) async-start(), calls=%async_computation.5 | async-start | bytes 589824 | tf_op jit(solution)/shard_map/reduce_scatter | solution.py:134
  68.9 7.0 %copy-start.6 = (f32[256,64]{1,0:T(8,128)}, f32[256,64]{1,0:T(8,128)S(1)}, u32[]{:S(2)}) copy-start(f32[256,64]{1,0:T(8,128)S(1)} %get-tuple-element.242) | copy-start | bytes 196612
  68.9 7.0 %copy-start.8 = (f32[256,64]{1,0:T(8,128)}, f32[256,64]{1,0:T(8,128)S(1)}, u32[]{:S(2)}) copy-start(f32[256,64]{1,0:T(8,128)S(1)} %get-tuple-element.243) | copy-start | bytes 196612
  84.7 0.6 copy-start.10
  94.0 64.7 %reduce-scatter.11.cloned.1.call-start = ((), (), s32[]{:S(2)}) async-start(), calls=%async_computation.7 | async-start | bytes 589824 | tf_op jit(solution)/shard_map/reduce_scatter | solution.py:134
  96.9 30.4 %copy-start.11 = (f32[1,256]{1,0:T(1,128)S(1)}, f32[1,256]{1,0:T(1,128)}, u32[]{:S(2)}) copy-start(f32[1,256]{1,0:T(1,128)} %param.45) | copy-start | bytes 3076
  99.4 100.2 %reduce-scatter.9.cloned.1.call-start = ((), (), s32[]{:S(2)}) async-start(), calls=%async_computation.6 | async-start | bytes 327680 | tf_op jit(solution)/shard_map/reduce_scatter | solution.py:152
  178.0 1.0 copy-start
  179.6 0.9 copy-start.5
  179.6 20.0 %copy-start.4 = (f32[256,128]{1,0:T(8,128)S(1)}, f32[256,128]{1,0:T(8,128)}, u32[]{:S(2)}) copy-start(f32[256,128]{1,0:T(8,128)} %param.48) | copy-start | bytes 393220
  179.6 20.0 %copy-start.7 = (f32[256,64]{1,0:T(8,128)S(1)}, f32[256,64]{1,0:T(8,128)}, u32[]{:S(2)}) copy-start(f32[256,64]{1,0:T(8,128)} %copy-done.6) | copy-start | bytes 196612
  179.6 20.0 %copy-start.9 = (f32[256,64]{1,0:T(8,128)S(1)}, f32[256,64]{1,0:T(8,128)}, u32[]{:S(2)}) copy-start(f32[256,64]{1,0:T(8,128)} %copy-done.8) | copy-start | bytes 196612
Sparse Core Ops, SparseCore 0:
  43.4 24.2 reduce-scatter.4
  94.1 33.1 reduce-scatter.6
  129.6 29.1 reduce-scatter.10
  180.6 18.9 reduce-scatter.8
where the time goes:
time: 209 us; the launch traced here: 208 us
  waiting for transfers between devices  101 us (48%)
  blocking collectives  43.2 us (21%)
  other arithmetic  22.2 us (11%)
  between operations  16 us (8%)
  matrix products  13.6 us (7%)
  local copies, waits for them, and re-layouts  11.7 us (6%)
    reduce_scatter x2, waiting for transfers between devices, coupled_rates(): lax.psum_scatter(summed.astype(jnp.bfloat16), ('tgt', 'rep'), scatter_dim...  58.3 us
    reduce_scatter x2, waiting for transfers between devices, coupled_rates(): lax.psum_scatter(summed.astype(jnp.bfloat16), ('prj', 'rep'), scatter_dim...  42.7 us
    all_gather x2, blocking collectives, coupled_rates(): lax.all_gather(proj_send, ('tgt', 'rep'), axis=0, tiled=True)  31.6 us
    all_gather x2, blocking collectives, coupled_rates(): shard_rows = lax.all_gather(tgt_send, ('prj', 'rep'), axis=0, tiled=True)  11.6 us
    convert_element_type x4, other arithmetic, coupled_rates(): summed.astype(jnp.bfloat16)  7.47 us
    dot_general x4, matrix products, conj_project(): lax.dot_general(basis_imag, turned(amplitude), contract, preferred_elemen...  5.59 us
    dot_general x4, matrix products, expand(): jnp.dot(basis_imag, turned(projected), preferred_element_type=jnp.float32)  5.08 us
    another operation x8, local copies, waits for them, and re-layouts  4.91 us
  transfers between devices with their start and end apart: 4, of which 4 were waited for; matrix products, arithmetic and copies ran while one was open for 3% of the time, Pallas kernels for 0%

commit v1 on v0

v1 whole, which is shorter than its diff:
```python
import functools

import jax
import jax.numpy as jnp
from jax import lax
from jax.experimental import pallas as pl
from jax.experimental.pallas import tpu as pltpu
from jax.sharding import PartitionSpec as P

time_step = 0.4
half_step = 0.5 * time_step
PEERS = ("tgt", "prj")
HBM = pl.BlockSpec(memory_space=pl.ANY)
VMEM = pl.BlockSpec(memory_space=pltpu.VMEM)
SMEM = pl.BlockSpec(memory_space=pltpu.SMEM)


def turned(block):
    half = block.shape[0] // 2
    return jnp.concatenate([block[half:], -block[:half]], axis=0)


def load_basis(tgt_hbm, proj_hbm, tgt_buf, proj_buf, sems):
    rows = tgt_buf.shape[1]
    groups = proj_buf.shape[1]
    row_start = pl.multiple_of(lax.axis_index("prj") * rows, rows)
    group_start = lax.axis_index("tgt") * groups
    copies = []
    for part in range(2):
        copies.append(
            pltpu.make_async_copy(
                tgt_hbm.at[part, pl.ds(row_start, rows)], tgt_buf.at[part], sems.at[part]
            )
        )
        copies.append(
            pltpu.make_async_copy(
                proj_hbm.at[part, pl.ds(group_start, groups)], proj_buf.at[part], sems.at[2 + part]
            )
        )
    for copy in copies:
        copy.start()
    return copies


def views(tgt_buf, proj_buf):
    rows = tgt_buf.shape[1] // 2

    def tgt_view(part, core):
        return tgt_buf[part, pl.ds(pl.multiple_of(core * rows, rows), rows), :]

    def proj_view(part, core):
        return proj_buf[part, core]

    return tgt_view, proj_view


def project(view, states):
    total = None
    for core, amp in states:
        term = jnp.dot(
            amp.astype(jnp.bfloat16), view(0, core), preferred_element_type=jnp.float32
        ) + jnp.dot(
            turned(amp).astype(jnp.bfloat16), view(1, core), preferred_element_type=jnp.float32
        )
        total = term if total is None else total + term
    return total


def expand(view, core, field, turned_field):
    contract = (((1,), (1,)), ((), ()))
    return lax.dot_general(
        turned_field, view(0, core), contract, preferred_element_type=jnp.float32
    ) + lax.dot_general(field, view(1, core), contract, preferred_element_type=jnp.float32)


def spread(out_ref, kind, block):
    peers, _, cols, _ = out_ref.shape
    for peer in range(peers):
        out_ref[peer, kind] = block[peer * cols : (peer + 1) * cols].astype(jnp.bfloat16)


def collect(in_ref, kind):
    peers, _, cols, _ = in_ref.shape
    block = jnp.concatenate([in_ref[peer, kind].astype(jnp.float32) for peer in range(peers)], axis=0)
    return block.astype(jnp.bfloat16), turned(block).astype(jnp.bfloat16)


def first_kernel(
    tgt_hbm, proj_hbm, weight, tgt_own, tgt_other, proj_own, proj_other, out_ref, tgt_buf, proj_buf, sems
):
    copies = load_basis(tgt_hbm, proj_hbm, tgt_buf, proj_buf, sems)
    core = lax.axis_index("rep")
    tgt_view, proj_view = views(tgt_buf, proj_buf)
    weights = weight[...][None, :]
    tgt_states = [(core, tgt_own[...].T), (1 - core, tgt_other[...].T)]
    proj_states = [(core, proj_own[0].T), (1 - core, proj_other[0].T)]
    for copy in copies:
        copy.wait()
    spread(out_ref, 0, weights * project(tgt_view, tgt_states))
    spread(out_ref, 1, weights * project(proj_view, proj_states))


def mask_kernel(flags, counts, in_ref, out_ref):
    n_tgt, n_prj = flags.shape
    core = lax.axis_index("rep")
    width = in_ref.shape[-1] // 2
    for tile in range(2):
        lanes = pl.ds(tile * width, width)
        tile_id = 2 * core + tile

        def active(a, b):
            live = jnp.logical_and(flags[a, b] > 0, tile_id < counts[a, b])
            return jnp.where(live, 1.0, 0.0).astype(jnp.float32)

        def read(a, b, kind):
            return in_ref[a * n_prj + b, kind, :, lanes].astype(jnp.float32)

        zt = [sum(read(a, b, 0) for b in range(n_prj)) for a in range(n_tgt)]
        zp = [sum(read(a, b, 1) for a in range(n_tgt)) for b in range(n_prj)]
        gates = [[active(a, b) for b in range(n_prj)] for a in range(n_tgt)]
        for a in range(n_tgt):
            field = sum(gates[a][b] * zp[b] for b in range(n_prj)).astype(jnp.bfloat16)
            for b in range(n_prj):
                out_ref[a * n_prj + b, 0, :, lanes] = field
        for b in range(n_prj):
            field = sum(gates[a][b] * zt[a] for a in range(n_tgt)).astype(jnp.bfloat16)
            for a in range(n_tgt):
                out_ref[a * n_prj + b, 1, :, lanes] = field


def half_kernel(
    tgt_hbm, proj_hbm, in_ref, tgt_energy, proj_energy, tgt_own, proj_own, send, keep, tgt_buf, proj_buf, sems
):
    copies = load_basis(tgt_hbm, proj_hbm, tgt_buf, proj_buf, sems)
    core = lax.axis_index("rep")
    amps = (tgt_own[...].T, proj_own[0].T)
    energies = (tgt_energy[...][None, :], proj_energy[...])
    fields = (collect(in_ref, 0), collect(in_ref, 1))
    for copy in copies:
        copy.wait()
    for kind, view in enumerate(views(tgt_buf, proj_buf)):
        field, turned_field = fields[kind]
        amp = amps[kind]
        own = amp + half_step * (
            energies[kind] * turned(amp) + expand(view, core, field, turned_field)
        )
        other = half_step * expand(view, 1 - core, field, turned_field)
        keep[kind, 0] = own
        keep[kind, 1] = other
        send[kind, 0] = own.astype(jnp.bfloat16)
        send[kind, 1] = other.astype(jnp.bfloat16)


def second_kernel(
    tgt_hbm, proj_hbm, weight, keep, received, out_ref, half_ref, tgt_buf, proj_buf, sems
):
    copies = load_basis(tgt_hbm, proj_hbm, tgt_buf, proj_buf, sems)
    core = lax.axis_index("rep")
    weights = weight[...][None, :]
    for copy in copies:
        copy.wait()
    for kind, view in enumerate(views(tgt_buf, proj_buf)):
        own = keep[kind, 0] + received[kind, 1].astype(jnp.float32)
        other = keep[kind, 1] + received[kind, 0].astype(jnp.float32)
        half_ref[kind] = own
        spread(out_ref, kind, weights * project(view, [(core, own), (1 - core, other)]))


def last_kernel(
    tgt_hbm,
    proj_hbm,
    in_ref,
    tgt_energy,
    proj_energy,
    tgt_own,
    proj_own,
    half_ref,
    send,
    tgt_keep,
    proj_keep,
    tgt_buf,
    proj_buf,
    sems,
):
    copies = load_basis(tgt_hbm, proj_hbm, tgt_buf, proj_buf, sems)
    core = lax.axis_index("rep")
    energies = (tgt_energy[...][None, :], proj_energy[...])
    fields = (collect(in_ref, 0), collect(in_ref, 1))
    for copy in copies:
        copy.wait()
    for kind, view in enumerate(views(tgt_buf, proj_buf)):
        field, turned_field = fields[kind]
        change = time_step * (
            energies[kind] * turned(half_ref[kind]) + expand(view, core, field, turned_field)
        )
        if kind == 0:
            tgt_keep[...] = tgt_own[...] + change.T
        else:
            proj_keep[0] = proj_own[0] + change.T
        other = time_step * expand(view, 1 - core, field, turned_field)
        send[kind] = other.T.astype(jnp.bfloat16)


def shards(
    tgt_basis,
    proj_basis,
    quad_weight,
    tgt_energy,
    proj_energy,
    pair_flags,
    tile_counts,
    tgt_amp,
    proj_amp,
):
    peers = lax.axis_size(PEERS)
    points = quad_weight.shape[0]
    rows, two_cols = tgt_amp.shape
    group_rows = proj_amp.shape[1]
    basis_scratch = [
        pltpu.VMEM((2, 2 * rows, points), jnp.bfloat16),
        pltpu.VMEM((2, 2, group_rows, points), jnp.bfloat16),
        pltpu.SemaphoreType.DMA((4,)),
    ]
    pieces = jax.ShapeDtypeStruct((peers, 2, two_cols // peers, points), jnp.bfloat16)

    def other_core(block):
        return lax.ppermute(block, "rep", [(0, 1), (1, 0)])

    def exchange(block):
        return lax.all_to_all(block, PEERS, split_axis=0, concat_axis=0, tiled=True)

    def masked(block):
        return pl.pallas_call(
            mask_kernel, out_shape=pieces, in_specs=[SMEM, SMEM, VMEM], out_specs=VMEM
        )(pair_flags, tile_counts, block)

    first = pl.pallas_call(
        first_kernel,
        out_shape=pieces,
        in_specs=[HBM, HBM] + [VMEM] * 5,
        out_specs=VMEM,
        scratch_shapes=basis_scratch,
    )(tgt_basis, proj_basis, quad_weight, tgt_amp, other_core(tgt_amp), proj_amp, other_core(proj_amp))
    fields = exchange(masked(exchange(first)))

    state = (2, 2, two_cols, rows)
    send, keep = pl.pallas_call(
        half_kernel,
        out_shape=(
            jax.ShapeDtypeStruct(state, jnp.bfloat16),
            jax.ShapeDtypeStruct(state, jnp.float32),
        ),
        in_specs=[HBM, HBM] + [VMEM] * 5,
        out_specs=(VMEM, VMEM),
        scratch_shapes=basis_scratch,
    )(tgt_basis, proj_basis, fields, tgt_energy, proj_energy, tgt_amp, proj_amp)
    second, half = pl.pallas_call(
        second_kernel,
        out_shape=(pieces, jax.ShapeDtypeStruct((2, two_cols, rows), jnp.float32)),
        in_specs=[HBM, HBM] + [VMEM] * 3,
        out_specs=(VMEM, VMEM),
        scratch_shapes=basis_scratch,
    )(tgt_basis, proj_basis, quad_weight, keep, other_core(send))
    fields = exchange(masked(exchange(second)))
    send, tgt_keep, proj_keep = pl.pallas_call(
        last_kernel,
        out_shape=(
            jax.ShapeDtypeStruct((2, rows, two_cols), jnp.bfloat16),
            jax.ShapeDtypeStruct(tgt_amp.shape, jnp.float32),
            jax.ShapeDtypeStruct(proj_amp.shape, jnp.float32),
        ),
        in_specs=[HBM, HBM] + [VMEM] * 6,
        out_specs=(VMEM,) * 3,
        scratch_shapes=basis_scratch,
    )(tgt_basis, proj_basis, fields, tgt_energy, proj_energy, tgt_amp, proj_amp, half)
    received = other_core(send).astype(jnp.float32)
    return tgt_keep + received[0], proj_keep + received[1:]


def solution(mesh):
    in_specs = (
        P(None, "tgt", "rep"),
        P(None, None, "prj", "rep"),
        P(("bpar", "rep")),
        P(("tgt", "prj", "rep")),
        P(("tgt", "rep"), "prj"),
        P("bpar", None),
        P("bpar", None),
        P(("bpar", "tgt", "prj", "rep"), None),
        P(("bpar", "tgt", "rep"), "prj", None),
    )
    out_specs = (P(("bpar", "tgt", "prj", "rep"), None), P(("bpar", "tgt", "rep"), "prj", None))
    return jax.shard_map(shards, mesh=mesh, in_specs=in_specs, out_specs=out_specs, check_vma=False)
```

time: 209 us -> 78.3 us (0.37)
  waiting for transfers between devices: 101 us -> 10.7 us
  other arithmetic: 22.2 us -> 3.17 us
  Pallas kernels: 0 us -> 17.2 us
  between operations: 16 us -> 0.71 us
  matrix products: 13.6 us -> 0 us
  blocking collectives: 43.2 us -> 34.2 us
  local copies, waits for them, and re-layouts: 11.7 us -> 3.67 us
  starting transfers between devices: 0.16 us -> 7.91 us
    reduce_scatter x4 -> x0, waiting for transfers between devices: 101 us -> none  [the longest x2 58.3 us: coupled_rates(): lax.psum_scatter(summed.astype(jnp.bfloat16), ('tgt', 'rep'), scatter_dim...]
    all_gather x4 -> x0, blocking collectives: 43.2 us -> none  [the longest x2 31.6 us: coupled_rates(): lax.all_gather(proj_send, ('tgt', 'rep'), axis=0, tiled=True)]
    all_to_all x0 -> x3, blocking collectives: none -> 34.2 us  [exchange(): return lax.all_to_all(block, PEERS, split_axis=0, concat_axis=0, tiled=True)]
    pallas_call x0 -> x6, Pallas kernels: none -> 17.2 us  [the longest x1 3.69 us: shards(): pl.pallas_call(half_kernel, out_shape=(jax.ShapeDtypeStruct(state, jnp.bf...]
    convert_element_type x11 -> x1, other arithmetic: 13.8 us -> 0.02 us  [shards(): received = other_core(send).astype(jnp.float32)]
    dot_general x16 -> x0, matrix products: 13.6 us -> none  [the longest x4 5.59 us: conj_project(): lax.dot_general(basis_imag, turned(amplitude), contract, preferred_elemen...]
    all_to_all x0 -> x1, starting transfers between devices: none -> 7.17 us  [exchange(): return lax.all_to_all(block, PEERS, split_axis=0, concat_axis=0, tiled=True)]
    all_to_all x0 -> x1, waiting for transfers between devices: none -> 6 us  [exchange(): return lax.all_to_all(block, PEERS, split_axis=0, concat_axis=0, tiled=True)]
  transfers between devices with their start and end apart: 4 -> 5, of which waited for: 4 -> 5; matrix products, arithmetic and copies ran while one was open for 3% -> 2% of each run, Pallas kernels for 0% -> 0%
where the time goes in v1:
time: 78.3 us; the launch traced here: 77.6 us
  blocking collectives  34.2 us (44%)
  Pallas kernels  17.2 us (22%)
  waiting for transfers between devices  10.7 us (14%)
  starting transfers between devices  7.91 us (10%)
  local copies, waits for them, and re-layouts  3.67 us (5%)
  other arithmetic  3.17 us (4%)
    all_to_all x3, blocking collectives, exchange(): return lax.all_to_all(block, PEERS, split_axis=0, concat_axis=0, tiled=True)  34.2 us
    all_to_all x1, starting transfers between devices, exchange(): return lax.all_to_all(block, PEERS, split_axis=0, concat_axis=0, tiled=True)  7.17 us
    all_to_all x1, waiting for transfers between devices, exchange(): return lax.all_to_all(block, PEERS, split_axis=0, concat_axis=0, tiled=True)  6 us
    ppermute x4, waiting for transfers between devices, other_core(): return lax.ppermute(block, 'rep', [(0, 1), (1, 0)])  4.75 us
    pallas_call x1, Pallas kernels, shards(): pl.pallas_call(half_kernel, out_shape=(jax.ShapeDtypeStruct(state, jnp.bf...  3.69 us
    unnamed x14, local copies, waits for them, and re-layouts  3.67 us
    pallas_call x1, Pallas kernels, shards(): pl.pallas_call(last_kernel, out_shape=(jax.ShapeDtypeStruct((2, rows, two...  3.66 us
    pallas_call x1, Pallas kernels, shards(): pl.pallas_call(second_kernel, out_shape=(pieces, jax.ShapeDtypeStruct((2,...  3.31 us
  transfers between devices with their start and end apart: 5, of which 5 were waited for; matrix products, arithmetic and copies ran while one was open for 2% of the time, Pallas kernels for 0%

profile of v1, /device:TPU:0, one launch (start us, length us, event | category | flops | bytes accessed | tf_op | source)
XLA Modules:
  0.0 77.6 jit_solution(2397580836035517450)
XLA Ops:
  0.6 0.5 collective-permute-start
  1.2 1.1 %collective-permute-done.tgt_other = f32[256,128]{1,0:T(8,128)S(1)} collective-permute-done((f32[256,128]{1,0:T(8,128)}, f32[256,128]{1,0:T(8,128)S(1)}, u32[]{:S(2)}, u32[]{:S(2)}) %collective-permute-start) | collective-permute-done | bytes 131104 | tf_op jit(solution)/shard_map/ppermute | solution.py:227
  2.4 0.4 collective-permute-done.1.proj_other
  2.7 0.3 copy-done.2
  3.0 0.7 copy-done.3
  3.7 3.3 %shard_map.104 = bf16[8,2,16,256]{3,2,1,0:T(8,128)(2,1)} custom-call(bf16[2,1024,256]{2,1,0:T(8,128)(2,1)} %tgt_hbm.7, bf16[2,8,256,256]{3,2,1,0:T(8,128)(2,1)} %proj_hbm.7, f32[256]{0:T(256)} %weight.3, f32[256,128]{1,0:T(8,128)} %tgt_own.5, f32[256,128]{1,0:T(8,128)} %copy-done.2, f32[1,256,128]{2,1,0:T(8,128)} %proj_own.5, f32[1,256,128]{2,1,0:T(8,128)} %copy-done.3), custom_call_target="tpu_custom_call" | custom-call | tf_op jit(solution)/shard_map/pallas_call | solution.py:237
  7.0 7.2 %all-to-all-start = ((bf16[8,2,16,256]{3,2,1,0:T(8,128)(2,1)}), bf16[8,2,16,256]{3,2,1,0:T(8,128)(2,1)S(1)}, u32[]{:S(2)}, u32[]{:S(2)}) async-start(bf16[8,2,16,256]{3,2,1,0:T(8,128)(2,1)} %shard_map.104), calls=%async_computation | async-start | bytes 262144 | tf_op jit(solution)/shard_map/all_to_all | solution.py:230
  14.2 0.7 copy.13.flags
  14.8 0.7 copy.14.counts
  15.5 6.0 %all-to-all-done.in_ref = bf16[8,2,16,256]{3,2,1,0:T(8,128)(2,1)S(1)} async-done(((bf16[8,2,16,256]{3,2,1,0:T(8,128)(2,1)}), bf16[8,2,16,256]{3,2,1,0:T(8,128)(2,1)S(1)}, u32[]{:S(2)}, u32[]{:S(2)}) %all-to-all-start) | async-done | bytes 131104 | tf_op jit(solution)/shard_map/all_to_all | solution.py:230
  21.5 0.7 copy-done
  22.2 1.6 %shard_map.105 = bf16[8,2,16,256]{3,2,1,0:T(8,128)(2,1)} custom-call(s32[4,2]{1,0:T(4,128)} %copy.13.flags, s32[4,2]{1,0:T(4,128)} %copy.14.counts, bf16[8,2,16,256]{3,2,1,0:T(8,128)(2,1)} %copy-done), custom_call_target="tpu_custom_call" | custom-call | tf_op jit(solution)/shard_map/pallas_call | solution.py:233
  23.8 11.3 %all_to_all.20.in_ref = bf16[8,2,16,256]{3,2,1,0:T(8,128)(2,1)} all-to-all(bf16[8,2,16,256]{3,2,1,0:T(8,128)(2,1)} %shard_map.105), channel_id=1, replica_groups=mesh['bpar'=2,'tgt'=4,'prj'=2,'rep'=2] {'tgt','prj'}, dimensions={0} | all-to-all | bytes 262144 | tf_op jit(solution)/shard_map/all_to_all | solution.py:230
  35.1 3.7 %shard_map.106 = (bf16[2,2,128,256]{3,2,1,0:T(8,128)(2,1)}, f32[2,2,128,256]{3,2,1,0:T(8,128)}) custom-call(bf16[2,1024,256]{2,1,0:T(8,128)(2,1)} %tgt_hbm.7, bf16[2,8,256,256]{3,2,1,0:T(8,128)(2,1)} %proj_hbm.7, bf16[8,2,16,256]{3,2,1,0:T(8,128)(2,1)} %all_to_all.20.in_ref, f32[256]{0:T(256)} %tgt_energy.3, f32[1,256]{1,0:T(1,128)} %proj_energy.3, ...), custom_call_target="tpu_custom_call" | custom-call | tf_op jit(solution)/shard_map/pallas_call | solution.py:247
  38.9 1.7 %collective-permute-done.2.received = bf16[2,2,128,256]{3,2,1,0:T(8,128)(2,1)S(1)} collective-permute-done((bf16[2,2,128,256]{3,2,1,0:T(8,128)(2,1)}, bf16[2,2,128,256]{3,2,1,0:T(8,128)(2,1)S(1)}, u32[]{:S(2)}, u32[]{:S(2)}) %collective-permute-start.2) | collective-permute-done | bytes 262176 | tf_op jit(solution)/shard_map/ppermute | solution.py:227
  40.6 0.7 copy-done.1
  41.3 3.3 %shard_map.107 = (bf16[8,2,16,256]{3,2,1,0:T(8,128)(2,1)}, f32[2,128,256]{2,1,0:T(8,128)}) custom-call(bf16[2,1024,256]{2,1,0:T(8,128)(2,1)} %tgt_hbm.7, bf16[2,8,256,256]{3,2,1,0:T(8,128)(2,1)} %proj_hbm.7, f32[256]{0:T(256)} %weight.3, f32[2,2,128,256]{3,2,1,0:T(8,128)} %get-tuple-element.9.keep, bf16[2,2,128,256]{3,2,1,0:T(8,128)(2,1)} %copy-done.1), custom_call_target="tpu_custom_call" | custom-call | tf_op jit(solution)/shard_map/pallas_call | solution.py:257
  44.6 11.6 %all_to_all.21.in_ref = bf16[8,2,16,256]{3,2,1,0:T(8,128)(2,1)} all-to-all(bf16[8,2,16,256]{3,2,1,0:T(8,128)(2,1)} %get-tuple-element.11), channel_id=1, replica_groups=mesh['bpar'=2,'tgt'=4,'prj'=2,'rep'=2] {'tgt','prj'}, dimensions={0} | all-to-all | bytes 262144 | tf_op jit(solution)/shard_map/all_to_all | solution.py:230
  56.2 1.6 %shard_map.108 = bf16[8,2,16,256]{3,2,1,0:T(8,128)(2,1)} custom-call(s32[4,2]{1,0:T(4,128)} %copy.13.flags, s32[4,2]{1,0:T(4,128)} %copy.14.counts, bf16[8,2,16,256]{3,2,1,0:T(8,128)(2,1)} %all_to_all.21.in_ref), custom_call_target="tpu_custom_call" | custom-call | tf_op jit(solution)/shard_map/pallas_call | solution.py:233
  57.8 11.3 %all_to_all.22.in_ref = bf16[8,2,16,256]{3,2,1,0:T(8,128)(2,1)} all-to-all(bf16[8,2,16,256]{3,2,1,0:T(8,128)(2,1)} %shard_map.108), channel_id=1, replica_groups=mesh['bpar'=2,'tgt'=4,'prj'=2,'rep'=2] {'tgt','prj'}, dimensions={0} | all-to-all | bytes 262144 | tf_op jit(solution)/shard_map/all_to_all | solution.py:230
  69.1 3.7 %shard_map.109 = (bf16[2,256,128]{2,1,0:T(8,128)(2,1)}, f32[256,128]{1,0:T(8,128)}, f32[1,256,128]{2,1,0:T(8,128)}) custom-call(bf16[2,1024,256]{2,1,0:T(8,128)(2,1)} %tgt_hbm.7, bf16[2,8,256,256]{3,2,1,0:T(8,128)(2,1)} %proj_hbm.7, bf16[8,2,16,256]{3,2,1,0:T(8,128)(2,1)} %all_to_all.22.in_ref, f32[256]{0:T(256)} %tgt_energy.3, f32[1,256]{1,0:T(1,128)} %proj_energy.3, ...), custom_call_target="tpu_custom_call" | custom-call | tf_op jit(solution)/shard_map/pallas_call | solution.py:265
  72.9 1.5 %collective-permute-done.3 = bf16[2,256,128]{2,1,0:T(8,128)(2,1)S(1)} collective-permute-done((bf16[2,256,128]{2,1,0:T(8,128)(2,1)}, bf16[2,256,128]{2,1,0:T(8,128)(2,1)S(1)}, u32[]{:S(2)}, u32[]{:S(2)}) %collective-permute-start.3) | collective-permute-done | bytes 131104 | tf_op jit(solution)/shard_map/ppermute | solution.py:227
  74.4 1.6 %slice_add_fusion = f32[1,256,128]{2,1,0:T(8,128)} fusion(f32[1,256,128]{2,1,0:T(8,128)} %get-tuple-element.15, f32[2,256,128]{2,1,0:T(8,128)S(1)} %convert_element_type.3), kind=kLoop, calls=%fused_computation | loop fusion | flops 32768 | bytes 393216 | tf_op jit(solution)/shard_map/add | solution.py:277
  76.0 1.6 %fusion = f32[256,128]{1,0:T(8,128)} fusion(f32[256,128]{1,0:T(8,128)} %get-tuple-element.13, f32[2,256,128]{2,1,0:T(8,128)S(1)} %convert_element_type.3), kind=kLoop, calls=%fused_computation.2 | loop fusion | flops 32768 | bytes 393216 | tf_op jit(solution)/shard_map/add | solution.py:277
  (12 shorter events, 0.3 us)
Async XLA Ops:
  0.6 13.5 %copy-start.4 = (s32[4,2]{0,1:T(2,128)S(1)}, s32[4,2]{0,1:T(2,128)}, u32[]{:S(2)}) copy-start(s32[4,2]{0,1:T(2,128)} %param.14) | copy-start | bytes 100
  0.6 14.2 %copy-start.5 = (s32[4,2]{0,1:T(2,128)S(1)}, s32[4,2]{0,1:T(2,128)}, u32[]{:S(2)}) copy-start(s32[4,2]{0,1:T(2,128)} %param.15) | copy-start | bytes 100
  0.6 1.7 %collective-permute-start = (f32[256,128]{1,0:T(8,128)}, f32[256,128]{1,0:T(8,128)S(1)}, u32[]{:S(2)}, u32[]{:S(2)}) collective-permute-start(f32[256,128]{1,0:T(8,128)} %tgt_own.5), channel_id=1, source_target_pairs={{0,1},{1,0},{2,3},{3,2},{4,5},{5,4},{6,7},{7,6},{8,9},{9,8},{10,11... | collective-permute-start | bytes 393224 | tf_op jit(solution)/shard_map/ppermute | solution.py:227
  1.2 1.6 %collective-permute-start.1 = (f32[1,256,128]{2,1,0:T(8,128)}, f32[1,256,128]{2,1,0:T(8,128)S(1)}, u32[]{:S(2)}, u32[]{:S(2)}) collective-permute-start(f32[1,256,128]{2,1,0:T(8,128)} %proj_own.5), channel_id=1, source_target_pairs={{0,1},{1,0},{2,3},{3,2},{4,5},{5,4},{6,7},{7,6},{8,9},{9,8},{10,11... | collective-permute-start | bytes 393224 | tf_op jit(solution)/shard_map/ppermute | solution.py:227
  2.4 0.7 copy-start.2
  3.0 0.7 copy-start.3
  7.0 14.5 %all-to-all-start = ((bf16[8,2,16,256]{3,2,1,0:T(8,128)(2,1)}), bf16[8,2,16,256]{3,2,1,0:T(8,128)(2,1)S(1)}, u32[]{:S(2)}, u32[]{:S(2)}) async-start(bf16[8,2,16,256]{3,2,1,0:T(8,128)(2,1)} %shard_map.104), calls=%async_computation | async-start | bytes 262144 | tf_op jit(solution)/shard_map/all_to_all | solution.py:230
  21.5 0.7 copy-start
  38.8 1.8 %collective-permute-start.2 = (bf16[2,2,128,256]{3,2,1,0:T(8,128)(2,1)}, bf16[2,2,128,256]{3,2,1,0:T(8,128)(2,1)S(1)}, u32[]{:S(2)}, u32[]{:S(2)}) collective-permute-start(bf16[2,2,128,256]{3,2,1,0:T(8,128)(2,1)} %get-tuple-element.10), channel_id=1, source_target_pairs={{0,1},{1,0},{2,3},{3,2},{4,5},{5,4},{6,7},{7,6},{8,9},{9,8},{10,11... | collective-permute-start | bytes 786440 | tf_op jit(solution)/shard_map/ppermute | solution.py:227
  40.6 0.7 copy-start.1
  72.8 1.6 %collective-permute-start.3 = (bf16[2,256,128]{2,1,0:T(8,128)(2,1)}, bf16[2,256,128]{2,1,0:T(8,128)(2,1)S(1)}, u32[]{:S(2)}, u32[]{:S(2)}) collective-permute-start(bf16[2,256,128]{2,1,0:T(8,128)(2,1)} %get-tuple-element.14), channel_id=1, source_target_pairs={{0,1},{1,0},{2,3},{3,2},{4,5},{5,4},{6,7},{7,6},{8,9},{9,8},{10,11... | collective-permute-start | bytes 393224 | tf_op jit(solution)/shard_map/ppermute | solution.py:227

commit v2 on v1

--- a/solution.py
+++ b/solution.py
@@ -10,6 +10,7 @@
 time_step = 0.4
 half_step = 0.5 * time_step
 PEERS = ("tgt", "prj")
+VMEM_LIMIT = 8 * 1024 * 1024
 HBM = pl.BlockSpec(memory_space=pl.ANY)
 VMEM = pl.BlockSpec(memory_space=pltpu.VMEM)
 SMEM = pl.BlockSpec(memory_space=pltpu.SMEM)
@@ -73,20 +74,28 @@
     ) + lax.dot_general(field, view(1, core), contract, preferred_element_type=jnp.float32)
 
 
-def spread(out_ref, kind, block):
-    peers, _, cols, _ = out_ref.shape
-    for peer in range(peers):
-        out_ref[peer, kind] = block[peer * cols : (peer + 1) * cols].astype(jnp.bfloat16)
-
-
-def collect(in_ref, kind):
-    peers, _, cols, _ = in_ref.shape
-    block = jnp.concatenate([in_ref[peer, kind].astype(jnp.float32) for peer in range(peers)], axis=0)
+def peer_rows(piece, cols):
+    me = lax.axis_index("tgt") * lax.axis_size("prj") + lax.axis_index("prj")
+    return pl.ds(pl.multiple_of(jnp.bitwise_xor(me, piece) * cols, cols), cols)
+
+
+def spread(out_refs, kind, block, rows_buf):
+    rows_buf[kind] = block
+    for piece, out_ref in enumerate(out_refs):
+        rows = peer_rows(piece, out_ref.shape[1])
+        out_ref[kind] = rows_buf[kind, rows, :].astype(jnp.bfloat16)
+
+
+def collect(in_refs, kind, rows_buf):
+    for piece, in_ref in enumerate(in_refs):
+        rows = peer_rows(piece, in_ref.shape[1])
+        rows_buf[kind, rows, :] = in_ref[kind].astype(jnp.float32)
+    block = rows_buf[kind]
     return block.astype(jnp.bfloat16), turned(block).astype(jnp.bfloat16)
 
 
 def first_kernel(
-    tgt_hbm, proj_hbm, weight, tgt_own, tgt_other, proj_own, proj_other, out_ref, tgt_buf, proj_buf, sems
+    tgt_hbm, proj_hbm, weight, tgt_own, tgt_other, proj_own, proj_other, out_refs, tgt_buf, proj_buf, sems, rows_buf
 ):
     copies = load_basis(tgt_hbm, proj_hbm, tgt_buf, proj_buf, sems)
     core = lax.axis_index("rep")
@@ -96,24 +105,28 @@
     proj_states = [(core, proj_own[0].T), (1 - core, proj_other[0].T)]
     for copy in copies:
         copy.wait()
-    spread(out_ref, 0, weights * project(tgt_view, tgt_states))
-    spread(out_ref, 1, weights * project(proj_view, proj_states))
-
-
-def mask_kernel(flags, counts, in_ref, out_ref):
+    spread(out_refs, 0, weights * project(tgt_view, tgt_states), rows_buf)
+    spread(out_refs, 1, weights * project(proj_view, proj_states), rows_buf)
+
+
+def mask_kernel(flags, counts, in_refs, out_refs):
     n_tgt, n_prj = flags.shape
     core = lax.axis_index("rep")
-    width = in_ref.shape[-1] // 2
+    tgt_index = lax.axis_index("tgt")
+    prj_index = lax.axis_index("prj")
+    width = in_refs[0].shape[-1] // 2
     for tile in range(2):
         lanes = pl.ds(tile * width, width)
         tile_id = 2 * core + tile
 
         def active(a, b):
+            a = jnp.bitwise_xor(tgt_index, a)
+            b = jnp.bitwise_xor(prj_index, b)
             live = jnp.logical_and(flags[a, b] > 0, tile_id < counts[a, b])
             return jnp.where(live, 1.0, 0.0).astype(jnp.float32)
 
         def read(a, b, kind):
-            return in_ref[a * n_prj + b, kind, :, lanes].astype(jnp.float32)
+            return in_refs[a * n_prj + b][kind, :, lanes].astype(jnp.float32)
 
         zt = [sum(read(a, b, 0) for b in range(n_prj)) for a in range(n_tgt)]
         zp = [sum(read(a, b, 1) for a in range(n_tgt)) for b in range(n_prj)]
@@ -121,21 +134,21 @@
         for a in range(n_tgt):
             field = sum(gates[a][b] * zp[b] for b in range(n_prj)).astype(jnp.bfloat16)
             for b in range(n_prj):
-                out_ref[a * n_prj + b, 0, :, lanes] = field
+                out_refs[a * n_prj + b][0, :, lanes] = field
         for b in range(n_prj):
             field = sum(gates[a][b] * zt[a] for a in range(n_tgt)).astype(jnp.bfloat16)
             for a in range(n_tgt):
-                out_ref[a * n_prj + b, 1, :, lanes] = field
+                out_refs[a * n_prj + b][1, :, lanes] = field
 
 
 def half_kernel(
-    tgt_hbm, proj_hbm, in_ref, tgt_energy, proj_energy, tgt_own, proj_own, send, keep, tgt_buf, proj_buf, sems
+    tgt_hbm, proj_hbm, in_refs, tgt_energy, proj_energy, tgt_own, proj_own, send, keep, tgt_buf, proj_buf, sems, rows_buf
 ):
     copies = load_basis(tgt_hbm, proj_hbm, tgt_buf, proj_buf, sems)
     core = lax.axis_index("rep")
     amps = (tgt_own[...].T, proj_own[0].T)
     energies = (tgt_energy[...][None, :], proj_energy[...])
-    fields = (collect(in_ref, 0), collect(in_ref, 1))
+    fields = (collect(in_refs, 0, rows_buf), collect(in_refs, 1, rows_buf))
     for copy in copies:
         copy.wait()
     for kind, view in enumerate(views(tgt_buf, proj_buf)):
@@ -152,7 +165,7 @@
 
 
 def second_kernel(
-    tgt_hbm, proj_hbm, weight, keep, received, out_ref, half_ref, tgt_buf, proj_buf, sems
+    tgt_hbm, proj_hbm, weight, keep, received, out_refs, half_ref, tgt_buf, proj_buf, sems, rows_buf
 ):
     copies = load_basis(tgt_hbm, proj_hbm, tgt_buf, proj_buf, sems)
     core = lax.axis_index("rep")
@@ -163,13 +176,13 @@
         own = keep[kind, 0] + received[kind, 1].astype(jnp.float32)
         other = keep[kind, 1] + received[kind, 0].astype(jnp.float32)
         half_ref[kind] = own
-        spread(out_ref, kind, weights * project(view, [(core, own), (1 - core, other)]))
+        spread(out_refs, kind, weights * project(view, [(core, own), (1 - core, other)]), rows_buf)
 
 
 def last_kernel(
     tgt_hbm,
     proj_hbm,
-    in_ref,
+    in_refs,
     tgt_energy,
     proj_energy,
     tgt_own,
@@ -181,11 +194,12 @@
     tgt_buf,
     proj_buf,
     sems,
+    rows_buf,
 ):
     copies = load_basis(tgt_hbm, proj_hbm, tgt_buf, proj_buf, sems)
     core = lax.axis_index("rep")
     energies = (tgt_energy[...][None, :], proj_energy[...])
-    fields = (collect(in_ref, 0), collect(in_ref, 1))
+    fields = (collect(in_refs, 0, rows_buf), collect(in_refs, 1, rows_buf))
     for copy in copies:
         copy.wait()
     for kind, view in enumerate(views(tgt_buf, proj_buf)):
@@ -216,62 +230,80 @@
     points = quad_weight.shape[0]
     rows, two_cols = tgt_amp.shape
     group_rows = proj_amp.shape[1]
-    basis_scratch = [
+    cols = two_cols // peers
+    scratch = [
         pltpu.VMEM((2, 2 * rows, points), jnp.bfloat16),
         pltpu.VMEM((2, 2, group_rows, points), jnp.bfloat16),
         pltpu.SemaphoreType.DMA((4,)),
+        pltpu.VMEM((2, two_cols, points), jnp.float32),
     ]
-    pieces = jax.ShapeDtypeStruct((peers, 2, two_cols // peers, points), jnp.bfloat16)
+    pieces = [jax.ShapeDtypeStruct((2, cols, points), jnp.bfloat16)] * peers
+    pieces_spec = [VMEM] * peers
+
+    def call(kernel, out_shape, in_specs, out_specs, scratch_shapes=()):
+        specs = in_specs + list(out_specs) + [None] * len(scratch_shapes)
+
+        def with_lists(*refs):
+            refs = jax.tree.leaves(refs)
+            args = [
+                [refs.pop(0) for _ in spec] if isinstance(spec, list) else refs.pop(0) for spec in specs
+            ]
+            kernel(*args)
+
+        return pl.pallas_call(
+            with_lists,
+            out_shape=out_shape,
+            in_specs=in_specs,
+            out_specs=out_specs,
+            scratch_shapes=scratch_shapes,
+            compiler_params=pltpu.CompilerParams(vmem_limit_bytes=VMEM_LIMIT),
+        )
 
     def other_core(block):
         return lax.ppermute(block, "rep", [(0, 1), (1, 0)])
 
-    def exchange(block):
-        return lax.all_to_all(block, PEERS, split_axis=0, concat_axis=0, tiled=True)
-
-    def masked(block):
-        return pl.pallas_call(
-            mask_kernel, out_shape=pieces, in_specs=[SMEM, SMEM, VMEM], out_specs=VMEM
-        )(pair_flags, tile_counts, block)
-
-    first = pl.pallas_call(
-        first_kernel,
-        out_shape=pieces,
-        in_specs=[HBM, HBM] + [VMEM] * 5,
-        out_specs=VMEM,
-        scratch_shapes=basis_scratch,
-    )(tgt_basis, proj_basis, quad_weight, tgt_amp, other_core(tgt_amp), proj_amp, other_core(proj_amp))
+    def exchange(blocks):
+        return [
+            block if piece == 0 else lax.ppermute(block, PEERS, [(me, me ^ piece) for me in range(peers)])
+            for piece, block in enumerate(blocks)
+        ]
+
+    def masked(blocks):
+        return call(mask_kernel, [pieces], [SMEM, SMEM, pieces_spec], [pieces_spec])(
+            pair_flags, tile_counts, blocks
+        )[0]
+
+    (first,) = call(first_kernel, [pieces], [HBM, HBM] + [VMEM] * 5, [pieces_spec], scratch)(
+        tgt_basis, proj_basis, quad_weight, tgt_amp, other_core(tgt_amp), proj_amp, other_core(proj_amp)
+    )
     fields = exchange(masked(exchange(first)))
 
     state = (2, 2, two_cols, rows)
-    send, keep = pl.pallas_call(
+    send, keep = call(
         half_kernel,
-        out_shape=(
-            jax.ShapeDtypeStruct(state, jnp.bfloat16),
-            jax.ShapeDtypeStruct(state, jnp.float32),
-        ),
-        in_specs=[HBM, HBM] + [VMEM] * 5,
-        out_specs=(VMEM, VMEM),
-        scratch_shapes=basis_scratch,
+        (jax.ShapeDtypeStruct(state, jnp.bfloat16), jax.ShapeDtypeStruct(state, jnp.float32)),
+        [HBM, HBM, pieces_spec] + [VMEM] * 4,
+        (VMEM, VMEM),
+        scratch,
     )(tgt_basis, proj_basis, fields, tgt_energy, proj_energy, tgt_amp, proj_amp)
-    second, half = pl.pallas_call(
+    second, half = call(
         second_kernel,
-        out_shape=(pieces, jax.ShapeDtypeStruct((2, two_cols, rows), jnp.float32)),
-        in_specs=[HBM, HBM] + [VMEM] * 3,
-        out_specs=(VMEM, VMEM),
-        scratch_shapes=basis_scratch,
+        (pieces, jax.ShapeDtypeStruct((2, two_cols, rows), jnp.float32)),
+        [HBM, HBM] + [VMEM] * 3,
+        (pieces_spec, VMEM),
+        scratch,
     )(tgt_basis, proj_basis, quad_weight, keep, other_core(send))
     fields = exchange(masked(exchange(second)))
-    send, tgt_keep, proj_keep = pl.pallas_call(
+    send, tgt_keep, proj_keep = call(
         last_kernel,
-        out_shape=(
+        (
             jax.ShapeDtypeStruct((2, rows, two_cols), jnp.bfloat16),
             jax.ShapeDtypeStruct(tgt_amp.shape, jnp.float32),
             jax.ShapeDtypeStruct(proj_amp.shape, jnp.float32),
         ),
-        in_specs=[HBM, HBM] + [VMEM] * 6,
-        out_specs=(VMEM,) * 3,
-        scratch_shapes=basis_scratch,
+        [HBM, HBM, pieces_spec] + [VMEM] * 5,
+        (VMEM,) * 3,
+        scratch,
     )(tgt_basis, proj_basis, fields, tgt_energy, proj_energy, tgt_amp, proj_amp, half)
     received = other_core(send).astype(jnp.float32)
     return tgt_keep + received[0], proj_keep + received[1:]

time: 78.3 us -> 80.6 us (1.029)
  starting transfers between devices: 7.91 us -> 46.6 us
  blocking collectives: 34.2 us -> 0 us
  Pallas kernels: 17.2 us -> 4.55 us
  waiting for transfers between devices: 10.7 us -> 20.1 us
  local copies, waits for them, and re-layouts: 3.67 us -> 6.86 us
  other arithmetic: 3.17 us -> 1.36 us
    ppermute x0 -> x28, starting transfers between devices: none -> 45.8 us  [exchange(): lax.ppermute(block, PEERS, [(me, me ^ piece) for me in range(peers)])]
    all_to_all x3 -> x0, blocking collectives: 34.2 us -> none  [exchange(): return lax.all_to_all(block, PEERS, split_axis=0, concat_axis=0, tiled=True)]
    ppermute x0 -> x28, waiting for transfers between devices: none -> 15.8 us  [exchange(): lax.ppermute(block, PEERS, [(me, me ^ piece) for me in range(peers)])]
    pallas_call x6, Pallas kernels: 17.2 us -> 4.55 us  [the longest x2 1.32 us: masked(): call(mask_kernel, [pieces], [SMEM, SMEM, pieces_spec], [pieces_spec])]
    all_to_all x1 -> x0, starting transfers between devices: 7.17 us -> none  [exchange(): return lax.all_to_all(block, PEERS, split_axis=0, concat_axis=0, tiled=True)]
    all_to_all x1 -> x0, waiting for transfers between devices: 6 us -> none  [exchange(): return lax.all_to_all(block, PEERS, split_axis=0, concat_axis=0, tiled=True)]
    unnamed x14 -> x28, local copies, waits for them, and re-layouts: 3.67 us -> 6.86 us
    add x2, other arithmetic: 3.15 us -> 1.34 us  [shards(): return (tgt_keep + received[0], proj_keep + received[1:])]
  transfers between devices with their start and end apart: 5 -> 32, of which waited for: 5 -> 13; matrix products, arithmetic and copies ran while one was open for 2% -> 1% of each run, Pallas kernels for 0% -> 0%
where the time goes in v2:
time: 80.6 us; the launch traced here: 80.3 us
  starting transfers between devices  46.6 us (58%)
  waiting for transfers between devices  20.1 us (25%)
  local copies, waits for them, and re-layouts  6.86 us (9%)
  Pallas kernels  4.55 us (6%)
  other arithmetic  1.36 us (2%)
    ppermute x28, starting transfers between devices, exchange(): lax.ppermute(block, PEERS, [(me, me ^ piece) for me in range(peers)])  45.8 us
    ppermute x28, waiting for transfers between devices, exchange(): lax.ppermute(block, PEERS, [(me, me ^ piece) for me in range(peers)])  15.8 us
    unnamed x28, local copies, waits for them, and re-layouts  6.86 us
    ppermute x4, waiting for transfers between devices, other_core(): return lax.ppermute(block, 'rep', [(0, 1), (1, 0)])  4.34 us
  transfers between devices with their start and end apart: 32, of which 13 were waited for; matrix products, arithmetic and copies ran while one was open for 1% of the time, Pallas kernels for 0%

profile of v2, /device:TPU:0, one launch (start us, length us, event | category | flops | bytes accessed | tf_op | source)
XLA Modules:
  0.0 80.3 jit_solution(17441048088159478225)
XLA Ops:
  2.7 1.6 %copy-done = bf16[2,8,256,256]{3,2,1,0:T(8,128)(2,1)S(1)} copy-done((bf16[2,8,256,256]{3,2,1,0:T(8,128)(2,1)S(1)}, bf16[2,8,256,256]{3,2,1,0:T(8,128)(2,1)}, u32[]{:S(2)}) %copy-start) | copy-done | bytes 2097176
  8.1 1.3 %shard_map.104 = (bf16[2,16,256]{2,1,0:T(8,128)(2,1)S(1)}, bf16[2,16,256]{2,1,0:T(8,128)(2,1)S(1)}, bf16[2,16,256]{2,1,0:T(8,128)(2,1)S(1)}, bf16[2,16,256]{2,1,...) custom-call(bf16[2,1024,256]{2,1,0:T(8,128)(2,1)S(1)} %copy-done.2, ...), custom_call_target="tpu_custom_call" | custom-call | tf_op jit(solution)/shard_map/pallas_call | solution.py:276
  9.4 2.7 %collective-permute-start.2 = (bf16[2,16,256]{2,1,0:T(8,128)(2,1)S(1)}, bf16[2,16,256]{2,1,0:T(8,128)(2,1)S(1)}, u32[]{:S(2)}, u32[]{:S(2)}) collective-permute-start(bf16[2,16,256]{2,1,0:T(8,128)(2,1)S(1)} %get-tuple-element.41), channel_id=1, source_target_pairs={{0,2},{2,0},{4,6},{6,4},{8,10},{10,8},{12,14},{14,12},{1,3},{3,1},... | collective-permute-start | bytes 49160 | tf_op jit(solution)/shard_map/ppermute | solution.py:267
  12.1 1.6 %collective-permute-start.3 = (bf16[2,16,256]{2,1,0:T(8,128)(2,1)S(1)}, bf16[2,16,256]{2,1,0:T(8,128)(2,1)S(1)}, u32[]{:S(2)}, u32[]{:S(2)}) collective-permute-start(bf16[2,16,256]{2,1,0:T(8,128)(2,1)S(1)} %get-tuple-element.42), channel_id=1, source_target_pairs={{0,4},{2,6},{4,0},{6,2},{8,12},{10,14},{12,8},{14,10},{1,5},{3,7},... | collective-permute-start | bytes 49160 | tf_op jit(solution)/shard_map/ppermute | solution.py:267
  13.7 3.0 %collective-permute-start.5 = (bf16[2,16,256]{2,1,0:T(8,128)(2,1)}, bf16[2,16,256]{2,1,0:T(8,128)(2,1)S(1)}, u32[]{:S(2)}, u32[]{:S(2)}) collective-permute-start(bf16[2,16,256]{2,1,0:T(8,128)(2,1)} %get-tuple-element.44), channel_id=1, source_target_pairs={{0,8},{2,10},{4,12},{6,14},{8,0},{10,2},{12,4},{14,6},{1,9},{3,11}... | collective-permute-start | bytes 49160 | tf_op jit(solution)/shard_map/ppermute | solution.py:267
  16.7 1.3 %collective-permute-start.6 = (bf16[2,16,256]{2,1,0:T(8,128)(2,1)}, bf16[2,16,256]{2,1,0:T(8,128)(2,1)S(1)}, u32[]{:S(2)}, u32[]{:S(2)}) collective-permute-start(bf16[2,16,256]{2,1,0:T(8,128)(2,1)} %get-tuple-element.45), channel_id=1, source_target_pairs={{0,10},{2,8},{4,14},{6,12},{8,2},{10,0},{12,6},{14,4},{1,11},{3,9}... | collective-permute-start | bytes 49160 | tf_op jit(solution)/shard_map/ppermute | solution.py:267
  17.9 3.6 %collective-permute-start.7 = (bf16[2,16,256]{2,1,0:T(8,128)(2,1)}, bf16[2,16,256]{2,1,0:T(8,128)(2,1)S(1)}, u32[]{:S(2)}, u32[]{:S(2)}) collective-permute-start(bf16[2,16,256]{2,1,0:T(8,128)(2,1)} %get-tuple-element.46), channel_id=1, source_target_pairs={{0,12},{2,14},{4,8},{6,10},{8,4},{10,6},{12,0},{14,2},{1,13},{3,15... | collective-permute-start | bytes 49160 | tf_op jit(solution)/shard_map/ppermute | solution.py:267
  22.5 1.2 %collective-permute-done.7.refs_2__6_ = bf16[2,16,256]{2,1,0:T(8,128)(2,1)S(1)} collective-permute-done((bf16[2,16,256]{2,1,0:T(8,128)(2,1)}, bf16[2,16,256]{2,1,0:T(8,128)(2,1)S(1)}, u32[]{:S(2)}, u32[]{:S(2)}) %collective-permute-start.7) | collective-permute-done | bytes 16416 | tf_op jit(solution)/shard_map/ppermute | solution.py:267
  23.7 4.5 %collective-permute-done.8.refs_2__7_ = bf16[2,16,256]{2,1,0:T(8,128)(2,1)S(1)} collective-permute-done((bf16[2,16,256]{2,1,0:T(8,128)(2,1)}, bf16[2,16,256]{2,1,0:T(8,128)(2,1)S(1)}, u32[]{:S(2)}, u32[]{:S(2)}) %collective-permute-start.8) | collective-permute-done | bytes 16416 | tf_op jit(solution)/shard_map/ppermute | solution.py:267
  29.5 3.0 %collective-permute-start.11 = (bf16[2,16,256]{2,1,0:T(8,128)(2,1)S(1)}, bf16[2,16,256]{2,1,0:T(8,128)(2,1)S(1)}, u32[]{:S(2)}, u32[]{:S(2)}) collective-permute-start(bf16[2,16,256]{2,1,0:T(8,128)(2,1)S(1)} %get-tuple-element.51), channel_id=1, source_target_pairs={{0,6},{2,4},{4,2},{6,0},{8,14},{10,12},{12,10},{14,8},{1,7},{3,5},... | collective-permute-start | bytes 49160 | tf_op jit(solution)/shard_map/ppermute | solution.py:267
  32.4 2.9 %collective-permute-start.13 = (bf16[2,16,256]{2,1,0:T(8,128)(2,1)S(1)}, bf16[2,16,256]{2,1,0:T(8,128)(2,1)S(1)}, u32[]{:S(2)}, u32[]{:S(2)}) collective-permute-start(bf16[2,16,256]{2,1,0:T(8,128)(2,1)S(1)} %get-tuple-element.53), channel_id=1, source_target_pairs={{0,10},{2,8},{4,14},{6,12},{8,2},{10,0},{12,6},{14,4},{1,11},{3,9}... | collective-permute-start | bytes 49160 | tf_op jit(solution)/shard_map/ppermute | solution.py:267
  35.5 4.6 %collective-permute-start.15 = (bf16[2,16,256]{2,1,0:T(8,128)(2,1)S(1)}, bf16[2,16,256]{2,1,0:T(8,128)(2,1)S(1)}, u32[]{:S(2)}, u32[]{:S(2)}) collective-permute-start(bf16[2,16,256]{2,1,0:T(8,128)(2,1)S(1)} %get-tuple-element.55), channel_id=1, source_target_pairs={{0,14},{2,12},{4,10},{6,8},{8,6},{10,4},{12,2},{14,0},{1,15},{3,13... | collective-permute-start | bytes 49160 | tf_op jit(solution)/shard_map/ppermute | solution.py:267
  42.9 1.5 %collective-permute-done.16.refs_4_ = bf16[2,2,128,256]{3,2,1,0:T(8,128)(2,1)S(1)} collective-permute-done((bf16[2,2,128,256]{3,2,1,0:T(8,128)(2,1)S(1)}, bf16[2,2,128,256]{3,2,1,0:T(8,128)(2,1)S(1)}, u32[]{:S(2)}, u32[]{:S(2)}) %collective-permute-start.16) | collective-permute-done | bytes 262176 | tf_op jit(solution)/shard_map/ppermute | solution.py:263
  45.5 1.6 %collective-permute-start.17 = (bf16[2,16,256]{2,1,0:T(8,128)(2,1)S(1)}, bf16[2,16,256]{2,1,0:T(8,128)(2,1)S(1)}, u32[]{:S(2)}, u32[]{:S(2)}) collective-permute-start(bf16[2,16,256]{2,1,0:T(8,128)(2,1)S(1)} %get-tuple-element.59), channel_id=1, source_target_pairs={{0,2},{2,0},{4,6},{6,4},{8,10},{10,8},{12,14},{14,12},{1,3},{3,1},... | collective-permute-start | bytes 49160 | tf_op jit(solution)/shard_map/ppermute | solution.py:267
  47.1 2.0 %collective-permute-start.19 = (bf16[2,16,256]{2,1,0:T(8,128)(2,1)S(1)}, bf16[2,16,256]{2,1,0:T(8,128)(2,1)S(1)}, u32[]{:S(2)}, u32[]{:S(2)}) collective-permute-start(bf16[2,16,256]{2,1,0:T(8,128)(2,1)S(1)} %get-tuple-element.61), channel_id=1, source_target_pairs={{0,6},{2,4},{4,2},{6,0},{8,14},{10,12},{12,10},{14,8},{1,7},{3,5},... | collective-permute-start | bytes 49160 | tf_op jit(solution)/shard_map/ppermute | solution.py:267
  49.1 2.2 %collective-permute-start.20 = (bf16[2,16,256]{2,1,0:T(8,128)(2,1)S(1)}, bf16[2,16,256]{2,1,0:T(8,128)(2,1)S(1)}, u32[]{:S(2)}, u32[]{:S(2)}) collective-permute-start(bf16[2,16,256]{2,1,0:T(8,128)(2,1)S(1)} %get-tuple-element.62), channel_id=1, source_target_pairs={{0,8},{2,10},{4,12},{6,14},{8,0},{10,2},{12,4},{14,6},{1,9},{3,11}... | collective-permute-start | bytes 49160 | tf_op jit(solution)/shard_map/ppermute | solution.py:267
  51.3 1.7 %collective-permute-start.21 = (bf16[2,16,256]{2,1,0:T(8,128)(2,1)S(1)}, bf16[2,16,256]{2,1,0:T(8,128)(2,1)S(1)}, u32[]{:S(2)}, u32[]{:S(2)}) collective-permute-start(bf16[2,16,256]{2,1,0:T(8,128)(2,1)S(1)} %get-tuple-element.63), channel_id=1, source_target_pairs={{0,10},{2,8},{4,14},{6,12},{8,2},{10,0},{12,6},{14,4},{1,11},{3,9}... | collective-permute-start | bytes 49160 | tf_op jit(solution)/shard_map/ppermute | solution.py:267
  52.9 3.6 %collective-permute-start.22 = (bf16[2,16,256]{2,1,0:T(8,128)(2,1)S(1)}, bf16[2,16,256]{2,1,0:T(8,128)(2,1)S(1)}, u32[]{:S(2)}, u32[]{:S(2)}) collective-permute-start(bf16[2,16,256]{2,1,0:T(8,128)(2,1)S(1)} %get-tuple-element.64), channel_id=1, source_target_pairs={{0,12},{2,14},{4,8},{6,10},{8,4},{10,6},{12,0},{14,2},{1,13},{3,15... | collective-permute-start | bytes 49160 | tf_op jit(solution)/shard_map/ppermute | solution.py:267
  56.8 1.7 %collective-permute-done.22.refs_2__6_ = bf16[2,16,256]{2,1,0:T(8,128)(2,1)S(1)} collective-permute-done((bf16[2,16,256]{2,1,0:T(8,128)(2,1)S(1)}, bf16[2,16,256]{2,1,0:T(8,128)(2,1)S(1)}, u32[]{:S(2)}, u32[]{:S(2)}) %collective-permute-start.22) | collective-permute-done | bytes 16416 | tf_op jit(solution)/shard_map/ppermute | solution.py:267
  58.5 4.5 %collective-permute-done.23.refs_2__7_ = bf16[2,16,256]{2,1,0:T(8,128)(2,1)S(1)} collective-permute-done((bf16[2,16,256]{2,1,0:T(8,128)(2,1)S(1)}, bf16[2,16,256]{2,1,0:T(8,128)(2,1)S(1)}, u32[]{:S(2)}, u32[]{:S(2)}) %collective-permute-start.23) | collective-permute-done | bytes 16416 | tf_op jit(solution)/shard_map/ppermute | solution.py:267
  64.3 2.9 %collective-permute-start.26 = (bf16[2,16,256]{2,1,0:T(8,128)(2,1)S(1)}, bf16[2,16,256]{2,1,0:T(8,128)(2,1)S(1)}, u32[]{:S(2)}, u32[]{:S(2)}) collective-permute-start(bf16[2,16,256]{2,1,0:T(8,128)(2,1)S(1)} %get-tuple-element.69), channel_id=1, source_target_pairs={{0,6},{2,4},{4,2},{6,0},{8,14},{10,12},{12,10},{14,8},{1,7},{3,5},... | collective-permute-start | bytes 49160 | tf_op jit(solution)/shard_map/ppermute | solution.py:267
  67.2 2.9 %collective-permute-start.28 = (bf16[2,16,256]{2,1,0:T(8,128)(2,1)S(1)}, bf16[2,16,256]{2,1,0:T(8,128)(2,1)S(1)}, u32[]{:S(2)}, u32[]{:S(2)}) collective-permute-start(bf16[2,16,256]{2,1,0:T(8,128)(2,1)S(1)} %get-tuple-element.71), channel_id=1, source_target_pairs={{0,10},{2,8},{4,14},{6,12},{8,2},{10,0},{12,6},{14,4},{1,11},{3,9}... | collective-permute-start | bytes 49160 | tf_op jit(solution)/shard_map/ppermute | solution.py:267
  70.3 4.6 %collective-permute-start.30 = (bf16[2,16,256]{2,1,0:T(8,128)(2,1)S(1)}, bf16[2,16,256]{2,1,0:T(8,128)(2,1)S(1)}, u32[]{:S(2)}, u32[]{:S(2)}) collective-permute-start(bf16[2,16,256]{2,1,0:T(8,128)(2,1)S(1)} %get-tuple-element.73), channel_id=1, source_target_pairs={{0,14},{2,12},{4,10},{6,8},{8,6},{10,4},{12,2},{14,0},{1,15},{3,13... | collective-permute-start | bytes 49160 | tf_op jit(solution)/shard_map/ppermute | solution.py:267
  77.6 1.3 %collective-permute-done.31 = bf16[2,256,128]{2,1,0:T(8,128)(2,1)S(1)} collective-permute-done((bf16[2,256,128]{2,1,0:T(8,128)(2,1)S(1)}, bf16[2,256,128]{2,1,0:T(8,128)(2,1)S(1)}, u32[]{:S(2)}, u32[]{:S(2)}) %collective-permute-start.31) | collective-permute-done | bytes 131104 | tf_op jit(solution)/shard_map/ppermute | solution.py:263
  (77 shorter events, 17.8 us)
Async XLA Ops:
  9.4 8.6 %collective-permute-start.2 = (bf16[2,16,256]{2,1,0:T(8,128)(2,1)S(1)}, bf16[2,16,256]{2,1,0:T(8,128)(2,1)S(1)}, u32[]{:S(2)}, u32[]{:S(2)}) collective-permute-start(bf16[2,16,256]{2,1,0:T(8,128)(2,1)S(1)} %get-tuple-element.41), channel_id=1, source_target_pairs={{0,2},{2,0},{4,6},{6,4},{8,10},{10,8},{12,14},{14,12},{1,3},{3,1},... | collective-permute-start | bytes 49160 | tf_op jit(solution)/shard_map/ppermute | solution.py:267
  12.1 9.5 %collective-permute-start.3 = (bf16[2,16,256]{2,1,0:T(8,128)(2,1)S(1)}, bf16[2,16,256]{2,1,0:T(8,128)(2,1)S(1)}, u32[]{:S(2)}, u32[]{:S(2)}) collective-permute-start(bf16[2,16,256]{2,1,0:T(8,128)(2,1)S(1)} %get-tuple-element.42), channel_id=1, source_target_pairs={{0,4},{2,6},{4,0},{6,2},{8,12},{10,14},{12,8},{14,10},{1,5},{3,7},... | collective-permute-start | bytes 49160 | tf_op jit(solution)/shard_map/ppermute | solution.py:267
  13.7 8.8 %collective-permute-start.4 = (bf16[2,16,256]{2,1,0:T(8,128)(2,1)}, bf16[2,16,256]{2,1,0:T(8,128)(2,1)S(1)}, u32[]{:S(2)}, u32[]{:S(2)}) collective-permute-start(bf16[2,16,256]{2,1,0:T(8,128)(2,1)} %get-tuple-element.43), channel_id=1, source_target_pairs={{0,6},{2,4},{4,2},{6,0},{8,14},{10,12},{12,10},{14,8},{1,7},{3,5},... | collective-permute-start | bytes 49160 | tf_op jit(solution)/shard_map/ppermute | solution.py:267
  13.7 8.8 %collective-permute-start.5 = (bf16[2,16,256]{2,1,0:T(8,128)(2,1)}, bf16[2,16,256]{2,1,0:T(8,128)(2,1)S(1)}, u32[]{:S(2)}, u32[]{:S(2)}) collective-permute-start(bf16[2,16,256]{2,1,0:T(8,128)(2,1)} %get-tuple-element.44), channel_id=1, source_target_pairs={{0,8},{2,10},{4,12},{6,14},{8,0},{10,2},{12,4},{14,6},{1,9},{3,11}... | collective-permute-start | bytes 49160 | tf_op jit(solution)/shard_map/ppermute | solution.py:267
  16.7 5.8 %collective-permute-start.6 = (bf16[2,16,256]{2,1,0:T(8,128)(2,1)}, bf16[2,16,256]{2,1,0:T(8,128)(2,1)S(1)}, u32[]{:S(2)}, u32[]{:S(2)}) collective-permute-start(bf16[2,16,256]{2,1,0:T(8,128)(2,1)} %get-tuple-element.45), channel_id=1, source_target_pairs={{0,10},{2,8},{4,14},{6,12},{8,2},{10,0},{12,6},{14,4},{1,11},{3,9}... | collective-permute-start | bytes 49160 | tf_op jit(solution)/shard_map/ppermute | solution.py:267
  17.9 5.7 %collective-permute-start.7 = (bf16[2,16,256]{2,1,0:T(8,128)(2,1)}, bf16[2,16,256]{2,1,0:T(8,128)(2,1)S(1)}, u32[]{:S(2)}, u32[]{:S(2)}) collective-permute-start(bf16[2,16,256]{2,1,0:T(8,128)(2,1)} %get-tuple-element.46), channel_id=1, source_target_pairs={{0,12},{2,14},{4,8},{6,10},{8,4},{10,6},{12,0},{14,2},{1,13},{3,15... | collective-permute-start | bytes 49160 | tf_op jit(solution)/shard_map/ppermute | solution.py:267
  21.6 6.6 %collective-permute-start.8 = (bf16[2,16,256]{2,1,0:T(8,128)(2,1)}, bf16[2,16,256]{2,1,0:T(8,128)(2,1)S(1)}, u32[]{:S(2)}, u32[]{:S(2)}) collective-permute-start(bf16[2,16,256]{2,1,0:T(8,128)(2,1)} %get-tuple-element.47), channel_id=1, source_target_pairs={{0,14},{2,12},{4,10},{6,8},{8,6},{10,4},{12,2},{14,0},{1,15},{3,13... | collective-permute-start | bytes 49160 | tf_op jit(solution)/shard_map/ppermute | solution.py:267
  28.9 6.5 %collective-permute-start.9 = (bf16[2,16,256]{2,1,0:T(8,128)(2,1)S(1)}, bf16[2,16,256]{2,1,0:T(8,128)(2,1)S(1)}, u32[]{:S(2)}, u32[]{:S(2)}) collective-permute-start(bf16[2,16,256]{2,1,0:T(8,128)(2,1)S(1)} %get-tuple-element.49), channel_id=1, source_target_pairs={{0,2},{2,0},{4,6},{6,4},{8,10},{10,8},{12,14},{14,12},{1,3},{3,1},... | collective-permute-start | bytes 49160 | tf_op jit(solution)/shard_map/ppermute | solution.py:267
  29.5 6.1 %collective-permute-start.10 = (bf16[2,16,256]{2,1,0:T(8,128)(2,1)S(1)}, bf16[2,16,256]{2,1,0:T(8,128)(2,1)S(1)}, u32[]{:S(2)}, u32[]{:S(2)}) collective-permute-start(bf16[2,16,256]{2,1,0:T(8,128)(2,1)S(1)} %get-tuple-element.50), channel_id=1, source_target_pairs={{0,4},{2,6},{4,0},{6,2},{8,12},{10,14},{12,8},{14,10},{1,5},{3,7},... | collective-permute-start | bytes 49160 | tf_op jit(solution)/shard_map/ppermute | solution.py:267
  29.5 10.6 %collective-permute-start.11 = (bf16[2,16,256]{2,1,0:T(8,128)(2,1)S(1)}, bf16[2,16,256]{2,1,0:T(8,128)(2,1)S(1)}, u32[]{:S(2)}, u32[]{:S(2)}) collective-permute-start(bf16[2,16,256]{2,1,0:T(8,128)(2,1)S(1)} %get-tuple-element.51), channel_id=1, source_target_pairs={{0,6},{2,4},{4,2},{6,0},{8,14},{10,12},{12,10},{14,8},{1,7},{3,5},... | collective-permute-start | bytes 49160 | tf_op jit(solution)/shard_map/ppermute | solution.py:267
  32.4 7.7 %collective-permute-start.12 = (bf16[2,16,256]{2,1,0:T(8,128)(2,1)S(1)}, bf16[2,16,256]{2,1,0:T(8,128)(2,1)S(1)}, u32[]{:S(2)}, u32[]{:S(2)}) collective-permute-start(bf16[2,16,256]{2,1,0:T(8,128)(2,1)S(1)} %get-tuple-element.52), channel_id=1, source_target_pairs={{0,8},{2,10},{4,12},{6,14},{8,0},{10,2},{12,4},{14,6},{1,9},{3,11}... | collective-permute-start | bytes 49160 | tf_op jit(solution)/shard_map/ppermute | solution.py:267
  32.4 7.7 %collective-permute-start.13 = (bf16[2,16,256]{2,1,0:T(8,128)(2,1)S(1)}, bf16[2,16,256]{2,1,0:T(8,128)(2,1)S(1)}, u32[]{:S(2)}, u32[]{:S(2)}) collective-permute-start(bf16[2,16,256]{2,1,0:T(8,128)(2,1)S(1)} %get-tuple-element.53), channel_id=1, source_target_pairs={{0,10},{2,8},{4,14},{6,12},{8,2},{10,0},{12,6},{14,4},{1,11},{3,9}... | collective-permute-start | bytes 49160 | tf_op jit(solution)/shard_map/ppermute | solution.py:267
  35.5 6.4 %collective-permute-start.15 = (bf16[2,16,256]{2,1,0:T(8,128)(2,1)S(1)}, bf16[2,16,256]{2,1,0:T(8,128)(2,1)S(1)}, u32[]{:S(2)}, u32[]{:S(2)}) collective-permute-start(bf16[2,16,256]{2,1,0:T(8,128)(2,1)S(1)} %get-tuple-element.55), channel_id=1, source_target_pairs={{0,14},{2,12},{4,10},{6,8},{8,6},{10,4},{12,2},{14,0},{1,15},{3,13... | collective-permute-start | bytes 49160 | tf_op jit(solution)/shard_map/ppermute | solution.py:267
  45.5 7.4 %collective-permute-start.17 = (bf16[2,16,256]{2,1,0:T(8,128)(2,1)S(1)}, bf16[2,16,256]{2,1,0:T(8,128)(2,1)S(1)}, u32[]{:S(2)}, u32[]{:S(2)}) collective-permute-start(bf16[2,16,256]{2,1,0:T(8,128)(2,1)S(1)} %get-tuple-element.59), channel_id=1, source_target_pairs={{0,2},{2,0},{4,6},{6,4},{8,10},{10,8},{12,14},{14,12},{1,3},{3,1},... | collective-permute-start | bytes 49160 | tf_op jit(solution)/shard_map/ppermute | solution.py:267
  47.1 9.5 %collective-permute-start.18 = (bf16[2,16,256]{2,1,0:T(8,128)(2,1)S(1)}, bf16[2,16,256]{2,1,0:T(8,128)(2,1)S(1)}, u32[]{:S(2)}, u32[]{:S(2)}) collective-permute-start(bf16[2,16,256]{2,1,0:T(8,128)(2,1)S(1)} %get-tuple-element.60), channel_id=1, source_target_pairs={{0,4},{2,6},{4,0},{6,2},{8,12},{10,14},{12,8},{14,10},{1,5},{3,7},... | collective-permute-start | bytes 49160 | tf_op jit(solution)/shard_map/ppermute | solution.py:267
  47.1 9.6 %collective-permute-start.19 = (bf16[2,16,256]{2,1,0:T(8,128)(2,1)S(1)}, bf16[2,16,256]{2,1,0:T(8,128)(2,1)S(1)}, u32[]{:S(2)}, u32[]{:S(2)}) collective-permute-start(bf16[2,16,256]{2,1,0:T(8,128)(2,1)S(1)} %get-tuple-element.61), channel_id=1, source_target_pairs={{0,6},{2,4},{4,2},{6,0},{8,14},{10,12},{12,10},{14,8},{1,7},{3,5},... | collective-permute-start | bytes 49160 | tf_op jit(solution)/shard_map/ppermute | solution.py:267
  49.1 7.7 %collective-permute-start.20 = (bf16[2,16,256]{2,1,0:T(8,128)(2,1)S(1)}, bf16[2,16,256]{2,1,0:T(8,128)(2,1)S(1)}, u32[]{:S(2)}, u32[]{:S(2)}) collective-permute-start(bf16[2,16,256]{2,1,0:T(8,128)(2,1)S(1)} %get-tuple-element.62), channel_id=1, source_target_pairs={{0,8},{2,10},{4,12},{6,14},{8,0},{10,2},{12,4},{14,6},{1,9},{3,11}... | collective-permute-start | bytes 49160 | tf_op jit(solution)/shard_map/ppermute | solution.py:267
  56.6 6.4 %collective-permute-start.23 = (bf16[2,16,256]{2,1,0:T(8,128)(2,1)S(1)}, bf16[2,16,256]{2,1,0:T(8,128)(2,1)S(1)}, u32[]{:S(2)}, u32[]{:S(2)}) collective-permute-start(bf16[2,16,256]{2,1,0:T(8,128)(2,1)S(1)} %get-tuple-element.65), channel_id=1, source_target_pairs={{0,14},{2,12},{4,10},{6,8},{8,6},{10,4},{12,2},{14,0},{1,15},{3,13... | collective-permute-start | bytes 49160 | tf_op jit(solution)/shard_map/ppermute | solution.py:267
  63.7 6.5 %collective-permute-start.24 = (bf16[2,16,256]{2,1,0:T(8,128)(2,1)S(1)}, bf16[2,16,256]{2,1,0:T(8,128)(2,1)S(1)}, u32[]{:S(2)}, u32[]{:S(2)}) collective-permute-start(bf16[2,16,256]{2,1,0:T(8,128)(2,1)S(1)} %get-tuple-element.67), channel_id=1, source_target_pairs={{0,2},{2,0},{4,6},{6,4},{8,10},{10,8},{12,14},{14,12},{1,3},{3,1},... | collective-permute-start | bytes 49160 | tf_op jit(solution)/shard_map/ppermute | solution.py:267
  64.3 6.1 %collective-permute-start.25 = (bf16[2,16,256]{2,1,0:T(8,128)(2,1)S(1)}, bf16[2,16,256]{2,1,0:T(8,128)(2,1)S(1)}, u32[]{:S(2)}, u32[]{:S(2)}) collective-permute-start(bf16[2,16,256]{2,1,0:T(8,128)(2,1)S(1)} %get-tuple-element.68), channel_id=1, source_target_pairs={{0,4},{2,6},{4,0},{6,2},{8,12},{10,14},{12,8},{14,10},{1,5},{3,7},... | collective-permute-start | bytes 49160 | tf_op jit(solution)/shard_map/ppermute | solution.py:267
  64.3 10.6 %collective-permute-start.26 = (bf16[2,16,256]{2,1,0:T(8,128)(2,1)S(1)}, bf16[2,16,256]{2,1,0:T(8,128)(2,1)S(1)}, u32[]{:S(2)}, u32[]{:S(2)}) collective-permute-start(bf16[2,16,256]{2,1,0:T(8,128)(2,1)S(1)} %get-tuple-element.69), channel_id=1, source_target_pairs={{0,6},{2,4},{4,2},{6,0},{8,14},{10,12},{12,10},{14,8},{1,7},{3,5},... | collective-permute-start | bytes 49160 | tf_op jit(solution)/shard_map/ppermute | solution.py:267
  67.2 7.7 %collective-permute-start.27 = (bf16[2,16,256]{2,1,0:T(8,128)(2,1)S(1)}, bf16[2,16,256]{2,1,0:T(8,128)(2,1)S(1)}, u32[]{:S(2)}, u32[]{:S(2)}) collective-permute-start(bf16[2,16,256]{2,1,0:T(8,128)(2,1)S(1)} %get-tuple-element.70), channel_id=1, source_target_pairs={{0,8},{2,10},{4,12},{6,14},{8,0},{10,2},{12,4},{14,6},{1,9},{3,11}... | collective-permute-start | bytes 49160 | tf_op jit(solution)/shard_map/ppermute | solution.py:267
  67.2 7.7 %collective-permute-start.28 = (bf16[2,16,256]{2,1,0:T(8,128)(2,1)S(1)}, bf16[2,16,256]{2,1,0:T(8,128)(2,1)S(1)}, u32[]{:S(2)}, u32[]{:S(2)}) collective-permute-start(bf16[2,16,256]{2,1,0:T(8,128)(2,1)S(1)} %get-tuple-element.71), channel_id=1, source_target_pairs={{0,10},{2,8},{4,14},{6,12},{8,2},{10,0},{12,6},{14,4},{1,11},{3,9}... | collective-permute-start | bytes 49160 | tf_op jit(solution)/shard_map/ppermute | solution.py:267
  70.3 6.4 %collective-permute-start.30 = (bf16[2,16,256]{2,1,0:T(8,128)(2,1)S(1)}, bf16[2,16,256]{2,1,0:T(8,128)(2,1)S(1)}, u32[]{:S(2)}, u32[]{:S(2)}) collective-permute-start(bf16[2,16,256]{2,1,0:T(8,128)(2,1)S(1)} %get-tuple-element.73), channel_id=1, source_target_pairs={{0,14},{2,12},{4,10},{6,8},{8,6},{10,4},{12,2},{14,0},{1,15},{3,13... | collective-permute-start | bytes 49160 | tf_op jit(solution)/shard_map/ppermute | solution.py:267
  (21 other events, 251.8 us)

commit v3 on v2

v3 whole, which is shorter than its diff:
```python
import jax
import jax.numpy as jnp
from jax import lax
from jax.experimental import pallas as pl
from jax.experimental.pallas import tpu as pltpu
from jax.sharding import PartitionSpec as P

time_step = 0.4
half_step = 0.5 * time_step
VMEM_LIMIT = 8 * 1024 * 1024
HBM = pl.BlockSpec(memory_space=pl.ANY)
VMEM = pl.BlockSpec(memory_space=pltpu.VMEM)
SMEM = pl.BlockSpec(memory_space=pltpu.SMEM)


def turned(block):
    half = block.shape[0] // 2
    return jnp.concatenate([block[half:], -block[:half]], axis=0)


def bf16(block):
    return block.astype(jnp.bfloat16)


def f32(block):
    return block.astype(jnp.float32)


def views(tgt_buf, proj_buf):
    rows = tgt_buf.shape[1] // 2

    def tgt_view(part, core):
        return tgt_buf[part, pl.ds(pl.multiple_of(core * rows, rows), rows), :]

    def proj_view(part, core):
        return proj_buf[part, core]

    return tgt_view, proj_view


def project(view, core, amp):
    return jnp.dot(
        bf16(amp), view(0, core), preferred_element_type=jnp.float32
    ) + jnp.dot(bf16(turned(amp)), view(1, core), preferred_element_type=jnp.float32)


def expand(view, core, field, turned_field):
    contract = (((1,), (1,)), ((), ()))
    return lax.dot_general(
        turned_field, view(0, core), contract, preferred_element_type=jnp.float32
    ) + lax.dot_general(field, view(1, core), contract, preferred_element_type=jnp.float32)


def load_kernel(
    flags,
    counts,
    tgt_hbm,
    proj_hbm,
    tgt_energy,
    proj_energy,
    tgt_own,
    proj_own,
    tgt_buf,
    proj_buf,
    gates,
    start_ref,
    part_ref,
    sems,
):
    n_prj, n_tgt = flags.shape
    core = lax.axis_index("rep")
    tgt_index = lax.axis_index("tgt")
    prj_index = lax.axis_index("prj")
    rows = tgt_buf.shape[1]
    groups = proj_buf.shape[1]
    row_start = pl.multiple_of(prj_index * rows, rows)
    group_start = tgt_index * groups
    copies = []
    for part in range(2):
        copies.append(
            pltpu.make_async_copy(
                tgt_hbm.at[part, pl.ds(row_start, rows)], tgt_buf.at[part], sems.at[part]
            )
        )
        copies.append(
            pltpu.make_async_copy(
                proj_hbm.at[part, pl.ds(group_start, groups)], proj_buf.at[part], sems.at[2 + part]
            )
        )
    for copy in copies:
        copy.start()

    width = gates.shape[1] // 2

    def write_gate(slot, a, b):
        for tile in range(2):
            live = jnp.logical_and(flags[b, a] > 0, 2 * core + tile < counts[b, a])
            value = jnp.where(live, 1.0, 0.0).astype(jnp.float32)
            gates[slot : slot + 1, tile * width : (tile + 1) * width] = jnp.full(
                (1, width), value, jnp.float32
            )

    for a in range(n_tgt):
        write_gate(a, a, prj_index)
    for b in range(n_prj):
        write_gate(n_tgt + b, tgt_index, jnp.bitwise_xor(prj_index, b))

    amps = (tgt_own[...].T, proj_own[0].T)
    energies = (tgt_energy[...][None, :], proj_energy[...])
    for kind in range(2):
        start_ref[kind] = amps[kind] + half_step * (energies[kind] * turned(amps[kind]))
    for copy in copies:
        copy.wait()
    for kind, view in enumerate(views(tgt_buf, proj_buf)):
        part_ref[kind] = project(view, core, amps[kind])


def first_kernel(tgt_buf, proj_buf, weight, part_ref, tgt_other, proj_other, zt_ref, zp_ref):
    other = 1 - lax.axis_index("rep")
    weights = weight[...][None, :]
    tgt_view, proj_view = views(tgt_buf, proj_buf)
    zt_ref[...] = bf16(weights * (part_ref[0] + project(tgt_view, other, tgt_other[...].T)))
    zp_ref[...] = bf16(weights * (part_ref[1] + project(proj_view, other, proj_other[0].T)))


def sum_kernel(zt_parts, zp_parts, zt_ref, zp_ref):
    zt_ref[...] = bf16(sum(f32(part[...]) for part in zt_parts))
    zp_ref[...] = bf16(sum(f32(zp_parts[a]) for a in range(zp_parts.shape[0])))


def fields_of(gates, zt_all, zp_parts):
    n_tgt = zt_all.shape[0]
    tgt_field = sum(gates[n_tgt + b : n_tgt + b + 1, :] * f32(part[...]) for b, part in enumerate(zp_parts))
    proj_field = sum(gates[a : a + 1, :] * f32(zt_all[a]) for a in range(n_tgt))
    return [(bf16(field), bf16(turned(field))) for field in (tgt_field, proj_field)]


def half_kernel(tgt_buf, proj_buf, gates, zt_all, zp_parts, start_ref, send, keep):
    core = lax.axis_index("rep")
    fields = fields_of(gates, zt_all, zp_parts)
    for kind, view in enumerate(views(tgt_buf, proj_buf)):
        own = start_ref[kind] + half_step * expand(view, core, *fields[kind])
        other = half_step * expand(view, 1 - core, *fields[kind])
        keep[kind, 0] = own
        keep[kind, 1] = other
        send[kind, 0] = bf16(own)
        send[kind, 1] = bf16(other)


def second_kernel(tgt_buf, proj_buf, weight, keep, received, zt_ref, zp_ref, half_ref):
    core = lax.axis_index("rep")
    weights = weight[...][None, :]
    for kind, view in enumerate(views(tgt_buf, proj_buf)):
        own = keep[kind, 0] + f32(received[kind, 1])
        other = keep[kind, 1] + f32(received[kind, 0])
        half_ref[kind] = own
        total = project(view, core, own) + project(view, 1 - core, other)
        (zt_ref, zp_ref)[kind][...] = bf16(weights * total)


def last_kernel(
    tgt_buf,
    proj_buf,
    gates,
    zt_all,
    zp_parts,
    tgt_energy,
    proj_energy,
    tgt_own,
    proj_own,
    half_ref,
    send,
    tgt_keep,
    proj_keep,
):
    core = lax.axis_index("rep")
    energies = (tgt_energy[...][None, :], proj_energy[...])
    fields = fields_of(gates, zt_all, zp_parts)
    for kind, view in enumerate(views(tgt_buf, proj_buf)):
        send[kind] = bf16((time_step * expand(view, 1 - core, *fields[kind])).T)
        change = time_step * (
            energies[kind] * turned(half_ref[kind]) + expand(view, core, *fields[kind])
        )
        if kind == 0:
            tgt_keep[...] = tgt_own[...] + change.T
        else:
            proj_keep[...] = proj_own[0] + change.T


def add_kernel(tgt_keep, proj_keep, received, new_tgt, new_proj):
    new_tgt[...] = tgt_keep[...] + f32(received[0])
    new_proj[0] = proj_keep[...] + f32(received[1])


def shards(
    tgt_basis,
    proj_basis,
    quad_weight,
    tgt_energy,
    proj_energy,
    pair_flags,
    tile_counts,
    tgt_amp,
    proj_amp,
):
    n_tgt = lax.axis_size("tgt")
    n_prj = lax.axis_size("prj")
    points = quad_weight.shape[0]
    rows, two_cols = tgt_amp.shape
    group_rows = proj_amp.shape[1]

    def call(kernel, out_shape, in_specs, scratch_shapes=(), cost=None):
        specs = list(in_specs) + [None] * (len(out_shape) + len(scratch_shapes))

        def with_lists(*refs):
            refs = jax.tree.leaves(refs)
            args = [
                [refs.pop(0) for _ in spec] if isinstance(spec, list) else refs.pop(0) for spec in specs
            ]
            kernel(*args)

        return pl.pallas_call(
            with_lists,
            out_shape=out_shape,
            in_specs=in_specs,
            out_specs=[VMEM] * len(out_shape),
            scratch_shapes=scratch_shapes,
            cost_estimate=cost,
            compiler_params=pltpu.CompilerParams(vmem_limit_bytes=VMEM_LIMIT),
        )

    def in_vmem(shape, dtype):
        return pltpu.VMEM(shape, dtype)

    def other_core(block):
        return lax.ppermute(block, "rep", [(0, 1), (1, 0)])

    def over_prj(block):
        return [block] + [
            lax.ppermute(block, "prj", [(me, me ^ flip) for me in range(n_prj)])
            for flip in range(1, n_prj)
        ]

    def over_tgt(block):
        return lax.all_gather(block, "tgt", axis=0, tiled=False)

    coefs = in_vmem((two_cols, points), jnp.bfloat16)
    states = in_vmem((2, two_cols, rows), jnp.float32)

    def reduced(zt, zp):
        zt_parts, zp_parts = over_prj(zt), over_tgt(zp)
        zt, zp = call(sum_kernel, [coefs, coefs], [[VMEM] * n_prj, VMEM])(zt_parts, zp_parts)
        zp_parts, zt_all = over_prj(zp), over_tgt(zt)
        return zt_all, zp_parts

    tgt_other, proj_other = other_core(tgt_amp), other_core(proj_amp)
    tgt_buf, proj_buf, gates, start, part = call(
        load_kernel,
        [
            in_vmem((2, 2 * rows, points), jnp.bfloat16),
            in_vmem((2, 2, group_rows, points), jnp.bfloat16),
            in_vmem((n_tgt + n_prj, points), jnp.float32),
            states,
            in_vmem((2, two_cols, points), jnp.float32),
        ],
        [SMEM, SMEM, HBM, HBM] + [VMEM] * 4,
        [pltpu.SemaphoreType.DMA((4,))],
        pl.CostEstimate(flops=2 * 4 * rows * two_cols * points, bytes_accessed=3 * 1024 * 1024, transcendentals=0),
    )(
        pair_flags.T,
        tile_counts.T,
        pltpu.with_memory_space_constraint(tgt_basis, pltpu.HBM),
        pltpu.with_memory_space_constraint(proj_basis, pltpu.HBM),
        tgt_energy,
        proj_energy,
        tgt_amp,
        proj_amp,
    )
    zt, zp = call(first_kernel, [coefs, coefs], [VMEM] * 6)(
        tgt_buf, proj_buf, quad_weight, part, tgt_other, proj_other
    )
    zt_all, zp_parts = reduced(zt, zp)
    pair = (2, 2, two_cols, rows)
    lists = [VMEM] * 4 + [[VMEM] * n_prj]
    send, keep = call(
        half_kernel, [in_vmem(pair, jnp.bfloat16), in_vmem(pair, jnp.float32)], lists + [VMEM]
    )(tgt_buf, proj_buf, gates, zt_all, zp_parts, start)
    zt, zp, half = call(second_kernel, [coefs, coefs, states], [VMEM] * 5)(
        tgt_buf, proj_buf, quad_weight, keep, other_core(send)
    )
    zt_all, zp_parts = reduced(zt, zp)
    send, tgt_keep, proj_keep = call(
        last_kernel,
        [
            in_vmem((2, rows, two_cols), jnp.bfloat16),
            in_vmem((rows, two_cols), jnp.float32),
            in_vmem((rows, two_cols), jnp.float32),
        ],
        lists + [VMEM] * 5,
    )(tgt_buf, proj_buf, gates, zt_all, zp_parts, tgt_energy, proj_energy, tgt_amp, proj_amp, half)
    return call(
        add_kernel,
        [
            jax.ShapeDtypeStruct(tgt_amp.shape, jnp.float32),
            jax.ShapeDtypeStruct(proj_amp.shape, jnp.float32),
        ],
        [VMEM] * 3,
    )(tgt_keep, proj_keep, other_core(send))


def solution(mesh):
    in_specs = (
        P(None, "tgt", "rep"),
        P(None, None, "prj", "rep"),
        P(("bpar", "rep")),
        P(("tgt", "prj", "rep")),
        P(("tgt", "rep"), "prj"),
        P("bpar", None),
        P("bpar", None),
        P(("bpar", "tgt", "prj", "rep"), None),
        P(("bpar", "tgt", "rep"), "prj", None),
    )
    out_specs = (P(("bpar", "tgt", "prj", "rep"), None), P(("bpar", "tgt", "rep"), "prj", None))

    def step(*args):
        return tuple(shards(*args))

    return jax.shard_map(step, mesh=mesh, in_specs=in_specs, out_specs=out_specs, check_vma=False)
```

time: 80.6 us -> 76.7 us (0.952)
  blocking collectives: 0 us -> 57.1 us
  starting transfers between devices: 46.6 us -> 6.54 us
  waiting for transfers between devices: 20.1 us -> 2.87 us
  local copies, waits for them, and re-layouts: 6.86 us -> 4.55 us
  other arithmetic: 1.36 us -> 0 us
    all_gather x0 -> x4, blocking collectives: none -> 57.1 us  [over_tgt(): return lax.all_gather(block, 'tgt', axis=0, tiled=False)]
    ppermute x28 -> x4, starting transfers between devices: 45.8 us -> 5.8 us  [over_prj(): lax.ppermute(block, 'prj', [(me, me ^ flip) for me in range(n_prj)])]
    ppermute x28 -> x4, waiting for transfers between devices: 15.8 us -> 0.01 us  [over_prj(): lax.ppermute(block, 'prj', [(me, me ^ flip) for me in range(n_prj)])]
    unnamed x28 -> x22, local copies, waits for them, and re-layouts: 6.86 us -> 4.55 us
    ppermute x4, waiting for transfers between devices: 4.34 us -> 2.86 us  [other_core(): return lax.ppermute(block, 'rep', [(0, 1), (1, 0)])]
    add x2 -> x0, other arithmetic: 1.34 us -> none  [shards(): return (tgt_keep + received[0], proj_keep + received[1:])]
    pallas_call x6 -> x8, Pallas kernels: 4.55 us -> 4.63 us  [the longest x1 2.04 us: shards(): call(load_kernel, [in_vmem((2, 2 * rows, points), jnp.bfloat16), in_vmem(...]
  transfers between devices with their start and end apart: 32 -> 8, of which waited for: 13 -> 2; matrix products, arithmetic and copies ran while one was open for 1% -> 0% of each run, Pallas kernels for 0% -> 3%
where the time goes in v3:
time: 76.7 us; the launch traced here: 76.5 us
  blocking collectives  57.1 us (74%)
  starting transfers between devices  6.54 us (9%)
  Pallas kernels  4.63 us (6%)
  local copies, waits for them, and re-layouts  4.55 us (6%)
  waiting for transfers between devices  2.87 us (4%)
  between operations  0.78 us (1%)
    all_gather x4, blocking collectives, over_tgt(): return lax.all_gather(block, 'tgt', axis=0, tiled=False)  57.1 us
    ppermute x4, starting transfers between devices, over_prj(): lax.ppermute(block, 'prj', [(me, me ^ flip) for me in range(n_prj)])  5.8 us
    unnamed x22, local copies, waits for them, and re-layouts  4.55 us
    ppermute x4, waiting for transfers between devices, other_core(): return lax.ppermute(block, 'rep', [(0, 1), (1, 0)])  2.86 us
    pallas_call x1, Pallas kernels, shards(): call(load_kernel, [in_vmem((2, 2 * rows, points), jnp.bfloat16), in_vmem(...  2.04 us
  transfers between devices with their start and end apart: 8, of which 2 were waited for; matrix products, arithmetic and copies ran while one was open for 0% of the time, Pallas kernels for 3%

profile of v3, /device:TPU:0, one launch (start us, length us, event | category | flops | bytes accessed | tf_op | source)
XLA Modules:
  0.0 76.5 jit_solution(13169106091788019502)
XLA Ops:
  0.6 0.5 collective-permute-start
  1.2 0.1 collective-permute-start.1
  1.2 0.9 %copy-done = f32[256,128]{1,0:T(8,128)S(1)} copy-done((f32[256,128]{1,0:T(8,128)S(1)}, f32[256,128]{1,0:T(8,128)}, u32[]{:S(2)}) %copy-start) | copy-done | bytes 131096
  2.1 0.9 %copy-done.2 = f32[1,256,128]{2,1,0:T(8,128)S(1)} copy-done((f32[1,256,128]{2,1,0:T(8,128)S(1)}, f32[1,256,128]{2,1,0:T(8,128)}, u32[]{:S(2)}) %copy-start.2) | copy-done | bytes 131096
  3.1 0.7 copy-done.4
  3.7 0.7 copy-done.6
  4.4 0.7 copy-done.9
  5.1 0.7 copy-done.10
  5.8 2.0 %shard_map.104 = (bf16[2,512,256]{2,1,0:T(8,128)(2,1)S(1)}, bf16[2,2,256,256]{3,2,1,0:T(8,128)(2,1)S(1)}, f32[6,256]{1,0:T(8,128)S(1)}, f32[2,128,256]{2,1,0:T(8,128)S(1)}, f32[2,128,256]{2,1,0:T(8,128)S(1)}) custom-call(s32[2,4]{1,0:T(2,128)S(1)} %bitcast.10, s32[2,4]{1,0:T(2,128)S(1)} %bitcast.11, bf16[2,1024,256]{2,1,0:T(8,128)(2,1)} %refs_2_.3, ...), custom_call_target="tpu_custom_call" | custom-call | flops 67108864 | bytes 3145728 | tf_op jit(solution)/shard_map/pallas_call | solution.py:257
  7.8 0.3 shard_map.105
  8.2 3.0 %collective-permute-start.2 = (bf16[128,256]{1,0:T(8,128)(2,1)S(1)}, bf16[128,256]{1,0:T(8,128)(2,1)S(1)}, u32[]{:S(2)}, u32[]{:S(2)}) collective-permute-start(bf16[128,256]{1,0:T(8,128)(2,1)S(1)} %get-tuple-element.25.refs_0__0_), channel_id=1, source_target_pairs={{0,2},{2,0},{1,3},{3,1},{4,6},{6,4},{5,7},{7,5},{8,10},{10,8},{9,1... | collective-permute-start | bytes 196616 | tf_op jit(solution)/shard_map/ppermute | solution.py:240
  11.2 14.1 %all-gather = bf16[512,256]{1,0:T(8,128)(2,1)S(1)} all-gather(bf16[128,256]{1,0:T(8,128)(2,1)S(1)} %get-tuple-element.26), channel_id=2, replica_groups=mesh['bpar'=2,'tgt'=4,'prj'=2,'rep'=2] {'tgt'}, dimensions={0}, use_global_device_ids=true | all-gather | bytes 327680 | tf_op jit(solution)/shard_map/all_gather | solution.py:245
  25.4 0.6 collective-permute-start.3
  25.9 14.4 %all-gather.1 = bf16[512,256]{1,0:T(8,128)(2,1)S(1)} all-gather(bf16[128,256]{1,0:T(8,128)(2,1)S(1)} %get-tuple-element.27), channel_id=3, replica_groups=mesh['bpar'=2,'tgt'=4,'prj'=2,'rep'=2] {'tgt'}, dimensions={0}, use_global_device_ids=true | all-gather | bytes 327680 | tf_op jit(solution)/shard_map/all_gather | solution.py:245
  40.4 0.5 shard_map.107
  40.9 1.5 %collective-permute-done.4.refs_4_ = bf16[2,2,128,256]{3,2,1,0:T(8,128)(2,1)S(1)} collective-permute-done((bf16[2,2,128,256]{3,2,1,0:T(8,128)(2,1)S(1)}, bf16[2,2,128,256]{3,2,1,0:T(8,128)(2,1)S(1)}, u32[]{:S(2)}, u32[]{:S(2)}) %collective-permute-start.4) | collective-permute-done | bytes 262176 | tf_op jit(solution)/shard_map/ppermute | solution.py:236
  42.5 0.3 shard_map.108
  42.8 1.7 %collective-permute-start.5 = (bf16[128,256]{1,0:T(8,128)(2,1)S(1)}, bf16[128,256]{1,0:T(8,128)(2,1)S(1)}, u32[]{:S(2)}, u32[]{:S(2)}) collective-permute-start(bf16[128,256]{1,0:T(8,128)(2,1)S(1)} %get-tuple-element.32.refs_0__0_), channel_id=1, source_target_pairs={{0,2},{2,0},{1,3},{3,1},{4,6},{6,4},{5,7},{7,5},{8,10},{10,8},{9,1... | collective-permute-start | bytes 196616 | tf_op jit(solution)/shard_map/ppermute | solution.py:240
  44.5 14.0 %all-gather.2 = bf16[512,256]{1,0:T(8,128)(2,1)S(1)} all-gather(bf16[128,256]{1,0:T(8,128)(2,1)S(1)} %get-tuple-element.33), channel_id=4, replica_groups=mesh['bpar'=2,'tgt'=4,'prj'=2,'rep'=2] {'tgt'}, dimensions={0}, use_global_device_ids=true | all-gather | bytes 327680 | tf_op jit(solution)/shard_map/all_gather | solution.py:245
  58.6 0.6 collective-permute-start.6
  59.2 14.5 %all-gather.3 = bf16[512,256]{1,0:T(8,128)(2,1)S(1)} all-gather(bf16[128,256]{1,0:T(8,128)(2,1)S(1)} %get-tuple-element.34), channel_id=5, replica_groups=mesh['bpar'=2,'tgt'=4,'prj'=2,'rep'=2] {'tgt'}, dimensions={0}, use_global_device_ids=true | all-gather | bytes 327680 | tf_op jit(solution)/shard_map/all_gather | solution.py:245
  73.7 0.6 shard_map.110
  74.4 1.3 %collective-permute-done.7.refs_2_ = bf16[2,256,128]{2,1,0:T(8,128)(2,1)S(1)} collective-permute-done((bf16[2,256,128]{2,1,0:T(8,128)(2,1)S(1)}, bf16[2,256,128]{2,1,0:T(8,128)(2,1)S(1)}, u32[]{:S(2)}, u32[]{:S(2)}) %collective-permute-start.7) | collective-permute-done | bytes 131104 | tf_op jit(solution)/shard_map/ppermute | solution.py:236
  75.7 0.7 shard_map.111
  (26 shorter events, 0.3 us)
Async XLA Ops:
  0.6 7.2 %copy-start.8 = (f32[256]{0:T(256)S(1)}, f32[256]{0:T(256)}, u32[]{:S(2)}) copy-start(f32[256]{0:T(256)} %refs_2_.5) | copy-start | bytes 3076
  0.6 7.2 %collective-permute-start = (f32[256,128]{1,0:T(8,128)}, f32[256,128]{1,0:T(8,128)S(1)}, u32[]{:S(2)}, u32[]{:S(2)}) collective-permute-start(f32[256,128]{1,0:T(8,128)} %refs_7_.3), channel_id=1, source_target_pairs={{0,1},{1,0},{2,3},{3,2},{4,5},{5,4},{6,7},{7,6},{8,9},{9,8},{10,11... | collective-permute-start | bytes 393224 | tf_op jit(solution)/shard_map/ppermute | solution.py:236
  1.2 6.7 %collective-permute-start.1 = (f32[1,256,128]{2,1,0:T(8,128)}, f32[1,256,128]{2,1,0:T(8,128)S(1)}, u32[]{:S(2)}, u32[]{:S(2)}) collective-permute-start(f32[1,256,128]{2,1,0:T(8,128)} %refs_8_.1), channel_id=1, source_target_pairs={{0,1},{1,0},{2,3},{3,2},{4,5},{5,4},{6,7},{7,6},{8,9},{9,8},{10,11... | collective-permute-start | bytes 393224 | tf_op jit(solution)/shard_map/ppermute | solution.py:236
  1.2 0.9 %copy-start = (f32[256,128]{1,0:T(8,128)S(1)}, f32[256,128]{1,0:T(8,128)}, u32[]{:S(2)}) copy-start(f32[256,128]{1,0:T(8,128)} %refs_7_.3) | copy-start | bytes 393220
  2.1 0.9 %copy-start.2 = (f32[1,256,128]{2,1,0:T(8,128)S(1)}, f32[1,256,128]{2,1,0:T(8,128)}, u32[]{:S(2)}) copy-start(f32[1,256,128]{2,1,0:T(8,128)} %refs_8_.1) | copy-start | bytes 393220
  3.0 0.7 copy-start.4
  3.7 0.7 copy-start.6
  4.4 0.7 copy-start.9
  5.1 0.7 copy-start.10
  8.2 17.1 %collective-permute-start.2 = (bf16[128,256]{1,0:T(8,128)(2,1)S(1)}, bf16[128,256]{1,0:T(8,128)(2,1)S(1)}, u32[]{:S(2)}, u32[]{:S(2)}) collective-permute-start(bf16[128,256]{1,0:T(8,128)(2,1)S(1)} %get-tuple-element.25.refs_0__0_), channel_id=1, source_target_pairs={{0,2},{2,0},{1,3},{3,1},{4,6},{6,4},{5,7},{7,5},{8,10},{10,8},{9,1... | collective-permute-start | bytes 196616 | tf_op jit(solution)/shard_map/ppermute | solution.py:240
  25.4 15.0 %collective-permute-start.3 = (bf16[128,256]{1,0:T(8,128)(2,1)S(1)}, bf16[128,256]{1,0:T(8,128)(2,1)S(1)}, u32[]{:S(2)}, u32[]{:S(2)}) collective-permute-start(bf16[128,256]{1,0:T(8,128)(2,1)S(1)} %get-tuple-element.28.refs_4__0_), channel_id=1, source_target_pairs={{0,2},{2,0},{1,3},{3,1},{4,6},{6,4},{5,7},{7,5},{8,10},{10,8},{9,1... | collective-permute-start | bytes 196616 | tf_op jit(solution)/shard_map/ppermute | solution.py:240
  40.3 33.3 %copy-start.1 = (f32[256,128]{1,0:T(8,128)S(1)}, f32[256,128]{1,0:T(8,128)}, u32[]{:S(2)}) copy-start(f32[256,128]{1,0:T(8,128)} %refs_7_.3) | copy-start | bytes 393220
  40.3 33.3 %copy-start.3 = (f32[1,256,128]{2,1,0:T(8,128)S(1)}, f32[1,256,128]{2,1,0:T(8,128)}, u32[]{:S(2)}) copy-start(f32[1,256,128]{2,1,0:T(8,128)} %refs_8_.1) | copy-start | bytes 393220
  40.3 33.4 %copy-start.5 = (f32[256]{0:T(256)S(1)}, f32[256]{0:T(256)}, u32[]{:S(2)}) copy-start(f32[256]{0:T(256)} %refs_5_.3) | copy-start | bytes 3076
  40.3 33.3 %copy-start.7 = (f32[1,256]{1,0:T(1,128)S(1)}, f32[1,256]{1,0:T(1,128)}, u32[]{:S(2)}) copy-start(f32[1,256]{1,0:T(1,128)} %refs_6_.3) | copy-start | bytes 3076
  40.9 1.6 %collective-permute-start.4 = (bf16[2,2,128,256]{3,2,1,0:T(8,128)(2,1)S(1)}, bf16[2,2,128,256]{3,2,1,0:T(8,128)(2,1)S(1)}, u32[]{:S(2)}, u32[]{:S(2)}) collective-permute-start(bf16[2,2,128,256]{3,2,1,0:T(8,128)(2,1)S(1)} %get-tuple-element.31), channel_id=1, source_target_pairs={{0,1},{1,0},{2,3},{3,2},{4,5},{5,4},{6,7},{7,6},{8,9},{9,8},{10,11... | collective-permute-start | bytes 786440 | tf_op jit(solution)/shard_map/ppermute | solution.py:236
  42.8 15.7 %collective-permute-start.5 = (bf16[128,256]{1,0:T(8,128)(2,1)S(1)}, bf16[128,256]{1,0:T(8,128)(2,1)S(1)}, u32[]{:S(2)}, u32[]{:S(2)}) collective-permute-start(bf16[128,256]{1,0:T(8,128)(2,1)S(1)} %get-tuple-element.32.refs_0__0_), channel_id=1, source_target_pairs={{0,2},{2,0},{1,3},{3,1},{4,6},{6,4},{5,7},{7,5},{8,10},{10,8},{9,1... | collective-permute-start | bytes 196616 | tf_op jit(solution)/shard_map/ppermute | solution.py:240
  58.6 15.1 %collective-permute-start.6 = (bf16[128,256]{1,0:T(8,128)(2,1)S(1)}, bf16[128,256]{1,0:T(8,128)(2,1)S(1)}, u32[]{:S(2)}, u32[]{:S(2)}) collective-permute-start(bf16[128,256]{1,0:T(8,128)(2,1)S(1)} %get-tuple-element.35.refs_4__0_), channel_id=1, source_target_pairs={{0,2},{2,0},{1,3},{3,1},{4,6},{6,4},{5,7},{7,5},{8,10},{10,8},{9,1... | collective-permute-start | bytes 196616 | tf_op jit(solution)/shard_map/ppermute | solution.py:240
  74.3 1.4 %collective-permute-start.7 = (bf16[2,256,128]{2,1,0:T(8,128)(2,1)S(1)}, bf16[2,256,128]{2,1,0:T(8,128)(2,1)S(1)}, u32[]{:S(2)}, u32[]{:S(2)}) collective-permute-start(bf16[2,256,128]{2,1,0:T(8,128)(2,1)S(1)} %get-tuple-element.39), channel_id=1, source_target_pairs={{0,1},{1,0},{2,3},{3,2},{4,5},{5,4},{6,7},{7,6},{8,9},{9,8},{10,11... | collective-permute-start | bytes 393224 | tf_op jit(solution)/shard_map/ppermute | solution.py:236

commit v4 on v3

v4 whole, which is shorter than its diff:
```python
import functools

import jax
import jax.numpy as jnp
from jax import lax
from jax.experimental import pallas as pl
from jax.experimental.pallas import tpu as pltpu
from jax.sharding import PartitionSpec as P

time_step = 0.4
half_step = 0.5 * time_step
VMEM_LIMIT = 8 * 1024 * 1024
HBM = pl.BlockSpec(memory_space=pl.ANY)
VMEM = pl.BlockSpec(memory_space=pltpu.VMEM)


def turned(block):
    half = block.shape[0] // 2
    return jnp.concatenate([block[half:], -block[:half]], axis=0)


def bf16(block):
    return block.astype(jnp.bfloat16)


def f32(block):
    return block.astype(jnp.float32)


def views(tgt_buf, proj_buf):
    rows = tgt_buf.shape[1] // 2

    def tgt_view(part, core):
        return tgt_buf[part, pl.ds(pl.multiple_of(core * rows, rows), rows), :]

    def proj_view(part, core):
        return proj_buf[part, core]

    return tgt_view, proj_view


def project(view, core, amp):
    return jnp.dot(
        bf16(amp), view(0, core), preferred_element_type=jnp.float32
    ) + jnp.dot(bf16(turned(amp)), view(1, core), preferred_element_type=jnp.float32)


def expand(view, core, field, turned_field):
    contract = (((1,), (1,)), ((), ()))
    return lax.dot_general(
        turned_field, view(0, core), contract, preferred_element_type=jnp.float32
    ) + lax.dot_general(field, view(1, core), contract, preferred_element_type=jnp.float32)


def load_kernel(
    flags_hbm,
    counts_hbm,
    weight_hbm,
    tgt_hbm,
    proj_hbm,
    tgt_energy_hbm,
    proj_energy_hbm,
    tgt_own_hbm,
    proj_own_hbm,
    tgt_buf,
    proj_buf,
    gate,
    weight,
    energy,
    amp_ref,
    part_ref,
    flags,
    counts,
    flat_weight,
    flat_energy,
    tgt_own,
    proj_own,
    sems,
):
    core = lax.axis_index("rep")
    tgt_index = lax.axis_index("tgt")
    prj_index = lax.axis_index("prj")
    rows = tgt_buf.shape[1]
    groups = proj_buf.shape[1]
    row_start = pl.multiple_of(prj_index * rows, rows)
    group_start = tgt_index * groups
    pairs = [
        (tgt_own_hbm, tgt_own),
        (proj_own_hbm, proj_own),
        (tgt_hbm.at[0, pl.ds(row_start, rows)], tgt_buf.at[0]),
        (tgt_hbm.at[1, pl.ds(row_start, rows)], tgt_buf.at[1]),
        (proj_hbm.at[0, pl.ds(group_start, groups)], proj_buf.at[0]),
        (proj_hbm.at[1, pl.ds(group_start, groups)], proj_buf.at[1]),
        (flags_hbm, flags),
        (counts_hbm, counts),
        (weight_hbm, flat_weight),
        (tgt_energy_hbm, flat_energy),
        (proj_energy_hbm, energy.at[1]),
    ]
    copies = [pltpu.make_async_copy(src, dst, sems.at[k]) for k, (src, dst) in enumerate(pairs)]
    for copy in copies:
        copy.start()
    for copy in copies:
        copy.wait()
    weight[...] = flat_weight[...][None, :]
    energy[0] = flat_energy[...][None, :]
    width = gate.shape[1] // 2
    for tile in range(2):
        live = jnp.logical_and(
            flags[prj_index, tgt_index] > 0, 2 * core + tile < counts[prj_index, tgt_index]
        )
        value = jnp.where(live, 1.0, 0.0).astype(jnp.float32)
        gate[:, tile * width : (tile + 1) * width] = jnp.full((1, width), value, jnp.float32)
    amps = (tgt_own[...].T, proj_own[0].T)
    for kind, view in enumerate(views(tgt_buf, proj_buf)):
        amp_ref[kind] = amps[kind]
        part_ref[kind] = project(view, core, amps[kind])


def first_kernel(tgt_buf, proj_buf, weight, part_ref, tgt_other, proj_other, zt_ref, zp_ref):
    other = 1 - lax.axis_index("rep")
    tgt_view, proj_view = views(tgt_buf, proj_buf)
    zt_ref[...] = bf16(weight[...] * (part_ref[0] + project(tgt_view, other, tgt_other[...].T)))
    zp_ref[...] = bf16(weight[...] * (part_ref[1] + project(proj_view, other, proj_other[0].T)))


def add_step(gated, gate, parts, *out_refs):
    for kind in range(2):
        own, other = parts[2 * kind : 2 * kind + 2]
        total = f32(own[...]) + f32(other[...])
        out_refs[kind][...] = bf16(gate[...] * total if gated[kind] else total)


def fields_of(parts):
    proj_field = f32(parts[0][...]) + f32(parts[1][...])
    tgt_field = f32(parts[2][...]) + f32(parts[3][...])
    return [(bf16(field), bf16(turned(field))) for field in (tgt_field, proj_field)]


def half_kernel(tgt_buf, proj_buf, parts, energy, amp_ref, send, keep):
    core = lax.axis_index("rep")
    fields = fields_of(parts)
    for kind, view in enumerate(views(tgt_buf, proj_buf)):
        amp = amp_ref[kind]
        own = amp + half_step * (energy[kind] * turned(amp) + expand(view, core, *fields[kind]))
        other = half_step * expand(view, 1 - core, *fields[kind])
        keep[kind, 0] = own
        keep[kind, 1] = other
        send[kind, 0] = bf16(own)
        send[kind, 1] = bf16(other)


def second_kernel(tgt_buf, proj_buf, weight, keep, received, zt_ref, zp_ref, half_ref):
    core = lax.axis_index("rep")
    for kind, view in enumerate(views(tgt_buf, proj_buf)):
        own = keep[kind, 0] + f32(received[kind, 1])
        other = keep[kind, 1] + f32(received[kind, 0])
        half_ref[kind] = own
        total = project(view, core, own) + project(view, 1 - core, other)
        (zt_ref, zp_ref)[kind][...] = bf16(weight[...] * total)


def last_kernel(tgt_buf, proj_buf, parts, energy, amp_ref, half_ref, send, keep):
    core = lax.axis_index("rep")
    fields = fields_of(parts)
    for kind, view in enumerate(views(tgt_buf, proj_buf)):
        send[kind] = bf16((time_step * expand(view, 1 - core, *fields[kind])).T)
        change = energy[kind] * turned(half_ref[kind]) + expand(view, core, *fields[kind])
        keep[kind] = (amp_ref[kind] + time_step * change).T


def add_kernel(keep, received, new_tgt, new_proj):
    new_tgt[...] = keep[0] + f32(received[0])
    new_proj[0] = keep[1] + f32(received[1])


def shards(
    tgt_basis,
    proj_basis,
    quad_weight,
    tgt_energy,
    proj_energy,
    pair_flags,
    tile_counts,
    tgt_amp,
    proj_amp,
):
    points = quad_weight.shape[0]
    rows, two_cols = tgt_amp.shape
    group_rows = proj_amp.shape[1]

    def call(kernel, out_shape, in_specs, scratch_shapes=(), cost=None):
        specs = list(in_specs) + [None] * (len(out_shape) + len(scratch_shapes))

        def with_lists(*refs):
            refs = jax.tree.leaves(refs)
            args = [
                [refs.pop(0) for _ in spec] if isinstance(spec, list) else refs.pop(0) for spec in specs
            ]
            kernel(*args)

        return pl.pallas_call(
            with_lists,
            out_shape=out_shape,
            in_specs=in_specs,
            out_specs=[VMEM] * len(out_shape),
            scratch_shapes=scratch_shapes,
            cost_estimate=cost,
            compiler_params=pltpu.CompilerParams(vmem_limit_bytes=VMEM_LIMIT),
        )

    in_vmem = pltpu.VMEM

    def other_core(block):
        return lax.ppermute(block, "rep", [(0, 1), (1, 0)])

    def steps_along(axis):
        size = lax.axis_size(axis)
        flips = [1 << bit for bit in range(size.bit_length() - 1)]
        return [(axis, [(me, me ^ flip) for me in range(size)]) for flip in flips]

    along_prj, along_tgt = steps_along("prj"), steps_along("tgt")
    zt_steps, zp_steps = along_prj + along_tgt, along_tgt + along_prj
    coefs = in_vmem((two_cols, points), jnp.bfloat16)
    states = in_vmem((2, two_cols, rows), jnp.float32)

    def reduced(zt, zp):
        for step, (zt_step, zp_step) in enumerate(zip(zt_steps, zp_steps)):
            parts = [zt, lax.ppermute(zt, *zt_step), zp, lax.ppermute(zp, *zp_step)]
            if step == len(zt_steps) - 1:
                return parts
            gated = (step + 1 == len(along_prj), step + 1 == len(along_tgt))
            kernel = functools.partial(add_step, gated)
            zt, zp = call(kernel, [coefs, coefs], [VMEM, [VMEM] * 4])(gate, parts)

    tgt_other, proj_other = other_core(tgt_amp), other_core(proj_amp)
    inputs = (
        pair_flags.T,
        tile_counts.T,
        quad_weight,
        tgt_basis,
        proj_basis,
        tgt_energy,
        proj_energy,
        tgt_amp,
        proj_amp,
    )
    tgt_buf, proj_buf, gate, weight, energy, amp, part = call(
        load_kernel,
        [
            in_vmem((2, 2 * rows, points), jnp.bfloat16),
            in_vmem((2, 2, group_rows, points), jnp.bfloat16),
            in_vmem((1, points), jnp.float32),
            in_vmem((1, points), jnp.float32),
            in_vmem((2, 1, rows), jnp.float32),
            states,
            in_vmem((2, two_cols, points), jnp.float32),
        ],
        [HBM] * len(inputs),
        [
            pltpu.SMEM(pair_flags.T.shape, jnp.int32),
            pltpu.SMEM(tile_counts.T.shape, jnp.int32),
            pltpu.VMEM((points,), jnp.float32),
            pltpu.VMEM((rows,), jnp.float32),
            pltpu.VMEM(tgt_amp.shape, jnp.float32),
            pltpu.VMEM(proj_amp.shape, jnp.float32),
            pltpu.SemaphoreType.DMA((11,)),
        ],
        pl.CostEstimate(
            flops=2 * 4 * rows * two_cols * points, bytes_accessed=3 * 1024 * 1024, transcendentals=0
        ),
    )(*[pltpu.with_memory_space_constraint(block, pltpu.HBM) for block in inputs])
    zt, zp = call(first_kernel, [coefs, coefs], [VMEM] * 6)(
        tgt_buf, proj_buf, weight, part, tgt_other, proj_other
    )
    parts = reduced(zt, zp)
    pair = (2, 2, two_cols, rows)
    send, keep = call(
        half_kernel,
        [in_vmem(pair, jnp.bfloat16), in_vmem(pair, jnp.float32)],
        [VMEM, VMEM, [VMEM] * 4, VMEM, VMEM],
    )(tgt_buf, proj_buf, parts, energy, amp)
    zt, zp, half = call(second_kernel, [coefs, coefs, states], [VMEM] * 5)(
        tgt_buf, proj_buf, weight, keep, other_core(send)
    )
    parts = reduced(zt, zp)
    final = (2, rows, two_cols)
    send, keep = call(
        last_kernel,
        [in_vmem(final, jnp.bfloat16), in_vmem(final, jnp.float32)],
        [VMEM, VMEM, [VMEM] * 4, VMEM, VMEM, VMEM],
    )(tgt_buf, proj_buf, parts, energy, amp, half)
    return call(
        add_kernel,
        [
            jax.ShapeDtypeStruct(tgt_amp.shape, jnp.float32),
            jax.ShapeDtypeStruct(proj_amp.shape, jnp.float32),
        ],
        [VMEM] * 2,
    )(keep, other_core(send))


def solution(mesh):
    in_specs = (
        P(None, "tgt", "rep"),
        P(None, None, "prj", "rep"),
        P(("bpar", "rep")),
        P(("tgt", "prj", "rep")),
        P(("tgt", "rep"), "prj"),
        P("bpar", None),
        P("bpar", None),
        P(("bpar", "tgt", "prj", "rep"), None),
        P(("bpar", "tgt", "rep"), "prj", None),
    )
    out_specs = (P(("bpar", "tgt", "prj", "rep"), None), P(("bpar", "tgt", "rep"), "prj", None))

    def step(*args):
        return tuple(shards(*args))

    return jax.shard_map(step, mesh=mesh, in_specs=in_specs, out_specs=out_specs, check_vma=False)
```

time: 76.7 us -> 45.6 us (0.59)
  blocking collectives: 57.1 us -> 0 us
  waiting for transfers between devices: 2.87 us -> 23.4 us
  starting transfers between devices: 6.54 us -> 17 us
  local copies, waits for them, and re-layouts: 4.55 us -> 0 us
    all_gather x4 -> x0, blocking collectives: 57.1 us -> none  [over_tgt(): return lax.all_gather(block, 'tgt', axis=0, tiled=False)]
    ppermute x4 -> x12, waiting for transfers between devices: 0.01 us -> 20.6 us  [reduced(): parts = [zt, lax.ppermute(zt, *zt_step), zp, lax.ppermute(zp, *zp_step)]]
    ppermute x4 -> x12, starting transfers between devices: 5.8 us -> 16.2 us  [reduced(): parts = [zt, lax.ppermute(zt, *zt_step), zp, lax.ppermute(zp, *zp_step)]]
    unnamed x22 -> x0, local copies, waits for them, and re-layouts: 4.55 us -> none
  transfers between devices with their start and end apart: 8 -> 16, of which waited for: 2 -> 14; matrix products, arithmetic and copies ran while one was open for 0% -> 0% of each run, Pallas kernels for 3% -> 4%
where the time goes in v4:
time: 45.6 us; the launch traced here: 45.5 us
  waiting for transfers between devices  23.4 us (51%)
  starting transfers between devices  17 us (37%)
  Pallas kernels  4.36 us (10%)
  between operations  0.72 us (2%)
    ppermute x12, waiting for transfers between devices, reduced(): parts = [zt, lax.ppermute(zt, *zt_step), zp, lax.ppermute(zp, *zp_step)]  20.6 us
    ppermute x12, starting transfers between devices, reduced(): parts = [zt, lax.ppermute(zt, *zt_step), zp, lax.ppermute(zp, *zp_step)]  16.2 us
    ppermute x4, waiting for transfers between devices, other_core(): return lax.ppermute(block, 'rep', [(0, 1), (1, 0)])  2.86 us
    pallas_call x1, Pallas kernels, shards(): call(load_kernel, [in_vmem((2, 2 * rows, points), jnp.bfloat16), in_vmem(...  1.77 us
  transfers between devices with their start and end apart: 16, of which 14 were waited for; matrix products, arithmetic and copies ran while one was open for 0% of the time, Pallas kernels for 4%

profile of v4, /device:TPU:0, one launch (start us, length us, event | category | flops | bytes accessed | tf_op | source)
XLA Modules:
  0.0 45.5 jit_solution(12639036642100435332)
XLA Ops:
  1.2 1.8 %shard_map.104 = (bf16[2,512,256]{2,1,0:T(8,128)(2,1)S(1)}, bf16[2,2,256,256]{3,2,1,0:T(8,128)(2,1)S(1)}, f32[1,256]{1,0:T(1,128)S(1)}, f32[1,256]{1,0:T(1,128)S...) custom-call(s32[2,4]{1,0:T(2,128)} %bitcast.2, s32[2,4]{1,0:T(2,128)} %bitcast.3, ...), custom_call_target="tpu_custom_call" | custom-call | flops 67108864 | bytes 3145728 | tf_op jit(solution)/shard_map/pallas_call | solution.py:248
  3.4 3.0 %collective-permute-start.2 = (bf16[128,256]{1,0:T(8,128)(2,1)S(1)}, bf16[128,256]{1,0:T(8,128)(2,1)S(1)}, u32[]{:S(2)}, u32[]{:S(2)}) collective-permute-start(bf16[128,256]{1,0:T(8,128)(2,1)S(1)} %get-tuple-element.31.refs_1__0_), channel_id=1, source_target_pairs={{0,2},{2,0},{1,3},{3,1},{4,6},{6,4},{5,7},{7,5},{8,10},{10,8},{9,1... | collective-permute-start | bytes 196616 | tf_op jit(solution)/shard_map/ppermute | solution.py:229
  6.3 1.6 %collective-permute-start.3 = (bf16[128,256]{1,0:T(8,128)(2,1)S(1)}, bf16[128,256]{1,0:T(8,128)(2,1)S(1)}, u32[]{:S(2)}, u32[]{:S(2)}) collective-permute-start(bf16[128,256]{1,0:T(8,128)(2,1)S(1)} %get-tuple-element.32.refs_1__2_), channel_id=1, source_target_pairs={{0,4},{4,0},{8,12},{12,8},{1,5},{5,1},{9,13},{13,9},{2,6},{6,2},{1... | collective-permute-start | bytes 196616 | tf_op jit(solution)/shard_map/ppermute | solution.py:229
  7.9 0.8 %collective-permute-done.2.refs_1__1_ = bf16[128,256]{1,0:T(8,128)(2,1)S(1)} collective-permute-done((bf16[128,256]{1,0:T(8,128)(2,1)S(1)}, bf16[128,256]{1,0:T(8,128)(2,1)S(1)}, u32[]{:S(2)}, u32[]{:S(2)}) %collective-permute-start.2) | collective-permute-done | bytes 65568 | tf_op jit(solution)/shard_map/ppermute | solution.py:229
  8.7 1.9 %collective-permute-done.3.refs_1__3_ = bf16[128,256]{1,0:T(8,128)(2,1)S(1)} collective-permute-done((bf16[128,256]{1,0:T(8,128)(2,1)S(1)}, bf16[128,256]{1,0:T(8,128)(2,1)S(1)}, u32[]{:S(2)}, u32[]{:S(2)}) %collective-permute-start.3) | collective-permute-done | bytes 65568 | tf_op jit(solution)/shard_map/ppermute | solution.py:229
  10.7 1.6 %collective-permute-start.4 = (bf16[128,256]{1,0:T(8,128)(2,1)S(1)}, bf16[128,256]{1,0:T(8,128)(2,1)S(1)}, u32[]{:S(2)}, u32[]{:S(2)}) collective-permute-start(bf16[128,256]{1,0:T(8,128)(2,1)S(1)} %get-tuple-element.33.refs_1__0_), channel_id=1, source_target_pairs={{0,4},{4,0},{8,12},{12,8},{1,5},{5,1},{9,13},{13,9},{2,6},{6,2},{1... | collective-permute-start | bytes 196616 | tf_op jit(solution)/shard_map/ppermute | solution.py:229
  12.3 2.6 %collective-permute-start.5 = (bf16[128,256]{1,0:T(8,128)(2,1)S(1)}, bf16[128,256]{1,0:T(8,128)(2,1)S(1)}, u32[]{:S(2)}, u32[]{:S(2)}) collective-permute-start(bf16[128,256]{1,0:T(8,128)(2,1)S(1)} %get-tuple-element.34.refs_1__2_), channel_id=1, source_target_pairs={{0,8},{4,12},{8,0},{12,4},{1,9},{5,13},{9,1},{13,5},{2,10},{6,14},... | collective-permute-start | bytes 196616 | tf_op jit(solution)/shard_map/ppermute | solution.py:229
  14.9 0.6 %collective-permute-done.4.refs_1__1_ = bf16[128,256]{1,0:T(8,128)(2,1)S(1)} collective-permute-done((bf16[128,256]{1,0:T(8,128)(2,1)S(1)}, bf16[128,256]{1,0:T(8,128)(2,1)S(1)}, u32[]{:S(2)}, u32[]{:S(2)}) %collective-permute-start.4) | collective-permute-done | bytes 65568 | tf_op jit(solution)/shard_map/ppermute | solution.py:229
  15.5 2.7 %collective-permute-done.5.refs_1__3_ = bf16[128,256]{1,0:T(8,128)(2,1)S(1)} collective-permute-done((bf16[128,256]{1,0:T(8,128)(2,1)S(1)}, bf16[128,256]{1,0:T(8,128)(2,1)S(1)}, u32[]{:S(2)}, u32[]{:S(2)}) %collective-permute-start.5) | collective-permute-done | bytes 65568 | tf_op jit(solution)/shard_map/ppermute | solution.py:229
  18.2 2.0 %collective-permute-start.6 = (bf16[128,256]{1,0:T(8,128)(2,1)S(1)}, bf16[128,256]{1,0:T(8,128)(2,1)S(1)}, u32[]{:S(2)}, u32[]{:S(2)}) collective-permute-start(bf16[128,256]{1,0:T(8,128)(2,1)S(1)} %get-tuple-element.35.refs_2__0_), channel_id=1, source_target_pairs={{0,8},{4,12},{8,0},{12,4},{1,9},{5,13},{9,1},{13,5},{2,10},{6,14},... | collective-permute-start | bytes 196616 | tf_op jit(solution)/shard_map/ppermute | solution.py:229
  20.7 3.1 %collective-permute-done.6.refs_2__1_ = bf16[128,256]{1,0:T(8,128)(2,1)S(1)} collective-permute-done((bf16[128,256]{1,0:T(8,128)(2,1)S(1)}, bf16[128,256]{1,0:T(8,128)(2,1)S(1)}, u32[]{:S(2)}, u32[]{:S(2)}) %collective-permute-start.6) | collective-permute-done | bytes 65568 | tf_op jit(solution)/shard_map/ppermute | solution.py:229
  23.8 0.7 %collective-permute-done.7.refs_2__3_ = bf16[128,256]{1,0:T(8,128)(2,1)S(1)} collective-permute-done((bf16[128,256]{1,0:T(8,128)(2,1)S(1)}, bf16[128,256]{1,0:T(8,128)(2,1)S(1)}, u32[]{:S(2)}, u32[]{:S(2)}) %collective-permute-start.7) | collective-permute-done | bytes 65568 | tf_op jit(solution)/shard_map/ppermute | solution.py:229
  25.0 1.5 %collective-permute-done.8.refs_4_ = bf16[2,2,128,256]{3,2,1,0:T(8,128)(2,1)S(1)} collective-permute-done((bf16[2,2,128,256]{3,2,1,0:T(8,128)(2,1)S(1)}, bf16[2,2,128,256]{3,2,1,0:T(8,128)(2,1)S(1)}, u32[]{:S(2)}, u32[]{:S(2)}) %collective-permute-start.8) | collective-permute-done | bytes 262176 | tf_op jit(solution)/shard_map/ppermute | solution.py:215
  26.9 0.6 %collective-permute-start.9 = (bf16[128,256]{1,0:T(8,128)(2,1)S(1)}, bf16[128,256]{1,0:T(8,128)(2,1)S(1)}, u32[]{:S(2)}, u32[]{:S(2)}) collective-permute-start(bf16[128,256]{1,0:T(8,128)(2,1)S(1)} %get-tuple-element.41.refs_1__0_), channel_id=1, source_target_pairs={{0,2},{2,0},{1,3},{3,1},{4,6},{6,4},{5,7},{7,5},{8,10},{10,8},{9,1... | collective-permute-start | bytes 196616 | tf_op jit(solution)/shard_map/ppermute | solution.py:229
  27.9 3.3 %collective-permute-done.9.refs_1__1_ = bf16[128,256]{1,0:T(8,128)(2,1)S(1)} collective-permute-done((bf16[128,256]{1,0:T(8,128)(2,1)S(1)}, bf16[128,256]{1,0:T(8,128)(2,1)S(1)}, u32[]{:S(2)}, u32[]{:S(2)}) %collective-permute-start.9) | collective-permute-done | bytes 65568 | tf_op jit(solution)/shard_map/ppermute | solution.py:229
  32.3 0.9 %collective-permute-start.12 = (bf16[128,256]{1,0:T(8,128)(2,1)S(1)}, bf16[128,256]{1,0:T(8,128)(2,1)S(1)}, u32[]{:S(2)}, u32[]{:S(2)}) collective-permute-start(bf16[128,256]{1,0:T(8,128)(2,1)S(1)} %get-tuple-element.44.refs_1__2_), channel_id=1, source_target_pairs={{0,8},{4,12},{8,0},{12,4},{1,9},{5,13},{9,1},{13,5},{2,10},{6,14},... | collective-permute-start | bytes 196616 | tf_op jit(solution)/shard_map/ppermute | solution.py:229
  33.2 2.9 %collective-permute-done.11.refs_1__1_ = bf16[128,256]{1,0:T(8,128)(2,1)S(1)} collective-permute-done((bf16[128,256]{1,0:T(8,128)(2,1)S(1)}, bf16[128,256]{1,0:T(8,128)(2,1)S(1)}, u32[]{:S(2)}, u32[]{:S(2)}) %collective-permute-start.11) | collective-permute-done | bytes 65568 | tf_op jit(solution)/shard_map/ppermute | solution.py:229
  36.1 1.4 %collective-permute-done.12.refs_1__3_ = bf16[128,256]{1,0:T(8,128)(2,1)S(1)} collective-permute-done((bf16[128,256]{1,0:T(8,128)(2,1)S(1)}, bf16[128,256]{1,0:T(8,128)(2,1)S(1)}, u32[]{:S(2)}, u32[]{:S(2)}) %collective-permute-start.12) | collective-permute-done | bytes 65568 | tf_op jit(solution)/shard_map/ppermute | solution.py:229
  37.5 1.0 %collective-permute-start.13 = (bf16[128,256]{1,0:T(8,128)(2,1)S(1)}, bf16[128,256]{1,0:T(8,128)(2,1)S(1)}, u32[]{:S(2)}, u32[]{:S(2)}) collective-permute-start(bf16[128,256]{1,0:T(8,128)(2,1)S(1)} %get-tuple-element.45.refs_2__0_), channel_id=1, source_target_pairs={{0,8},{4,12},{8,0},{12,4},{1,9},{5,13},{9,1},{13,5},{2,10},{6,14},... | collective-permute-start | bytes 196616 | tf_op jit(solution)/shard_map/ppermute | solution.py:229
  38.5 1.5 %collective-permute-start.14 = (bf16[128,256]{1,0:T(8,128)(2,1)S(1)}, bf16[128,256]{1,0:T(8,128)(2,1)S(1)}, u32[]{:S(2)}, u32[]{:S(2)}) collective-permute-start(bf16[128,256]{1,0:T(8,128)(2,1)S(1)} %get-tuple-element.46.refs_2__2_), channel_id=1, source_target_pairs={{0,2},{2,0},{1,3},{3,1},{4,6},{6,4},{5,7},{7,5},{8,10},{10,8},{9,1... | collective-permute-start | bytes 196616 | tf_op jit(solution)/shard_map/ppermute | solution.py:229
  40.0 2.7 %collective-permute-done.13.refs_2__1_ = bf16[128,256]{1,0:T(8,128)(2,1)S(1)} collective-permute-done((bf16[128,256]{1,0:T(8,128)(2,1)S(1)}, bf16[128,256]{1,0:T(8,128)(2,1)S(1)}, u32[]{:S(2)}, u32[]{:S(2)}) %collective-permute-start.13) | collective-permute-done | bytes 65568 | tf_op jit(solution)/shard_map/ppermute | solution.py:229
  42.8 0.6 %shard_map.112 = (bf16[2,256,128]{2,1,0:T(8,128)(2,1)S(1)}, f32[2,256,128]{2,1,0:T(8,128)S(1)}) custom-call(bf16[2,512,256]{2,1,0:T(8,128)(2,1)S(1)} %get-tuple-element.26.refs_0_, bf16[2,2,256,256]{3,2,1,0:T(8,128)(2,1)S(1)} %get-tuple-element.27.refs_1_, bf16[128,256]{1,0:T(8,128)(2,1)S(1)} %get-tuple-element.45.refs_2__0_, ...), custom_call_target="tpu_custom_call" | custom-call | tf_op jit(solution)/shard_map/pallas_call | solution.py:288
  43.4 1.3 %collective-permute-done.15.refs_1_ = bf16[2,256,128]{2,1,0:T(8,128)(2,1)S(1)} collective-permute-done((bf16[2,256,128]{2,1,0:T(8,128)(2,1)S(1)}, bf16[2,256,128]{2,1,0:T(8,128)(2,1)S(1)}, u32[]{:S(2)}, u32[]{:S(2)}) %collective-permute-start.15) | collective-permute-done | bytes 131104 | tf_op jit(solution)/shard_map/ppermute | solution.py:215
  44.8 0.7 %shard_map.113 = (f32[256,128]{1,0:T(8,128)}, f32[1,256,128]{2,1,0:T(8,128)}) custom-call(f32[2,256,128]{2,1,0:T(8,128)S(1)} %get-tuple-element.48.refs_0_, bf16[2,256,128]{2,1,0:T(8,128)(2,1)S(1)} %collective-permute-done.15.refs_1_), custom_call_target="tpu_custom_call" | custom-call | tf_op jit(solution)/shard_map/pallas_call | solution.py:293
  (18 shorter events, 4.1 us)
Async XLA Ops:
  0.6 2.4 %collective-permute-start = (f32[256,128]{1,0:T(8,128)}, f32[256,128]{1,0:T(8,128)S(1)}, u32[]{:S(2)}, u32[]{:S(2)}) collective-permute-start(f32[256,128]{1,0:T(8,128)} %refs_7_.1), channel_id=1, source_target_pairs={{0,1},{1,0},{2,3},{3,2},{4,5},{5,4},{6,7},{7,6},{8,9},{9,8},{10,11... | collective-permute-start | bytes 393224 | tf_op jit(solution)/shard_map/ppermute | solution.py:215
  1.2 1.9 %collective-permute-start.1 = (f32[1,256,128]{2,1,0:T(8,128)}, f32[1,256,128]{2,1,0:T(8,128)S(1)}, u32[]{:S(2)}, u32[]{:S(2)}) collective-permute-start(f32[1,256,128]{2,1,0:T(8,128)} %refs_8_.1), channel_id=1, source_target_pairs={{0,1},{1,0},{2,3},{3,2},{4,5},{5,4},{6,7},{7,6},{8,9},{9,8},{10,11... | collective-permute-start | bytes 393224 | tf_op jit(solution)/shard_map/ppermute | solution.py:215
  3.4 5.3 %collective-permute-start.2 = (bf16[128,256]{1,0:T(8,128)(2,1)S(1)}, bf16[128,256]{1,0:T(8,128)(2,1)S(1)}, u32[]{:S(2)}, u32[]{:S(2)}) collective-permute-start(bf16[128,256]{1,0:T(8,128)(2,1)S(1)} %get-tuple-element.31.refs_1__0_), channel_id=1, source_target_pairs={{0,2},{2,0},{1,3},{3,1},{4,6},{6,4},{5,7},{7,5},{8,10},{10,8},{9,1... | collective-permute-start | bytes 196616 | tf_op jit(solution)/shard_map/ppermute | solution.py:229
  6.3 4.3 %collective-permute-start.3 = (bf16[128,256]{1,0:T(8,128)(2,1)S(1)}, bf16[128,256]{1,0:T(8,128)(2,1)S(1)}, u32[]{:S(2)}, u32[]{:S(2)}) collective-permute-start(bf16[128,256]{1,0:T(8,128)(2,1)S(1)} %get-tuple-element.32.refs_1__2_), channel_id=1, source_target_pairs={{0,4},{4,0},{8,12},{12,8},{1,5},{5,1},{9,13},{13,9},{2,6},{6,2},{1... | collective-permute-start | bytes 196616 | tf_op jit(solution)/shard_map/ppermute | solution.py:229
  10.7 4.8 %collective-permute-start.4 = (bf16[128,256]{1,0:T(8,128)(2,1)S(1)}, bf16[128,256]{1,0:T(8,128)(2,1)S(1)}, u32[]{:S(2)}, u32[]{:S(2)}) collective-permute-start(bf16[128,256]{1,0:T(8,128)(2,1)S(1)} %get-tuple-element.33.refs_1__0_), channel_id=1, source_target_pairs={{0,4},{4,0},{8,12},{12,8},{1,5},{5,1},{9,13},{13,9},{2,6},{6,2},{1... | collective-permute-start | bytes 196616 | tf_op jit(solution)/shard_map/ppermute | solution.py:229
  12.3 5.9 %collective-permute-start.5 = (bf16[128,256]{1,0:T(8,128)(2,1)S(1)}, bf16[128,256]{1,0:T(8,128)(2,1)S(1)}, u32[]{:S(2)}, u32[]{:S(2)}) collective-permute-start(bf16[128,256]{1,0:T(8,128)(2,1)S(1)} %get-tuple-element.34.refs_1__2_), channel_id=1, source_target_pairs={{0,8},{4,12},{8,0},{12,4},{1,9},{5,13},{9,1},{13,5},{2,10},{6,14},... | collective-permute-start | bytes 196616 | tf_op jit(solution)/shard_map/ppermute | solution.py:229
  18.2 5.6 %collective-permute-start.6 = (bf16[128,256]{1,0:T(8,128)(2,1)S(1)}, bf16[128,256]{1,0:T(8,128)(2,1)S(1)}, u32[]{:S(2)}, u32[]{:S(2)}) collective-permute-start(bf16[128,256]{1,0:T(8,128)(2,1)S(1)} %get-tuple-element.35.refs_2__0_), channel_id=1, source_target_pairs={{0,8},{4,12},{8,0},{12,4},{1,9},{5,13},{9,1},{13,5},{2,10},{6,14},... | collective-permute-start | bytes 196616 | tf_op jit(solution)/shard_map/ppermute | solution.py:229
  20.2 4.3 %collective-permute-start.7 = (bf16[128,256]{1,0:T(8,128)(2,1)S(1)}, bf16[128,256]{1,0:T(8,128)(2,1)S(1)}, u32[]{:S(2)}, u32[]{:S(2)}) collective-permute-start(bf16[128,256]{1,0:T(8,128)(2,1)S(1)} %get-tuple-element.36.refs_2__2_), channel_id=1, source_target_pairs={{0,2},{2,0},{1,3},{3,1},{4,6},{6,4},{5,7},{7,5},{8,10},{10,8},{9,1... | collective-permute-start | bytes 196616 | tf_op jit(solution)/shard_map/ppermute | solution.py:229
  24.9 1.6 %collective-permute-start.8 = (bf16[2,2,128,256]{3,2,1,0:T(8,128)(2,1)S(1)}, bf16[2,2,128,256]{3,2,1,0:T(8,128)(2,1)S(1)}, u32[]{:S(2)}, u32[]{:S(2)}) collective-permute-start(bf16[2,2,128,256]{3,2,1,0:T(8,128)(2,1)S(1)} %get-tuple-element.40), channel_id=1, source_target_pairs={{0,1},{1,0},{2,3},{3,2},{4,5},{5,4},{6,7},{7,6},{8,9},{9,8},{10,11... | collective-permute-start | bytes 786440 | tf_op jit(solution)/shard_map/ppermute | solution.py:215
  26.9 4.3 %collective-permute-start.9 = (bf16[128,256]{1,0:T(8,128)(2,1)S(1)}, bf16[128,256]{1,0:T(8,128)(2,1)S(1)}, u32[]{:S(2)}, u32[]{:S(2)}) collective-permute-start(bf16[128,256]{1,0:T(8,128)(2,1)S(1)} %get-tuple-element.41.refs_1__0_), channel_id=1, source_target_pairs={{0,2},{2,0},{1,3},{3,1},{4,6},{6,4},{5,7},{7,5},{8,10},{10,8},{9,1... | collective-permute-start | bytes 196616 | tf_op jit(solution)/shard_map/ppermute | solution.py:229
  27.5 4.3 %collective-permute-start.10 = (bf16[128,256]{1,0:T(8,128)(2,1)S(1)}, bf16[128,256]{1,0:T(8,128)(2,1)S(1)}, u32[]{:S(2)}, u32[]{:S(2)}) collective-permute-start(bf16[128,256]{1,0:T(8,128)(2,1)S(1)} %get-tuple-element.42.refs_1__2_), channel_id=1, source_target_pairs={{0,4},{4,0},{8,12},{12,8},{1,5},{5,1},{9,13},{13,9},{2,6},{6,2},{1... | collective-permute-start | bytes 196616 | tf_op jit(solution)/shard_map/ppermute | solution.py:229
  31.8 4.3 %collective-permute-start.11 = (bf16[128,256]{1,0:T(8,128)(2,1)S(1)}, bf16[128,256]{1,0:T(8,128)(2,1)S(1)}, u32[]{:S(2)}, u32[]{:S(2)}) collective-permute-start(bf16[128,256]{1,0:T(8,128)(2,1)S(1)} %get-tuple-element.43.refs_1__0_), channel_id=1, source_target_pairs={{0,4},{4,0},{8,12},{12,8},{1,5},{5,1},{9,13},{13,9},{2,6},{6,2},{1... | collective-permute-start | bytes 196616 | tf_op jit(solution)/shard_map/ppermute | solution.py:229
  32.3 5.2 %collective-permute-start.12 = (bf16[128,256]{1,0:T(8,128)(2,1)S(1)}, bf16[128,256]{1,0:T(8,128)(2,1)S(1)}, u32[]{:S(2)}, u32[]{:S(2)}) collective-permute-start(bf16[128,256]{1,0:T(8,128)(2,1)S(1)} %get-tuple-element.44.refs_1__2_), channel_id=1, source_target_pairs={{0,8},{4,12},{8,0},{12,4},{1,9},{5,13},{9,1},{13,5},{2,10},{6,14},... | collective-permute-start | bytes 196616 | tf_op jit(solution)/shard_map/ppermute | solution.py:229
  37.5 5.2 %collective-permute-start.13 = (bf16[128,256]{1,0:T(8,128)(2,1)S(1)}, bf16[128,256]{1,0:T(8,128)(2,1)S(1)}, u32[]{:S(2)}, u32[]{:S(2)}) collective-permute-start(bf16[128,256]{1,0:T(8,128)(2,1)S(1)} %get-tuple-element.45.refs_2__0_), channel_id=1, source_target_pairs={{0,8},{4,12},{8,0},{12,4},{1,9},{5,13},{9,1},{13,5},{2,10},{6,14},... | collective-permute-start | bytes 196616 | tf_op jit(solution)/shard_map/ppermute | solution.py:229
  38.5 4.3 %collective-permute-start.14 = (bf16[128,256]{1,0:T(8,128)(2,1)S(1)}, bf16[128,256]{1,0:T(8,128)(2,1)S(1)}, u32[]{:S(2)}, u32[]{:S(2)}) collective-permute-start(bf16[128,256]{1,0:T(8,128)(2,1)S(1)} %get-tuple-element.46.refs_2__2_), channel_id=1, source_target_pairs={{0,2},{2,0},{1,3},{3,1},{4,6},{6,4},{5,7},{7,5},{8,10},{10,8},{9,1... | collective-permute-start | bytes 196616 | tf_op jit(solution)/shard_map/ppermute | solution.py:229
  43.4 1.4 %collective-permute-start.15 = (bf16[2,256,128]{2,1,0:T(8,128)(2,1)S(1)}, bf16[2,256,128]{2,1,0:T(8,128)(2,1)S(1)}, u32[]{:S(2)}, u32[]{:S(2)}) collective-permute-start(bf16[2,256,128]{2,1,0:T(8,128)(2,1)S(1)} %get-tuple-element.49), channel_id=1, source_target_pairs={{0,1},{1,0},{2,3},{3,2},{4,5},{5,4},{6,7},{7,6},{8,9},{9,8},{10,11... | collective-permute-start | bytes 393224 | tf_op jit(solution)/shard_map/ppermute | solution.py:215

commit v5 on v4

--- a/solution.py
+++ b/solution.py
@@ -124,11 +124,9 @@
     zp_ref[...] = bf16(weight[...] * (part_ref[1] + project(proj_view, other, proj_other[0].T)))
 
 
-def add_step(gated, gate, parts, *out_refs):
-    for kind in range(2):
-        own, other = parts[2 * kind : 2 * kind + 2]
-        total = f32(own[...]) + f32(other[...])
-        out_refs[kind][...] = bf16(gate[...] * total if gated[kind] else total)
+def add_step(gated, gate, own, other, out_ref):
+    total = f32(own[...]) + f32(other[...])
+    out_ref[...] = bf16(gate[...] * total if gated else total)
 
 
 def fields_of(parts):
@@ -225,13 +223,15 @@
     states = in_vmem((2, two_cols, rows), jnp.float32)
 
     def reduced(zt, zp):
-        for step, (zt_step, zp_step) in enumerate(zip(zt_steps, zp_steps)):
-            parts = [zt, lax.ppermute(zt, *zt_step), zp, lax.ppermute(zp, *zp_step)]
-            if step == len(zt_steps) - 1:
-                return parts
-            gated = (step + 1 == len(along_prj), step + 1 == len(along_tgt))
-            kernel = functools.partial(add_step, gated)
-            zt, zp = call(kernel, [coefs, coefs], [VMEM, [VMEM] * 4])(gate, parts)
+        parts = []
+        for block, steps, first_steps in ((zt, zt_steps, along_prj), (zp, zp_steps, along_tgt)):
+            for step, (axis, pairs) in enumerate(steps, 1):
+                other = lax.ppermute(block, axis, pairs)
+                if step < len(steps):
+                    kernel = functools.partial(add_step, step == len(first_steps))
+                    (block,) = call(kernel, [coefs], [VMEM] * 3)(gate, block, other)
+            parts += [block, other]
+        return parts
 
     tgt_other, proj_other = other_core(tgt_amp), other_core(proj_amp)
     inputs = (

time: 45.6 us -> 45 us (0.987)
  waiting for transfers between devices: 23.4 us -> 19.6 us
  starting transfers between devices: 17 us -> 20.2 us
    ppermute x12, waiting for transfers between devices: 20.6 us -> 16.7 us  [reduced(): other = lax.ppermute(block, axis, pairs)]
    ppermute x12, starting transfers between devices: 16.2 us -> 19.4 us  [reduced(): other = lax.ppermute(block, axis, pairs)]
  transfers between devices with their start and end apart: 16 -> 16, of which waited for: 14 -> 11; matrix products, arithmetic and copies ran while one was open for 0% -> 0% of each run, Pallas kernels for 4% -> 4%
where the time goes in v5:
time: 45 us; the launch traced here: 44.9 us
  starting transfers between devices  20.2 us (45%)
  waiting for transfers between devices  19.6 us (44%)
  Pallas kernels  4.38 us (10%)
  between operations  0.73 us (2%)
    ppermute x12, starting transfers between devices, reduced(): other = lax.ppermute(block, axis, pairs)  19.4 us
    ppermute x12, waiting for transfers between devices, reduced(): other = lax.ppermute(block, axis, pairs)  16.7 us
    ppermute x4, waiting for transfers between devices, other_core(): return lax.ppermute(block, 'rep', [(0, 1), (1, 0)])  2.86 us
    pallas_call x1, Pallas kernels, shards(): call(load_kernel, [in_vmem((2, 2 * rows, points), jnp.bfloat16), in_vmem(...  1.77 us
  transfers between devices with their start and end apart: 16, of which 11 were waited for; matrix products, arithmetic and copies ran while one was open for 0% of the time, Pallas kernels for 4%

profile of v5, /device:TPU:0, one launch (start us, length us, event | category | flops | bytes accessed | tf_op | source)
XLA Modules:
  0.0 44.9 jit_solution(18161066501886367761)
XLA Ops:
  0.6 0.5 %collective-permute-start = (f32[256,128]{1,0:T(8,128)}, f32[256,128]{1,0:T(8,128)S(1)}, u32[]{:S(2)}, u32[]{:S(2)}) collective-permute-start(f32[256,128]{1,0:T(8,128)} %refs_7_.1), channel_id=1, source_target_pairs={{0,1},{1,0},{2,3},{3,2},{4,5},{5,4},{6,7},{7,6},{8,9},{9,8},{10,11... | collective-permute-start | bytes 393224 | tf_op jit(solution)/shard_map/ppermute | solution.py:213
  1.2 1.8 %shard_map.104 = (bf16[2,512,256]{2,1,0:T(8,128)(2,1)S(1)}, bf16[2,2,256,256]{3,2,1,0:T(8,128)(2,1)S(1)}, f32[1,256]{1,0:T(1,128)S(1)}, f32[1,256]{1,0:T(1,128)S...) custom-call(s32[2,4]{1,0:T(2,128)} %bitcast.2, s32[2,4]{1,0:T(2,128)} %bitcast.3, ...), custom_call_target="tpu_custom_call" | custom-call | flops 67108864 | bytes 3145728 | tf_op jit(solution)/shard_map/pallas_call | solution.py:248
  3.4 3.0 %collective-permute-start.2 = (bf16[128,256]{1,0:T(8,128)(2,1)S(1)}, bf16[128,256]{1,0:T(8,128)(2,1)S(1)}, u32[]{:S(2)}, u32[]{:S(2)}) collective-permute-start(bf16[128,256]{1,0:T(8,128)(2,1)S(1)} %get-tuple-element.23.refs_1_), channel_id=1, source_target_pairs={{0,2},{2,0},{1,3},{3,1},{4,6},{6,4},{5,7},{7,5},{8,10},{10,8},{9,1... | collective-permute-start | bytes 196616 | tf_op jit(solution)/shard_map/ppermute | solution.py:229
  6.3 1.6 %collective-permute-start.5 = (bf16[128,256]{1,0:T(8,128)(2,1)S(1)}, bf16[128,256]{1,0:T(8,128)(2,1)S(1)}, u32[]{:S(2)}, u32[]{:S(2)}) collective-permute-start(bf16[128,256]{1,0:T(8,128)(2,1)S(1)} %get-tuple-element.24.refs_1_), channel_id=1, source_target_pairs={{0,4},{4,0},{8,12},{12,8},{1,5},{5,1},{9,13},{13,9},{2,6},{6,2},{1... | collective-permute-start | bytes 196616 | tf_op jit(solution)/shard_map/ppermute | solution.py:229
  7.9 0.8 %collective-permute-done.2.refs_2_ = bf16[128,256]{1,0:T(8,128)(2,1)S(1)} collective-permute-done((bf16[128,256]{1,0:T(8,128)(2,1)S(1)}, bf16[128,256]{1,0:T(8,128)(2,1)S(1)}, u32[]{:S(2)}, u32[]{:S(2)}) %collective-permute-start.2) | collective-permute-done | bytes 65568 | tf_op jit(solution)/shard_map/ppermute | solution.py:229
  8.7 2.1 %collective-permute-start.3 = (bf16[128,256]{1,0:T(8,128)(2,1)S(1)}, bf16[128,256]{1,0:T(8,128)(2,1)S(1)}, u32[]{:S(2)}, u32[]{:S(2)}) collective-permute-start(bf16[128,256]{1,0:T(8,128)(2,1)S(1)} %shard_map.106.refs_1_), channel_id=1, source_target_pairs={{0,4},{4,0},{8,12},{12,8},{1,5},{5,1},{9,13},{13,9},{2,6},{6,2},{1... | collective-permute-start | bytes 196616 | tf_op jit(solution)/shard_map/ppermute | solution.py:229
  10.8 2.7 %collective-permute-start.6 = (bf16[128,256]{1,0:T(8,128)(2,1)S(1)}, bf16[128,256]{1,0:T(8,128)(2,1)S(1)}, u32[]{:S(2)}, u32[]{:S(2)}) collective-permute-start(bf16[128,256]{1,0:T(8,128)(2,1)S(1)} %shard_map.108.refs_1_), channel_id=1, source_target_pairs={{0,8},{4,12},{8,0},{12,4},{1,9},{5,13},{9,1},{13,5},{2,10},{6,14},... | collective-permute-start | bytes 196616 | tf_op jit(solution)/shard_map/ppermute | solution.py:229
  13.5 2.7 %collective-permute-start.4 = (bf16[128,256]{1,0:T(8,128)(2,1)S(1)}, bf16[128,256]{1,0:T(8,128)(2,1)S(1)}, u32[]{:S(2)}, u32[]{:S(2)}) collective-permute-start(bf16[128,256]{1,0:T(8,128)(2,1)S(1)} %shard_map.107.refs_2__0_), channel_id=1, source_target_pairs={{0,8},{4,12},{8,0},{12,4},{1,9},{5,13},{9,1},{13,5},{2,10},{6,14},... | collective-permute-start | bytes 196616 | tf_op jit(solution)/shard_map/ppermute | solution.py:229
  16.2 1.9 %collective-permute-done.6.refs_2_ = bf16[128,256]{1,0:T(8,128)(2,1)S(1)} collective-permute-done((bf16[128,256]{1,0:T(8,128)(2,1)S(1)}, bf16[128,256]{1,0:T(8,128)(2,1)S(1)}, u32[]{:S(2)}, u32[]{:S(2)}) %collective-permute-start.6) | collective-permute-done | bytes 65568 | tf_op jit(solution)/shard_map/ppermute | solution.py:229
  18.1 1.5 %collective-permute-start.7 = (bf16[128,256]{1,0:T(8,128)(2,1)S(1)}, bf16[128,256]{1,0:T(8,128)(2,1)S(1)}, u32[]{:S(2)}, u32[]{:S(2)}) collective-permute-start(bf16[128,256]{1,0:T(8,128)(2,1)S(1)} %shard_map.109.refs_2__2_), channel_id=1, source_target_pairs={{0,2},{2,0},{1,3},{3,1},{4,6},{6,4},{5,7},{7,5},{8,10},{10,8},{9,1... | collective-permute-start | bytes 196616 | tf_op jit(solution)/shard_map/ppermute | solution.py:229
  19.7 2.8 %collective-permute-done.7.refs_2__3_ = bf16[128,256]{1,0:T(8,128)(2,1)S(1)} collective-permute-done((bf16[128,256]{1,0:T(8,128)(2,1)S(1)}, bf16[128,256]{1,0:T(8,128)(2,1)S(1)}, u32[]{:S(2)}, u32[]{:S(2)}) %collective-permute-start.7) | collective-permute-done | bytes 65568 | tf_op jit(solution)/shard_map/ppermute | solution.py:229
  23.0 1.5 %collective-permute-done.8.refs_4_ = bf16[2,2,128,256]{3,2,1,0:T(8,128)(2,1)S(1)} collective-permute-done((bf16[2,2,128,256]{3,2,1,0:T(8,128)(2,1)S(1)}, bf16[2,2,128,256]{3,2,1,0:T(8,128)(2,1)S(1)}, u32[]{:S(2)}, u32[]{:S(2)}) %collective-permute-start.8) | collective-permute-done | bytes 262176 | tf_op jit(solution)/shard_map/ppermute | solution.py:213
  24.9 1.6 %collective-permute-start.9 = (bf16[128,256]{1,0:T(8,128)(2,1)S(1)}, bf16[128,256]{1,0:T(8,128)(2,1)S(1)}, u32[]{:S(2)}, u32[]{:S(2)}) collective-permute-start(bf16[128,256]{1,0:T(8,128)(2,1)S(1)} %get-tuple-element.29.refs_1_), channel_id=1, source_target_pairs={{0,2},{2,0},{1,3},{3,1},{4,6},{6,4},{5,7},{7,5},{8,10},{10,8},{9,1... | collective-permute-start | bytes 196616 | tf_op jit(solution)/shard_map/ppermute | solution.py:229
  26.4 2.8 %collective-permute-done.9.refs_2_ = bf16[128,256]{1,0:T(8,128)(2,1)S(1)} collective-permute-done((bf16[128,256]{1,0:T(8,128)(2,1)S(1)}, bf16[128,256]{1,0:T(8,128)(2,1)S(1)}, u32[]{:S(2)}, u32[]{:S(2)}) %collective-permute-start.9) | collective-permute-done | bytes 65568 | tf_op jit(solution)/shard_map/ppermute | solution.py:229
  29.5 1.1 %collective-permute-done.12.refs_2_ = bf16[128,256]{1,0:T(8,128)(2,1)S(1)} collective-permute-done((bf16[128,256]{1,0:T(8,128)(2,1)S(1)}, bf16[128,256]{1,0:T(8,128)(2,1)S(1)}, u32[]{:S(2)}, u32[]{:S(2)}) %collective-permute-start.12) | collective-permute-done | bytes 65568 | tf_op jit(solution)/shard_map/ppermute | solution.py:229
  30.7 2.3 %collective-permute-start.13 = (bf16[128,256]{1,0:T(8,128)(2,1)S(1)}, bf16[128,256]{1,0:T(8,128)(2,1)S(1)}, u32[]{:S(2)}, u32[]{:S(2)}) collective-permute-start(bf16[128,256]{1,0:T(8,128)(2,1)S(1)} %shard_map.114.refs_1_), channel_id=1, source_target_pairs={{0,8},{4,12},{8,0},{12,4},{1,9},{5,13},{9,1},{13,5},{2,10},{6,14},... | collective-permute-start | bytes 196616 | tf_op jit(solution)/shard_map/ppermute | solution.py:229
  33.0 0.7 %collective-permute-done.10.refs_2_ = bf16[128,256]{1,0:T(8,128)(2,1)S(1)} collective-permute-done((bf16[128,256]{1,0:T(8,128)(2,1)S(1)}, bf16[128,256]{1,0:T(8,128)(2,1)S(1)}, u32[]{:S(2)}, u32[]{:S(2)}) %collective-permute-start.10) | collective-permute-done | bytes 65568 | tf_op jit(solution)/shard_map/ppermute | solution.py:229
  33.7 1.5 %collective-permute-start.11 = (bf16[128,256]{1,0:T(8,128)(2,1)S(1)}, bf16[128,256]{1,0:T(8,128)(2,1)S(1)}, u32[]{:S(2)}, u32[]{:S(2)}) collective-permute-start(bf16[128,256]{1,0:T(8,128)(2,1)S(1)} %shard_map.113.refs_2__0_), channel_id=1, source_target_pairs={{0,8},{4,12},{8,0},{12,4},{1,9},{5,13},{9,1},{13,5},{2,10},{6,14},... | collective-permute-start | bytes 196616 | tf_op jit(solution)/shard_map/ppermute | solution.py:229
  35.2 2.6 %collective-permute-done.13.refs_2_ = bf16[128,256]{1,0:T(8,128)(2,1)S(1)} collective-permute-done((bf16[128,256]{1,0:T(8,128)(2,1)S(1)}, bf16[128,256]{1,0:T(8,128)(2,1)S(1)}, u32[]{:S(2)}, u32[]{:S(2)}) %collective-permute-start.13) | collective-permute-done | bytes 65568 | tf_op jit(solution)/shard_map/ppermute | solution.py:229
  38.1 1.6 %collective-permute-done.11.refs_2__1_ = bf16[128,256]{1,0:T(8,128)(2,1)S(1)} collective-permute-done((bf16[128,256]{1,0:T(8,128)(2,1)S(1)}, bf16[128,256]{1,0:T(8,128)(2,1)S(1)}, u32[]{:S(2)}, u32[]{:S(2)}) %collective-permute-start.11) | collective-permute-done | bytes 65568 | tf_op jit(solution)/shard_map/ppermute | solution.py:229
  39.7 2.5 %collective-permute-done.14.refs_2__3_ = bf16[128,256]{1,0:T(8,128)(2,1)S(1)} collective-permute-done((bf16[128,256]{1,0:T(8,128)(2,1)S(1)}, bf16[128,256]{1,0:T(8,128)(2,1)S(1)}, u32[]{:S(2)}, u32[]{:S(2)}) %collective-permute-start.14) | collective-permute-done | bytes 65568 | tf_op jit(solution)/shard_map/ppermute | solution.py:229
  42.2 0.6 %shard_map.116 = (bf16[2,256,128]{2,1,0:T(8,128)(2,1)S(1)}, f32[2,256,128]{2,1,0:T(8,128)S(1)}) custom-call(bf16[2,512,256]{2,1,0:T(8,128)(2,1)S(1)} %get-tuple-element.18.refs_0_, bf16[2,2,256,256]{3,2,1,0:T(8,128)(2,1)S(1)} %get-tuple-element.19.refs_1_, bf16[128,256]{1,0:T(8,128)(2,1)S(1)} %shard_map.113.refs_2__0_, ...), custom_call_target="tpu_custom_call" | custom-call | tf_op jit(solution)/shard_map/pallas_call | solution.py:288
  42.8 1.3 %collective-permute-done.15.refs_1_ = bf16[2,256,128]{2,1,0:T(8,128)(2,1)S(1)} collective-permute-done((bf16[2,256,128]{2,1,0:T(8,128)(2,1)S(1)}, bf16[2,256,128]{2,1,0:T(8,128)(2,1)S(1)}, u32[]{:S(2)}, u32[]{:S(2)}) %collective-permute-start.15) | collective-permute-done | bytes 131104 | tf_op jit(solution)/shard_map/ppermute | solution.py:213
  44.2 0.7 %shard_map.117 = (f32[256,128]{1,0:T(8,128)}, f32[1,256,128]{2,1,0:T(8,128)}) custom-call(f32[2,256,128]{2,1,0:T(8,128)S(1)} %get-tuple-element.32.refs_0_, bf16[2,256,128]{2,1,0:T(8,128)(2,1)S(1)} %collective-permute-done.15.refs_1_), custom_call_target="tpu_custom_call" | custom-call | tf_op jit(solution)/shard_map/pallas_call | solution.py:293
  (22 shorter events, 2.1 us)
Async XLA Ops:
  0.6 2.4 %collective-permute-start = (f32[256,128]{1,0:T(8,128)}, f32[256,128]{1,0:T(8,128)S(1)}, u32[]{:S(2)}, u32[]{:S(2)}) collective-permute-start(f32[256,128]{1,0:T(8,128)} %refs_7_.1), channel_id=1, source_target_pairs={{0,1},{1,0},{2,3},{3,2},{4,5},{5,4},{6,7},{7,6},{8,9},{9,8},{10,11... | collective-permute-start | bytes 393224 | tf_op jit(solution)/shard_map/ppermute | solution.py:213
  1.2 1.9 %collective-permute-start.1 = (f32[1,256,128]{2,1,0:T(8,128)}, f32[1,256,128]{2,1,0:T(8,128)S(1)}, u32[]{:S(2)}, u32[]{:S(2)}) collective-permute-start(f32[1,256,128]{2,1,0:T(8,128)} %refs_8_.1), channel_id=1, source_target_pairs={{0,1},{1,0},{2,3},{3,2},{4,5},{5,4},{6,7},{7,6},{8,9},{9,8},{10,11... | collective-permute-start | bytes 393224 | tf_op jit(solution)/shard_map/ppermute | solution.py:213
  3.4 5.3 %collective-permute-start.2 = (bf16[128,256]{1,0:T(8,128)(2,1)S(1)}, bf16[128,256]{1,0:T(8,128)(2,1)S(1)}, u32[]{:S(2)}, u32[]{:S(2)}) collective-permute-start(bf16[128,256]{1,0:T(8,128)(2,1)S(1)} %get-tuple-element.23.refs_1_), channel_id=1, source_target_pairs={{0,2},{2,0},{1,3},{3,1},{4,6},{6,4},{5,7},{7,5},{8,10},{10,8},{9,1... | collective-permute-start | bytes 196616 | tf_op jit(solution)/shard_map/ppermute | solution.py:229
  6.3 4.4 %collective-permute-start.5 = (bf16[128,256]{1,0:T(8,128)(2,1)S(1)}, bf16[128,256]{1,0:T(8,128)(2,1)S(1)}, u32[]{:S(2)}, u32[]{:S(2)}) collective-permute-start(bf16[128,256]{1,0:T(8,128)(2,1)S(1)} %get-tuple-element.24.refs_1_), channel_id=1, source_target_pairs={{0,4},{4,0},{8,12},{12,8},{1,5},{5,1},{9,13},{13,9},{2,6},{6,2},{1... | collective-permute-start | bytes 196616 | tf_op jit(solution)/shard_map/ppermute | solution.py:229
  8.7 4.8 %collective-permute-start.3 = (bf16[128,256]{1,0:T(8,128)(2,1)S(1)}, bf16[128,256]{1,0:T(8,128)(2,1)S(1)}, u32[]{:S(2)}, u32[]{:S(2)}) collective-permute-start(bf16[128,256]{1,0:T(8,128)(2,1)S(1)} %shard_map.106.refs_1_), channel_id=1, source_target_pairs={{0,4},{4,0},{8,12},{12,8},{1,5},{5,1},{9,13},{13,9},{2,6},{6,2},{1... | collective-permute-start | bytes 196616 | tf_op jit(solution)/shard_map/ppermute | solution.py:229
  10.8 7.3 %collective-permute-start.6 = (bf16[128,256]{1,0:T(8,128)(2,1)S(1)}, bf16[128,256]{1,0:T(8,128)(2,1)S(1)}, u32[]{:S(2)}, u32[]{:S(2)}) collective-permute-start(bf16[128,256]{1,0:T(8,128)(2,1)S(1)} %shard_map.108.refs_1_), channel_id=1, source_target_pairs={{0,8},{4,12},{8,0},{12,4},{1,9},{5,13},{9,1},{13,5},{2,10},{6,14},... | collective-permute-start | bytes 196616 | tf_op jit(solution)/shard_map/ppermute | solution.py:229
  13.5 6.2 %collective-permute-start.4 = (bf16[128,256]{1,0:T(8,128)(2,1)S(1)}, bf16[128,256]{1,0:T(8,128)(2,1)S(1)}, u32[]{:S(2)}, u32[]{:S(2)}) collective-permute-start(bf16[128,256]{1,0:T(8,128)(2,1)S(1)} %shard_map.107.refs_2__0_), channel_id=1, source_target_pairs={{0,8},{4,12},{8,0},{12,4},{1,9},{5,13},{9,1},{13,5},{2,10},{6,14},... | collective-permute-start | bytes 196616 | tf_op jit(solution)/shard_map/ppermute | solution.py:229
  18.1 4.3 %collective-permute-start.7 = (bf16[128,256]{1,0:T(8,128)(2,1)S(1)}, bf16[128,256]{1,0:T(8,128)(2,1)S(1)}, u32[]{:S(2)}, u32[]{:S(2)}) collective-permute-start(bf16[128,256]{1,0:T(8,128)(2,1)S(1)} %shard_map.109.refs_2__2_), channel_id=1, source_target_pairs={{0,2},{2,0},{1,3},{3,1},{4,6},{6,4},{5,7},{7,5},{8,10},{10,8},{9,1... | collective-permute-start | bytes 196616 | tf_op jit(solution)/shard_map/ppermute | solution.py:229
  22.9 1.6 %collective-permute-start.8 = (bf16[2,2,128,256]{3,2,1,0:T(8,128)(2,1)S(1)}, bf16[2,2,128,256]{3,2,1,0:T(8,128)(2,1)S(1)}, u32[]{:S(2)}, u32[]{:S(2)}) collective-permute-start(bf16[2,2,128,256]{3,2,1,0:T(8,128)(2,1)S(1)} %get-tuple-element.28), channel_id=1, source_target_pairs={{0,1},{1,0},{2,3},{3,2},{4,5},{5,4},{6,7},{7,6},{8,9},{9,8},{10,11... | collective-permute-start | bytes 786440 | tf_op jit(solution)/shard_map/ppermute | solution.py:213
  24.9 4.3 %collective-permute-start.9 = (bf16[128,256]{1,0:T(8,128)(2,1)S(1)}, bf16[128,256]{1,0:T(8,128)(2,1)S(1)}, u32[]{:S(2)}, u32[]{:S(2)}) collective-permute-start(bf16[128,256]{1,0:T(8,128)(2,1)S(1)} %get-tuple-element.29.refs_1_), channel_id=1, source_target_pairs={{0,2},{2,0},{1,3},{3,1},{4,6},{6,4},{5,7},{7,5},{8,10},{10,8},{9,1... | collective-permute-start | bytes 196616 | tf_op jit(solution)/shard_map/ppermute | solution.py:229
  26.4 4.3 %collective-permute-start.12 = (bf16[128,256]{1,0:T(8,128)(2,1)S(1)}, bf16[128,256]{1,0:T(8,128)(2,1)S(1)}, u32[]{:S(2)}, u32[]{:S(2)}) collective-permute-start(bf16[128,256]{1,0:T(8,128)(2,1)S(1)} %get-tuple-element.30.refs_1_), channel_id=1, source_target_pairs={{0,4},{4,0},{8,12},{12,8},{1,5},{5,1},{9,13},{13,9},{2,6},{6,2},{1... | collective-permute-start | bytes 196616 | tf_op jit(solution)/shard_map/ppermute | solution.py:229
  29.2 4.5 %collective-permute-start.10 = (bf16[128,256]{1,0:T(8,128)(2,1)S(1)}, bf16[128,256]{1,0:T(8,128)(2,1)S(1)}, u32[]{:S(2)}, u32[]{:S(2)}) collective-permute-start(bf16[128,256]{1,0:T(8,128)(2,1)S(1)} %shard_map.112.refs_1_), channel_id=1, source_target_pairs={{0,4},{4,0},{8,12},{12,8},{1,5},{5,1},{9,13},{13,9},{2,6},{6,2},{1... | collective-permute-start | bytes 196616 | tf_op jit(solution)/shard_map/ppermute | solution.py:229
  30.7 7.1 %collective-permute-start.13 = (bf16[128,256]{1,0:T(8,128)(2,1)S(1)}, bf16[128,256]{1,0:T(8,128)(2,1)S(1)}, u32[]{:S(2)}, u32[]{:S(2)}) collective-permute-start(bf16[128,256]{1,0:T(8,128)(2,1)S(1)} %shard_map.114.refs_1_), channel_id=1, source_target_pairs={{0,8},{4,12},{8,0},{12,4},{1,9},{5,13},{9,1},{13,5},{2,10},{6,14},... | collective-permute-start | bytes 196616 | tf_op jit(solution)/shard_map/ppermute | solution.py:229
  33.7 5.9 %collective-permute-start.11 = (bf16[128,256]{1,0:T(8,128)(2,1)S(1)}, bf16[128,256]{1,0:T(8,128)(2,1)S(1)}, u32[]{:S(2)}, u32[]{:S(2)}) collective-permute-start(bf16[128,256]{1,0:T(8,128)(2,1)S(1)} %shard_map.113.refs_2__0_), channel_id=1, source_target_pairs={{0,8},{4,12},{8,0},{12,4},{1,9},{5,13},{9,1},{13,5},{2,10},{6,14},... | collective-permute-start | bytes 196616 | tf_op jit(solution)/shard_map/ppermute | solution.py:229
  37.8 4.3 %collective-permute-start.14 = (bf16[128,256]{1,0:T(8,128)(2,1)S(1)}, bf16[128,256]{1,0:T(8,128)(2,1)S(1)}, u32[]{:S(2)}, u32[]{:S(2)}) collective-permute-start(bf16[128,256]{1,0:T(8,128)(2,1)S(1)} %shard_map.115.refs_2__2_), channel_id=1, source_target_pairs={{0,2},{2,0},{1,3},{3,1},{4,6},{6,4},{5,7},{7,5},{8,10},{10,8},{9,1... | collective-permute-start | bytes 196616 | tf_op jit(solution)/shard_map/ppermute | solution.py:229
  42.8 1.4 %collective-permute-start.15 = (bf16[2,256,128]{2,1,0:T(8,128)(2,1)S(1)}, bf16[2,256,128]{2,1,0:T(8,128)(2,1)S(1)}, u32[]{:S(2)}, u32[]{:S(2)}) collective-permute-start(bf16[2,256,128]{2,1,0:T(8,128)(2,1)S(1)} %get-tuple-element.33), channel_id=1, source_target_pairs={{0,1},{1,0},{2,3},{3,2},{4,5},{5,4},{6,7},{7,6},{8,9},{9,8},{10,11... | collective-permute-start | bytes 393224 | tf_op jit(solution)/shard_map/ppermute | solution.py:213

commit v6 on v5

v6 whole, which is shorter than its diff:
```python
import functools

import jax
import jax.numpy as jnp
from jax import lax
from jax.experimental import pallas as pl
from jax.experimental.pallas import tpu as pltpu
from jax.sharding import PartitionSpec as P

time_step = 0.4
half_step = 0.5 * time_step
VMEM_LIMIT = 8 * 1024 * 1024
DEVICES = ("tgt", "prj", "rep")
HBM = pl.BlockSpec(memory_space=pl.ANY)
VMEM = pl.BlockSpec(memory_space=pltpu.VMEM)


def turned(block):
    half = block.shape[0] // 2
    return jnp.concatenate([block[half:], -block[:half]], axis=0)


def bf16(block):
    return block.astype(jnp.bfloat16)


def f32(block):
    return block.astype(jnp.float32)


def project(basis_real, basis_imag, amp):
    return jnp.dot(bf16(amp), basis_real, preferred_element_type=jnp.float32) + jnp.dot(
        bf16(turned(amp)), basis_imag, preferred_element_type=jnp.float32
    )


def expand(basis_real, basis_imag, field):
    contract = (((1,), (1,)), ((), ()))
    return lax.dot_general(
        turned(field), basis_real, contract, preferred_element_type=jnp.float32
    ) + lax.dot_general(field, basis_imag, contract, preferred_element_type=jnp.float32)


def load_kernel(
    gate_steps,
    flags_hbm,
    counts_hbm,
    weight_hbm,
    tgt_hbm,
    proj_hbm,
    tgt_energy_hbm,
    proj_energy_hbm,
    tgt_own_hbm,
    proj_own_hbm,
    mine,
    send,
    send_own,
    small_send,
    gate,
    weight,
    energy,
    amp_ref,
    flags,
    counts,
    flat_weight,
    flat_energy,
    tgt_own,
    proj_own,
    sems,
):
    core = lax.axis_index("rep")
    tgt_index = lax.axis_index("tgt")
    prj_index = lax.axis_index("prj")
    sources = (tgt_hbm, proj_hbm)
    firsts = (2 * prj_index, 2 * tgt_index)

    def basis_copies(kind):
        same, other = sources[kind], sources[1 - kind]
        return [
            copy
            for part in range(2)
            for copy in (
                pltpu.make_async_copy(
                    other.at[part, pl.ds(firsts[1 - kind], 2)], send.at[part], sems.at[3 * part]
                ),
                pltpu.make_async_copy(
                    same.at[part, pl.ds(firsts[kind], 2)], mine.at[part], sems.at[3 * part + 1]
                ),
                pltpu.make_async_copy(
                    same.at[part, firsts[kind] + 1 - kind], send_own.at[part], sems.at[3 * part + 2]
                ),
            )
        ]

    for kind in range(2):

        @pl.when(core == kind)
        def _():
            for copy in basis_copies(kind):
                copy.start()

    pairs = [
        (flags_hbm, flags),
        (counts_hbm, counts),
        (weight_hbm, flat_weight),
        (tgt_energy_hbm, flat_energy),
        (proj_energy_hbm, energy.at[1]),
        (tgt_own_hbm, tgt_own),
        (proj_own_hbm, proj_own),
    ]
    copies = [pltpu.make_async_copy(src, dst, sems.at[6 + k]) for k, (src, dst) in enumerate(pairs)]
    for copy in copies:
        copy.start()
    for copy in copies:
        copy.wait()
    weight[...] = flat_weight[...][None, :]
    energy[0] = flat_energy[...][None, :]
    small_send[0] = weight[...]
    small_send[1, :, : energy.shape[2]] = energy[1 - core]
    tiles = 2
    width = gate.shape[-1] // tiles
    gate_step = jnp.where(core == 0, *gate_steps)
    for half in range(2):
        for tile in range(tiles):
            live = jnp.logical_and(
                flags[prj_index, tgt_index] > 0, tiles * half + tile < counts[prj_index, tgt_index]
            )
            value = jnp.where(live, 1.0, 0.0).astype(jnp.float32)
            for step in range(gate.shape[0]):
                here = jnp.where(step == gate_step, value, jnp.float32(1.0))
                gate[step, half, :, tile * width : (tile + 1) * width] = jnp.full(
                    (1, width), here, jnp.float32
                )
    amp_ref[0] = tgt_own[...].T
    amp_ref[1] = proj_own[0].T
    for copy in basis_copies(0):
        copy.wait()


def near_kernel(mine, weight, amp_ref, tgt_other, proj_other, near_ref, other_ref):
    core = lax.axis_index("rep")
    other = jnp.where(core == 0, tgt_other[...], proj_other[0]).T
    other_ref[...] = other
    total = project(mine[0, core], mine[1, core], amp_ref[core]) + project(
        mine[0, 1 - core], mine[1, 1 - core], other
    )
    near_ref[...] = bf16(weight[...] * total)


def far_kernel(theirs, small, amp_ref, other_ref, near_ref, z_ref):
    core = lax.axis_index("rep")
    total = project(theirs[0, core], theirs[1, core], amp_ref[core]) + project(
        theirs[0, 1 - core], theirs[1, 1 - core], other_ref[...]
    )
    z_ref[core] = near_ref[...]
    z_ref[1 - core] = bf16(small[0] * total)


def add_kernel(step, gate, own, other, out_ref):
    for half in range(2):
        out_ref[half] = bf16(gate[step, half] * (f32(own[half]) + f32(other[half])))


def second_kernel(
    mine, theirs, field, weight, small, energy, amp_ref, other_ref, z_ref, half_ref
):
    core = lax.axis_index("rep")
    near, far = field[core], field[1 - core]

    def change(segment):
        return expand(mine[0, segment], mine[1, segment], near) + expand(
            theirs[0, segment], theirs[1, segment], far
        )

    amp, other = amp_ref[core], other_ref[...]
    other_energy = small[1, :, : energy.shape[2]]
    amp = amp + half_step * (energy[core] * turned(amp) + change(core))
    other = other + half_step * (other_energy * turned(other) + change(1 - core))
    half_ref[...] = amp
    for basis, half, weights in ((mine, core, weight[...]), (theirs, 1 - core, small[0])):
        total = project(basis[0, core], basis[1, core], amp) + project(
            basis[0, 1 - core], basis[1, 1 - core], other
        )
        z_ref[half] = bf16(weights * total)


def other_half_kernel(sent, own_far, field, energy, amp_ref, half_ref):
    core = lax.axis_index("rep")
    amp = amp_ref[1 - core]
    change = expand(sent[0, core], sent[1, core], field[core]) + expand(
        own_far[0], own_far[1], field[1 - core]
    )
    half_ref[...] = amp + half_step * (energy[1 - core] * turned(amp) + change)


def last_kernel(
    mine,
    theirs,
    sent,
    own_far,
    my_field,
    other_field,
    energy,
    amp_ref,
    my_half,
    other_half,
    new_tgt,
    new_proj,
):
    core = lax.axis_index("rep")
    my_change = expand(mine[0, core], mine[1, core], my_field[core]) + expand(
        theirs[0, core], theirs[1, core], my_field[1 - core]
    )
    other_change = expand(sent[0, core], sent[1, core], other_field[core]) + expand(
        own_far[0], own_far[1], other_field[1 - core]
    )
    my_rate = energy[core] * turned(my_half[...]) + my_change
    other_rate = energy[1 - core] * turned(other_half[...]) + other_change
    my_new = (amp_ref[core] + time_step * my_rate).T
    other_new = (amp_ref[1 - core] + time_step * other_rate).T
    new_tgt[...] = jnp.where(core == 0, my_new, other_new)
    new_proj[0] = jnp.where(core == 0, other_new, my_new)


def shards(
    tgt_basis,
    proj_basis,
    quad_weight,
    tgt_energy,
    proj_energy,
    pair_flags,
    tile_counts,
    tgt_amp,
    proj_amp,
):
    points = quad_weight.shape[0]
    rows, two_cols = tgt_amp.shape
    sizes = [lax.axis_size(axis) for axis in DEVICES]

    def call(kernel, out_shape, in_specs, scratch_shapes=(), cost=None):
        return pl.pallas_call(
            kernel,
            out_shape=out_shape,
            in_specs=in_specs,
            out_specs=[VMEM] * len(out_shape),
            scratch_shapes=scratch_shapes,
            cost_estimate=cost,
            compiler_params=pltpu.CompilerParams(vmem_limit_bytes=VMEM_LIMIT),
        )

    def run(kernel, out_shape, *blocks):
        return call(kernel, out_shape, [VMEM] * len(blocks))(*blocks)

    def other_core(block):
        return lax.ppermute(block, "rep", [(0, 1), (1, 0)])

    n_tgt, n_prj, n_core = sizes
    tgt_flips = [n_prj * n_core << bit for bit in range(n_tgt.bit_length() - 1)]
    prj_flips = [n_core << bit for bit in range(n_prj.bit_length() - 1)]
    steps = list(zip(prj_flips + tgt_flips, tgt_flips + prj_flips))
    gate_steps = (len(prj_flips) - 1, len(tgt_flips) - 1)

    in_vmem = pltpu.VMEM
    basis = in_vmem((2, 2, rows, points), jnp.bfloat16)
    sums = in_vmem((2, two_cols, points), jnp.bfloat16)
    segment = in_vmem((two_cols, rows), jnp.float32)

    def summed(block):
        for step, flips in enumerate(steps):
            pairs = [(me, me ^ flips[me % n_core]) for me in range(n_tgt * n_prj * n_core)]
            other = lax.ppermute(block, DEVICES, pairs)
            (block,) = run(functools.partial(add_kernel, step), [sums], gate, block, other)
        return block

    tgt_other, proj_other = other_core(tgt_amp), other_core(proj_amp)
    inputs = (
        pair_flags.T,
        tile_counts.T,
        quad_weight,
        tgt_basis.reshape(2, -1, rows, points),
        proj_basis,
        tgt_energy,
        proj_energy,
        tgt_amp,
        proj_amp,
    )
    mine, sent, send_own, small_send, gate, weight, energy, amp = call(
        functools.partial(load_kernel, gate_steps),
        [
            basis,
            basis,
            in_vmem((2, rows, points), jnp.bfloat16),
            in_vmem((2, 1, points), jnp.float32),
            in_vmem((len(steps), 2, 1, points), jnp.float32),
            in_vmem((1, points), jnp.float32),
            in_vmem((2, 1, rows), jnp.float32),
            in_vmem((2, two_cols, rows), jnp.float32),
        ],
        [HBM] * len(inputs),
        [
            pltpu.SMEM(pair_flags.T.shape, jnp.int32),
            pltpu.SMEM(tile_counts.T.shape, jnp.int32),
            pltpu.VMEM((points,), jnp.float32),
            pltpu.VMEM((rows,), jnp.float32),
            pltpu.VMEM(tgt_amp.shape, jnp.float32),
            pltpu.VMEM(proj_amp.shape, jnp.float32),
            pltpu.SemaphoreType.DMA((13,)),
        ],
        pl.CostEstimate(flops=0, bytes_accessed=4 * 1024 * 1024, transcendentals=0),
    )(*[pltpu.with_memory_space_constraint(block, pltpu.HBM) for block in inputs])
    theirs, small = other_core(sent), other_core(small_send)
    near, other = run(
        near_kernel,
        [in_vmem((two_cols, points), jnp.bfloat16), segment],
        mine,
        weight,
        amp,
        tgt_other,
        proj_other,
    )
    (z,) = run(far_kernel, [sums], theirs, small, amp, other, near)
    send_own, z = lax.optimization_barrier((send_own, z))
    own_far = other_core(send_own)
    other_field = summed(z)
    z, my_half = run(
        second_kernel,
        [sums, segment],
        mine,
        theirs,
        other_core(other_field),
        weight,
        small,
        energy,
        amp,
        other,
    )
    (other_half,) = run(
        other_half_kernel, [segment], sent, own_far, other_field, energy, amp
    )
    other_field = summed(z)
    return run(
        last_kernel,
        [
            jax.ShapeDtypeStruct(tgt_amp.shape, jnp.float32),
            jax.ShapeDtypeStruct(proj_amp.shape, jnp.float32),
        ],
        mine,
        theirs,
        sent,
        own_far,
        other_core(other_field),
        other_field,
        energy,
        amp,
        my_half,
        other_half,
    )


def solution(mesh):
    in_specs = (
        P(None, "tgt", "rep"),
        P(None, None, "prj", "rep"),
        P(("bpar", "rep")),
        P(("tgt", "prj", "rep")),
        P(("tgt", "rep"), "prj"),
        P("bpar", None),
        P("bpar", None),
        P(("bpar", "tgt", "prj", "rep"), None),
        P(("bpar", "tgt", "rep"), "prj", None),
    )
    out_specs = (P(("bpar", "tgt", "prj", "rep"), None), P(("bpar", "tgt", "rep"), "prj", None))

    def step(*args):
        return tuple(shards(*args))

    return jax.shard_map(step, mesh=mesh, in_specs=in_specs, out_specs=out_specs, check_vma=False)
```

time: 45 us -> 45.9 us (1.020)
  waiting for transfers between devices: 19.6 us -> 24.3 us
  starting transfers between devices: 20.2 us -> 15.8 us
    ppermute x12 -> x6, starting transfers between devices: 19.4 us -> 14.2 us  [summed(): other = lax.ppermute(block, DEVICES, pairs)]
    ppermute x12 -> x6, waiting for transfers between devices: 16.7 us -> 20.6 us  [summed(): other = lax.ppermute(block, DEVICES, pairs)]
    ppermute x4 -> x7, starting transfers between devices: 0.74 us -> 1.58 us  [other_core(): return lax.ppermute(block, 'rep', [(0, 1), (1, 0)])]
    ppermute x4 -> x7, waiting for transfers between devices: 2.86 us -> 3.65 us  [other_core(): return lax.ppermute(block, 'rep', [(0, 1), (1, 0)])]
    pallas_call x14 -> x12, Pallas kernels: 4.38 us -> 4.8 us  [the longest x11 3.13 us: run(): return call(kernel, out_shape, [VMEM] * len(blocks))(*blocks)]
  transfers between devices with their start and end apart: 16 -> 13, of which waited for: 11 -> 10; matrix products, arithmetic and copies ran while one was open for 0% -> 0% of each run, Pallas kernels for 4% -> 1%
where the time goes in v6:
time: 45.9 us; the launch traced here: 45.6 us
  waiting for transfers between devices  24.3 us (53%)
  starting transfers between devices  15.8 us (34%)
  Pallas kernels  4.8 us (10%)
  between operations  0.75 us (2%)
    ppermute x6, waiting for transfers between devices, summed(): other = lax.ppermute(block, DEVICES, pairs)  20.6 us
    ppermute x6, starting transfers between devices, summed(): other = lax.ppermute(block, DEVICES, pairs)  14.2 us
    ppermute x7, waiting for transfers between devices, other_core(): return lax.ppermute(block, 'rep', [(0, 1), (1, 0)])  3.65 us
    pallas_call x11, Pallas kernels, run(): return call(kernel, out_shape, [VMEM] * len(blocks))(*blocks)  3.13 us
    pallas_call x1, Pallas kernels, shards(): call(functools.partial(load_kernel, gate_steps), [basis, basis, in_vmem((...  1.67 us
    ppermute x7, starting transfers between devices, other_core(): return lax.ppermute(block, 'rep', [(0, 1), (1, 0)])  1.58 us
  transfers between devices with their start and end apart: 13, of which 10 were waited for; matrix products, arithmetic and copies ran while one was open for 0% of the time, Pallas kernels for 1%

profile of v6, /device:TPU:0, one launch (start us, length us, event | category | flops | bytes accessed | tf_op | source)
XLA Modules:
  0.0 45.6 jit_solution(7497696049940566937)
XLA Ops:
  0.7 1.7 %shard_map.104 = (bf16[2,2,256,256]{3,2,1,0:T(8,128)(2,1)S(1)}, bf16[2,2,256,256]{3,2,1,0:T(8,128)(2,1)S(1)}, bf16[2,256,256]{2,1,0:T(8,128)(2,1)S(1)}, f32[2,1,...) custom-call(s32[2,4]{1,0:T(2,128)} %bitcast.4, ...), custom_call_target="tpu_custom_call" | custom-call | bytes 4194304 | tf_op jit(solution)/shard_map/pallas_call | solution.py:287
  2.3 0.5 %collective-permute-start = (bf16[2,2,256,256]{3,2,1,0:T(8,128)(2,1)S(1)}, bf16[2,2,256,256]{3,2,1,0:T(8,128)(2,1)S(1)}, u32[]{:S(2)}, u32[]{:S(2)}) collective-permute-start(bf16[2,2,256,256]{3,2,1,0:T(8,128)(2,1)S(1)} %get-tuple-element.17.sent), channel_id=1, source_target_pairs={{0,1},{1,0},{2,3},{3,2},{4,5},{5,4},{6,7},{7,6},{8,9},{9,8},{10,11... | collective-permute-start | bytes 1572872 | tf_op jit(solution)/shard_map/ppermute | solution.py:255
  3.0 0.4 collective-permute-start.3
  3.5 1.1 %collective-permute-done.2.tgt_other = f32[256,128]{1,0:T(8,128)S(1)} collective-permute-done((f32[256,128]{1,0:T(8,128)S(1)}, f32[256,128]{1,0:T(8,128)S(1)}, u32[]{:S(2)}, u32[]{:S(2)}) %collective-permute-start.2) | collective-permute-done | bytes 131104 | tf_op jit(solution)/shard_map/ppermute | solution.py:255
  4.8 0.3 shard_map.105
  5.1 0.3 shard_map.106.own
  5.3 2.9 %collective-permute-start.5 = (bf16[2,128,256]{2,1,0:T(8,128)(2,1)S(1)}, bf16[2,128,256]{2,1,0:T(8,128)(2,1)S(1)}, u32[]{:S(2)}, u32[]{:S(2)}) collective-permute-start(bf16[2,128,256]{2,1,0:T(8,128)(2,1)S(1)} %shard_map.106.own), channel_id=1, source_target_pairs={{0,2},{1,5},{2,0},{3,7},{4,6},{5,1},{6,4},{7,3},{8,10},{9,13},{10,... | collective-permute-start | bytes 393224 | tf_op jit(solution)/shard_map/ppermute | solution.py:271
  8.2 2.9 %collective-permute-done.5.other = bf16[2,128,256]{2,1,0:T(8,128)(2,1)S(1)} collective-permute-done((bf16[2,128,256]{2,1,0:T(8,128)(2,1)S(1)}, bf16[2,128,256]{2,1,0:T(8,128)(2,1)S(1)}, u32[]{:S(2)}, u32[]{:S(2)}) %collective-permute-start.5) | collective-permute-done | bytes 131104 | tf_op jit(solution)/shard_map/ppermute | solution.py:271
  11.2 2.2 %collective-permute-start.6 = (bf16[2,128,256]{2,1,0:T(8,128)(2,1)S(1)}, bf16[2,128,256]{2,1,0:T(8,128)(2,1)S(1)}, u32[]{:S(2)}, u32[]{:S(2)}) collective-permute-start(bf16[2,128,256]{2,1,0:T(8,128)(2,1)S(1)} %shard_map.107.own), channel_id=1, source_target_pairs={{0,4},{1,9},{2,6},{3,11},{4,0},{5,13},{6,2},{7,15},{8,12},{9,1},{1... | collective-permute-start | bytes 393224 | tf_op jit(solution)/shard_map/ppermute | solution.py:271
  13.4 3.7 %collective-permute-done.6.other = bf16[2,128,256]{2,1,0:T(8,128)(2,1)S(1)} collective-permute-done((bf16[2,128,256]{2,1,0:T(8,128)(2,1)S(1)}, bf16[2,128,256]{2,1,0:T(8,128)(2,1)S(1)}, u32[]{:S(2)}, u32[]{:S(2)}) %collective-permute-start.6) | collective-permute-done | bytes 131104 | tf_op jit(solution)/shard_map/ppermute | solution.py:271
  17.2 2.7 %collective-permute-start.7 = (bf16[2,128,256]{2,1,0:T(8,128)(2,1)S(1)}, bf16[2,128,256]{2,1,0:T(8,128)(2,1)S(1)}, u32[]{:S(2)}, u32[]{:S(2)}) collective-permute-start(bf16[2,128,256]{2,1,0:T(8,128)(2,1)S(1)} %shard_map.108.own), channel_id=1, source_target_pairs={{0,8},{1,3},{2,10},{3,1},{4,12},{5,7},{6,14},{7,5},{8,0},{9,11},{1... | collective-permute-start | bytes 393224 | tf_op jit(solution)/shard_map/ppermute | solution.py:271
  19.9 3.2 %collective-permute-done.7.other = bf16[2,128,256]{2,1,0:T(8,128)(2,1)S(1)} collective-permute-done((bf16[2,128,256]{2,1,0:T(8,128)(2,1)S(1)}, bf16[2,128,256]{2,1,0:T(8,128)(2,1)S(1)}, u32[]{:S(2)}, u32[]{:S(2)}) %collective-permute-start.7) | collective-permute-done | bytes 131104 | tf_op jit(solution)/shard_map/ppermute | solution.py:271
  23.2 1.3 %collective-permute-done.8.field = bf16[2,128,256]{2,1,0:T(8,128)(2,1)S(1)} collective-permute-done((bf16[2,128,256]{2,1,0:T(8,128)(2,1)S(1)}, bf16[2,128,256]{2,1,0:T(8,128)(2,1)S(1)}, u32[]{:S(2)}, u32[]{:S(2)}) %collective-permute-start.8) | collective-permute-done | bytes 131104 | tf_op jit(solution)/shard_map/ppermute | solution.py:255
  24.6 0.7 %shard_map.110 = (bf16[2,128,256]{2,1,0:T(8,128)(2,1)S(1)}, f32[128,256]{1,0:T(8,128)S(1)}) custom-call(bf16[2,2,256,256]{3,2,1,0:T(8,128)(2,1)S(1)} %get-tuple-element.16.mine, bf16[2,2,256,256]{3,2,1,0:T(8,128)(2,1)S(1)} %collective-permute-done.theirs, bf16[2,128,256]{2,1,0:T(8,128)(2,1)S(1)} %collective-permute-done.8.field, ...), custom_call_target="tpu_custom_call" | custom-call | tf_op jit(solution)/shard_map/pallas_call | solution.py:252
  25.3 1.6 %collective-permute-start.9 = (bf16[2,128,256]{2,1,0:T(8,128)(2,1)S(1)}, bf16[2,128,256]{2,1,0:T(8,128)(2,1)S(1)}, u32[]{:S(2)}, u32[]{:S(2)}) collective-permute-start(bf16[2,128,256]{2,1,0:T(8,128)(2,1)S(1)} %get-tuple-element.28.own), channel_id=1, source_target_pairs={{0,2},{1,5},{2,0},{3,7},{4,6},{5,1},{6,4},{7,3},{8,10},{9,13},{10,... | collective-permute-start | bytes 393224 | tf_op jit(solution)/shard_map/ppermute | solution.py:271
  26.9 3.5 %collective-permute-done.9.other = bf16[2,128,256]{2,1,0:T(8,128)(2,1)S(1)} collective-permute-done((bf16[2,128,256]{2,1,0:T(8,128)(2,1)S(1)}, bf16[2,128,256]{2,1,0:T(8,128)(2,1)S(1)}, u32[]{:S(2)}, u32[]{:S(2)}) %collective-permute-start.9) | collective-permute-done | bytes 131104 | tf_op jit(solution)/shard_map/ppermute | solution.py:271
  30.4 2.3 %collective-permute-start.10 = (bf16[2,128,256]{2,1,0:T(8,128)(2,1)S(1)}, bf16[2,128,256]{2,1,0:T(8,128)(2,1)S(1)}, u32[]{:S(2)}, u32[]{:S(2)}) collective-permute-start(bf16[2,128,256]{2,1,0:T(8,128)(2,1)S(1)} %shard_map.111.own), channel_id=1, source_target_pairs={{0,4},{1,9},{2,6},{3,11},{4,0},{5,13},{6,2},{7,15},{8,12},{9,1},{1... | collective-permute-start | bytes 393224 | tf_op jit(solution)/shard_map/ppermute | solution.py:271
  32.7 0.3 collective-permute-start.4
  33.0 3.9 %collective-permute-done.10.other = bf16[2,128,256]{2,1,0:T(8,128)(2,1)S(1)} collective-permute-done((bf16[2,128,256]{2,1,0:T(8,128)(2,1)S(1)}, bf16[2,128,256]{2,1,0:T(8,128)(2,1)S(1)}, u32[]{:S(2)}, u32[]{:S(2)}) %collective-permute-start.10) | collective-permute-done | bytes 131104 | tf_op jit(solution)/shard_map/ppermute | solution.py:271
  37.0 2.6 %collective-permute-start.11 = (bf16[2,128,256]{2,1,0:T(8,128)(2,1)S(1)}, bf16[2,128,256]{2,1,0:T(8,128)(2,1)S(1)}, u32[]{:S(2)}, u32[]{:S(2)}) collective-permute-start(bf16[2,128,256]{2,1,0:T(8,128)(2,1)S(1)} %shard_map.112.own), channel_id=1, source_target_pairs={{0,8},{1,3},{2,10},{3,1},{4,12},{5,7},{6,14},{7,5},{8,0},{9,11},{1... | collective-permute-start | bytes 393224 | tf_op jit(solution)/shard_map/ppermute | solution.py:271
  39.6 3.3 %collective-permute-done.11.other = bf16[2,128,256]{2,1,0:T(8,128)(2,1)S(1)} collective-permute-done((bf16[2,128,256]{2,1,0:T(8,128)(2,1)S(1)}, bf16[2,128,256]{2,1,0:T(8,128)(2,1)S(1)}, u32[]{:S(2)}, u32[]{:S(2)}) %collective-permute-start.11) | collective-permute-done | bytes 131104 | tf_op jit(solution)/shard_map/ppermute | solution.py:271
  43.0 0.3 shard_map.114.other_half
  43.3 1.0 %collective-permute-done.12.my_field = bf16[2,128,256]{2,1,0:T(8,128)(2,1)S(1)} collective-permute-done((bf16[2,128,256]{2,1,0:T(8,128)(2,1)S(1)}, bf16[2,128,256]{2,1,0:T(8,128)(2,1)S(1)}, u32[]{:S(2)}, u32[]{:S(2)}) %collective-permute-start.12) | collective-permute-done | bytes 131104 | tf_op jit(solution)/shard_map/ppermute | solution.py:255
  44.3 1.3 %shard_map.115 = (f32[256,128]{1,0:T(8,128)}, f32[1,256,128]{2,1,0:T(8,128)}) custom-call(bf16[2,2,256,256]{3,2,1,0:T(8,128)(2,1)S(1)} %get-tuple-element.16.mine, bf16[2,2,256,256]{3,2,1,0:T(8,128)(2,1)S(1)} %collective-permute-done.theirs, bf16[2,2,256,256]{3,2,1,0:T(8,128)(2,1)S(1)} %get-tuple-element.17.sent, ...), custom_call_target="tpu_custom_call" | custom-call | tf_op jit(solution)/shard_map/pallas_call | solution.py:252
  (18 shorter events, 0.8 us)
Async XLA Ops:
  0.6 2.2 %copy-start = (f32[256,128]{1,0:T(8,128)S(1)}, f32[256,128]{1,0:T(8,128)}, u32[]{:S(2)}) copy-start(f32[256,128]{1,0:T(8,128)} %tgt_own_hbm.1) | copy-start | bytes 393220
  0.6 2.3 %copy-start.1 = (f32[1,256,128]{2,1,0:T(8,128)S(1)}, f32[1,256,128]{2,1,0:T(8,128)}, u32[]{:S(2)}) copy-start(f32[1,256,128]{2,1,0:T(8,128)} %proj_own_hbm.1) | copy-start | bytes 393220
  2.3 2.7 %collective-permute-start = (bf16[2,2,256,256]{3,2,1,0:T(8,128)(2,1)S(1)}, bf16[2,2,256,256]{3,2,1,0:T(8,128)(2,1)S(1)}, u32[]{:S(2)}, u32[]{:S(2)}) collective-permute-start(bf16[2,2,256,256]{3,2,1,0:T(8,128)(2,1)S(1)} %get-tuple-element.17.sent), channel_id=1, source_target_pairs={{0,1},{1,0},{2,3},{3,2},{4,5},{5,4},{6,7},{7,6},{8,9},{9,8},{10,11... | collective-permute-start | bytes 1572872 | tf_op jit(solution)/shard_map/ppermute | solution.py:255
  2.9 1.7 %collective-permute-start.2 = (f32[256,128]{1,0:T(8,128)S(1)}, f32[256,128]{1,0:T(8,128)S(1)}, u32[]{:S(2)}, u32[]{:S(2)}) collective-permute-start(f32[256,128]{1,0:T(8,128)S(1)} %copy-done), channel_id=1, source_target_pairs={{0,1},{1,0},{2,3},{3,2},{4,5},{5,4},{6,7},{7,6},{8,9},{9,8},{10,11... | collective-permute-start | bytes 393224 | tf_op jit(solution)/shard_map/ppermute | solution.py:255
  3.0 1.8 %collective-permute-start.3 = (f32[1,256,128]{2,1,0:T(8,128)S(1)}, f32[1,256,128]{2,1,0:T(8,128)S(1)}, u32[]{:S(2)}, u32[]{:S(2)}) collective-permute-start(f32[1,256,128]{2,1,0:T(8,128)S(1)} %copy-done.1), channel_id=1, source_target_pairs={{0,1},{1,0},{2,3},{3,2},{4,5},{5,4},{6,7},{7,6},{8,9},{9,8},{10,11... | collective-permute-start | bytes 393224 | tf_op jit(solution)/shard_map/ppermute | solution.py:255
  3.4 1.7 %collective-permute-start.1 = (f32[2,1,256]{2,1,0:T(1,128)S(1)}, f32[2,1,256]{2,1,0:T(1,128)S(1)}, u32[]{:S(2)}, u32[]{:S(2)}) collective-permute-start(f32[2,1,256]{2,1,0:T(1,128)S(1)} %get-tuple-element.19), channel_id=1, source_target_pairs={{0,1},{1,0},{2,3},{3,2},{4,5},{5,4},{6,7},{7,6},{8,9},{9,8},{10,11... | collective-permute-start | bytes 6152 | tf_op jit(solution)/shard_map/ppermute | solution.py:255
  5.3 5.8 %collective-permute-start.5 = (bf16[2,128,256]{2,1,0:T(8,128)(2,1)S(1)}, bf16[2,128,256]{2,1,0:T(8,128)(2,1)S(1)}, u32[]{:S(2)}, u32[]{:S(2)}) collective-permute-start(bf16[2,128,256]{2,1,0:T(8,128)(2,1)S(1)} %shard_map.106.own), channel_id=1, source_target_pairs={{0,2},{1,5},{2,0},{3,7},{4,6},{5,1},{6,4},{7,3},{8,10},{9,13},{10,... | collective-permute-start | bytes 393224 | tf_op jit(solution)/shard_map/ppermute | solution.py:271
  11.2 5.9 %collective-permute-start.6 = (bf16[2,128,256]{2,1,0:T(8,128)(2,1)S(1)}, bf16[2,128,256]{2,1,0:T(8,128)(2,1)S(1)}, u32[]{:S(2)}, u32[]{:S(2)}) collective-permute-start(bf16[2,128,256]{2,1,0:T(8,128)(2,1)S(1)} %shard_map.107.own), channel_id=1, source_target_pairs={{0,4},{1,9},{2,6},{3,11},{4,0},{5,13},{6,2},{7,15},{8,12},{9,1},{1... | collective-permute-start | bytes 393224 | tf_op jit(solution)/shard_map/ppermute | solution.py:271
  17.2 5.9 %collective-permute-start.7 = (bf16[2,128,256]{2,1,0:T(8,128)(2,1)S(1)}, bf16[2,128,256]{2,1,0:T(8,128)(2,1)S(1)}, u32[]{:S(2)}, u32[]{:S(2)}) collective-permute-start(bf16[2,128,256]{2,1,0:T(8,128)(2,1)S(1)} %shard_map.108.own), channel_id=1, source_target_pairs={{0,8},{1,3},{2,10},{3,1},{4,12},{5,7},{6,14},{7,5},{8,0},{9,11},{1... | collective-permute-start | bytes 393224 | tf_op jit(solution)/shard_map/ppermute | solution.py:271
  23.2 1.4 %collective-permute-start.8 = (bf16[2,128,256]{2,1,0:T(8,128)(2,1)S(1)}, bf16[2,128,256]{2,1,0:T(8,128)(2,1)S(1)}, u32[]{:S(2)}, u32[]{:S(2)}) collective-permute-start(bf16[2,128,256]{2,1,0:T(8,128)(2,1)S(1)} %shard_map.109.field), channel_id=1, source_target_pairs={{0,1},{1,0},{2,3},{3,2},{4,5},{5,4},{6,7},{7,6},{8,9},{9,8},{10,11... | collective-permute-start | bytes 393224 | tf_op jit(solution)/shard_map/ppermute | solution.py:255
  25.3 5.0 %collective-permute-start.9 = (bf16[2,128,256]{2,1,0:T(8,128)(2,1)S(1)}, bf16[2,128,256]{2,1,0:T(8,128)(2,1)S(1)}, u32[]{:S(2)}, u32[]{:S(2)}) collective-permute-start(bf16[2,128,256]{2,1,0:T(8,128)(2,1)S(1)} %get-tuple-element.28.own), channel_id=1, source_target_pairs={{0,2},{1,5},{2,0},{3,7},{4,6},{5,1},{6,4},{7,3},{8,10},{9,13},{10,... | collective-permute-start | bytes 393224 | tf_op jit(solution)/shard_map/ppermute | solution.py:271
  30.4 6.5 %collective-permute-start.10 = (bf16[2,128,256]{2,1,0:T(8,128)(2,1)S(1)}, bf16[2,128,256]{2,1,0:T(8,128)(2,1)S(1)}, u32[]{:S(2)}, u32[]{:S(2)}) collective-permute-start(bf16[2,128,256]{2,1,0:T(8,128)(2,1)S(1)} %shard_map.111.own), channel_id=1, source_target_pairs={{0,4},{1,9},{2,6},{3,11},{4,0},{5,13},{6,2},{7,15},{8,12},{9,1},{1... | collective-permute-start | bytes 393224 | tf_op jit(solution)/shard_map/ppermute | solution.py:271
  32.7 10.4 %collective-permute-start.4 = (bf16[2,256,256]{2,1,0:T(8,128)(2,1)S(1)}, bf16[2,256,256]{2,1,0:T(8,128)(2,1)S(1)}, u32[]{:S(2)}, u32[]{:S(2)}) collective-permute-start(bf16[2,256,256]{2,1,0:T(8,128)(2,1)S(1)} %get-tuple-element.24), channel_id=1, source_target_pairs={{0,1},{1,0},{2,3},{3,2},{4,5},{5,4},{6,7},{7,6},{8,9},{9,8},{10,11... | collective-permute-start | bytes 786440 | tf_op jit(solution)/shard_map/ppermute | solution.py:255
  37.0 5.9 %collective-permute-start.11 = (bf16[2,128,256]{2,1,0:T(8,128)(2,1)S(1)}, bf16[2,128,256]{2,1,0:T(8,128)(2,1)S(1)}, u32[]{:S(2)}, u32[]{:S(2)}) collective-permute-start(bf16[2,128,256]{2,1,0:T(8,128)(2,1)S(1)} %shard_map.112.own), channel_id=1, source_target_pairs={{0,8},{1,3},{2,10},{3,1},{4,12},{5,7},{6,14},{7,5},{8,0},{9,11},{1... | collective-permute-start | bytes 393224 | tf_op jit(solution)/shard_map/ppermute | solution.py:271
  42.9 1.4 %collective-permute-start.12 = (bf16[2,128,256]{2,1,0:T(8,128)(2,1)S(1)}, bf16[2,128,256]{2,1,0:T(8,128)(2,1)S(1)}, u32[]{:S(2)}, u32[]{:S(2)}) collective-permute-start(bf16[2,128,256]{2,1,0:T(8,128)(2,1)S(1)} %shard_map.113.other_field), channel_id=1, source_target_pairs={{0,1},{1,0},{2,3},{3,2},{4,5},{5,4},{6,7},{7,6},{8,9},{9,8},{10,11... | collective-permute-start | bytes 393224 | tf_op jit(solution)/shard_map/ppermute | solution.py:255

commit v7 on v6

--- a/solution.py
+++ b/solution.py
@@ -55,6 +55,7 @@
     mine,
     send,
     send_own,
+    amp_send,
     small_send,
     gate,
     weight,
@@ -113,17 +114,17 @@
         copy.start()
     for copy in copies:
         copy.wait()
-    weight[...] = flat_weight[...][None, :]
+    weight[0] = flat_weight[...][None, :]
     energy[0] = flat_energy[...][None, :]
-    small_send[0] = weight[...]
+    small_send[0] = weight[0]
     small_send[1, :, : energy.shape[2]] = energy[1 - core]
     tiles = 2
     width = gate.shape[-1] // tiles
     gate_step = jnp.where(core == 0, *gate_steps)
-    for half in range(2):
+    for half, home in enumerate((core, 1 - core)):
         for tile in range(tiles):
             live = jnp.logical_and(
-                flags[prj_index, tgt_index] > 0, tiles * half + tile < counts[prj_index, tgt_index]
+                flags[prj_index, tgt_index] > 0, tiles * home + tile < counts[prj_index, tgt_index]
             )
             value = jnp.where(live, 1.0, 0.0).astype(jnp.float32)
             for step in range(gate.shape[0]):
@@ -133,43 +134,31 @@
                 )
     amp_ref[0] = tgt_own[...].T
     amp_ref[1] = proj_own[0].T
+    amp_send[...] = amp_ref[1 - core]
     for copy in basis_copies(0):
         copy.wait()
 
 
-def near_kernel(mine, weight, amp_ref, tgt_other, proj_other, near_ref, other_ref):
-    core = lax.axis_index("rep")
-    other = jnp.where(core == 0, tgt_other[...], proj_other[0]).T
-    other_ref[...] = other
-    total = project(mine[0, core], mine[1, core], amp_ref[core]) + project(
-        mine[0, 1 - core], mine[1, 1 - core], other
-    )
-    near_ref[...] = bf16(weight[...] * total)
-
-
-def far_kernel(theirs, small, amp_ref, other_ref, near_ref, z_ref):
-    core = lax.axis_index("rep")
-    total = project(theirs[0, core], theirs[1, core], amp_ref[core]) + project(
-        theirs[0, 1 - core], theirs[1, 1 - core], other_ref[...]
-    )
-    z_ref[core] = near_ref[...]
-    z_ref[1 - core] = bf16(small[0] * total)
-
-
-def add_kernel(step, gate, own, other, out_ref):
-    for half in range(2):
-        out_ref[half] = bf16(gate[step, half] * (f32(own[half]) + f32(other[half])))
+def first_kernel(basis, weight, amp_ref, other_ref, out_ref):
+    core = lax.axis_index("rep")
+    total = project(basis[0, core], basis[1, core], amp_ref[core]) + project(
+        basis[0, 1 - core], basis[1, 1 - core], other_ref[...]
+    )
+    out_ref[...] = bf16(weight[0] * total)
+
+
+def add_kernel(step, half, gate, own, other, out_ref):
+    out_ref[...] = bf16(gate[step, half] * (f32(own[...]) + f32(other[...])))
 
 
 def second_kernel(
-    mine, theirs, field, weight, small, energy, amp_ref, other_ref, z_ref, half_ref
+    mine, theirs, near, far, weight, small, energy, amp_ref, other_ref, near_ref, far_ref, half_ref
 ):
     core = lax.axis_index("rep")
-    near, far = field[core], field[1 - core]
 
     def change(segment):
-        return expand(mine[0, segment], mine[1, segment], near) + expand(
-            theirs[0, segment], theirs[1, segment], far
+        return expand(mine[0, segment], mine[1, segment], near[...]) + expand(
+            theirs[0, segment], theirs[1, segment], far[...]
         )
 
     amp, other = amp_ref[core], other_ref[...]
@@ -177,19 +166,17 @@
     amp = amp + half_step * (energy[core] * turned(amp) + change(core))
     other = other + half_step * (other_energy * turned(other) + change(1 - core))
     half_ref[...] = amp
-    for basis, half, weights in ((mine, core, weight[...]), (theirs, 1 - core, small[0])):
+    for basis, out_ref, weights in ((mine, near_ref, weight[0]), (theirs, far_ref, small[0])):
         total = project(basis[0, core], basis[1, core], amp) + project(
             basis[0, 1 - core], basis[1, 1 - core], other
         )
-        z_ref[half] = bf16(weights * total)
-
-
-def other_half_kernel(sent, own_far, field, energy, amp_ref, half_ref):
+        out_ref[...] = bf16(weights * total)
+
+
+def other_half_kernel(sent, own_far, near, far, energy, amp_ref, half_ref):
     core = lax.axis_index("rep")
     amp = amp_ref[1 - core]
-    change = expand(sent[0, core], sent[1, core], field[core]) + expand(
-        own_far[0], own_far[1], field[1 - core]
-    )
+    change = expand(sent[0, core], sent[1, core], near[...]) + expand(own_far[0], own_far[1], far[...])
     half_ref[...] = amp + half_step * (energy[1 - core] * turned(amp) + change)
 
 
@@ -198,8 +185,10 @@
     theirs,
     sent,
     own_far,
-    my_field,
-    other_field,
+    my_near,
+    my_far,
+    other_near,
+    other_far,
     energy,
     amp_ref,
     my_half,
@@ -208,11 +197,11 @@
     new_proj,
 ):
     core = lax.axis_index("rep")
-    my_change = expand(mine[0, core], mine[1, core], my_field[core]) + expand(
-        theirs[0, core], theirs[1, core], my_field[1 - core]
-    )
-    other_change = expand(sent[0, core], sent[1, core], other_field[core]) + expand(
-        own_far[0], own_far[1], other_field[1 - core]
+    my_change = expand(mine[0, core], mine[1, core], my_near[...]) + expand(
+        theirs[0, core], theirs[1, core], my_far[...]
+    )
+    other_change = expand(sent[0, core], sent[1, core], other_near[...]) + expand(
+        own_far[0], own_far[1], other_far[...]
     )
     my_rate = energy[core] * turned(my_half[...]) + my_change
     other_rate = energy[1 - core] * turned(other_half[...]) + other_change
@@ -262,17 +251,22 @@
 
     in_vmem = pltpu.VMEM
     basis = in_vmem((2, 2, rows, points), jnp.bfloat16)
-    sums = in_vmem((2, two_cols, points), jnp.bfloat16)
+    sums = in_vmem((two_cols, points), jnp.bfloat16)
     segment = in_vmem((two_cols, rows), jnp.float32)
 
-    def summed(block):
-        for step, flips in enumerate(steps):
-            pairs = [(me, me ^ flips[me % n_core]) for me in range(n_tgt * n_prj * n_core)]
-            other = lax.ppermute(block, DEVICES, pairs)
-            (block,) = run(functools.partial(add_kernel, step), [sums], gate, block, other)
-        return block
-
-    tgt_other, proj_other = other_core(tgt_amp), other_core(proj_amp)
+    def summed(*halves):
+        totals = []
+        for half, block in enumerate(halves):
+            for step, flips in enumerate(steps):
+                pairs = [(me, me ^ flips[me % n_core]) for me in range(n_tgt * n_prj * n_core)]
+                other = lax.ppermute(block, DEVICES, pairs)
+                (block,) = run(functools.partial(add_kernel, step, half), [sums], gate, block, other)
+            totals.append(block)
+        return totals
+
+    def swapped(near, far):
+        return other_core(far), other_core(near)
+
     inputs = (
         pair_flags.T,
         tile_counts.T,
@@ -284,15 +278,16 @@
         tgt_amp,
         proj_amp,
     )
-    mine, sent, send_own, small_send, gate, weight, energy, amp = call(
+    mine, sent, send_own, amp_send, small_send, gate, weight, energy, amp = call(
         functools.partial(load_kernel, gate_steps),
         [
             basis,
             basis,
             in_vmem((2, rows, points), jnp.bfloat16),
+            segment,
             in_vmem((2, 1, points), jnp.float32),
             in_vmem((len(steps), 2, 1, points), jnp.float32),
-            in_vmem((1, points), jnp.float32),
+            in_vmem((1, 1, points), jnp.float32),
             in_vmem((2, 1, rows), jnp.float32),
             in_vmem((2, two_cols, rows), jnp.float32),
         ],
@@ -308,36 +303,26 @@
         ],
         pl.CostEstimate(flops=0, bytes_accessed=4 * 1024 * 1024, transcendentals=0),
     )(*[pltpu.with_memory_space_constraint(block, pltpu.HBM) for block in inputs])
-    theirs, small = other_core(sent), other_core(small_send)
-    near, other = run(
-        near_kernel,
-        [in_vmem((two_cols, points), jnp.bfloat16), segment],
-        mine,
-        weight,
-        amp,
-        tgt_other,
-        proj_other,
-    )
-    (z,) = run(far_kernel, [sums], theirs, small, amp, other, near)
-    send_own, z = lax.optimization_barrier((send_own, z))
+    other, small, theirs = other_core(amp_send), other_core(small_send), other_core(sent)
+    (near,) = run(first_kernel, [sums], mine, weight, amp, other)
+    (far,) = run(first_kernel, [sums], theirs, small, amp, other)
+    send_own, far = lax.optimization_barrier((send_own, far))
     own_far = other_core(send_own)
-    other_field = summed(z)
-    z, my_half = run(
+    fields = summed(near, far)
+    near, far, my_half = run(
         second_kernel,
-        [sums, segment],
+        [sums, sums, segment],
         mine,
         theirs,
-        other_core(other_field),
+        *swapped(*fields),
         weight,
         small,
         energy,
         amp,
         other,
     )
-    (other_half,) = run(
-        other_half_kernel, [segment], sent, own_far, other_field, energy, amp
-    )
-    other_field = summed(z)
+    (other_half,) = run(other_half_kernel, [segment], sent, own_far, *fields, energy, amp)
+    fields = summed(near, far)
     return run(
         last_kernel,
         [
@@ -348,8 +333,8 @@
         theirs,
         sent,
         own_far,
-        other_core(other_field),
-        other_field,
+        *swapped(*fields),
+        *fields,
         energy,
         amp,
         my_half,

time: 45.9 us -> 44.4 us (0.967)
  waiting for transfers between devices: 24.3 us -> 16.5 us
  starting transfers between devices: 15.8 us -> 22.2 us
    ppermute x6 -> x12, waiting for transfers between devices: 20.6 us -> 13.2 us  [summed(): other = lax.ppermute(block, DEVICES, pairs)]
    ppermute x6 -> x12, starting transfers between devices: 14.2 us -> 20.9 us  [summed(): other = lax.ppermute(block, DEVICES, pairs)]
    ppermute x7 -> x8, waiting for transfers between devices: 3.65 us -> 3.35 us  [other_core(): return lax.ppermute(block, 'rep', [(0, 1), (1, 0)])]
    ppermute x7 -> x8, starting transfers between devices: 1.58 us -> 1.3 us  [other_core(): return lax.ppermute(block, 'rep', [(0, 1), (1, 0)])]
    pallas_call x11 -> x17, Pallas kernels: 3.13 us -> 3.14 us  [run(): return call(kernel, out_shape, [VMEM] * len(blocks))(*blocks)]
  transfers between devices with their start and end apart: 13 -> 20, of which waited for: 10 -> 12; matrix products, arithmetic and copies ran while one was open for 0% -> 0% of each run, Pallas kernels for 1% -> 2%
where the time goes in v7:
time: 44.4 us; the launch traced here: 44.3 us
  starting transfers between devices  22.2 us (50%)
  waiting for transfers between devices  16.5 us (37%)
  Pallas kernels  4.81 us (11%)
  between operations  0.78 us (2%)
    ppermute x12, starting transfers between devices, summed(): other = lax.ppermute(block, DEVICES, pairs)  20.9 us
    ppermute x12, waiting for transfers between devices, summed(): other = lax.ppermute(block, DEVICES, pairs)  13.2 us
    ppermute x8, waiting for transfers between devices, other_core(): return lax.ppermute(block, 'rep', [(0, 1), (1, 0)])  3.35 us
    pallas_call x17, Pallas kernels, run(): return call(kernel, out_shape, [VMEM] * len(blocks))(*blocks)  3.14 us
    pallas_call x1, Pallas kernels, shards(): call(functools.partial(load_kernel, gate_steps), [basis, basis, in_vmem((...  1.68 us
    ppermute x8, starting transfers between devices, other_core(): return lax.ppermute(block, 'rep', [(0, 1), (1, 0)])  1.3 us
  transfers between devices with their start and end apart: 20, of which 12 were waited for; matrix products, arithmetic and copies ran while one was open for 0% of the time, Pallas kernels for 2%

profile of v7, /device:TPU:0, one launch (start us, length us, event | category | flops | bytes accessed | tf_op | source)
XLA Modules:
  0.0 44.3 jit_solution(270758336248712665)
XLA Ops:
  0.6 1.7 %shard_map.104 = (bf16[2,2,256,256]{3,2,1,0:T(8,128)(2,1)S(1)}, bf16[2,2,256,256]{3,2,1,0:T(8,128)(2,1)S(1)}, bf16[2,256,256]{2,1,0:T(8,128)(2,1)S(1)}, f32[128,...) custom-call(s32[2,4]{1,0:T(2,128)} %bitcast.4, ...), custom_call_target="tpu_custom_call" | custom-call | bytes 4194304 | tf_op jit(solution)/shard_map/pallas_call | solution.py:281
  3.3 1.2 %collective-permute-done.2.other_ref = f32[128,256]{1,0:T(8,128)S(1)} collective-permute-done((f32[128,256]{1,0:T(8,128)S(1)}, f32[128,256]{1,0:T(8,128)S(1)}, u32[]{:S(2)}, u32[]{:S(2)}) %collective-permute-start.2) | collective-permute-done | bytes 131104 | tf_op jit(solution)/shard_map/ppermute | solution.py:244
  4.8 2.9 %collective-permute-start.8 = (bf16[128,256]{1,0:T(8,128)(2,1)S(1)}, bf16[128,256]{1,0:T(8,128)(2,1)S(1)}, u32[]{:S(2)}, u32[]{:S(2)}) collective-permute-start(bf16[128,256]{1,0:T(8,128)(2,1)S(1)} %shard_map.109.own), channel_id=1, source_target_pairs={{0,2},{1,5},{2,0},{3,7},{4,6},{5,1},{6,4},{7,3},{8,10},{9,13},{10,... | collective-permute-start | bytes 196616 | tf_op jit(solution)/shard_map/ppermute | solution.py:262
  8.1 1.9 %collective-permute-done.8.other = bf16[128,256]{1,0:T(8,128)(2,1)S(1)} collective-permute-done((bf16[128,256]{1,0:T(8,128)(2,1)S(1)}, bf16[128,256]{1,0:T(8,128)(2,1)S(1)}, u32[]{:S(2)}, u32[]{:S(2)}) %collective-permute-start.8) | collective-permute-done | bytes 65568 | tf_op jit(solution)/shard_map/ppermute | solution.py:262
  10.0 2.2 %collective-permute-start.9 = (bf16[128,256]{1,0:T(8,128)(2,1)S(1)}, bf16[128,256]{1,0:T(8,128)(2,1)S(1)}, u32[]{:S(2)}, u32[]{:S(2)}) collective-permute-start(bf16[128,256]{1,0:T(8,128)(2,1)S(1)} %shard_map.110.own), channel_id=1, source_target_pairs={{0,4},{1,9},{2,6},{3,11},{4,0},{5,13},{6,2},{7,15},{8,12},{9,1},{1... | collective-permute-start | bytes 196616 | tf_op jit(solution)/shard_map/ppermute | solution.py:262
  12.3 1.6 %collective-permute-start.5 = (bf16[128,256]{1,0:T(8,128)(2,1)S(1)}, bf16[128,256]{1,0:T(8,128)(2,1)S(1)}, u32[]{:S(2)}, u32[]{:S(2)}) collective-permute-start(bf16[128,256]{1,0:T(8,128)(2,1)S(1)} %shard_map.106.own), channel_id=1, source_target_pairs={{0,4},{1,9},{2,6},{3,11},{4,0},{5,13},{6,2},{7,15},{8,12},{9,1},{1... | collective-permute-start | bytes 196616 | tf_op jit(solution)/shard_map/ppermute | solution.py:262
  14.0 0.6 %collective-permute-done.9.other = bf16[128,256]{1,0:T(8,128)(2,1)S(1)} collective-permute-done((bf16[128,256]{1,0:T(8,128)(2,1)S(1)}, bf16[128,256]{1,0:T(8,128)(2,1)S(1)}, u32[]{:S(2)}, u32[]{:S(2)}) %collective-permute-start.9) | collective-permute-done | bytes 65568 | tf_op jit(solution)/shard_map/ppermute | solution.py:262
  14.6 3.3 %collective-permute-start.10 = (bf16[128,256]{1,0:T(8,128)(2,1)S(1)}, bf16[128,256]{1,0:T(8,128)(2,1)S(1)}, u32[]{:S(2)}, u32[]{:S(2)}) collective-permute-start(bf16[128,256]{1,0:T(8,128)(2,1)S(1)} %shard_map.111.own), channel_id=1, source_target_pairs={{0,8},{1,3},{2,10},{3,1},{4,12},{5,7},{6,14},{7,5},{8,0},{9,11},{1... | collective-permute-start | bytes 196616 | tf_op jit(solution)/shard_map/ppermute | solution.py:262
  18.0 1.4 %collective-permute-start.6 = (bf16[128,256]{1,0:T(8,128)(2,1)S(1)}, bf16[128,256]{1,0:T(8,128)(2,1)S(1)}, u32[]{:S(2)}, u32[]{:S(2)}) collective-permute-start(bf16[128,256]{1,0:T(8,128)(2,1)S(1)} %shard_map.107.own), channel_id=1, source_target_pairs={{0,8},{1,3},{2,10},{3,1},{4,12},{5,7},{6,14},{7,5},{8,0},{9,11},{1... | collective-permute-start | bytes 196616 | tf_op jit(solution)/shard_map/ppermute | solution.py:262
  19.4 0.8 %collective-permute-done.10.other = bf16[128,256]{1,0:T(8,128)(2,1)S(1)} collective-permute-done((bf16[128,256]{1,0:T(8,128)(2,1)S(1)}, bf16[128,256]{1,0:T(8,128)(2,1)S(1)}, u32[]{:S(2)}, u32[]{:S(2)}) %collective-permute-start.10) | collective-permute-done | bytes 65568 | tf_op jit(solution)/shard_map/ppermute | solution.py:262
  20.3 2.9 %collective-permute-done.6.other = bf16[128,256]{1,0:T(8,128)(2,1)S(1)} collective-permute-done((bf16[128,256]{1,0:T(8,128)(2,1)S(1)}, bf16[128,256]{1,0:T(8,128)(2,1)S(1)}, u32[]{:S(2)}, u32[]{:S(2)}) %collective-permute-start.6) | collective-permute-done | bytes 65568 | tf_op jit(solution)/shard_map/ppermute | solution.py:262
  23.3 1.2 %collective-permute-done.7.near = bf16[128,256]{1,0:T(8,128)(2,1)S(1)} collective-permute-done((bf16[128,256]{1,0:T(8,128)(2,1)S(1)}, bf16[128,256]{1,0:T(8,128)(2,1)S(1)}, u32[]{:S(2)}, u32[]{:S(2)}) %collective-permute-start.7) | collective-permute-done | bytes 65568 | tf_op jit(solution)/shard_map/ppermute | solution.py:244
  24.6 0.7 %shard_map.113 = (bf16[128,256]{1,0:T(8,128)(2,1)S(1)}, bf16[128,256]{1,0:T(8,128)(2,1)S(1)}, f32[128,256]{1,0:T(8,128)S(1)}) custom-call(bf16[2,2,256,256]{3,2,1,0:T(8,128)(2,1)S(1)} %get-tuple-element.16.basis.mine, bf16[2,2,256,256]{3,2,1,0:T(8,128)(2,1)S(1)} %collective-permute-done.basis.theirs, bf16[128,256]{1,0:T(8,128)(2,1)S(1)} %collective-permute-done.7.near, ...), custom_call_target="tpu_custom_call" | custom-call | tf_op jit(solution)/shard_map/pallas_call | solution.py:241
  25.3 1.6 %collective-permute-start.16 = (bf16[128,256]{1,0:T(8,128)(2,1)S(1)}, bf16[128,256]{1,0:T(8,128)(2,1)S(1)}, u32[]{:S(2)}, u32[]{:S(2)}) collective-permute-start(bf16[128,256]{1,0:T(8,128)(2,1)S(1)} %get-tuple-element.28.own), channel_id=1, source_target_pairs={{0,2},{1,5},{2,0},{3,7},{4,6},{5,1},{6,4},{7,3},{8,10},{9,13},{10,... | collective-permute-start | bytes 196616 | tf_op jit(solution)/shard_map/ppermute | solution.py:262
  27.4 2.2 %collective-permute-done.16.other = bf16[128,256]{1,0:T(8,128)(2,1)S(1)} collective-permute-done((bf16[128,256]{1,0:T(8,128)(2,1)S(1)}, bf16[128,256]{1,0:T(8,128)(2,1)S(1)}, u32[]{:S(2)}, u32[]{:S(2)}) %collective-permute-start.16) | collective-permute-done | bytes 65568 | tf_op jit(solution)/shard_map/ppermute | solution.py:262
  29.7 1.8 %collective-permute-start.17 = (bf16[128,256]{1,0:T(8,128)(2,1)S(1)}, bf16[128,256]{1,0:T(8,128)(2,1)S(1)}, u32[]{:S(2)}, u32[]{:S(2)}) collective-permute-start(bf16[128,256]{1,0:T(8,128)(2,1)S(1)} %shard_map.117.own), channel_id=1, source_target_pairs={{0,4},{1,9},{2,6},{3,11},{4,0},{5,13},{6,2},{7,15},{8,12},{9,1},{1... | collective-permute-start | bytes 196616 | tf_op jit(solution)/shard_map/ppermute | solution.py:262
  31.5 1.8 %collective-permute-start.13 = (bf16[128,256]{1,0:T(8,128)(2,1)S(1)}, bf16[128,256]{1,0:T(8,128)(2,1)S(1)}, u32[]{:S(2)}, u32[]{:S(2)}) collective-permute-start(bf16[128,256]{1,0:T(8,128)(2,1)S(1)} %shard_map.114.own), channel_id=1, source_target_pairs={{0,4},{1,9},{2,6},{3,11},{4,0},{5,13},{6,2},{7,15},{8,12},{9,1},{1... | collective-permute-start | bytes 196616 | tf_op jit(solution)/shard_map/ppermute | solution.py:262
  33.3 0.7 %collective-permute-done.17.other = bf16[128,256]{1,0:T(8,128)(2,1)S(1)} collective-permute-done((bf16[128,256]{1,0:T(8,128)(2,1)S(1)}, bf16[128,256]{1,0:T(8,128)(2,1)S(1)}, u32[]{:S(2)}, u32[]{:S(2)}) %collective-permute-start.17) | collective-permute-done | bytes 65568 | tf_op jit(solution)/shard_map/ppermute | solution.py:262
  34.0 1.9 %collective-permute-start.18 = (bf16[128,256]{1,0:T(8,128)(2,1)S(1)}, bf16[128,256]{1,0:T(8,128)(2,1)S(1)}, u32[]{:S(2)}, u32[]{:S(2)}) collective-permute-start(bf16[128,256]{1,0:T(8,128)(2,1)S(1)} %shard_map.118.own), channel_id=1, source_target_pairs={{0,8},{1,3},{2,10},{3,1},{4,12},{5,7},{6,14},{7,5},{8,0},{9,11},{1... | collective-permute-start | bytes 196616 | tf_op jit(solution)/shard_map/ppermute | solution.py:262
  35.9 1.7 %collective-permute-start.14 = (bf16[128,256]{1,0:T(8,128)(2,1)S(1)}, bf16[128,256]{1,0:T(8,128)(2,1)S(1)}, u32[]{:S(2)}, u32[]{:S(2)}) collective-permute-start(bf16[128,256]{1,0:T(8,128)(2,1)S(1)} %shard_map.115.own), channel_id=1, source_target_pairs={{0,8},{1,3},{2,10},{3,1},{4,12},{5,7},{6,14},{7,5},{8,0},{9,11},{1... | collective-permute-start | bytes 196616 | tf_op jit(solution)/shard_map/ppermute | solution.py:262
  37.7 1.6 %collective-permute-done.18.other = bf16[128,256]{1,0:T(8,128)(2,1)S(1)} collective-permute-done((bf16[128,256]{1,0:T(8,128)(2,1)S(1)}, bf16[128,256]{1,0:T(8,128)(2,1)S(1)}, u32[]{:S(2)}, u32[]{:S(2)}) %collective-permute-start.18) | collective-permute-done | bytes 65568 | tf_op jit(solution)/shard_map/ppermute | solution.py:262
  39.4 2.3 %collective-permute-done.14.other = bf16[128,256]{1,0:T(8,128)(2,1)S(1)} collective-permute-done((bf16[128,256]{1,0:T(8,128)(2,1)S(1)}, bf16[128,256]{1,0:T(8,128)(2,1)S(1)}, u32[]{:S(2)}, u32[]{:S(2)}) %collective-permute-start.14) | collective-permute-done | bytes 65568 | tf_op jit(solution)/shard_map/ppermute | solution.py:262
  42.1 0.9 %collective-permute-done.15.my_near = bf16[128,256]{1,0:T(8,128)(2,1)S(1)} collective-permute-done((bf16[128,256]{1,0:T(8,128)(2,1)S(1)}, bf16[128,256]{1,0:T(8,128)(2,1)S(1)}, u32[]{:S(2)}, u32[]{:S(2)}) %collective-permute-start.15) | collective-permute-done | bytes 65568 | tf_op jit(solution)/shard_map/ppermute | solution.py:244
  43.0 1.3 %shard_map.121 = (f32[256,128]{1,0:T(8,128)}, f32[1,256,128]{2,1,0:T(8,128)}) custom-call(bf16[2,2,256,256]{3,2,1,0:T(8,128)(2,1)S(1)} %get-tuple-element.16.basis.mine, bf16[2,2,256,256]{3,2,1,0:T(8,128)(2,1)S(1)} %collective-permute-done.basis.theirs, bf16[2,2,256,256]{3,2,1,0:T(8,128)(2,1)S(1)} %get-tuple-element.17.sent, ...), custom_call_target="tpu_custom_call" | custom-call | tf_op jit(solution)/shard_map/pallas_call | solution.py:241
  (34 shorter events, 3.2 us)
Async XLA Ops:
  2.3 5.4 %collective-permute-start = (bf16[2,2,256,256]{3,2,1,0:T(8,128)(2,1)S(1)}, bf16[2,2,256,256]{3,2,1,0:T(8,128)(2,1)S(1)}, u32[]{:S(2)}, u32[]{:S(2)}) collective-permute-start(bf16[2,2,256,256]{3,2,1,0:T(8,128)(2,1)S(1)} %get-tuple-element.17.sent), channel_id=1, source_target_pairs={{0,1},{1,0},{2,3},{3,2},{4,5},{5,4},{6,7},{7,6},{8,9},{9,8},{10,11... | collective-permute-start | bytes 1572872 | tf_op jit(solution)/shard_map/ppermute | solution.py:244
  2.8 1.7 %collective-permute-start.2 = (f32[128,256]{1,0:T(8,128)S(1)}, f32[128,256]{1,0:T(8,128)S(1)}, u32[]{:S(2)}, u32[]{:S(2)}) collective-permute-start(f32[128,256]{1,0:T(8,128)S(1)} %get-tuple-element.21), channel_id=1, source_target_pairs={{0,1},{1,0},{2,3},{3,2},{4,5},{5,4},{6,7},{7,6},{8,9},{9,8},{10,11... | collective-permute-start | bytes 393224 | tf_op jit(solution)/shard_map/ppermute | solution.py:244
  2.9 4.8 %collective-permute-start.1 = (f32[2,1,256]{2,1,0:T(1,128)S(1)}, f32[2,1,256]{2,1,0:T(1,128)S(1)}, u32[]{:S(2)}, u32[]{:S(2)}) collective-permute-start(f32[2,1,256]{2,1,0:T(1,128)S(1)} %get-tuple-element.19), channel_id=1, source_target_pairs={{0,1},{1,0},{2,3},{3,2},{4,5},{5,4},{6,7},{7,6},{8,9},{9,8},{10,11... | collective-permute-start | bytes 6152 | tf_op jit(solution)/shard_map/ppermute | solution.py:244
  4.8 5.2 %collective-permute-start.8 = (bf16[128,256]{1,0:T(8,128)(2,1)S(1)}, bf16[128,256]{1,0:T(8,128)(2,1)S(1)}, u32[]{:S(2)}, u32[]{:S(2)}) collective-permute-start(bf16[128,256]{1,0:T(8,128)(2,1)S(1)} %shard_map.109.own), channel_id=1, source_target_pairs={{0,2},{1,5},{2,0},{3,7},{4,6},{5,1},{6,4},{7,3},{8,10},{9,13},{10,... | collective-permute-start | bytes 196616 | tf_op jit(solution)/shard_map/ppermute | solution.py:262
  8.0 4.3 %collective-permute-start.4 = (bf16[128,256]{1,0:T(8,128)(2,1)S(1)}, bf16[128,256]{1,0:T(8,128)(2,1)S(1)}, u32[]{:S(2)}, u32[]{:S(2)}) collective-permute-start(bf16[128,256]{1,0:T(8,128)(2,1)S(1)} %shard_map.105.own), channel_id=1, source_target_pairs={{0,2},{1,5},{2,0},{3,7},{4,6},{5,1},{6,4},{7,3},{8,10},{9,13},{10,... | collective-permute-start | bytes 196616 | tf_op jit(solution)/shard_map/ppermute | solution.py:262
  10.0 4.6 %collective-permute-start.9 = (bf16[128,256]{1,0:T(8,128)(2,1)S(1)}, bf16[128,256]{1,0:T(8,128)(2,1)S(1)}, u32[]{:S(2)}, u32[]{:S(2)}) collective-permute-start(bf16[128,256]{1,0:T(8,128)(2,1)S(1)} %shard_map.110.own), channel_id=1, source_target_pairs={{0,4},{1,9},{2,6},{3,11},{4,0},{5,13},{6,2},{7,15},{8,12},{9,1},{1... | collective-permute-start | bytes 196616 | tf_op jit(solution)/shard_map/ppermute | solution.py:262
  12.3 5.6 %collective-permute-start.5 = (bf16[128,256]{1,0:T(8,128)(2,1)S(1)}, bf16[128,256]{1,0:T(8,128)(2,1)S(1)}, u32[]{:S(2)}, u32[]{:S(2)}) collective-permute-start(bf16[128,256]{1,0:T(8,128)(2,1)S(1)} %shard_map.106.own), channel_id=1, source_target_pairs={{0,4},{1,9},{2,6},{3,11},{4,0},{5,13},{6,2},{7,15},{8,12},{9,1},{1... | collective-permute-start | bytes 196616 | tf_op jit(solution)/shard_map/ppermute | solution.py:262
  14.6 5.5 %collective-permute-start.10 = (bf16[128,256]{1,0:T(8,128)(2,1)S(1)}, bf16[128,256]{1,0:T(8,128)(2,1)S(1)}, u32[]{:S(2)}, u32[]{:S(2)}) collective-permute-start(bf16[128,256]{1,0:T(8,128)(2,1)S(1)} %shard_map.111.own), channel_id=1, source_target_pairs={{0,8},{1,3},{2,10},{3,1},{4,12},{5,7},{6,14},{7,5},{8,0},{9,11},{1... | collective-permute-start | bytes 196616 | tf_op jit(solution)/shard_map/ppermute | solution.py:262
  18.0 5.2 %collective-permute-start.6 = (bf16[128,256]{1,0:T(8,128)(2,1)S(1)}, bf16[128,256]{1,0:T(8,128)(2,1)S(1)}, u32[]{:S(2)}, u32[]{:S(2)}) collective-permute-start(bf16[128,256]{1,0:T(8,128)(2,1)S(1)} %shard_map.107.own), channel_id=1, source_target_pairs={{0,8},{1,3},{2,10},{3,1},{4,12},{5,7},{6,14},{7,5},{8,0},{9,11},{1... | collective-permute-start | bytes 196616 | tf_op jit(solution)/shard_map/ppermute | solution.py:262
  20.2 3.1 %collective-permute-start.11 = (bf16[128,256]{1,0:T(8,128)(2,1)S(1)}, bf16[128,256]{1,0:T(8,128)(2,1)S(1)}, u32[]{:S(2)}, u32[]{:S(2)}) collective-permute-start(bf16[128,256]{1,0:T(8,128)(2,1)S(1)} %shard_map.112.near), channel_id=1, source_target_pairs={{0,1},{1,0},{2,3},{3,2},{4,5},{5,4},{6,7},{7,6},{8,9},{9,8},{10,11... | collective-permute-start | bytes 196616 | tf_op jit(solution)/shard_map/ppermute | solution.py:244
  23.2 1.3 %collective-permute-start.7 = (bf16[128,256]{1,0:T(8,128)(2,1)S(1)}, bf16[128,256]{1,0:T(8,128)(2,1)S(1)}, u32[]{:S(2)}, u32[]{:S(2)}) collective-permute-start(bf16[128,256]{1,0:T(8,128)(2,1)S(1)} %shard_map.108.far), channel_id=1, source_target_pairs={{0,1},{1,0},{2,3},{3,2},{4,5},{5,4},{6,7},{7,6},{8,9},{9,8},{10,11... | collective-permute-start | bytes 196616 | tf_op jit(solution)/shard_map/ppermute | solution.py:244
  25.3 4.3 %collective-permute-start.16 = (bf16[128,256]{1,0:T(8,128)(2,1)S(1)}, bf16[128,256]{1,0:T(8,128)(2,1)S(1)}, u32[]{:S(2)}, u32[]{:S(2)}) collective-permute-start(bf16[128,256]{1,0:T(8,128)(2,1)S(1)} %get-tuple-element.28.own), channel_id=1, source_target_pairs={{0,2},{1,5},{2,0},{3,7},{4,6},{5,1},{6,4},{7,3},{8,10},{9,13},{10,... | collective-permute-start | bytes 196616 | tf_op jit(solution)/shard_map/ppermute | solution.py:262
  26.9 4.6 %collective-permute-start.12 = (bf16[128,256]{1,0:T(8,128)(2,1)S(1)}, bf16[128,256]{1,0:T(8,128)(2,1)S(1)}, u32[]{:S(2)}, u32[]{:S(2)}) collective-permute-start(bf16[128,256]{1,0:T(8,128)(2,1)S(1)} %get-tuple-element.27.own), channel_id=1, source_target_pairs={{0,2},{1,5},{2,0},{3,7},{4,6},{5,1},{6,4},{7,3},{8,10},{9,13},{10,... | collective-permute-start | bytes 196616 | tf_op jit(solution)/shard_map/ppermute | solution.py:262
  27.4 14.4 %collective-permute-start.3 = (bf16[2,256,256]{2,1,0:T(8,128)(2,1)S(1)}, bf16[2,256,256]{2,1,0:T(8,128)(2,1)S(1)}, u32[]{:S(2)}, u32[]{:S(2)}) collective-permute-start(bf16[2,256,256]{2,1,0:T(8,128)(2,1)S(1)} %get-tuple-element.22), channel_id=1, source_target_pairs={{0,1},{1,0},{2,3},{3,2},{4,5},{5,4},{6,7},{7,6},{8,9},{9,8},{10,11... | collective-permute-start | bytes 786440 | tf_op jit(solution)/shard_map/ppermute | solution.py:244
  29.7 4.3 %collective-permute-start.17 = (bf16[128,256]{1,0:T(8,128)(2,1)S(1)}, bf16[128,256]{1,0:T(8,128)(2,1)S(1)}, u32[]{:S(2)}, u32[]{:S(2)}) collective-permute-start(bf16[128,256]{1,0:T(8,128)(2,1)S(1)} %shard_map.117.own), channel_id=1, source_target_pairs={{0,4},{1,9},{2,6},{3,11},{4,0},{5,13},{6,2},{7,15},{8,12},{9,1},{1... | collective-permute-start | bytes 196616 | tf_op jit(solution)/shard_map/ppermute | solution.py:262
  31.5 4.4 %collective-permute-start.13 = (bf16[128,256]{1,0:T(8,128)(2,1)S(1)}, bf16[128,256]{1,0:T(8,128)(2,1)S(1)}, u32[]{:S(2)}, u32[]{:S(2)}) collective-permute-start(bf16[128,256]{1,0:T(8,128)(2,1)S(1)} %shard_map.114.own), channel_id=1, source_target_pairs={{0,4},{1,9},{2,6},{3,11},{4,0},{5,13},{6,2},{7,15},{8,12},{9,1},{1... | collective-permute-start | bytes 196616 | tf_op jit(solution)/shard_map/ppermute | solution.py:262
  34.0 5.2 %collective-permute-start.18 = (bf16[128,256]{1,0:T(8,128)(2,1)S(1)}, bf16[128,256]{1,0:T(8,128)(2,1)S(1)}, u32[]{:S(2)}, u32[]{:S(2)}) collective-permute-start(bf16[128,256]{1,0:T(8,128)(2,1)S(1)} %shard_map.118.own), channel_id=1, source_target_pairs={{0,8},{1,3},{2,10},{3,1},{4,12},{5,7},{6,14},{7,5},{8,0},{9,11},{1... | collective-permute-start | bytes 196616 | tf_op jit(solution)/shard_map/ppermute | solution.py:262
  35.9 5.7 %collective-permute-start.14 = (bf16[128,256]{1,0:T(8,128)(2,1)S(1)}, bf16[128,256]{1,0:T(8,128)(2,1)S(1)}, u32[]{:S(2)}, u32[]{:S(2)}) collective-permute-start(bf16[128,256]{1,0:T(8,128)(2,1)S(1)} %shard_map.115.own), channel_id=1, source_target_pairs={{0,8},{1,3},{2,10},{3,1},{4,12},{5,7},{6,14},{7,5},{8,0},{9,11},{1... | collective-permute-start | bytes 196616 | tf_op jit(solution)/shard_map/ppermute | solution.py:262
  39.3 2.8 %collective-permute-start.19 = (bf16[128,256]{1,0:T(8,128)(2,1)S(1)}, bf16[128,256]{1,0:T(8,128)(2,1)S(1)}, u32[]{:S(2)}, u32[]{:S(2)}) collective-permute-start(bf16[128,256]{1,0:T(8,128)(2,1)S(1)} %shard_map.119.other_near), channel_id=1, source_target_pairs={{0,1},{1,0},{2,3},{3,2},{4,5},{5,4},{6,7},{7,6},{8,9},{9,8},{10,11... | collective-permute-start | bytes 196616 | tf_op jit(solution)/shard_map/ppermute | solution.py:244
  41.7 1.3 %collective-permute-start.15 = (bf16[128,256]{1,0:T(8,128)(2,1)S(1)}, bf16[128,256]{1,0:T(8,128)(2,1)S(1)}, u32[]{:S(2)}, u32[]{:S(2)}) collective-permute-start(bf16[128,256]{1,0:T(8,128)(2,1)S(1)} %shard_map.116.other_far), channel_id=1, source_target_pairs={{0,1},{1,0},{2,3},{3,2},{4,5},{5,4},{6,7},{7,6},{8,9},{9,8},{10,11... | collective-permute-start | bytes 196616 | tf_op jit(solution)/shard_map/ppermute | solution.py:244

commit v8 on v7

--- a/solution.py
+++ b/solution.py
@@ -55,12 +55,12 @@
     mine,
     send,
     send_own,
-    amp_send,
     small_send,
     gate,
     weight,
     energy,
     amp_ref,
+    part_ref,
     flags,
     counts,
     flat_weight,
@@ -134,21 +134,28 @@
                 )
     amp_ref[0] = tgt_own[...].T
     amp_ref[1] = proj_own[0].T
-    amp_send[...] = amp_ref[1 - core]
     for copy in basis_copies(0):
         copy.wait()
-
-
-def first_kernel(basis, weight, amp_ref, other_ref, out_ref):
-    core = lax.axis_index("rep")
-    total = project(basis[0, core], basis[1, core], amp_ref[core]) + project(
-        basis[0, 1 - core], basis[1, 1 - core], other_ref[...]
-    )
-    out_ref[...] = bf16(weight[0] * total)
-
-
-def add_kernel(step, half, gate, own, other, out_ref):
-    out_ref[...] = bf16(gate[step, half] * (f32(own[...]) + f32(other[...])))
+    for slot, (basis, kind) in enumerate(((mine, core), (send, 1 - core))):
+        part_ref[slot] = project(basis[0, core], basis[1, core], amp_ref[kind])
+
+
+def first_kernel(mine, sent, weight, part_ref, tgt_other, proj_other, near_ref, swap_ref, other_ref):
+    core = lax.axis_index("rep")
+    tgt_amp, proj_amp = tgt_other[...].T, proj_other[0].T
+    my_amp = jnp.where(core == 0, tgt_amp, proj_amp)
+    other_amp = jnp.where(core == 0, proj_amp, tgt_amp)
+    other_ref[...] = my_amp
+    for slot, (basis, amp, out_ref) in enumerate(((mine, my_amp, near_ref), (sent, other_amp, swap_ref))):
+        total = part_ref[slot] + project(basis[0, 1 - core], basis[1, 1 - core], amp)
+        out_ref[...] = bf16(weight[0] * total)
+
+
+def add_kernel(step, gate, *refs):
+    count = len(refs) // 3
+    for half in range(count):
+        own, other, out_ref = refs[half::count]
+        out_ref[...] = bf16(gate[step, half] * (f32(own[...]) + f32(other[...])))
 
 
 def second_kernel(
@@ -180,35 +187,22 @@
     half_ref[...] = amp + half_step * (energy[1 - core] * turned(amp) + change)
 
 
-def last_kernel(
-    mine,
-    theirs,
-    sent,
-    own_far,
-    my_near,
-    my_far,
-    other_near,
-    other_far,
-    energy,
-    amp_ref,
-    my_half,
-    other_half,
-    new_tgt,
-    new_proj,
-):
-    core = lax.axis_index("rep")
-    my_change = expand(mine[0, core], mine[1, core], my_near[...]) + expand(
-        theirs[0, core], theirs[1, core], my_far[...]
-    )
-    other_change = expand(sent[0, core], sent[1, core], other_near[...]) + expand(
-        own_far[0], own_far[1], other_far[...]
-    )
-    my_rate = energy[core] * turned(my_half[...]) + my_change
-    other_rate = energy[1 - core] * turned(other_half[...]) + other_change
-    my_new = (amp_ref[core] + time_step * my_rate).T
-    other_new = (amp_ref[1 - core] + time_step * other_rate).T
-    new_tgt[...] = jnp.where(core == 0, my_new, other_new)
-    new_proj[0] = jnp.where(core == 0, other_new, my_new)
+def other_last_kernel(sent, own_far, near, far, energy, amp_ref, half_ref, new_ref):
+    core = lax.axis_index("rep")
+    change = expand(sent[0, core], sent[1, core], near[...]) + expand(own_far[0], own_far[1], far[...])
+    rate = energy[1 - core] * turned(half_ref[...]) + change
+    new_ref[...] = (amp_ref[1 - core] + time_step * rate).T
+
+
+def last_kernel(mine, theirs, near, far, energy, amp_ref, half_ref, other_new, new_tgt, new_proj):
+    core = lax.axis_index("rep")
+    change = expand(mine[0, core], mine[1, core], near[...]) + expand(
+        theirs[0, core], theirs[1, core], far[...]
+    )
+    rate = energy[core] * turned(half_ref[...]) + change
+    my_new = (amp_ref[core] + time_step * rate).T
+    new_tgt[...] = jnp.where(core == 0, my_new, other_new[...])
+    new_proj[0] = jnp.where(core == 0, other_new[...], my_new)
 
 
 def shards(
@@ -255,18 +249,16 @@
     segment = in_vmem((two_cols, rows), jnp.float32)
 
     def summed(*halves):
-        totals = []
-        for half, block in enumerate(halves):
-            for step, flips in enumerate(steps):
-                pairs = [(me, me ^ flips[me % n_core]) for me in range(n_tgt * n_prj * n_core)]
-                other = lax.ppermute(block, DEVICES, pairs)
-                (block,) = run(functools.partial(add_kernel, step, half), [sums], gate, block, other)
-            totals.append(block)
-        return totals
+        for step, flips in enumerate(steps):
+            pairs = [(me, me ^ flips[me % n_core]) for me in range(n_tgt * n_prj * n_core)]
+            others = [lax.ppermute(block, DEVICES, pairs) for block in halves]
+            halves = run(functools.partial(add_kernel, step), [sums] * 2, gate, *halves, *others)
+        return halves
 
     def swapped(near, far):
         return other_core(far), other_core(near)
 
+    tgt_other, proj_other = other_core(tgt_amp), other_core(proj_amp)
     inputs = (
         pair_flags.T,
         tile_counts.T,
@@ -278,18 +270,18 @@
         tgt_amp,
         proj_amp,
     )
-    mine, sent, send_own, amp_send, small_send, gate, weight, energy, amp = call(
+    mine, sent, send_own, small_send, gate, weight, energy, amp, part = call(
         functools.partial(load_kernel, gate_steps),
         [
             basis,
             basis,
             in_vmem((2, rows, points), jnp.bfloat16),
-            segment,
             in_vmem((2, 1, points), jnp.float32),
             in_vmem((len(steps), 2, 1, points), jnp.float32),
             in_vmem((1, 1, points), jnp.float32),
             in_vmem((2, 1, rows), jnp.float32),
             in_vmem((2, two_cols, rows), jnp.float32),
+            in_vmem((2, two_cols, points), jnp.float32),
         ],
         [HBM] * len(inputs),
         [
@@ -301,13 +293,14 @@
             pltpu.VMEM(proj_amp.shape, jnp.float32),
             pltpu.SemaphoreType.DMA((13,)),
         ],
-        pl.CostEstimate(flops=0, bytes_accessed=4 * 1024 * 1024, transcendentals=0),
+        pl.CostEstimate(flops=2 * 4 * rows * two_cols * points, bytes_accessed=4 * 1024 * 1024, transcendentals=0),
     )(*[pltpu.with_memory_space_constraint(block, pltpu.HBM) for block in inputs])
-    other, small, theirs = other_core(amp_send), other_core(small_send), other_core(sent)
-    (near,) = run(first_kernel, [sums], mine, weight, amp, other)
-    (far,) = run(first_kernel, [sums], theirs, small, amp, other)
-    send_own, far = lax.optimization_barrier((send_own, far))
-    own_far = other_core(send_own)
+    near, far, other = run(
+        first_kernel, [sums, sums, segment], mine, sent, weight, part, tgt_other, proj_other
+    )
+    far = other_core(far)
+    sent, send_own, small_send, far = lax.optimization_barrier((sent, send_own, small_send, far))
+    theirs, own_far, small = other_core(sent), other_core(send_own), other_core(small_send)
     fields = summed(near, far)
     near, far, my_half = run(
         second_kernel,
@@ -323,6 +316,16 @@
     )
     (other_half,) = run(other_half_kernel, [segment], sent, own_far, *fields, energy, amp)
     fields = summed(near, far)
+    (other_new,) = run(
+        other_last_kernel,
+        [in_vmem((rows, two_cols), jnp.float32)],
+        sent,
+        own_far,
+        *fields,
+        energy,
+        amp,
+        other_half,
+    )
     return run(
         last_kernel,
         [
@@ -331,14 +334,11 @@
         ],
         mine,
         theirs,
-        sent,
-        own_far,
         *swapped(*fields),
-        *fields,
         energy,
         amp,
         my_half,
-        other_half,
+        other_new,
     )
 
 

time: 44.4 us -> 49.5 us (1.11)
  waiting for transfers between devices: 16.5 us -> 26.1 us
  starting transfers between devices: 22.2 us -> 17.6 us
    ppermute x12, waiting for transfers between devices: 13.2 us -> 23.9 us  [summed(): others = [lax.ppermute(block, DEVICES, pairs) for block in halves]]
    ppermute x12, starting transfers between devices: 20.9 us -> 14.9 us  [summed(): others = [lax.ppermute(block, DEVICES, pairs) for block in halves]]
    ppermute x8 -> x10, starting transfers between devices: 1.3 us -> 2.66 us  [other_core(): return lax.ppermute(block, 'rep', [(0, 1), (1, 0)])]
    ppermute x8 -> x10, waiting for transfers between devices: 3.35 us -> 2.18 us  [other_core(): return lax.ppermute(block, 'rep', [(0, 1), (1, 0)])]
    pallas_call x17 -> x11, Pallas kernels: 3.14 us -> 3.12 us  [run(): return call(kernel, out_shape, [VMEM] * len(blocks))(*blocks)]
  transfers between devices with their start and end apart: 20 -> 22, of which waited for: 12 -> 15; matrix products, arithmetic and copies ran while one was open for 0% -> 0% of each run, Pallas kernels for 2% -> 6%
where the time goes in v8:
time: 49.5 us; the launch traced here: 49.4 us
  waiting for transfers between devices  26.1 us (53%)
  starting transfers between devices  17.6 us (36%)
  Pallas kernels  4.99 us (10%)
  between operations  0.74 us (1%)
    ppermute x12, waiting for transfers between devices, summed(): others = [lax.ppermute(block, DEVICES, pairs) for block in halves]  23.9 us
    ppermute x12, starting transfers between devices, summed(): others = [lax.ppermute(block, DEVICES, pairs) for block in halves]  14.9 us
    pallas_call x11, Pallas kernels, run(): return call(kernel, out_shape, [VMEM] * len(blocks))(*blocks)  3.12 us
    ppermute x10, starting transfers between devices, other_core(): return lax.ppermute(block, 'rep', [(0, 1), (1, 0)])  2.66 us
    ppermute x10, waiting for transfers between devices, other_core(): return lax.ppermute(block, 'rep', [(0, 1), (1, 0)])  2.18 us
    pallas_call x1, Pallas kernels, shards(): call(functools.partial(load_kernel, gate_steps), [basis, basis, in_vmem((...  1.87 us
  transfers between devices with their start and end apart: 22, of which 15 were waited for; matrix products, arithmetic and copies ran while one was open for 0% of the time, Pallas kernels for 6%

profile of v8, /device:TPU:0, one launch (start us, length us, event | category | flops | bytes accessed | tf_op | source)
XLA Modules:
  0.0 49.4 jit_solution(13486777669073471406)
XLA Ops:
  1.2 1.9 %shard_map.104 = (bf16[2,2,256,256]{3,2,1,0:T(8,128)(2,1)S(1)}, bf16[2,2,256,256]{3,2,1,0:T(8,128)(2,1)S(1)}, bf16[2,256,256]{2,1,0:T(8,128)(2,1)S(1)}, f32[2,1,...) custom-call(s32[2,4]{1,0:T(2,128)} %bitcast.4, ...), custom_call_target="tpu_custom_call" | custom-call | flops 67108864 | bytes 4194304 | tf_op jit(solution)/shard_map/pallas_call | solution.py:273
  4.0 0.9 %collective-permute-done.2.refs_1_ = bf16[128,256]{1,0:T(8,128)(2,1)S(1)} collective-permute-done((bf16[128,256]{1,0:T(8,128)(2,1)S(1)}, bf16[128,256]{1,0:T(8,128)(2,1)S(1)}, u32[]{:S(2)}, u32[]{:S(2)}) %collective-permute-start.2) | collective-permute-done | bytes 65568 | tf_op jit(solution)/shard_map/ppermute | solution.py:238
  5.2 2.6 %collective-permute-start.4 = (bf16[128,256]{1,0:T(8,128)(2,1)S(1)}, bf16[128,256]{1,0:T(8,128)(2,1)S(1)}, u32[]{:S(2)}, u32[]{:S(2)}) collective-permute-start(bf16[128,256]{1,0:T(8,128)(2,1)S(1)} %get-tuple-element.42.refs_0_), channel_id=1, source_target_pairs={{0,2},{1,5},{2,0},{3,7},{4,6},{5,1},{6,4},{7,3},{8,10},{9,13},{10,... | collective-permute-start | bytes 196616 | tf_op jit(solution)/shard_map/ppermute | solution.py:254
  7.9 2.2 %collective-permute-done.4.refs_2_ = bf16[128,256]{1,0:T(8,128)(2,1)S(1)} collective-permute-done((bf16[128,256]{1,0:T(8,128)(2,1)S(1)}, bf16[128,256]{1,0:T(8,128)(2,1)S(1)}, u32[]{:S(2)}, u32[]{:S(2)}) %collective-permute-start.4) | collective-permute-done | bytes 65568 | tf_op jit(solution)/shard_map/ppermute | solution.py:254
  10.1 2.0 %collective-permute-done.5.refs_3_ = bf16[128,256]{1,0:T(8,128)(2,1)S(1)} collective-permute-done((bf16[128,256]{1,0:T(8,128)(2,1)S(1)}, bf16[128,256]{1,0:T(8,128)(2,1)S(1)}, u32[]{:S(2)}, u32[]{:S(2)}) %collective-permute-start.5) | collective-permute-done | bytes 65568 | tf_op jit(solution)/shard_map/ppermute | solution.py:254
  12.2 1.6 %collective-permute-start.6 = (bf16[128,256]{1,0:T(8,128)(2,1)S(1)}, bf16[128,256]{1,0:T(8,128)(2,1)S(1)}, u32[]{:S(2)}, u32[]{:S(2)}) collective-permute-start(bf16[128,256]{1,0:T(8,128)(2,1)S(1)} %get-tuple-element.44.refs_0_), channel_id=1, source_target_pairs={{0,4},{1,9},{2,6},{3,11},{4,0},{5,13},{6,2},{7,15},{8,12},{9,1},{1... | collective-permute-start | bytes 196616 | tf_op jit(solution)/shard_map/ppermute | solution.py:254
  14.3 2.2 %collective-permute-done.6.refs_2_ = bf16[128,256]{1,0:T(8,128)(2,1)S(1)} collective-permute-done((bf16[128,256]{1,0:T(8,128)(2,1)S(1)}, bf16[128,256]{1,0:T(8,128)(2,1)S(1)}, u32[]{:S(2)}, u32[]{:S(2)}) %collective-permute-start.6) | collective-permute-done | bytes 65568 | tf_op jit(solution)/shard_map/ppermute | solution.py:254
  16.5 1.9 %collective-permute-done.7.refs_3_ = bf16[128,256]{1,0:T(8,128)(2,1)S(1)} collective-permute-done((bf16[128,256]{1,0:T(8,128)(2,1)S(1)}, bf16[128,256]{1,0:T(8,128)(2,1)S(1)}, u32[]{:S(2)}, u32[]{:S(2)}) %collective-permute-start.7) | collective-permute-done | bytes 65568 | tf_op jit(solution)/shard_map/ppermute | solution.py:254
  18.5 2.3 %collective-permute-start.8 = (bf16[128,256]{1,0:T(8,128)(2,1)S(1)}, bf16[128,256]{1,0:T(8,128)(2,1)S(1)}, u32[]{:S(2)}, u32[]{:S(2)}) collective-permute-start(bf16[128,256]{1,0:T(8,128)(2,1)S(1)} %get-tuple-element.46.refs_0_), channel_id=1, source_target_pairs={{0,8},{1,3},{2,10},{3,1},{4,12},{5,7},{6,14},{7,5},{8,0},{9,11},{1... | collective-permute-start | bytes 196616 | tf_op jit(solution)/shard_map/ppermute | solution.py:254
  21.5 2.9 %collective-permute-done.8.refs_2_ = bf16[128,256]{1,0:T(8,128)(2,1)S(1)} collective-permute-done((bf16[128,256]{1,0:T(8,128)(2,1)S(1)}, bf16[128,256]{1,0:T(8,128)(2,1)S(1)}, u32[]{:S(2)}, u32[]{:S(2)}) %collective-permute-start.8) | collective-permute-done | bytes 65568 | tf_op jit(solution)/shard_map/ppermute | solution.py:254
  24.4 1.5 %collective-permute-done.9.refs_3_ = bf16[128,256]{1,0:T(8,128)(2,1)S(1)} collective-permute-done((bf16[128,256]{1,0:T(8,128)(2,1)S(1)}, bf16[128,256]{1,0:T(8,128)(2,1)S(1)}, u32[]{:S(2)}, u32[]{:S(2)}) %collective-permute-start.9) | collective-permute-done | bytes 65568 | tf_op jit(solution)/shard_map/ppermute | solution.py:254
  26.6 1.1 %collective-permute-done.12.small = f32[2,1,256]{2,1,0:T(1,128)S(1)} collective-permute-done((f32[2,1,256]{2,1,0:T(1,128)S(1)}, f32[2,1,256]{2,1,0:T(1,128)S(1)}, u32[]{:S(2)}, u32[]{:S(2)}) %collective-permute-start.12) | collective-permute-done | bytes 2080 | tf_op jit(solution)/shard_map/ppermute | solution.py:238
  27.7 0.7 %shard_map.109 = (bf16[128,256]{1,0:T(8,128)(2,1)S(1)}, bf16[128,256]{1,0:T(8,128)(2,1)S(1)}, f32[128,256]{1,0:T(8,128)S(1)}) custom-call(bf16[2,2,256,256]{3,2,1,0:T(8,128)(2,1)S(1)} %get-tuple-element.33.mine, bf16[2,2,256,256]{3,2,1,0:T(8,128)(2,1)S(1)} %collective-permute-done.3.theirs, bf16[128,256]{1,0:T(8,128)(2,1)S(1)} %collective-permute-done.10.near, ...), custom_call_target="tpu_custom_call" | custom-call | tf_op jit(solution)/shard_map/pallas_call | solution.py:235
  28.5 0.8 %collective-permute-start.13 = (bf16[128,256]{1,0:T(8,128)(2,1)S(1)}, bf16[128,256]{1,0:T(8,128)(2,1)S(1)}, u32[]{:S(2)}, u32[]{:S(2)}) collective-permute-start(bf16[128,256]{1,0:T(8,128)(2,1)S(1)} %get-tuple-element.54.refs_0_), channel_id=1, source_target_pairs={{0,2},{1,5},{2,0},{3,7},{4,6},{5,1},{6,4},{7,3},{8,10},{9,13},{10,... | collective-permute-start | bytes 196616 | tf_op jit(solution)/shard_map/ppermute | solution.py:254
  29.3 1.3 %collective-permute-start.14 = (bf16[128,256]{1,0:T(8,128)(2,1)S(1)}, bf16[128,256]{1,0:T(8,128)(2,1)S(1)}, u32[]{:S(2)}, u32[]{:S(2)}) collective-permute-start(bf16[128,256]{1,0:T(8,128)(2,1)S(1)} %get-tuple-element.55.refs_1_), channel_id=1, source_target_pairs={{0,2},{1,5},{2,0},{3,7},{4,6},{5,1},{6,4},{7,3},{8,10},{9,13},{10,... | collective-permute-start | bytes 196616 | tf_op jit(solution)/shard_map/ppermute | solution.py:254
  30.6 2.2 %collective-permute-done.13.refs_2_ = bf16[128,256]{1,0:T(8,128)(2,1)S(1)} collective-permute-done((bf16[128,256]{1,0:T(8,128)(2,1)S(1)}, bf16[128,256]{1,0:T(8,128)(2,1)S(1)}, u32[]{:S(2)}, u32[]{:S(2)}) %collective-permute-start.13) | collective-permute-done | bytes 65568 | tf_op jit(solution)/shard_map/ppermute | solution.py:254
  33.6 1.8 %collective-permute-start.15 = (bf16[128,256]{1,0:T(8,128)(2,1)S(1)}, bf16[128,256]{1,0:T(8,128)(2,1)S(1)}, u32[]{:S(2)}, u32[]{:S(2)}) collective-permute-start(bf16[128,256]{1,0:T(8,128)(2,1)S(1)} %get-tuple-element.56.refs_0_), channel_id=1, source_target_pairs={{0,4},{1,9},{2,6},{3,11},{4,0},{5,13},{6,2},{7,15},{8,12},{9,1},{1... | collective-permute-start | bytes 196616 | tf_op jit(solution)/shard_map/ppermute | solution.py:254
  35.7 2.8 %collective-permute-done.15.refs_2_ = bf16[128,256]{1,0:T(8,128)(2,1)S(1)} collective-permute-done((bf16[128,256]{1,0:T(8,128)(2,1)S(1)}, bf16[128,256]{1,0:T(8,128)(2,1)S(1)}, u32[]{:S(2)}, u32[]{:S(2)}) %collective-permute-start.15) | collective-permute-done | bytes 65568 | tf_op jit(solution)/shard_map/ppermute | solution.py:254
  38.4 1.6 %collective-permute-done.16.refs_3_ = bf16[128,256]{1,0:T(8,128)(2,1)S(1)} collective-permute-done((bf16[128,256]{1,0:T(8,128)(2,1)S(1)}, bf16[128,256]{1,0:T(8,128)(2,1)S(1)}, u32[]{:S(2)}, u32[]{:S(2)}) %collective-permute-start.16) | collective-permute-done | bytes 65568 | tf_op jit(solution)/shard_map/ppermute | solution.py:254
  40.0 1.6 %collective-permute-start.17 = (bf16[128,256]{1,0:T(8,128)(2,1)S(1)}, bf16[128,256]{1,0:T(8,128)(2,1)S(1)}, u32[]{:S(2)}, u32[]{:S(2)}) collective-permute-start(bf16[128,256]{1,0:T(8,128)(2,1)S(1)} %get-tuple-element.58.refs_0_), channel_id=1, source_target_pairs={{0,8},{1,3},{2,10},{3,1},{4,12},{5,7},{6,14},{7,5},{8,0},{9,11},{1... | collective-permute-start | bytes 196616 | tf_op jit(solution)/shard_map/ppermute | solution.py:254
  41.6 1.4 %collective-permute-start.18 = (bf16[128,256]{1,0:T(8,128)(2,1)S(1)}, bf16[128,256]{1,0:T(8,128)(2,1)S(1)}, u32[]{:S(2)}, u32[]{:S(2)}) collective-permute-start(bf16[128,256]{1,0:T(8,128)(2,1)S(1)} %get-tuple-element.59.refs_1_), channel_id=1, source_target_pairs={{0,8},{1,3},{2,10},{3,1},{4,12},{5,7},{6,14},{7,5},{8,0},{9,11},{1... | collective-permute-start | bytes 196616 | tf_op jit(solution)/shard_map/ppermute | solution.py:254
  43.0 2.9 %collective-permute-done.17.refs_2_ = bf16[128,256]{1,0:T(8,128)(2,1)S(1)} collective-permute-done((bf16[128,256]{1,0:T(8,128)(2,1)S(1)}, bf16[128,256]{1,0:T(8,128)(2,1)S(1)}, u32[]{:S(2)}, u32[]{:S(2)}) %collective-permute-start.17) | collective-permute-done | bytes 65568 | tf_op jit(solution)/shard_map/ppermute | solution.py:254
  46.0 0.8 %collective-permute-done.18.refs_3_ = bf16[128,256]{1,0:T(8,128)(2,1)S(1)} collective-permute-done((bf16[128,256]{1,0:T(8,128)(2,1)S(1)}, bf16[128,256]{1,0:T(8,128)(2,1)S(1)}, u32[]{:S(2)}, u32[]{:S(2)}) %collective-permute-start.18) | collective-permute-done | bytes 65568 | tf_op jit(solution)/shard_map/ppermute | solution.py:254
  48.3 1.1 %shard_map.115 = (f32[256,128]{1,0:T(8,128)}, f32[1,256,128]{2,1,0:T(8,128)}) custom-call(bf16[2,2,256,256]{3,2,1,0:T(8,128)(2,1)S(1)} %get-tuple-element.33.mine, bf16[2,2,256,256]{3,2,1,0:T(8,128)(2,1)S(1)} %collective-permute-done.3.theirs, bf16[128,256]{1,0:T(8,128)(2,1)S(1)} %collective-permute-done.19.near, ...), custom_call_target="tpu_custom_call" | custom-call | tf_op jit(solution)/shard_map/pallas_call | solution.py:235
  (32 shorter events, 6.4 us)
Async XLA Ops:
  0.6 2.5 %collective-permute-start = (f32[256,128]{1,0:T(8,128)}, f32[256,128]{1,0:T(8,128)S(1)}, u32[]{:S(2)}, u32[]{:S(2)}) collective-permute-start(f32[256,128]{1,0:T(8,128)} %tgt_own_hbm.1), channel_id=1, source_target_pairs={{0,1},{1,0},{2,3},{3,2},{4,5},{5,4},{6,7},{7,6},{8,9},{9,8},{10,11... | collective-permute-start | bytes 393224 | tf_op jit(solution)/shard_map/ppermute | solution.py:238
  1.2 2.0 %collective-permute-start.1 = (f32[1,256,128]{2,1,0:T(8,128)}, f32[1,256,128]{2,1,0:T(8,128)S(1)}, u32[]{:S(2)}, u32[]{:S(2)}) collective-permute-start(f32[1,256,128]{2,1,0:T(8,128)} %proj_own_hbm.1), channel_id=1, source_target_pairs={{0,1},{1,0},{2,3},{3,2},{4,5},{5,4},{6,7},{7,6},{8,9},{9,8},{10,11... | collective-permute-start | bytes 393224 | tf_op jit(solution)/shard_map/ppermute | solution.py:238
  3.5 1.4 %collective-permute-start.2 = (bf16[128,256]{1,0:T(8,128)(2,1)S(1)}, bf16[128,256]{1,0:T(8,128)(2,1)S(1)}, u32[]{:S(2)}, u32[]{:S(2)}) collective-permute-start(bf16[128,256]{1,0:T(8,128)(2,1)S(1)} %get-tuple-element.39), channel_id=1, source_target_pairs={{0,1},{1,0},{2,3},{3,2},{4,5},{5,4},{6,7},{7,6},{8,9},{9,8},{10,11... | collective-permute-start | bytes 196616 | tf_op jit(solution)/shard_map/ppermute | solution.py:238
  4.9 22.9 %collective-permute-start.3 = (bf16[2,2,256,256]{3,2,1,0:T(8,128)(2,1)S(1)}, bf16[2,2,256,256]{3,2,1,0:T(8,128)(2,1)S(1)}, u32[]{:S(2)}, u32[]{:S(2)}) collective-permute-start(bf16[2,2,256,256]{3,2,1,0:T(8,128)(2,1)S(1)} %get-tuple-element.40.sent), channel_id=1, source_target_pairs={{0,1},{1,0},{2,3},{3,2},{4,5},{5,4},{6,7},{7,6},{8,9},{9,8},{10,11... | collective-permute-start | bytes 1572872 | tf_op jit(solution)/shard_map/ppermute | solution.py:238
  5.2 4.9 %collective-permute-start.4 = (bf16[128,256]{1,0:T(8,128)(2,1)S(1)}, bf16[128,256]{1,0:T(8,128)(2,1)S(1)}, u32[]{:S(2)}, u32[]{:S(2)}) collective-permute-start(bf16[128,256]{1,0:T(8,128)(2,1)S(1)} %get-tuple-element.42.refs_0_), channel_id=1, source_target_pairs={{0,2},{1,5},{2,0},{3,7},{4,6},{5,1},{6,4},{7,3},{8,10},{9,13},{10,... | collective-permute-start | bytes 196616 | tf_op jit(solution)/shard_map/ppermute | solution.py:254
  7.9 4.3 %collective-permute-start.5 = (bf16[128,256]{1,0:T(8,128)(2,1)S(1)}, bf16[128,256]{1,0:T(8,128)(2,1)S(1)}, u32[]{:S(2)}, u32[]{:S(2)}) collective-permute-start(bf16[128,256]{1,0:T(8,128)(2,1)S(1)} %collective-permute-done.2.refs_1_), channel_id=1, source_target_pairs={{0,2},{1,5},{2,0},{3,7},{4,6},{5,1},{6,4},{7,3},{8,10},{9,13},{10,... | collective-permute-start | bytes 196616 | tf_op jit(solution)/shard_map/ppermute | solution.py:254
  12.2 4.3 %collective-permute-start.6 = (bf16[128,256]{1,0:T(8,128)(2,1)S(1)}, bf16[128,256]{1,0:T(8,128)(2,1)S(1)}, u32[]{:S(2)}, u32[]{:S(2)}) collective-permute-start(bf16[128,256]{1,0:T(8,128)(2,1)S(1)} %get-tuple-element.44.refs_0_), channel_id=1, source_target_pairs={{0,4},{1,9},{2,6},{3,11},{4,0},{5,13},{6,2},{7,15},{8,12},{9,1},{1... | collective-permute-start | bytes 196616 | tf_op jit(solution)/shard_map/ppermute | solution.py:254
  13.8 4.6 %collective-permute-start.7 = (bf16[128,256]{1,0:T(8,128)(2,1)S(1)}, bf16[128,256]{1,0:T(8,128)(2,1)S(1)}, u32[]{:S(2)}, u32[]{:S(2)}) collective-permute-start(bf16[128,256]{1,0:T(8,128)(2,1)S(1)} %get-tuple-element.45.refs_1_), channel_id=1, source_target_pairs={{0,4},{1,9},{2,6},{3,11},{4,0},{5,13},{6,2},{7,15},{8,12},{9,1},{1... | collective-permute-start | bytes 196616 | tf_op jit(solution)/shard_map/ppermute | solution.py:254
  18.5 5.9 %collective-permute-start.8 = (bf16[128,256]{1,0:T(8,128)(2,1)S(1)}, bf16[128,256]{1,0:T(8,128)(2,1)S(1)}, u32[]{:S(2)}, u32[]{:S(2)}) collective-permute-start(bf16[128,256]{1,0:T(8,128)(2,1)S(1)} %get-tuple-element.46.refs_0_), channel_id=1, source_target_pairs={{0,8},{1,3},{2,10},{3,1},{4,12},{5,7},{6,14},{7,5},{8,0},{9,11},{1... | collective-permute-start | bytes 196616 | tf_op jit(solution)/shard_map/ppermute | solution.py:254
  20.8 5.2 %collective-permute-start.9 = (bf16[128,256]{1,0:T(8,128)(2,1)S(1)}, bf16[128,256]{1,0:T(8,128)(2,1)S(1)}, u32[]{:S(2)}, u32[]{:S(2)}) collective-permute-start(bf16[128,256]{1,0:T(8,128)(2,1)S(1)} %get-tuple-element.47.refs_1_), channel_id=1, source_target_pairs={{0,8},{1,3},{2,10},{3,1},{4,12},{5,7},{6,14},{7,5},{8,0},{9,11},{1... | collective-permute-start | bytes 196616 | tf_op jit(solution)/shard_map/ppermute | solution.py:254
  26.0 1.7 %collective-permute-start.10 = (bf16[128,256]{1,0:T(8,128)(2,1)S(1)}, bf16[128,256]{1,0:T(8,128)(2,1)S(1)}, u32[]{:S(2)}, u32[]{:S(2)}) collective-permute-start(bf16[128,256]{1,0:T(8,128)(2,1)S(1)} %get-tuple-element.48.far), channel_id=1, source_target_pairs={{0,1},{1,0},{2,3},{3,2},{4,5},{5,4},{6,7},{7,6},{8,9},{9,8},{10,11... | collective-permute-start | bytes 196616 | tf_op jit(solution)/shard_map/ppermute | solution.py:238
  26.1 1.7 %collective-permute-start.11 = (bf16[128,256]{1,0:T(8,128)(2,1)S(1)}, bf16[128,256]{1,0:T(8,128)(2,1)S(1)}, u32[]{:S(2)}, u32[]{:S(2)}) collective-permute-start(bf16[128,256]{1,0:T(8,128)(2,1)S(1)} %get-tuple-element.49.near), channel_id=1, source_target_pairs={{0,1},{1,0},{2,3},{3,2},{4,5},{5,4},{6,7},{7,6},{8,9},{9,8},{10,11... | collective-permute-start | bytes 196616 | tf_op jit(solution)/shard_map/ppermute | solution.py:238
  26.6 1.2 %collective-permute-start.12 = (f32[2,1,256]{2,1,0:T(1,128)S(1)}, f32[2,1,256]{2,1,0:T(1,128)S(1)}, u32[]{:S(2)}, u32[]{:S(2)}) collective-permute-start(f32[2,1,256]{2,1,0:T(1,128)S(1)} %get-tuple-element.50), channel_id=1, source_target_pairs={{0,1},{1,0},{2,3},{3,2},{4,5},{5,4},{6,7},{7,6},{8,9},{9,8},{10,11... | collective-permute-start | bytes 6152 | tf_op jit(solution)/shard_map/ppermute | solution.py:238
  28.5 4.3 %collective-permute-start.13 = (bf16[128,256]{1,0:T(8,128)(2,1)S(1)}, bf16[128,256]{1,0:T(8,128)(2,1)S(1)}, u32[]{:S(2)}, u32[]{:S(2)}) collective-permute-start(bf16[128,256]{1,0:T(8,128)(2,1)S(1)} %get-tuple-element.54.refs_0_), channel_id=1, source_target_pairs={{0,2},{1,5},{2,0},{3,7},{4,6},{5,1},{6,4},{7,3},{8,10},{9,13},{10,... | collective-permute-start | bytes 196616 | tf_op jit(solution)/shard_map/ppermute | solution.py:254
  29.3 4.3 %collective-permute-start.14 = (bf16[128,256]{1,0:T(8,128)(2,1)S(1)}, bf16[128,256]{1,0:T(8,128)(2,1)S(1)}, u32[]{:S(2)}, u32[]{:S(2)}) collective-permute-start(bf16[128,256]{1,0:T(8,128)(2,1)S(1)} %get-tuple-element.55.refs_1_), channel_id=1, source_target_pairs={{0,2},{1,5},{2,0},{3,7},{4,6},{5,1},{6,4},{7,3},{8,10},{9,13},{10,... | collective-permute-start | bytes 196616 | tf_op jit(solution)/shard_map/ppermute | solution.py:254
  30.6 16.8 %collective-permute-start.21 = (bf16[2,256,256]{2,1,0:T(8,128)(2,1)S(1)}, bf16[2,256,256]{2,1,0:T(8,128)(2,1)S(1)}, u32[]{:S(2)}, u32[]{:S(2)}) collective-permute-start(bf16[2,256,256]{2,1,0:T(8,128)(2,1)S(1)} %get-tuple-element.63), channel_id=1, source_target_pairs={{0,1},{1,0},{2,3},{3,2},{4,5},{5,4},{6,7},{7,6},{8,9},{9,8},{10,11... | collective-permute-start | bytes 786440 | tf_op jit(solution)/shard_map/ppermute | solution.py:238
  33.6 4.9 %collective-permute-start.15 = (bf16[128,256]{1,0:T(8,128)(2,1)S(1)}, bf16[128,256]{1,0:T(8,128)(2,1)S(1)}, u32[]{:S(2)}, u32[]{:S(2)}) collective-permute-start(bf16[128,256]{1,0:T(8,128)(2,1)S(1)} %get-tuple-element.56.refs_0_), channel_id=1, source_target_pairs={{0,4},{1,9},{2,6},{3,11},{4,0},{5,13},{6,2},{7,15},{8,12},{9,1},{1... | collective-permute-start | bytes 196616 | tf_op jit(solution)/shard_map/ppermute | solution.py:254
  35.3 4.6 %collective-permute-start.16 = (bf16[128,256]{1,0:T(8,128)(2,1)S(1)}, bf16[128,256]{1,0:T(8,128)(2,1)S(1)}, u32[]{:S(2)}, u32[]{:S(2)}) collective-permute-start(bf16[128,256]{1,0:T(8,128)(2,1)S(1)} %get-tuple-element.57.refs_1_), channel_id=1, source_target_pairs={{0,4},{1,9},{2,6},{3,11},{4,0},{5,13},{6,2},{7,15},{8,12},{9,1},{1... | collective-permute-start | bytes 196616 | tf_op jit(solution)/shard_map/ppermute | solution.py:254
  40.0 5.9 %collective-permute-start.17 = (bf16[128,256]{1,0:T(8,128)(2,1)S(1)}, bf16[128,256]{1,0:T(8,128)(2,1)S(1)}, u32[]{:S(2)}, u32[]{:S(2)}) collective-permute-start(bf16[128,256]{1,0:T(8,128)(2,1)S(1)} %get-tuple-element.58.refs_0_), channel_id=1, source_target_pairs={{0,8},{1,3},{2,10},{3,1},{4,12},{5,7},{6,14},{7,5},{8,0},{9,11},{1... | collective-permute-start | bytes 196616 | tf_op jit(solution)/shard_map/ppermute | solution.py:254
  41.6 5.2 %collective-permute-start.18 = (bf16[128,256]{1,0:T(8,128)(2,1)S(1)}, bf16[128,256]{1,0:T(8,128)(2,1)S(1)}, u32[]{:S(2)}, u32[]{:S(2)}) collective-permute-start(bf16[128,256]{1,0:T(8,128)(2,1)S(1)} %get-tuple-element.59.refs_1_), channel_id=1, source_target_pairs={{0,8},{1,3},{2,10},{3,1},{4,12},{5,7},{6,14},{7,5},{8,0},{9,11},{1... | collective-permute-start | bytes 196616 | tf_op jit(solution)/shard_map/ppermute | solution.py:254
  46.8 1.3 %collective-permute-start.19 = (bf16[128,256]{1,0:T(8,128)(2,1)S(1)}, bf16[128,256]{1,0:T(8,128)(2,1)S(1)}, u32[]{:S(2)}, u32[]{:S(2)}) collective-permute-start(bf16[128,256]{1,0:T(8,128)(2,1)S(1)} %get-tuple-element.60.far), channel_id=1, source_target_pairs={{0,1},{1,0},{2,3},{3,2},{4,5},{5,4},{6,7},{7,6},{8,9},{9,8},{10,11... | collective-permute-start | bytes 196616 | tf_op jit(solution)/shard_map/ppermute | solution.py:238
  46.9 1.4 %collective-permute-start.20 = (bf16[128,256]{1,0:T(8,128)(2,1)S(1)}, bf16[128,256]{1,0:T(8,128)(2,1)S(1)}, u32[]{:S(2)}, u32[]{:S(2)}) collective-permute-start(bf16[128,256]{1,0:T(8,128)(2,1)S(1)} %get-tuple-element.61.near), channel_id=1, source_target_pairs={{0,1},{1,0},{2,3},{3,2},{4,5},{5,4},{6,7},{7,6},{8,9},{9,8},{10,11... | collective-permute-start | bytes 196616 | tf_op jit(solution)/shard_map/ppermute | solution.py:238

commit v9 on v8

--- a/solution.py
+++ b/solution.py
@@ -151,21 +151,25 @@
         out_ref[...] = bf16(weight[0] * total)
 
 
-def add_kernel(step, gate, *refs):
-    count = len(refs) // 3
-    for half in range(count):
-        own, other, out_ref = refs[half::count]
-        out_ref[...] = bf16(gate[step, half] * (f32(own[...]) + f32(other[...])))
+def add_kernel(step, gate, both, out_ref):
+    for half in range(2):
+        out_ref[half] = bf16(gate[step, half] * (f32(both[0, half]) + f32(both[1, half])))
+
+
+def pack_kernel(near, far, out_ref):
+    out_ref[0] = near[...]
+    out_ref[1] = far[...]
 
 
 def second_kernel(
-    mine, theirs, near, far, weight, small, energy, amp_ref, other_ref, near_ref, far_ref, half_ref
+    mine, theirs, field, weight, small, energy, amp_ref, other_ref, z_ref, half_ref
 ):
     core = lax.axis_index("rep")
+    far, near = field[0], field[1]
 
     def change(segment):
-        return expand(mine[0, segment], mine[1, segment], near[...]) + expand(
-            theirs[0, segment], theirs[1, segment], far[...]
+        return expand(mine[0, segment], mine[1, segment], near) + expand(
+            theirs[0, segment], theirs[1, segment], far
         )
 
     amp, other = amp_ref[core], other_ref[...]
@@ -173,31 +177,31 @@
     amp = amp + half_step * (energy[core] * turned(amp) + change(core))
     other = other + half_step * (other_energy * turned(other) + change(1 - core))
     half_ref[...] = amp
-    for basis, out_ref, weights in ((mine, near_ref, weight[0]), (theirs, far_ref, small[0])):
+    for half, (basis, weights) in enumerate(((mine, weight[0]), (theirs, small[0]))):
         total = project(basis[0, core], basis[1, core], amp) + project(
             basis[0, 1 - core], basis[1, 1 - core], other
         )
-        out_ref[...] = bf16(weights * total)
-
-
-def other_half_kernel(sent, own_far, near, far, energy, amp_ref, half_ref):
+        z_ref[half] = bf16(weights * total)
+
+
+def other_half_kernel(sent, own_far, field, energy, amp_ref, half_ref):
     core = lax.axis_index("rep")
     amp = amp_ref[1 - core]
-    change = expand(sent[0, core], sent[1, core], near[...]) + expand(own_far[0], own_far[1], far[...])
+    change = expand(sent[0, core], sent[1, core], field[0]) + expand(own_far[0], own_far[1], field[1])
     half_ref[...] = amp + half_step * (energy[1 - core] * turned(amp) + change)
 
 
-def other_last_kernel(sent, own_far, near, far, energy, amp_ref, half_ref, new_ref):
-    core = lax.axis_index("rep")
-    change = expand(sent[0, core], sent[1, core], near[...]) + expand(own_far[0], own_far[1], far[...])
+def other_last_kernel(sent, own_far, field, energy, amp_ref, half_ref, new_ref):
+    core = lax.axis_index("rep")
+    change = expand(sent[0, core], sent[1, core], field[0]) + expand(own_far[0], own_far[1], field[1])
     rate = energy[1 - core] * turned(half_ref[...]) + change
     new_ref[...] = (amp_ref[1 - core] + time_step * rate).T
 
 
-def last_kernel(mine, theirs, near, far, energy, amp_ref, half_ref, other_new, new_tgt, new_proj):
-    core = lax.axis_index("rep")
-    change = expand(mine[0, core], mine[1, core], near[...]) + expand(
-        theirs[0, core], theirs[1, core], far[...]
+def last_kernel(mine, theirs, field, energy, amp_ref, half_ref, other_new, new_tgt, new_proj):
+    core = lax.axis_index("rep")
+    change = expand(mine[0, core], mine[1, core], field[1]) + expand(
+        theirs[0, core], theirs[1, core], field[0]
     )
     rate = energy[core] * turned(half_ref[...]) + change
     my_new = (amp_ref[core] + time_step * rate).T
@@ -246,17 +250,16 @@
     in_vmem = pltpu.VMEM
     basis = in_vmem((2, 2, rows, points), jnp.bfloat16)
     sums = in_vmem((two_cols, points), jnp.bfloat16)
+    both_halves = in_vmem((2, two_cols, points), jnp.bfloat16)
     segment = in_vmem((two_cols, rows), jnp.float32)
 
-    def summed(*halves):
+    def summed(block):
         for step, flips in enumerate(steps):
             pairs = [(me, me ^ flips[me % n_core]) for me in range(n_tgt * n_prj * n_core)]
-            others = [lax.ppermute(block, DEVICES, pairs) for block in halves]
-            halves = run(functools.partial(add_kernel, step), [sums] * 2, gate, *halves, *others)
-        return halves
-
-    def swapped(near, far):
-        return other_core(far), other_core(near)
+            groups = [list(pair) for pair in pairs if pair[0] < pair[1]]
+            both = lax.all_gather(block, DEVICES, axis_index_groups=groups)
+            (block,) = run(functools.partial(add_kernel, step), [both_halves], gate, both)
+        return block
 
     tgt_other, proj_other = other_core(tgt_amp), other_core(proj_amp)
     inputs = (
@@ -301,27 +304,28 @@
     far = other_core(far)
     sent, send_own, small_send, far = lax.optimization_barrier((sent, send_own, small_send, far))
     theirs, own_far, small = other_core(sent), other_core(send_own), other_core(small_send)
-    fields = summed(near, far)
-    near, far, my_half = run(
+    (z,) = run(pack_kernel, [both_halves], near, far)
+    field = summed(z)
+    z, my_half = run(
         second_kernel,
-        [sums, sums, segment],
+        [both_halves, segment],
         mine,
         theirs,
-        *swapped(*fields),
+        other_core(field),
         weight,
         small,
         energy,
         amp,
         other,
     )
-    (other_half,) = run(other_half_kernel, [segment], sent, own_far, *fields, energy, amp)
-    fields = summed(near, far)
+    (other_half,) = run(other_half_kernel, [segment], sent, own_far, field, energy, amp)
+    field = summed(z)
     (other_new,) = run(
         other_last_kernel,
         [in_vmem((rows, two_cols), jnp.float32)],
         sent,
         own_far,
-        *fields,
+        field,
         energy,
         amp,
         other_half,
@@ -334,7 +338,7 @@
         ],
         mine,
         theirs,
-        *swapped(*fields),
+        other_core(field),
         energy,
         amp,
         my_half,

time: 49.5 us -> 49.2 us (level)
  blocking collectives: 0 us -> 38.7 us
  waiting for transfers between devices: 26.1 us -> 2.27 us
  starting transfers between devices: 17.6 us -> 2.17 us
    all_gather x0 -> x6, blocking collectives: none -> 38.7 us  [summed(): both = lax.all_gather(block, DEVICES, axis_index_groups=groups)]
    ppermute x12 -> x0, waiting for transfers between devices: 23.9 us -> none  [summed(): others = [lax.ppermute(block, DEVICES, pairs) for block in halves]]
    ppermute x12 -> x0, starting transfers between devices: 14.9 us -> none  [summed(): others = [lax.ppermute(block, DEVICES, pairs) for block in halves]]
    ppermute x10 -> x8, starting transfers between devices: 2.66 us -> 2.17 us  [other_core(): return lax.ppermute(block, 'rep', [(0, 1), (1, 0)])]
    ppermute x10 -> x8, waiting for transfers between devices: 2.18 us -> 2.27 us  [other_core(): return lax.ppermute(block, 'rep', [(0, 1), (1, 0)])]
    pallas_call x11 -> x12, Pallas kernels: 3.12 us -> 3.12 us  [run(): return call(kernel, out_shape, [VMEM] * len(blocks))(*blocks)]
  transfers between devices with their start and end apart: 22 -> 8, of which waited for: 15 -> 3; matrix products, arithmetic and copies ran while one was open for 0% -> 0% of each run, Pallas kernels for 6% -> 7%
where the time goes in v9:
time: 49.2 us; the launch traced here: 48.9 us
  blocking collectives  38.7 us (79%)
  Pallas kernels  4.99 us (10%)
  waiting for transfers between devices  2.27 us (5%)
  starting transfers between devices  2.17 us (4%)
  between operations  0.74 us (2%)
    all_gather x6, blocking collectives, summed(): both = lax.all_gather(block, DEVICES, axis_index_groups=groups)  38.7 us
    pallas_call x12, Pallas kernels, run(): return call(kernel, out_shape, [VMEM] * len(blocks))(*blocks)  3.12 us
    ppermute x8, waiting for transfers between devices, other_core(): return lax.ppermute(block, 'rep', [(0, 1), (1, 0)])  2.27 us
    ppermute x8, starting transfers between devices, other_core(): return lax.ppermute(block, 'rep', [(0, 1), (1, 0)])  2.17 us
    pallas_call x1, Pallas kernels, shards(): call(functools.partial(load_kernel, gate_steps), [basis, basis, in_vmem((...  1.87 us
  transfers between devices with their start and end apart: 8, of which 3 were waited for; matrix products, arithmetic and copies ran while one was open for 0% of the time, Pallas kernels for 7%

profile of v9, /device:TPU:0, one launch (start us, length us, event | category | flops | bytes accessed | tf_op | source)
XLA Modules:
  0.0 48.9 jit_solution(7067684791029547621)
XLA Ops:
  0.6 0.5 %collective-permute-start = (f32[256,128]{1,0:T(8,128)}, f32[256,128]{1,0:T(8,128)S(1)}, u32[]{:S(2)}, u32[]{:S(2)}) collective-permute-start(f32[256,128]{1,0:T(8,128)} %tgt_own_hbm.1), channel_id=1, source_target_pairs={{0,1},{1,0},{2,3},{3,2},{4,5},{5,4},{6,7},{7,6},{8,9},{9,8},{10,11... | collective-permute-start | bytes 393224 | tf_op jit(solution)/shard_map/ppermute | solution.py:242
  1.2 0.1 collective-permute-start.1
  1.2 1.9 %shard_map.104 = (bf16[2,2,256,256]{3,2,1,0:T(8,128)(2,1)S(1)}, bf16[2,2,256,256]{3,2,1,0:T(8,128)(2,1)S(1)}, bf16[2,256,256]{2,1,0:T(8,128)(2,1)S(1)}, f32[2,1,...) custom-call(s32[2,4]{1,0:T(2,128)} %bitcast.16, ...), custom_call_target="tpu_custom_call" | custom-call | flops 67108864 | bytes 4194304 | tf_op jit(solution)/shard_map/pallas_call | solution.py:276
  3.1 0.3 shard_map.105
  3.5 0.5 %collective-permute-start.2 = (bf16[128,256]{1,0:T(8,128)(2,1)S(1)}, bf16[128,256]{1,0:T(8,128)(2,1)S(1)}, u32[]{:S(2)}, u32[]{:S(2)}) collective-permute-start(bf16[128,256]{1,0:T(8,128)(2,1)S(1)} %get-tuple-element.26), channel_id=1, source_target_pairs={{0,1},{1,0},{2,3},{3,2},{4,5},{5,4},{6,7},{7,6},{8,9},{9,8},{10,11... | collective-permute-start | bytes 196616 | tf_op jit(solution)/shard_map/ppermute | solution.py:242
  4.0 0.9 %collective-permute-done.2.far = bf16[128,256]{1,0:T(8,128)(2,1)S(1)} collective-permute-done((bf16[128,256]{1,0:T(8,128)(2,1)S(1)}, bf16[128,256]{1,0:T(8,128)(2,1)S(1)}, u32[]{:S(2)}, u32[]{:S(2)}) %collective-permute-start.2) | collective-permute-done | bytes 65568 | tf_op jit(solution)/shard_map/ppermute | solution.py:242
  4.9 0.4 collective-permute-start.3
  5.2 6.2 %all-gather = bf16[4,128,256]{2,1,0:T(8,128)(2,1)S(1)} all-gather(bf16[2,128,256]{2,1,0:T(8,128)(2,1)S(1)} %shard_map.106), channel_id=2, replica_groups={{0,2},{1,5},{3,7},{4,6},{8,10},{9,13},{11,15},{12,14},{16,18},{17,21},{..., dimensions={0}, use_global_device_ids=true | all-gather | bytes 393216 | tf_op jit(solution)/shard_map/all_gather | solution.py:260
  11.5 6.7 %all-gather.1 = bf16[4,128,256]{2,1,0:T(8,128)(2,1)S(1)} all-gather(bf16[2,128,256]{2,1,0:T(8,128)(2,1)S(1)} %shard_map.107), channel_id=3, replica_groups={{0,4},{1,9},{2,6},{3,11},{5,13},{7,15},{8,12},{10,14},{16,20},{17,25},{..., dimensions={0}, use_global_device_ids=true | all-gather | bytes 393216 | tf_op jit(solution)/shard_map/all_gather | solution.py:260
  18.3 6.5 %all-gather.2 = bf16[4,128,256]{2,1,0:T(8,128)(2,1)S(1)} all-gather(bf16[2,128,256]{2,1,0:T(8,128)(2,1)S(1)} %shard_map.108), channel_id=4, replica_groups={{0,8},{1,3},{2,10},{4,12},{5,7},{6,14},{9,11},{13,15},{16,24},{17,19},{..., dimensions={0}, use_global_device_ids=true | all-gather | bytes 393216 | tf_op jit(solution)/shard_map/all_gather | solution.py:260
  24.9 0.1 collective-permute-start.4
  25.0 0.5 %collective-permute-start.5 = (f32[2,1,256]{2,1,0:T(1,128)S(1)}, f32[2,1,256]{2,1,0:T(1,128)S(1)}, u32[]{:S(2)}, u32[]{:S(2)}) collective-permute-start(f32[2,1,256]{2,1,0:T(1,128)S(1)} %get-tuple-element.31), channel_id=1, source_target_pairs={{0,1},{1,0},{2,3},{3,2},{4,5},{5,4},{6,7},{7,6},{8,9},{9,8},{10,11... | collective-permute-start | bytes 6152 | tf_op jit(solution)/shard_map/ppermute | solution.py:242
  25.5 0.1 collective-permute-start.7
  25.5 0.8 %collective-permute-done.5.small = f32[2,1,256]{2,1,0:T(1,128)S(1)} collective-permute-done((f32[2,1,256]{2,1,0:T(1,128)S(1)}, f32[2,1,256]{2,1,0:T(1,128)S(1)}, u32[]{:S(2)}, u32[]{:S(2)}) %collective-permute-start.5) | collective-permute-done | bytes 2080 | tf_op jit(solution)/shard_map/ppermute | solution.py:242
  26.3 0.0 collective-permute-done.4.field
  26.3 0.7 %shard_map.110 = (bf16[2,128,256]{2,1,0:T(8,128)(2,1)S(1)}, f32[128,256]{1,0:T(8,128)S(1)}) custom-call(bf16[2,2,256,256]{3,2,1,0:T(8,128)(2,1)S(1)} %get-tuple-element.20.mine, bf16[2,2,256,256]{3,2,1,0:T(8,128)(2,1)S(1)} %collective-permute-done.3.theirs, bf16[2,128,256]{2,1,0:T(8,128)(2,1)S(1)} %collective-permute-done.4.field, ...), custom_call_target="tpu_custom_call" | custom-call | tf_op jit(solution)/shard_map/pallas_call | solution.py:239
  27.1 5.6 %all-gather.3 = bf16[4,128,256]{2,1,0:T(8,128)(2,1)S(1)} all-gather(bf16[2,128,256]{2,1,0:T(8,128)(2,1)S(1)} %get-tuple-element.35), channel_id=5, replica_groups={{0,2},{1,5},{3,7},{4,6},{8,10},{9,13},{11,15},{12,14},{16,18},{17,21},{..., dimensions={0}, use_global_device_ids=true | all-gather | bytes 393216 | tf_op jit(solution)/shard_map/all_gather | solution.py:260
  32.8 7.0 %all-gather.4 = bf16[4,128,256]{2,1,0:T(8,128)(2,1)S(1)} all-gather(bf16[2,128,256]{2,1,0:T(8,128)(2,1)S(1)} %shard_map.111), channel_id=6, replica_groups={{0,4},{1,9},{2,6},{3,11},{5,13},{7,15},{8,12},{10,14},{16,20},{17,25},{..., dimensions={0}, use_global_device_ids=true | all-gather | bytes 393216 | tf_op jit(solution)/shard_map/all_gather | solution.py:260
  39.8 6.5 %all-gather.5 = bf16[4,128,256]{2,1,0:T(8,128)(2,1)S(1)} all-gather(bf16[2,128,256]{2,1,0:T(8,128)(2,1)S(1)} %shard_map.112), channel_id=7, replica_groups={{0,8},{1,3},{2,10},{4,12},{5,7},{6,14},{9,11},{13,15},{16,24},{17,19},{..., dimensions={0}, use_global_device_ids=true | all-gather | bytes 393216 | tf_op jit(solution)/shard_map/all_gather | solution.py:260
  46.4 0.1 collective-permute-start.6
  46.5 0.3 shard_map.114.half_ref
  46.8 0.4 shard_map.115.other_new
  47.2 0.6 %collective-permute-done.6.field = bf16[2,128,256]{2,1,0:T(8,128)(2,1)S(1)} collective-permute-done((bf16[2,128,256]{2,1,0:T(8,128)(2,1)S(1)}, bf16[2,128,256]{2,1,0:T(8,128)(2,1)S(1)}, u32[]{:S(2)}, u32[]{:S(2)}) %collective-permute-start.6) | collective-permute-done | bytes 131104 | tf_op jit(solution)/shard_map/ppermute | solution.py:242
  47.8 1.1 %shard_map.116 = (f32[256,128]{1,0:T(8,128)}, f32[1,256,128]{2,1,0:T(8,128)}) custom-call(bf16[2,2,256,256]{3,2,1,0:T(8,128)(2,1)S(1)} %get-tuple-element.20.mine, bf16[2,2,256,256]{3,2,1,0:T(8,128)(2,1)S(1)} %collective-permute-done.3.theirs, bf16[2,128,256]{2,1,0:T(8,128)(2,1)S(1)} %collective-permute-done.6.field, ...), custom_call_target="tpu_custom_call" | custom-call | tf_op jit(solution)/shard_map/pallas_call | solution.py:239
  (11 shorter events, 0.3 us)
Async XLA Ops:
  0.6 2.5 %collective-permute-start = (f32[256,128]{1,0:T(8,128)}, f32[256,128]{1,0:T(8,128)S(1)}, u32[]{:S(2)}, u32[]{:S(2)}) collective-permute-start(f32[256,128]{1,0:T(8,128)} %tgt_own_hbm.1), channel_id=1, source_target_pairs={{0,1},{1,0},{2,3},{3,2},{4,5},{5,4},{6,7},{7,6},{8,9},{9,8},{10,11... | collective-permute-start | bytes 393224 | tf_op jit(solution)/shard_map/ppermute | solution.py:242
  1.2 2.0 %collective-permute-start.1 = (f32[1,256,128]{2,1,0:T(8,128)}, f32[1,256,128]{2,1,0:T(8,128)S(1)}, u32[]{:S(2)}, u32[]{:S(2)}) collective-permute-start(f32[1,256,128]{2,1,0:T(8,128)} %proj_own_hbm.1), channel_id=1, source_target_pairs={{0,1},{1,0},{2,3},{3,2},{4,5},{5,4},{6,7},{7,6},{8,9},{9,8},{10,11... | collective-permute-start | bytes 393224 | tf_op jit(solution)/shard_map/ppermute | solution.py:242
  3.5 1.4 %collective-permute-start.2 = (bf16[128,256]{1,0:T(8,128)(2,1)S(1)}, bf16[128,256]{1,0:T(8,128)(2,1)S(1)}, u32[]{:S(2)}, u32[]{:S(2)}) collective-permute-start(bf16[128,256]{1,0:T(8,128)(2,1)S(1)} %get-tuple-element.26), channel_id=1, source_target_pairs={{0,1},{1,0},{2,3},{3,2},{4,5},{5,4},{6,7},{7,6},{8,9},{9,8},{10,11... | collective-permute-start | bytes 196616 | tf_op jit(solution)/shard_map/ppermute | solution.py:242
  4.9 21.4 %collective-permute-start.3 = (bf16[2,2,256,256]{3,2,1,0:T(8,128)(2,1)S(1)}, bf16[2,2,256,256]{3,2,1,0:T(8,128)(2,1)S(1)}, u32[]{:S(2)}, u32[]{:S(2)}) collective-permute-start(bf16[2,2,256,256]{3,2,1,0:T(8,128)(2,1)S(1)} %get-tuple-element.27.sent), channel_id=1, source_target_pairs={{0,1},{1,0},{2,3},{3,2},{4,5},{5,4},{6,7},{7,6},{8,9},{9,8},{10,11... | collective-permute-start | bytes 1572872 | tf_op jit(solution)/shard_map/ppermute | solution.py:242
  24.9 1.4 %collective-permute-start.4 = (bf16[2,128,256]{2,1,0:T(8,128)(2,1)S(1)}, bf16[2,128,256]{2,1,0:T(8,128)(2,1)S(1)}, u32[]{:S(2)}, u32[]{:S(2)}) collective-permute-start(bf16[2,128,256]{2,1,0:T(8,128)(2,1)S(1)} %shard_map.109.field), channel_id=1, source_target_pairs={{0,1},{1,0},{2,3},{3,2},{4,5},{5,4},{6,7},{7,6},{8,9},{9,8},{10,11... | collective-permute-start | bytes 393224 | tf_op jit(solution)/shard_map/ppermute | solution.py:242
  25.0 1.3 %collective-permute-start.5 = (f32[2,1,256]{2,1,0:T(1,128)S(1)}, f32[2,1,256]{2,1,0:T(1,128)S(1)}, u32[]{:S(2)}, u32[]{:S(2)}) collective-permute-start(f32[2,1,256]{2,1,0:T(1,128)S(1)} %get-tuple-element.31), channel_id=1, source_target_pairs={{0,1},{1,0},{2,3},{3,2},{4,5},{5,4},{6,7},{7,6},{8,9},{9,8},{10,11... | collective-permute-start | bytes 6152 | tf_op jit(solution)/shard_map/ppermute | solution.py:242
  25.5 21.0 %collective-permute-start.7 = (bf16[2,256,256]{2,1,0:T(8,128)(2,1)S(1)}, bf16[2,256,256]{2,1,0:T(8,128)(2,1)S(1)}, u32[]{:S(2)}, u32[]{:S(2)}) collective-permute-start(bf16[2,256,256]{2,1,0:T(8,128)(2,1)S(1)} %get-tuple-element.37), channel_id=1, source_target_pairs={{0,1},{1,0},{2,3},{3,2},{4,5},{5,4},{6,7},{7,6},{8,9},{9,8},{10,11... | collective-permute-start | bytes 786440 | tf_op jit(solution)/shard_map/ppermute | solution.py:242
  46.4 1.4 %collective-permute-start.6 = (bf16[2,128,256]{2,1,0:T(8,128)(2,1)S(1)}, bf16[2,128,256]{2,1,0:T(8,128)(2,1)S(1)}, u32[]{:S(2)}, u32[]{:S(2)}) collective-permute-start(bf16[2,128,256]{2,1,0:T(8,128)(2,1)S(1)} %shard_map.113.field), channel_id=1, source_target_pairs={{0,1},{1,0},{2,3},{3,2},{4,5},{5,4},{6,7},{7,6},{8,9},{9,8},{10,11... | collective-permute-start | bytes 393224 | tf_op jit(solution)/shard_map/ppermute | solution.py:242

commit v10 on v8

v10 whole, which is shorter than its diff:
```python
import functools

import jax
import jax.numpy as jnp
from jax import lax
from jax.experimental import pallas as pl
from jax.experimental.pallas import tpu as pltpu
from jax.sharding import PartitionSpec as P

time_step = 0.4
half_step = 0.5 * time_step
VMEM_LIMIT = 8 * 1024 * 1024
DEVICES = ("tgt", "prj", "rep")
HBM = pl.BlockSpec(memory_space=pl.ANY)
VMEM = pl.BlockSpec(memory_space=pltpu.VMEM)


def parity(place):
    odd = 0
    while place:
        odd, place = odd ^ (place & 1), place >> 1
    return odd


def my_kind():
    n_tgt, n_prj = lax.axis_size("tgt"), lax.axis_size("prj")
    place = lax.axis_index("tgt") * n_prj + lax.axis_index("prj")
    kind = lax.axis_index("rep")
    for bit in range((n_tgt * n_prj).bit_length() - 1):
        kind = jnp.bitwise_xor(kind, jnp.bitwise_and(lax.shift_right_logical(place, bit), 1))
    return kind


def ordered(core, first, second):
    return jnp.where(core == 0, first, second), jnp.where(core == 0, second, first)


def turned(block):
    half = block.shape[0] // 2
    return jnp.concatenate([block[half:], -block[:half]], axis=0)


def bf16(block):
    return block.astype(jnp.bfloat16)


def f32(block):
    return block.astype(jnp.float32)


def project(basis_real, basis_imag, amp):
    return jnp.dot(bf16(amp), basis_real, preferred_element_type=jnp.float32) + jnp.dot(
        bf16(turned(amp)), basis_imag, preferred_element_type=jnp.float32
    )


def expand(basis_real, basis_imag, field):
    contract = (((1,), (1,)), ((), ()))
    return lax.dot_general(
        turned(field), basis_real, contract, preferred_element_type=jnp.float32
    ) + lax.dot_general(field, basis_imag, contract, preferred_element_type=jnp.float32)


def load_kernel(
    weight_hbm,
    tgt_hbm,
    proj_hbm,
    tgt_own_hbm,
    proj_own_hbm,
    mine,
    sent,
    weight,
    amp_ref,
    part_ref,
    flat_weight,
    tgt_own,
    proj_own,
    sems,
):
    core = lax.axis_index("rep")
    my = my_kind()
    sources = (
        tgt_hbm.at[:, pl.ds(2 * lax.axis_index("prj"), 2)],
        proj_hbm.at[:, pl.ds(2 * lax.axis_index("tgt"), 2)],
    )

    def basis_copies(kind):
        return [
            pltpu.make_async_copy(sources[source].at[part], basis.at[part], sems.at[2 * slot + part])
            for slot, (source, basis) in enumerate(((kind, mine), (1 - kind, sent)))
            for part in range(2)
        ]

    pairs = [(tgt_own_hbm, tgt_own), (proj_own_hbm, proj_own), (weight_hbm, flat_weight)]
    copies = [pltpu.make_async_copy(src, dst, sems.at[4 + k]) for k, (src, dst) in enumerate(pairs)]
    for copy in copies:
        copy.start()
    for kind in range(2):

        @pl.when(my == kind)
        def _():
            for copy in basis_copies(kind):
                copy.start()

    for copy in copies:
        copy.wait()
    weight[0] = flat_weight[...][None, :]
    amp_ref[0] = tgt_own[...].T
    amp_ref[1] = proj_own[0].T
    for copy in basis_copies(0):
        copy.wait()
    for slot, (basis, kind) in enumerate(((mine, my), (sent, 1 - my))):
        part_ref[slot] = project(basis[0, core], basis[1, core], amp_ref[kind])


def first_kernel(mine, sent, weight, part_ref, tgt_other, proj_other, near_ref, swap_ref, other_ref):
    core = lax.axis_index("rep")
    my = my_kind()
    my_amp, other_amp = ordered(my, tgt_other[...].T, proj_other[0].T)
    other_ref[...] = my_amp
    for slot, (basis, amp, out_ref) in enumerate(((mine, my_amp, near_ref), (sent, other_amp, swap_ref))):
        total = part_ref[slot] + project(basis[0, 1 - core], basis[1, 1 - core], amp)
        out_ref[...] = bf16(weight[0] * total)


def side_kernel(
    gate_steps,
    flags_hbm,
    counts_hbm,
    weight,
    tgt_energy_hbm,
    proj_energy_hbm,
    mine,
    near,
    gate,
    energy,
    small_send,
    send_own,
    flags,
    counts,
    flat_energy,
    sems,
):
    core = lax.axis_index("rep")
    my = my_kind()
    tgt_index = lax.axis_index("tgt")
    prj_index = lax.axis_index("prj")
    pairs = [
        (flags_hbm, flags),
        (counts_hbm, counts),
        (tgt_energy_hbm, flat_energy),
        (proj_energy_hbm, energy.at[1]),
    ]
    copies = [pltpu.make_async_copy(src, dst, sems.at[k]) for k, (src, dst) in enumerate(pairs)]
    for copy in copies:
        copy.start()
    for part in range(2):
        send_own[part] = mine[part, 1 - core]
    for copy in copies:
        copy.wait()
    energy[0] = flat_energy[...][None, :]
    small_send[0] = weight[0]
    small_send[1, :, : energy.shape[2]] = energy[1 - my]
    tiles = 2
    width = gate.shape[-1] // tiles
    gate_step = jnp.where(my == 0, *gate_steps)
    for half in range(2):
        for tile in range(tiles):
            live = jnp.logical_and(
                flags[prj_index, tgt_index] > 0, tiles * half + tile < counts[prj_index, tgt_index]
            )
            value = jnp.where(live, 1.0, 0.0).astype(jnp.float32)
            for step in range(gate.shape[0]):
                here = jnp.where(step == gate_step, value, jnp.float32(1.0))
                gate[step, half, :, tile * width : (tile + 1) * width] = jnp.full(
                    (1, width), here, jnp.float32
                )


def pack_kernel(near, far, low, high):
    low[...], high[...] = ordered(lax.axis_index("rep"), near[...], far[...])


def add_kernel(step, half, gate, own, other, out_ref):
    out_ref[...] = bf16(gate[step, half] * (f32(own[...]) + f32(other[...])))


def second_kernel(
    mine, theirs, low, high, weight, small, energy, amp_ref, other_ref, low_ref, high_ref, half_ref
):
    core = lax.axis_index("rep")
    my = my_kind()
    near, far = ordered(core, low[...], high[...])

    def change(segment):
        return expand(mine[0, segment], mine[1, segment], near) + expand(
            theirs[0, segment], theirs[1, segment], far
        )

    amp, other = amp_ref[my], other_ref[...]
    other_energy = small[1, :, : energy.shape[2]]
    amp = amp + half_step * (energy[my] * turned(amp) + change(core))
    other = other + half_step * (other_energy * turned(other) + change(1 - core))
    half_ref[...] = amp
    near, far = [
        bf16(
            weights
            * (
                project(basis[0, core], basis[1, core], amp)
                + project(basis[0, 1 - core], basis[1, 1 - core], other)
            )
        )
        for basis, weights in ((mine, weight[0]), (theirs, small[0]))
    ]
    low_ref[...], high_ref[...] = ordered(core, near, far)


def other_half_kernel(sent, own_far, low, high, energy, amp_ref, half_ref):
    core = lax.axis_index("rep")
    kind = 1 - my_kind()
    near, far = ordered(core, low[...], high[...])
    amp = amp_ref[kind]
    change = expand(sent[0, core], sent[1, core], near) + expand(own_far[0], own_far[1], far)
    half_ref[...] = amp + half_step * (energy[kind] * turned(amp) + change)


def other_last_kernel(sent, own_far, low, high, energy, amp_ref, half_ref, new_ref):
    core = lax.axis_index("rep")
    kind = 1 - my_kind()
    near, far = ordered(core, low[...], high[...])
    change = expand(sent[0, core], sent[1, core], near) + expand(own_far[0], own_far[1], far)
    rate = energy[kind] * turned(half_ref[...]) + change
    new_ref[...] = (amp_ref[kind] + time_step * rate).T


def last_kernel(mine, theirs, low, high, energy, amp_ref, half_ref, other_new, new_tgt, new_proj):
    core = lax.axis_index("rep")
    my = my_kind()
    near, far = ordered(core, low[...], high[...])
    change = expand(mine[0, core], mine[1, core], near) + expand(theirs[0, core], theirs[1, core], far)
    rate = energy[my] * turned(half_ref[...]) + change
    my_new = (amp_ref[my] + time_step * rate).T
    new_tgt[...], new_proj[0] = ordered(my, my_new, other_new[...])


def shards(
    tgt_basis,
    proj_basis,
    quad_weight,
    tgt_energy,
    proj_energy,
    pair_flags,
    tile_counts,
    tgt_amp,
    proj_amp,
):
    points = quad_weight.shape[0]
    rows, two_cols = tgt_amp.shape
    sizes = [lax.axis_size(axis) for axis in DEVICES]

    def call(kernel, out_shape, in_specs, scratch_shapes=(), cost=None):
        return pl.pallas_call(
            kernel,
            out_shape=out_shape,
            in_specs=in_specs,
            out_specs=[VMEM] * len(out_shape),
            scratch_shapes=scratch_shapes,
            cost_estimate=cost,
            compiler_params=pltpu.CompilerParams(vmem_limit_bytes=VMEM_LIMIT),
        )

    def run(kernel, out_shape, *blocks):
        return call(kernel, out_shape, [VMEM] * len(blocks))(*blocks)

    def other_core(block):
        return lax.ppermute(block, "rep", [(0, 1), (1, 0)])

    n_tgt, n_prj, n_core = sizes
    tgt_flips = [n_prj << bit for bit in range(n_tgt.bit_length() - 1)]
    prj_flips = [1 << bit for bit in range(n_prj.bit_length() - 1)]
    flips = [(prj_flips + along_tgt, along_tgt + prj_flips) for along_tgt in (tgt_flips, tgt_flips[::-1])]
    gate_steps = (len(prj_flips) - 1, len(tgt_flips) - 1)
    n_steps = len(tgt_flips) + len(prj_flips)

    def step_pairs(half, step):
        pairs = []
        for place in range(n_tgt * n_prj):
            for kind in range(2):
                there = place ^ flips[half][kind][step]
                pairs.append((place * n_core + (kind ^ parity(place)), there * n_core + (kind ^ parity(there))))
        return pairs

    in_vmem = pltpu.VMEM
    basis = in_vmem((2, 2, rows, points), jnp.bfloat16)
    sums = in_vmem((two_cols, points), jnp.bfloat16)
    segment = in_vmem((two_cols, rows), jnp.float32)

    def summed(*halves):
        totals = []
        for half, block in enumerate(halves):
            for step in range(n_steps):
                other = lax.ppermute(block, DEVICES, step_pairs(half, step))
                (block,) = run(functools.partial(add_kernel, step, half), [sums], gate, block, other)
            totals.append(block)
        return totals

    def swapped(fields):
        return [other_core(block) for block in fields]

    tgt_other, proj_other = other_core(tgt_amp), other_core(proj_amp)
    def in_hbm(*blocks):
        return [pltpu.with_memory_space_constraint(block, pltpu.HBM) for block in blocks]

    mine, sent, weight, amp, part = call(
        load_kernel,
        [
            basis,
            basis,
            in_vmem((1, 1, points), jnp.float32),
            in_vmem((2, two_cols, rows), jnp.float32),
            in_vmem((2, two_cols, points), jnp.float32),
        ],
        [HBM] * 5,
        [
            pltpu.VMEM((points,), jnp.float32),
            pltpu.VMEM(tgt_amp.shape, jnp.float32),
            pltpu.VMEM(proj_amp.shape, jnp.float32),
            pltpu.SemaphoreType.DMA((7,)),
        ],
        pl.CostEstimate(
            flops=2 * 4 * rows * two_cols * points, bytes_accessed=4 * 1024 * 1024, transcendentals=0
        ),
    )(*in_hbm(quad_weight, tgt_basis.reshape(2, -1, rows, points), proj_basis, tgt_amp, proj_amp))
    near, swap, other = run(
        first_kernel, [sums, sums, segment], mine, sent, weight, part, tgt_other, proj_other
    )
    far = other_core(swap)
    flags, counts = pair_flags.T, tile_counts.T
    gate, energy, small_send, send_own = call(
        functools.partial(side_kernel, gate_steps),
        [
            in_vmem((n_steps, 2, 1, points), jnp.float32),
            in_vmem((2, 1, rows), jnp.float32),
            in_vmem((2, 1, points), jnp.float32),
            in_vmem((2, rows, points), jnp.bfloat16),
        ],
        [HBM, HBM, VMEM, HBM, HBM, VMEM, VMEM],
        [
            pltpu.SMEM(flags.shape, jnp.int32),
            pltpu.SMEM(counts.shape, jnp.int32),
            pltpu.VMEM((rows,), jnp.float32),
            pltpu.SemaphoreType.DMA((4,)),
        ],
    )(*in_hbm(flags, counts), weight, *in_hbm(tgt_energy, proj_energy), mine, near)
    sent, far = lax.optimization_barrier((sent, far))
    theirs, own_far, small = other_core(sent), other_core(send_own), other_core(small_send)
    near, far = run(pack_kernel, [sums, sums], near, far)
    fields = summed(near, far)
    near, far, my_half = run(
        second_kernel,
        [sums, sums, segment],
        mine,
        theirs,
        *swapped(fields),
        weight,
        small,
        energy,
        amp,
        other,
    )
    (other_half,) = run(other_half_kernel, [segment], sent, own_far, *fields, energy, amp)
    fields = summed(near, far)
    (other_new,) = run(
        other_last_kernel,
        [in_vmem((rows, two_cols), jnp.float32)],
        sent,
        own_far,
        *fields,
        energy,
        amp,
        other_half,
    )
    return run(
        last_kernel,
        [
            jax.ShapeDtypeStruct(tgt_amp.shape, jnp.float32),
            jax.ShapeDtypeStruct(proj_amp.shape, jnp.float32),
        ],
        mine,
        theirs,
        *swapped(fields),
        energy,
        amp,
        my_half,
        other_new,
    )


def solution(mesh):
    in_specs = (
        P(None, "tgt", "rep"),
        P(None, None, "prj", "rep"),
        P(("bpar", "rep")),
        P(("tgt", "prj", "rep")),
        P(("tgt", "rep"), "prj"),
        P("bpar", None),
        P("bpar", None),
        P(("bpar", "tgt", "prj", "rep"), None),
        P(("bpar", "tgt", "rep"), "prj", None),
    )
    out_specs = (P(("bpar", "tgt", "prj", "rep"), None), P(("bpar", "tgt", "rep"), "prj", None))

    def step(*args):
        return tuple(shards(*args))

    return jax.shard_map(step, mesh=mesh, in_specs=in_specs, out_specs=out_specs, check_vma=False)
```

time: 49.5 us -> 40.4 us (0.82)
  waiting for transfers between devices: 26.1 us -> 7.19 us
  starting transfers between devices: 17.6 us -> 26.7 us
  Pallas kernels: 4.99 us -> 5.6 us
    ppermute x12, waiting for transfers between devices: 23.9 us -> 5.02 us  [summed(): other = lax.ppermute(block, DEVICES, step_pairs(half, step))]
    ppermute x10, starting transfers between devices: 2.66 us -> 7.25 us  [other_core(): return lax.ppermute(block, 'rep', [(0, 1), (1, 0)])]
    ppermute x12, starting transfers between devices: 14.9 us -> 19.4 us  [summed(): other = lax.ppermute(block, DEVICES, step_pairs(half, step))]
    pallas_call x1 -> x2, Pallas kernels: 1.87 us -> 2.39 us  [the longest x1 1.64 us: shards(): call(load_kernel, [basis, basis, in_vmem((1, 1, points), jnp.float32), in...]
    pallas_call x11 -> x18, Pallas kernels: 3.12 us -> 3.2 us  [run(): return call(kernel, out_shape, [VMEM] * len(blocks))(*blocks)]
  transfers between devices with their start and end apart: 22 -> 22, of which waited for: 15 -> 11; matrix products, arithmetic and copies ran while one was open for 0% -> 0% of each run, Pallas kernels for 6% -> 8%
where the time goes in v10:
time: 40.4 us; the launch traced here: 40.2 us
  starting transfers between devices  26.7 us (66%)
  waiting for transfers between devices  7.19 us (18%)
  Pallas kernels  5.6 us (14%)
  between operations  0.76 us (2%)
    ppermute x12, starting transfers between devices, summed(): other = lax.ppermute(block, DEVICES, step_pairs(half, step))  19.4 us
    ppermute x10, starting transfers between devices, other_core(): return lax.ppermute(block, 'rep', [(0, 1), (1, 0)])  7.25 us
    ppermute x12, waiting for transfers between devices, summed(): other = lax.ppermute(block, DEVICES, step_pairs(half, step))  5.02 us
    pallas_call x18, Pallas kernels, run(): return call(kernel, out_shape, [VMEM] * len(blocks))(*blocks)  3.2 us
    ppermute x10, waiting for transfers between devices, other_core(): return lax.ppermute(block, 'rep', [(0, 1), (1, 0)])  2.17 us
    pallas_call x1, Pallas kernels, shards(): call(load_kernel, [basis, basis, in_vmem((1, 1, points), jnp.float32), in...  1.64 us
  transfers between devices with their start and end apart: 22, of which 11 were waited for; matrix products, arithmetic and copies ran while one was open for 0% of the time, Pallas kernels for 8%

profile of v10, /device:TPU:0, one launch (start us, length us, event | category | flops | bytes accessed | tf_op | source)
XLA Modules:
  0.0 40.2 jit_solution(12955023656780099791)
XLA Ops:
  1.2 1.6 %shard_map.104 = (bf16[2,2,256,256]{3,2,1,0:T(8,128)(2,1)S(1)}, bf16[2,2,256,256]{3,2,1,0:T(8,128)(2,1)S(1)}, f32[1,1,256]{2,1,0:T(1,128)S(1)}, f32[2,128,256]{2,1,0:T(8,128)S(1)}, f32[2,128,256]{2,1,0:T(8,128)S(1)}) custom-call(f32[256]{0:T(256)} %weight_hbm.1, bf16[2,4,256,256]{3,2,1,0:T(8,128)(2,1)} %bitcast.3, bf16[2,8,256,256]{3,2,1,0:T(8,128)(2,1)} %proj_hbm.1, ...), custom_call_target="tpu_custom_call" | custom-call | flops 67108864 | bytes 4194304 | tf_op jit(solution)/shard_map/pallas_call | solution.py:314
  3.7 0.9 %collective-permute-done.2.far = bf16[128,256]{1,0:T(8,128)(2,1)S(1)} collective-permute-done((bf16[128,256]{1,0:T(8,128)(2,1)S(1)}, bf16[128,256]{1,0:T(8,128)(2,1)S(1)}, u32[]{:S(2)}, u32[]{:S(2)}) %collective-permute-start.2) | collective-permute-done | bytes 65568 | tf_op jit(solution)/shard_map/ppermute | solution.py:276
  5.0 2.7 %collective-permute-start.4 = (bf16[128,256]{1,0:T(8,128)(2,1)S(1)}, bf16[128,256]{1,0:T(8,128)(2,1)S(1)}, u32[]{:S(2)}, u32[]{:S(2)}) collective-permute-start(bf16[128,256]{1,0:T(8,128)(2,1)S(1)} %get-tuple-element.30.own), channel_id=1, source_target_pairs={{0,3},{1,4},{3,0},{2,7},{5,6},{4,1},{6,5},{7,2},{9,10},{8,13},{10,... | collective-permute-start | bytes 196616 | tf_op jit(solution)/shard_map/ppermute | solution.py:302
  7.7 0.8 %shard_map.106 = (f32[3,2,1,256]{3,2,1,0:T(1,128)S(1)}, f32[2,1,256]{2,1,0:T(1,128)S(1)}, f32[2,1,256]{2,1,0:T(1,128)S(1)}, bf16[2,256,256]{2,1,0:T(8,128)(2,1)S(1)}) custom-call(s32[2,4]{1,0:T(2,128)} %bitcast.4, s32[2,4]{1,0:T(2,128)} %bitcast.5, f32[1,1,256]{2,1,0:T(1,128)S(1)} %get-tuple-element.23.weight, f32[256]{0:T(256)} %tgt_energy_hbm.1, ...), custom_call_target="tpu_custom_call" | custom-call | tf_op jit(solution)/shard_map/pallas_call | solution.py:339
  8.5 1.1 %collective-permute-done.4.other = bf16[128,256]{1,0:T(8,128)(2,1)S(1)} collective-permute-done((bf16[128,256]{1,0:T(8,128)(2,1)S(1)}, bf16[128,256]{1,0:T(8,128)(2,1)S(1)}, u32[]{:S(2)}, u32[]{:S(2)}) %collective-permute-start.4) | collective-permute-done | bytes 65568 | tf_op jit(solution)/shard_map/ppermute | solution.py:302
  9.6 1.9 %collective-permute-start.5 = (bf16[128,256]{1,0:T(8,128)(2,1)S(1)}, bf16[128,256]{1,0:T(8,128)(2,1)S(1)}, u32[]{:S(2)}, u32[]{:S(2)}) collective-permute-start(bf16[128,256]{1,0:T(8,128)(2,1)S(1)} %shard_map.108.own), channel_id=1, source_target_pairs={{0,5},{1,8},{3,6},{2,11},{5,0},{4,13},{6,3},{7,14},{9,12},{8,1},{1... | collective-permute-start | bytes 196616 | tf_op jit(solution)/shard_map/ppermute | solution.py:302
  11.6 2.5 %collective-permute-start.9 = (bf16[128,256]{1,0:T(8,128)(2,1)S(1)}, bf16[128,256]{1,0:T(8,128)(2,1)S(1)}, u32[]{:S(2)}, u32[]{:S(2)}) collective-permute-start(bf16[128,256]{1,0:T(8,128)(2,1)S(1)} %shard_map.111.own), channel_id=1, source_target_pairs={{0,9},{1,4},{3,10},{2,7},{5,12},{4,1},{6,15},{7,2},{9,0},{8,13},{1... | collective-permute-start | bytes 196616 | tf_op jit(solution)/shard_map/ppermute | solution.py:302
  14.1 2.6 %collective-permute-start.6 = (bf16[128,256]{1,0:T(8,128)(2,1)S(1)}, bf16[128,256]{1,0:T(8,128)(2,1)S(1)}, u32[]{:S(2)}, u32[]{:S(2)}) collective-permute-start(bf16[128,256]{1,0:T(8,128)(2,1)S(1)} %shard_map.109.own), channel_id=1, source_target_pairs={{0,9},{1,2},{3,10},{2,1},{5,12},{4,7},{6,15},{7,4},{9,0},{8,11},{1... | collective-permute-start | bytes 196616 | tf_op jit(solution)/shard_map/ppermute | solution.py:302
  17.1 0.8 %collective-permute-start.10 = (bf16[128,256]{1,0:T(8,128)(2,1)S(1)}, bf16[128,256]{1,0:T(8,128)(2,1)S(1)}, u32[]{:S(2)}, u32[]{:S(2)}) collective-permute-start(bf16[128,256]{1,0:T(8,128)(2,1)S(1)} %shard_map.112.own), channel_id=1, source_target_pairs={{0,5},{1,2},{3,6},{2,1},{5,0},{4,7},{6,3},{7,4},{9,12},{8,11},{10,... | collective-permute-start | bytes 196616 | tf_op jit(solution)/shard_map/ppermute | solution.py:302
  17.9 0.9 %collective-permute-done.6.other = bf16[128,256]{1,0:T(8,128)(2,1)S(1)} collective-permute-done((bf16[128,256]{1,0:T(8,128)(2,1)S(1)}, bf16[128,256]{1,0:T(8,128)(2,1)S(1)}, u32[]{:S(2)}, u32[]{:S(2)}) %collective-permute-start.6) | collective-permute-done | bytes 65568 | tf_op jit(solution)/shard_map/ppermute | solution.py:302
  18.8 2.2 %collective-permute-start.7 = (bf16[128,256]{1,0:T(8,128)(2,1)S(1)}, bf16[128,256]{1,0:T(8,128)(2,1)S(1)}, u32[]{:S(2)}, u32[]{:S(2)}) collective-permute-start(bf16[128,256]{1,0:T(8,128)(2,1)S(1)} %shard_map.110.low), channel_id=1, source_target_pairs={{0,1},{1,0},{2,3},{3,2},{4,5},{5,4},{6,7},{7,6},{8,9},{9,8},{10,11... | collective-permute-start | bytes 196616 | tf_op jit(solution)/shard_map/ppermute | solution.py:276
  21.1 0.6 %collective-permute-start.11 = (bf16[128,256]{1,0:T(8,128)(2,1)S(1)}, bf16[128,256]{1,0:T(8,128)(2,1)S(1)}, u32[]{:S(2)}, u32[]{:S(2)}) collective-permute-start(bf16[128,256]{1,0:T(8,128)(2,1)S(1)} %shard_map.113.high), channel_id=1, source_target_pairs={{0,1},{1,0},{2,3},{3,2},{4,5},{5,4},{6,7},{7,6},{8,9},{9,8},{10,11... | collective-permute-start | bytes 196616 | tf_op jit(solution)/shard_map/ppermute | solution.py:276
  21.8 1.1 %collective-permute-done.12.small = f32[2,1,256]{2,1,0:T(1,128)S(1)} collective-permute-done((f32[2,1,256]{2,1,0:T(1,128)S(1)}, f32[2,1,256]{2,1,0:T(1,128)S(1)}, u32[]{:S(2)}, u32[]{:S(2)}) %collective-permute-start.12) | collective-permute-done | bytes 2080 | tf_op jit(solution)/shard_map/ppermute | solution.py:276
  22.9 0.8 %shard_map.114 = (bf16[128,256]{1,0:T(8,128)(2,1)S(1)}, bf16[128,256]{1,0:T(8,128)(2,1)S(1)}, f32[128,256]{1,0:T(8,128)S(1)}) custom-call(bf16[2,2,256,256]{3,2,1,0:T(8,128)(2,1)S(1)} %get-tuple-element.21.mine, bf16[2,2,256,256]{3,2,1,0:T(8,128)(2,1)S(1)} %collective-permute-done.3.theirs, bf16[128,256]{1,0:T(8,128)(2,1)S(1)} %collective-permute-done.7.low, ...), custom_call_target="tpu_custom_call" | custom-call | tf_op jit(solution)/shard_map/pallas_call | solution.py:273
  23.7 1.2 %collective-permute-start.13 = (bf16[128,256]{1,0:T(8,128)(2,1)S(1)}, bf16[128,256]{1,0:T(8,128)(2,1)S(1)}, u32[]{:S(2)}, u32[]{:S(2)}) collective-permute-start(bf16[128,256]{1,0:T(8,128)(2,1)S(1)} %get-tuple-element.36.own), channel_id=1, source_target_pairs={{0,3},{1,4},{3,0},{2,7},{5,6},{4,1},{6,5},{7,2},{9,10},{8,13},{10,... | collective-permute-start | bytes 196616 | tf_op jit(solution)/shard_map/ppermute | solution.py:302
  24.9 0.6 %collective-permute-start.17 = (bf16[128,256]{1,0:T(8,128)(2,1)S(1)}, bf16[128,256]{1,0:T(8,128)(2,1)S(1)}, u32[]{:S(2)}, u32[]{:S(2)}) collective-permute-start(bf16[128,256]{1,0:T(8,128)(2,1)S(1)} %get-tuple-element.37.own), channel_id=1, source_target_pairs={{0,3},{1,8},{3,0},{2,11},{5,6},{4,13},{6,5},{7,14},{9,10},{8,1},{1... | collective-permute-start | bytes 196616 | tf_op jit(solution)/shard_map/ppermute | solution.py:302
  25.5 1.7 %collective-permute-start.21 = (bf16[2,256,256]{2,1,0:T(8,128)(2,1)S(1)}, bf16[2,256,256]{2,1,0:T(8,128)(2,1)S(1)}, u32[]{:S(2)}, u32[]{:S(2)}) collective-permute-start(bf16[2,256,256]{2,1,0:T(8,128)(2,1)S(1)} %get-tuple-element.39), channel_id=1, source_target_pairs={{0,1},{1,0},{2,3},{3,2},{4,5},{5,4},{6,7},{7,6},{8,9},{9,8},{10,11... | collective-permute-start | bytes 786440 | tf_op jit(solution)/shard_map/ppermute | solution.py:276
  27.4 1.3 %collective-permute-start.14 = (bf16[128,256]{1,0:T(8,128)(2,1)S(1)}, bf16[128,256]{1,0:T(8,128)(2,1)S(1)}, u32[]{:S(2)}, u32[]{:S(2)}) collective-permute-start(bf16[128,256]{1,0:T(8,128)(2,1)S(1)} %shard_map.115.own), channel_id=1, source_target_pairs={{0,5},{1,8},{3,6},{2,11},{5,0},{4,13},{6,3},{7,14},{9,12},{8,1},{1... | collective-permute-start | bytes 196616 | tf_op jit(solution)/shard_map/ppermute | solution.py:302
  28.8 1.9 %collective-permute-start.18 = (bf16[128,256]{1,0:T(8,128)(2,1)S(1)}, bf16[128,256]{1,0:T(8,128)(2,1)S(1)}, u32[]{:S(2)}, u32[]{:S(2)}) collective-permute-start(bf16[128,256]{1,0:T(8,128)(2,1)S(1)} %shard_map.118.own), channel_id=1, source_target_pairs={{0,9},{1,4},{3,10},{2,7},{5,12},{4,1},{6,15},{7,2},{9,0},{8,13},{1... | collective-permute-start | bytes 196616 | tf_op jit(solution)/shard_map/ppermute | solution.py:302
  31.2 2.1 %collective-permute-start.15 = (bf16[128,256]{1,0:T(8,128)(2,1)S(1)}, bf16[128,256]{1,0:T(8,128)(2,1)S(1)}, u32[]{:S(2)}, u32[]{:S(2)}) collective-permute-start(bf16[128,256]{1,0:T(8,128)(2,1)S(1)} %shard_map.116.own), channel_id=1, source_target_pairs={{0,9},{1,2},{3,10},{2,1},{5,12},{4,7},{6,15},{7,4},{9,0},{8,11},{1... | collective-permute-start | bytes 196616 | tf_op jit(solution)/shard_map/ppermute | solution.py:302
  34.0 1.7 %collective-permute-start.19 = (bf16[128,256]{1,0:T(8,128)(2,1)S(1)}, bf16[128,256]{1,0:T(8,128)(2,1)S(1)}, u32[]{:S(2)}, u32[]{:S(2)}) collective-permute-start(bf16[128,256]{1,0:T(8,128)(2,1)S(1)} %shard_map.119.own), channel_id=1, source_target_pairs={{0,5},{1,2},{3,6},{2,1},{5,0},{4,7},{6,3},{7,4},{9,12},{8,11},{10,... | collective-permute-start | bytes 196616 | tf_op jit(solution)/shard_map/ppermute | solution.py:302
  36.1 0.7 %collective-permute-start.16 = (bf16[128,256]{1,0:T(8,128)(2,1)S(1)}, bf16[128,256]{1,0:T(8,128)(2,1)S(1)}, u32[]{:S(2)}, u32[]{:S(2)}) collective-permute-start(bf16[128,256]{1,0:T(8,128)(2,1)S(1)} %shard_map.117.low), channel_id=1, source_target_pairs={{0,1},{1,0},{2,3},{3,2},{4,5},{5,4},{6,7},{7,6},{8,9},{9,8},{10,11... | collective-permute-start | bytes 196616 | tf_op jit(solution)/shard_map/ppermute | solution.py:276
  36.8 0.9 %collective-permute-done.19.other = bf16[128,256]{1,0:T(8,128)(2,1)S(1)} collective-permute-done((bf16[128,256]{1,0:T(8,128)(2,1)S(1)}, bf16[128,256]{1,0:T(8,128)(2,1)S(1)}, u32[]{:S(2)}, u32[]{:S(2)}) %collective-permute-start.19) | collective-permute-done | bytes 65568 | tf_op jit(solution)/shard_map/ppermute | solution.py:302
  39.1 1.1 %shard_map.123 = (f32[256,128]{1,0:T(8,128)}, f32[1,256,128]{2,1,0:T(8,128)}) custom-call(bf16[2,2,256,256]{3,2,1,0:T(8,128)(2,1)S(1)} %get-tuple-element.21.mine, bf16[2,2,256,256]{3,2,1,0:T(8,128)(2,1)S(1)} %collective-permute-done.3.theirs, bf16[128,256]{1,0:T(8,128)(2,1)S(1)} %collective-permute-done.16.low, ...), custom_call_target="tpu_custom_call" | custom-call | tf_op jit(solution)/shard_map/pallas_call | solution.py:273
  (40 shorter events, 5.7 us)
Async XLA Ops:
  0.6 2.2 %collective-permute-start = (f32[256,128]{1,0:T(8,128)}, f32[256,128]{1,0:T(8,128)S(1)}, u32[]{:S(2)}, u32[]{:S(2)}) collective-permute-start(f32[256,128]{1,0:T(8,128)} %tgt_own_hbm.1), channel_id=1, source_target_pairs={{0,1},{1,0},{2,3},{3,2},{4,5},{5,4},{6,7},{7,6},{8,9},{9,8},{10,11... | collective-permute-start | bytes 393224 | tf_op jit(solution)/shard_map/ppermute | solution.py:276
  1.1 1.7 %collective-permute-start.1 = (f32[1,256,128]{2,1,0:T(8,128)}, f32[1,256,128]{2,1,0:T(8,128)S(1)}, u32[]{:S(2)}, u32[]{:S(2)}) collective-permute-start(f32[1,256,128]{2,1,0:T(8,128)} %proj_own_hbm.1), channel_id=1, source_target_pairs={{0,1},{1,0},{2,3},{3,2},{4,5},{5,4},{6,7},{7,6},{8,9},{9,8},{10,11... | collective-permute-start | bytes 393224 | tf_op jit(solution)/shard_map/ppermute | solution.py:276
  3.2 1.4 %collective-permute-start.2 = (bf16[128,256]{1,0:T(8,128)(2,1)S(1)}, bf16[128,256]{1,0:T(8,128)(2,1)S(1)}, u32[]{:S(2)}, u32[]{:S(2)}) collective-permute-start(bf16[128,256]{1,0:T(8,128)(2,1)S(1)} %get-tuple-element.25), channel_id=1, source_target_pairs={{0,1},{1,0},{2,3},{3,2},{4,5},{5,4},{6,7},{7,6},{8,9},{9,8},{10,11... | collective-permute-start | bytes 196616 | tf_op jit(solution)/shard_map/ppermute | solution.py:276
  4.6 18.2 %collective-permute-start.3 = (bf16[2,2,256,256]{3,2,1,0:T(8,128)(2,1)S(1)}, bf16[2,2,256,256]{3,2,1,0:T(8,128)(2,1)S(1)}, u32[]{:S(2)}, u32[]{:S(2)}) collective-permute-start(bf16[2,2,256,256]{3,2,1,0:T(8,128)(2,1)S(1)} %get-tuple-element.26.sent), channel_id=1, source_target_pairs={{0,1},{1,0},{2,3},{3,2},{4,5},{5,4},{6,7},{7,6},{8,9},{9,8},{10,11... | collective-permute-start | bytes 1572872 | tf_op jit(solution)/shard_map/ppermute | solution.py:276
  5.0 4.6 %collective-permute-start.4 = (bf16[128,256]{1,0:T(8,128)(2,1)S(1)}, bf16[128,256]{1,0:T(8,128)(2,1)S(1)}, u32[]{:S(2)}, u32[]{:S(2)}) collective-permute-start(bf16[128,256]{1,0:T(8,128)(2,1)S(1)} %get-tuple-element.30.own), channel_id=1, source_target_pairs={{0,3},{1,4},{3,0},{2,7},{5,6},{4,1},{6,5},{7,2},{9,10},{8,13},{10,... | collective-permute-start | bytes 196616 | tf_op jit(solution)/shard_map/ppermute | solution.py:302
  7.7 3.9 %collective-permute-start.8 = (bf16[128,256]{1,0:T(8,128)(2,1)S(1)}, bf16[128,256]{1,0:T(8,128)(2,1)S(1)}, u32[]{:S(2)}, u32[]{:S(2)}) collective-permute-start(bf16[128,256]{1,0:T(8,128)(2,1)S(1)} %get-tuple-element.31.own), channel_id=1, source_target_pairs={{0,3},{1,8},{3,0},{2,11},{5,6},{4,13},{6,5},{7,14},{9,10},{8,1},{1... | collective-permute-start | bytes 196616 | tf_op jit(solution)/shard_map/ppermute | solution.py:302
  9.6 4.5 %collective-permute-start.5 = (bf16[128,256]{1,0:T(8,128)(2,1)S(1)}, bf16[128,256]{1,0:T(8,128)(2,1)S(1)}, u32[]{:S(2)}, u32[]{:S(2)}) collective-permute-start(bf16[128,256]{1,0:T(8,128)(2,1)S(1)} %shard_map.108.own), channel_id=1, source_target_pairs={{0,5},{1,8},{3,6},{2,11},{5,0},{4,13},{6,3},{7,14},{9,12},{8,1},{1... | collective-permute-start | bytes 196616 | tf_op jit(solution)/shard_map/ppermute | solution.py:302
  11.6 5.5 %collective-permute-start.9 = (bf16[128,256]{1,0:T(8,128)(2,1)S(1)}, bf16[128,256]{1,0:T(8,128)(2,1)S(1)}, u32[]{:S(2)}, u32[]{:S(2)}) collective-permute-start(bf16[128,256]{1,0:T(8,128)(2,1)S(1)} %shard_map.111.own), channel_id=1, source_target_pairs={{0,9},{1,4},{3,10},{2,7},{5,12},{4,1},{6,15},{7,2},{9,0},{8,13},{1... | collective-permute-start | bytes 196616 | tf_op jit(solution)/shard_map/ppermute | solution.py:302
  14.1 4.7 %collective-permute-start.6 = (bf16[128,256]{1,0:T(8,128)(2,1)S(1)}, bf16[128,256]{1,0:T(8,128)(2,1)S(1)}, u32[]{:S(2)}, u32[]{:S(2)}) collective-permute-start(bf16[128,256]{1,0:T(8,128)(2,1)S(1)} %shard_map.109.own), channel_id=1, source_target_pairs={{0,9},{1,2},{3,10},{2,1},{5,12},{4,7},{6,15},{7,4},{9,0},{8,11},{1... | collective-permute-start | bytes 196616 | tf_op jit(solution)/shard_map/ppermute | solution.py:302
  17.1 4.0 %collective-permute-start.10 = (bf16[128,256]{1,0:T(8,128)(2,1)S(1)}, bf16[128,256]{1,0:T(8,128)(2,1)S(1)}, u32[]{:S(2)}, u32[]{:S(2)}) collective-permute-start(bf16[128,256]{1,0:T(8,128)(2,1)S(1)} %shard_map.112.own), channel_id=1, source_target_pairs={{0,5},{1,2},{3,6},{2,1},{5,0},{4,7},{6,3},{7,4},{9,12},{8,11},{10,... | collective-permute-start | bytes 196616 | tf_op jit(solution)/shard_map/ppermute | solution.py:302
  18.8 4.1 %collective-permute-start.7 = (bf16[128,256]{1,0:T(8,128)(2,1)S(1)}, bf16[128,256]{1,0:T(8,128)(2,1)S(1)}, u32[]{:S(2)}, u32[]{:S(2)}) collective-permute-start(bf16[128,256]{1,0:T(8,128)(2,1)S(1)} %shard_map.110.low), channel_id=1, source_target_pairs={{0,1},{1,0},{2,3},{3,2},{4,5},{5,4},{6,7},{7,6},{8,9},{9,8},{10,11... | collective-permute-start | bytes 196616 | tf_op jit(solution)/shard_map/ppermute | solution.py:276
  21.1 1.8 %collective-permute-start.11 = (bf16[128,256]{1,0:T(8,128)(2,1)S(1)}, bf16[128,256]{1,0:T(8,128)(2,1)S(1)}, u32[]{:S(2)}, u32[]{:S(2)}) collective-permute-start(bf16[128,256]{1,0:T(8,128)(2,1)S(1)} %shard_map.113.high), channel_id=1, source_target_pairs={{0,1},{1,0},{2,3},{3,2},{4,5},{5,4},{6,7},{7,6},{8,9},{9,8},{10,11... | collective-permute-start | bytes 196616 | tf_op jit(solution)/shard_map/ppermute | solution.py:276
  21.7 1.2 %collective-permute-start.12 = (f32[2,1,256]{2,1,0:T(1,128)S(1)}, f32[2,1,256]{2,1,0:T(1,128)S(1)}, u32[]{:S(2)}, u32[]{:S(2)}) collective-permute-start(f32[2,1,256]{2,1,0:T(1,128)S(1)} %get-tuple-element.32), channel_id=1, source_target_pairs={{0,1},{1,0},{2,3},{3,2},{4,5},{5,4},{6,7},{7,6},{8,9},{9,8},{10,11... | collective-permute-start | bytes 6152 | tf_op jit(solution)/shard_map/ppermute | solution.py:276
  23.7 3.8 %collective-permute-start.13 = (bf16[128,256]{1,0:T(8,128)(2,1)S(1)}, bf16[128,256]{1,0:T(8,128)(2,1)S(1)}, u32[]{:S(2)}, u32[]{:S(2)}) collective-permute-start(bf16[128,256]{1,0:T(8,128)(2,1)S(1)} %get-tuple-element.36.own), channel_id=1, source_target_pairs={{0,3},{1,4},{3,0},{2,7},{5,6},{4,1},{6,5},{7,2},{9,10},{8,13},{10,... | collective-permute-start | bytes 196616 | tf_op jit(solution)/shard_map/ppermute | solution.py:302
  24.9 3.9 %collective-permute-start.17 = (bf16[128,256]{1,0:T(8,128)(2,1)S(1)}, bf16[128,256]{1,0:T(8,128)(2,1)S(1)}, u32[]{:S(2)}, u32[]{:S(2)}) collective-permute-start(bf16[128,256]{1,0:T(8,128)(2,1)S(1)} %get-tuple-element.37.own), channel_id=1, source_target_pairs={{0,3},{1,8},{3,0},{2,11},{5,6},{4,13},{6,5},{7,14},{9,10},{8,1},{1... | collective-permute-start | bytes 196616 | tf_op jit(solution)/shard_map/ppermute | solution.py:302
  25.5 12.8 %collective-permute-start.21 = (bf16[2,256,256]{2,1,0:T(8,128)(2,1)S(1)}, bf16[2,256,256]{2,1,0:T(8,128)(2,1)S(1)}, u32[]{:S(2)}, u32[]{:S(2)}) collective-permute-start(bf16[2,256,256]{2,1,0:T(8,128)(2,1)S(1)} %get-tuple-element.39), channel_id=1, source_target_pairs={{0,1},{1,0},{2,3},{3,2},{4,5},{5,4},{6,7},{7,6},{8,9},{9,8},{10,11... | collective-permute-start | bytes 786440 | tf_op jit(solution)/shard_map/ppermute | solution.py:276
  27.4 3.8 %collective-permute-start.14 = (bf16[128,256]{1,0:T(8,128)(2,1)S(1)}, bf16[128,256]{1,0:T(8,128)(2,1)S(1)}, u32[]{:S(2)}, u32[]{:S(2)}) collective-permute-start(bf16[128,256]{1,0:T(8,128)(2,1)S(1)} %shard_map.115.own), channel_id=1, source_target_pairs={{0,5},{1,8},{3,6},{2,11},{5,0},{4,13},{6,3},{7,14},{9,12},{8,1},{1... | collective-permute-start | bytes 196616 | tf_op jit(solution)/shard_map/ppermute | solution.py:302
  28.8 5.2 %collective-permute-start.18 = (bf16[128,256]{1,0:T(8,128)(2,1)S(1)}, bf16[128,256]{1,0:T(8,128)(2,1)S(1)}, u32[]{:S(2)}, u32[]{:S(2)}) collective-permute-start(bf16[128,256]{1,0:T(8,128)(2,1)S(1)} %shard_map.118.own), channel_id=1, source_target_pairs={{0,9},{1,4},{3,10},{2,7},{5,12},{4,1},{6,15},{7,2},{9,0},{8,13},{1... | collective-permute-start | bytes 196616 | tf_op jit(solution)/shard_map/ppermute | solution.py:302
  31.2 4.8 %collective-permute-start.15 = (bf16[128,256]{1,0:T(8,128)(2,1)S(1)}, bf16[128,256]{1,0:T(8,128)(2,1)S(1)}, u32[]{:S(2)}, u32[]{:S(2)}) collective-permute-start(bf16[128,256]{1,0:T(8,128)(2,1)S(1)} %shard_map.116.own), channel_id=1, source_target_pairs={{0,9},{1,2},{3,10},{2,1},{5,12},{4,7},{6,15},{7,4},{9,0},{8,11},{1... | collective-permute-start | bytes 196616 | tf_op jit(solution)/shard_map/ppermute | solution.py:302
  34.0 3.8 %collective-permute-start.19 = (bf16[128,256]{1,0:T(8,128)(2,1)S(1)}, bf16[128,256]{1,0:T(8,128)(2,1)S(1)}, u32[]{:S(2)}, u32[]{:S(2)}) collective-permute-start(bf16[128,256]{1,0:T(8,128)(2,1)S(1)} %shard_map.119.own), channel_id=1, source_target_pairs={{0,5},{1,2},{3,6},{2,1},{5,0},{4,7},{6,3},{7,4},{9,12},{8,11},{10,... | collective-permute-start | bytes 196616 | tf_op jit(solution)/shard_map/ppermute | solution.py:302
  36.1 2.9 %collective-permute-start.16 = (bf16[128,256]{1,0:T(8,128)(2,1)S(1)}, bf16[128,256]{1,0:T(8,128)(2,1)S(1)}, u32[]{:S(2)}, u32[]{:S(2)}) collective-permute-start(bf16[128,256]{1,0:T(8,128)(2,1)S(1)} %shard_map.117.low), channel_id=1, source_target_pairs={{0,1},{1,0},{2,3},{3,2},{4,5},{5,4},{6,7},{7,6},{8,9},{9,8},{10,11... | collective-permute-start | bytes 196616 | tf_op jit(solution)/shard_map/ppermute | solution.py:276
  37.8 1.4 %collective-permute-start.20 = (bf16[128,256]{1,0:T(8,128)(2,1)S(1)}, bf16[128,256]{1,0:T(8,128)(2,1)S(1)}, u32[]{:S(2)}, u32[]{:S(2)}) collective-permute-start(bf16[128,256]{1,0:T(8,128)(2,1)S(1)} %shard_map.120.high), channel_id=1, source_target_pairs={{0,1},{1,0},{2,3},{3,2},{4,5},{5,4},{6,7},{7,6},{8,9},{9,8},{10,11... | collective-permute-start | bytes 196616 | tf_op jit(solution)/shard_map/ppermute | solution.py:276

commit v11 on v10

v11 whole, which is shorter than its diff:
```python
import functools

import jax
import jax.numpy as jnp
from jax import lax
from jax.experimental import pallas as pl
from jax.experimental.pallas import tpu as pltpu
from jax.sharding import PartitionSpec as P

time_step = 0.4
half_step = 0.5 * time_step
VMEM_LIMIT = 8 * 1024 * 1024
DEVICES = ("tgt", "prj", "rep")
HBM = pl.BlockSpec(memory_space=pl.ANY)
VMEM = pl.BlockSpec(memory_space=pltpu.VMEM)


def parity(place):
    odd = 0
    while place:
        odd, place = odd ^ (place & 1), place >> 1
    return odd


def my_kind():
    n_tgt, n_prj = lax.axis_size("tgt"), lax.axis_size("prj")
    place = lax.axis_index("tgt") * n_prj + lax.axis_index("prj")
    kind = lax.axis_index("rep")
    for bit in range((n_tgt * n_prj).bit_length() - 1):
        kind = jnp.bitwise_xor(kind, jnp.bitwise_and(lax.shift_right_logical(place, bit), 1))
    return kind


def my_segment(kind):
    place = jnp.where(kind == 0, lax.axis_index("prj"), lax.axis_index("tgt"))
    return 2 * jnp.bitwise_and(place, 1) + lax.axis_index("rep")


def ordered(core, first, second):
    return jnp.where(core == 0, first, second), jnp.where(core == 0, second, first)


def turned(block):
    half = block.shape[0] // 2
    return jnp.concatenate([block[half:], -block[:half]], axis=0)


def bf16(block):
    return block.astype(jnp.bfloat16)


def f32(block):
    return block.astype(jnp.float32)


def project(basis_real, basis_imag, amp):
    return jnp.dot(bf16(amp), basis_real, preferred_element_type=jnp.float32) + jnp.dot(
        bf16(turned(amp)), basis_imag, preferred_element_type=jnp.float32
    )


def expand(basis_real, basis_imag, field):
    contract = (((1,), (1,)), ((), ()))
    return lax.dot_general(
        turned(field), basis_real, contract, preferred_element_type=jnp.float32
    ) + lax.dot_general(field, basis_imag, contract, preferred_element_type=jnp.float32)


def load_kernel(
    weight_hbm,
    tgt_hbm,
    proj_hbm,
    tgt_energy_hbm,
    proj_energy_hbm,
    tgt_own_hbm,
    proj_own_hbm,
    mine,
    sent,
    weight,
    energy,
    amp_ref,
    flat_weight,
    flat_energy,
    tgt_own,
    proj_own,
    sems,
):
    my = my_kind()

    def first_segment(axis):
        place = lax.axis_index(axis)
        return 2 * (place - jnp.bitwise_and(place, 1))

    sources = (
        tgt_hbm.at[:, pl.ds(first_segment("prj"), 4)],
        proj_hbm.at[:, pl.ds(first_segment("tgt"), 4)],
    )

    def basis_copies(kind):
        return [
            pltpu.make_async_copy(sources[source].at[part], basis.at[part], sems.at[2 * slot + part])
            for slot, (source, basis) in enumerate(((1 - kind, sent), (kind, mine)))
            for part in range(2)
        ]

    pairs = [
        (tgt_own_hbm, tgt_own),
        (proj_own_hbm, proj_own),
        (weight_hbm, flat_weight),
        (tgt_energy_hbm, flat_energy),
        (proj_energy_hbm, energy.at[1]),
    ]
    copies = [pltpu.make_async_copy(src, dst, sems.at[4 + k]) for k, (src, dst) in enumerate(pairs)]
    for copy in copies:
        copy.start()
    for kind in range(2):

        @pl.when(my == kind)
        def _():
            for copy in basis_copies(kind):
                copy.start()

    for copy in copies:
        copy.wait()
    weight[0] = flat_weight[...][None, :]
    energy[0] = flat_energy[...][None, :]
    amp_ref[0] = tgt_own[...].T
    amp_ref[1] = proj_own[0].T
    for copy in basis_copies(0):
        copy.wait()


def pack_kernel(
    amp_ref,
    energy,
    tgt_other,
    proj_other,
    tgt_energy_other,
    proj_energy_other,
    near_weight,
    far_weight,
    chip_amp,
    chip_energy,
    weights,
    message,
):
    core = lax.axis_index("rep")
    my = my_kind()
    cols = chip_amp.shape[1]
    other_amp, _ = ordered(my, tgt_other[...].T, proj_other[0].T)
    other_energy, _ = ordered(my, tgt_energy_other[...][None, :], proj_energy_other[...])
    amps = ordered(core, amp_ref[my], other_amp)
    energies = ordered(core, energy[my], other_energy)
    weights[0] = near_weight[0]
    weights[1] = far_weight[...][None, :]
    extra = message.shape[1] - cols
    for segment in range(2):
        chip_amp[segment] = amps[segment]
        chip_energy[segment] = energies[segment]
        message[segment, :cols] = bf16(amps[segment])
        row = lax.broadcasted_iota(jnp.int32, (extra, energies[segment].shape[1]), 0)
        rest = energies[segment]
        block = jnp.zeros(row.shape, jnp.float32)
        for piece in range(3):
            rounded = f32(bf16(rest))
            block = jnp.where(row == piece, rounded, block)
            rest = rest - rounded
        message[segment, cols:] = bf16(block)


def side_kernel(gate_levels, flags_hbm, counts_hbm, amp_ref, mine, gate, send_own, flags, counts, sems):
    my = my_kind()
    tgt_index = lax.axis_index("tgt")
    prj_index = lax.axis_index("prj")
    pairs = [(flags_hbm, flags), (counts_hbm, counts)]
    copies = [pltpu.make_async_copy(src, dst, sems.at[k]) for k, (src, dst) in enumerate(pairs)]
    for copy in copies:
        copy.start()
    other = my_segment(my) + 1 - 2 * lax.axis_index("rep")
    for part in range(2):
        send_own[part] = mine[part, other]
    for copy in copies:
        copy.wait()
    tiles = 2
    width = gate.shape[-1] // tiles
    gate_level = jnp.where(my == 0, *gate_levels)
    for half in range(2):
        for tile in range(tiles):
            live = jnp.logical_and(
                flags[prj_index, tgt_index] > 0, tiles * half + tile < counts[prj_index, tgt_index]
            )
            value = jnp.where(live, 1.0, 0.0).astype(jnp.float32)
            for level in range(gate.shape[0]):
                here = jnp.where(level == gate_level, value, jnp.float32(1.0))
                gate[level, half, :, tile * width : (tile + 1) * width] = jnp.full(
                    (1, width), here, jnp.float32
                )


def chip_kernel(mine, theirs, chip_amp, part_ref):
    first = my_segment(my_kind()) - lax.axis_index("rep")
    for slot, basis in enumerate((mine, theirs)):
        part_ref[slot] = project(basis[0, first], basis[1, first], chip_amp[0]) + project(
            basis[0, first + 1], basis[1, first + 1], chip_amp[1]
        )


def weigh(gate, weights, near, far, low_ref, high_ref):
    low, high = ordered(lax.axis_index("rep"), weights[0] * near, weights[1] * far)
    low_ref[...] = bf16(gate[0, 0] * low)
    high_ref[...] = bf16(gate[0, 1] * high)


def first_kernel(mine, theirs, gate, weights, part_ref, message, low_ref, high_ref):
    first = 2 - my_segment(my_kind()) + lax.axis_index("rep")
    cols = part_ref.shape[1]
    near, far = [
        part_ref[slot]
        + project(basis[0, first], basis[1, first], f32(message[0, :cols]))
        + project(basis[0, first + 1], basis[1, first + 1], f32(message[1, :cols]))
        for slot, basis in enumerate((mine, theirs))
    ]
    weigh(gate, weights, near, far, low_ref, high_ref)


def add_kernel(level, half, gate, own, other, out_ref):
    out_ref[...] = bf16(gate[level, half] * (f32(own[...]) + f32(other[...])))


def second_kernel(
    mine,
    theirs,
    low,
    high,
    gate,
    weights,
    chip_amp,
    chip_energy,
    message,
    low_ref,
    high_ref,
    half_ref,
    send_ref,
):
    core = lax.axis_index("rep")
    first = my_segment(my_kind()) - core
    cols = chip_amp.shape[1]
    fields = ordered(core, low[...], high[...])
    halves = []
    for segment in range(4):
        if segment < 2:
            place, amp, energy = first + segment, chip_amp[segment], chip_energy[segment]
        else:
            place = 2 - first + segment - 2
            amp = f32(message[segment - 2, :cols])
            pieces = f32(message[segment - 2, cols:])
            energy = pieces[0:1] + pieces[1:2] + pieces[2:3]
        change = sum(
            expand(basis[0, place], basis[1, place], field)
            for basis, field in zip((mine, theirs), fields)
        )
        halves.append((place, amp + half_step * (energy * turned(amp) + change)))
    half_ref[...], send_ref[...] = ordered(core, halves[0][1], halves[1][1])
    near, far = [
        sum(project(basis[0, place], basis[1, place], half) for place, half in halves)
        for basis in (mine, theirs)
    ]
    weigh(gate, weights, near, far, low_ref, high_ref)


def other_last_kernel(sent, own_far, low, high, energy, amp_ref, half_ref, new_ref):
    kind = 1 - my_kind()
    place = my_segment(kind)
    near, far = ordered(lax.axis_index("rep"), low[...], high[...])
    change = expand(sent[0, place], sent[1, place], near) + expand(own_far[0], own_far[1], far)
    rate = energy[kind] * turned(half_ref[...]) + change
    new_ref[...] = (amp_ref[kind] + time_step * rate).T


def last_kernel(mine, theirs, low, high, energy, amp_ref, half_ref, other_new, new_tgt, new_proj):
    my = my_kind()
    place = my_segment(my)
    near, far = ordered(lax.axis_index("rep"), low[...], high[...])
    change = expand(mine[0, place], mine[1, place], near) + expand(theirs[0, place], theirs[1, place], far)
    rate = energy[my] * turned(half_ref[...]) + change
    my_new = (amp_ref[my] + time_step * rate).T
    new_tgt[...], new_proj[0] = ordered(my, my_new, other_new[...])


def shards(
    tgt_basis,
    proj_basis,
    quad_weight,
    tgt_energy,
    proj_energy,
    pair_flags,
    tile_counts,
    tgt_amp,
    proj_amp,
):
    points = quad_weight.shape[0]
    rows, two_cols = tgt_amp.shape
    sizes = [lax.axis_size(axis) for axis in DEVICES]

    def call(kernel, out_shape, in_specs, scratch_shapes=(), cost=None):
        return pl.pallas_call(
            kernel,
            out_shape=out_shape,
            in_specs=in_specs,
            out_specs=[VMEM] * len(out_shape),
            scratch_shapes=scratch_shapes,
            cost_estimate=cost,
            compiler_params=pltpu.CompilerParams(vmem_limit_bytes=VMEM_LIMIT),
        )

    def run(kernel, out_shape, *blocks):
        return call(kernel, out_shape, [VMEM] * len(blocks))(*blocks)

    def other_core(block):
        return lax.ppermute(block, "rep", [(0, 1), (1, 0)])

    n_tgt, n_prj, n_core = sizes
    tgt_flips = [n_prj << bit for bit in range(n_tgt.bit_length() - 1)]
    prj_flips = [1 << bit for bit in range(n_prj.bit_length() - 1)]
    flips = (prj_flips + tgt_flips, tgt_flips + prj_flips)
    gate_levels = (len(prj_flips) - 1, len(tgt_flips) - 1)
    n_steps = len(tgt_flips) + len(prj_flips)

    def exchanged(step, block):
        pairs = []
        for place in range(n_tgt * n_prj):
            for kind in range(2):
                there = place ^ flips[kind][step]
                pairs.append((place * n_core + (kind ^ parity(place)), there * n_core + (kind ^ parity(there))))
        return lax.ppermute(block, DEVICES, pairs)

    in_vmem = pltpu.VMEM
    basis = in_vmem((2, 4, rows, points), jnp.bfloat16)
    sums = in_vmem((two_cols, points), jnp.bfloat16)
    segment = in_vmem((two_cols, rows), jnp.float32)

    def summed(*halves):
        totals = []
        for half, block in enumerate(halves):
            for step in range(1, n_steps):
                other = exchanged(step, block)
                (block,) = run(functools.partial(add_kernel, step, half), [sums], gate, block, other)
            totals.append(block)
        return totals

    def swapped(fields):
        return [other_core(block) for block in fields]

    def in_hbm(*blocks):
        return [pltpu.with_memory_space_constraint(block, pltpu.HBM) for block in blocks]

    others = swapped([tgt_amp, proj_amp, tgt_energy, proj_energy])
    far_weight = other_core(quad_weight)
    bases = (tgt_basis.reshape(2, -1, rows, points), proj_basis)
    mine, sent, weight, energy, amp = call(
        load_kernel,
        [
            basis,
            basis,
            in_vmem((1, 1, points), jnp.float32),
            in_vmem((2, 1, rows), jnp.float32),
            in_vmem((2, two_cols, rows), jnp.float32),
        ],
        [HBM] * 7,
        [
            pltpu.VMEM((points,), jnp.float32),
            pltpu.VMEM((rows,), jnp.float32),
            pltpu.VMEM(tgt_amp.shape, jnp.float32),
            pltpu.VMEM(proj_amp.shape, jnp.float32),
            pltpu.SemaphoreType.DMA((9,)),
        ],
        pl.CostEstimate(
            flops=2 * 4 * rows * two_cols * points, bytes_accessed=4 * 1024 * 1024, transcendentals=0
        ),
    )(*in_hbm(quad_weight, *bases, tgt_energy, proj_energy, tgt_amp, proj_amp))
    chip_amp, chip_energy, weights, message = run(
        pack_kernel,
        [
            in_vmem((2, two_cols, rows), jnp.float32),
            in_vmem((2, 1, rows), jnp.float32),
            in_vmem((2, 1, points), jnp.float32),
            in_vmem((2, two_cols + 16, rows), jnp.bfloat16),
        ],
        amp,
        energy,
        *others,
        weight,
        far_weight,
    )
    sent, message = lax.optimization_barrier((sent, message))
    message = exchanged(0, message)
    theirs = other_core(sent)
    flags, counts = pair_flags.T, tile_counts.T
    gate, send_own = call(
        functools.partial(side_kernel, gate_levels),
        [
            in_vmem((n_steps, 2, 1, points), jnp.float32),
            in_vmem((2, rows, points), jnp.bfloat16),
        ],
        [HBM, HBM, VMEM, VMEM],
        [
            pltpu.SMEM(flags.shape, jnp.int32),
            pltpu.SMEM(counts.shape, jnp.int32),
            pltpu.SemaphoreType.DMA((2,)),
        ],
    )(*in_hbm(flags, counts), chip_amp, mine)
    own_far = other_core(send_own)
    (part,) = run(
        chip_kernel, [in_vmem((2, two_cols, points), jnp.float32)], mine, theirs, chip_amp
    )
    halves = run(first_kernel, [sums] * 2, mine, theirs, gate, weights, part, message)
    fields = summed(*halves)
    *halves, my_half, half_send = run(
        second_kernel,
        [sums, sums, segment, segment],
        mine,
        theirs,
        *swapped(fields),
        gate,
        weights,
        chip_amp,
        chip_energy,
        message,
    )
    other_half = other_core(half_send)
    fields = summed(*halves)
    (other_new,) = run(
        other_last_kernel,
        [in_vmem((rows, two_cols), jnp.float32)],
        sent,
        own_far,
        *fields,
        energy,
        amp,
        other_half,
    )
    return run(
        last_kernel,
        [
            jax.ShapeDtypeStruct(tgt_amp.shape, jnp.float32),
            jax.ShapeDtypeStruct(proj_amp.shape, jnp.float32),
        ],
        mine,
        theirs,
        *swapped(fields),
        energy,
        amp,
        my_half,
        other_new,
    )


def solution(mesh):
    in_specs = (
        P(None, "tgt", "rep"),
        P(None, None, "prj", "rep"),
        P(("bpar", "rep")),
        P(("tgt", "prj", "rep")),
        P(("tgt", "rep"), "prj"),
        P("bpar", None),
        P("bpar", None),
        P(("bpar", "tgt", "prj", "rep"), None),
        P(("bpar", "tgt", "rep"), "prj", None),
    )
    out_specs = (P(("bpar", "tgt", "prj", "rep"), None), P(("bpar", "tgt", "rep"), "prj", None))

    def step(*args):
        return tuple(shards(*args))

    return jax.shard_map(step, mesh=mesh, in_specs=in_specs, out_specs=out_specs, check_vma=False)
```

time: 40.4 us -> 38.4 us (0.950)
  starting transfers between devices: 26.7 us -> 20.1 us
  waiting for transfers between devices: 7.19 us -> 11.3 us
  Pallas kernels: 5.6 us -> 6.08 us
    ppermute x12 -> x9, waiting for transfers between devices: 5.02 us -> 9.83 us  [exchanged(): return lax.ppermute(block, DEVICES, pairs)]
    ppermute x12 -> x9, starting transfers between devices: 19.4 us -> 15.6 us  [exchanged(): return lax.ppermute(block, DEVICES, pairs)]
    ppermute x10 -> x12, starting transfers between devices: 7.25 us -> 4.44 us  [other_core(): return lax.ppermute(block, 'rep', [(0, 1), (1, 0)])]
    ppermute x10 -> x12, waiting for transfers between devices: 2.17 us -> 1.47 us  [other_core(): return lax.ppermute(block, 'rep', [(0, 1), (1, 0)])]
    pallas_call x18 -> x14, Pallas kernels: 3.2 us -> 3.57 us  [run(): return call(kernel, out_shape, [VMEM] * len(blocks))(*blocks)]
  transfers between devices with their start and end apart: 22 -> 21, of which waited for: 11 -> 9; matrix products, arithmetic and copies ran while one was open for 0% -> 0% of each run, Pallas kernels for 8% -> 12%
where the time goes in v11:
time: 38.4 us; the launch traced here: 38.3 us
  starting transfers between devices  20.1 us (52%)
  waiting for transfers between devices  11.3 us (29%)
  Pallas kernels  6.08 us (16%)
  between operations  0.79 us (2%)
    ppermute x9, starting transfers between devices, exchanged(): return lax.ppermute(block, DEVICES, pairs)  15.6 us
    ppermute x9, waiting for transfers between devices, exchanged(): return lax.ppermute(block, DEVICES, pairs)  9.83 us
    ppermute x12, starting transfers between devices, other_core(): return lax.ppermute(block, 'rep', [(0, 1), (1, 0)])  4.44 us
    pallas_call x14, Pallas kernels, run(): return call(kernel, out_shape, [VMEM] * len(blocks))(*blocks)  3.57 us
    pallas_call x1, Pallas kernels, shards(): call(load_kernel, [basis, basis, in_vmem((1, 1, points), jnp.float32), in...  1.78 us
    ppermute x12, waiting for transfers between devices, other_core(): return lax.ppermute(block, 'rep', [(0, 1), (1, 0)])  1.47 us
  transfers between devices with their start and end apart: 21, of which 9 were waited for; matrix products, arithmetic and copies ran while one was open for 0% of the time, Pallas kernels for 12%

profile of v11, /device:TPU:0, one launch (start us, length us, event | category | flops | bytes accessed | tf_op | source)
XLA Modules:
  0.0 38.3 jit_solution(4362390777382921605)
XLA Ops:
  0.6 0.5 %collective-permute-start = (f32[256,128]{1,0:T(8,128)}, f32[256,128]{1,0:T(8,128)S(1)}, u32[]{:S(2)}, u32[]{:S(2)}) collective-permute-start(f32[256,128]{1,0:T(8,128)} %tgt_own_hbm.1), channel_id=1, source_target_pairs={{0,1},{1,0},{2,3},{3,2},{4,5},{5,4},{6,7},{7,6},{8,9},{9,8},{10,11... | collective-permute-start | bytes 393224 | tf_op jit(solution)/shard_map/ppermute | solution.py:320
  2.2 1.8 %shard_map.104 = (bf16[2,4,256,256]{3,2,1,0:T(8,128)(2,1)S(1)}, bf16[2,4,256,256]{3,2,1,0:T(8,128)(2,1)S(1)}, f32[1,1,256]{2,1,0:T(1,128)S(1)}, f32[2,1,256]{2,1,0:T(1,128)S(1)}, f32[2,128,256]{2,1,0:T(8,128)S(1)}) custom-call(f32[256]{0:T(256)} %weight_hbm.1, bf16[2,4,256,256]{3,2,1,0:T(8,128)(2,1)} %bitcast.3, bf16[2,8,256,256]{3,2,1,0:T(8,128)(2,1)} %proj_hbm.1, ...), custom_call_target="tpu_custom_call" | custom-call | flops 67108864 | bytes 4194304 | tf_op jit(solution)/shard_map/pallas_call | solution.py:360
  4.3 2.6 %collective-permute-start.6 = (bf16[2,144,256]{2,1,0:T(8,128)(2,1)S(1)}, bf16[2,144,256]{2,1,0:T(8,128)(2,1)S(1)}, u32[]{:S(2)}, u32[]{:S(2)}) collective-permute-start(bf16[2,144,256]{2,1,0:T(8,128)(2,1)S(1)} %get-tuple-element.31), channel_id=1, source_target_pairs={{0,3},{1,4},{3,0},{2,7},{5,6},{4,1},{6,5},{7,2},{9,10},{8,13},{10,... | collective-permute-start | bytes 442376 | tf_op jit(solution)/shard_map/ppermute | solution.py:335
  6.9 0.7 %shard_map.106 = (f32[3,2,1,256]{3,2,1,0:T(1,128)S(1)}, bf16[2,256,256]{2,1,0:T(8,128)(2,1)S(1)}) custom-call(s32[2,4]{1,0:T(2,128)} %bitcast.4, s32[2,4]{1,0:T(2,128)} %bitcast.5, f32[2,128,256]{2,1,0:T(8,128)S(1)} %get-tuple-element.28.amp_ref.chip_amp, bf16[2,4,256,256]{3,2,1,0:T(8,128)(2,1)S(1)} %get-tuple-element.21.mine), custom_call_target="tpu_custom_call" | custom-call | tf_op jit(solution)/shard_map/pallas_call | solution.py:399
  8.0 1.7 %collective-permute-done.6.message = bf16[2,144,256]{2,1,0:T(8,128)(2,1)S(1)} collective-permute-done((bf16[2,144,256]{2,1,0:T(8,128)(2,1)S(1)}, bf16[2,144,256]{2,1,0:T(8,128)(2,1)S(1)}, u32[]{:S(2)}, u32[]{:S(2)}) %collective-permute-start.6) | collective-permute-done | bytes 147488 | tf_op jit(solution)/shard_map/ppermute | solution.py:335
  10.1 1.9 %collective-permute-start.7 = (bf16[128,256]{1,0:T(8,128)(2,1)S(1)}, bf16[128,256]{1,0:T(8,128)(2,1)S(1)}, u32[]{:S(2)}, u32[]{:S(2)}) collective-permute-start(bf16[128,256]{1,0:T(8,128)(2,1)S(1)} %get-tuple-element.32.own), channel_id=1, source_target_pairs={{0,5},{1,8},{3,6},{2,11},{5,0},{4,13},{6,3},{7,14},{9,12},{8,1},{1... | collective-permute-start | bytes 196616 | tf_op jit(solution)/shard_map/ppermute | solution.py:335
  12.1 1.9 %collective-permute-done.7.other = bf16[128,256]{1,0:T(8,128)(2,1)S(1)} collective-permute-done((bf16[128,256]{1,0:T(8,128)(2,1)S(1)}, bf16[128,256]{1,0:T(8,128)(2,1)S(1)}, u32[]{:S(2)}, u32[]{:S(2)}) %collective-permute-start.7) | collective-permute-done | bytes 65568 | tf_op jit(solution)/shard_map/ppermute | solution.py:335
  14.0 3.4 %collective-permute-start.8 = (bf16[128,256]{1,0:T(8,128)(2,1)S(1)}, bf16[128,256]{1,0:T(8,128)(2,1)S(1)}, u32[]{:S(2)}, u32[]{:S(2)}) collective-permute-start(bf16[128,256]{1,0:T(8,128)(2,1)S(1)} %shard_map.109.own), channel_id=1, source_target_pairs={{0,9},{1,2},{3,10},{2,1},{5,12},{4,7},{6,15},{7,4},{9,0},{8,11},{1... | collective-permute-start | bytes 196616 | tf_op jit(solution)/shard_map/ppermute | solution.py:335
  17.4 1.6 %collective-permute-start.11 = (bf16[128,256]{1,0:T(8,128)(2,1)S(1)}, bf16[128,256]{1,0:T(8,128)(2,1)S(1)}, u32[]{:S(2)}, u32[]{:S(2)}) collective-permute-start(bf16[128,256]{1,0:T(8,128)(2,1)S(1)} %shard_map.111.own), channel_id=1, source_target_pairs={{0,9},{1,2},{3,10},{2,1},{5,12},{4,7},{6,15},{7,4},{9,0},{8,11},{1... | collective-permute-start | bytes 196616 | tf_op jit(solution)/shard_map/ppermute | solution.py:335
  19.0 0.6 %collective-permute-done.8.other = bf16[128,256]{1,0:T(8,128)(2,1)S(1)} collective-permute-done((bf16[128,256]{1,0:T(8,128)(2,1)S(1)}, bf16[128,256]{1,0:T(8,128)(2,1)S(1)}, u32[]{:S(2)}, u32[]{:S(2)}) %collective-permute-start.8) | collective-permute-done | bytes 65568 | tf_op jit(solution)/shard_map/ppermute | solution.py:335
  19.8 2.3 %collective-permute-done.11.other = bf16[128,256]{1,0:T(8,128)(2,1)S(1)} collective-permute-done((bf16[128,256]{1,0:T(8,128)(2,1)S(1)}, bf16[128,256]{1,0:T(8,128)(2,1)S(1)}, u32[]{:S(2)}, u32[]{:S(2)}) %collective-permute-start.11) | collective-permute-done | bytes 65568 | tf_op jit(solution)/shard_map/ppermute | solution.py:335
  22.7 0.7 %collective-permute-done.12.high = bf16[128,256]{1,0:T(8,128)(2,1)S(1)} collective-permute-done((bf16[128,256]{1,0:T(8,128)(2,1)S(1)}, bf16[128,256]{1,0:T(8,128)(2,1)S(1)}, u32[]{:S(2)}, u32[]{:S(2)}) %collective-permute-start.12) | collective-permute-done | bytes 65568 | tf_op jit(solution)/shard_map/ppermute | solution.py:320
  23.4 1.1 %shard_map.113 = (bf16[128,256]{1,0:T(8,128)(2,1)S(1)}, bf16[128,256]{1,0:T(8,128)(2,1)S(1)}, f32[128,256]{1,0:T(8,128)S(1)}, f32[128,256]{1,0:T(8,128)S(1)}) custom-call(bf16[2,4,256,256]{3,2,1,0:T(8,128)(2,1)S(1)} %get-tuple-element.21.mine, bf16[2,4,256,256]{3,2,1,0:T(8,128)(2,1)S(1)} %collective-permute-done.5.theirs, ...), custom_call_target="tpu_custom_call" | custom-call | tf_op jit(solution)/shard_map/pallas_call | solution.py:317
  24.5 1.2 %collective-permute-start.13 = (bf16[128,256]{1,0:T(8,128)(2,1)S(1)}, bf16[128,256]{1,0:T(8,128)(2,1)S(1)}, u32[]{:S(2)}, u32[]{:S(2)}) collective-permute-start(bf16[128,256]{1,0:T(8,128)(2,1)S(1)} %get-tuple-element.35.own), channel_id=1, source_target_pairs={{0,5},{1,8},{3,6},{2,11},{5,0},{4,13},{6,3},{7,14},{9,12},{8,1},{1... | collective-permute-start | bytes 196616 | tf_op jit(solution)/shard_map/ppermute | solution.py:335
  25.7 0.6 %collective-permute-start.16 = (bf16[128,256]{1,0:T(8,128)(2,1)S(1)}, bf16[128,256]{1,0:T(8,128)(2,1)S(1)}, u32[]{:S(2)}, u32[]{:S(2)}) collective-permute-start(bf16[128,256]{1,0:T(8,128)(2,1)S(1)} %get-tuple-element.36.own), channel_id=1, source_target_pairs={{0,5},{1,8},{3,6},{2,11},{5,0},{4,13},{6,3},{7,14},{9,12},{8,1},{1... | collective-permute-start | bytes 196616 | tf_op jit(solution)/shard_map/ppermute | solution.py:335
  26.4 1.1 %collective-permute-start.20 = (f32[128,256]{1,0:T(8,128)S(1)}, f32[128,256]{1,0:T(8,128)S(1)}, u32[]{:S(2)}, u32[]{:S(2)}) collective-permute-start(f32[128,256]{1,0:T(8,128)S(1)} %get-tuple-element.39), channel_id=1, source_target_pairs={{0,1},{1,0},{2,3},{3,2},{4,5},{5,4},{6,7},{7,6},{8,9},{9,8},{10,11... | collective-permute-start | bytes 393224 | tf_op jit(solution)/shard_map/ppermute | solution.py:320
  27.4 0.9 %collective-permute-done.13.other = bf16[128,256]{1,0:T(8,128)(2,1)S(1)} collective-permute-done((bf16[128,256]{1,0:T(8,128)(2,1)S(1)}, bf16[128,256]{1,0:T(8,128)(2,1)S(1)}, u32[]{:S(2)}, u32[]{:S(2)}) %collective-permute-start.13) | collective-permute-done | bytes 65568 | tf_op jit(solution)/shard_map/ppermute | solution.py:335
  28.3 2.7 %collective-permute-start.14 = (bf16[128,256]{1,0:T(8,128)(2,1)S(1)}, bf16[128,256]{1,0:T(8,128)(2,1)S(1)}, u32[]{:S(2)}, u32[]{:S(2)}) collective-permute-start(bf16[128,256]{1,0:T(8,128)(2,1)S(1)} %shard_map.114.own), channel_id=1, source_target_pairs={{0,9},{1,2},{3,10},{2,1},{5,12},{4,7},{6,15},{7,4},{9,0},{8,11},{1... | collective-permute-start | bytes 196616 | tf_op jit(solution)/shard_map/ppermute | solution.py:335
  31.1 1.4 %collective-permute-start.17 = (bf16[128,256]{1,0:T(8,128)(2,1)S(1)}, bf16[128,256]{1,0:T(8,128)(2,1)S(1)}, u32[]{:S(2)}, u32[]{:S(2)}) collective-permute-start(bf16[128,256]{1,0:T(8,128)(2,1)S(1)} %shard_map.116.own), channel_id=1, source_target_pairs={{0,9},{1,2},{3,10},{2,1},{5,12},{4,7},{6,15},{7,4},{9,0},{8,11},{1... | collective-permute-start | bytes 196616 | tf_op jit(solution)/shard_map/ppermute | solution.py:335
  32.5 0.8 %collective-permute-done.14.other = bf16[128,256]{1,0:T(8,128)(2,1)S(1)} collective-permute-done((bf16[128,256]{1,0:T(8,128)(2,1)S(1)}, bf16[128,256]{1,0:T(8,128)(2,1)S(1)}, u32[]{:S(2)}, u32[]{:S(2)}) %collective-permute-start.14) | collective-permute-done | bytes 65568 | tf_op jit(solution)/shard_map/ppermute | solution.py:335
  33.4 0.8 %collective-permute-start.15 = (bf16[128,256]{1,0:T(8,128)(2,1)S(1)}, bf16[128,256]{1,0:T(8,128)(2,1)S(1)}, u32[]{:S(2)}, u32[]{:S(2)}) collective-permute-start(bf16[128,256]{1,0:T(8,128)(2,1)S(1)} %shard_map.115.low), channel_id=1, source_target_pairs={{0,1},{1,0},{2,3},{3,2},{4,5},{5,4},{6,7},{7,6},{8,9},{9,8},{10,11... | collective-permute-start | bytes 196616 | tf_op jit(solution)/shard_map/ppermute | solution.py:320
  34.2 1.6 %collective-permute-done.17.other = bf16[128,256]{1,0:T(8,128)(2,1)S(1)} collective-permute-done((bf16[128,256]{1,0:T(8,128)(2,1)S(1)}, bf16[128,256]{1,0:T(8,128)(2,1)S(1)}, u32[]{:S(2)}, u32[]{:S(2)}) %collective-permute-start.17) | collective-permute-done | bytes 65568 | tf_op jit(solution)/shard_map/ppermute | solution.py:335
  36.5 0.7 %collective-permute-done.18.high = bf16[128,256]{1,0:T(8,128)(2,1)S(1)} collective-permute-done((bf16[128,256]{1,0:T(8,128)(2,1)S(1)}, bf16[128,256]{1,0:T(8,128)(2,1)S(1)}, u32[]{:S(2)}, u32[]{:S(2)}) %collective-permute-start.18) | collective-permute-done | bytes 65568 | tf_op jit(solution)/shard_map/ppermute | solution.py:320
  37.2 1.1 %shard_map.119 = (f32[256,128]{1,0:T(8,128)}, f32[1,256,128]{2,1,0:T(8,128)}) custom-call(bf16[2,4,256,256]{3,2,1,0:T(8,128)(2,1)S(1)} %get-tuple-element.21.mine, bf16[2,4,256,256]{3,2,1,0:T(8,128)(2,1)S(1)} %collective-permute-done.5.theirs, bf16[128,256]{1,0:T(8,128)(2,1)S(1)} %collective-permute-done.15.low, ...), custom_call_target="tpu_custom_call" | custom-call | tf_op jit(solution)/shard_map/pallas_call | solution.py:317
  (34 shorter events, 3.5 us)
Async XLA Ops:
  0.6 3.4 %collective-permute-start = (f32[256,128]{1,0:T(8,128)}, f32[256,128]{1,0:T(8,128)S(1)}, u32[]{:S(2)}, u32[]{:S(2)}) collective-permute-start(f32[256,128]{1,0:T(8,128)} %tgt_own_hbm.1), channel_id=1, source_target_pairs={{0,1},{1,0},{2,3},{3,2},{4,5},{5,4},{6,7},{7,6},{8,9},{9,8},{10,11... | collective-permute-start | bytes 393224 | tf_op jit(solution)/shard_map/ppermute | solution.py:320
  1.1 2.9 %collective-permute-start.1 = (f32[1,256,128]{2,1,0:T(8,128)}, f32[1,256,128]{2,1,0:T(8,128)S(1)}, u32[]{:S(2)}, u32[]{:S(2)}) collective-permute-start(f32[1,256,128]{2,1,0:T(8,128)} %proj_own_hbm.1), channel_id=1, source_target_pairs={{0,1},{1,0},{2,3},{3,2},{4,5},{5,4},{6,7},{7,6},{8,9},{9,8},{10,11... | collective-permute-start | bytes 393224 | tf_op jit(solution)/shard_map/ppermute | solution.py:320
  1.2 2.7 %collective-permute-start.4 = (f32[256]{0:T(256)}, f32[256]{0:T(256)S(1)}, u32[]{:S(2)}, u32[]{:S(2)}) collective-permute-start(f32[256]{0:T(256)} %weight_hbm.1), channel_id=1, source_target_pairs={{0,1},{1,0},{2,3},{3,2},{4,5},{5,4},{6,7},{7,6},{8,9},{9,8},{10,11... | collective-permute-start | bytes 3080 | tf_op jit(solution)/shard_map/ppermute | solution.py:320
  1.7 2.3 %collective-permute-start.2 = (f32[256]{0:T(256)}, f32[256]{0:T(256)S(1)}, u32[]{:S(2)}, u32[]{:S(2)}) collective-permute-start(f32[256]{0:T(256)} %tgt_energy_hbm.1), channel_id=1, source_target_pairs={{0,1},{1,0},{2,3},{3,2},{4,5},{5,4},{6,7},{7,6},{8,9},{9,8},{10,11... | collective-permute-start | bytes 3080 | tf_op jit(solution)/shard_map/ppermute | solution.py:320
  1.7 2.2 %collective-permute-start.3 = (f32[1,256]{1,0:T(1,128)}, f32[1,256]{1,0:T(1,128)S(1)}, u32[]{:S(2)}, u32[]{:S(2)}) collective-permute-start(f32[1,256]{1,0:T(1,128)} %proj_energy_hbm.1), channel_id=1, source_target_pairs={{0,1},{1,0},{2,3},{3,2},{4,5},{5,4},{6,7},{7,6},{8,9},{9,8},{10,11... | collective-permute-start | bytes 3080 | tf_op jit(solution)/shard_map/ppermute | solution.py:320
  4.2 3.5 %collective-permute-start.5 = (bf16[2,4,256,256]{3,2,1,0:T(8,128)(2,1)S(1)}, bf16[2,4,256,256]{3,2,1,0:T(8,128)(2,1)S(1)}, u32[]{:S(2)}, u32[]{:S(2)}) collective-permute-start(bf16[2,4,256,256]{3,2,1,0:T(8,128)(2,1)S(1)} %get-tuple-element.27.sent), channel_id=1, source_target_pairs={{0,1},{1,0},{2,3},{3,2},{4,5},{5,4},{6,7},{7,6},{8,9},{9,8},{10,11... | collective-permute-start | bytes 3145736 | tf_op jit(solution)/shard_map/ppermute | solution.py:320
  4.3 5.4 %collective-permute-start.6 = (bf16[2,144,256]{2,1,0:T(8,128)(2,1)S(1)}, bf16[2,144,256]{2,1,0:T(8,128)(2,1)S(1)}, u32[]{:S(2)}, u32[]{:S(2)}) collective-permute-start(bf16[2,144,256]{2,1,0:T(8,128)(2,1)S(1)} %get-tuple-element.31), channel_id=1, source_target_pairs={{0,3},{1,4},{3,0},{2,7},{5,6},{4,1},{6,5},{7,2},{9,10},{8,13},{10,... | collective-permute-start | bytes 442376 | tf_op jit(solution)/shard_map/ppermute | solution.py:335
  10.1 3.9 %collective-permute-start.7 = (bf16[128,256]{1,0:T(8,128)(2,1)S(1)}, bf16[128,256]{1,0:T(8,128)(2,1)S(1)}, u32[]{:S(2)}, u32[]{:S(2)}) collective-permute-start(bf16[128,256]{1,0:T(8,128)(2,1)S(1)} %get-tuple-element.32.own), channel_id=1, source_target_pairs={{0,5},{1,8},{3,6},{2,11},{5,0},{4,13},{6,3},{7,14},{9,12},{8,1},{1... | collective-permute-start | bytes 196616 | tf_op jit(solution)/shard_map/ppermute | solution.py:335
  12.0 5.4 %collective-permute-start.10 = (bf16[128,256]{1,0:T(8,128)(2,1)S(1)}, bf16[128,256]{1,0:T(8,128)(2,1)S(1)}, u32[]{:S(2)}, u32[]{:S(2)}) collective-permute-start(bf16[128,256]{1,0:T(8,128)(2,1)S(1)} %get-tuple-element.33.own), channel_id=1, source_target_pairs={{0,5},{1,8},{3,6},{2,11},{5,0},{4,13},{6,3},{7,14},{9,12},{8,1},{1... | collective-permute-start | bytes 196616 | tf_op jit(solution)/shard_map/ppermute | solution.py:335
  14.0 5.7 %collective-permute-start.8 = (bf16[128,256]{1,0:T(8,128)(2,1)S(1)}, bf16[128,256]{1,0:T(8,128)(2,1)S(1)}, u32[]{:S(2)}, u32[]{:S(2)}) collective-permute-start(bf16[128,256]{1,0:T(8,128)(2,1)S(1)} %shard_map.109.own), channel_id=1, source_target_pairs={{0,9},{1,2},{3,10},{2,1},{5,12},{4,7},{6,15},{7,4},{9,0},{8,11},{1... | collective-permute-start | bytes 196616 | tf_op jit(solution)/shard_map/ppermute | solution.py:335
  17.4 4.7 %collective-permute-start.11 = (bf16[128,256]{1,0:T(8,128)(2,1)S(1)}, bf16[128,256]{1,0:T(8,128)(2,1)S(1)}, u32[]{:S(2)}, u32[]{:S(2)}) collective-permute-start(bf16[128,256]{1,0:T(8,128)(2,1)S(1)} %shard_map.111.own), channel_id=1, source_target_pairs={{0,9},{1,2},{3,10},{2,1},{5,12},{4,7},{6,15},{7,4},{9,0},{8,11},{1... | collective-permute-start | bytes 196616 | tf_op jit(solution)/shard_map/ppermute | solution.py:335
  19.7 3.0 %collective-permute-start.9 = (bf16[128,256]{1,0:T(8,128)(2,1)S(1)}, bf16[128,256]{1,0:T(8,128)(2,1)S(1)}, u32[]{:S(2)}, u32[]{:S(2)}) collective-permute-start(bf16[128,256]{1,0:T(8,128)(2,1)S(1)} %shard_map.110), channel_id=1, source_target_pairs={{0,1},{1,0},{2,3},{3,2},{4,5},{5,4},{6,7},{7,6},{8,9},{9,8},{10,11... | collective-permute-start | bytes 196616 | tf_op jit(solution)/shard_map/ppermute | solution.py:320
  22.1 1.3 %collective-permute-start.12 = (bf16[128,256]{1,0:T(8,128)(2,1)S(1)}, bf16[128,256]{1,0:T(8,128)(2,1)S(1)}, u32[]{:S(2)}, u32[]{:S(2)}) collective-permute-start(bf16[128,256]{1,0:T(8,128)(2,1)S(1)} %shard_map.112), channel_id=1, source_target_pairs={{0,1},{1,0},{2,3},{3,2},{4,5},{5,4},{6,7},{7,6},{8,9},{9,8},{10,11... | collective-permute-start | bytes 196616 | tf_op jit(solution)/shard_map/ppermute | solution.py:320
  22.3 13.8 %collective-permute-start.19 = (bf16[2,256,256]{2,1,0:T(8,128)(2,1)S(1)}, bf16[2,256,256]{2,1,0:T(8,128)(2,1)S(1)}, u32[]{:S(2)}, u32[]{:S(2)}) collective-permute-start(bf16[2,256,256]{2,1,0:T(8,128)(2,1)S(1)} %get-tuple-element.38), channel_id=1, source_target_pairs={{0,1},{1,0},{2,3},{3,2},{4,5},{5,4},{6,7},{7,6},{8,9},{9,8},{10,11... | collective-permute-start | bytes 786440 | tf_op jit(solution)/shard_map/ppermute | solution.py:320
  24.5 3.8 %collective-permute-start.13 = (bf16[128,256]{1,0:T(8,128)(2,1)S(1)}, bf16[128,256]{1,0:T(8,128)(2,1)S(1)}, u32[]{:S(2)}, u32[]{:S(2)}) collective-permute-start(bf16[128,256]{1,0:T(8,128)(2,1)S(1)} %get-tuple-element.35.own), channel_id=1, source_target_pairs={{0,5},{1,8},{3,6},{2,11},{5,0},{4,13},{6,3},{7,14},{9,12},{8,1},{1... | collective-permute-start | bytes 196616 | tf_op jit(solution)/shard_map/ppermute | solution.py:335
  25.7 5.3 %collective-permute-start.16 = (bf16[128,256]{1,0:T(8,128)(2,1)S(1)}, bf16[128,256]{1,0:T(8,128)(2,1)S(1)}, u32[]{:S(2)}, u32[]{:S(2)}) collective-permute-start(bf16[128,256]{1,0:T(8,128)(2,1)S(1)} %get-tuple-element.36.own), channel_id=1, source_target_pairs={{0,5},{1,8},{3,6},{2,11},{5,0},{4,13},{6,3},{7,14},{9,12},{8,1},{1... | collective-permute-start | bytes 196616 | tf_op jit(solution)/shard_map/ppermute | solution.py:335
  26.4 9.7 %collective-permute-start.20 = (f32[128,256]{1,0:T(8,128)S(1)}, f32[128,256]{1,0:T(8,128)S(1)}, u32[]{:S(2)}, u32[]{:S(2)}) collective-permute-start(f32[128,256]{1,0:T(8,128)S(1)} %get-tuple-element.39), channel_id=1, source_target_pairs={{0,1},{1,0},{2,3},{3,2},{4,5},{5,4},{6,7},{7,6},{8,9},{9,8},{10,11... | collective-permute-start | bytes 393224 | tf_op jit(solution)/shard_map/ppermute | solution.py:320
  28.3 5.0 %collective-permute-start.14 = (bf16[128,256]{1,0:T(8,128)(2,1)S(1)}, bf16[128,256]{1,0:T(8,128)(2,1)S(1)}, u32[]{:S(2)}, u32[]{:S(2)}) collective-permute-start(bf16[128,256]{1,0:T(8,128)(2,1)S(1)} %shard_map.114.own), channel_id=1, source_target_pairs={{0,9},{1,2},{3,10},{2,1},{5,12},{4,7},{6,15},{7,4},{9,0},{8,11},{1... | collective-permute-start | bytes 196616 | tf_op jit(solution)/shard_map/ppermute | solution.py:335
  31.1 4.7 %collective-permute-start.17 = (bf16[128,256]{1,0:T(8,128)(2,1)S(1)}, bf16[128,256]{1,0:T(8,128)(2,1)S(1)}, u32[]{:S(2)}, u32[]{:S(2)}) collective-permute-start(bf16[128,256]{1,0:T(8,128)(2,1)S(1)} %shard_map.116.own), channel_id=1, source_target_pairs={{0,9},{1,2},{3,10},{2,1},{5,12},{4,7},{6,15},{7,4},{9,0},{8,11},{1... | collective-permute-start | bytes 196616 | tf_op jit(solution)/shard_map/ppermute | solution.py:335
  33.4 3.1 %collective-permute-start.15 = (bf16[128,256]{1,0:T(8,128)(2,1)S(1)}, bf16[128,256]{1,0:T(8,128)(2,1)S(1)}, u32[]{:S(2)}, u32[]{:S(2)}) collective-permute-start(bf16[128,256]{1,0:T(8,128)(2,1)S(1)} %shard_map.115.low), channel_id=1, source_target_pairs={{0,1},{1,0},{2,3},{3,2},{4,5},{5,4},{6,7},{7,6},{8,9},{9,8},{10,11... | collective-permute-start | bytes 196616 | tf_op jit(solution)/shard_map/ppermute | solution.py:320
  35.9 1.3 %collective-permute-start.18 = (bf16[128,256]{1,0:T(8,128)(2,1)S(1)}, bf16[128,256]{1,0:T(8,128)(2,1)S(1)}, u32[]{:S(2)}, u32[]{:S(2)}) collective-permute-start(bf16[128,256]{1,0:T(8,128)(2,1)S(1)} %shard_map.117.high), channel_id=1, source_target_pairs={{0,1},{1,0},{2,3},{3,2},{4,5},{5,4},{6,7},{7,6},{8,9},{9,8},{10,11... | collective-permute-start | bytes 196616 | tf_op jit(solution)/shard_map/ppermute | solution.py:320

commit v12 on v11

v12 whole, which is shorter than its diff:
```python
import functools

import jax
import jax.numpy as jnp
from jax import lax
from jax.experimental import pallas as pl
from jax.experimental.pallas import tpu as pltpu
from jax.sharding import PartitionSpec as P

time_step = 0.4
half_step = 0.5 * time_step
VMEM_LIMIT = 8 * 1024 * 1024
DEVICES = ("tgt", "prj", "rep")
HBM = pl.BlockSpec(memory_space=pl.ANY)
VMEM = pl.BlockSpec(memory_space=pltpu.VMEM)


def parity(place):
    odd = 0
    while place:
        odd, place = odd ^ (place & 1), place >> 1
    return odd


def my_kind():
    n_tgt, n_prj = lax.axis_size("tgt"), lax.axis_size("prj")
    place = lax.axis_index("tgt") * n_prj + lax.axis_index("prj")
    kind = lax.axis_index("rep")
    for bit in range((n_tgt * n_prj).bit_length() - 1):
        kind = jnp.bitwise_xor(kind, jnp.bitwise_and(lax.shift_right_logical(place, bit), 1))
    return kind


def by_core(body):
    for core in range(2):

        @pl.when(lax.axis_index("rep") == core)
        def _():
            body(core)


def ordered(core, first, second):
    return jnp.where(core == 0, first, second), jnp.where(core == 0, second, first)


def turned(block):
    half = block.shape[0] // 2
    return jnp.concatenate([block[half:], -block[:half]], axis=0)


def bf16(block):
    return block.astype(jnp.bfloat16)


def f32(block):
    return block.astype(jnp.float32)


def project(basis_real, basis_imag, amp):
    return jnp.dot(bf16(amp), basis_real, preferred_element_type=jnp.float32) + jnp.dot(
        bf16(turned(amp)), basis_imag, preferred_element_type=jnp.float32
    )


def expand(basis_real, basis_imag, field):
    contract = (((1,), (1,)), ((), ()))
    return lax.dot_general(
        turned(field), basis_real, contract, preferred_element_type=jnp.float32
    ) + lax.dot_general(field, basis_imag, contract, preferred_element_type=jnp.float32)


def load_kernel(
    neighbours,
    weight_hbm,
    tgt_hbm,
    proj_hbm,
    tgt_energy_hbm,
    proj_energy_hbm,
    tgt_own_hbm,
    proj_own_hbm,
    mine,
    sent,
    small,
    energy,
    amp_ref,
    flat_weight,
    flat_energy,
    tgt_own,
    proj_own,
    sems,
):
    my = my_kind()
    places = (lax.axis_index("prj"), lax.axis_index("tgt"))
    sources = (tgt_hbm, proj_hbm)

    def basis_copies(my):
        return [
            pltpu.make_async_copy(
                sources[kind].at[part, pl.ds(2 * place, 2)],
                basis.at[part, 2 * chip : 2 * chip + 2],
                sems.at[4 * slot + 2 * chip + part],
            )
            for slot, (kind, basis) in enumerate(((1 - my, sent), (my, mine)))
            for chip, place in enumerate(
                (places[kind], jnp.bitwise_xor(places[kind], neighbours[kind]))
            )
            for part in range(2)
        ]

    pairs = [
        (tgt_own_hbm, tgt_own),
        (proj_own_hbm, proj_own),
        (weight_hbm, flat_weight),
        (tgt_energy_hbm, flat_energy),
        (proj_energy_hbm, energy.at[1]),
    ]
    copies = [pltpu.make_async_copy(src, dst, sems.at[8 + k]) for k, (src, dst) in enumerate(pairs)]
    for copy in copies:
        copy.start()
    for kind in range(2):

        @pl.when(my == kind)
        def _():
            for copy in basis_copies(kind):
                copy.start()

    for copy in copies:
        copy.wait()
    energy[0] = flat_energy[...][None, :]
    small[0] = flat_weight[...][None, :]
    small[1, :, : energy.shape[2]] = energy[1 - my]
    amp_ref[0] = tgt_own[...].T
    amp_ref[1] = proj_own[0].T
    for copy in basis_copies(0):
        copy.wait()


def pack_kernel(amp_ref, mine, tgt_other, proj_other, chip_amp, message, send_own):
    core = lax.axis_index("rep")
    my = my_kind()
    other_amp, _ = ordered(my, tgt_other[...].T, proj_other[0].T)
    amps = ordered(core, amp_ref[my], other_amp)
    for segment in range(2):
        chip_amp[segment] = amps[segment]
        message[segment] = bf16(amps[segment])
    for part in range(2):
        send_own[part] = mine[part, 1 - core]


def small_kernel(small, far_small, energy, weights, energies):
    rows = energy.shape[2]
    core = lax.axis_index("rep")
    weights[0], weights[1] = ordered(core, small[0], far_small[0])
    energies[0], energies[1] = ordered(core, energy[my_kind()], far_small[1, :, :rows])


def side_kernel(gate_levels, flags_hbm, counts_hbm, chip_amp, gate, flags, counts, sems):
    my = my_kind()
    tgt_index = lax.axis_index("tgt")
    prj_index = lax.axis_index("prj")
    pairs = [(flags_hbm, flags), (counts_hbm, counts)]
    copies = [pltpu.make_async_copy(src, dst, sems.at[k]) for k, (src, dst) in enumerate(pairs)]
    for copy in copies:
        copy.start()
    for copy in copies:
        copy.wait()
    tiles = 2
    width = gate.shape[-1] // tiles
    gate_level = jnp.where(my == 0, *gate_levels)
    for half in range(2):
        for tile in range(tiles):
            live = jnp.logical_and(
                flags[prj_index, tgt_index] > 0, tiles * half + tile < counts[prj_index, tgt_index]
            )
            value = jnp.where(live, 1.0, 0.0).astype(jnp.float32)
            for level in range(gate.shape[0]):
                here = jnp.where(level == gate_level, value, jnp.float32(1.0))
                gate[level, half, :, tile * width : (tile + 1) * width] = jnp.full(
                    (1, width), here, jnp.float32
                )


def chip_kernel(mine, theirs, chip_amp, own_far, part_ref):
    def body(core):
        for half, basis in enumerate((mine, theirs) if core == 0 else (theirs, mine)):
            part_ref[half] = sum(
                project(basis[0, segment], basis[1, segment], chip_amp[segment]) for segment in range(2)
            )

    by_core(body)


def first_kernel(mine, theirs, gate, weights, part_ref, message, neighbour_energies, *outs):
    def body(core):
        for half, basis in enumerate((mine, theirs) if core == 0 else (theirs, mine)):
            total = part_ref[half] + sum(
                project(basis[0, 2 + segment], basis[1, 2 + segment], f32(message[segment]))
                for segment in range(2)
            )
            outs[half][...] = bf16(gate[0, half] * (weights[half] * total))

    by_core(body)


def add_kernel(level, half, gate, own, other, out_ref):
    out_ref[...] = bf16(gate[level, half] * (f32(own[...]) + f32(other[...])))


def low_kernel(mine, theirs, low, change_ref):
    def body(core):
        basis = (mine, theirs)[core]
        for segment in range(4):
            change_ref[segment] = expand(basis[0, segment], basis[1, segment], low[...])

    by_core(body)


def second_kernel(
    mine,
    theirs,
    change_ref,
    high,
    gate,
    weights,
    chip_amp,
    energies,
    message,
    neighbour_energies,
    low_ref,
    high_ref,
    half_ref,
    send_ref,
):
    def body(core):
        bases = (mine, theirs) if core == 0 else (theirs, mine)
        halves = []
        for segment in range(4):
            if segment < 2:
                amp, energy = chip_amp[segment], energies[segment]
            else:
                amp, energy = f32(message[segment - 2]), neighbour_energies[segment - 2]
            change = change_ref[segment] + expand(bases[1][0, segment], bases[1][1, segment], high[...])
            halves.append(amp + half_step * (energy * turned(amp) + change))
        half_ref[...] = halves[core]
        send_ref[...] = halves[1 - core]
        for half, out_ref in enumerate((low_ref, high_ref)):
            total = sum(
                project(bases[half][0, segment], bases[half][1, segment], halves[segment])
                for segment in range(4)
            )
            out_ref[...] = bf16(gate[0, half] * (weights[half] * total))

    by_core(body)


def other_last_kernel(sent, own_far, low, high, energy, amp_ref, half_ref, new_ref):
    def body(core):
        near, far = (low, high) if core == 0 else (high, low)
        kind = 1 - my_kind()
        change = expand(sent[0, core], sent[1, core], near[...]) + expand(own_far[0], own_far[1], far[...])
        rate = energy[kind] * turned(half_ref[...]) + change
        new_ref[...] = (amp_ref[kind] + time_step * rate).T

    by_core(body)


def last_kernel(mine, theirs, low, high, energy, amp_ref, half_ref, other_new, new_tgt, new_proj):
    def body(core):
        near, far = (low, high) if core == 0 else (high, low)
        my = my_kind()
        change = expand(mine[0, core], mine[1, core], near[...]) + expand(
            theirs[0, core], theirs[1, core], far[...]
        )
        rate = energy[my] * turned(half_ref[...]) + change
        my_new = (amp_ref[my] + time_step * rate).T
        new_tgt[...], new_proj[0] = ordered(my, my_new, other_new[...])

    by_core(body)


def shards(
    tgt_basis,
    proj_basis,
    quad_weight,
    tgt_energy,
    proj_energy,
    pair_flags,
    tile_counts,
    tgt_amp,
    proj_amp,
):
    points = quad_weight.shape[0]
    rows, two_cols = tgt_amp.shape
    sizes = [lax.axis_size(axis) for axis in DEVICES]

    def call(kernel, out_shape, in_specs, scratch_shapes=(), cost=None):
        return pl.pallas_call(
            kernel,
            out_shape=out_shape,
            in_specs=in_specs,
            out_specs=[VMEM] * len(out_shape),
            scratch_shapes=scratch_shapes,
            cost_estimate=cost,
            compiler_params=pltpu.CompilerParams(vmem_limit_bytes=VMEM_LIMIT),
        )

    def run(kernel, out_shape, *blocks):
        return call(kernel, out_shape, [VMEM] * len(blocks))(*blocks)

    def other_core(block):
        return lax.ppermute(block, "rep", [(0, 1), (1, 0)])

    n_tgt, n_prj, n_core = sizes
    tgt_flips = [n_prj << bit for bit in range(n_tgt.bit_length() - 1)]
    prj_flips = [1 << bit for bit in range(n_prj.bit_length() - 1)]
    flips = (prj_flips + tgt_flips[::-1], tgt_flips[::-1] + prj_flips)
    neighbours = (flips[0][0], flips[1][0] // n_prj)
    gate_levels = (len(prj_flips) - 1, len(tgt_flips) - 1)
    n_steps = len(tgt_flips) + len(prj_flips)

    def exchanged(step, block):
        pairs = []
        for place in range(n_tgt * n_prj):
            for kind in range(2):
                there = place ^ flips[kind][step]
                pairs.append((place * n_core + (kind ^ parity(place)), there * n_core + (kind ^ parity(there))))
        return lax.ppermute(block, DEVICES, pairs)

    in_vmem = pltpu.VMEM
    basis = in_vmem((2, 4, rows, points), jnp.bfloat16)
    sums = in_vmem((two_cols, points), jnp.bfloat16)
    segment = in_vmem((two_cols, rows), jnp.float32)

    def summed(*halves):
        totals = []
        for half, block in enumerate(halves):
            for step in range(1, n_steps):
                other = exchanged(step, block)
                (block,) = run(functools.partial(add_kernel, step, half), [sums], gate, block, other)
            totals.append(block)
        return totals

    def swapped(fields):
        return [other_core(block) for block in fields]

    def in_hbm(*blocks):
        return [pltpu.with_memory_space_constraint(block, pltpu.HBM) for block in blocks]

    tgt_other, proj_other = other_core(tgt_amp), other_core(proj_amp)
    bases = (tgt_basis.reshape(2, -1, rows, points), proj_basis)
    mine, sent, small, energy, amp = call(
        functools.partial(load_kernel, neighbours),
        [
            basis,
            basis,
            in_vmem((2, 1, points), jnp.float32),
            in_vmem((2, 1, rows), jnp.float32),
            in_vmem((2, two_cols, rows), jnp.float32),
        ],
        [HBM] * 7,
        [
            pltpu.VMEM((points,), jnp.float32),
            pltpu.VMEM((rows,), jnp.float32),
            pltpu.VMEM(tgt_amp.shape, jnp.float32),
            pltpu.VMEM(proj_amp.shape, jnp.float32),
            pltpu.SemaphoreType.DMA((13,)),
        ],
        pl.CostEstimate(
            flops=2 * 4 * rows * two_cols * points, bytes_accessed=4 * 1024 * 1024, transcendentals=0
        ),
    )(*in_hbm(quad_weight, *bases, tgt_energy, proj_energy, tgt_amp, proj_amp))
    chip_amp, message, send_own = run(
        pack_kernel,
        [
            in_vmem((2, two_cols, rows), jnp.float32),
            in_vmem((2, two_cols, rows), jnp.bfloat16),
            in_vmem((2, rows, points), jnp.bfloat16),
        ],
        amp,
        mine,
        tgt_other,
        proj_other,
    )
    sent, small, send_own, message = lax.optimization_barrier((sent, small, send_own, message))
    theirs, far_small, own_far = swapped([sent, small, send_own])
    message = exchanged(0, message)
    weights, energies = run(
        small_kernel,
        [in_vmem((2, 1, points), jnp.float32), in_vmem((2, 1, rows), jnp.float32)],
        small,
        far_small,
        energy,
    )
    neighbour_energies = exchanged(0, energies)
    flags, counts = pair_flags.T, tile_counts.T
    (gate,) = call(
        functools.partial(side_kernel, gate_levels),
        [in_vmem((n_steps, 2, 1, points), jnp.float32)],
        [HBM, HBM, VMEM],
        [
            pltpu.SMEM(flags.shape, jnp.int32),
            pltpu.SMEM(counts.shape, jnp.int32),
            pltpu.SemaphoreType.DMA((2,)),
        ],
    )(*in_hbm(flags, counts), chip_amp)
    (part,) = run(
        chip_kernel, [in_vmem((2, two_cols, points), jnp.float32)], mine, theirs, chip_amp, own_far
    )
    halves = run(
        first_kernel, [sums] * 2, mine, theirs, gate, weights, part, message, neighbour_energies
    )
    fields = summed(*halves)
    low, high = swapped(fields)
    (change,) = run(low_kernel, [in_vmem((4, two_cols, rows), jnp.float32)], mine, theirs, low)
    *halves, my_half, half_send = run(
        second_kernel,
        [sums, sums, segment, segment],
        mine,
        theirs,
        change,
        high,
        gate,
        weights,
        chip_amp,
        energies,
        message,
        neighbour_energies,
    )
    other_half = other_core(half_send)
    fields = summed(*halves)
    (other_new,) = run(
        other_last_kernel,
        [in_vmem((rows, two_cols), jnp.float32)],
        sent,
        own_far,
        *fields,
        energy,
        amp,
        other_half,
    )
    return run(
        last_kernel,
        [
            jax.ShapeDtypeStruct(tgt_amp.shape, jnp.float32),
            jax.ShapeDtypeStruct(proj_amp.shape, jnp.float32),
        ],
        mine,
        theirs,
        *swapped(fields),
        energy,
        amp,
        my_half,
        other_new,
    )


def solution(mesh):
    in_specs = (
        P(None, "tgt", "rep"),
        P(None, None, "prj", "rep"),
        P(("bpar", "rep")),
        P(("tgt", "prj", "rep")),
        P(("tgt", "rep"), "prj"),
        P("bpar", None),
        P("bpar", None),
        P(("bpar", "tgt", "prj", "rep"), None),
        P(("bpar", "tgt", "rep"), "prj", None),
    )
    out_specs = (P(("bpar", "tgt", "prj", "rep"), None), P(("bpar", "tgt", "rep"), "prj", None))

    def step(*args):
        return tuple(shards(*args))

    return jax.shard_map(step, mesh=mesh, in_specs=in_specs, out_specs=out_specs, check_vma=False)
```

time: 38.4 us -> 38.1 us (level)
  starting transfers between devices: 20.1 us -> 18.6 us
  waiting for transfers between devices: 11.3 us -> 12.2 us
    ppermute x12 -> x10, starting transfers between devices: 4.44 us -> 3.51 us  [other_core(): return lax.ppermute(block, 'rep', [(0, 1), (1, 0)])]
    ppermute x12 -> x10, waiting for transfers between devices: 1.47 us -> 2.3 us  [other_core(): return lax.ppermute(block, 'rep', [(0, 1), (1, 0)])]
    ppermute x9 -> x10, starting transfers between devices: 15.6 us -> 15.1 us  [exchanged(): return lax.ppermute(block, DEVICES, pairs)]
    pallas_call x14 -> x16, Pallas kernels: 3.57 us -> 3.78 us  [run(): return call(kernel, out_shape, [VMEM] * len(blocks))(*blocks)]
    ppermute x9 -> x10, waiting for transfers between devices: 9.83 us -> 9.94 us  [exchanged(): return lax.ppermute(block, DEVICES, pairs)]
  transfers between devices with their start and end apart: 21 -> 20, of which waited for: 9 -> 12; matrix products, arithmetic and copies ran while one was open for 0% -> 0% of each run, Pallas kernels for 12% -> 10%
where the time goes in v12:
time: 38.1 us; the launch traced here: 37.9 us
  starting transfers between devices  18.6 us (49%)
  waiting for transfers between devices  12.2 us (32%)
  Pallas kernels  6.31 us (17%)
  between operations  0.79 us (2%)
    ppermute x10, starting transfers between devices, exchanged(): return lax.ppermute(block, DEVICES, pairs)  15.1 us
    ppermute x10, waiting for transfers between devices, exchanged(): return lax.ppermute(block, DEVICES, pairs)  9.94 us
    pallas_call x16, Pallas kernels, run(): return call(kernel, out_shape, [VMEM] * len(blocks))(*blocks)  3.78 us
    ppermute x10, starting transfers between devices, other_core(): return lax.ppermute(block, 'rep', [(0, 1), (1, 0)])  3.51 us
    ppermute x10, waiting for transfers between devices, other_core(): return lax.ppermute(block, 'rep', [(0, 1), (1, 0)])  2.3 us
    pallas_call x1, Pallas kernels, shards(): call(functools.partial(load_kernel, neighbours), [basis, basis, in_vmem((...  1.8 us
  transfers between devices with their start and end apart: 20, of which 12 were waited for; matrix products, arithmetic and copies ran while one was open for 0% of the time, Pallas kernels for 10%

profile of v12, /device:TPU:0, one launch (start us, length us, event | category | flops | bytes accessed | tf_op | source)
XLA Modules:
  0.0 37.9 jit_solution(183103994110113695)
XLA Ops:
  1.2 1.8 %shard_map.104 = (bf16[2,4,256,256]{3,2,1,0:T(8,128)(2,1)S(1)}, bf16[2,4,256,256]{3,2,1,0:T(8,128)(2,1)S(1)}, f32[2,1,256]{2,1,0:T(1,128)S(1)}, f32[2,1,256]{2,1,0:T(1,128)S(1)}, f32[2,128,256]{2,1,0:T(8,128)S(1)}) custom-call(f32[256]{0:T(256)} %weight_hbm.1, bf16[2,4,256,256]{3,2,1,0:T(8,128)(2,1)} %bitcast.3, bf16[2,8,256,256]{3,2,1,0:T(8,128)(2,1)} %proj_hbm.1, ...), custom_call_target="tpu_custom_call" | custom-call | flops 67108864 | bytes 4194304 | tf_op jit(solution)/shard_map/pallas_call | solution.py:351
  3.8 2.6 %collective-permute-start.5 = (bf16[2,128,256]{2,1,0:T(8,128)(2,1)S(1)}, bf16[2,128,256]{2,1,0:T(8,128)(2,1)S(1)}, u32[]{:S(2)}, u32[]{:S(2)}) collective-permute-start(bf16[2,128,256]{2,1,0:T(8,128)(2,1)S(1)} %get-tuple-element.34), channel_id=1, source_target_pairs={{0,3},{1,8},{3,0},{2,11},{5,6},{4,13},{6,5},{7,14},{9,10},{8,1},{1... | collective-permute-start | bytes 393224 | tf_op jit(solution)/shard_map/ppermute | solution.py:327
  6.4 1.5 %collective-permute-start.3 = (f32[2,1,256]{2,1,0:T(1,128)S(1)}, f32[2,1,256]{2,1,0:T(1,128)S(1)}, u32[]{:S(2)}, u32[]{:S(2)}) collective-permute-start(f32[2,1,256]{2,1,0:T(1,128)S(1)} %get-tuple-element.30.small), channel_id=1, source_target_pairs={{0,1},{1,0},{2,3},{3,2},{4,5},{5,4},{6,7},{7,6},{8,9},{9,8},{10,11... | collective-permute-start | bytes 6152 | tf_op jit(solution)/shard_map/ppermute | solution.py:311
  7.9 0.8 %collective-permute-done.3.far_small = f32[2,1,256]{2,1,0:T(1,128)S(1)} collective-permute-done((f32[2,1,256]{2,1,0:T(1,128)S(1)}, f32[2,1,256]{2,1,0:T(1,128)S(1)}, u32[]{:S(2)}, u32[]{:S(2)}) %collective-permute-start.3) | collective-permute-done | bytes 2080 | tf_op jit(solution)/shard_map/ppermute | solution.py:311
  8.7 1.2 %collective-permute-start.6 = (f32[2,1,256]{2,1,0:T(1,128)S(1)}, f32[2,1,256]{2,1,0:T(1,128)S(1)}, u32[]{:S(2)}, u32[]{:S(2)}) collective-permute-start(f32[2,1,256]{2,1,0:T(1,128)S(1)} %get-tuple-element.35.energies), channel_id=1, source_target_pairs={{0,3},{1,8},{3,0},{2,11},{5,6},{4,13},{6,5},{7,14},{9,10},{8,1},{1... | collective-permute-start | bytes 6152 | tf_op jit(solution)/shard_map/ppermute | solution.py:327
  9.9 0.7 %shard_map.106.gate = f32[3,2,1,256]{3,2,1,0:T(1,128)S(1)} custom-call(s32[2,4]{1,0:T(2,128)} %bitcast.4, s32[2,4]{1,0:T(2,128)} %bitcast.5, f32[2,128,256]{2,1,0:T(8,128)S(1)} %get-tuple-element.29.chip_amp), custom_call_target="tpu_custom_call" | custom-call | tf_op jit(solution)/shard_map/pallas_call | solution.py:396
  11.0 0.7 %collective-permute-done.6.neighbour_energies = f32[2,1,256]{2,1,0:T(1,128)S(1)} collective-permute-done((f32[2,1,256]{2,1,0:T(1,128)S(1)}, f32[2,1,256]{2,1,0:T(1,128)S(1)}, u32[]{:S(2)}, u32[]{:S(2)}) %collective-permute-start.6) | collective-permute-done | bytes 2080 | tf_op jit(solution)/shard_map/ppermute | solution.py:327
  12.1 1.5 %collective-permute-start.7 = (bf16[128,256]{1,0:T(8,128)(2,1)S(1)}, bf16[128,256]{1,0:T(8,128)(2,1)S(1)}, u32[]{:S(2)}, u32[]{:S(2)}) collective-permute-start(bf16[128,256]{1,0:T(8,128)(2,1)S(1)} %get-tuple-element.36.own), channel_id=1, source_target_pairs={{0,9},{1,4},{3,10},{2,7},{5,12},{4,1},{6,15},{7,2},{9,0},{8,13},{1... | collective-permute-start | bytes 196616 | tf_op jit(solution)/shard_map/ppermute | solution.py:327
  13.6 1.2 %collective-permute-start.10 = (bf16[128,256]{1,0:T(8,128)(2,1)S(1)}, bf16[128,256]{1,0:T(8,128)(2,1)S(1)}, u32[]{:S(2)}, u32[]{:S(2)}) collective-permute-start(bf16[128,256]{1,0:T(8,128)(2,1)S(1)} %get-tuple-element.37.own), channel_id=1, source_target_pairs={{0,9},{1,4},{3,10},{2,7},{5,12},{4,1},{6,15},{7,2},{9,0},{8,13},{1... | collective-permute-start | bytes 196616 | tf_op jit(solution)/shard_map/ppermute | solution.py:327
  14.8 2.0 %collective-permute-done.7.other = bf16[128,256]{1,0:T(8,128)(2,1)S(1)} collective-permute-done((bf16[128,256]{1,0:T(8,128)(2,1)S(1)}, bf16[128,256]{1,0:T(8,128)(2,1)S(1)}, u32[]{:S(2)}, u32[]{:S(2)}) %collective-permute-start.7) | collective-permute-done | bytes 65568 | tf_op jit(solution)/shard_map/ppermute | solution.py:327
  16.8 2.0 %collective-permute-start.8 = (bf16[128,256]{1,0:T(8,128)(2,1)S(1)}, bf16[128,256]{1,0:T(8,128)(2,1)S(1)}, u32[]{:S(2)}, u32[]{:S(2)}) collective-permute-start(bf16[128,256]{1,0:T(8,128)(2,1)S(1)} %shard_map.110.own), channel_id=1, source_target_pairs={{0,5},{1,2},{3,6},{2,1},{5,0},{4,7},{6,3},{7,4},{9,12},{8,11},{10,... | collective-permute-start | bytes 196616 | tf_op jit(solution)/shard_map/ppermute | solution.py:327
  18.9 1.1 %collective-permute-start.11 = (bf16[128,256]{1,0:T(8,128)(2,1)S(1)}, bf16[128,256]{1,0:T(8,128)(2,1)S(1)}, u32[]{:S(2)}, u32[]{:S(2)}) collective-permute-start(bf16[128,256]{1,0:T(8,128)(2,1)S(1)} %shard_map.113.own), channel_id=1, source_target_pairs={{0,5},{1,2},{3,6},{2,1},{5,0},{4,7},{6,3},{7,4},{9,12},{8,11},{10,... | collective-permute-start | bytes 196616 | tf_op jit(solution)/shard_map/ppermute | solution.py:327
  20.0 0.7 %collective-permute-done.8.other = bf16[128,256]{1,0:T(8,128)(2,1)S(1)} collective-permute-done((bf16[128,256]{1,0:T(8,128)(2,1)S(1)}, bf16[128,256]{1,0:T(8,128)(2,1)S(1)}, u32[]{:S(2)}, u32[]{:S(2)}) %collective-permute-start.8) | collective-permute-done | bytes 65568 | tf_op jit(solution)/shard_map/ppermute | solution.py:327
  21.1 1.5 %collective-permute-done.11.other = bf16[128,256]{1,0:T(8,128)(2,1)S(1)} collective-permute-done((bf16[128,256]{1,0:T(8,128)(2,1)S(1)}, bf16[128,256]{1,0:T(8,128)(2,1)S(1)}, u32[]{:S(2)}, u32[]{:S(2)}) %collective-permute-start.11) | collective-permute-done | bytes 65568 | tf_op jit(solution)/shard_map/ppermute | solution.py:327
  24.0 0.8 %shard_map.115 = (bf16[128,256]{1,0:T(8,128)(2,1)S(1)}, bf16[128,256]{1,0:T(8,128)(2,1)S(1)}, f32[128,256]{1,0:T(8,128)S(1)}, f32[128,256]{1,0:T(8,128)S(1)}) custom-call(bf16[2,4,256,256]{3,2,1,0:T(8,128)(2,1)S(1)} %get-tuple-element.22.mine, bf16[2,4,256,256]{3,2,1,0:T(8,128)(2,1)S(1)} %collective-permute-done.2.theirs, ...), custom_call_target="tpu_custom_call" | custom-call | tf_op jit(solution)/shard_map/pallas_call | solution.py:308
  24.9 1.6 %collective-permute-start.13 = (bf16[128,256]{1,0:T(8,128)(2,1)S(1)}, bf16[128,256]{1,0:T(8,128)(2,1)S(1)}, u32[]{:S(2)}, u32[]{:S(2)}) collective-permute-start(bf16[128,256]{1,0:T(8,128)(2,1)S(1)} %get-tuple-element.38.own), channel_id=1, source_target_pairs={{0,9},{1,4},{3,10},{2,7},{5,12},{4,1},{6,15},{7,2},{9,0},{8,13},{1... | collective-permute-start | bytes 196616 | tf_op jit(solution)/shard_map/ppermute | solution.py:327
  26.4 1.1 %collective-permute-start.16 = (bf16[128,256]{1,0:T(8,128)(2,1)S(1)}, bf16[128,256]{1,0:T(8,128)(2,1)S(1)}, u32[]{:S(2)}, u32[]{:S(2)}) collective-permute-start(bf16[128,256]{1,0:T(8,128)(2,1)S(1)} %get-tuple-element.39.own), channel_id=1, source_target_pairs={{0,9},{1,4},{3,10},{2,7},{5,12},{4,1},{6,15},{7,2},{9,0},{8,13},{1... | collective-permute-start | bytes 196616 | tf_op jit(solution)/shard_map/ppermute | solution.py:327
  27.6 2.0 %collective-permute-done.13.other = bf16[128,256]{1,0:T(8,128)(2,1)S(1)} collective-permute-done((bf16[128,256]{1,0:T(8,128)(2,1)S(1)}, bf16[128,256]{1,0:T(8,128)(2,1)S(1)}, u32[]{:S(2)}, u32[]{:S(2)}) %collective-permute-start.13) | collective-permute-done | bytes 65568 | tf_op jit(solution)/shard_map/ppermute | solution.py:327
  29.7 1.9 %collective-permute-start.14 = (bf16[128,256]{1,0:T(8,128)(2,1)S(1)}, bf16[128,256]{1,0:T(8,128)(2,1)S(1)}, u32[]{:S(2)}, u32[]{:S(2)}) collective-permute-start(bf16[128,256]{1,0:T(8,128)(2,1)S(1)} %shard_map.116.own), channel_id=1, source_target_pairs={{0,5},{1,2},{3,6},{2,1},{5,0},{4,7},{6,3},{7,4},{9,12},{8,11},{10,... | collective-permute-start | bytes 196616 | tf_op jit(solution)/shard_map/ppermute | solution.py:327
  31.8 0.9 %collective-permute-start.17 = (bf16[128,256]{1,0:T(8,128)(2,1)S(1)}, bf16[128,256]{1,0:T(8,128)(2,1)S(1)}, u32[]{:S(2)}, u32[]{:S(2)}) collective-permute-start(bf16[128,256]{1,0:T(8,128)(2,1)S(1)} %shard_map.118.own), channel_id=1, source_target_pairs={{0,5},{1,2},{3,6},{2,1},{5,0},{4,7},{6,3},{7,4},{9,12},{8,11},{10,... | collective-permute-start | bytes 196616 | tf_op jit(solution)/shard_map/ppermute | solution.py:327
  32.6 0.8 %collective-permute-done.14.other = bf16[128,256]{1,0:T(8,128)(2,1)S(1)} collective-permute-done((bf16[128,256]{1,0:T(8,128)(2,1)S(1)}, bf16[128,256]{1,0:T(8,128)(2,1)S(1)}, u32[]{:S(2)}, u32[]{:S(2)}) %collective-permute-start.14) | collective-permute-done | bytes 65568 | tf_op jit(solution)/shard_map/ppermute | solution.py:327
  33.7 1.8 %collective-permute-done.17.other = bf16[128,256]{1,0:T(8,128)(2,1)S(1)} collective-permute-done((bf16[128,256]{1,0:T(8,128)(2,1)S(1)}, bf16[128,256]{1,0:T(8,128)(2,1)S(1)}, u32[]{:S(2)}, u32[]{:S(2)}) %collective-permute-start.17) | collective-permute-done | bytes 65568 | tf_op jit(solution)/shard_map/ppermute | solution.py:327
  36.0 0.8 %collective-permute-done.18.high = bf16[128,256]{1,0:T(8,128)(2,1)S(1)} collective-permute-done((bf16[128,256]{1,0:T(8,128)(2,1)S(1)}, bf16[128,256]{1,0:T(8,128)(2,1)S(1)}, u32[]{:S(2)}, u32[]{:S(2)}) %collective-permute-start.18) | collective-permute-done | bytes 65568 | tf_op jit(solution)/shard_map/ppermute | solution.py:311
  36.9 1.1 %shard_map.121 = (f32[256,128]{1,0:T(8,128)}, f32[1,256,128]{2,1,0:T(8,128)}) custom-call(bf16[2,4,256,256]{3,2,1,0:T(8,128)(2,1)S(1)} %get-tuple-element.22.mine, bf16[2,4,256,256]{3,2,1,0:T(8,128)(2,1)S(1)} %collective-permute-done.2.theirs, bf16[128,256]{1,0:T(8,128)(2,1)S(1)} %collective-permute-done.15.low, ...), custom_call_target="tpu_custom_call" | custom-call | tf_op jit(solution)/shard_map/pallas_call | solution.py:308
  (34 shorter events, 4.8 us)
Async XLA Ops:
  0.6 2.4 %collective-permute-start = (f32[256,128]{1,0:T(8,128)}, f32[256,128]{1,0:T(8,128)S(1)}, u32[]{:S(2)}, u32[]{:S(2)}) collective-permute-start(f32[256,128]{1,0:T(8,128)} %tgt_own_hbm.1), channel_id=1, source_target_pairs={{0,1},{1,0},{2,3},{3,2},{4,5},{5,4},{6,7},{7,6},{8,9},{9,8},{10,11... | collective-permute-start | bytes 393224 | tf_op jit(solution)/shard_map/ppermute | solution.py:311
  1.1 1.9 %collective-permute-start.1 = (f32[1,256,128]{2,1,0:T(8,128)}, f32[1,256,128]{2,1,0:T(8,128)S(1)}, u32[]{:S(2)}, u32[]{:S(2)}) collective-permute-start(f32[1,256,128]{2,1,0:T(8,128)} %proj_own_hbm.1), channel_id=1, source_target_pairs={{0,1},{1,0},{2,3},{3,2},{4,5},{5,4},{6,7},{7,6},{8,9},{9,8},{10,11... | collective-permute-start | bytes 393224 | tf_op jit(solution)/shard_map/ppermute | solution.py:311
  3.2 7.5 %collective-permute-start.2 = (bf16[2,4,256,256]{3,2,1,0:T(8,128)(2,1)S(1)}, bf16[2,4,256,256]{3,2,1,0:T(8,128)(2,1)S(1)}, u32[]{:S(2)}, u32[]{:S(2)}) collective-permute-start(bf16[2,4,256,256]{3,2,1,0:T(8,128)(2,1)S(1)} %get-tuple-element.28.sent), channel_id=1, source_target_pairs={{0,1},{1,0},{2,3},{3,2},{4,5},{5,4},{6,7},{7,6},{8,9},{9,8},{10,11... | collective-permute-start | bytes 3145736 | tf_op jit(solution)/shard_map/ppermute | solution.py:311
  3.7 7.0 %collective-permute-start.4 = (bf16[2,256,256]{2,1,0:T(8,128)(2,1)S(1)}, bf16[2,256,256]{2,1,0:T(8,128)(2,1)S(1)}, u32[]{:S(2)}, u32[]{:S(2)}) collective-permute-start(bf16[2,256,256]{2,1,0:T(8,128)(2,1)S(1)} %get-tuple-element.33), channel_id=1, source_target_pairs={{0,1},{1,0},{2,3},{3,2},{4,5},{5,4},{6,7},{7,6},{8,9},{9,8},{10,11... | collective-permute-start | bytes 786440 | tf_op jit(solution)/shard_map/ppermute | solution.py:311
  3.8 8.0 %collective-permute-start.5 = (bf16[2,128,256]{2,1,0:T(8,128)(2,1)S(1)}, bf16[2,128,256]{2,1,0:T(8,128)(2,1)S(1)}, u32[]{:S(2)}, u32[]{:S(2)}) collective-permute-start(bf16[2,128,256]{2,1,0:T(8,128)(2,1)S(1)} %get-tuple-element.34), channel_id=1, source_target_pairs={{0,3},{1,8},{3,0},{2,11},{5,6},{4,13},{6,5},{7,14},{9,10},{8,1},{1... | collective-permute-start | bytes 393224 | tf_op jit(solution)/shard_map/ppermute | solution.py:327
  6.4 2.4 %collective-permute-start.3 = (f32[2,1,256]{2,1,0:T(1,128)S(1)}, f32[2,1,256]{2,1,0:T(1,128)S(1)}, u32[]{:S(2)}, u32[]{:S(2)}) collective-permute-start(f32[2,1,256]{2,1,0:T(1,128)S(1)} %get-tuple-element.30.small), channel_id=1, source_target_pairs={{0,1},{1,0},{2,3},{3,2},{4,5},{5,4},{6,7},{7,6},{8,9},{9,8},{10,11... | collective-permute-start | bytes 6152 | tf_op jit(solution)/shard_map/ppermute | solution.py:311
  8.7 3.0 %collective-permute-start.6 = (f32[2,1,256]{2,1,0:T(1,128)S(1)}, f32[2,1,256]{2,1,0:T(1,128)S(1)}, u32[]{:S(2)}, u32[]{:S(2)}) collective-permute-start(f32[2,1,256]{2,1,0:T(1,128)S(1)} %get-tuple-element.35.energies), channel_id=1, source_target_pairs={{0,3},{1,8},{3,0},{2,11},{5,6},{4,13},{6,5},{7,14},{9,10},{8,1},{1... | collective-permute-start | bytes 6152 | tf_op jit(solution)/shard_map/ppermute | solution.py:327
  12.1 4.7 %collective-permute-start.7 = (bf16[128,256]{1,0:T(8,128)(2,1)S(1)}, bf16[128,256]{1,0:T(8,128)(2,1)S(1)}, u32[]{:S(2)}, u32[]{:S(2)}) collective-permute-start(bf16[128,256]{1,0:T(8,128)(2,1)S(1)} %get-tuple-element.36.own), channel_id=1, source_target_pairs={{0,9},{1,4},{3,10},{2,7},{5,12},{4,1},{6,15},{7,2},{9,0},{8,13},{1... | collective-permute-start | bytes 196616 | tf_op jit(solution)/shard_map/ppermute | solution.py:327
  13.6 5.3 %collective-permute-start.10 = (bf16[128,256]{1,0:T(8,128)(2,1)S(1)}, bf16[128,256]{1,0:T(8,128)(2,1)S(1)}, u32[]{:S(2)}, u32[]{:S(2)}) collective-permute-start(bf16[128,256]{1,0:T(8,128)(2,1)S(1)} %get-tuple-element.37.own), channel_id=1, source_target_pairs={{0,9},{1,4},{3,10},{2,7},{5,12},{4,1},{6,15},{7,2},{9,0},{8,13},{1... | collective-permute-start | bytes 196616 | tf_op jit(solution)/shard_map/ppermute | solution.py:327
  16.8 4.0 %collective-permute-start.8 = (bf16[128,256]{1,0:T(8,128)(2,1)S(1)}, bf16[128,256]{1,0:T(8,128)(2,1)S(1)}, u32[]{:S(2)}, u32[]{:S(2)}) collective-permute-start(bf16[128,256]{1,0:T(8,128)(2,1)S(1)} %shard_map.110.own), channel_id=1, source_target_pairs={{0,5},{1,2},{3,6},{2,1},{5,0},{4,7},{6,3},{7,4},{9,12},{8,11},{10,... | collective-permute-start | bytes 196616 | tf_op jit(solution)/shard_map/ppermute | solution.py:327
  18.9 3.8 %collective-permute-start.11 = (bf16[128,256]{1,0:T(8,128)(2,1)S(1)}, bf16[128,256]{1,0:T(8,128)(2,1)S(1)}, u32[]{:S(2)}, u32[]{:S(2)}) collective-permute-start(bf16[128,256]{1,0:T(8,128)(2,1)S(1)} %shard_map.113.own), channel_id=1, source_target_pairs={{0,5},{1,2},{3,6},{2,1},{5,0},{4,7},{6,3},{7,4},{9,12},{8,11},{10,... | collective-permute-start | bytes 196616 | tf_op jit(solution)/shard_map/ppermute | solution.py:327
  20.8 2.1 %collective-permute-start.9 = (bf16[128,256]{1,0:T(8,128)(2,1)S(1)}, bf16[128,256]{1,0:T(8,128)(2,1)S(1)}, u32[]{:S(2)}, u32[]{:S(2)}) collective-permute-start(bf16[128,256]{1,0:T(8,128)(2,1)S(1)} %shard_map.111), channel_id=1, source_target_pairs={{0,1},{1,0},{2,3},{3,2},{4,5},{5,4},{6,7},{7,6},{8,9},{9,8},{10,11... | collective-permute-start | bytes 196616 | tf_op jit(solution)/shard_map/ppermute | solution.py:311
  22.7 1.3 %collective-permute-start.12 = (bf16[128,256]{1,0:T(8,128)(2,1)S(1)}, bf16[128,256]{1,0:T(8,128)(2,1)S(1)}, u32[]{:S(2)}, u32[]{:S(2)}) collective-permute-start(bf16[128,256]{1,0:T(8,128)(2,1)S(1)} %shard_map.114), channel_id=1, source_target_pairs={{0,1},{1,0},{2,3},{3,2},{4,5},{5,4},{6,7},{7,6},{8,9},{9,8},{10,11... | collective-permute-start | bytes 196616 | tf_op jit(solution)/shard_map/ppermute | solution.py:311
  24.9 4.8 %collective-permute-start.13 = (bf16[128,256]{1,0:T(8,128)(2,1)S(1)}, bf16[128,256]{1,0:T(8,128)(2,1)S(1)}, u32[]{:S(2)}, u32[]{:S(2)}) collective-permute-start(bf16[128,256]{1,0:T(8,128)(2,1)S(1)} %get-tuple-element.38.own), channel_id=1, source_target_pairs={{0,9},{1,4},{3,10},{2,7},{5,12},{4,1},{6,15},{7,2},{9,0},{8,13},{1... | collective-permute-start | bytes 196616 | tf_op jit(solution)/shard_map/ppermute | solution.py:327
  26.4 5.3 %collective-permute-start.16 = (bf16[128,256]{1,0:T(8,128)(2,1)S(1)}, bf16[128,256]{1,0:T(8,128)(2,1)S(1)}, u32[]{:S(2)}, u32[]{:S(2)}) collective-permute-start(bf16[128,256]{1,0:T(8,128)(2,1)S(1)} %get-tuple-element.39.own), channel_id=1, source_target_pairs={{0,9},{1,4},{3,10},{2,7},{5,12},{4,1},{6,15},{7,2},{9,0},{8,13},{1... | collective-permute-start | bytes 196616 | tf_op jit(solution)/shard_map/ppermute | solution.py:327
  27.6 8.0 %collective-permute-start.19 = (f32[128,256]{1,0:T(8,128)S(1)}, f32[128,256]{1,0:T(8,128)S(1)}, u32[]{:S(2)}, u32[]{:S(2)}) collective-permute-start(f32[128,256]{1,0:T(8,128)S(1)} %get-tuple-element.41), channel_id=1, source_target_pairs={{0,1},{1,0},{2,3},{3,2},{4,5},{5,4},{6,7},{7,6},{8,9},{9,8},{10,11... | collective-permute-start | bytes 393224 | tf_op jit(solution)/shard_map/ppermute | solution.py:311
  29.7 3.8 %collective-permute-start.14 = (bf16[128,256]{1,0:T(8,128)(2,1)S(1)}, bf16[128,256]{1,0:T(8,128)(2,1)S(1)}, u32[]{:S(2)}, u32[]{:S(2)}) collective-permute-start(bf16[128,256]{1,0:T(8,128)(2,1)S(1)} %shard_map.116.own), channel_id=1, source_target_pairs={{0,5},{1,2},{3,6},{2,1},{5,0},{4,7},{6,3},{7,4},{9,12},{8,11},{10,... | collective-permute-start | bytes 196616 | tf_op jit(solution)/shard_map/ppermute | solution.py:327
  31.8 3.8 %collective-permute-start.17 = (bf16[128,256]{1,0:T(8,128)(2,1)S(1)}, bf16[128,256]{1,0:T(8,128)(2,1)S(1)}, u32[]{:S(2)}, u32[]{:S(2)}) collective-permute-start(bf16[128,256]{1,0:T(8,128)(2,1)S(1)} %shard_map.118.own), channel_id=1, source_target_pairs={{0,5},{1,2},{3,6},{2,1},{5,0},{4,7},{6,3},{7,4},{9,12},{8,11},{10,... | collective-permute-start | bytes 196616 | tf_op jit(solution)/shard_map/ppermute | solution.py:327
  33.5 2.5 %collective-permute-start.15 = (bf16[128,256]{1,0:T(8,128)(2,1)S(1)}, bf16[128,256]{1,0:T(8,128)(2,1)S(1)}, u32[]{:S(2)}, u32[]{:S(2)}) collective-permute-start(bf16[128,256]{1,0:T(8,128)(2,1)S(1)} %shard_map.117.low), channel_id=1, source_target_pairs={{0,1},{1,0},{2,3},{3,2},{4,5},{5,4},{6,7},{7,6},{8,9},{9,8},{10,11... | collective-permute-start | bytes 196616 | tf_op jit(solution)/shard_map/ppermute | solution.py:311
  35.5 1.3 %collective-permute-start.18 = (bf16[128,256]{1,0:T(8,128)(2,1)S(1)}, bf16[128,256]{1,0:T(8,128)(2,1)S(1)}, u32[]{:S(2)}, u32[]{:S(2)}) collective-permute-start(bf16[128,256]{1,0:T(8,128)(2,1)S(1)} %shard_map.119.high), channel_id=1, source_target_pairs={{0,1},{1,0},{2,3},{3,2},{4,5},{5,4},{6,7},{7,6},{8,9},{9,8},{10,11... | collective-permute-start | bytes 196616 | tf_op jit(solution)/shard_map/ppermute | solution.py:311

commit v13 on v12

--- a/solution.py
+++ b/solution.py
@@ -56,17 +56,57 @@
     return block.astype(jnp.float32)
 
 
-def project(basis_real, basis_imag, amp):
-    return jnp.dot(bf16(amp), basis_real, preferred_element_type=jnp.float32) + jnp.dot(
-        bf16(turned(amp)), basis_imag, preferred_element_type=jnp.float32
-    )
-
-
-def expand(basis_real, basis_imag, field):
+def rows_of(basis, segment, amount):
+    return [basis[part, segment * amount : (segment + 1) * amount, :] for part in range(2)]
+
+
+def project(basis, amp):
+    return jnp.dot(bf16(amp), basis[0], preferred_element_type=jnp.float32) + jnp.dot(
+        bf16(turned(amp)), basis[1], preferred_element_type=jnp.float32
+    )
+
+
+def expand(basis, field):
     contract = (((1,), (1,)), ((), ()))
     return lax.dot_general(
-        turned(field), basis_real, contract, preferred_element_type=jnp.float32
-    ) + lax.dot_general(field, basis_imag, contract, preferred_element_type=jnp.float32)
+        turned(field), basis[0], contract, preferred_element_type=jnp.float32
+    ) + lax.dot_general(field, basis[1], contract, preferred_element_type=jnp.float32)
+
+
+PIECES = 16
+
+
+def split(row):
+    index = lax.broadcasted_iota(jnp.int32, (PIECES, row.shape[1]), 0)
+    block = jnp.zeros(index.shape, jnp.float32)
+    for piece in range(3):
+        rounded = f32(bf16(row))
+        block = jnp.where(index == piece, rounded, block)
+        row = row - rounded
+    return bf16(block)
+
+
+def joined(block):
+    pieces = f32(block)
+    return pieces[0:1] + pieces[1:2] + pieces[2:3]
+
+
+def basis_copies(basis, sem, my, neighbours, sources):
+    axis = ("prj", "tgt")[my]
+    rows = sources[my].shape[2]
+    place = lax.axis_index(axis)
+    copies = []
+    for chip, there in enumerate((place, jnp.bitwise_xor(place, neighbours[my]))):
+        for core in range(2):
+            segment = 2 * chip + core
+            copies.append(
+                pltpu.make_async_copy(
+                    sources[my].at[:, 2 * there + core],
+                    basis.at[:, segment * rows : (segment + 1) * rows],
+                    sem.at[segment],
+                )
+            )
+    return copies
 
 
 def load_kernel(
@@ -78,9 +118,8 @@
     proj_energy_hbm,
     tgt_own_hbm,
     proj_own_hbm,
-    mine,
     sent,
-    small,
+    weight,
     energy,
     amp_ref,
     flat_weight,
@@ -90,22 +129,16 @@
     sems,
 ):
     my = my_kind()
-    places = (lax.axis_index("prj"), lax.axis_index("tgt"))
     sources = (tgt_hbm, proj_hbm)
-
-    def basis_copies(my):
-        return [
-            pltpu.make_async_copy(
-                sources[kind].at[part, pl.ds(2 * place, 2)],
-                basis.at[part, 2 * chip : 2 * chip + 2],
-                sems.at[4 * slot + 2 * chip + part],
-            )
-            for slot, (kind, basis) in enumerate(((1 - my, sent), (my, mine)))
-            for chip, place in enumerate(
-                (places[kind], jnp.bitwise_xor(places[kind], neighbours[kind]))
-            )
-            for part in range(2)
-        ]
+    rows = energy.shape[2]
+
+    def copies_of(kind):
+        last = pltpu.make_async_copy(
+            sources[kind].at[:, 2 * lax.axis_index(("prj", "tgt")[kind]) + 1 - lax.axis_index("rep")],
+            sent.at[:, 4 * rows : 5 * rows],
+            sems.at[4],
+        )
+        return basis_copies(sent, sems, 1 - kind, neighbours, sources) + [last]
 
     pairs = [
         (tgt_own_hbm, tgt_own),
@@ -114,54 +147,71 @@
         (tgt_energy_hbm, flat_energy),
         (proj_energy_hbm, energy.at[1]),
     ]
-    copies = [pltpu.make_async_copy(src, dst, sems.at[8 + k]) for k, (src, dst) in enumerate(pairs)]
+    copies = [pltpu.make_async_copy(src, dst, sems.at[5 + k]) for k, (src, dst) in enumerate(pairs)]
     for copy in copies:
         copy.start()
     for kind in range(2):
 
         @pl.when(my == kind)
         def _():
-            for copy in basis_copies(kind):
+            for copy in copies_of(kind):
                 copy.start()
 
     for copy in copies:
         copy.wait()
     energy[0] = flat_energy[...][None, :]
-    small[0] = flat_weight[...][None, :]
-    small[1, :, : energy.shape[2]] = energy[1 - my]
+    weight[0] = flat_weight[...][None, :]
+    for part in range(2):
+        sent[part, 5 * rows :] = split(weight[0])
     amp_ref[0] = tgt_own[...].T
     amp_ref[1] = proj_own[0].T
-    for copy in basis_copies(0):
+    for copy in copies_of(0):
         copy.wait()
 
 
-def pack_kernel(amp_ref, mine, tgt_other, proj_other, chip_amp, message, send_own):
+def pack_kernel(
+    amp_ref,
+    energy,
+    tgt_other,
+    proj_other,
+    tgt_energy_other,
+    proj_energy_other,
+    chip_amp,
+    energies,
+    message,
+):
     core = lax.axis_index("rep")
     my = my_kind()
+    cols = chip_amp.shape[1]
     other_amp, _ = ordered(my, tgt_other[...].T, proj_other[0].T)
+    other_energy, _ = ordered(my, tgt_energy_other[...][None, :], proj_energy_other[...])
     amps = ordered(core, amp_ref[my], other_amp)
+    rows = ordered(core, energy[my], other_energy)
     for segment in range(2):
         chip_amp[segment] = amps[segment]
-        message[segment] = bf16(amps[segment])
-    for part in range(2):
-        send_own[part] = mine[part, 1 - core]
-
-
-def small_kernel(small, far_small, energy, weights, energies):
-    rows = energy.shape[2]
-    core = lax.axis_index("rep")
-    weights[0], weights[1] = ordered(core, small[0], far_small[0])
-    energies[0], energies[1] = ordered(core, energy[my_kind()], far_small[1, :, :rows])
-
-
-def side_kernel(gate_levels, flags_hbm, counts_hbm, chip_amp, gate, flags, counts, sems):
+        energies[segment] = rows[segment]
+        message[segment, :cols] = bf16(amps[segment])
+        message[segment, cols:] = split(rows[segment])
+
+
+def side_kernel(
+    gate_levels, neighbours, flags_hbm, counts_hbm, tgt_hbm, proj_hbm, chip_amp, mine, gate, flags, counts, sems
+):
     my = my_kind()
     tgt_index = lax.axis_index("tgt")
     prj_index = lax.axis_index("prj")
+    sources = (tgt_hbm, proj_hbm)
     pairs = [(flags_hbm, flags), (counts_hbm, counts)]
-    copies = [pltpu.make_async_copy(src, dst, sems.at[k]) for k, (src, dst) in enumerate(pairs)]
+    copies = [pltpu.make_async_copy(src, dst, sems.at[4 + k]) for k, (src, dst) in enumerate(pairs)]
     for copy in copies:
         copy.start()
+    for kind in range(2):
+
+        @pl.when(my == kind)
+        def _():
+            for copy in basis_copies(mine, sems, kind, neighbours, sources):
+                copy.start()
+
     for copy in copies:
         copy.wait()
     tiles = 2
@@ -178,23 +228,32 @@
                 gate[level, half, :, tile * width : (tile + 1) * width] = jnp.full(
                     (1, width), here, jnp.float32
                 )
-
-
-def chip_kernel(mine, theirs, chip_amp, own_far, part_ref):
+    for copy in basis_copies(mine, sems, 0, neighbours, sources):
+        copy.wait()
+
+
+def chip_kernel(mine, theirs, chip_amp, weight, part_ref, weights):
+    rows = chip_amp.shape[2]
+
     def body(core):
         for half, basis in enumerate((mine, theirs) if core == 0 else (theirs, mine)):
             part_ref[half] = sum(
-                project(basis[0, segment], basis[1, segment], chip_amp[segment]) for segment in range(2)
+                project(rows_of(basis, segment, rows), chip_amp[segment]) for segment in range(2)
             )
+        weights[core] = weight[0]
+        weights[1 - core] = joined(theirs[0, 5 * rows :, :])
 
     by_core(body)
 
 
-def first_kernel(mine, theirs, gate, weights, part_ref, message, neighbour_energies, *outs):
+def first_kernel(mine, theirs, gate, weights, part_ref, message, *outs):
+    rows = message.shape[2]
+    cols = part_ref.shape[1]
+
     def body(core):
         for half, basis in enumerate((mine, theirs) if core == 0 else (theirs, mine)):
             total = part_ref[half] + sum(
-                project(basis[0, 2 + segment], basis[1, 2 + segment], f32(message[segment]))
+                project(rows_of(basis, 2 + segment, rows), f32(message[segment, :cols]))
                 for segment in range(2)
             )
             outs[half][...] = bf16(gate[0, half] * (weights[half] * total))
@@ -208,9 +267,9 @@
 
 def low_kernel(mine, theirs, low, change_ref):
     def body(core):
-        basis = (mine, theirs)[core]
         for segment in range(4):
-            change_ref[segment] = expand(basis[0, segment], basis[1, segment], low[...])
+            basis = rows_of((mine, theirs)[core], segment, change_ref.shape[2])
+            change_ref[segment] = expand(basis, low[...])
 
     by_core(body)
 
@@ -225,12 +284,13 @@
     chip_amp,
     energies,
     message,
-    neighbour_energies,
     low_ref,
     high_ref,
     half_ref,
     send_ref,
 ):
+    _, cols, rows = chip_amp.shape
+
     def body(core):
         bases = (mine, theirs) if core == 0 else (theirs, mine)
         halves = []
@@ -238,26 +298,27 @@
             if segment < 2:
                 amp, energy = chip_amp[segment], energies[segment]
             else:
-                amp, energy = f32(message[segment - 2]), neighbour_energies[segment - 2]
-            change = change_ref[segment] + expand(bases[1][0, segment], bases[1][1, segment], high[...])
+                amp, energy = f32(message[segment - 2, :cols]), joined(message[segment - 2, cols:])
+            change = change_ref[segment] + expand(rows_of(bases[1], segment, rows), high[...])
             halves.append(amp + half_step * (energy * turned(amp) + change))
         half_ref[...] = halves[core]
         send_ref[...] = halves[1 - core]
         for half, out_ref in enumerate((low_ref, high_ref)):
             total = sum(
-                project(bases[half][0, segment], bases[half][1, segment], halves[segment])
-                for segment in range(4)
+                project(rows_of(bases[half], segment, rows), halves[segment]) for segment in range(4)
             )
             out_ref[...] = bf16(gate[0, half] * (weights[half] * total))
 
     by_core(body)
 
 
-def other_last_kernel(sent, own_far, low, high, energy, amp_ref, half_ref, new_ref):
+def other_last_kernel(sent, theirs, low, high, energy, amp_ref, half_ref, new_ref):
+    rows = amp_ref.shape[2]
+
     def body(core):
         near, far = (low, high) if core == 0 else (high, low)
         kind = 1 - my_kind()
-        change = expand(sent[0, core], sent[1, core], near[...]) + expand(own_far[0], own_far[1], far[...])
+        change = expand(rows_of(sent, core, rows), near[...]) + expand(rows_of(theirs, 4, rows), far[...])
         rate = energy[kind] * turned(half_ref[...]) + change
         new_ref[...] = (amp_ref[kind] + time_step * rate).T
 
@@ -265,11 +326,13 @@
 
 
 def last_kernel(mine, theirs, low, high, energy, amp_ref, half_ref, other_new, new_tgt, new_proj):
+    rows = amp_ref.shape[2]
+
     def body(core):
         near, far = (low, high) if core == 0 else (high, low)
         my = my_kind()
-        change = expand(mine[0, core], mine[1, core], near[...]) + expand(
-            theirs[0, core], theirs[1, core], far[...]
+        change = expand(rows_of(mine, core, rows), near[...]) + expand(
+            rows_of(theirs, core, rows), far[...]
         )
         rate = energy[my] * turned(half_ref[...]) + change
         my_new = (amp_ref[my] + time_step * rate).T
@@ -327,7 +390,6 @@
         return lax.ppermute(block, DEVICES, pairs)
 
     in_vmem = pltpu.VMEM
-    basis = in_vmem((2, 4, rows, points), jnp.bfloat16)
     sums = in_vmem((two_cols, points), jnp.bfloat16)
     segment = in_vmem((two_cols, rows), jnp.float32)
 
@@ -346,14 +408,13 @@
     def in_hbm(*blocks):
         return [pltpu.with_memory_space_constraint(block, pltpu.HBM) for block in blocks]
 
-    tgt_other, proj_other = other_core(tgt_amp), other_core(proj_amp)
-    bases = (tgt_basis.reshape(2, -1, rows, points), proj_basis)
-    mine, sent, small, energy, amp = call(
+    others = swapped([tgt_amp, proj_amp, tgt_energy, proj_energy])
+    bases = in_hbm(tgt_basis.reshape(2, -1, rows, points), proj_basis)
+    sent, weight, energy, amp = call(
         functools.partial(load_kernel, neighbours),
         [
-            basis,
-            basis,
-            in_vmem((2, 1, points), jnp.float32),
+            in_vmem((2, 5 * rows + PIECES, points), jnp.bfloat16),
+            in_vmem((1, 1, points), jnp.float32),
             in_vmem((2, 1, rows), jnp.float32),
             in_vmem((2, two_cols, rows), jnp.float32),
         ],
@@ -363,52 +424,49 @@
             pltpu.VMEM((rows,), jnp.float32),
             pltpu.VMEM(tgt_amp.shape, jnp.float32),
             pltpu.VMEM(proj_amp.shape, jnp.float32),
-            pltpu.SemaphoreType.DMA((13,)),
+            pltpu.SemaphoreType.DMA((10,)),
         ],
         pl.CostEstimate(
             flops=2 * 4 * rows * two_cols * points, bytes_accessed=4 * 1024 * 1024, transcendentals=0
         ),
-    )(*in_hbm(quad_weight, *bases, tgt_energy, proj_energy, tgt_amp, proj_amp))
-    chip_amp, message, send_own = run(
+    )(*in_hbm(quad_weight), *bases, *in_hbm(tgt_energy, proj_energy, tgt_amp, proj_amp))
+    chip_amp, energies, message = run(
         pack_kernel,
         [
             in_vmem((2, two_cols, rows), jnp.float32),
-            in_vmem((2, two_cols, rows), jnp.bfloat16),
-            in_vmem((2, rows, points), jnp.bfloat16),
+            in_vmem((2, 1, rows), jnp.float32),
+            in_vmem((2, two_cols + PIECES, rows), jnp.bfloat16),
         ],
         amp,
-        mine,
-        tgt_other,
-        proj_other,
-    )
-    sent, small, send_own, message = lax.optimization_barrier((sent, small, send_own, message))
-    theirs, far_small, own_far = swapped([sent, small, send_own])
+        energy,
+        *others,
+    )
+    sent, message = lax.optimization_barrier((sent, message))
+    theirs = other_core(sent)
     message = exchanged(0, message)
-    weights, energies = run(
-        small_kernel,
-        [in_vmem((2, 1, points), jnp.float32), in_vmem((2, 1, rows), jnp.float32)],
-        small,
-        far_small,
-        energy,
-    )
-    neighbour_energies = exchanged(0, energies)
     flags, counts = pair_flags.T, tile_counts.T
-    (gate,) = call(
-        functools.partial(side_kernel, gate_levels),
-        [in_vmem((n_steps, 2, 1, points), jnp.float32)],
-        [HBM, HBM, VMEM],
+    mine, gate = call(
+        functools.partial(side_kernel, gate_levels, neighbours),
+        [
+            in_vmem((2, 4 * rows, points), jnp.bfloat16),
+            in_vmem((n_steps, 2, 1, points), jnp.float32),
+        ],
+        [HBM] * 4 + [VMEM],
         [
             pltpu.SMEM(flags.shape, jnp.int32),
             pltpu.SMEM(counts.shape, jnp.int32),
-            pltpu.SemaphoreType.DMA((2,)),
+            pltpu.SemaphoreType.DMA((6,)),
         ],
-    )(*in_hbm(flags, counts), chip_amp)
-    (part,) = run(
-        chip_kernel, [in_vmem((2, two_cols, points), jnp.float32)], mine, theirs, chip_amp, own_far
-    )
-    halves = run(
-        first_kernel, [sums] * 2, mine, theirs, gate, weights, part, message, neighbour_energies
-    )
+    )(*in_hbm(flags, counts), *bases, chip_amp)
+    part, weights = run(
+        chip_kernel,
+        [in_vmem((2, two_cols, points), jnp.float32), in_vmem((2, 1, points), jnp.float32)],
+        mine,
+        theirs,
+        chip_amp,
+        weight,
+    )
+    halves = run(first_kernel, [sums] * 2, mine, theirs, gate, weights, part, message)
     fields = summed(*halves)
     low, high = swapped(fields)
     (change,) = run(low_kernel, [in_vmem((4, two_cols, rows), jnp.float32)], mine, theirs, low)
@@ -424,7 +482,6 @@
         chip_amp,
         energies,
         message,
-        neighbour_energies,
     )
     other_half = other_core(half_send)
     fields = summed(*halves)
@@ -432,7 +489,7 @@
         other_last_kernel,
         [in_vmem((rows, two_cols), jnp.float32)],
         sent,
-        own_far,
+        theirs,
         *fields,
         energy,
         amp,

time: 38.1 us -> 37.7 us (0.990)
  starting transfers between devices: 18.6 us -> 18.2 us
    ppermute x10, waiting for transfers between devices: 2.3 us -> 1.49 us  [other_core(): return lax.ppermute(block, 'rep', [(0, 1), (1, 0)])]
    ppermute x10, starting transfers between devices: 3.51 us -> 2.83 us  [other_core(): return lax.ppermute(block, 'rep', [(0, 1), (1, 0)])]
    ppermute x10 -> x9, waiting for transfers between devices: 9.94 us -> 10.6 us  [exchanged(): return lax.ppermute(block, DEVICES, pairs)]
    ppermute x10 -> x9, starting transfers between devices: 15.1 us -> 15.4 us  [exchanged(): return lax.ppermute(block, DEVICES, pairs)]
    pallas_call x16 -> x15, Pallas kernels: 3.78 us -> 3.74 us  [run(): return call(kernel, out_shape, [VMEM] * len(blocks))(*blocks)]
  transfers between devices with their start and end apart: 20 -> 19, of which waited for: 12 -> 10; matrix products, arithmetic and copies ran while one was open for 0% -> 0% of each run, Pallas kernels for 10% -> 11%
where the time goes in v13:
time: 37.7 us; the launch traced here: 37.6 us
  starting transfers between devices  18.2 us (48%)
  waiting for transfers between devices  12.1 us (32%)
  Pallas kernels  6.51 us (17%)
  between operations  0.8 us (2%)
    ppermute x9, starting transfers between devices, exchanged(): return lax.ppermute(block, DEVICES, pairs)  15.4 us
    ppermute x9, waiting for transfers between devices, exchanged(): return lax.ppermute(block, DEVICES, pairs)  10.6 us
    pallas_call x15, Pallas kernels, run(): return call(kernel, out_shape, [VMEM] * len(blocks))(*blocks)  3.74 us
    ppermute x10, starting transfers between devices, other_core(): return lax.ppermute(block, 'rep', [(0, 1), (1, 0)])  2.83 us
    pallas_call x1, Pallas kernels, shards(): call(functools.partial(load_kernel, neighbours), [in_vmem((2, 5 * rows +...  1.53 us
    ppermute x10, waiting for transfers between devices, other_core(): return lax.ppermute(block, 'rep', [(0, 1), (1, 0)])  1.49 us
    pallas_call x1, Pallas kernels, shards(): call(functools.partial(side_kernel, gate_levels, neighbours), [in_vmem((2...  1.24 us
  transfers between devices with their start and end apart: 19, of which 10 were waited for; matrix products, arithmetic and copies ran while one was open for 0% of the time, Pallas kernels for 11%

profile of v13, /device:TPU:0, one launch (start us, length us, event | category | flops | bytes accessed | tf_op | source)
XLA Modules:
  0.0 37.6 jit_solution(2392624555455206998)
XLA Ops:
  0.6 0.5 %collective-permute-start = (f32[256,128]{1,0:T(8,128)}, f32[256,128]{1,0:T(8,128)S(1)}, u32[]{:S(2)}, u32[]{:S(2)}) collective-permute-start(f32[256,128]{1,0:T(8,128)} %tgt_own_hbm.1), channel_id=1, source_target_pairs={{0,1},{1,0},{2,3},{3,2},{4,5},{5,4},{6,7},{7,6},{8,9},{9,8},{10,11... | collective-permute-start | bytes 393224 | tf_op jit(solution)/shard_map/ppermute | solution.py:374
  1.7 1.5 %shard_map.104 = (bf16[2,1296,256]{2,1,0:T(8,128)(2,1)S(1)}, f32[1,1,256]{2,1,0:T(1,128)S(1)}, f32[2,1,256]{2,1,0:T(1,128)S(1)}, f32[2,128,256]{2,1,0:T(8,128)S(1)}) custom-call(f32[256]{0:T(256)} %weight_hbm.1, bf16[2,4,256,256]{3,2,1,0:T(8,128)(2,1)} %bitcast.3, bf16[2,8,256,256]{3,2,1,0:T(8,128)(2,1)} %proj_hbm.3, f32[256]{0:T(256)} %tgt_energy_hbm.1, ...), custom_call_target="tpu_custom_call" | custom-call | flops 67108864 | bytes 4194304 | tf_op jit(solution)/shard_map/pallas_call | solution.py:413
  3.5 0.5 %collective-permute-start.4 = (bf16[2,1296,256]{2,1,0:T(8,128)(2,1)S(1)}, bf16[2,1296,256]{2,1,0:T(8,128)(2,1)S(1)}, u32[]{:S(2)}, u32[]{:S(2)}) collective-permute-start(bf16[2,1296,256]{2,1,0:T(8,128)(2,1)S(1)} %get-tuple-element.27.sent), channel_id=1, source_target_pairs={{0,1},{1,0},{2,3},{3,2},{4,5},{5,4},{6,7},{7,6},{8,9},{9,8},{10,11... | collective-permute-start | bytes 3981320 | tf_op jit(solution)/shard_map/ppermute | solution.py:374
  4.0 2.6 %collective-permute-start.5 = (bf16[2,144,256]{2,1,0:T(8,128)(2,1)S(1)}, bf16[2,144,256]{2,1,0:T(8,128)(2,1)S(1)}, u32[]{:S(2)}, u32[]{:S(2)}) collective-permute-start(bf16[2,144,256]{2,1,0:T(8,128)(2,1)S(1)} %get-tuple-element.32), channel_id=1, source_target_pairs={{0,3},{1,8},{3,0},{2,11},{5,6},{4,13},{6,5},{7,14},{9,10},{8,1},{1... | collective-permute-start | bytes 442376 | tf_op jit(solution)/shard_map/ppermute | solution.py:390
  6.6 1.2 %shard_map.106 = (bf16[2,1024,256]{2,1,0:T(8,128)(2,1)S(1)}, f32[3,2,1,256]{3,2,1,0:T(1,128)S(1)}) custom-call(s32[2,4]{1,0:T(2,128)} %bitcast.5, s32[2,4]{1,0:T(2,128)} %bitcast.6, bf16[2,4,256,256]{3,2,1,0:T(8,128)(2,1)} %bitcast.4, bf16[2,8,256,256]{3,2,1,0:T(8,128)(2,1)} %proj_hbm.3, f32[2,128,256]{2,1,0:T(8,128)S(1)} %get-tuple-element.23.chip_amp), custom_call_target="tpu_custom_call" | custom-call | tf_op jit(solution)/shard_map/pallas_call | solution.py:448
  8.1 1.2 %collective-permute-done.5.message = bf16[2,144,256]{2,1,0:T(8,128)(2,1)S(1)} collective-permute-done((bf16[2,144,256]{2,1,0:T(8,128)(2,1)S(1)}, bf16[2,144,256]{2,1,0:T(8,128)(2,1)S(1)}, u32[]{:S(2)}, u32[]{:S(2)}) %collective-permute-start.5) | collective-permute-done | bytes 147488 | tf_op jit(solution)/shard_map/ppermute | solution.py:390
  9.7 3.2 %collective-permute-start.6 = (bf16[128,256]{1,0:T(8,128)(2,1)S(1)}, bf16[128,256]{1,0:T(8,128)(2,1)S(1)}, u32[]{:S(2)}, u32[]{:S(2)}) collective-permute-start(bf16[128,256]{1,0:T(8,128)(2,1)S(1)} %get-tuple-element.33.own), channel_id=1, source_target_pairs={{0,9},{1,4},{3,10},{2,7},{5,12},{4,1},{6,15},{7,2},{9,0},{8,13},{1... | collective-permute-start | bytes 196616 | tf_op jit(solution)/shard_map/ppermute | solution.py:390
  13.0 2.4 %collective-permute-done.6.other = bf16[128,256]{1,0:T(8,128)(2,1)S(1)} collective-permute-done((bf16[128,256]{1,0:T(8,128)(2,1)S(1)}, bf16[128,256]{1,0:T(8,128)(2,1)S(1)}, u32[]{:S(2)}, u32[]{:S(2)}) %collective-permute-start.6) | collective-permute-done | bytes 65568 | tf_op jit(solution)/shard_map/ppermute | solution.py:390
  15.4 1.2 %collective-permute-start.7 = (bf16[128,256]{1,0:T(8,128)(2,1)S(1)}, bf16[128,256]{1,0:T(8,128)(2,1)S(1)}, u32[]{:S(2)}, u32[]{:S(2)}) collective-permute-start(bf16[128,256]{1,0:T(8,128)(2,1)S(1)} %shard_map.109.own), channel_id=1, source_target_pairs={{0,5},{1,2},{3,6},{2,1},{5,0},{4,7},{6,3},{7,4},{9,12},{8,11},{10,... | collective-permute-start | bytes 196616 | tf_op jit(solution)/shard_map/ppermute | solution.py:390
  16.6 1.0 %collective-permute-done.9.other = bf16[128,256]{1,0:T(8,128)(2,1)S(1)} collective-permute-done((bf16[128,256]{1,0:T(8,128)(2,1)S(1)}, bf16[128,256]{1,0:T(8,128)(2,1)S(1)}, u32[]{:S(2)}, u32[]{:S(2)}) %collective-permute-start.9) | collective-permute-done | bytes 65568 | tf_op jit(solution)/shard_map/ppermute | solution.py:390
  17.6 1.1 %collective-permute-start.10 = (bf16[128,256]{1,0:T(8,128)(2,1)S(1)}, bf16[128,256]{1,0:T(8,128)(2,1)S(1)}, u32[]{:S(2)}, u32[]{:S(2)}) collective-permute-start(bf16[128,256]{1,0:T(8,128)(2,1)S(1)} %shard_map.112.own), channel_id=1, source_target_pairs={{0,5},{1,2},{3,6},{2,1},{5,0},{4,7},{6,3},{7,4},{9,12},{8,11},{10,... | collective-permute-start | bytes 196616 | tf_op jit(solution)/shard_map/ppermute | solution.py:390
  18.7 0.4 %collective-permute-done.7.other = bf16[128,256]{1,0:T(8,128)(2,1)S(1)} collective-permute-done((bf16[128,256]{1,0:T(8,128)(2,1)S(1)}, bf16[128,256]{1,0:T(8,128)(2,1)S(1)}, u32[]{:S(2)}, u32[]{:S(2)}) %collective-permute-start.7) | collective-permute-done | bytes 65568 | tf_op jit(solution)/shard_map/ppermute | solution.py:390
  19.2 0.9 %collective-permute-start.8 = (bf16[128,256]{1,0:T(8,128)(2,1)S(1)}, bf16[128,256]{1,0:T(8,128)(2,1)S(1)}, u32[]{:S(2)}, u32[]{:S(2)}) collective-permute-start(bf16[128,256]{1,0:T(8,128)(2,1)S(1)} %shard_map.110), channel_id=1, source_target_pairs={{0,1},{1,0},{2,3},{3,2},{4,5},{5,4},{6,7},{7,6},{8,9},{9,8},{10,11... | collective-permute-start | bytes 196616 | tf_op jit(solution)/shard_map/ppermute | solution.py:374
  20.1 1.3 %collective-permute-done.10.other = bf16[128,256]{1,0:T(8,128)(2,1)S(1)} collective-permute-done((bf16[128,256]{1,0:T(8,128)(2,1)S(1)}, bf16[128,256]{1,0:T(8,128)(2,1)S(1)}, u32[]{:S(2)}, u32[]{:S(2)}) %collective-permute-start.10) | collective-permute-done | bytes 65568 | tf_op jit(solution)/shard_map/ppermute | solution.py:390
  21.6 0.5 %shard_map.111.change_ref = f32[4,128,256]{2,1,0:T(8,128)S(1)} custom-call(bf16[2,1024,256]{2,1,0:T(8,128)(2,1)S(1)} %get-tuple-element.24.mine, bf16[2,1296,256]{2,1,0:T(8,128)(2,1)S(1)} %collective-permute-done.4.theirs, bf16[128,256]{1,0:T(8,128)(2,1)S(1)} %collective-permute-done.8.low), custom_call_target="tpu_custom_call" | custom-call | tf_op jit(solution)/shard_map/pallas_call | solution.py:371
  22.1 0.7 %collective-permute-done.11.high = bf16[128,256]{1,0:T(8,128)(2,1)S(1)} collective-permute-done((bf16[128,256]{1,0:T(8,128)(2,1)S(1)}, bf16[128,256]{1,0:T(8,128)(2,1)S(1)}, u32[]{:S(2)}, u32[]{:S(2)}) %collective-permute-start.11) | collective-permute-done | bytes 65568 | tf_op jit(solution)/shard_map/ppermute | solution.py:374
  22.7 0.8 %shard_map.114 = (bf16[128,256]{1,0:T(8,128)(2,1)S(1)}, bf16[128,256]{1,0:T(8,128)(2,1)S(1)}, f32[128,256]{1,0:T(8,128)S(1)}, f32[128,256]{1,0:T(8,128)S(1)}) custom-call(bf16[2,1024,256]{2,1,0:T(8,128)(2,1)S(1)} %get-tuple-element.24.mine, bf16[2,1296,256]{2,1,0:T(8,128)(2,1)S(1)} %collective-permute-done.4.theirs, ...), custom_call_target="tpu_custom_call" | custom-call | tf_op jit(solution)/shard_map/pallas_call | solution.py:371
  23.6 2.6 %collective-permute-start.12 = (bf16[128,256]{1,0:T(8,128)(2,1)S(1)}, bf16[128,256]{1,0:T(8,128)(2,1)S(1)}, u32[]{:S(2)}, u32[]{:S(2)}) collective-permute-start(bf16[128,256]{1,0:T(8,128)(2,1)S(1)} %get-tuple-element.36.own), channel_id=1, source_target_pairs={{0,9},{1,4},{3,10},{2,7},{5,12},{4,1},{6,15},{7,2},{9,0},{8,13},{1... | collective-permute-start | bytes 196616 | tf_op jit(solution)/shard_map/ppermute | solution.py:390
  26.3 2.0 %collective-permute-done.12.other = bf16[128,256]{1,0:T(8,128)(2,1)S(1)} collective-permute-done((bf16[128,256]{1,0:T(8,128)(2,1)S(1)}, bf16[128,256]{1,0:T(8,128)(2,1)S(1)}, u32[]{:S(2)}, u32[]{:S(2)}) %collective-permute-start.12) | collective-permute-done | bytes 65568 | tf_op jit(solution)/shard_map/ppermute | solution.py:390
  28.4 2.6 %collective-permute-start.13 = (bf16[128,256]{1,0:T(8,128)(2,1)S(1)}, bf16[128,256]{1,0:T(8,128)(2,1)S(1)}, u32[]{:S(2)}, u32[]{:S(2)}) collective-permute-start(bf16[128,256]{1,0:T(8,128)(2,1)S(1)} %shard_map.115.own), channel_id=1, source_target_pairs={{0,5},{1,2},{3,6},{2,1},{5,0},{4,7},{6,3},{7,4},{9,12},{8,11},{10,... | collective-permute-start | bytes 196616 | tf_op jit(solution)/shard_map/ppermute | solution.py:390
  31.3 1.9 %collective-permute-start.16 = (bf16[128,256]{1,0:T(8,128)(2,1)S(1)}, bf16[128,256]{1,0:T(8,128)(2,1)S(1)}, u32[]{:S(2)}, u32[]{:S(2)}) collective-permute-start(bf16[128,256]{1,0:T(8,128)(2,1)S(1)} %shard_map.117.own), channel_id=1, source_target_pairs={{0,5},{1,2},{3,6},{2,1},{5,0},{4,7},{6,3},{7,4},{9,12},{8,11},{10,... | collective-permute-start | bytes 196616 | tf_op jit(solution)/shard_map/ppermute | solution.py:390
  33.3 1.8 %collective-permute-done.16.other = bf16[128,256]{1,0:T(8,128)(2,1)S(1)} collective-permute-done((bf16[128,256]{1,0:T(8,128)(2,1)S(1)}, bf16[128,256]{1,0:T(8,128)(2,1)S(1)}, u32[]{:S(2)}, u32[]{:S(2)}) %collective-permute-start.16) | collective-permute-done | bytes 65568 | tf_op jit(solution)/shard_map/ppermute | solution.py:390
  35.7 0.8 %collective-permute-done.17.high = bf16[128,256]{1,0:T(8,128)(2,1)S(1)} collective-permute-done((bf16[128,256]{1,0:T(8,128)(2,1)S(1)}, bf16[128,256]{1,0:T(8,128)(2,1)S(1)}, u32[]{:S(2)}, u32[]{:S(2)}) %collective-permute-start.17) | collective-permute-done | bytes 65568 | tf_op jit(solution)/shard_map/ppermute | solution.py:374
  36.5 1.1 %shard_map.120 = (f32[256,128]{1,0:T(8,128)}, f32[1,256,128]{2,1,0:T(8,128)}) custom-call(bf16[2,1024,256]{2,1,0:T(8,128)(2,1)S(1)} %get-tuple-element.24.mine, bf16[2,1296,256]{2,1,0:T(8,128)(2,1)S(1)} %collective-permute-done.4.theirs, bf16[128,256]{1,0:T(8,128)(2,1)S(1)} %collective-permute-done.14.low, ...), custom_call_target="tpu_custom_call" | custom-call | tf_op jit(solution)/shard_map/pallas_call | solution.py:371
  (31 shorter events, 2.8 us)
Async XLA Ops:
  0.6 2.7 %collective-permute-start = (f32[256,128]{1,0:T(8,128)}, f32[256,128]{1,0:T(8,128)S(1)}, u32[]{:S(2)}, u32[]{:S(2)}) collective-permute-start(f32[256,128]{1,0:T(8,128)} %tgt_own_hbm.1), channel_id=1, source_target_pairs={{0,1},{1,0},{2,3},{3,2},{4,5},{5,4},{6,7},{7,6},{8,9},{9,8},{10,11... | collective-permute-start | bytes 393224 | tf_op jit(solution)/shard_map/ppermute | solution.py:374
  1.1 2.2 %collective-permute-start.1 = (f32[1,256,128]{2,1,0:T(8,128)}, f32[1,256,128]{2,1,0:T(8,128)S(1)}, u32[]{:S(2)}, u32[]{:S(2)}) collective-permute-start(f32[1,256,128]{2,1,0:T(8,128)} %proj_own_hbm.1), channel_id=1, source_target_pairs={{0,1},{1,0},{2,3},{3,2},{4,5},{5,4},{6,7},{7,6},{8,9},{9,8},{10,11... | collective-permute-start | bytes 393224 | tf_op jit(solution)/shard_map/ppermute | solution.py:374
  1.2 2.1 %collective-permute-start.2 = (f32[256]{0:T(256)}, f32[256]{0:T(256)S(1)}, u32[]{:S(2)}, u32[]{:S(2)}) collective-permute-start(f32[256]{0:T(256)} %tgt_energy_hbm.1), channel_id=1, source_target_pairs={{0,1},{1,0},{2,3},{3,2},{4,5},{5,4},{6,7},{7,6},{8,9},{9,8},{10,11... | collective-permute-start | bytes 3080 | tf_op jit(solution)/shard_map/ppermute | solution.py:374
  1.7 1.6 %collective-permute-start.3 = (f32[1,256]{1,0:T(1,128)}, f32[1,256]{1,0:T(1,128)S(1)}, u32[]{:S(2)}, u32[]{:S(2)}) collective-permute-start(f32[1,256]{1,0:T(1,128)} %proj_energy_hbm.1), channel_id=1, source_target_pairs={{0,1},{1,0},{2,3},{3,2},{4,5},{5,4},{6,7},{7,6},{8,9},{9,8},{10,11... | collective-permute-start | bytes 3080 | tf_op jit(solution)/shard_map/ppermute | solution.py:374
  3.5 4.3 %collective-permute-start.4 = (bf16[2,1296,256]{2,1,0:T(8,128)(2,1)S(1)}, bf16[2,1296,256]{2,1,0:T(8,128)(2,1)S(1)}, u32[]{:S(2)}, u32[]{:S(2)}) collective-permute-start(bf16[2,1296,256]{2,1,0:T(8,128)(2,1)S(1)} %get-tuple-element.27.sent), channel_id=1, source_target_pairs={{0,1},{1,0},{2,3},{3,2},{4,5},{5,4},{6,7},{7,6},{8,9},{9,8},{10,11... | collective-permute-start | bytes 3981320 | tf_op jit(solution)/shard_map/ppermute | solution.py:374
  4.0 5.4 %collective-permute-start.5 = (bf16[2,144,256]{2,1,0:T(8,128)(2,1)S(1)}, bf16[2,144,256]{2,1,0:T(8,128)(2,1)S(1)}, u32[]{:S(2)}, u32[]{:S(2)}) collective-permute-start(bf16[2,144,256]{2,1,0:T(8,128)(2,1)S(1)} %get-tuple-element.32), channel_id=1, source_target_pairs={{0,3},{1,8},{3,0},{2,11},{5,6},{4,13},{6,5},{7,14},{9,10},{8,1},{1... | collective-permute-start | bytes 442376 | tf_op jit(solution)/shard_map/ppermute | solution.py:390
  9.7 5.7 %collective-permute-start.6 = (bf16[128,256]{1,0:T(8,128)(2,1)S(1)}, bf16[128,256]{1,0:T(8,128)(2,1)S(1)}, u32[]{:S(2)}, u32[]{:S(2)}) collective-permute-start(bf16[128,256]{1,0:T(8,128)(2,1)S(1)} %get-tuple-element.33.own), channel_id=1, source_target_pairs={{0,9},{1,4},{3,10},{2,7},{5,12},{4,1},{6,15},{7,2},{9,0},{8,13},{1... | collective-permute-start | bytes 196616 | tf_op jit(solution)/shard_map/ppermute | solution.py:390
  12.9 4.7 %collective-permute-start.9 = (bf16[128,256]{1,0:T(8,128)(2,1)S(1)}, bf16[128,256]{1,0:T(8,128)(2,1)S(1)}, u32[]{:S(2)}, u32[]{:S(2)}) collective-permute-start(bf16[128,256]{1,0:T(8,128)(2,1)S(1)} %get-tuple-element.34.own), channel_id=1, source_target_pairs={{0,9},{1,4},{3,10},{2,7},{5,12},{4,1},{6,15},{7,2},{9,0},{8,13},{1... | collective-permute-start | bytes 196616 | tf_op jit(solution)/shard_map/ppermute | solution.py:390
  15.4 3.8 %collective-permute-start.7 = (bf16[128,256]{1,0:T(8,128)(2,1)S(1)}, bf16[128,256]{1,0:T(8,128)(2,1)S(1)}, u32[]{:S(2)}, u32[]{:S(2)}) collective-permute-start(bf16[128,256]{1,0:T(8,128)(2,1)S(1)} %shard_map.109.own), channel_id=1, source_target_pairs={{0,5},{1,2},{3,6},{2,1},{5,0},{4,7},{6,3},{7,4},{9,12},{8,11},{10,... | collective-permute-start | bytes 196616 | tf_op jit(solution)/shard_map/ppermute | solution.py:390
  17.6 3.8 %collective-permute-start.10 = (bf16[128,256]{1,0:T(8,128)(2,1)S(1)}, bf16[128,256]{1,0:T(8,128)(2,1)S(1)}, u32[]{:S(2)}, u32[]{:S(2)}) collective-permute-start(bf16[128,256]{1,0:T(8,128)(2,1)S(1)} %shard_map.112.own), channel_id=1, source_target_pairs={{0,5},{1,2},{3,6},{2,1},{5,0},{4,7},{6,3},{7,4},{9,12},{8,11},{10,... | collective-permute-start | bytes 196616 | tf_op jit(solution)/shard_map/ppermute | solution.py:390
  19.2 2.4 %collective-permute-start.8 = (bf16[128,256]{1,0:T(8,128)(2,1)S(1)}, bf16[128,256]{1,0:T(8,128)(2,1)S(1)}, u32[]{:S(2)}, u32[]{:S(2)}) collective-permute-start(bf16[128,256]{1,0:T(8,128)(2,1)S(1)} %shard_map.110), channel_id=1, source_target_pairs={{0,1},{1,0},{2,3},{3,2},{4,5},{5,4},{6,7},{7,6},{8,9},{9,8},{10,11... | collective-permute-start | bytes 196616 | tf_op jit(solution)/shard_map/ppermute | solution.py:374
  21.4 1.3 %collective-permute-start.11 = (bf16[128,256]{1,0:T(8,128)(2,1)S(1)}, bf16[128,256]{1,0:T(8,128)(2,1)S(1)}, u32[]{:S(2)}, u32[]{:S(2)}) collective-permute-start(bf16[128,256]{1,0:T(8,128)(2,1)S(1)} %shard_map.113), channel_id=1, source_target_pairs={{0,1},{1,0},{2,3},{3,2},{4,5},{5,4},{6,7},{7,6},{8,9},{9,8},{10,11... | collective-permute-start | bytes 196616 | tf_op jit(solution)/shard_map/ppermute | solution.py:374
  23.6 4.8 %collective-permute-start.12 = (bf16[128,256]{1,0:T(8,128)(2,1)S(1)}, bf16[128,256]{1,0:T(8,128)(2,1)S(1)}, u32[]{:S(2)}, u32[]{:S(2)}) collective-permute-start(bf16[128,256]{1,0:T(8,128)(2,1)S(1)} %get-tuple-element.36.own), channel_id=1, source_target_pairs={{0,9},{1,4},{3,10},{2,7},{5,12},{4,1},{6,15},{7,2},{9,0},{8,13},{1... | collective-permute-start | bytes 196616 | tf_op jit(solution)/shard_map/ppermute | solution.py:390
  26.2 5.1 %collective-permute-start.15 = (bf16[128,256]{1,0:T(8,128)(2,1)S(1)}, bf16[128,256]{1,0:T(8,128)(2,1)S(1)}, u32[]{:S(2)}, u32[]{:S(2)}) collective-permute-start(bf16[128,256]{1,0:T(8,128)(2,1)S(1)} %get-tuple-element.37.own), channel_id=1, source_target_pairs={{0,9},{1,4},{3,10},{2,7},{5,12},{4,1},{6,15},{7,2},{9,0},{8,13},{1... | collective-permute-start | bytes 196616 | tf_op jit(solution)/shard_map/ppermute | solution.py:390
  26.3 9.0 %collective-permute-start.18 = (f32[128,256]{1,0:T(8,128)S(1)}, f32[128,256]{1,0:T(8,128)S(1)}, u32[]{:S(2)}, u32[]{:S(2)}) collective-permute-start(f32[128,256]{1,0:T(8,128)S(1)} %get-tuple-element.39), channel_id=1, source_target_pairs={{0,1},{1,0},{2,3},{3,2},{4,5},{5,4},{6,7},{7,6},{8,9},{9,8},{10,11... | collective-permute-start | bytes 393224 | tf_op jit(solution)/shard_map/ppermute | solution.py:374
  28.4 4.8 %collective-permute-start.13 = (bf16[128,256]{1,0:T(8,128)(2,1)S(1)}, bf16[128,256]{1,0:T(8,128)(2,1)S(1)}, u32[]{:S(2)}, u32[]{:S(2)}) collective-permute-start(bf16[128,256]{1,0:T(8,128)(2,1)S(1)} %shard_map.115.own), channel_id=1, source_target_pairs={{0,5},{1,2},{3,6},{2,1},{5,0},{4,7},{6,3},{7,4},{9,12},{8,11},{10,... | collective-permute-start | bytes 196616 | tf_op jit(solution)/shard_map/ppermute | solution.py:390
  31.3 3.8 %collective-permute-start.16 = (bf16[128,256]{1,0:T(8,128)(2,1)S(1)}, bf16[128,256]{1,0:T(8,128)(2,1)S(1)}, u32[]{:S(2)}, u32[]{:S(2)}) collective-permute-start(bf16[128,256]{1,0:T(8,128)(2,1)S(1)} %shard_map.117.own), channel_id=1, source_target_pairs={{0,5},{1,2},{3,6},{2,1},{5,0},{4,7},{6,3},{7,4},{9,12},{8,11},{10,... | collective-permute-start | bytes 196616 | tf_op jit(solution)/shard_map/ppermute | solution.py:390
  33.2 2.4 %collective-permute-start.14 = (bf16[128,256]{1,0:T(8,128)(2,1)S(1)}, bf16[128,256]{1,0:T(8,128)(2,1)S(1)}, u32[]{:S(2)}, u32[]{:S(2)}) collective-permute-start(bf16[128,256]{1,0:T(8,128)(2,1)S(1)} %shard_map.116.low), channel_id=1, source_target_pairs={{0,1},{1,0},{2,3},{3,2},{4,5},{5,4},{6,7},{7,6},{8,9},{9,8},{10,11... | collective-permute-start | bytes 196616 | tf_op jit(solution)/shard_map/ppermute | solution.py:374
  35.2 1.3 %collective-permute-start.17 = (bf16[128,256]{1,0:T(8,128)(2,1)S(1)}, bf16[128,256]{1,0:T(8,128)(2,1)S(1)}, u32[]{:S(2)}, u32[]{:S(2)}) collective-permute-start(bf16[128,256]{1,0:T(8,128)(2,1)S(1)} %shard_map.118.high), channel_id=1, source_target_pairs={{0,1},{1,0},{2,3},{3,2},{4,5},{5,4},{6,7},{7,6},{8,9},{9,8},{10,11... | collective-permute-start | bytes 196616 | tf_op jit(solution)/shard_map/ppermute | solution.py:374

commit v14 on v13

--- a/solution.py
+++ b/solution.py
@@ -246,7 +246,7 @@
     by_core(body)
 
 
-def first_kernel(mine, theirs, gate, weights, part_ref, message, *outs):
+def first_kernel(mine, theirs, gate, weights, part_ref, message, out_ref):
     rows = message.shape[2]
     cols = part_ref.shape[1]
 
@@ -256,38 +256,18 @@
                 project(rows_of(basis, 2 + segment, rows), f32(message[segment, :cols]))
                 for segment in range(2)
             )
-            outs[half][...] = bf16(gate[0, half] * (weights[half] * total))
+            out_ref[half] = bf16(gate[0, half] * (weights[half] * total))
 
     by_core(body)
 
 
-def add_kernel(level, half, gate, own, other, out_ref):
-    out_ref[...] = bf16(gate[level, half] * (f32(own[...]) + f32(other[...])))
-
-
-def low_kernel(mine, theirs, low, change_ref):
-    def body(core):
-        for segment in range(4):
-            basis = rows_of((mine, theirs)[core], segment, change_ref.shape[2])
-            change_ref[segment] = expand(basis, low[...])
-
-    by_core(body)
+def add_kernel(level, gate, own, other, out_ref):
+    for half in range(2):
+        out_ref[half] = bf16(gate[level, half] * (f32(own[half]) + f32(other[half])))
 
 
 def second_kernel(
-    mine,
-    theirs,
-    change_ref,
-    high,
-    gate,
-    weights,
-    chip_amp,
-    energies,
-    message,
-    low_ref,
-    high_ref,
-    half_ref,
-    send_ref,
+    mine, theirs, field, gate, weights, chip_amp, energies, message, z_ref, half_ref, send_ref
 ):
     _, cols, rows = chip_amp.shape
 
@@ -299,44 +279,45 @@
                 amp, energy = chip_amp[segment], energies[segment]
             else:
                 amp, energy = f32(message[segment - 2, :cols]), joined(message[segment - 2, cols:])
-            change = change_ref[segment] + expand(rows_of(bases[1], segment, rows), high[...])
+            change = sum(
+                expand(rows_of(bases[half], segment, rows), field[half]) for half in range(2)
+            )
             halves.append(amp + half_step * (energy * turned(amp) + change))
         half_ref[...] = halves[core]
         send_ref[...] = halves[1 - core]
-        for half, out_ref in enumerate((low_ref, high_ref)):
+        for half in range(2):
             total = sum(
                 project(rows_of(bases[half], segment, rows), halves[segment]) for segment in range(4)
             )
-            out_ref[...] = bf16(gate[0, half] * (weights[half] * total))
+            z_ref[half] = bf16(gate[0, half] * (weights[half] * total))
 
     by_core(body)
 
 
-def other_last_kernel(sent, theirs, low, high, energy, amp_ref, half_ref, new_ref):
+def late_kernel(theirs, sent, field, energy, amp_ref, my_half, other_half, my_part, other_new):
     rows = amp_ref.shape[2]
 
     def body(core):
-        near, far = (low, high) if core == 0 else (high, low)
-        kind = 1 - my_kind()
-        change = expand(rows_of(sent, core, rows), near[...]) + expand(rows_of(theirs, 4, rows), far[...])
-        rate = energy[kind] * turned(half_ref[...]) + change
-        new_ref[...] = (amp_ref[kind] + time_step * rate).T
+        my = my_kind()
+        change = expand(rows_of(sent, core, rows), field[core]) + expand(
+            rows_of(theirs, 4, rows), field[1 - core]
+        )
+        rate = energy[1 - my] * turned(other_half[...]) + change
+        other_new[...] = (amp_ref[1 - my] + time_step * rate).T
+        my_part[...] = amp_ref[my] + time_step * (energy[my] * turned(my_half[...]))
 
     by_core(body)
 
 
-def last_kernel(mine, theirs, low, high, energy, amp_ref, half_ref, other_new, new_tgt, new_proj):
-    rows = amp_ref.shape[2]
+def last_kernel(mine, theirs, field, my_part, other_new, new_tgt, new_proj):
+    rows = my_part.shape[1]
 
     def body(core):
-        near, far = (low, high) if core == 0 else (high, low)
-        my = my_kind()
-        change = expand(rows_of(mine, core, rows), near[...]) + expand(
-            rows_of(theirs, core, rows), far[...]
+        change = expand(rows_of(mine, core, rows), field[core]) + expand(
+            rows_of(theirs, core, rows), field[1 - core]
         )
-        rate = energy[my] * turned(half_ref[...]) + change
-        my_new = (amp_ref[my] + time_step * rate).T
-        new_tgt[...], new_proj[0] = ordered(my, my_new, other_new[...])
+        my_new = (my_part[...] + time_step * change).T
+        new_tgt[...], new_proj[0] = ordered(my_kind(), my_new, other_new[...])
 
     by_core(body)
 
@@ -390,17 +371,14 @@
         return lax.ppermute(block, DEVICES, pairs)
 
     in_vmem = pltpu.VMEM
-    sums = in_vmem((two_cols, points), jnp.bfloat16)
+    sums = in_vmem((2, two_cols, points), jnp.bfloat16)
     segment = in_vmem((two_cols, rows), jnp.float32)
 
-    def summed(*halves):
-        totals = []
-        for half, block in enumerate(halves):
-            for step in range(1, n_steps):
-                other = exchanged(step, block)
-                (block,) = run(functools.partial(add_kernel, step, half), [sums], gate, block, other)
-            totals.append(block)
-        return totals
+    def summed(block):
+        for step in range(1, n_steps):
+            other = exchanged(step, block)
+            (block,) = run(functools.partial(add_kernel, step), [sums], gate, block, other)
+        return block
 
     def swapped(fields):
         return [other_core(block) for block in fields]
@@ -466,17 +444,14 @@
         chip_amp,
         weight,
     )
-    halves = run(first_kernel, [sums] * 2, mine, theirs, gate, weights, part, message)
-    fields = summed(*halves)
-    low, high = swapped(fields)
-    (change,) = run(low_kernel, [in_vmem((4, two_cols, rows), jnp.float32)], mine, theirs, low)
-    *halves, my_half, half_send = run(
+    (z,) = run(first_kernel, [sums], mine, theirs, gate, weights, part, message)
+    field = summed(z)
+    z, my_half, half_send = run(
         second_kernel,
-        [sums, sums, segment, segment],
+        [sums, segment, segment],
         mine,
         theirs,
-        change,
-        high,
+        other_core(field),
         gate,
         weights,
         chip_amp,
@@ -484,15 +459,16 @@
         message,
     )
     other_half = other_core(half_send)
-    fields = summed(*halves)
-    (other_new,) = run(
-        other_last_kernel,
-        [in_vmem((rows, two_cols), jnp.float32)],
+    field = summed(z)
+    my_part, other_new = run(
+        late_kernel,
+        [segment, in_vmem((rows, two_cols), jnp.float32)],
+        theirs,
         sent,
-        theirs,
-        *fields,
+        field,
         energy,
         amp,
+        my_half,
         other_half,
     )
     return run(
@@ -503,10 +479,8 @@
         ],
         mine,
         theirs,
-        *swapped(fields),
-        energy,
-        amp,
-        my_half,
+        other_core(field),
+        my_part,
         other_new,
     )
 

time: 37.7 us -> 37.7 us (level)
  waiting for transfers between devices: 12.1 us -> 15.2 us
  starting transfers between devices: 18.2 us -> 15.2 us
    ppermute x9 -> x5, waiting for transfers between devices: 10.6 us -> 13.3 us  [exchanged(): return lax.ppermute(block, DEVICES, pairs)]
    ppermute x9 -> x5, starting transfers between devices: 15.4 us -> 13 us  [exchanged(): return lax.ppermute(block, DEVICES, pairs)]
    ppermute x10 -> x8, starting transfers between devices: 2.83 us -> 2.21 us  [other_core(): return lax.ppermute(block, 'rep', [(0, 1), (1, 0)])]
    ppermute x10 -> x8, waiting for transfers between devices: 1.49 us -> 1.93 us  [other_core(): return lax.ppermute(block, 'rep', [(0, 1), (1, 0)])]
    pallas_call x15 -> x10, Pallas kernels: 3.74 us -> 3.57 us  [run(): return call(kernel, out_shape, [VMEM] * len(blocks))(*blocks)]
  transfers between devices with their start and end apart: 19 -> 13, of which waited for: 10 -> 7; matrix products, arithmetic and copies ran while one was open for 0% -> 0% of each run, Pallas kernels for 11% -> 9%
where the time goes in v14:
time: 37.7 us; the launch traced here: 37.5 us
  starting transfers between devices  15.2 us (40%)
  waiting for transfers between devices  15.2 us (40%)
  Pallas kernels  6.35 us (17%)
  between operations  0.76 us (2%)
    ppermute x5, waiting for transfers between devices, exchanged(): return lax.ppermute(block, DEVICES, pairs)  13.3 us
    ppermute x5, starting transfers between devices, exchanged(): return lax.ppermute(block, DEVICES, pairs)  13 us
    pallas_call x10, Pallas kernels, run(): return call(kernel, out_shape, [VMEM] * len(blocks))(*blocks)  3.57 us
    ppermute x8, starting transfers between devices, other_core(): return lax.ppermute(block, 'rep', [(0, 1), (1, 0)])  2.21 us
    ppermute x8, waiting for transfers between devices, other_core(): return lax.ppermute(block, 'rep', [(0, 1), (1, 0)])  1.93 us
    pallas_call x1, Pallas kernels, shards(): call(functools.partial(load_kernel, neighbours), [in_vmem((2, 5 * rows +...  1.53 us
    pallas_call x1, Pallas kernels, shards(): call(functools.partial(side_kernel, gate_levels, neighbours), [in_vmem((2...  1.24 us
  transfers between devices with their start and end apart: 13, of which 7 were waited for; matrix products, arithmetic and copies ran while one was open for 0% of the time, Pallas kernels for 9%

profile of v14, /device:TPU:0, one launch (start us, length us, event | category | flops | bytes accessed | tf_op | source)
XLA Modules:
  0.0 37.5 jit_solution(9510862912203519883)
XLA Ops:
  0.6 0.5 %collective-permute-start = (f32[256,128]{1,0:T(8,128)}, f32[256,128]{1,0:T(8,128)S(1)}, u32[]{:S(2)}, u32[]{:S(2)}) collective-permute-start(f32[256,128]{1,0:T(8,128)} %tgt_own_hbm.1), channel_id=1, source_target_pairs={{0,1},{1,0},{2,3},{3,2},{4,5},{5,4},{6,7},{7,6},{8,9},{9,8},{10,11... | collective-permute-start | bytes 393224 | tf_op jit(solution)/shard_map/ppermute | solution.py:355
  1.2 0.4 %collective-permute-start.2 = (f32[256]{0:T(256)}, f32[256]{0:T(256)S(1)}, u32[]{:S(2)}, u32[]{:S(2)}) collective-permute-start(f32[256]{0:T(256)} %tgt_energy_hbm.1), channel_id=1, source_target_pairs={{0,1},{1,0},{2,3},{3,2},{4,5},{5,4},{6,7},{7,6},{8,9},{9,8},{10,11... | collective-permute-start | bytes 3080 | tf_op jit(solution)/shard_map/ppermute | solution.py:355
  1.7 1.5 %shard_map.104 = (bf16[2,1296,256]{2,1,0:T(8,128)(2,1)S(1)}, f32[1,1,256]{2,1,0:T(1,128)S(1)}, f32[2,1,256]{2,1,0:T(1,128)S(1)}, f32[2,128,256]{2,1,0:T(8,128)S(1)}) custom-call(f32[256]{0:T(256)} %weight_hbm.1, bf16[2,4,256,256]{3,2,1,0:T(8,128)(2,1)} %bitcast.3, bf16[2,8,256,256]{3,2,1,0:T(8,128)(2,1)} %proj_hbm.3, f32[256]{0:T(256)} %tgt_energy_hbm.1, ...), custom_call_target="tpu_custom_call" | custom-call | flops 67108864 | bytes 4194304 | tf_op jit(solution)/shard_map/pallas_call | solution.py:391
  3.3 0.1 shard_map.105
  3.5 0.5 %collective-permute-start.4 = (bf16[2,1296,256]{2,1,0:T(8,128)(2,1)S(1)}, bf16[2,1296,256]{2,1,0:T(8,128)(2,1)S(1)}, u32[]{:S(2)}, u32[]{:S(2)}) collective-permute-start(bf16[2,1296,256]{2,1,0:T(8,128)(2,1)S(1)} %get-tuple-element.26.sent), channel_id=1, source_target_pairs={{0,1},{1,0},{2,3},{3,2},{4,5},{5,4},{6,7},{7,6},{8,9},{9,8},{10,11... | collective-permute-start | bytes 3981320 | tf_op jit(solution)/shard_map/ppermute | solution.py:355
  4.0 2.6 %collective-permute-start.5 = (bf16[2,144,256]{2,1,0:T(8,128)(2,1)S(1)}, bf16[2,144,256]{2,1,0:T(8,128)(2,1)S(1)}, u32[]{:S(2)}, u32[]{:S(2)}) collective-permute-start(bf16[2,144,256]{2,1,0:T(8,128)(2,1)S(1)} %get-tuple-element.31), channel_id=1, source_target_pairs={{0,3},{1,8},{3,0},{2,11},{5,6},{4,13},{6,5},{7,14},{9,10},{8,1},{1... | collective-permute-start | bytes 442376 | tf_op jit(solution)/shard_map/ppermute | solution.py:371
  6.6 1.2 %shard_map.106 = (bf16[2,1024,256]{2,1,0:T(8,128)(2,1)S(1)}, f32[3,2,1,256]{3,2,1,0:T(1,128)S(1)}) custom-call(s32[2,4]{1,0:T(2,128)} %bitcast.5, s32[2,4]{1,0:T(2,128)} %bitcast.6, bf16[2,4,256,256]{3,2,1,0:T(8,128)(2,1)} %bitcast.4, bf16[2,8,256,256]{3,2,1,0:T(8,128)(2,1)} %proj_hbm.3, f32[2,128,256]{2,1,0:T(8,128)S(1)} %get-tuple-element.22.chip_amp), custom_call_target="tpu_custom_call" | custom-call | tf_op jit(solution)/shard_map/pallas_call | solution.py:426
  7.8 0.3 shard_map.107
  8.2 1.2 %collective-permute-done.5.message = bf16[2,144,256]{2,1,0:T(8,128)(2,1)S(1)} collective-permute-done((bf16[2,144,256]{2,1,0:T(8,128)(2,1)S(1)}, bf16[2,144,256]{2,1,0:T(8,128)(2,1)S(1)}, u32[]{:S(2)}, u32[]{:S(2)}) %collective-permute-start.5) | collective-permute-done | bytes 147488 | tf_op jit(solution)/shard_map/ppermute | solution.py:371
  9.4 0.3 shard_map.108.own
  9.7 3.2 %collective-permute-start.6 = (bf16[2,128,256]{2,1,0:T(8,128)(2,1)S(1)}, bf16[2,128,256]{2,1,0:T(8,128)(2,1)S(1)}, u32[]{:S(2)}, u32[]{:S(2)}) collective-permute-start(bf16[2,128,256]{2,1,0:T(8,128)(2,1)S(1)} %shard_map.108.own), channel_id=1, source_target_pairs={{0,9},{1,4},{3,10},{2,7},{5,12},{4,1},{6,15},{7,2},{9,0},{8,13},{1... | collective-permute-start | bytes 393224 | tf_op jit(solution)/shard_map/ppermute | solution.py:371
  12.9 3.5 %collective-permute-done.6.other = bf16[2,128,256]{2,1,0:T(8,128)(2,1)S(1)} collective-permute-done((bf16[2,128,256]{2,1,0:T(8,128)(2,1)S(1)}, bf16[2,128,256]{2,1,0:T(8,128)(2,1)S(1)}, u32[]{:S(2)}, u32[]{:S(2)}) %collective-permute-start.6) | collective-permute-done | bytes 131104 | tf_op jit(solution)/shard_map/ppermute | solution.py:371
  16.5 1.4 %collective-permute-start.7 = (bf16[2,128,256]{2,1,0:T(8,128)(2,1)S(1)}, bf16[2,128,256]{2,1,0:T(8,128)(2,1)S(1)}, u32[]{:S(2)}, u32[]{:S(2)}) collective-permute-start(bf16[2,128,256]{2,1,0:T(8,128)(2,1)S(1)} %shard_map.109.own), channel_id=1, source_target_pairs={{0,5},{1,2},{3,6},{2,1},{5,0},{4,7},{6,3},{7,4},{9,12},{8,11},{10,... | collective-permute-start | bytes 393224 | tf_op jit(solution)/shard_map/ppermute | solution.py:371
  17.9 3.1 %collective-permute-done.7.other = bf16[2,128,256]{2,1,0:T(8,128)(2,1)S(1)} collective-permute-done((bf16[2,128,256]{2,1,0:T(8,128)(2,1)S(1)}, bf16[2,128,256]{2,1,0:T(8,128)(2,1)S(1)}, u32[]{:S(2)}, u32[]{:S(2)}) %collective-permute-start.7) | collective-permute-done | bytes 131104 | tf_op jit(solution)/shard_map/ppermute | solution.py:371
  21.0 0.5 %collective-permute-start.8 = (bf16[2,128,256]{2,1,0:T(8,128)(2,1)S(1)}, bf16[2,128,256]{2,1,0:T(8,128)(2,1)S(1)}, u32[]{:S(2)}, u32[]{:S(2)}) collective-permute-start(bf16[2,128,256]{2,1,0:T(8,128)(2,1)S(1)} %shard_map.110), channel_id=1, source_target_pairs={{0,1},{1,0},{2,3},{3,2},{4,5},{5,4},{6,7},{7,6},{8,9},{9,8},{10,11... | collective-permute-start | bytes 393224 | tf_op jit(solution)/shard_map/ppermute | solution.py:355
  21.6 1.0 %collective-permute-done.8.field = bf16[2,128,256]{2,1,0:T(8,128)(2,1)S(1)} collective-permute-done((bf16[2,128,256]{2,1,0:T(8,128)(2,1)S(1)}, bf16[2,128,256]{2,1,0:T(8,128)(2,1)S(1)}, u32[]{:S(2)}, u32[]{:S(2)}) %collective-permute-start.8) | collective-permute-done | bytes 131104 | tf_op jit(solution)/shard_map/ppermute | solution.py:355
  22.5 1.1 %shard_map.111 = (bf16[2,128,256]{2,1,0:T(8,128)(2,1)S(1)}, f32[128,256]{1,0:T(8,128)S(1)}, f32[128,256]{1,0:T(8,128)S(1)}) custom-call(bf16[2,1024,256]{2,1,0:T(8,128)(2,1)S(1)} %get-tuple-element.23.mine, bf16[2,1296,256]{2,1,0:T(8,128)(2,1)S(1)} %collective-permute-done.4.theirs, bf16[2,128,256]{2,1,0:T(8,128)(2,1)S(1)} %collective-permute-done.8.field, ...), custom_call_target="tpu_custom_call" | custom-call | tf_op jit(solution)/shard_map/pallas_call | solution.py:352
  23.7 2.8 %collective-permute-start.9 = (bf16[2,128,256]{2,1,0:T(8,128)(2,1)S(1)}, bf16[2,128,256]{2,1,0:T(8,128)(2,1)S(1)}, u32[]{:S(2)}, u32[]{:S(2)}) collective-permute-start(bf16[2,128,256]{2,1,0:T(8,128)(2,1)S(1)} %get-tuple-element.33.own), channel_id=1, source_target_pairs={{0,9},{1,4},{3,10},{2,7},{5,12},{4,1},{6,15},{7,2},{9,0},{8,13},{1... | collective-permute-start | bytes 393224 | tf_op jit(solution)/shard_map/ppermute | solution.py:371
  26.4 2.8 %collective-permute-done.9.other = bf16[2,128,256]{2,1,0:T(8,128)(2,1)S(1)} collective-permute-done((bf16[2,128,256]{2,1,0:T(8,128)(2,1)S(1)}, bf16[2,128,256]{2,1,0:T(8,128)(2,1)S(1)}, u32[]{:S(2)}, u32[]{:S(2)}) %collective-permute-start.9) | collective-permute-done | bytes 131104 | tf_op jit(solution)/shard_map/ppermute | solution.py:371
  29.3 3.1 %collective-permute-start.10 = (bf16[2,128,256]{2,1,0:T(8,128)(2,1)S(1)}, bf16[2,128,256]{2,1,0:T(8,128)(2,1)S(1)}, u32[]{:S(2)}, u32[]{:S(2)}) collective-permute-start(bf16[2,128,256]{2,1,0:T(8,128)(2,1)S(1)} %shard_map.112.own), channel_id=1, source_target_pairs={{0,5},{1,2},{3,6},{2,1},{5,0},{4,7},{6,3},{7,4},{9,12},{8,11},{10,... | collective-permute-start | bytes 393224 | tf_op jit(solution)/shard_map/ppermute | solution.py:371
  32.4 2.6 %collective-permute-done.10.other = bf16[2,128,256]{2,1,0:T(8,128)(2,1)S(1)} collective-permute-done((bf16[2,128,256]{2,1,0:T(8,128)(2,1)S(1)}, bf16[2,128,256]{2,1,0:T(8,128)(2,1)S(1)}, u32[]{:S(2)}, u32[]{:S(2)}) %collective-permute-start.10) | collective-permute-done | bytes 131104 | tf_op jit(solution)/shard_map/ppermute | solution.py:371
  35.1 0.4 %shard_map.114 = (f32[128,256]{1,0:T(8,128)S(1)}, f32[256,128]{1,0:T(8,128)S(1)}) custom-call(bf16[2,1296,256]{2,1,0:T(8,128)(2,1)S(1)} %collective-permute-done.4.theirs, bf16[2,1296,256]{2,1,0:T(8,128)(2,1)S(1)} %get-tuple-element.26.sent, bf16[2,128,256]{2,1,0:T(8,128)(2,1)S(1)} %shard_map.113.field, f32[2,1,256]{2,1,0:T(1,128)S(1)} %get-tuple-element.21.energy, ...), custom_call_target="tpu_custom_call" | custom-call | tf_op jit(solution)/shard_map/pallas_call | solution.py:352
  35.5 0.9 %collective-permute-done.11.field = bf16[2,128,256]{2,1,0:T(8,128)(2,1)S(1)} collective-permute-done((bf16[2,128,256]{2,1,0:T(8,128)(2,1)S(1)}, bf16[2,128,256]{2,1,0:T(8,128)(2,1)S(1)}, u32[]{:S(2)}, u32[]{:S(2)}) %collective-permute-start.11) | collective-permute-done | bytes 131104 | tf_op jit(solution)/shard_map/ppermute | solution.py:355
  36.5 1.1 %shard_map.115 = (f32[256,128]{1,0:T(8,128)}, f32[1,256,128]{2,1,0:T(8,128)}) custom-call(bf16[2,1024,256]{2,1,0:T(8,128)(2,1)S(1)} %get-tuple-element.23.mine, bf16[2,1296,256]{2,1,0:T(8,128)(2,1)S(1)} %collective-permute-done.4.theirs, bf16[2,128,256]{2,1,0:T(8,128)(2,1)S(1)} %collective-permute-done.11.field, f32[128,256]{1,0:T(8,128)S(1)} %get-tuple-element.36.my_part, ...), custom_call_target="tpu_custom_call" | custom-call | tf_op jit(solution)/shard_map/pallas_call | solution.py:352
  (14 shorter events, 0.4 us)
Async XLA Ops:
  0.6 2.7 %collective-permute-start = (f32[256,128]{1,0:T(8,128)}, f32[256,128]{1,0:T(8,128)S(1)}, u32[]{:S(2)}, u32[]{:S(2)}) collective-permute-start(f32[256,128]{1,0:T(8,128)} %tgt_own_hbm.1), channel_id=1, source_target_pairs={{0,1},{1,0},{2,3},{3,2},{4,5},{5,4},{6,7},{7,6},{8,9},{9,8},{10,11... | collective-permute-start | bytes 393224 | tf_op jit(solution)/shard_map/ppermute | solution.py:355
  1.1 2.2 %collective-permute-start.1 = (f32[1,256,128]{2,1,0:T(8,128)}, f32[1,256,128]{2,1,0:T(8,128)S(1)}, u32[]{:S(2)}, u32[]{:S(2)}) collective-permute-start(f32[1,256,128]{2,1,0:T(8,128)} %proj_own_hbm.1), channel_id=1, source_target_pairs={{0,1},{1,0},{2,3},{3,2},{4,5},{5,4},{6,7},{7,6},{8,9},{9,8},{10,11... | collective-permute-start | bytes 393224 | tf_op jit(solution)/shard_map/ppermute | solution.py:355
  1.2 2.1 %collective-permute-start.2 = (f32[256]{0:T(256)}, f32[256]{0:T(256)S(1)}, u32[]{:S(2)}, u32[]{:S(2)}) collective-permute-start(f32[256]{0:T(256)} %tgt_energy_hbm.1), channel_id=1, source_target_pairs={{0,1},{1,0},{2,3},{3,2},{4,5},{5,4},{6,7},{7,6},{8,9},{9,8},{10,11... | collective-permute-start | bytes 3080 | tf_op jit(solution)/shard_map/ppermute | solution.py:355
  1.7 1.6 %collective-permute-start.3 = (f32[1,256]{1,0:T(1,128)}, f32[1,256]{1,0:T(1,128)S(1)}, u32[]{:S(2)}, u32[]{:S(2)}) collective-permute-start(f32[1,256]{1,0:T(1,128)} %proj_energy_hbm.1), channel_id=1, source_target_pairs={{0,1},{1,0},{2,3},{3,2},{4,5},{5,4},{6,7},{7,6},{8,9},{9,8},{10,11... | collective-permute-start | bytes 3080 | tf_op jit(solution)/shard_map/ppermute | solution.py:355
  3.5 4.3 %collective-permute-start.4 = (bf16[2,1296,256]{2,1,0:T(8,128)(2,1)S(1)}, bf16[2,1296,256]{2,1,0:T(8,128)(2,1)S(1)}, u32[]{:S(2)}, u32[]{:S(2)}) collective-permute-start(bf16[2,1296,256]{2,1,0:T(8,128)(2,1)S(1)} %get-tuple-element.26.sent), channel_id=1, source_target_pairs={{0,1},{1,0},{2,3},{3,2},{4,5},{5,4},{6,7},{7,6},{8,9},{9,8},{10,11... | collective-permute-start | bytes 3981320 | tf_op jit(solution)/shard_map/ppermute | solution.py:355
  4.0 5.4 %collective-permute-start.5 = (bf16[2,144,256]{2,1,0:T(8,128)(2,1)S(1)}, bf16[2,144,256]{2,1,0:T(8,128)(2,1)S(1)}, u32[]{:S(2)}, u32[]{:S(2)}) collective-permute-start(bf16[2,144,256]{2,1,0:T(8,128)(2,1)S(1)} %get-tuple-element.31), channel_id=1, source_target_pairs={{0,3},{1,8},{3,0},{2,11},{5,6},{4,13},{6,5},{7,14},{9,10},{8,1},{1... | collective-permute-start | bytes 442376 | tf_op jit(solution)/shard_map/ppermute | solution.py:371
  9.7 6.7 %collective-permute-start.6 = (bf16[2,128,256]{2,1,0:T(8,128)(2,1)S(1)}, bf16[2,128,256]{2,1,0:T(8,128)(2,1)S(1)}, u32[]{:S(2)}, u32[]{:S(2)}) collective-permute-start(bf16[2,128,256]{2,1,0:T(8,128)(2,1)S(1)} %shard_map.108.own), channel_id=1, source_target_pairs={{0,9},{1,4},{3,10},{2,7},{5,12},{4,1},{6,15},{7,2},{9,0},{8,13},{1... | collective-permute-start | bytes 393224 | tf_op jit(solution)/shard_map/ppermute | solution.py:371
  16.5 4.5 %collective-permute-start.7 = (bf16[2,128,256]{2,1,0:T(8,128)(2,1)S(1)}, bf16[2,128,256]{2,1,0:T(8,128)(2,1)S(1)}, u32[]{:S(2)}, u32[]{:S(2)}) collective-permute-start(bf16[2,128,256]{2,1,0:T(8,128)(2,1)S(1)} %shard_map.109.own), channel_id=1, source_target_pairs={{0,5},{1,2},{3,6},{2,1},{5,0},{4,7},{6,3},{7,4},{9,12},{8,11},{10,... | collective-permute-start | bytes 393224 | tf_op jit(solution)/shard_map/ppermute | solution.py:371
  21.0 1.5 %collective-permute-start.8 = (bf16[2,128,256]{2,1,0:T(8,128)(2,1)S(1)}, bf16[2,128,256]{2,1,0:T(8,128)(2,1)S(1)}, u32[]{:S(2)}, u32[]{:S(2)}) collective-permute-start(bf16[2,128,256]{2,1,0:T(8,128)(2,1)S(1)} %shard_map.110), channel_id=1, source_target_pairs={{0,1},{1,0},{2,3},{3,2},{4,5},{5,4},{6,7},{7,6},{8,9},{9,8},{10,11... | collective-permute-start | bytes 393224 | tf_op jit(solution)/shard_map/ppermute | solution.py:355
  23.7 5.5 %collective-permute-start.9 = (bf16[2,128,256]{2,1,0:T(8,128)(2,1)S(1)}, bf16[2,128,256]{2,1,0:T(8,128)(2,1)S(1)}, u32[]{:S(2)}, u32[]{:S(2)}) collective-permute-start(bf16[2,128,256]{2,1,0:T(8,128)(2,1)S(1)} %get-tuple-element.33.own), channel_id=1, source_target_pairs={{0,9},{1,4},{3,10},{2,7},{5,12},{4,1},{6,15},{7,2},{9,0},{8,13},{1... | collective-permute-start | bytes 393224 | tf_op jit(solution)/shard_map/ppermute | solution.py:371
  29.3 5.7 %collective-permute-start.10 = (bf16[2,128,256]{2,1,0:T(8,128)(2,1)S(1)}, bf16[2,128,256]{2,1,0:T(8,128)(2,1)S(1)}, u32[]{:S(2)}, u32[]{:S(2)}) collective-permute-start(bf16[2,128,256]{2,1,0:T(8,128)(2,1)S(1)} %shard_map.112.own), channel_id=1, source_target_pairs={{0,5},{1,2},{3,6},{2,1},{5,0},{4,7},{6,3},{7,4},{9,12},{8,11},{10,... | collective-permute-start | bytes 393224 | tf_op jit(solution)/shard_map/ppermute | solution.py:371
  32.4 2.8 %collective-permute-start.12 = (f32[128,256]{1,0:T(8,128)S(1)}, f32[128,256]{1,0:T(8,128)S(1)}, u32[]{:S(2)}, u32[]{:S(2)}) collective-permute-start(f32[128,256]{1,0:T(8,128)S(1)} %get-tuple-element.35), channel_id=1, source_target_pairs={{0,1},{1,0},{2,3},{3,2},{4,5},{5,4},{6,7},{7,6},{8,9},{9,8},{10,11... | collective-permute-start | bytes 393224 | tf_op jit(solution)/shard_map/ppermute | solution.py:355
  35.1 1.4 %collective-permute-start.11 = (bf16[2,128,256]{2,1,0:T(8,128)(2,1)S(1)}, bf16[2,128,256]{2,1,0:T(8,128)(2,1)S(1)}, u32[]{:S(2)}, u32[]{:S(2)}) collective-permute-start(bf16[2,128,256]{2,1,0:T(8,128)(2,1)S(1)} %shard_map.113.field), channel_id=1, source_target_pairs={{0,1},{1,0},{2,3},{3,2},{4,5},{5,4},{6,7},{7,6},{8,9},{9,8},{10,11... | collective-permute-start | bytes 393224 | tf_op jit(solution)/shard_map/ppermute | solution.py:355

commit v15 on v13

--- a/solution.py
+++ b/solution.py
@@ -74,6 +74,8 @@
 
 
 PIECES = 16
+
+BEHIND = pl.CostEstimate(flops=1 << 35, bytes_accessed=1 << 16, transcendentals=0)
 
 
 def split(row):
@@ -110,63 +112,31 @@
 
 
 def load_kernel(
-    neighbours,
-    weight_hbm,
-    tgt_hbm,
-    proj_hbm,
     tgt_energy_hbm,
     proj_energy_hbm,
     tgt_own_hbm,
     proj_own_hbm,
-    sent,
-    weight,
     energy,
     amp_ref,
-    flat_weight,
     flat_energy,
     tgt_own,
     proj_own,
     sems,
 ):
-    my = my_kind()
-    sources = (tgt_hbm, proj_hbm)
-    rows = energy.shape[2]
-
-    def copies_of(kind):
-        last = pltpu.make_async_copy(
-            sources[kind].at[:, 2 * lax.axis_index(("prj", "tgt")[kind]) + 1 - lax.axis_index("rep")],
-            sent.at[:, 4 * rows : 5 * rows],
-            sems.at[4],
-        )
-        return basis_copies(sent, sems, 1 - kind, neighbours, sources) + [last]
-
     pairs = [
         (tgt_own_hbm, tgt_own),
         (proj_own_hbm, proj_own),
-        (weight_hbm, flat_weight),
         (tgt_energy_hbm, flat_energy),
         (proj_energy_hbm, energy.at[1]),
     ]
-    copies = [pltpu.make_async_copy(src, dst, sems.at[5 + k]) for k, (src, dst) in enumerate(pairs)]
+    copies = [pltpu.make_async_copy(src, dst, sems.at[k]) for k, (src, dst) in enumerate(pairs)]
     for copy in copies:
         copy.start()
-    for kind in range(2):
-
-        @pl.when(my == kind)
-        def _():
-            for copy in copies_of(kind):
-                copy.start()
-
     for copy in copies:
         copy.wait()
     energy[0] = flat_energy[...][None, :]
-    weight[0] = flat_weight[...][None, :]
-    for part in range(2):
-        sent[part, 5 * rows :] = split(weight[0])
     amp_ref[0] = tgt_own[...].T
     amp_ref[1] = proj_own[0].T
-    for copy in copies_of(0):
-        copy.wait()
 
 
 def pack_kernel(
@@ -194,24 +164,14 @@
         message[segment, cols:] = split(rows[segment])
 
 
-def side_kernel(
-    gate_levels, neighbours, flags_hbm, counts_hbm, tgt_hbm, proj_hbm, chip_amp, mine, gate, flags, counts, sems
-):
+def gate_kernel(gate_levels, flags_hbm, counts_hbm, chip_amp, gate, flags, counts, sems):
     my = my_kind()
     tgt_index = lax.axis_index("tgt")
     prj_index = lax.axis_index("prj")
-    sources = (tgt_hbm, proj_hbm)
     pairs = [(flags_hbm, flags), (counts_hbm, counts)]
-    copies = [pltpu.make_async_copy(src, dst, sems.at[4 + k]) for k, (src, dst) in enumerate(pairs)]
+    copies = [pltpu.make_async_copy(src, dst, sems.at[k]) for k, (src, dst) in enumerate(pairs)]
     for copy in copies:
         copy.start()
-    for kind in range(2):
-
-        @pl.when(my == kind)
-        def _():
-            for copy in basis_copies(mine, sems, kind, neighbours, sources):
-                copy.start()
-
     for copy in copies:
         copy.wait()
     tiles = 2
@@ -228,7 +188,50 @@
                 gate[level, half, :, tile * width : (tile + 1) * width] = jnp.full(
                     (1, width), here, jnp.float32
                 )
-    for copy in basis_copies(mine, sems, 0, neighbours, sources):
+
+
+def basis_kernel(
+    neighbours,
+    weight_hbm,
+    tgt_hbm,
+    proj_hbm,
+    chip_amp,
+    sent,
+    mine,
+    weight,
+    flat_weight,
+    sems,
+):
+    my = my_kind()
+    sources = (tgt_hbm, proj_hbm)
+    rows = chip_amp.shape[2]
+
+    def copies_of(kind):
+        last = pltpu.make_async_copy(
+            sources[kind].at[:, 2 * lax.axis_index(("prj", "tgt")[kind]) + 1 - lax.axis_index("rep")],
+            sent.at[:, 4 * rows : 5 * rows],
+            sems.at[8],
+        )
+        return (
+            basis_copies(sent, sems.at[0:4], 1 - kind, neighbours, sources)
+            + [last]
+            + basis_copies(mine, sems.at[4:8], kind, neighbours, sources)
+        )
+
+    weight_copy = pltpu.make_async_copy(weight_hbm, flat_weight, sems.at[9])
+    weight_copy.start()
+    for kind in range(2):
+
+        @pl.when(my == kind)
+        def _():
+            for copy in copies_of(kind):
+                copy.start()
+
+    weight_copy.wait()
+    weight[0] = flat_weight[...][None, :]
+    for part in range(2):
+        sent[part, 5 * rows :] = split(weight[0])
+    for copy in copies_of(0):
         copy.wait()
 
 
@@ -265,42 +268,30 @@
     out_ref[...] = bf16(gate[level, half] * (f32(own[...]) + f32(other[...])))
 
 
-def low_kernel(mine, theirs, low, change_ref):
+def low_kernel(mine, theirs, low, chip_amp, energies, message, states_ref):
+    _, cols, rows = chip_amp.shape
+
     def body(core):
-        for segment in range(4):
-            basis = rows_of((mine, theirs)[core], segment, change_ref.shape[2])
-            change_ref[segment] = expand(basis, low[...])
-
-    by_core(body)
-
-
-def second_kernel(
-    mine,
-    theirs,
-    change_ref,
-    high,
-    gate,
-    weights,
-    chip_amp,
-    energies,
-    message,
-    low_ref,
-    high_ref,
-    half_ref,
-    send_ref,
-):
-    _, cols, rows = chip_amp.shape
-
-    def body(core):
-        bases = (mine, theirs) if core == 0 else (theirs, mine)
-        halves = []
         for segment in range(4):
             if segment < 2:
                 amp, energy = chip_amp[segment], energies[segment]
             else:
                 amp, energy = f32(message[segment - 2, :cols]), joined(message[segment - 2, cols:])
-            change = change_ref[segment] + expand(rows_of(bases[1], segment, rows), high[...])
-            halves.append(amp + half_step * (energy * turned(amp) + change))
+            change = expand(rows_of((mine, theirs)[core], segment, rows), low[...])
+            states_ref[segment] = amp + half_step * (energy * turned(amp) + change)
+
+    by_core(body)
+
+
+def second_kernel(mine, theirs, states_ref, high, gate, weights, low_ref, high_ref, half_ref, send_ref):
+    rows = states_ref.shape[2]
+
+    def body(core):
+        bases = (mine, theirs) if core == 0 else (theirs, mine)
+        halves = [
+            states_ref[segment] + half_step * expand(rows_of(bases[1], segment, rows), high[...])
+            for segment in range(4)
+        ]
         half_ref[...] = halves[core]
         send_ref[...] = halves[1 - core]
         for half, out_ref in enumerate((low_ref, high_ref)):
@@ -312,31 +303,30 @@
     by_core(body)
 
 
-def other_last_kernel(sent, theirs, low, high, energy, amp_ref, half_ref, new_ref):
+def late_kernel(theirs, sent, low, high, energy, amp_ref, my_half, other_half, my_part, other_new):
     rows = amp_ref.shape[2]
+
+    def body(core):
+        my = my_kind()
+        near, far = (low, high) if core == 0 else (high, low)
+        change = expand(rows_of(sent, core, rows), near[...]) + expand(rows_of(theirs, 4, rows), far[...])
+        rate = energy[1 - my] * turned(other_half[...]) + change
+        other_new[...] = (amp_ref[1 - my] + time_step * rate).T
+        my_part[...] = amp_ref[my] + time_step * (energy[my] * turned(my_half[...]))
+
+    by_core(body)
+
+
+def last_kernel(mine, theirs, low, high, my_part, other_new, new_tgt, new_proj):
+    rows = my_part.shape[1]
 
     def body(core):
         near, far = (low, high) if core == 0 else (high, low)
-        kind = 1 - my_kind()
-        change = expand(rows_of(sent, core, rows), near[...]) + expand(rows_of(theirs, 4, rows), far[...])
-        rate = energy[kind] * turned(half_ref[...]) + change
-        new_ref[...] = (amp_ref[kind] + time_step * rate).T
-
-    by_core(body)
-
-
-def last_kernel(mine, theirs, low, high, energy, amp_ref, half_ref, other_new, new_tgt, new_proj):
-    rows = amp_ref.shape[2]
-
-    def body(core):
-        near, far = (low, high) if core == 0 else (high, low)
-        my = my_kind()
         change = expand(rows_of(mine, core, rows), near[...]) + expand(
             rows_of(theirs, core, rows), far[...]
         )
-        rate = energy[my] * turned(half_ref[...]) + change
-        my_new = (amp_ref[my] + time_step * rate).T
-        new_tgt[...], new_proj[0] = ordered(my, my_new, other_new[...])
+        my_new = (my_part[...] + time_step * change).T
+        new_tgt[...], new_proj[0] = ordered(my_kind(), my_new, other_new[...])
 
     by_core(body)
 
@@ -409,27 +399,20 @@
         return [pltpu.with_memory_space_constraint(block, pltpu.HBM) for block in blocks]
 
     others = swapped([tgt_amp, proj_amp, tgt_energy, proj_energy])
-    bases = in_hbm(tgt_basis.reshape(2, -1, rows, points), proj_basis)
-    sent, weight, energy, amp = call(
-        functools.partial(load_kernel, neighbours),
+    energy, amp = call(
+        load_kernel,
+        [in_vmem((2, 1, rows), jnp.float32), in_vmem((2, two_cols, rows), jnp.float32)],
+        [HBM] * 4,
         [
-            in_vmem((2, 5 * rows + PIECES, points), jnp.bfloat16),
-            in_vmem((1, 1, points), jnp.float32),
-            in_vmem((2, 1, rows), jnp.float32),
-            in_vmem((2, two_cols, rows), jnp.float32),
-        ],
-        [HBM] * 7,
-        [
-            pltpu.VMEM((points,), jnp.float32),
             pltpu.VMEM((rows,), jnp.float32),
             pltpu.VMEM(tgt_amp.shape, jnp.float32),
             pltpu.VMEM(proj_amp.shape, jnp.float32),
-            pltpu.SemaphoreType.DMA((10,)),
+            pltpu.SemaphoreType.DMA((4,)),
         ],
         pl.CostEstimate(
             flops=2 * 4 * rows * two_cols * points, bytes_accessed=4 * 1024 * 1024, transcendentals=0
         ),
-    )(*in_hbm(quad_weight), *bases, *in_hbm(tgt_energy, proj_energy, tgt_amp, proj_amp))
+    )(*in_hbm(tgt_energy, proj_energy, tgt_amp, proj_amp))
     chip_amp, energies, message = run(
         pack_kernel,
         [
@@ -441,23 +424,33 @@
         energy,
         *others,
     )
-    sent, message = lax.optimization_barrier((sent, message))
-    theirs = other_core(sent)
     message = exchanged(0, message)
     flags, counts = pair_flags.T, tile_counts.T
-    mine, gate = call(
-        functools.partial(side_kernel, gate_levels, neighbours),
-        [
-            in_vmem((2, 4 * rows, points), jnp.bfloat16),
-            in_vmem((n_steps, 2, 1, points), jnp.float32),
-        ],
-        [HBM] * 4 + [VMEM],
+    (gate,) = call(
+        functools.partial(gate_kernel, gate_levels),
+        [in_vmem((n_steps, 2, 1, points), jnp.float32)],
+        [HBM, HBM, VMEM],
         [
             pltpu.SMEM(flags.shape, jnp.int32),
             pltpu.SMEM(counts.shape, jnp.int32),
-            pltpu.SemaphoreType.DMA((6,)),
+            pltpu.SemaphoreType.DMA((2,)),
         ],
-    )(*in_hbm(flags, counts), *bases, chip_amp)
+        BEHIND,
+    )(*in_hbm(flags, counts), chip_amp)
+    sent, mine, weight = call(
+        functools.partial(basis_kernel, neighbours),
+        [
+            in_vmem((2, 5 * rows + PIECES, points), jnp.bfloat16),
+            in_vmem((2, 4 * rows, points), jnp.bfloat16),
+            in_vmem((1, 1, points), jnp.float32),
+        ],
+        [HBM] * 3 + [VMEM],
+        [pltpu.VMEM((points,), jnp.float32), pltpu.SemaphoreType.DMA((10,))],
+    )(
+        *in_hbm(quad_weight, tgt_basis.reshape(2, -1, rows, points), proj_basis),
+        chip_amp,
+    )
+    theirs = other_core(sent)
     part, weights = run(
         chip_kernel,
         [in_vmem((2, two_cols, points), jnp.float32), in_vmem((2, 1, points), jnp.float32)],
@@ -469,30 +462,38 @@
     halves = run(first_kernel, [sums] * 2, mine, theirs, gate, weights, part, message)
     fields = summed(*halves)
     low, high = swapped(fields)
-    (change,) = run(low_kernel, [in_vmem((4, two_cols, rows), jnp.float32)], mine, theirs, low)
+    (states,) = run(
+        low_kernel,
+        [in_vmem((4, two_cols, rows), jnp.float32)],
+        mine,
+        theirs,
+        low,
+        chip_amp,
+        energies,
+        message,
+    )
     *halves, my_half, half_send = run(
         second_kernel,
         [sums, sums, segment, segment],
         mine,
         theirs,
-        change,
+        states,
         high,
         gate,
         weights,
-        chip_amp,
-        energies,
-        message,
     )
     other_half = other_core(half_send)
     fields = summed(*halves)
-    (other_new,) = run(
-        other_last_kernel,
-        [in_vmem((rows, two_cols), jnp.float32)],
+    low, high = swapped(fields)
+    my_part, other_new = run(
+        late_kernel,
+        [segment, in_vmem((rows, two_cols), jnp.float32)],
+        theirs,
         sent,
-        theirs,
         *fields,
         energy,
         amp,
+        my_half,
         other_half,
     )
     return run(
@@ -503,10 +504,9 @@
         ],
         mine,
         theirs,
-        *swapped(fields),
-        energy,
-        amp,
-        my_half,
+        low,
+        high,
+        my_part,
         other_new,
     )
 

time: 37.7 us -> 37.6 us (level)
  starting transfers between devices: 18.2 us -> 16 us
  waiting for transfers between devices: 12.1 us -> 13.3 us
  Pallas kernels: 6.51 us -> 7.31 us
    ppermute x9, starting transfers between devices: 15.4 us -> 12.9 us  [exchanged(): return lax.ppermute(block, DEVICES, pairs)]
    ppermute x10, waiting for transfers between devices: 1.49 us -> 3.61 us  [other_core(): return lax.ppermute(block, 'rep', [(0, 1), (1, 0)])]
    ppermute x9, waiting for transfers between devices: 10.6 us -> 9.73 us  [exchanged(): return lax.ppermute(block, DEVICES, pairs)]
    pallas_call x2 -> x3, Pallas kernels: 2.77 us -> 3.56 us  [the longest x1 1.68 us: shards(): call(functools.partial(basis_kernel, neighbours), [in_vmem((2, 5 * rows +...]
  transfers between devices with their start and end apart: 19 -> 19, of which waited for: 10 -> 12; matrix products, arithmetic and copies ran while one was open for 0% -> 0% of each run, Pallas kernels for 11% -> 13%
where the time goes in v15:
time: 37.6 us; the launch traced here: 37.4 us
  starting transfers between devices  16 us (43%)
  waiting for transfers between devices  13.3 us (35%)
  Pallas kernels  7.31 us (19%)
  between operations  0.8 us (2%)
    ppermute x9, starting transfers between devices, exchanged(): return lax.ppermute(block, DEVICES, pairs)  12.9 us
    ppermute x9, waiting for transfers between devices, exchanged(): return lax.ppermute(block, DEVICES, pairs)  9.73 us
    pallas_call x15, Pallas kernels, run(): return call(kernel, out_shape, [VMEM] * len(blocks))(*blocks)  3.76 us
    ppermute x10, waiting for transfers between devices, other_core(): return lax.ppermute(block, 'rep', [(0, 1), (1, 0)])  3.61 us
    ppermute x10, starting transfers between devices, other_core(): return lax.ppermute(block, 'rep', [(0, 1), (1, 0)])  3.12 us
    pallas_call x1, Pallas kernels, shards(): call(functools.partial(basis_kernel, neighbours), [in_vmem((2, 5 * rows +...  1.68 us
    pallas_call x1, Pallas kernels, shards(): call(load_kernel, [in_vmem((2, 1, rows), jnp.float32), in_vmem((2, two_co...  1.14 us
  transfers between devices with their start and end apart: 19, of which 12 were waited for; matrix products, arithmetic and copies ran while one was open for 0% of the time, Pallas kernels for 13%

profile of v15, /device:TPU:0, one launch (start us, length us, event | category | flops | bytes accessed | tf_op | source)
XLA Modules:
  0.0 37.4 jit_solution(18209506620392206068)
XLA Ops:
  1.7 1.1 %shard_map.104 = (f32[2,1,256]{2,1,0:T(1,128)S(1)}, f32[2,128,256]{2,1,0:T(8,128)S(1)}) custom-call(f32[256]{0:T(256)} %tgt_energy_hbm.1, f32[1,256]{1,0:T(1,128)} %proj_energy_hbm.1, f32[256,128]{1,0:T(8,128)} %tgt_own_hbm.1, f32[1,256,128]{2,1,0:T(8,128)} %proj_own_hbm.1), custom_call_target="tpu_custom_call" | custom-call | flops 67108864 | bytes 4194304 | tf_op jit(solution)/shard_map/pallas_call | solution.py:402
  3.2 2.7 %collective-permute-start.5 = (bf16[2,144,256]{2,1,0:T(8,128)(2,1)S(1)}, bf16[2,144,256]{2,1,0:T(8,128)(2,1)S(1)}, u32[]{:S(2)}, u32[]{:S(2)}) collective-permute-start(bf16[2,144,256]{2,1,0:T(8,128)(2,1)S(1)} %get-tuple-element.28), channel_id=1, source_target_pairs={{0,3},{1,8},{3,0},{2,11},{5,6},{4,13},{6,5},{7,14},{9,10},{8,1},{1... | collective-permute-start | bytes 442376 | tf_op jit(solution)/shard_map/ppermute | solution.py:380
  5.8 1.7 %shard_map.106 = (bf16[2,1296,256]{2,1,0:T(8,128)(2,1)S(1)}, bf16[2,1024,256]{2,1,0:T(8,128)(2,1)S(1)}, f32[1,1,256]{2,1,0:T(1,128)S(1)}) custom-call(f32[256]{0:T(256)} %weight_hbm.1, bf16[2,4,256,256]{3,2,1,0:T(8,128)(2,1)} %bitcast.3, bf16[2,8,256,256]{3,2,1,0:T(8,128)(2,1)} %proj_hbm.1, f32[2,128,256]{2,1,0:T(8,128)S(1)} %get-tuple-element.22.chip_amp), custom_call_target="tpu_custom_call" | custom-call | tf_op jit(solution)/shard_map/pallas_call | solution.py:440
  7.5 1.5 %collective-permute-start.4 = (bf16[2,1296,256]{2,1,0:T(8,128)(2,1)S(1)}, bf16[2,1296,256]{2,1,0:T(8,128)(2,1)S(1)}, u32[]{:S(2)}, u32[]{:S(2)}) collective-permute-start(bf16[2,1296,256]{2,1,0:T(8,128)(2,1)S(1)} %get-tuple-element.24.sent), channel_id=1, source_target_pairs={{0,1},{1,0},{2,3},{3,2},{4,5},{5,4},{6,7},{7,6},{8,9},{9,8},{10,11... | collective-permute-start | bytes 3981320 | tf_op jit(solution)/shard_map/ppermute | solution.py:364
  9.0 0.7 %shard_map.107.gate = f32[3,2,1,256]{3,2,1,0:T(1,128)S(1)} custom-call(s32[2,4]{1,0:T(2,128)} %bitcast.4, s32[2,4]{1,0:T(2,128)} %bitcast.5, f32[2,128,256]{2,1,0:T(8,128)S(1)} %get-tuple-element.22.chip_amp), custom_call_target="tpu_custom_call" | custom-call | flops 34359738368 | bytes 65536 | tf_op jit(solution)/shard_map/pallas_call | solution.py:429
  9.8 1.9 %collective-permute-done.4.theirs = bf16[2,1296,256]{2,1,0:T(8,128)(2,1)S(1)} collective-permute-done((bf16[2,1296,256]{2,1,0:T(8,128)(2,1)S(1)}, bf16[2,1296,256]{2,1,0:T(8,128)(2,1)S(1)}, u32[]{:S(2)}, u32[]{:S(2)}) %collective-permute-start.4) | collective-permute-done | bytes 1327136 | tf_op jit(solution)/shard_map/ppermute | solution.py:364
  12.4 1.5 %collective-permute-start.6 = (bf16[128,256]{1,0:T(8,128)(2,1)S(1)}, bf16[128,256]{1,0:T(8,128)(2,1)S(1)}, u32[]{:S(2)}, u32[]{:S(2)}) collective-permute-start(bf16[128,256]{1,0:T(8,128)(2,1)S(1)} %get-tuple-element.29.own), channel_id=1, source_target_pairs={{0,9},{1,4},{3,10},{2,7},{5,12},{4,1},{6,15},{7,2},{9,0},{8,13},{1... | collective-permute-start | bytes 196616 | tf_op jit(solution)/shard_map/ppermute | solution.py:380
  13.9 1.2 %collective-permute-start.9 = (bf16[128,256]{1,0:T(8,128)(2,1)S(1)}, bf16[128,256]{1,0:T(8,128)(2,1)S(1)}, u32[]{:S(2)}, u32[]{:S(2)}) collective-permute-start(bf16[128,256]{1,0:T(8,128)(2,1)S(1)} %get-tuple-element.31.own), channel_id=1, source_target_pairs={{0,9},{1,4},{3,10},{2,7},{5,12},{4,1},{6,15},{7,2},{9,0},{8,13},{1... | collective-permute-start | bytes 196616 | tf_op jit(solution)/shard_map/ppermute | solution.py:380
  15.1 2.1 %collective-permute-done.6.other = bf16[128,256]{1,0:T(8,128)(2,1)S(1)} collective-permute-done((bf16[128,256]{1,0:T(8,128)(2,1)S(1)}, bf16[128,256]{1,0:T(8,128)(2,1)S(1)}, u32[]{:S(2)}, u32[]{:S(2)}) %collective-permute-start.6) | collective-permute-done | bytes 65568 | tf_op jit(solution)/shard_map/ppermute | solution.py:380
  17.2 1.8 %collective-permute-start.7 = (bf16[128,256]{1,0:T(8,128)(2,1)S(1)}, bf16[128,256]{1,0:T(8,128)(2,1)S(1)}, u32[]{:S(2)}, u32[]{:S(2)}) collective-permute-start(bf16[128,256]{1,0:T(8,128)(2,1)S(1)} %shard_map.110.own), channel_id=1, source_target_pairs={{0,5},{1,2},{3,6},{2,1},{5,0},{4,7},{6,3},{7,4},{9,12},{8,11},{10,... | collective-permute-start | bytes 196616 | tf_op jit(solution)/shard_map/ppermute | solution.py:380
  19.1 0.8 %collective-permute-start.10 = (bf16[128,256]{1,0:T(8,128)(2,1)S(1)}, bf16[128,256]{1,0:T(8,128)(2,1)S(1)}, u32[]{:S(2)}, u32[]{:S(2)}) collective-permute-start(bf16[128,256]{1,0:T(8,128)(2,1)S(1)} %shard_map.113.own), channel_id=1, source_target_pairs={{0,5},{1,2},{3,6},{2,1},{5,0},{4,7},{6,3},{7,4},{9,12},{8,11},{10,... | collective-permute-start | bytes 196616 | tf_op jit(solution)/shard_map/ppermute | solution.py:380
  19.9 1.0 %collective-permute-done.7.other = bf16[128,256]{1,0:T(8,128)(2,1)S(1)} collective-permute-done((bf16[128,256]{1,0:T(8,128)(2,1)S(1)}, bf16[128,256]{1,0:T(8,128)(2,1)S(1)}, u32[]{:S(2)}, u32[]{:S(2)}) %collective-permute-start.7) | collective-permute-done | bytes 65568 | tf_op jit(solution)/shard_map/ppermute | solution.py:380
  21.1 1.7 %collective-permute-done.10.other = bf16[128,256]{1,0:T(8,128)(2,1)S(1)} collective-permute-done((bf16[128,256]{1,0:T(8,128)(2,1)S(1)}, bf16[128,256]{1,0:T(8,128)(2,1)S(1)}, u32[]{:S(2)}, u32[]{:S(2)}) %collective-permute-start.10) | collective-permute-done | bytes 65568 | tf_op jit(solution)/shard_map/ppermute | solution.py:380
  23.5 0.7 %collective-permute-done.11.high = bf16[128,256]{1,0:T(8,128)(2,1)S(1)} collective-permute-done((bf16[128,256]{1,0:T(8,128)(2,1)S(1)}, bf16[128,256]{1,0:T(8,128)(2,1)S(1)}, u32[]{:S(2)}, u32[]{:S(2)}) %collective-permute-start.11) | collective-permute-done | bytes 65568 | tf_op jit(solution)/shard_map/ppermute | solution.py:364
  24.2 0.8 %shard_map.115 = (bf16[128,256]{1,0:T(8,128)(2,1)S(1)}, bf16[128,256]{1,0:T(8,128)(2,1)S(1)}, f32[128,256]{1,0:T(8,128)S(1)}, f32[128,256]{1,0:T(8,128)S(1)}) custom-call(bf16[2,1024,256]{2,1,0:T(8,128)(2,1)S(1)} %get-tuple-element.23.mine, bf16[2,1296,256]{2,1,0:T(8,128)(2,1)S(1)} %collective-permute-done.4.theirs, ...), custom_call_target="tpu_custom_call" | custom-call | tf_op jit(solution)/shard_map/pallas_call | solution.py:361
  25.0 1.3 %collective-permute-start.12 = (bf16[128,256]{1,0:T(8,128)(2,1)S(1)}, bf16[128,256]{1,0:T(8,128)(2,1)S(1)}, u32[]{:S(2)}, u32[]{:S(2)}) collective-permute-start(bf16[128,256]{1,0:T(8,128)(2,1)S(1)} %get-tuple-element.32.own), channel_id=1, source_target_pairs={{0,9},{1,4},{3,10},{2,7},{5,12},{4,1},{6,15},{7,2},{9,0},{8,13},{1... | collective-permute-start | bytes 196616 | tf_op jit(solution)/shard_map/ppermute | solution.py:380
  26.3 1.4 %collective-permute-start.15 = (bf16[128,256]{1,0:T(8,128)(2,1)S(1)}, bf16[128,256]{1,0:T(8,128)(2,1)S(1)}, u32[]{:S(2)}, u32[]{:S(2)}) collective-permute-start(bf16[128,256]{1,0:T(8,128)(2,1)S(1)} %get-tuple-element.33.own), channel_id=1, source_target_pairs={{0,9},{1,4},{3,10},{2,7},{5,12},{4,1},{6,15},{7,2},{9,0},{8,13},{1... | collective-permute-start | bytes 196616 | tf_op jit(solution)/shard_map/ppermute | solution.py:380
  27.7 2.0 %collective-permute-done.12.other = bf16[128,256]{1,0:T(8,128)(2,1)S(1)} collective-permute-done((bf16[128,256]{1,0:T(8,128)(2,1)S(1)}, bf16[128,256]{1,0:T(8,128)(2,1)S(1)}, u32[]{:S(2)}, u32[]{:S(2)}) %collective-permute-start.12) | collective-permute-done | bytes 65568 | tf_op jit(solution)/shard_map/ppermute | solution.py:380
  29.8 0.7 %collective-permute-start.13 = (bf16[128,256]{1,0:T(8,128)(2,1)S(1)}, bf16[128,256]{1,0:T(8,128)(2,1)S(1)}, u32[]{:S(2)}, u32[]{:S(2)}) collective-permute-start(bf16[128,256]{1,0:T(8,128)(2,1)S(1)} %shard_map.116.own), channel_id=1, source_target_pairs={{0,5},{1,2},{3,6},{2,1},{5,0},{4,7},{6,3},{7,4},{9,12},{8,11},{10,... | collective-permute-start | bytes 196616 | tf_op jit(solution)/shard_map/ppermute | solution.py:380
  31.2 1.4 %collective-permute-start.16 = (bf16[128,256]{1,0:T(8,128)(2,1)S(1)}, bf16[128,256]{1,0:T(8,128)(2,1)S(1)}, u32[]{:S(2)}, u32[]{:S(2)}) collective-permute-start(bf16[128,256]{1,0:T(8,128)(2,1)S(1)} %shard_map.118.own), channel_id=1, source_target_pairs={{0,5},{1,2},{3,6},{2,1},{5,0},{4,7},{6,3},{7,4},{9,12},{8,11},{10,... | collective-permute-start | bytes 196616 | tf_op jit(solution)/shard_map/ppermute | solution.py:380
  32.7 0.9 %collective-permute-done.13.other = bf16[128,256]{1,0:T(8,128)(2,1)S(1)} collective-permute-done((bf16[128,256]{1,0:T(8,128)(2,1)S(1)}, bf16[128,256]{1,0:T(8,128)(2,1)S(1)}, u32[]{:S(2)}, u32[]{:S(2)}) %collective-permute-start.13) | collective-permute-done | bytes 65568 | tf_op jit(solution)/shard_map/ppermute | solution.py:380
  33.8 1.2 %collective-permute-done.16.other = bf16[128,256]{1,0:T(8,128)(2,1)S(1)} collective-permute-done((bf16[128,256]{1,0:T(8,128)(2,1)S(1)}, bf16[128,256]{1,0:T(8,128)(2,1)S(1)}, u32[]{:S(2)}, u32[]{:S(2)}) %collective-permute-start.16) | collective-permute-done | bytes 65568 | tf_op jit(solution)/shard_map/ppermute | solution.py:380
  35.5 0.8 %collective-permute-done.17.high = bf16[128,256]{1,0:T(8,128)(2,1)S(1)} collective-permute-done((bf16[128,256]{1,0:T(8,128)(2,1)S(1)}, bf16[128,256]{1,0:T(8,128)(2,1)S(1)}, u32[]{:S(2)}, u32[]{:S(2)}) %collective-permute-start.17) | collective-permute-done | bytes 65568 | tf_op jit(solution)/shard_map/ppermute | solution.py:364
  36.4 1.1 %shard_map.121 = (f32[256,128]{1,0:T(8,128)}, f32[1,256,128]{2,1,0:T(8,128)}) custom-call(bf16[2,1024,256]{2,1,0:T(8,128)(2,1)S(1)} %get-tuple-element.23.mine, bf16[2,1296,256]{2,1,0:T(8,128)(2,1)S(1)} %collective-permute-done.4.theirs, bf16[128,256]{1,0:T(8,128)(2,1)S(1)} %collective-permute-done.14.low, ...), custom_call_target="tpu_custom_call" | custom-call | tf_op jit(solution)/shard_map/pallas_call | solution.py:361
  (32 shorter events, 4.4 us)
Async XLA Ops:
  0.6 2.4 %collective-permute-start = (f32[256,128]{1,0:T(8,128)}, f32[256,128]{1,0:T(8,128)S(1)}, u32[]{:S(2)}, u32[]{:S(2)}) collective-permute-start(f32[256,128]{1,0:T(8,128)} %tgt_own_hbm.1), channel_id=1, source_target_pairs={{0,1},{1,0},{2,3},{3,2},{4,5},{5,4},{6,7},{7,6},{8,9},{9,8},{10,11... | collective-permute-start | bytes 393224 | tf_op jit(solution)/shard_map/ppermute | solution.py:364
  1.1 1.9 %collective-permute-start.1 = (f32[1,256,128]{2,1,0:T(8,128)}, f32[1,256,128]{2,1,0:T(8,128)S(1)}, u32[]{:S(2)}, u32[]{:S(2)}) collective-permute-start(f32[1,256,128]{2,1,0:T(8,128)} %proj_own_hbm.1), channel_id=1, source_target_pairs={{0,1},{1,0},{2,3},{3,2},{4,5},{5,4},{6,7},{7,6},{8,9},{9,8},{10,11... | collective-permute-start | bytes 393224 | tf_op jit(solution)/shard_map/ppermute | solution.py:364
  1.2 1.7 %collective-permute-start.2 = (f32[256]{0:T(256)}, f32[256]{0:T(256)S(1)}, u32[]{:S(2)}, u32[]{:S(2)}) collective-permute-start(f32[256]{0:T(256)} %tgt_energy_hbm.1), channel_id=1, source_target_pairs={{0,1},{1,0},{2,3},{3,2},{4,5},{5,4},{6,7},{7,6},{8,9},{9,8},{10,11... | collective-permute-start | bytes 3080 | tf_op jit(solution)/shard_map/ppermute | solution.py:364
  1.7 1.4 %collective-permute-start.3 = (f32[1,256]{1,0:T(1,128)}, f32[1,256]{1,0:T(1,128)S(1)}, u32[]{:S(2)}, u32[]{:S(2)}) collective-permute-start(f32[1,256]{1,0:T(1,128)} %proj_energy_hbm.1), channel_id=1, source_target_pairs={{0,1},{1,0},{2,3},{3,2},{4,5},{5,4},{6,7},{7,6},{8,9},{9,8},{10,11... | collective-permute-start | bytes 3080 | tf_op jit(solution)/shard_map/ppermute | solution.py:364
  3.2 8.9 %collective-permute-start.5 = (bf16[2,144,256]{2,1,0:T(8,128)(2,1)S(1)}, bf16[2,144,256]{2,1,0:T(8,128)(2,1)S(1)}, u32[]{:S(2)}, u32[]{:S(2)}) collective-permute-start(bf16[2,144,256]{2,1,0:T(8,128)(2,1)S(1)} %get-tuple-element.28), channel_id=1, source_target_pairs={{0,3},{1,8},{3,0},{2,11},{5,6},{4,13},{6,5},{7,14},{9,10},{8,1},{1... | collective-permute-start | bytes 442376 | tf_op jit(solution)/shard_map/ppermute | solution.py:380
  7.5 4.2 %collective-permute-start.4 = (bf16[2,1296,256]{2,1,0:T(8,128)(2,1)S(1)}, bf16[2,1296,256]{2,1,0:T(8,128)(2,1)S(1)}, u32[]{:S(2)}, u32[]{:S(2)}) collective-permute-start(bf16[2,1296,256]{2,1,0:T(8,128)(2,1)S(1)} %get-tuple-element.24.sent), channel_id=1, source_target_pairs={{0,1},{1,0},{2,3},{3,2},{4,5},{5,4},{6,7},{7,6},{8,9},{9,8},{10,11... | collective-permute-start | bytes 3981320 | tf_op jit(solution)/shard_map/ppermute | solution.py:364
  12.4 4.8 %collective-permute-start.6 = (bf16[128,256]{1,0:T(8,128)(2,1)S(1)}, bf16[128,256]{1,0:T(8,128)(2,1)S(1)}, u32[]{:S(2)}, u32[]{:S(2)}) collective-permute-start(bf16[128,256]{1,0:T(8,128)(2,1)S(1)} %get-tuple-element.29.own), channel_id=1, source_target_pairs={{0,9},{1,4},{3,10},{2,7},{5,12},{4,1},{6,15},{7,2},{9,0},{8,13},{1... | collective-permute-start | bytes 196616 | tf_op jit(solution)/shard_map/ppermute | solution.py:380
  13.9 5.2 %collective-permute-start.9 = (bf16[128,256]{1,0:T(8,128)(2,1)S(1)}, bf16[128,256]{1,0:T(8,128)(2,1)S(1)}, u32[]{:S(2)}, u32[]{:S(2)}) collective-permute-start(bf16[128,256]{1,0:T(8,128)(2,1)S(1)} %get-tuple-element.31.own), channel_id=1, source_target_pairs={{0,9},{1,4},{3,10},{2,7},{5,12},{4,1},{6,15},{7,2},{9,0},{8,13},{1... | collective-permute-start | bytes 196616 | tf_op jit(solution)/shard_map/ppermute | solution.py:380
  17.2 3.8 %collective-permute-start.7 = (bf16[128,256]{1,0:T(8,128)(2,1)S(1)}, bf16[128,256]{1,0:T(8,128)(2,1)S(1)}, u32[]{:S(2)}, u32[]{:S(2)}) collective-permute-start(bf16[128,256]{1,0:T(8,128)(2,1)S(1)} %shard_map.110.own), channel_id=1, source_target_pairs={{0,5},{1,2},{3,6},{2,1},{5,0},{4,7},{6,3},{7,4},{9,12},{8,11},{10,... | collective-permute-start | bytes 196616 | tf_op jit(solution)/shard_map/ppermute | solution.py:380
  19.1 3.8 %collective-permute-start.10 = (bf16[128,256]{1,0:T(8,128)(2,1)S(1)}, bf16[128,256]{1,0:T(8,128)(2,1)S(1)}, u32[]{:S(2)}, u32[]{:S(2)}) collective-permute-start(bf16[128,256]{1,0:T(8,128)(2,1)S(1)} %shard_map.113.own), channel_id=1, source_target_pairs={{0,5},{1,2},{3,6},{2,1},{5,0},{4,7},{6,3},{7,4},{9,12},{8,11},{10,... | collective-permute-start | bytes 196616 | tf_op jit(solution)/shard_map/ppermute | solution.py:380
  20.9 2.0 %collective-permute-start.8 = (bf16[128,256]{1,0:T(8,128)(2,1)S(1)}, bf16[128,256]{1,0:T(8,128)(2,1)S(1)}, u32[]{:S(2)}, u32[]{:S(2)}) collective-permute-start(bf16[128,256]{1,0:T(8,128)(2,1)S(1)} %shard_map.111), channel_id=1, source_target_pairs={{0,1},{1,0},{2,3},{3,2},{4,5},{5,4},{6,7},{7,6},{8,9},{9,8},{10,11... | collective-permute-start | bytes 196616 | tf_op jit(solution)/shard_map/ppermute | solution.py:364
  22.9 1.3 %collective-permute-start.11 = (bf16[128,256]{1,0:T(8,128)(2,1)S(1)}, bf16[128,256]{1,0:T(8,128)(2,1)S(1)}, u32[]{:S(2)}, u32[]{:S(2)}) collective-permute-start(bf16[128,256]{1,0:T(8,128)(2,1)S(1)} %shard_map.114), channel_id=1, source_target_pairs={{0,1},{1,0},{2,3},{3,2},{4,5},{5,4},{6,7},{7,6},{8,9},{9,8},{10,11... | collective-permute-start | bytes 196616 | tf_op jit(solution)/shard_map/ppermute | solution.py:364
  25.0 4.8 %collective-permute-start.12 = (bf16[128,256]{1,0:T(8,128)(2,1)S(1)}, bf16[128,256]{1,0:T(8,128)(2,1)S(1)}, u32[]{:S(2)}, u32[]{:S(2)}) collective-permute-start(bf16[128,256]{1,0:T(8,128)(2,1)S(1)} %get-tuple-element.32.own), channel_id=1, source_target_pairs={{0,9},{1,4},{3,10},{2,7},{5,12},{4,1},{6,15},{7,2},{9,0},{8,13},{1... | collective-permute-start | bytes 196616 | tf_op jit(solution)/shard_map/ppermute | solution.py:380
  26.3 4.9 %collective-permute-start.15 = (bf16[128,256]{1,0:T(8,128)(2,1)S(1)}, bf16[128,256]{1,0:T(8,128)(2,1)S(1)}, u32[]{:S(2)}, u32[]{:S(2)}) collective-permute-start(bf16[128,256]{1,0:T(8,128)(2,1)S(1)} %get-tuple-element.33.own), channel_id=1, source_target_pairs={{0,9},{1,4},{3,10},{2,7},{5,12},{4,1},{6,15},{7,2},{9,0},{8,13},{1... | collective-permute-start | bytes 196616 | tf_op jit(solution)/shard_map/ppermute | solution.py:380
  27.7 7.4 %collective-permute-start.18 = (f32[128,256]{1,0:T(8,128)S(1)}, f32[128,256]{1,0:T(8,128)S(1)}, u32[]{:S(2)}, u32[]{:S(2)}) collective-permute-start(f32[128,256]{1,0:T(8,128)S(1)} %get-tuple-element.35), channel_id=1, source_target_pairs={{0,1},{1,0},{2,3},{3,2},{4,5},{5,4},{6,7},{7,6},{8,9},{9,8},{10,11... | collective-permute-start | bytes 393224 | tf_op jit(solution)/shard_map/ppermute | solution.py:364
  29.8 3.8 %collective-permute-start.13 = (bf16[128,256]{1,0:T(8,128)(2,1)S(1)}, bf16[128,256]{1,0:T(8,128)(2,1)S(1)}, u32[]{:S(2)}, u32[]{:S(2)}) collective-permute-start(bf16[128,256]{1,0:T(8,128)(2,1)S(1)} %shard_map.116.own), channel_id=1, source_target_pairs={{0,5},{1,2},{3,6},{2,1},{5,0},{4,7},{6,3},{7,4},{9,12},{8,11},{10,... | collective-permute-start | bytes 196616 | tf_op jit(solution)/shard_map/ppermute | solution.py:380
  31.2 3.8 %collective-permute-start.16 = (bf16[128,256]{1,0:T(8,128)(2,1)S(1)}, bf16[128,256]{1,0:T(8,128)(2,1)S(1)}, u32[]{:S(2)}, u32[]{:S(2)}) collective-permute-start(bf16[128,256]{1,0:T(8,128)(2,1)S(1)} %shard_map.118.own), channel_id=1, source_target_pairs={{0,5},{1,2},{3,6},{2,1},{5,0},{4,7},{6,3},{7,4},{9,12},{8,11},{10,... | collective-permute-start | bytes 196616 | tf_op jit(solution)/shard_map/ppermute | solution.py:380
  33.6 1.9 %collective-permute-start.14 = (bf16[128,256]{1,0:T(8,128)(2,1)S(1)}, bf16[128,256]{1,0:T(8,128)(2,1)S(1)}, u32[]{:S(2)}, u32[]{:S(2)}) collective-permute-start(bf16[128,256]{1,0:T(8,128)(2,1)S(1)} %shard_map.117.low), channel_id=1, source_target_pairs={{0,1},{1,0},{2,3},{3,2},{4,5},{5,4},{6,7},{7,6},{8,9},{9,8},{10,11... | collective-permute-start | bytes 196616 | tf_op jit(solution)/shard_map/ppermute | solution.py:364
  35.0 1.3 %collective-permute-start.17 = (bf16[128,256]{1,0:T(8,128)(2,1)S(1)}, bf16[128,256]{1,0:T(8,128)(2,1)S(1)}, u32[]{:S(2)}, u32[]{:S(2)}) collective-permute-start(bf16[128,256]{1,0:T(8,128)(2,1)S(1)} %shard_map.119.high), channel_id=1, source_target_pairs={{0,1},{1,0},{2,3},{3,2},{4,5},{5,4},{6,7},{7,6},{8,9},{9,8},{10,11... | collective-permute-start | bytes 196616 | tf_op jit(solution)/shard_map/ppermute | solution.py:364

commit v16 on v15

--- a/solution.py
+++ b/solution.py
@@ -164,14 +164,54 @@
         message[segment, cols:] = split(rows[segment])
 
 
-def gate_kernel(gate_levels, flags_hbm, counts_hbm, chip_amp, gate, flags, counts, sems):
+def sent_kernel(neighbours, weight_hbm, tgt_hbm, proj_hbm, chip_amp, sent, weight, flat_weight, sems):
+    my = my_kind()
+    sources = (tgt_hbm, proj_hbm)
+    rows = chip_amp.shape[2]
+
+    def copies_of(kind):
+        last = pltpu.make_async_copy(
+            sources[kind].at[:, 2 * lax.axis_index(("prj", "tgt")[kind]) + 1 - lax.axis_index("rep")],
+            sent.at[:, 4 * rows : 5 * rows],
+            sems.at[4],
+        )
+        return basis_copies(sent, sems, 1 - kind, neighbours, sources) + [last]
+
+    weight_copy = pltpu.make_async_copy(weight_hbm, flat_weight, sems.at[5])
+    weight_copy.start()
+    for kind in range(2):
+
+        @pl.when(my == kind)
+        def _():
+            for copy in copies_of(kind):
+                copy.start()
+
+    weight_copy.wait()
+    weight[0] = flat_weight[...][None, :]
+    for part in range(2):
+        sent[part, 5 * rows :] = split(weight[0])
+    for copy in copies_of(0):
+        copy.wait()
+
+
+def side_kernel(
+    gate_levels, neighbours, flags_hbm, counts_hbm, tgt_hbm, proj_hbm, chip_amp, mine, gate, flags, counts, sems
+):
     my = my_kind()
     tgt_index = lax.axis_index("tgt")
     prj_index = lax.axis_index("prj")
+    sources = (tgt_hbm, proj_hbm)
     pairs = [(flags_hbm, flags), (counts_hbm, counts)]
-    copies = [pltpu.make_async_copy(src, dst, sems.at[k]) for k, (src, dst) in enumerate(pairs)]
+    copies = [pltpu.make_async_copy(src, dst, sems.at[4 + k]) for k, (src, dst) in enumerate(pairs)]
     for copy in copies:
         copy.start()
+    for kind in range(2):
+
+        @pl.when(my == kind)
+        def _():
+            for copy in basis_copies(mine, sems, kind, neighbours, sources):
+                copy.start()
+
     for copy in copies:
         copy.wait()
     tiles = 2
@@ -188,50 +228,7 @@
                 gate[level, half, :, tile * width : (tile + 1) * width] = jnp.full(
                     (1, width), here, jnp.float32
                 )
-
-
-def basis_kernel(
-    neighbours,
-    weight_hbm,
-    tgt_hbm,
-    proj_hbm,
-    chip_amp,
-    sent,
-    mine,
-    weight,
-    flat_weight,
-    sems,
-):
-    my = my_kind()
-    sources = (tgt_hbm, proj_hbm)
-    rows = chip_amp.shape[2]
-
-    def copies_of(kind):
-        last = pltpu.make_async_copy(
-            sources[kind].at[:, 2 * lax.axis_index(("prj", "tgt")[kind]) + 1 - lax.axis_index("rep")],
-            sent.at[:, 4 * rows : 5 * rows],
-            sems.at[8],
-        )
-        return (
-            basis_copies(sent, sems.at[0:4], 1 - kind, neighbours, sources)
-            + [last]
-            + basis_copies(mine, sems.at[4:8], kind, neighbours, sources)
-        )
-
-    weight_copy = pltpu.make_async_copy(weight_hbm, flat_weight, sems.at[9])
-    weight_copy.start()
-    for kind in range(2):
-
-        @pl.when(my == kind)
-        def _():
-            for copy in copies_of(kind):
-                copy.start()
-
-    weight_copy.wait()
-    weight[0] = flat_weight[...][None, :]
-    for part in range(2):
-        sent[part, 5 * rows :] = split(weight[0])
-    for copy in copies_of(0):
+    for copy in basis_copies(mine, sems, 0, neighbours, sources):
         copy.wait()
 
 
@@ -268,8 +265,9 @@
     out_ref[...] = bf16(gate[level, half] * (f32(own[...]) + f32(other[...])))
 
 
-def low_kernel(mine, theirs, low, chip_amp, energies, message, states_ref):
+def low_kernel(mine, theirs, low, low_there, chip_amp, energies, message, states_ref):
     _, cols, rows = chip_amp.shape
+    field = bf16(f32(low[...]) + f32(low_there[...]))
 
     def body(core):
         for segment in range(4):
@@ -277,19 +275,22 @@
                 amp, energy = chip_amp[segment], energies[segment]
             else:
                 amp, energy = f32(message[segment - 2, :cols]), joined(message[segment - 2, cols:])
-            change = expand(rows_of((mine, theirs)[core], segment, rows), low[...])
+            change = expand(rows_of((mine, theirs)[core], segment, rows), field)
             states_ref[segment] = amp + half_step * (energy * turned(amp) + change)
 
     by_core(body)
 
 
-def second_kernel(mine, theirs, states_ref, high, gate, weights, low_ref, high_ref, half_ref, send_ref):
+def second_kernel(
+    mine, theirs, states_ref, high, high_there, gate, weights, low_ref, high_ref, half_ref, send_ref
+):
     rows = states_ref.shape[2]
+    field = bf16(f32(high[...]) + f32(high_there[...]))
 
     def body(core):
         bases = (mine, theirs) if core == 0 else (theirs, mine)
         halves = [
-            states_ref[segment] + half_step * expand(rows_of(bases[1], segment, rows), high[...])
+            states_ref[segment] + half_step * expand(rows_of(bases[1], segment, rows), field)
             for segment in range(4)
         ]
         half_ref[...] = halves[core]
@@ -371,22 +372,23 @@
     gate_levels = (len(prj_flips) - 1, len(tgt_flips) - 1)
     n_steps = len(tgt_flips) + len(prj_flips)
 
-    def exchanged(step, block):
+    def exchanged(step, block, crossed=0):
         pairs = []
         for place in range(n_tgt * n_prj):
             for kind in range(2):
                 there = place ^ flips[kind][step]
-                pairs.append((place * n_core + (kind ^ parity(place)), there * n_core + (kind ^ parity(there))))
+                to_core = kind ^ crossed ^ parity(there)
+                pairs.append((place * n_core + (kind ^ parity(place)), there * n_core + to_core))
         return lax.ppermute(block, DEVICES, pairs)
 
     in_vmem = pltpu.VMEM
     sums = in_vmem((two_cols, points), jnp.bfloat16)
     segment = in_vmem((two_cols, rows), jnp.float32)
 
-    def summed(*halves):
+    def summed(halves, until):
         totals = []
         for half, block in enumerate(halves):
-            for step in range(1, n_steps):
+            for step in range(1, until):
                 other = exchanged(step, block)
                 (block,) = run(functools.partial(add_kernel, step, half), [sums], gate, block, other)
             totals.append(block)
@@ -426,30 +428,30 @@
     )
     message = exchanged(0, message)
     flags, counts = pair_flags.T, tile_counts.T
-    (gate,) = call(
-        functools.partial(gate_kernel, gate_levels),
-        [in_vmem((n_steps, 2, 1, points), jnp.float32)],
-        [HBM, HBM, VMEM],
+    bases = in_hbm(tgt_basis.reshape(2, -1, rows, points), proj_basis)
+    sent, weight = call(
+        functools.partial(sent_kernel, neighbours),
+        [
+            in_vmem((2, 5 * rows + PIECES, points), jnp.bfloat16),
+            in_vmem((1, 1, points), jnp.float32),
+        ],
+        [HBM] * 3 + [VMEM],
+        [pltpu.VMEM((points,), jnp.float32), pltpu.SemaphoreType.DMA((6,))],
+    )(*in_hbm(quad_weight), *bases, chip_amp)
+    mine, gate = call(
+        functools.partial(side_kernel, gate_levels, neighbours),
+        [
+            in_vmem((2, 4 * rows, points), jnp.bfloat16),
+            in_vmem((n_steps, 2, 1, points), jnp.float32),
+        ],
+        [HBM] * 4 + [VMEM],
         [
             pltpu.SMEM(flags.shape, jnp.int32),
             pltpu.SMEM(counts.shape, jnp.int32),
-            pltpu.SemaphoreType.DMA((2,)),
+            pltpu.SemaphoreType.DMA((6,)),
         ],
         BEHIND,
-    )(*in_hbm(flags, counts), chip_amp)
-    sent, mine, weight = call(
-        functools.partial(basis_kernel, neighbours),
-        [
-            in_vmem((2, 5 * rows + PIECES, points), jnp.bfloat16),
-            in_vmem((2, 4 * rows, points), jnp.bfloat16),
-            in_vmem((1, 1, points), jnp.float32),
-        ],
-        [HBM] * 3 + [VMEM],
-        [pltpu.VMEM((points,), jnp.float32), pltpu.SemaphoreType.DMA((10,))],
-    )(
-        *in_hbm(quad_weight, tgt_basis.reshape(2, -1, rows, points), proj_basis),
-        chip_amp,
-    )
+    )(*in_hbm(flags, counts), *bases, chip_amp)
     theirs = other_core(sent)
     part, weights = run(
         chip_kernel,
@@ -460,14 +462,14 @@
         weight,
     )
     halves = run(first_kernel, [sums] * 2, mine, theirs, gate, weights, part, message)
-    fields = summed(*halves)
-    low, high = swapped(fields)
+    parts = summed(halves, n_steps - 1)
+    low, high = [(other_core(block), exchanged(n_steps - 1, block, 1)) for block in parts]
     (states,) = run(
         low_kernel,
         [in_vmem((4, two_cols, rows), jnp.float32)],
         mine,
         theirs,
-        low,
+        *low,
         chip_amp,
         energies,
         message,
@@ -478,12 +480,12 @@
         mine,
         theirs,
         states,
-        high,
+        *high,
         gate,
         weights,
     )
     other_half = other_core(half_send)
-    fields = summed(*halves)
+    fields = summed(halves, n_steps)
     low, high = swapped(fields)
     my_part, other_new = run(
         late_kernel,

time: 37.6 us -> 36.6 us (0.973)
  waiting for transfers between devices: 13.3 us -> 11.3 us
  starting transfers between devices: 16 us -> 16.9 us
    ppermute x10, waiting for transfers between devices: 3.61 us -> 2.34 us  [other_core(): return lax.ppermute(block, 'rep', [(0, 1), (1, 0)])]
    ppermute x9, starting transfers between devices: 12.9 us -> 13.7 us  [exchanged(): return lax.ppermute(block, DEVICES, pairs)]
    ppermute x9, waiting for transfers between devices: 9.73 us -> 8.94 us  [exchanged(): return lax.ppermute(block, DEVICES, pairs)]
    pallas_call x15 -> x13, Pallas kernels: 3.76 us -> 3.7 us  [run(): return call(kernel, out_shape, [VMEM] * len(blocks))(*blocks)]
  transfers between devices with their start and end apart: 19 -> 19, of which waited for: 12 -> 10; matrix products, arithmetic and copies ran while one was open for 0% -> 0% of each run, Pallas kernels for 13% -> 14%
where the time goes in v16:
time: 36.6 us; the launch traced here: 36.4 us
  starting transfers between devices  16.9 us (46%)
  waiting for transfers between devices  11.3 us (31%)
  Pallas kernels  7.41 us (20%)
  between operations  0.77 us (2%)
    ppermute x9, starting transfers between devices, exchanged(): return lax.ppermute(block, DEVICES, pairs)  13.7 us
    ppermute x9, waiting for transfers between devices, exchanged(): return lax.ppermute(block, DEVICES, pairs)  8.94 us
    pallas_call x13, Pallas kernels, run(): return call(kernel, out_shape, [VMEM] * len(blocks))(*blocks)  3.7 us
    ppermute x10, starting transfers between devices, other_core(): return lax.ppermute(block, 'rep', [(0, 1), (1, 0)])  3.18 us
    ppermute x10, waiting for transfers between devices, other_core(): return lax.ppermute(block, 'rep', [(0, 1), (1, 0)])  2.34 us
    pallas_call x1, Pallas kernels, shards(): call(functools.partial(sent_kernel, neighbours), [in_vmem((2, 5 * rows +...  1.33 us
    pallas_call x1, Pallas kernels, shards(): call(functools.partial(side_kernel, gate_levels, neighbours), [in_vmem((2...  1.24 us
    pallas_call x1, Pallas kernels, shards(): call(load_kernel, [in_vmem((2, 1, rows), jnp.float32), in_vmem((2, two_co...  1.14 us
  transfers between devices with their start and end apart: 19, of which 10 were waited for; matrix products, arithmetic and copies ran while one was open for 0% of the time, Pallas kernels for 14%

profile of v16, /device:TPU:0, one launch (start us, length us, event | category | flops | bytes accessed | tf_op | source)
XLA Modules:
  0.0 36.4 jit_solution(8564383096279185482)
XLA Ops:
  0.6 0.5 %collective-permute-start = (f32[256,128]{1,0:T(8,128)}, f32[256,128]{1,0:T(8,128)S(1)}, u32[]{:S(2)}, u32[]{:S(2)}) collective-permute-start(f32[256,128]{1,0:T(8,128)} %tgt_own_hbm.1), channel_id=1, source_target_pairs={{0,1},{1,0},{2,3},{3,2},{4,5},{5,4},{6,7},{7,6},{8,9},{9,8},{10,11... | collective-permute-start | bytes 393224 | tf_op jit(solution)/shard_map/ppermute | solution.py:365
  1.7 1.1 %shard_map.104 = (f32[2,1,256]{2,1,0:T(1,128)S(1)}, f32[2,128,256]{2,1,0:T(8,128)S(1)}) custom-call(f32[256]{0:T(256)} %tgt_energy_hbm.1, f32[1,256]{1,0:T(1,128)} %proj_energy_hbm.1, f32[256,128]{1,0:T(8,128)} %tgt_own_hbm.1, f32[1,256,128]{2,1,0:T(8,128)} %proj_own_hbm.1), custom_call_target="tpu_custom_call" | custom-call | flops 67108864 | bytes 4194304 | tf_op jit(solution)/shard_map/pallas_call | solution.py:404
  3.2 2.7 %collective-permute-start.5 = (bf16[2,144,256]{2,1,0:T(8,128)(2,1)S(1)}, bf16[2,144,256]{2,1,0:T(8,128)(2,1)S(1)}, u32[]{:S(2)}, u32[]{:S(2)}) collective-permute-start(bf16[2,144,256]{2,1,0:T(8,128)(2,1)S(1)} %get-tuple-element.30), channel_id=1, source_target_pairs={{0,3},{1,8},{3,0},{2,11},{5,6},{4,13},{6,5},{7,14},{9,10},{8,1},{1... | collective-permute-start | bytes 442376 | tf_op jit(solution)/shard_map/ppermute | solution.py:382
  5.8 1.3 %shard_map.107 = (bf16[2,1296,256]{2,1,0:T(8,128)(2,1)S(1)}, f32[1,1,256]{2,1,0:T(1,128)S(1)}) custom-call(f32[256]{0:T(256)} %weight_hbm.1, bf16[2,4,256,256]{3,2,1,0:T(8,128)(2,1)} %bitcast.3, bf16[2,8,256,256]{3,2,1,0:T(8,128)(2,1)} %proj_hbm.3, f32[2,128,256]{2,1,0:T(8,128)S(1)} %get-tuple-element.23.chip_amp), custom_call_target="tpu_custom_call" | custom-call | tf_op jit(solution)/shard_map/pallas_call | solution.py:432
  7.2 1.5 %collective-permute-start.4 = (bf16[2,1296,256]{2,1,0:T(8,128)(2,1)S(1)}, bf16[2,1296,256]{2,1,0:T(8,128)(2,1)S(1)}, u32[]{:S(2)}, u32[]{:S(2)}) collective-permute-start(bf16[2,1296,256]{2,1,0:T(8,128)(2,1)S(1)} %get-tuple-element.25.sent), channel_id=1, source_target_pairs={{0,1},{1,0},{2,3},{3,2},{4,5},{5,4},{6,7},{7,6},{8,9},{9,8},{10,11... | collective-permute-start | bytes 3981320 | tf_op jit(solution)/shard_map/ppermute | solution.py:365
  8.7 1.2 %shard_map.106 = (bf16[2,1024,256]{2,1,0:T(8,128)(2,1)S(1)}, f32[3,2,1,256]{3,2,1,0:T(1,128)S(1)}) custom-call(s32[2,4]{1,0:T(2,128)} %bitcast.5, s32[2,4]{1,0:T(2,128)} %bitcast.6, bf16[2,4,256,256]{3,2,1,0:T(8,128)(2,1)} %bitcast.4, bf16[2,8,256,256]{3,2,1,0:T(8,128)(2,1)} %proj_hbm.3, f32[2,128,256]{2,1,0:T(8,128)S(1)} %get-tuple-element.23.chip_amp), custom_call_target="tpu_custom_call" | custom-call | flops 34359738368 | bytes 65536 | tf_op jit(solution)/shard_map/pallas_call | solution.py:441
  9.9 1.4 %collective-permute-done.4.theirs = bf16[2,1296,256]{2,1,0:T(8,128)(2,1)S(1)} collective-permute-done((bf16[2,1296,256]{2,1,0:T(8,128)(2,1)S(1)}, bf16[2,1296,256]{2,1,0:T(8,128)(2,1)S(1)}, u32[]{:S(2)}, u32[]{:S(2)}) %collective-permute-start.4) | collective-permute-done | bytes 1327136 | tf_op jit(solution)/shard_map/ppermute | solution.py:365
  12.0 1.5 %collective-permute-start.6 = (bf16[128,256]{1,0:T(8,128)(2,1)S(1)}, bf16[128,256]{1,0:T(8,128)(2,1)S(1)}, u32[]{:S(2)}, u32[]{:S(2)}) collective-permute-start(bf16[128,256]{1,0:T(8,128)(2,1)S(1)} %get-tuple-element.31.own), channel_id=1, source_target_pairs={{0,9},{1,4},{3,10},{2,7},{5,12},{4,1},{6,15},{7,2},{9,0},{8,13},{1... | collective-permute-start | bytes 196616 | tf_op jit(solution)/shard_map/ppermute | solution.py:382
  13.5 1.2 %collective-permute-start.9 = (bf16[128,256]{1,0:T(8,128)(2,1)S(1)}, bf16[128,256]{1,0:T(8,128)(2,1)S(1)}, u32[]{:S(2)}, u32[]{:S(2)}) collective-permute-start(bf16[128,256]{1,0:T(8,128)(2,1)S(1)} %get-tuple-element.33.own), channel_id=1, source_target_pairs={{0,9},{1,4},{3,10},{2,7},{5,12},{4,1},{6,15},{7,2},{9,0},{8,13},{1... | collective-permute-start | bytes 196616 | tf_op jit(solution)/shard_map/ppermute | solution.py:382
  14.7 2.1 %collective-permute-done.6.other = bf16[128,256]{1,0:T(8,128)(2,1)S(1)} collective-permute-done((bf16[128,256]{1,0:T(8,128)(2,1)S(1)}, bf16[128,256]{1,0:T(8,128)(2,1)S(1)}, u32[]{:S(2)}, u32[]{:S(2)}) %collective-permute-start.6) | collective-permute-done | bytes 65568 | tf_op jit(solution)/shard_map/ppermute | solution.py:382
  16.8 1.0 %collective-permute-start.8 = (bf16[128,256]{1,0:T(8,128)(2,1)S(1)}, bf16[128,256]{1,0:T(8,128)(2,1)S(1)}, u32[]{:S(2)}, u32[]{:S(2)}) collective-permute-start(bf16[128,256]{1,0:T(8,128)(2,1)S(1)} %shard_map.110), channel_id=1, source_target_pairs={{0,4},{1,3},{3,7},{2,0},{5,1},{4,6},{6,2},{7,5},{9,13},{8,10},{10,... | collective-permute-start | bytes 196616 | tf_op jit(solution)/shard_map/ppermute | solution.py:382
  18.2 0.6 %collective-permute-done.9.other = bf16[128,256]{1,0:T(8,128)(2,1)S(1)} collective-permute-done((bf16[128,256]{1,0:T(8,128)(2,1)S(1)}, bf16[128,256]{1,0:T(8,128)(2,1)S(1)}, u32[]{:S(2)}, u32[]{:S(2)}) %collective-permute-start.9) | collective-permute-done | bytes 65568 | tf_op jit(solution)/shard_map/ppermute | solution.py:382
  18.8 1.7 %collective-permute-start.11 = (bf16[128,256]{1,0:T(8,128)(2,1)S(1)}, bf16[128,256]{1,0:T(8,128)(2,1)S(1)}, u32[]{:S(2)}, u32[]{:S(2)}) collective-permute-start(bf16[128,256]{1,0:T(8,128)(2,1)S(1)} %shard_map.112), channel_id=1, source_target_pairs={{0,4},{1,3},{3,7},{2,0},{5,1},{4,6},{6,2},{7,5},{9,13},{8,10},{10,... | collective-permute-start | bytes 196616 | tf_op jit(solution)/shard_map/ppermute | solution.py:382
  20.4 0.7 %collective-permute-done.8.low_there = bf16[128,256]{1,0:T(8,128)(2,1)S(1)} collective-permute-done((bf16[128,256]{1,0:T(8,128)(2,1)S(1)}, bf16[128,256]{1,0:T(8,128)(2,1)S(1)}, u32[]{:S(2)}, u32[]{:S(2)}) %collective-permute-start.8) | collective-permute-done | bytes 65568 | tf_op jit(solution)/shard_map/ppermute | solution.py:382
  21.6 1.4 %collective-permute-done.11.high_there = bf16[128,256]{1,0:T(8,128)(2,1)S(1)} collective-permute-done((bf16[128,256]{1,0:T(8,128)(2,1)S(1)}, bf16[128,256]{1,0:T(8,128)(2,1)S(1)}, u32[]{:S(2)}, u32[]{:S(2)}) %collective-permute-start.11) | collective-permute-done | bytes 65568 | tf_op jit(solution)/shard_map/ppermute | solution.py:382
  23.1 0.8 %shard_map.113 = (bf16[128,256]{1,0:T(8,128)(2,1)S(1)}, bf16[128,256]{1,0:T(8,128)(2,1)S(1)}, f32[128,256]{1,0:T(8,128)S(1)}, f32[128,256]{1,0:T(8,128)S(1)}) custom-call(bf16[2,1024,256]{2,1,0:T(8,128)(2,1)S(1)} %get-tuple-element.24.mine, bf16[2,1296,256]{2,1,0:T(8,128)(2,1)S(1)} %collective-permute-done.4.theirs, ...), custom_call_target="tpu_custom_call" | custom-call | tf_op jit(solution)/shard_map/pallas_call | solution.py:362
  24.2 2.4 %collective-permute-start.15 = (bf16[128,256]{1,0:T(8,128)(2,1)S(1)}, bf16[128,256]{1,0:T(8,128)(2,1)S(1)}, u32[]{:S(2)}, u32[]{:S(2)}) collective-permute-start(bf16[128,256]{1,0:T(8,128)(2,1)S(1)} %get-tuple-element.35.own), channel_id=1, source_target_pairs={{0,9},{1,4},{3,10},{2,7},{5,12},{4,1},{6,15},{7,2},{9,0},{8,13},{1... | collective-permute-start | bytes 196616 | tf_op jit(solution)/shard_map/ppermute | solution.py:382
  26.6 1.9 %collective-permute-done.12.other = bf16[128,256]{1,0:T(8,128)(2,1)S(1)} collective-permute-done((bf16[128,256]{1,0:T(8,128)(2,1)S(1)}, bf16[128,256]{1,0:T(8,128)(2,1)S(1)}, u32[]{:S(2)}, u32[]{:S(2)}) %collective-permute-start.12) | collective-permute-done | bytes 65568 | tf_op jit(solution)/shard_map/ppermute | solution.py:382
  28.6 1.6 %collective-permute-start.13 = (bf16[128,256]{1,0:T(8,128)(2,1)S(1)}, bf16[128,256]{1,0:T(8,128)(2,1)S(1)}, u32[]{:S(2)}, u32[]{:S(2)}) collective-permute-start(bf16[128,256]{1,0:T(8,128)(2,1)S(1)} %shard_map.114.own), channel_id=1, source_target_pairs={{0,5},{1,2},{3,6},{2,1},{5,0},{4,7},{6,3},{7,4},{9,12},{8,11},{10,... | collective-permute-start | bytes 196616 | tf_op jit(solution)/shard_map/ppermute | solution.py:382
  30.2 1.4 %collective-permute-start.16 = (bf16[128,256]{1,0:T(8,128)(2,1)S(1)}, bf16[128,256]{1,0:T(8,128)(2,1)S(1)}, u32[]{:S(2)}, u32[]{:S(2)}) collective-permute-start(bf16[128,256]{1,0:T(8,128)(2,1)S(1)} %shard_map.116.own), channel_id=1, source_target_pairs={{0,5},{1,2},{3,6},{2,1},{5,0},{4,7},{6,3},{7,4},{9,12},{8,11},{10,... | collective-permute-start | bytes 196616 | tf_op jit(solution)/shard_map/ppermute | solution.py:382
  31.6 0.8 %collective-permute-done.13.other = bf16[128,256]{1,0:T(8,128)(2,1)S(1)} collective-permute-done((bf16[128,256]{1,0:T(8,128)(2,1)S(1)}, bf16[128,256]{1,0:T(8,128)(2,1)S(1)}, u32[]{:S(2)}, u32[]{:S(2)}) %collective-permute-start.13) | collective-permute-done | bytes 65568 | tf_op jit(solution)/shard_map/ppermute | solution.py:382
  32.4 1.5 %collective-permute-done.16.other = bf16[128,256]{1,0:T(8,128)(2,1)S(1)} collective-permute-done((bf16[128,256]{1,0:T(8,128)(2,1)S(1)}, bf16[128,256]{1,0:T(8,128)(2,1)S(1)}, u32[]{:S(2)}, u32[]{:S(2)}) %collective-permute-start.16) | collective-permute-done | bytes 65568 | tf_op jit(solution)/shard_map/ppermute | solution.py:382
  34.5 0.8 %collective-permute-done.17.high = bf16[128,256]{1,0:T(8,128)(2,1)S(1)} collective-permute-done((bf16[128,256]{1,0:T(8,128)(2,1)S(1)}, bf16[128,256]{1,0:T(8,128)(2,1)S(1)}, u32[]{:S(2)}, u32[]{:S(2)}) %collective-permute-start.17) | collective-permute-done | bytes 65568 | tf_op jit(solution)/shard_map/ppermute | solution.py:365
  35.3 1.1 %shard_map.119 = (f32[256,128]{1,0:T(8,128)}, f32[1,256,128]{2,1,0:T(8,128)}) custom-call(bf16[2,1024,256]{2,1,0:T(8,128)(2,1)S(1)} %get-tuple-element.24.mine, bf16[2,1296,256]{2,1,0:T(8,128)(2,1)S(1)} %collective-permute-done.4.theirs, bf16[128,256]{1,0:T(8,128)(2,1)S(1)} %collective-permute-done.14.low, ...), custom_call_target="tpu_custom_call" | custom-call | tf_op jit(solution)/shard_map/pallas_call | solution.py:362
  (30 shorter events, 3.5 us)
Async XLA Ops:
  0.6 2.4 %collective-permute-start = (f32[256,128]{1,0:T(8,128)}, f32[256,128]{1,0:T(8,128)S(1)}, u32[]{:S(2)}, u32[]{:S(2)}) collective-permute-start(f32[256,128]{1,0:T(8,128)} %tgt_own_hbm.1), channel_id=1, source_target_pairs={{0,1},{1,0},{2,3},{3,2},{4,5},{5,4},{6,7},{7,6},{8,9},{9,8},{10,11... | collective-permute-start | bytes 393224 | tf_op jit(solution)/shard_map/ppermute | solution.py:365
  1.1 1.9 %collective-permute-start.1 = (f32[1,256,128]{2,1,0:T(8,128)}, f32[1,256,128]{2,1,0:T(8,128)S(1)}, u32[]{:S(2)}, u32[]{:S(2)}) collective-permute-start(f32[1,256,128]{2,1,0:T(8,128)} %proj_own_hbm.1), channel_id=1, source_target_pairs={{0,1},{1,0},{2,3},{3,2},{4,5},{5,4},{6,7},{7,6},{8,9},{9,8},{10,11... | collective-permute-start | bytes 393224 | tf_op jit(solution)/shard_map/ppermute | solution.py:365
  1.2 1.7 %collective-permute-start.2 = (f32[256]{0:T(256)}, f32[256]{0:T(256)S(1)}, u32[]{:S(2)}, u32[]{:S(2)}) collective-permute-start(f32[256]{0:T(256)} %tgt_energy_hbm.1), channel_id=1, source_target_pairs={{0,1},{1,0},{2,3},{3,2},{4,5},{5,4},{6,7},{7,6},{8,9},{9,8},{10,11... | collective-permute-start | bytes 3080 | tf_op jit(solution)/shard_map/ppermute | solution.py:365
  1.7 1.4 %collective-permute-start.3 = (f32[1,256]{1,0:T(1,128)}, f32[1,256]{1,0:T(1,128)S(1)}, u32[]{:S(2)}, u32[]{:S(2)}) collective-permute-start(f32[1,256]{1,0:T(1,128)} %proj_energy_hbm.1), channel_id=1, source_target_pairs={{0,1},{1,0},{2,3},{3,2},{4,5},{5,4},{6,7},{7,6},{8,9},{9,8},{10,11... | collective-permute-start | bytes 3080 | tf_op jit(solution)/shard_map/ppermute | solution.py:365
  3.2 8.5 %collective-permute-start.5 = (bf16[2,144,256]{2,1,0:T(8,128)(2,1)S(1)}, bf16[2,144,256]{2,1,0:T(8,128)(2,1)S(1)}, u32[]{:S(2)}, u32[]{:S(2)}) collective-permute-start(bf16[2,144,256]{2,1,0:T(8,128)(2,1)S(1)} %get-tuple-element.30), channel_id=1, source_target_pairs={{0,3},{1,8},{3,0},{2,11},{5,6},{4,13},{6,5},{7,14},{9,10},{8,1},{1... | collective-permute-start | bytes 442376 | tf_op jit(solution)/shard_map/ppermute | solution.py:382
  7.2 4.2 %collective-permute-start.4 = (bf16[2,1296,256]{2,1,0:T(8,128)(2,1)S(1)}, bf16[2,1296,256]{2,1,0:T(8,128)(2,1)S(1)}, u32[]{:S(2)}, u32[]{:S(2)}) collective-permute-start(bf16[2,1296,256]{2,1,0:T(8,128)(2,1)S(1)} %get-tuple-element.25.sent), channel_id=1, source_target_pairs={{0,1},{1,0},{2,3},{3,2},{4,5},{5,4},{6,7},{7,6},{8,9},{9,8},{10,11... | collective-permute-start | bytes 3981320 | tf_op jit(solution)/shard_map/ppermute | solution.py:365
  12.0 4.8 %collective-permute-start.6 = (bf16[128,256]{1,0:T(8,128)(2,1)S(1)}, bf16[128,256]{1,0:T(8,128)(2,1)S(1)}, u32[]{:S(2)}, u32[]{:S(2)}) collective-permute-start(bf16[128,256]{1,0:T(8,128)(2,1)S(1)} %get-tuple-element.31.own), channel_id=1, source_target_pairs={{0,9},{1,4},{3,10},{2,7},{5,12},{4,1},{6,15},{7,2},{9,0},{8,13},{1... | collective-permute-start | bytes 196616 | tf_op jit(solution)/shard_map/ppermute | solution.py:382
  13.5 5.2 %collective-permute-start.9 = (bf16[128,256]{1,0:T(8,128)(2,1)S(1)}, bf16[128,256]{1,0:T(8,128)(2,1)S(1)}, u32[]{:S(2)}, u32[]{:S(2)}) collective-permute-start(bf16[128,256]{1,0:T(8,128)(2,1)S(1)} %get-tuple-element.33.own), channel_id=1, source_target_pairs={{0,9},{1,4},{3,10},{2,7},{5,12},{4,1},{6,15},{7,2},{9,0},{8,13},{1... | collective-permute-start | bytes 196616 | tf_op jit(solution)/shard_map/ppermute | solution.py:382
  16.8 4.3 %collective-permute-start.8 = (bf16[128,256]{1,0:T(8,128)(2,1)S(1)}, bf16[128,256]{1,0:T(8,128)(2,1)S(1)}, u32[]{:S(2)}, u32[]{:S(2)}) collective-permute-start(bf16[128,256]{1,0:T(8,128)(2,1)S(1)} %shard_map.110), channel_id=1, source_target_pairs={{0,4},{1,3},{3,7},{2,0},{5,1},{4,6},{6,2},{7,5},{9,13},{8,10},{10,... | collective-permute-start | bytes 196616 | tf_op jit(solution)/shard_map/ppermute | solution.py:382
  17.8 3.3 %collective-permute-start.7 = (bf16[128,256]{1,0:T(8,128)(2,1)S(1)}, bf16[128,256]{1,0:T(8,128)(2,1)S(1)}, u32[]{:S(2)}, u32[]{:S(2)}) collective-permute-start(bf16[128,256]{1,0:T(8,128)(2,1)S(1)} %shard_map.110), channel_id=1, source_target_pairs={{0,1},{1,0},{2,3},{3,2},{4,5},{5,4},{6,7},{7,6},{8,9},{9,8},{10,11... | collective-permute-start | bytes 196616 | tf_op jit(solution)/shard_map/ppermute | solution.py:365
  18.8 4.3 %collective-permute-start.11 = (bf16[128,256]{1,0:T(8,128)(2,1)S(1)}, bf16[128,256]{1,0:T(8,128)(2,1)S(1)}, u32[]{:S(2)}, u32[]{:S(2)}) collective-permute-start(bf16[128,256]{1,0:T(8,128)(2,1)S(1)} %shard_map.112), channel_id=1, source_target_pairs={{0,4},{1,3},{3,7},{2,0},{5,1},{4,6},{6,2},{7,5},{9,13},{8,10},{10,... | collective-permute-start | bytes 196616 | tf_op jit(solution)/shard_map/ppermute | solution.py:382
  20.4 2.6 %collective-permute-start.10 = (bf16[128,256]{1,0:T(8,128)(2,1)S(1)}, bf16[128,256]{1,0:T(8,128)(2,1)S(1)}, u32[]{:S(2)}, u32[]{:S(2)}) collective-permute-start(bf16[128,256]{1,0:T(8,128)(2,1)S(1)} %shard_map.112), channel_id=1, source_target_pairs={{0,1},{1,0},{2,3},{3,2},{4,5},{5,4},{6,7},{7,6},{8,9},{9,8},{10,11... | collective-permute-start | bytes 196616 | tf_op jit(solution)/shard_map/ppermute | solution.py:365
  23.9 4.7 %collective-permute-start.12 = (bf16[128,256]{1,0:T(8,128)(2,1)S(1)}, bf16[128,256]{1,0:T(8,128)(2,1)S(1)}, u32[]{:S(2)}, u32[]{:S(2)}) collective-permute-start(bf16[128,256]{1,0:T(8,128)(2,1)S(1)} %get-tuple-element.34.own), channel_id=1, source_target_pairs={{0,9},{1,4},{3,10},{2,7},{5,12},{4,1},{6,15},{7,2},{9,0},{8,13},{1... | collective-permute-start | bytes 196616 | tf_op jit(solution)/shard_map/ppermute | solution.py:382
  24.2 5.9 %collective-permute-start.15 = (bf16[128,256]{1,0:T(8,128)(2,1)S(1)}, bf16[128,256]{1,0:T(8,128)(2,1)S(1)}, u32[]{:S(2)}, u32[]{:S(2)}) collective-permute-start(bf16[128,256]{1,0:T(8,128)(2,1)S(1)} %get-tuple-element.35.own), channel_id=1, source_target_pairs={{0,9},{1,4},{3,10},{2,7},{5,12},{4,1},{6,15},{7,2},{9,0},{8,13},{1... | collective-permute-start | bytes 196616 | tf_op jit(solution)/shard_map/ppermute | solution.py:382
  26.6 7.5 %collective-permute-start.18 = (f32[128,256]{1,0:T(8,128)S(1)}, f32[128,256]{1,0:T(8,128)S(1)}, u32[]{:S(2)}, u32[]{:S(2)}) collective-permute-start(f32[128,256]{1,0:T(8,128)S(1)} %get-tuple-element.37), channel_id=1, source_target_pairs={{0,1},{1,0},{2,3},{3,2},{4,5},{5,4},{6,7},{7,6},{8,9},{9,8},{10,11... | collective-permute-start | bytes 393224 | tf_op jit(solution)/shard_map/ppermute | solution.py:365
  28.6 3.8 %collective-permute-start.13 = (bf16[128,256]{1,0:T(8,128)(2,1)S(1)}, bf16[128,256]{1,0:T(8,128)(2,1)S(1)}, u32[]{:S(2)}, u32[]{:S(2)}) collective-permute-start(bf16[128,256]{1,0:T(8,128)(2,1)S(1)} %shard_map.114.own), channel_id=1, source_target_pairs={{0,5},{1,2},{3,6},{2,1},{5,0},{4,7},{6,3},{7,4},{9,12},{8,11},{10,... | collective-permute-start | bytes 196616 | tf_op jit(solution)/shard_map/ppermute | solution.py:382
  30.2 3.8 %collective-permute-start.16 = (bf16[128,256]{1,0:T(8,128)(2,1)S(1)}, bf16[128,256]{1,0:T(8,128)(2,1)S(1)}, u32[]{:S(2)}, u32[]{:S(2)}) collective-permute-start(bf16[128,256]{1,0:T(8,128)(2,1)S(1)} %shard_map.116.own), channel_id=1, source_target_pairs={{0,5},{1,2},{3,6},{2,1},{5,0},{4,7},{6,3},{7,4},{9,12},{8,11},{10,... | collective-permute-start | bytes 196616 | tf_op jit(solution)/shard_map/ppermute | solution.py:382
  32.4 2.1 %collective-permute-start.14 = (bf16[128,256]{1,0:T(8,128)(2,1)S(1)}, bf16[128,256]{1,0:T(8,128)(2,1)S(1)}, u32[]{:S(2)}, u32[]{:S(2)}) collective-permute-start(bf16[128,256]{1,0:T(8,128)(2,1)S(1)} %shard_map.115.low), channel_id=1, source_target_pairs={{0,1},{1,0},{2,3},{3,2},{4,5},{5,4},{6,7},{7,6},{8,9},{9,8},{10,11... | collective-permute-start | bytes 196616 | tf_op jit(solution)/shard_map/ppermute | solution.py:365
  34.0 1.3 %collective-permute-start.17 = (bf16[128,256]{1,0:T(8,128)(2,1)S(1)}, bf16[128,256]{1,0:T(8,128)(2,1)S(1)}, u32[]{:S(2)}, u32[]{:S(2)}) collective-permute-start(bf16[128,256]{1,0:T(8,128)(2,1)S(1)} %shard_map.117.high), channel_id=1, source_target_pairs={{0,1},{1,0},{2,3},{3,2},{4,5},{5,4},{6,7},{7,6},{8,9},{9,8},{10,11... | collective-permute-start | bytes 196616 | tf_op jit(solution)/shard_map/ppermute | solution.py:365

commit v17 on v16

--- a/solution.py
+++ b/solution.py
@@ -56,8 +56,9 @@
     return block.astype(jnp.float32)
 
 
-def rows_of(basis, segment, amount):
-    return [basis[part, segment * amount : (segment + 1) * amount, :] for part in range(2)]
+def rows_of(bases, segment, amount):
+    start = segment % 2 * amount
+    return [bases[segment // 2][part, start : start + amount, :] for part in range(2)]
 
 
 def project(basis, amp):
@@ -93,19 +94,17 @@
     return pieces[0:1] + pieces[1:2] + pieces[2:3]
 
 
-def basis_copies(basis, sem, my, neighbours, sources):
-    axis = ("prj", "tgt")[my]
+def basis_copies(bases, sem, my, neighbours, sources):
     rows = sources[my].shape[2]
-    place = lax.axis_index(axis)
+    place = lax.axis_index(("prj", "tgt")[my])
     copies = []
     for chip, there in enumerate((place, jnp.bitwise_xor(place, neighbours[my]))):
         for core in range(2):
-            segment = 2 * chip + core
             copies.append(
                 pltpu.make_async_copy(
                     sources[my].at[:, 2 * there + core],
-                    basis.at[:, segment * rows : (segment + 1) * rows],
-                    sem.at[segment],
+                    bases[chip].at[:, core * rows : (core + 1) * rows],
+                    sem.at[2 * chip + core],
                 )
             )
     return copies
@@ -164,18 +163,20 @@
         message[segment, cols:] = split(rows[segment])
 
 
-def sent_kernel(neighbours, weight_hbm, tgt_hbm, proj_hbm, chip_amp, sent, weight, flat_weight, sems):
+def sent_kernel(
+    neighbours, weight_hbm, tgt_hbm, proj_hbm, chip_amp, sent_chip, sent_far, sent_own, weight, flat_weight, sems
+):
     my = my_kind()
     sources = (tgt_hbm, proj_hbm)
     rows = chip_amp.shape[2]
 
     def copies_of(kind):
-        last = pltpu.make_async_copy(
+        own = pltpu.make_async_copy(
             sources[kind].at[:, 2 * lax.axis_index(("prj", "tgt")[kind]) + 1 - lax.axis_index("rep")],
-            sent.at[:, 4 * rows : 5 * rows],
+            sent_own,
             sems.at[4],
         )
-        return basis_copies(sent, sems, 1 - kind, neighbours, sources) + [last]
+        return basis_copies((sent_chip, sent_far), sems, 1 - kind, neighbours, sources) + [own]
 
     weight_copy = pltpu.make_async_copy(weight_hbm, flat_weight, sems.at[5])
     weight_copy.start()
@@ -189,13 +190,25 @@
     weight_copy.wait()
     weight[0] = flat_weight[...][None, :]
     for part in range(2):
-        sent[part, 5 * rows :] = split(weight[0])
+        sent_chip[part, 2 * rows :] = split(weight[0])
     for copy in copies_of(0):
         copy.wait()
 
 
 def side_kernel(
-    gate_levels, neighbours, flags_hbm, counts_hbm, tgt_hbm, proj_hbm, chip_amp, mine, gate, flags, counts, sems
+    gate_levels,
+    neighbours,
+    flags_hbm,
+    counts_hbm,
+    tgt_hbm,
+    proj_hbm,
+    chip_amp,
+    mine_chip,
+    mine_far,
+    gate,
+    flags,
+    counts,
+    sems,
 ):
     my = my_kind()
     tgt_index = lax.axis_index("tgt")
@@ -209,7 +222,7 @@
 
         @pl.when(my == kind)
         def _():
-            for copy in basis_copies(mine, sems, kind, neighbours, sources):
+            for copy in basis_copies((mine_chip, mine_far), sems, kind, neighbours, sources):
                 copy.start()
 
     for copy in copies:
@@ -228,11 +241,12 @@
                 gate[level, half, :, tile * width : (tile + 1) * width] = jnp.full(
                     (1, width), here, jnp.float32
                 )
-    for copy in basis_copies(mine, sems, 0, neighbours, sources):
+    for copy in basis_copies((mine_chip, mine_far), sems, 0, neighbours, sources):
         copy.wait()
 
 
-def chip_kernel(mine, theirs, chip_amp, weight, part_ref, weights):
+def chip_kernel(mine_chip, theirs_chip, chip_amp, weight, part_ref, weights):
+    mine, theirs = (mine_chip,), (theirs_chip,)
     rows = chip_amp.shape[2]
 
     def body(core):
@@ -241,12 +255,13 @@
                 project(rows_of(basis, segment, rows), chip_amp[segment]) for segment in range(2)
             )
         weights[core] = weight[0]
-        weights[1 - core] = joined(theirs[0, 5 * rows :, :])
+        weights[1 - core] = joined(theirs_chip[0, 2 * rows :, :])
 
     by_core(body)
 
 
-def first_kernel(mine, theirs, gate, weights, part_ref, message, *outs):
+def first_kernel(mine_far, theirs_far, gate, weights, part_ref, message, *outs):
+    mine, theirs = (None, mine_far), (None, theirs_far)
     rows = message.shape[2]
     cols = part_ref.shape[1]
 
@@ -265,7 +280,19 @@
     out_ref[...] = bf16(gate[level, half] * (f32(own[...]) + f32(other[...])))
 
 
-def low_kernel(mine, theirs, low, low_there, chip_amp, energies, message, states_ref):
+def low_kernel(
+    mine_chip,
+    mine_far,
+    theirs_chip,
+    theirs_far,
+    low,
+    low_there,
+    chip_amp,
+    energies,
+    message,
+    states_ref,
+):
+    mine, theirs = (mine_chip, mine_far), (theirs_chip, theirs_far)
     _, cols, rows = chip_amp.shape
     field = bf16(f32(low[...]) + f32(low_there[...]))
 
@@ -282,8 +309,21 @@
 
 
 def second_kernel(
-    mine, theirs, states_ref, high, high_there, gate, weights, low_ref, high_ref, half_ref, send_ref
-):
+    mine_chip,
+    mine_far,
+    theirs_chip,
+    theirs_far,
+    states_ref,
+    high,
+    high_there,
+    gate,
+    weights,
+    low_ref,
+    high_ref,
+    half_ref,
+    send_ref,
+):
+    mine, theirs = (mine_chip, mine_far), (theirs_chip, theirs_far)
     rows = states_ref.shape[2]
     field = bf16(f32(high[...]) + f32(high_there[...]))
 
@@ -304,13 +344,15 @@
     by_core(body)
 
 
-def late_kernel(theirs, sent, low, high, energy, amp_ref, my_half, other_half, my_part, other_new):
+def late_kernel(theirs_own, sent_chip, low, high, energy, amp_ref, my_half, other_half, my_part, other_new):
     rows = amp_ref.shape[2]
 
     def body(core):
         my = my_kind()
         near, far = (low, high) if core == 0 else (high, low)
-        change = expand(rows_of(sent, core, rows), near[...]) + expand(rows_of(theirs, 4, rows), far[...])
+        change = expand(rows_of((sent_chip,), core, rows), near[...]) + expand(
+            rows_of((theirs_own,), 0, rows), far[...]
+        )
         rate = energy[1 - my] * turned(other_half[...]) + change
         other_new[...] = (amp_ref[1 - my] + time_step * rate).T
         my_part[...] = amp_ref[my] + time_step * (energy[my] * turned(my_half[...]))
@@ -318,13 +360,13 @@
     by_core(body)
 
 
-def last_kernel(mine, theirs, low, high, my_part, other_new, new_tgt, new_proj):
+def last_kernel(mine_chip, theirs_chip, low, high, my_part, other_new, new_tgt, new_proj):
     rows = my_part.shape[1]
 
     def body(core):
         near, far = (low, high) if core == 0 else (high, low)
-        change = expand(rows_of(mine, core, rows), near[...]) + expand(
-            rows_of(theirs, core, rows), far[...]
+        change = expand(rows_of((mine_chip,), core, rows), near[...]) + expand(
+            rows_of((theirs_chip,), core, rows), far[...]
         )
         my_new = (my_part[...] + time_step * change).T
         new_tgt[...], new_proj[0] = ordered(my_kind(), my_new, other_new[...])
@@ -367,16 +409,17 @@
     n_tgt, n_prj, n_core = sizes
     tgt_flips = [n_prj << bit for bit in range(n_tgt.bit_length() - 1)]
     prj_flips = [1 << bit for bit in range(n_prj.bit_length() - 1)]
-    flips = (prj_flips + tgt_flips[::-1], tgt_flips[::-1] + prj_flips)
-    neighbours = (flips[0][0], flips[1][0] // n_prj)
+    far_first, near_first = tgt_flips[::-1], tgt_flips
+    flips = [(prj_flips + order, far_first + prj_flips) for order in (far_first, near_first)]
+    neighbours = (prj_flips[0], far_first[0] // n_prj)
     gate_levels = (len(prj_flips) - 1, len(tgt_flips) - 1)
     n_steps = len(tgt_flips) + len(prj_flips)
 
-    def exchanged(step, block, crossed=0):
+    def exchanged(step, block, half=0, crossed=0):
         pairs = []
         for place in range(n_tgt * n_prj):
             for kind in range(2):
-                there = place ^ flips[kind][step]
+                there = place ^ flips[half][kind][step]
                 to_core = kind ^ crossed ^ parity(there)
                 pairs.append((place * n_core + (kind ^ parity(place)), there * n_core + to_core))
         return lax.ppermute(block, DEVICES, pairs)
@@ -389,7 +432,7 @@
         totals = []
         for half, block in enumerate(halves):
             for step in range(1, until):
-                other = exchanged(step, block)
+                other = exchanged(step, block, half)
                 (block,) = run(functools.partial(add_kernel, step, half), [sums], gate, block, other)
             totals.append(block)
         return totals
@@ -429,19 +472,23 @@
     message = exchanged(0, message)
     flags, counts = pair_flags.T, tile_counts.T
     bases = in_hbm(tgt_basis.reshape(2, -1, rows, points), proj_basis)
-    sent, weight = call(
+    pair = in_vmem((2, 2 * rows, points), jnp.bfloat16)
+    *sent, weight = call(
         functools.partial(sent_kernel, neighbours),
         [
-            in_vmem((2, 5 * rows + PIECES, points), jnp.bfloat16),
+            in_vmem((2, 2 * rows + PIECES, points), jnp.bfloat16),
+            pair,
+            in_vmem((2, rows, points), jnp.bfloat16),
             in_vmem((1, 1, points), jnp.float32),
         ],
         [HBM] * 3 + [VMEM],
         [pltpu.VMEM((points,), jnp.float32), pltpu.SemaphoreType.DMA((6,))],
     )(*in_hbm(quad_weight), *bases, chip_amp)
-    mine, gate = call(
+    mine_chip, mine_far, gate = call(
         functools.partial(side_kernel, gate_levels, neighbours),
         [
-            in_vmem((2, 4 * rows, points), jnp.bfloat16),
+            pair,
+            pair,
             in_vmem((n_steps, 2, 1, points), jnp.float32),
         ],
         [HBM] * 4 + [VMEM],
@@ -452,23 +499,25 @@
         ],
         BEHIND,
     )(*in_hbm(flags, counts), *bases, chip_amp)
-    theirs = other_core(sent)
+    theirs_chip, theirs_far, theirs_own = swapped(sent)
+    bases = (mine_chip, mine_far, theirs_chip, theirs_far)
     part, weights = run(
         chip_kernel,
         [in_vmem((2, two_cols, points), jnp.float32), in_vmem((2, 1, points), jnp.float32)],
-        mine,
-        theirs,
+        mine_chip,
+        theirs_chip,
         chip_amp,
         weight,
     )
-    halves = run(first_kernel, [sums] * 2, mine, theirs, gate, weights, part, message)
+    halves = run(first_kernel, [sums] * 2, mine_far, theirs_far, gate, weights, part, message)
     parts = summed(halves, n_steps - 1)
-    low, high = [(other_core(block), exchanged(n_steps - 1, block, 1)) for block in parts]
+    low, high = [
+        (other_core(block), exchanged(n_steps - 1, block, half, 1)) for half, block in enumerate(parts)
+    ]
     (states,) = run(
         low_kernel,
         [in_vmem((4, two_cols, rows), jnp.float32)],
-        mine,
-        theirs,
+        *bases,
         *low,
         chip_amp,
         energies,
@@ -477,8 +526,7 @@
     *halves, my_half, half_send = run(
         second_kernel,
         [sums, sums, segment, segment],
-        mine,
-        theirs,
+        *bases,
         states,
         *high,
         gate,
@@ -490,8 +538,8 @@
     my_part, other_new = run(
         late_kernel,
         [segment, in_vmem((rows, two_cols), jnp.float32)],
-        theirs,
-        sent,
+        theirs_own,
+        sent[0],
         *fields,
         energy,
         amp,
@@ -504,8 +552,8 @@
             jax.ShapeDtypeStruct(tgt_amp.shape, jnp.float32),
             jax.ShapeDtypeStruct(proj_amp.shape, jnp.float32),
         ],
-        mine,
-        theirs,
+        mine_chip,
+        theirs_chip,
         low,
         high,
         my_part,

time: 36.6 us -> 36.8 us (level)
  starting transfers between devices: 16.9 us -> 18.9 us
  waiting for transfers between devices: 11.3 us -> 9.51 us
    ppermute x10 -> x12, starting transfers between devices: 3.18 us -> 4.76 us  [other_core(): return lax.ppermute(block, 'rep', [(0, 1), (1, 0)])]
    ppermute x9, waiting for transfers between devices: 8.94 us -> 7.67 us  [exchanged(): return lax.ppermute(block, DEVICES, pairs)]
    ppermute x10 -> x12, waiting for transfers between devices: 2.34 us -> 1.85 us  [other_core(): return lax.ppermute(block, 'rep', [(0, 1), (1, 0)])]
    ppermute x9, starting transfers between devices: 13.7 us -> 14.1 us  [exchanged(): return lax.ppermute(block, DEVICES, pairs)]
  transfers between devices with their start and end apart: 19 -> 21, of which waited for: 10 -> 9; matrix products, arithmetic and copies ran while one was open for 0% -> 0% of each run, Pallas kernels for 14% -> 16%
where the time goes in v17:
time: 36.8 us; the launch traced here: 36.6 us
  starting transfers between devices  18.9 us (51%)
  waiting for transfers between devices  9.51 us (26%)
  Pallas kernels  7.45 us (20%)
  between operations  0.78 us (2%)
    ppermute x9, starting transfers between devices, exchanged(): return lax.ppermute(block, DEVICES, pairs)  14.1 us
    ppermute x9, waiting for transfers between devices, exchanged(): return lax.ppermute(block, DEVICES, pairs)  7.67 us
    ppermute x12, starting transfers between devices, other_core(): return lax.ppermute(block, 'rep', [(0, 1), (1, 0)])  4.76 us
    pallas_call x13, Pallas kernels, run(): return call(kernel, out_shape, [VMEM] * len(blocks))(*blocks)  3.74 us
    ppermute x12, waiting for transfers between devices, other_core(): return lax.ppermute(block, 'rep', [(0, 1), (1, 0)])  1.85 us
    pallas_call x1, Pallas kernels, shards(): call(functools.partial(sent_kernel, neighbours), [in_vmem((2, 2 * rows +...  1.33 us
    pallas_call x1, Pallas kernels, shards(): call(functools.partial(side_kernel, gate_levels, neighbours), [pair, pair...  1.24 us
    pallas_call x1, Pallas kernels, shards(): call(load_kernel, [in_vmem((2, 1, rows), jnp.float32), in_vmem((2, two_co...  1.14 us
  transfers between devices with their start and end apart: 21, of which 9 were waited for; matrix products, arithmetic and copies ran while one was open for 0% of the time, Pallas kernels for 16%

profile of v17, /device:TPU:0, one launch (start us, length us, event | category | flops | bytes accessed | tf_op | source)
XLA Modules:
  0.0 36.6 jit_solution(9434127938698339827)
XLA Ops:
  0.6 0.5 %collective-permute-start = (f32[256,128]{1,0:T(8,128)}, f32[256,128]{1,0:T(8,128)S(1)}, u32[]{:S(2)}, u32[]{:S(2)}) collective-permute-start(f32[256,128]{1,0:T(8,128)} %tgt_own_hbm.1), channel_id=1, source_target_pairs={{0,1},{1,0},{2,3},{3,2},{4,5},{5,4},{6,7},{7,6},{8,9},{9,8},{10,11... | collective-permute-start | bytes 393224 | tf_op jit(solution)/shard_map/ppermute | solution.py:407
  1.7 1.1 %shard_map.104 = (f32[2,1,256]{2,1,0:T(1,128)S(1)}, f32[2,128,256]{2,1,0:T(8,128)S(1)}) custom-call(f32[256]{0:T(256)} %tgt_energy_hbm.1, f32[1,256]{1,0:T(1,128)} %proj_energy_hbm.1, f32[256,128]{1,0:T(8,128)} %tgt_own_hbm.1, f32[1,256,128]{2,1,0:T(8,128)} %proj_own_hbm.1), custom_call_target="tpu_custom_call" | custom-call | flops 67108864 | bytes 4194304 | tf_op jit(solution)/shard_map/pallas_call | solution.py:447
  3.2 2.7 %collective-permute-start.6 = (bf16[2,144,256]{2,1,0:T(8,128)(2,1)S(1)}, bf16[2,144,256]{2,1,0:T(8,128)(2,1)S(1)}, u32[]{:S(2)}, u32[]{:S(2)}) collective-permute-start(bf16[2,144,256]{2,1,0:T(8,128)(2,1)S(1)} %get-tuple-element.35), channel_id=1, source_target_pairs={{0,3},{1,8},{3,0},{2,11},{5,6},{4,13},{6,5},{7,14},{9,10},{8,1},{1... | collective-permute-start | bytes 442376 | tf_op jit(solution)/shard_map/ppermute | solution.py:425
  5.8 1.3 %shard_map.107 = (bf16[2,528,256]{2,1,0:T(8,128)(2,1)S(1)}, bf16[2,512,256]{2,1,0:T(8,128)(2,1)S(1)}, bf16[2,256,256]{2,1,0:T(8,128)(2,1)S(1)}, f32[1,1,256]{2,1,0:T(1,128)S(1)}) custom-call(f32[256]{0:T(256)} %weight_hbm.1, bf16[2,4,256,256]{3,2,1,0:T(8,128)(2,1)} %bitcast.3, bf16[2,8,256,256]{3,2,1,0:T(8,128)(2,1)} %proj_hbm.3, ...), custom_call_target="tpu_custom_call" | custom-call | tf_op jit(solution)/shard_map/pallas_call | solution.py:476
  7.2 1.5 %collective-permute-start.5 = (bf16[2,512,256]{2,1,0:T(8,128)(2,1)S(1)}, bf16[2,512,256]{2,1,0:T(8,128)(2,1)S(1)}, u32[]{:S(2)}, u32[]{:S(2)}) collective-permute-start(bf16[2,512,256]{2,1,0:T(8,128)(2,1)S(1)} %get-tuple-element.31), channel_id=1, source_target_pairs={{0,1},{1,0},{2,3},{3,2},{4,5},{5,4},{6,7},{7,6},{8,9},{9,8},{10,11... | collective-permute-start | bytes 1572872 | tf_op jit(solution)/shard_map/ppermute | solution.py:407
  8.8 1.2 %shard_map.106 = (bf16[2,512,256]{2,1,0:T(8,128)(2,1)S(1)}, bf16[2,512,256]{2,1,0:T(8,128)(2,1)S(1)}, f32[3,2,1,256]{3,2,1,0:T(1,128)S(1)}) custom-call(s32[2,4]{1,0:T(2,128)} %bitcast.5, s32[2,4]{1,0:T(2,128)} %bitcast.6, bf16[2,4,256,256]{3,2,1,0:T(8,128)(2,1)} %bitcast.4, bf16[2,8,256,256]{3,2,1,0:T(8,128)(2,1)} %proj_hbm.3, ...), custom_call_target="tpu_custom_call" | custom-call | flops 34359738368 | bytes 65536 | tf_op jit(solution)/shard_map/pallas_call | solution.py:487
  10.0 1.0 %collective-permute-done.4.theirs_chip = bf16[2,528,256]{2,1,0:T(8,128)(2,1)S(1)} collective-permute-done((bf16[2,528,256]{2,1,0:T(8,128)(2,1)S(1)}, bf16[2,528,256]{2,1,0:T(8,128)(2,1)S(1)}, u32[]{:S(2)}, u32[]{:S(2)}) %collective-permute-start.4) | collective-permute-done | bytes 540704 | tf_op jit(solution)/shard_map/ppermute | solution.py:407
  11.7 1.5 %collective-permute-start.7 = (bf16[128,256]{1,0:T(8,128)(2,1)S(1)}, bf16[128,256]{1,0:T(8,128)(2,1)S(1)}, u32[]{:S(2)}, u32[]{:S(2)}) collective-permute-start(bf16[128,256]{1,0:T(8,128)(2,1)S(1)} %get-tuple-element.36.own), channel_id=1, source_target_pairs={{0,9},{1,4},{3,10},{2,7},{5,12},{4,1},{6,15},{7,2},{9,0},{8,13},{1... | collective-permute-start | bytes 196616 | tf_op jit(solution)/shard_map/ppermute | solution.py:425
  13.2 1.4 %collective-permute-start.10 = (bf16[128,256]{1,0:T(8,128)(2,1)S(1)}, bf16[128,256]{1,0:T(8,128)(2,1)S(1)}, u32[]{:S(2)}, u32[]{:S(2)}) collective-permute-start(bf16[128,256]{1,0:T(8,128)(2,1)S(1)} %get-tuple-element.38.own), channel_id=1, source_target_pairs={{0,5},{1,4},{3,6},{2,7},{5,0},{4,1},{6,3},{7,2},{9,12},{8,13},{10,... | collective-permute-start | bytes 196616 | tf_op jit(solution)/shard_map/ppermute | solution.py:425
  14.5 1.9 %collective-permute-done.7.other = bf16[128,256]{1,0:T(8,128)(2,1)S(1)} collective-permute-done((bf16[128,256]{1,0:T(8,128)(2,1)S(1)}, bf16[128,256]{1,0:T(8,128)(2,1)S(1)}, u32[]{:S(2)}, u32[]{:S(2)}) %collective-permute-start.7) | collective-permute-done | bytes 65568 | tf_op jit(solution)/shard_map/ppermute | solution.py:425
  16.5 1.0 %collective-permute-start.9 = (bf16[128,256]{1,0:T(8,128)(2,1)S(1)}, bf16[128,256]{1,0:T(8,128)(2,1)S(1)}, u32[]{:S(2)}, u32[]{:S(2)}) collective-permute-start(bf16[128,256]{1,0:T(8,128)(2,1)S(1)} %shard_map.110), channel_id=1, source_target_pairs={{0,4},{1,3},{3,7},{2,0},{5,1},{4,6},{6,2},{7,5},{9,13},{8,10},{10,... | collective-permute-start | bytes 196616 | tf_op jit(solution)/shard_map/ppermute | solution.py:425
  17.9 2.9 %collective-permute-start.12 = (bf16[128,256]{1,0:T(8,128)(2,1)S(1)}, bf16[128,256]{1,0:T(8,128)(2,1)S(1)}, u32[]{:S(2)}, u32[]{:S(2)}) collective-permute-start(bf16[128,256]{1,0:T(8,128)(2,1)S(1)} %shard_map.112), channel_id=1, source_target_pairs={{0,8},{1,3},{3,11},{2,0},{5,13},{4,6},{6,14},{7,5},{9,1},{8,10},{1... | collective-permute-start | bytes 196616 | tf_op jit(solution)/shard_map/ppermute | solution.py:425
  20.8 0.5 %collective-permute-start.19 = (bf16[2,256,256]{2,1,0:T(8,128)(2,1)S(1)}, bf16[2,256,256]{2,1,0:T(8,128)(2,1)S(1)}, u32[]{:S(2)}, u32[]{:S(2)}) collective-permute-start(bf16[2,256,256]{2,1,0:T(8,128)(2,1)S(1)} %get-tuple-element.41), channel_id=1, source_target_pairs={{0,1},{1,0},{2,3},{3,2},{4,5},{5,4},{6,7},{7,6},{8,9},{9,8},{10,11... | collective-permute-start | bytes 786440 | tf_op jit(solution)/shard_map/ppermute | solution.py:407
  21.3 0.5 %shard_map.111.states_ref = f32[4,128,256]{2,1,0:T(8,128)S(1)} custom-call(bf16[2,512,256]{2,1,0:T(8,128)(2,1)S(1)} %get-tuple-element.27.mine_chip, bf16[2,512,256]{2,1,0:T(8,128)(2,1)S(1)} %get-tuple-element.30.mine_far, bf16[2,528,256]{2,1,0:T(8,128)(2,1)S(1)} %collective-permute-done.4.theirs_chip, ...), custom_call_target="tpu_custom_call" | custom-call | tf_op jit(solution)/shard_map/pallas_call | solution.py:404
  21.9 0.9 %collective-permute-done.12.high_there = bf16[128,256]{1,0:T(8,128)(2,1)S(1)} collective-permute-done((bf16[128,256]{1,0:T(8,128)(2,1)S(1)}, bf16[128,256]{1,0:T(8,128)(2,1)S(1)}, u32[]{:S(2)}, u32[]{:S(2)}) %collective-permute-start.12) | collective-permute-done | bytes 65568 | tf_op jit(solution)/shard_map/ppermute | solution.py:425
  22.7 0.8 %shard_map.113 = (bf16[128,256]{1,0:T(8,128)(2,1)S(1)}, bf16[128,256]{1,0:T(8,128)(2,1)S(1)}, f32[128,256]{1,0:T(8,128)S(1)}, f32[128,256]{1,0:T(8,128)S(1)}) custom-call(bf16[2,512,256]{2,1,0:T(8,128)(2,1)S(1)} %get-tuple-element.27.mine_chip, bf16[2,512,256]{2,1,0:T(8,128)(2,1)S(1)} %get-tuple-element.30.mine_far, ...), custom_call_target="tpu_custom_call" | custom-call | tf_op jit(solution)/shard_map/pallas_call | solution.py:404
  23.6 0.9 %collective-permute-start.13 = (bf16[128,256]{1,0:T(8,128)(2,1)S(1)}, bf16[128,256]{1,0:T(8,128)(2,1)S(1)}, u32[]{:S(2)}, u32[]{:S(2)}) collective-permute-start(bf16[128,256]{1,0:T(8,128)(2,1)S(1)} %get-tuple-element.39.own), channel_id=1, source_target_pairs={{0,9},{1,4},{3,10},{2,7},{5,12},{4,1},{6,15},{7,2},{9,0},{8,13},{1... | collective-permute-start | bytes 196616 | tf_op jit(solution)/shard_map/ppermute | solution.py:425
  24.4 1.6 %collective-permute-start.16 = (bf16[128,256]{1,0:T(8,128)(2,1)S(1)}, bf16[128,256]{1,0:T(8,128)(2,1)S(1)}, u32[]{:S(2)}, u32[]{:S(2)}) collective-permute-start(bf16[128,256]{1,0:T(8,128)(2,1)S(1)} %get-tuple-element.40.own), channel_id=1, source_target_pairs={{0,5},{1,4},{3,6},{2,7},{5,0},{4,1},{6,3},{7,2},{9,12},{8,13},{10,... | collective-permute-start | bytes 196616 | tf_op jit(solution)/shard_map/ppermute | solution.py:425
  26.1 3.0 %collective-permute-done.13.other = bf16[128,256]{1,0:T(8,128)(2,1)S(1)} collective-permute-done((bf16[128,256]{1,0:T(8,128)(2,1)S(1)}, bf16[128,256]{1,0:T(8,128)(2,1)S(1)}, u32[]{:S(2)}, u32[]{:S(2)}) %collective-permute-start.13) | collective-permute-done | bytes 65568 | tf_op jit(solution)/shard_map/ppermute | solution.py:425
  29.5 2.1 %collective-permute-start.17 = (bf16[128,256]{1,0:T(8,128)(2,1)S(1)}, bf16[128,256]{1,0:T(8,128)(2,1)S(1)}, u32[]{:S(2)}, u32[]{:S(2)}) collective-permute-start(bf16[128,256]{1,0:T(8,128)(2,1)S(1)} %shard_map.116.own), channel_id=1, source_target_pairs={{0,9},{1,2},{3,10},{2,1},{5,12},{4,7},{6,15},{7,4},{9,0},{8,11},{1... | collective-permute-start | bytes 196616 | tf_op jit(solution)/shard_map/ppermute | solution.py:425
  31.7 1.2 %collective-permute-done.14.other = bf16[128,256]{1,0:T(8,128)(2,1)S(1)} collective-permute-done((bf16[128,256]{1,0:T(8,128)(2,1)S(1)}, bf16[128,256]{1,0:T(8,128)(2,1)S(1)}, u32[]{:S(2)}, u32[]{:S(2)}) %collective-permute-start.14) | collective-permute-done | bytes 65568 | tf_op jit(solution)/shard_map/ppermute | solution.py:425
  32.8 0.9 %collective-permute-start.15 = (bf16[128,256]{1,0:T(8,128)(2,1)S(1)}, bf16[128,256]{1,0:T(8,128)(2,1)S(1)}, u32[]{:S(2)}, u32[]{:S(2)}) collective-permute-start(bf16[128,256]{1,0:T(8,128)(2,1)S(1)} %shard_map.115.low), channel_id=1, source_target_pairs={{0,1},{1,0},{2,3},{3,2},{4,5},{5,4},{6,7},{7,6},{8,9},{9,8},{10,11... | collective-permute-start | bytes 196616 | tf_op jit(solution)/shard_map/ppermute | solution.py:407
  34.8 0.7 %collective-permute-done.18.high = bf16[128,256]{1,0:T(8,128)(2,1)S(1)} collective-permute-done((bf16[128,256]{1,0:T(8,128)(2,1)S(1)}, bf16[128,256]{1,0:T(8,128)(2,1)S(1)}, u32[]{:S(2)}, u32[]{:S(2)}) %collective-permute-start.18) | collective-permute-done | bytes 65568 | tf_op jit(solution)/shard_map/ppermute | solution.py:407
  35.6 1.1 %shard_map.119 = (f32[256,128]{1,0:T(8,128)}, f32[1,256,128]{2,1,0:T(8,128)}) custom-call(bf16[2,512,256]{2,1,0:T(8,128)(2,1)S(1)} %get-tuple-element.27.mine_chip, bf16[2,528,256]{2,1,0:T(8,128)(2,1)S(1)} %collective-permute-done.4.theirs_chip, bf16[128,256]{1,0:T(8,128)(2,1)S(1)} %collective-permute-done.15.low, ...), custom_call_target="tpu_custom_call" | custom-call | tf_op jit(solution)/shard_map/pallas_call | solution.py:404
  (34 shorter events, 3.6 us)
Async XLA Ops:
  0.6 2.4 %collective-permute-start = (f32[256,128]{1,0:T(8,128)}, f32[256,128]{1,0:T(8,128)S(1)}, u32[]{:S(2)}, u32[]{:S(2)}) collective-permute-start(f32[256,128]{1,0:T(8,128)} %tgt_own_hbm.1), channel_id=1, source_target_pairs={{0,1},{1,0},{2,3},{3,2},{4,5},{5,4},{6,7},{7,6},{8,9},{9,8},{10,11... | collective-permute-start | bytes 393224 | tf_op jit(solution)/shard_map/ppermute | solution.py:407
  1.1 1.9 %collective-permute-start.1 = (f32[1,256,128]{2,1,0:T(8,128)}, f32[1,256,128]{2,1,0:T(8,128)S(1)}, u32[]{:S(2)}, u32[]{:S(2)}) collective-permute-start(f32[1,256,128]{2,1,0:T(8,128)} %proj_own_hbm.1), channel_id=1, source_target_pairs={{0,1},{1,0},{2,3},{3,2},{4,5},{5,4},{6,7},{7,6},{8,9},{9,8},{10,11... | collective-permute-start | bytes 393224 | tf_op jit(solution)/shard_map/ppermute | solution.py:407
  1.2 1.7 %collective-permute-start.2 = (f32[256]{0:T(256)}, f32[256]{0:T(256)S(1)}, u32[]{:S(2)}, u32[]{:S(2)}) collective-permute-start(f32[256]{0:T(256)} %tgt_energy_hbm.1), channel_id=1, source_target_pairs={{0,1},{1,0},{2,3},{3,2},{4,5},{5,4},{6,7},{7,6},{8,9},{9,8},{10,11... | collective-permute-start | bytes 3080 | tf_op jit(solution)/shard_map/ppermute | solution.py:407
  1.7 1.4 %collective-permute-start.3 = (f32[1,256]{1,0:T(1,128)}, f32[1,256]{1,0:T(1,128)S(1)}, u32[]{:S(2)}, u32[]{:S(2)}) collective-permute-start(f32[1,256]{1,0:T(1,128)} %proj_energy_hbm.1), channel_id=1, source_target_pairs={{0,1},{1,0},{2,3},{3,2},{4,5},{5,4},{6,7},{7,6},{8,9},{9,8},{10,11... | collective-permute-start | bytes 3080 | tf_op jit(solution)/shard_map/ppermute | solution.py:407
  3.2 8.1 %collective-permute-start.6 = (bf16[2,144,256]{2,1,0:T(8,128)(2,1)S(1)}, bf16[2,144,256]{2,1,0:T(8,128)(2,1)S(1)}, u32[]{:S(2)}, u32[]{:S(2)}) collective-permute-start(bf16[2,144,256]{2,1,0:T(8,128)(2,1)S(1)} %get-tuple-element.35), channel_id=1, source_target_pairs={{0,3},{1,8},{3,0},{2,11},{5,6},{4,13},{6,5},{7,14},{9,10},{8,1},{1... | collective-permute-start | bytes 442376 | tf_op jit(solution)/shard_map/ppermute | solution.py:425
  7.2 4.1 %collective-permute-start.5 = (bf16[2,512,256]{2,1,0:T(8,128)(2,1)S(1)}, bf16[2,512,256]{2,1,0:T(8,128)(2,1)S(1)}, u32[]{:S(2)}, u32[]{:S(2)}) collective-permute-start(bf16[2,512,256]{2,1,0:T(8,128)(2,1)S(1)} %get-tuple-element.31), channel_id=1, source_target_pairs={{0,1},{1,0},{2,3},{3,2},{4,5},{5,4},{6,7},{7,6},{8,9},{9,8},{10,11... | collective-permute-start | bytes 1572872 | tf_op jit(solution)/shard_map/ppermute | solution.py:407
  8.7 2.3 %collective-permute-start.4 = (bf16[2,528,256]{2,1,0:T(8,128)(2,1)S(1)}, bf16[2,528,256]{2,1,0:T(8,128)(2,1)S(1)}, u32[]{:S(2)}, u32[]{:S(2)}) collective-permute-start(bf16[2,528,256]{2,1,0:T(8,128)(2,1)S(1)} %get-tuple-element.28.sent_chip), channel_id=1, source_target_pairs={{0,1},{1,0},{2,3},{3,2},{4,5},{5,4},{6,7},{7,6},{8,9},{9,8},{10,11... | collective-permute-start | bytes 1622024 | tf_op jit(solution)/shard_map/ppermute | solution.py:407
  11.7 4.8 %collective-permute-start.7 = (bf16[128,256]{1,0:T(8,128)(2,1)S(1)}, bf16[128,256]{1,0:T(8,128)(2,1)S(1)}, u32[]{:S(2)}, u32[]{:S(2)}) collective-permute-start(bf16[128,256]{1,0:T(8,128)(2,1)S(1)} %get-tuple-element.36.own), channel_id=1, source_target_pairs={{0,9},{1,4},{3,10},{2,7},{5,12},{4,1},{6,15},{7,2},{9,0},{8,13},{1... | collective-permute-start | bytes 196616 | tf_op jit(solution)/shard_map/ppermute | solution.py:425
  13.2 4.7 %collective-permute-start.10 = (bf16[128,256]{1,0:T(8,128)(2,1)S(1)}, bf16[128,256]{1,0:T(8,128)(2,1)S(1)}, u32[]{:S(2)}, u32[]{:S(2)}) collective-permute-start(bf16[128,256]{1,0:T(8,128)(2,1)S(1)} %get-tuple-element.38.own), channel_id=1, source_target_pairs={{0,5},{1,4},{3,6},{2,7},{5,0},{4,1},{6,3},{7,2},{9,12},{8,13},{10,... | collective-permute-start | bytes 196616 | tf_op jit(solution)/shard_map/ppermute | solution.py:425
  16.5 4.9 %collective-permute-start.9 = (bf16[128,256]{1,0:T(8,128)(2,1)S(1)}, bf16[128,256]{1,0:T(8,128)(2,1)S(1)}, u32[]{:S(2)}, u32[]{:S(2)}) collective-permute-start(bf16[128,256]{1,0:T(8,128)(2,1)S(1)} %shard_map.110), channel_id=1, source_target_pairs={{0,4},{1,3},{3,7},{2,0},{5,1},{4,6},{6,2},{7,5},{9,13},{8,10},{10,... | collective-permute-start | bytes 196616 | tf_op jit(solution)/shard_map/ppermute | solution.py:425
  17.5 3.9 %collective-permute-start.8 = (bf16[128,256]{1,0:T(8,128)(2,1)S(1)}, bf16[128,256]{1,0:T(8,128)(2,1)S(1)}, u32[]{:S(2)}, u32[]{:S(2)}) collective-permute-start(bf16[128,256]{1,0:T(8,128)(2,1)S(1)} %shard_map.110), channel_id=1, source_target_pairs={{0,1},{1,0},{2,3},{3,2},{4,5},{5,4},{6,7},{7,6},{8,9},{9,8},{10,11... | collective-permute-start | bytes 196616 | tf_op jit(solution)/shard_map/ppermute | solution.py:407
  17.9 4.8 %collective-permute-start.12 = (bf16[128,256]{1,0:T(8,128)(2,1)S(1)}, bf16[128,256]{1,0:T(8,128)(2,1)S(1)}, u32[]{:S(2)}, u32[]{:S(2)}) collective-permute-start(bf16[128,256]{1,0:T(8,128)(2,1)S(1)} %shard_map.112), channel_id=1, source_target_pairs={{0,8},{1,3},{3,11},{2,0},{5,13},{4,6},{6,14},{7,5},{9,1},{8,10},{1... | collective-permute-start | bytes 196616 | tf_op jit(solution)/shard_map/ppermute | solution.py:425
  20.8 1.9 %collective-permute-start.11 = (bf16[128,256]{1,0:T(8,128)(2,1)S(1)}, bf16[128,256]{1,0:T(8,128)(2,1)S(1)}, u32[]{:S(2)}, u32[]{:S(2)}) collective-permute-start(bf16[128,256]{1,0:T(8,128)(2,1)S(1)} %shard_map.112), channel_id=1, source_target_pairs={{0,1},{1,0},{2,3},{3,2},{4,5},{5,4},{6,7},{7,6},{8,9},{9,8},{10,11... | collective-permute-start | bytes 196616 | tf_op jit(solution)/shard_map/ppermute | solution.py:407
  20.8 13.6 %collective-permute-start.19 = (bf16[2,256,256]{2,1,0:T(8,128)(2,1)S(1)}, bf16[2,256,256]{2,1,0:T(8,128)(2,1)S(1)}, u32[]{:S(2)}, u32[]{:S(2)}) collective-permute-start(bf16[2,256,256]{2,1,0:T(8,128)(2,1)S(1)} %get-tuple-element.41), channel_id=1, source_target_pairs={{0,1},{1,0},{2,3},{3,2},{4,5},{5,4},{6,7},{7,6},{8,9},{9,8},{10,11... | collective-permute-start | bytes 786440 | tf_op jit(solution)/shard_map/ppermute | solution.py:407
  23.6 5.5 %collective-permute-start.13 = (bf16[128,256]{1,0:T(8,128)(2,1)S(1)}, bf16[128,256]{1,0:T(8,128)(2,1)S(1)}, u32[]{:S(2)}, u32[]{:S(2)}) collective-permute-start(bf16[128,256]{1,0:T(8,128)(2,1)S(1)} %get-tuple-element.39.own), channel_id=1, source_target_pairs={{0,9},{1,4},{3,10},{2,7},{5,12},{4,1},{6,15},{7,2},{9,0},{8,13},{1... | collective-permute-start | bytes 196616 | tf_op jit(solution)/shard_map/ppermute | solution.py:425
  24.4 5.1 %collective-permute-start.16 = (bf16[128,256]{1,0:T(8,128)(2,1)S(1)}, bf16[128,256]{1,0:T(8,128)(2,1)S(1)}, u32[]{:S(2)}, u32[]{:S(2)}) collective-permute-start(bf16[128,256]{1,0:T(8,128)(2,1)S(1)} %get-tuple-element.40.own), channel_id=1, source_target_pairs={{0,5},{1,4},{3,6},{2,7},{5,0},{4,1},{6,3},{7,2},{9,12},{8,13},{10,... | collective-permute-start | bytes 196616 | tf_op jit(solution)/shard_map/ppermute | solution.py:425
  26.1 8.4 %collective-permute-start.20 = (f32[128,256]{1,0:T(8,128)S(1)}, f32[128,256]{1,0:T(8,128)S(1)}, u32[]{:S(2)}, u32[]{:S(2)}) collective-permute-start(f32[128,256]{1,0:T(8,128)S(1)} %get-tuple-element.43), channel_id=1, source_target_pairs={{0,1},{1,0},{2,3},{3,2},{4,5},{5,4},{6,7},{7,6},{8,9},{9,8},{10,11... | collective-permute-start | bytes 393224 | tf_op jit(solution)/shard_map/ppermute | solution.py:407
  29.1 3.8 %collective-permute-start.14 = (bf16[128,256]{1,0:T(8,128)(2,1)S(1)}, bf16[128,256]{1,0:T(8,128)(2,1)S(1)}, u32[]{:S(2)}, u32[]{:S(2)}) collective-permute-start(bf16[128,256]{1,0:T(8,128)(2,1)S(1)} %shard_map.114.own), channel_id=1, source_target_pairs={{0,5},{1,2},{3,6},{2,1},{5,0},{4,7},{6,3},{7,4},{9,12},{8,11},{10,... | collective-permute-start | bytes 196616 | tf_op jit(solution)/shard_map/ppermute | solution.py:425
  29.5 4.7 %collective-permute-start.17 = (bf16[128,256]{1,0:T(8,128)(2,1)S(1)}, bf16[128,256]{1,0:T(8,128)(2,1)S(1)}, u32[]{:S(2)}, u32[]{:S(2)}) collective-permute-start(bf16[128,256]{1,0:T(8,128)(2,1)S(1)} %shard_map.116.own), channel_id=1, source_target_pairs={{0,9},{1,2},{3,10},{2,1},{5,12},{4,7},{6,15},{7,4},{9,0},{8,11},{1... | collective-permute-start | bytes 196616 | tf_op jit(solution)/shard_map/ppermute | solution.py:425
  32.8 2.0 %collective-permute-start.15 = (bf16[128,256]{1,0:T(8,128)(2,1)S(1)}, bf16[128,256]{1,0:T(8,128)(2,1)S(1)}, u32[]{:S(2)}, u32[]{:S(2)}) collective-permute-start(bf16[128,256]{1,0:T(8,128)(2,1)S(1)} %shard_map.115.low), channel_id=1, source_target_pairs={{0,1},{1,0},{2,3},{3,2},{4,5},{5,4},{6,7},{7,6},{8,9},{9,8},{10,11... | collective-permute-start | bytes 196616 | tf_op jit(solution)/shard_map/ppermute | solution.py:407
  34.2 1.3 %collective-permute-start.18 = (bf16[128,256]{1,0:T(8,128)(2,1)S(1)}, bf16[128,256]{1,0:T(8,128)(2,1)S(1)}, u32[]{:S(2)}, u32[]{:S(2)}) collective-permute-start(bf16[128,256]{1,0:T(8,128)(2,1)S(1)} %shard_map.117.high), channel_id=1, source_target_pairs={{0,1},{1,0},{2,3},{3,2},{4,5},{5,4},{6,7},{7,6},{8,9},{9,8},{10,11... | collective-permute-start | bytes 196616 | tf_op jit(solution)/shard_map/ppermute | solution.py:407

commit v18 on v17

--- a/solution.py
+++ b/solution.py
@@ -415,11 +415,11 @@
     gate_levels = (len(prj_flips) - 1, len(tgt_flips) - 1)
     n_steps = len(tgt_flips) + len(prj_flips)
 
-    def exchanged(step, block, half=0, crossed=0):
+    def exchanged(step, block, order=0, crossed=0):
         pairs = []
         for place in range(n_tgt * n_prj):
             for kind in range(2):
-                there = place ^ flips[half][kind][step]
+                there = place ^ flips[order][kind][step]
                 to_core = kind ^ crossed ^ parity(there)
                 pairs.append((place * n_core + (kind ^ parity(place)), there * n_core + to_core))
         return lax.ppermute(block, DEVICES, pairs)
@@ -428,11 +428,11 @@
     sums = in_vmem((two_cols, points), jnp.bfloat16)
     segment = in_vmem((two_cols, rows), jnp.float32)
 
-    def summed(halves, until):
+    def summed(halves, until, orders):
         totals = []
         for half, block in enumerate(halves):
             for step in range(1, until):
-                other = exchanged(step, block, half)
+                other = exchanged(step, block, orders[half])
                 (block,) = run(functools.partial(add_kernel, step, half), [sums], gate, block, other)
             totals.append(block)
         return totals
@@ -510,10 +510,8 @@
         weight,
     )
     halves = run(first_kernel, [sums] * 2, mine_far, theirs_far, gate, weights, part, message)
-    parts = summed(halves, n_steps - 1)
-    low, high = [
-        (other_core(block), exchanged(n_steps - 1, block, half, 1)) for half, block in enumerate(parts)
-    ]
+    parts = summed(halves, n_steps - 1, (0, 0))
+    low, high = [(other_core(block), exchanged(n_steps - 1, block, crossed=1)) for block in parts]
     (states,) = run(
         low_kernel,
         [in_vmem((4, two_cols, rows), jnp.float32)],
@@ -533,7 +531,7 @@
         weights,
     )
     other_half = other_core(half_send)
-    fields = summed(halves, n_steps)
+    fields = summed(halves, n_steps, (0, 1))
     low, high = swapped(fields)
     my_part, other_new = run(
         late_kernel,

time: 36.8 us -> 36.9 us (level)
  starting transfers between devices: 18.9 us -> 17.6 us
  waiting for transfers between devices: 9.51 us -> 10.8 us
    ppermute x9, waiting for transfers between devices: 7.67 us -> 8.91 us  [exchanged(): return lax.ppermute(block, DEVICES, pairs)]
    ppermute x12, starting transfers between devices: 4.76 us -> 3.71 us  [other_core(): return lax.ppermute(block, 'rep', [(0, 1), (1, 0)])]
  transfers between devices with their start and end apart: 21 -> 21, of which waited for: 9 -> 10; matrix products, arithmetic and copies ran while one was open for 0% -> 0% of each run, Pallas kernels for 16% -> 16%
where the time goes in v18:
time: 36.9 us; the launch traced here: 36.7 us
  starting transfers between devices  17.6 us (48%)
  waiting for transfers between devices  10.8 us (29%)
  Pallas kernels  7.44 us (20%)
  between operations  0.8 us (2%)
    ppermute x9, starting transfers between devices, exchanged(): return lax.ppermute(block, DEVICES, pairs)  13.9 us
    ppermute x9, waiting for transfers between devices, exchanged(): return lax.ppermute(block, DEVICES, pairs)  8.91 us
    pallas_call x13, Pallas kernels, run(): return call(kernel, out_shape, [VMEM] * len(blocks))(*blocks)  3.73 us
    ppermute x12, starting transfers between devices, other_core(): return lax.ppermute(block, 'rep', [(0, 1), (1, 0)])  3.71 us
    ppermute x12, waiting for transfers between devices, other_core(): return lax.ppermute(block, 'rep', [(0, 1), (1, 0)])  1.92 us
    pallas_call x1, Pallas kernels, shards(): call(functools.partial(sent_kernel, neighbours), [in_vmem((2, 2 * rows +...  1.33 us
    pallas_call x1, Pallas kernels, shards(): call(functools.partial(side_kernel, gate_levels, neighbours), [pair, pair...  1.24 us
    pallas_call x1, Pallas kernels, shards(): call(load_kernel, [in_vmem((2, 1, rows), jnp.float32), in_vmem((2, two_co...  1.14 us
  transfers between devices with their start and end apart: 21, of which 10 were waited for; matrix products, arithmetic and copies ran while one was open for 0% of the time, Pallas kernels for 16%

profile of v18, /device:TPU:0, one launch (start us, length us, event | category | flops | bytes accessed | tf_op | source)
XLA Modules:
  0.0 36.7 jit_solution(10128769367733741305)
XLA Ops:
  0.6 0.5 %collective-permute-start = (f32[256,128]{1,0:T(8,128)}, f32[256,128]{1,0:T(8,128)S(1)}, u32[]{:S(2)}, u32[]{:S(2)}) collective-permute-start(f32[256,128]{1,0:T(8,128)} %tgt_own_hbm.1), channel_id=1, source_target_pairs={{0,1},{1,0},{2,3},{3,2},{4,5},{5,4},{6,7},{7,6},{8,9},{9,8},{10,11... | collective-permute-start | bytes 393224 | tf_op jit(solution)/shard_map/ppermute | solution.py:407
  1.7 1.1 %shard_map.104 = (f32[2,1,256]{2,1,0:T(1,128)S(1)}, f32[2,128,256]{2,1,0:T(8,128)S(1)}) custom-call(f32[256]{0:T(256)} %tgt_energy_hbm.1, f32[1,256]{1,0:T(1,128)} %proj_energy_hbm.1, f32[256,128]{1,0:T(8,128)} %tgt_own_hbm.1, f32[1,256,128]{2,1,0:T(8,128)} %proj_own_hbm.1), custom_call_target="tpu_custom_call" | custom-call | flops 67108864 | bytes 4194304 | tf_op jit(solution)/shard_map/pallas_call | solution.py:447
  3.2 2.7 %collective-permute-start.6 = (bf16[2,144,256]{2,1,0:T(8,128)(2,1)S(1)}, bf16[2,144,256]{2,1,0:T(8,128)(2,1)S(1)}, u32[]{:S(2)}, u32[]{:S(2)}) collective-permute-start(bf16[2,144,256]{2,1,0:T(8,128)(2,1)S(1)} %get-tuple-element.35), channel_id=1, source_target_pairs={{0,3},{1,8},{3,0},{2,11},{5,6},{4,13},{6,5},{7,14},{9,10},{8,1},{1... | collective-permute-start | bytes 442376 | tf_op jit(solution)/shard_map/ppermute | solution.py:425
  5.8 1.3 %shard_map.107 = (bf16[2,528,256]{2,1,0:T(8,128)(2,1)S(1)}, bf16[2,512,256]{2,1,0:T(8,128)(2,1)S(1)}, bf16[2,256,256]{2,1,0:T(8,128)(2,1)S(1)}, f32[1,1,256]{2,1,0:T(1,128)S(1)}) custom-call(f32[256]{0:T(256)} %weight_hbm.1, bf16[2,4,256,256]{3,2,1,0:T(8,128)(2,1)} %bitcast.3, bf16[2,8,256,256]{3,2,1,0:T(8,128)(2,1)} %proj_hbm.3, ...), custom_call_target="tpu_custom_call" | custom-call | tf_op jit(solution)/shard_map/pallas_call | solution.py:476
  7.2 1.5 %collective-permute-start.5 = (bf16[2,512,256]{2,1,0:T(8,128)(2,1)S(1)}, bf16[2,512,256]{2,1,0:T(8,128)(2,1)S(1)}, u32[]{:S(2)}, u32[]{:S(2)}) collective-permute-start(bf16[2,512,256]{2,1,0:T(8,128)(2,1)S(1)} %get-tuple-element.31), channel_id=1, source_target_pairs={{0,1},{1,0},{2,3},{3,2},{4,5},{5,4},{6,7},{7,6},{8,9},{9,8},{10,11... | collective-permute-start | bytes 1572872 | tf_op jit(solution)/shard_map/ppermute | solution.py:407
  8.8 1.2 %shard_map.106 = (bf16[2,512,256]{2,1,0:T(8,128)(2,1)S(1)}, bf16[2,512,256]{2,1,0:T(8,128)(2,1)S(1)}, f32[3,2,1,256]{3,2,1,0:T(1,128)S(1)}) custom-call(s32[2,4]{1,0:T(2,128)} %bitcast.5, s32[2,4]{1,0:T(2,128)} %bitcast.6, bf16[2,4,256,256]{3,2,1,0:T(8,128)(2,1)} %bitcast.4, bf16[2,8,256,256]{3,2,1,0:T(8,128)(2,1)} %proj_hbm.3, ...), custom_call_target="tpu_custom_call" | custom-call | flops 34359738368 | bytes 65536 | tf_op jit(solution)/shard_map/pallas_call | solution.py:487
  10.0 1.0 %collective-permute-done.4.theirs_chip = bf16[2,528,256]{2,1,0:T(8,128)(2,1)S(1)} collective-permute-done((bf16[2,528,256]{2,1,0:T(8,128)(2,1)S(1)}, bf16[2,528,256]{2,1,0:T(8,128)(2,1)S(1)}, u32[]{:S(2)}, u32[]{:S(2)}) %collective-permute-start.4) | collective-permute-done | bytes 540704 | tf_op jit(solution)/shard_map/ppermute | solution.py:407
  11.7 1.5 %collective-permute-start.7 = (bf16[128,256]{1,0:T(8,128)(2,1)S(1)}, bf16[128,256]{1,0:T(8,128)(2,1)S(1)}, u32[]{:S(2)}, u32[]{:S(2)}) collective-permute-start(bf16[128,256]{1,0:T(8,128)(2,1)S(1)} %get-tuple-element.36.own), channel_id=1, source_target_pairs={{0,9},{1,4},{3,10},{2,7},{5,12},{4,1},{6,15},{7,2},{9,0},{8,13},{1... | collective-permute-start | bytes 196616 | tf_op jit(solution)/shard_map/ppermute | solution.py:425
  13.2 1.2 %collective-permute-start.10 = (bf16[128,256]{1,0:T(8,128)(2,1)S(1)}, bf16[128,256]{1,0:T(8,128)(2,1)S(1)}, u32[]{:S(2)}, u32[]{:S(2)}) collective-permute-start(bf16[128,256]{1,0:T(8,128)(2,1)S(1)} %get-tuple-element.38.own), channel_id=1, source_target_pairs={{0,9},{1,4},{3,10},{2,7},{5,12},{4,1},{6,15},{7,2},{9,0},{8,13},{1... | collective-permute-start | bytes 196616 | tf_op jit(solution)/shard_map/ppermute | solution.py:425
  14.4 2.1 %collective-permute-done.7.other = bf16[128,256]{1,0:T(8,128)(2,1)S(1)} collective-permute-done((bf16[128,256]{1,0:T(8,128)(2,1)S(1)}, bf16[128,256]{1,0:T(8,128)(2,1)S(1)}, u32[]{:S(2)}, u32[]{:S(2)}) %collective-permute-start.7) | collective-permute-done | bytes 65568 | tf_op jit(solution)/shard_map/ppermute | solution.py:425
  16.5 1.0 %collective-permute-start.9 = (bf16[128,256]{1,0:T(8,128)(2,1)S(1)}, bf16[128,256]{1,0:T(8,128)(2,1)S(1)}, u32[]{:S(2)}, u32[]{:S(2)}) collective-permute-start(bf16[128,256]{1,0:T(8,128)(2,1)S(1)} %shard_map.110), channel_id=1, source_target_pairs={{0,4},{1,3},{3,7},{2,0},{5,1},{4,6},{6,2},{7,5},{9,13},{8,10},{10,... | collective-permute-start | bytes 196616 | tf_op jit(solution)/shard_map/ppermute | solution.py:425
  17.8 0.6 %collective-permute-done.10.other = bf16[128,256]{1,0:T(8,128)(2,1)S(1)} collective-permute-done((bf16[128,256]{1,0:T(8,128)(2,1)S(1)}, bf16[128,256]{1,0:T(8,128)(2,1)S(1)}, u32[]{:S(2)}, u32[]{:S(2)}) %collective-permute-start.10) | collective-permute-done | bytes 65568 | tf_op jit(solution)/shard_map/ppermute | solution.py:425
  18.4 1.4 %collective-permute-start.12 = (bf16[128,256]{1,0:T(8,128)(2,1)S(1)}, bf16[128,256]{1,0:T(8,128)(2,1)S(1)}, u32[]{:S(2)}, u32[]{:S(2)}) collective-permute-start(bf16[128,256]{1,0:T(8,128)(2,1)S(1)} %shard_map.112), channel_id=1, source_target_pairs={{0,4},{1,3},{3,7},{2,0},{5,1},{4,6},{6,2},{7,5},{9,13},{8,10},{10,... | collective-permute-start | bytes 196616 | tf_op jit(solution)/shard_map/ppermute | solution.py:425
  20.8 0.5 %shard_map.111.states_ref = f32[4,128,256]{2,1,0:T(8,128)S(1)} custom-call(bf16[2,512,256]{2,1,0:T(8,128)(2,1)S(1)} %get-tuple-element.27.mine_chip, bf16[2,512,256]{2,1,0:T(8,128)(2,1)S(1)} %get-tuple-element.30.mine_far, bf16[2,528,256]{2,1,0:T(8,128)(2,1)S(1)} %collective-permute-done.4.theirs_chip, ...), custom_call_target="tpu_custom_call" | custom-call | tf_op jit(solution)/shard_map/pallas_call | solution.py:404
  21.3 1.4 %collective-permute-done.12.high_there = bf16[128,256]{1,0:T(8,128)(2,1)S(1)} collective-permute-done((bf16[128,256]{1,0:T(8,128)(2,1)S(1)}, bf16[128,256]{1,0:T(8,128)(2,1)S(1)}, u32[]{:S(2)}, u32[]{:S(2)}) %collective-permute-start.12) | collective-permute-done | bytes 65568 | tf_op jit(solution)/shard_map/ppermute | solution.py:425
  22.7 0.8 %shard_map.113 = (bf16[128,256]{1,0:T(8,128)(2,1)S(1)}, bf16[128,256]{1,0:T(8,128)(2,1)S(1)}, f32[128,256]{1,0:T(8,128)S(1)}, f32[128,256]{1,0:T(8,128)S(1)}) custom-call(bf16[2,512,256]{2,1,0:T(8,128)(2,1)S(1)} %get-tuple-element.27.mine_chip, bf16[2,512,256]{2,1,0:T(8,128)(2,1)S(1)} %get-tuple-element.30.mine_far, ...), custom_call_target="tpu_custom_call" | custom-call | tf_op jit(solution)/shard_map/pallas_call | solution.py:404
  24.0 2.6 %collective-permute-start.16 = (bf16[128,256]{1,0:T(8,128)(2,1)S(1)}, bf16[128,256]{1,0:T(8,128)(2,1)S(1)}, u32[]{:S(2)}, u32[]{:S(2)}) collective-permute-start(bf16[128,256]{1,0:T(8,128)(2,1)S(1)} %get-tuple-element.40.own), channel_id=1, source_target_pairs={{0,5},{1,4},{3,6},{2,7},{5,0},{4,1},{6,3},{7,2},{9,12},{8,13},{10,... | collective-permute-start | bytes 196616 | tf_op jit(solution)/shard_map/ppermute | solution.py:425
  26.5 1.8 %collective-permute-done.13.other = bf16[128,256]{1,0:T(8,128)(2,1)S(1)} collective-permute-done((bf16[128,256]{1,0:T(8,128)(2,1)S(1)}, bf16[128,256]{1,0:T(8,128)(2,1)S(1)}, u32[]{:S(2)}, u32[]{:S(2)}) %collective-permute-start.13) | collective-permute-done | bytes 65568 | tf_op jit(solution)/shard_map/ppermute | solution.py:425
  28.3 1.3 %collective-permute-start.14 = (bf16[128,256]{1,0:T(8,128)(2,1)S(1)}, bf16[128,256]{1,0:T(8,128)(2,1)S(1)}, u32[]{:S(2)}, u32[]{:S(2)}) collective-permute-start(bf16[128,256]{1,0:T(8,128)(2,1)S(1)} %shard_map.114.own), channel_id=1, source_target_pairs={{0,5},{1,2},{3,6},{2,1},{5,0},{4,7},{6,3},{7,4},{9,12},{8,11},{10,... | collective-permute-start | bytes 196616 | tf_op jit(solution)/shard_map/ppermute | solution.py:425
  29.6 1.9 %collective-permute-start.17 = (bf16[128,256]{1,0:T(8,128)(2,1)S(1)}, bf16[128,256]{1,0:T(8,128)(2,1)S(1)}, u32[]{:S(2)}, u32[]{:S(2)}) collective-permute-start(bf16[128,256]{1,0:T(8,128)(2,1)S(1)} %shard_map.116.own), channel_id=1, source_target_pairs={{0,9},{1,2},{3,10},{2,1},{5,12},{4,7},{6,15},{7,4},{9,0},{8,11},{1... | collective-permute-start | bytes 196616 | tf_op jit(solution)/shard_map/ppermute | solution.py:425
  31.5 0.5 %collective-permute-done.14.other = bf16[128,256]{1,0:T(8,128)(2,1)S(1)} collective-permute-done((bf16[128,256]{1,0:T(8,128)(2,1)S(1)}, bf16[128,256]{1,0:T(8,128)(2,1)S(1)}, u32[]{:S(2)}, u32[]{:S(2)}) %collective-permute-start.14) | collective-permute-done | bytes 65568 | tf_op jit(solution)/shard_map/ppermute | solution.py:425
  32.2 2.1 %collective-permute-done.17.other = bf16[128,256]{1,0:T(8,128)(2,1)S(1)} collective-permute-done((bf16[128,256]{1,0:T(8,128)(2,1)S(1)}, bf16[128,256]{1,0:T(8,128)(2,1)S(1)}, u32[]{:S(2)}, u32[]{:S(2)}) %collective-permute-start.17) | collective-permute-done | bytes 65568 | tf_op jit(solution)/shard_map/ppermute | solution.py:425
  34.8 0.8 %collective-permute-done.18.high = bf16[128,256]{1,0:T(8,128)(2,1)S(1)} collective-permute-done((bf16[128,256]{1,0:T(8,128)(2,1)S(1)}, bf16[128,256]{1,0:T(8,128)(2,1)S(1)}, u32[]{:S(2)}, u32[]{:S(2)}) %collective-permute-start.18) | collective-permute-done | bytes 65568 | tf_op jit(solution)/shard_map/ppermute | solution.py:407
  35.6 1.1 %shard_map.119 = (f32[256,128]{1,0:T(8,128)}, f32[1,256,128]{2,1,0:T(8,128)}) custom-call(bf16[2,512,256]{2,1,0:T(8,128)(2,1)S(1)} %get-tuple-element.27.mine_chip, bf16[2,528,256]{2,1,0:T(8,128)(2,1)S(1)} %collective-permute-done.4.theirs_chip, bf16[128,256]{1,0:T(8,128)(2,1)S(1)} %collective-permute-done.15.low, ...), custom_call_target="tpu_custom_call" | custom-call | tf_op jit(solution)/shard_map/pallas_call | solution.py:404
  (34 shorter events, 4.0 us)
Async XLA Ops:
  0.6 2.4 %collective-permute-start = (f32[256,128]{1,0:T(8,128)}, f32[256,128]{1,0:T(8,128)S(1)}, u32[]{:S(2)}, u32[]{:S(2)}) collective-permute-start(f32[256,128]{1,0:T(8,128)} %tgt_own_hbm.1), channel_id=1, source_target_pairs={{0,1},{1,0},{2,3},{3,2},{4,5},{5,4},{6,7},{7,6},{8,9},{9,8},{10,11... | collective-permute-start | bytes 393224 | tf_op jit(solution)/shard_map/ppermute | solution.py:407
  1.1 1.9 %collective-permute-start.1 = (f32[1,256,128]{2,1,0:T(8,128)}, f32[1,256,128]{2,1,0:T(8,128)S(1)}, u32[]{:S(2)}, u32[]{:S(2)}) collective-permute-start(f32[1,256,128]{2,1,0:T(8,128)} %proj_own_hbm.1), channel_id=1, source_target_pairs={{0,1},{1,0},{2,3},{3,2},{4,5},{5,4},{6,7},{7,6},{8,9},{9,8},{10,11... | collective-permute-start | bytes 393224 | tf_op jit(solution)/shard_map/ppermute | solution.py:407
  1.2 1.7 %collective-permute-start.2 = (f32[256]{0:T(256)}, f32[256]{0:T(256)S(1)}, u32[]{:S(2)}, u32[]{:S(2)}) collective-permute-start(f32[256]{0:T(256)} %tgt_energy_hbm.1), channel_id=1, source_target_pairs={{0,1},{1,0},{2,3},{3,2},{4,5},{5,4},{6,7},{7,6},{8,9},{9,8},{10,11... | collective-permute-start | bytes 3080 | tf_op jit(solution)/shard_map/ppermute | solution.py:407
  1.7 1.4 %collective-permute-start.3 = (f32[1,256]{1,0:T(1,128)}, f32[1,256]{1,0:T(1,128)S(1)}, u32[]{:S(2)}, u32[]{:S(2)}) collective-permute-start(f32[1,256]{1,0:T(1,128)} %proj_energy_hbm.1), channel_id=1, source_target_pairs={{0,1},{1,0},{2,3},{3,2},{4,5},{5,4},{6,7},{7,6},{8,9},{9,8},{10,11... | collective-permute-start | bytes 3080 | tf_op jit(solution)/shard_map/ppermute | solution.py:407
  3.2 8.1 %collective-permute-start.6 = (bf16[2,144,256]{2,1,0:T(8,128)(2,1)S(1)}, bf16[2,144,256]{2,1,0:T(8,128)(2,1)S(1)}, u32[]{:S(2)}, u32[]{:S(2)}) collective-permute-start(bf16[2,144,256]{2,1,0:T(8,128)(2,1)S(1)} %get-tuple-element.35), channel_id=1, source_target_pairs={{0,3},{1,8},{3,0},{2,11},{5,6},{4,13},{6,5},{7,14},{9,10},{8,1},{1... | collective-permute-start | bytes 442376 | tf_op jit(solution)/shard_map/ppermute | solution.py:425
  7.2 4.1 %collective-permute-start.5 = (bf16[2,512,256]{2,1,0:T(8,128)(2,1)S(1)}, bf16[2,512,256]{2,1,0:T(8,128)(2,1)S(1)}, u32[]{:S(2)}, u32[]{:S(2)}) collective-permute-start(bf16[2,512,256]{2,1,0:T(8,128)(2,1)S(1)} %get-tuple-element.31), channel_id=1, source_target_pairs={{0,1},{1,0},{2,3},{3,2},{4,5},{5,4},{6,7},{7,6},{8,9},{9,8},{10,11... | collective-permute-start | bytes 1572872 | tf_op jit(solution)/shard_map/ppermute | solution.py:407
  8.7 2.3 %collective-permute-start.4 = (bf16[2,528,256]{2,1,0:T(8,128)(2,1)S(1)}, bf16[2,528,256]{2,1,0:T(8,128)(2,1)S(1)}, u32[]{:S(2)}, u32[]{:S(2)}) collective-permute-start(bf16[2,528,256]{2,1,0:T(8,128)(2,1)S(1)} %get-tuple-element.28.sent_chip), channel_id=1, source_target_pairs={{0,1},{1,0},{2,3},{3,2},{4,5},{5,4},{6,7},{7,6},{8,9},{9,8},{10,11... | collective-permute-start | bytes 1622024 | tf_op jit(solution)/shard_map/ppermute | solution.py:407
  11.7 4.8 %collective-permute-start.7 = (bf16[128,256]{1,0:T(8,128)(2,1)S(1)}, bf16[128,256]{1,0:T(8,128)(2,1)S(1)}, u32[]{:S(2)}, u32[]{:S(2)}) collective-permute-start(bf16[128,256]{1,0:T(8,128)(2,1)S(1)} %get-tuple-element.36.own), channel_id=1, source_target_pairs={{0,9},{1,4},{3,10},{2,7},{5,12},{4,1},{6,15},{7,2},{9,0},{8,13},{1... | collective-permute-start | bytes 196616 | tf_op jit(solution)/shard_map/ppermute | solution.py:425
  13.2 5.2 %collective-permute-start.10 = (bf16[128,256]{1,0:T(8,128)(2,1)S(1)}, bf16[128,256]{1,0:T(8,128)(2,1)S(1)}, u32[]{:S(2)}, u32[]{:S(2)}) collective-permute-start(bf16[128,256]{1,0:T(8,128)(2,1)S(1)} %get-tuple-element.38.own), channel_id=1, source_target_pairs={{0,9},{1,4},{3,10},{2,7},{5,12},{4,1},{6,15},{7,2},{9,0},{8,13},{1... | collective-permute-start | bytes 196616 | tf_op jit(solution)/shard_map/ppermute | solution.py:425
  16.5 4.3 %collective-permute-start.9 = (bf16[128,256]{1,0:T(8,128)(2,1)S(1)}, bf16[128,256]{1,0:T(8,128)(2,1)S(1)}, u32[]{:S(2)}, u32[]{:S(2)}) collective-permute-start(bf16[128,256]{1,0:T(8,128)(2,1)S(1)} %shard_map.110), channel_id=1, source_target_pairs={{0,4},{1,3},{3,7},{2,0},{5,1},{4,6},{6,2},{7,5},{9,13},{8,10},{10,... | collective-permute-start | bytes 196616 | tf_op jit(solution)/shard_map/ppermute | solution.py:425
  17.5 3.3 %collective-permute-start.8 = (bf16[128,256]{1,0:T(8,128)(2,1)S(1)}, bf16[128,256]{1,0:T(8,128)(2,1)S(1)}, u32[]{:S(2)}, u32[]{:S(2)}) collective-permute-start(bf16[128,256]{1,0:T(8,128)(2,1)S(1)} %shard_map.110), channel_id=1, source_target_pairs={{0,1},{1,0},{2,3},{3,2},{4,5},{5,4},{6,7},{7,6},{8,9},{9,8},{10,11... | collective-permute-start | bytes 196616 | tf_op jit(solution)/shard_map/ppermute | solution.py:407
  18.4 4.3 %collective-permute-start.12 = (bf16[128,256]{1,0:T(8,128)(2,1)S(1)}, bf16[128,256]{1,0:T(8,128)(2,1)S(1)}, u32[]{:S(2)}, u32[]{:S(2)}) collective-permute-start(bf16[128,256]{1,0:T(8,128)(2,1)S(1)} %shard_map.112), channel_id=1, source_target_pairs={{0,4},{1,3},{3,7},{2,0},{5,1},{4,6},{6,2},{7,5},{9,13},{8,10},{10,... | collective-permute-start | bytes 196616 | tf_op jit(solution)/shard_map/ppermute | solution.py:425
  19.8 2.9 %collective-permute-start.11 = (bf16[128,256]{1,0:T(8,128)(2,1)S(1)}, bf16[128,256]{1,0:T(8,128)(2,1)S(1)}, u32[]{:S(2)}, u32[]{:S(2)}) collective-permute-start(bf16[128,256]{1,0:T(8,128)(2,1)S(1)} %shard_map.112), channel_id=1, source_target_pairs={{0,1},{1,0},{2,3},{3,2},{4,5},{5,4},{6,7},{7,6},{8,9},{9,8},{10,11... | collective-permute-start | bytes 196616 | tf_op jit(solution)/shard_map/ppermute | solution.py:407
  19.9 14.5 %collective-permute-start.19 = (bf16[2,256,256]{2,1,0:T(8,128)(2,1)S(1)}, bf16[2,256,256]{2,1,0:T(8,128)(2,1)S(1)}, u32[]{:S(2)}, u32[]{:S(2)}) collective-permute-start(bf16[2,256,256]{2,1,0:T(8,128)(2,1)S(1)} %get-tuple-element.41), channel_id=1, source_target_pairs={{0,1},{1,0},{2,3},{3,2},{4,5},{5,4},{6,7},{7,6},{8,9},{9,8},{10,11... | collective-permute-start | bytes 786440 | tf_op jit(solution)/shard_map/ppermute | solution.py:407
  23.5 4.8 %collective-permute-start.13 = (bf16[128,256]{1,0:T(8,128)(2,1)S(1)}, bf16[128,256]{1,0:T(8,128)(2,1)S(1)}, u32[]{:S(2)}, u32[]{:S(2)}) collective-permute-start(bf16[128,256]{1,0:T(8,128)(2,1)S(1)} %get-tuple-element.39.own), channel_id=1, source_target_pairs={{0,9},{1,4},{3,10},{2,7},{5,12},{4,1},{6,15},{7,2},{9,0},{8,13},{1... | collective-permute-start | bytes 196616 | tf_op jit(solution)/shard_map/ppermute | solution.py:425
  24.0 5.6 %collective-permute-start.16 = (bf16[128,256]{1,0:T(8,128)(2,1)S(1)}, bf16[128,256]{1,0:T(8,128)(2,1)S(1)}, u32[]{:S(2)}, u32[]{:S(2)}) collective-permute-start(bf16[128,256]{1,0:T(8,128)(2,1)S(1)} %get-tuple-element.40.own), channel_id=1, source_target_pairs={{0,5},{1,4},{3,6},{2,7},{5,0},{4,1},{6,3},{7,2},{9,12},{8,13},{10,... | collective-permute-start | bytes 196616 | tf_op jit(solution)/shard_map/ppermute | solution.py:425
  26.5 7.9 %collective-permute-start.20 = (f32[128,256]{1,0:T(8,128)S(1)}, f32[128,256]{1,0:T(8,128)S(1)}, u32[]{:S(2)}, u32[]{:S(2)}) collective-permute-start(f32[128,256]{1,0:T(8,128)S(1)} %get-tuple-element.43), channel_id=1, source_target_pairs={{0,1},{1,0},{2,3},{3,2},{4,5},{5,4},{6,7},{7,6},{8,9},{9,8},{10,11... | collective-permute-start | bytes 393224 | tf_op jit(solution)/shard_map/ppermute | solution.py:407
  28.3 3.8 %collective-permute-start.14 = (bf16[128,256]{1,0:T(8,128)(2,1)S(1)}, bf16[128,256]{1,0:T(8,128)(2,1)S(1)}, u32[]{:S(2)}, u32[]{:S(2)}) collective-permute-start(bf16[128,256]{1,0:T(8,128)(2,1)S(1)} %shard_map.114.own), channel_id=1, source_target_pairs={{0,5},{1,2},{3,6},{2,1},{5,0},{4,7},{6,3},{7,4},{9,12},{8,11},{10,... | collective-permute-start | bytes 196616 | tf_op jit(solution)/shard_map/ppermute | solution.py:425
  29.6 4.7 %collective-permute-start.17 = (bf16[128,256]{1,0:T(8,128)(2,1)S(1)}, bf16[128,256]{1,0:T(8,128)(2,1)S(1)}, u32[]{:S(2)}, u32[]{:S(2)}) collective-permute-start(bf16[128,256]{1,0:T(8,128)(2,1)S(1)} %shard_map.116.own), channel_id=1, source_target_pairs={{0,9},{1,2},{3,10},{2,1},{5,12},{4,7},{6,15},{7,4},{9,0},{8,11},{1... | collective-permute-start | bytes 196616 | tf_op jit(solution)/shard_map/ppermute | solution.py:425
  32.1 2.7 %collective-permute-start.15 = (bf16[128,256]{1,0:T(8,128)(2,1)S(1)}, bf16[128,256]{1,0:T(8,128)(2,1)S(1)}, u32[]{:S(2)}, u32[]{:S(2)}) collective-permute-start(bf16[128,256]{1,0:T(8,128)(2,1)S(1)} %shard_map.115.low), channel_id=1, source_target_pairs={{0,1},{1,0},{2,3},{3,2},{4,5},{5,4},{6,7},{7,6},{8,9},{9,8},{10,11... | collective-permute-start | bytes 196616 | tf_op jit(solution)/shard_map/ppermute | solution.py:407
  34.3 1.3 %collective-permute-start.18 = (bf16[128,256]{1,0:T(8,128)(2,1)S(1)}, bf16[128,256]{1,0:T(8,128)(2,1)S(1)}, u32[]{:S(2)}, u32[]{:S(2)}) collective-permute-start(bf16[128,256]{1,0:T(8,128)(2,1)S(1)} %shard_map.117.high), channel_id=1, source_target_pairs={{0,1},{1,0},{2,3},{3,2},{4,5},{5,4},{6,7},{7,6},{8,9},{9,8},{10,11... | collective-permute-start | bytes 196616 | tf_op jit(solution)/shard_map/ppermute | solution.py:407

commit v19 on v18

--- a/solution.py
+++ b/solution.py
@@ -77,6 +77,7 @@
 PIECES = 16
 
 BEHIND = pl.CostEstimate(flops=1 << 35, bytes_accessed=1 << 16, transcendentals=0)
+EVEN = pl.CostEstimate(flops=1 << 30, bytes_accessed=1 << 16, transcendentals=0)
 
 
 def split(row):
@@ -227,20 +228,15 @@
 
     for copy in copies:
         copy.wait()
-    tiles = 2
+    tiles = 4
     width = gate.shape[-1] // tiles
     gate_level = jnp.where(my == 0, *gate_levels)
-    for half in range(2):
-        for tile in range(tiles):
-            live = jnp.logical_and(
-                flags[prj_index, tgt_index] > 0, tiles * half + tile < counts[prj_index, tgt_index]
-            )
-            value = jnp.where(live, 1.0, 0.0).astype(jnp.float32)
-            for level in range(gate.shape[0]):
-                here = jnp.where(level == gate_level, value, jnp.float32(1.0))
-                gate[level, half, :, tile * width : (tile + 1) * width] = jnp.full(
-                    (1, width), here, jnp.float32
-                )
+    for tile in range(tiles):
+        live = jnp.logical_and(flags[prj_index, tgt_index] > 0, tile < counts[prj_index, tgt_index])
+        value = jnp.where(live, 1.0, 0.0).astype(jnp.float32)
+        for level in range(gate.shape[0]):
+            here = jnp.where(level == gate_level, value, jnp.float32(1.0))
+            gate[level, :, tile * width : (tile + 1) * width] = jnp.full((1, width), here, jnp.float32)
     for copy in basis_copies((mine_chip, mine_far), sems, 0, neighbours, sources):
         copy.wait()
 
@@ -260,33 +256,54 @@
     by_core(body)
 
 
-def first_kernel(mine_far, theirs_far, gate, weights, part_ref, message, *outs):
+def store(sums, gate, weights, long_ref, short_ref):
+    points = weights.shape[-1]
+    first, second = [
+        bf16(gate[0, :, half * points : (half + 1) * points] * (weights[half] * total))
+        for half, total in enumerate(sums)
+    ]
+    extra = long_ref.shape[1] - points
+    long_ref[:, :points] = first
+    long_ref[:, points:] = second[:, :extra]
+    short_ref[...] = second[:, extra:]
+
+
+def halves_of(long, short):
+    points = (long.shape[1] + short.shape[1]) // 2
+    return long[:, :points], jnp.concatenate([long[:, points:], short], axis=1)
+
+
+def first_kernel(mine_far, theirs_far, gate, weights, part_ref, message, long_ref, short_ref):
     mine, theirs = (None, mine_far), (None, theirs_far)
     rows = message.shape[2]
     cols = part_ref.shape[1]
 
     def body(core):
-        for half, basis in enumerate((mine, theirs) if core == 0 else (theirs, mine)):
-            total = part_ref[half] + sum(
+        sums = [
+            part_ref[half]
+            + sum(
                 project(rows_of(basis, 2 + segment, rows), f32(message[segment, :cols]))
                 for segment in range(2)
             )
-            outs[half][...] = bf16(gate[0, half] * (weights[half] * total))
+            for half, basis in enumerate((mine, theirs) if core == 0 else (theirs, mine))
+        ]
+        store(sums, gate, weights, long_ref, short_ref)
 
     by_core(body)
 
 
-def add_kernel(level, half, gate, own, other, out_ref):
-    out_ref[...] = bf16(gate[level, half] * (f32(own[...]) + f32(other[...])))
-
-
-def low_kernel(
+def add_kernel(level, first_point, gate, own, other, out_ref):
+    points = slice(first_point, first_point + out_ref.shape[1])
+    out_ref[...] = bf16(gate[level, :, points] * (f32(own[...]) + f32(other[...])))
+
+
+def early_kernel(
     mine_chip,
     mine_far,
     theirs_chip,
     theirs_far,
-    low,
-    low_there,
+    field,
+    field_there,
     chip_amp,
     energies,
     message,
@@ -294,7 +311,8 @@
 ):
     mine, theirs = (mine_chip, mine_far), (theirs_chip, theirs_far)
     _, cols, rows = chip_amp.shape
-    field = bf16(f32(low[...]) + f32(low_there[...]))
+    points = mine_chip.shape[2]
+    low = bf16(f32(field[:, :points]) + f32(field_there[:, :points]))
 
     def body(core):
         for segment in range(4):
@@ -302,7 +320,7 @@
                 amp, energy = chip_amp[segment], energies[segment]
             else:
                 amp, energy = f32(message[segment - 2, :cols]), joined(message[segment - 2, cols:])
-            change = expand(rows_of((mine, theirs)[core], segment, rows), field)
+            change = expand(rows_of((mine, theirs)[core], segment, rows), low)
             states_ref[segment] = amp + half_step * (energy * turned(amp) + change)
 
     by_core(body)
@@ -314,44 +332,53 @@
     theirs_chip,
     theirs_far,
     states_ref,
-    high,
-    high_there,
+    field,
+    field_there,
+    short,
+    short_there,
     gate,
     weights,
-    low_ref,
-    high_ref,
+    long_ref,
+    short_ref,
     half_ref,
     send_ref,
 ):
     mine, theirs = (mine_chip, mine_far), (theirs_chip, theirs_far)
     rows = states_ref.shape[2]
-    field = bf16(f32(high[...]) + f32(high_there[...]))
+    points = mine_chip.shape[2]
+    high = bf16(
+        jnp.concatenate(
+            [f32(field[:, points:]) + f32(field_there[:, points:]), f32(short[...]) + f32(short_there[...])],
+            axis=1,
+        )
+    )
 
     def body(core):
         bases = (mine, theirs) if core == 0 else (theirs, mine)
         halves = [
-            states_ref[segment] + half_step * expand(rows_of(bases[1], segment, rows), field)
+            states_ref[segment] + half_step * expand(rows_of(bases[1], segment, rows), high)
             for segment in range(4)
         ]
         half_ref[...] = halves[core]
         send_ref[...] = halves[1 - core]
-        for half, out_ref in enumerate((low_ref, high_ref)):
-            total = sum(
-                project(rows_of(bases[half], segment, rows), halves[segment]) for segment in range(4)
-            )
-            out_ref[...] = bf16(gate[0, half] * (weights[half] * total))
+        sums = [
+            sum(project(rows_of(basis, segment, rows), halves[segment]) for segment in range(4))
+            for basis in bases
+        ]
+        store(sums, gate, weights, long_ref, short_ref)
 
     by_core(body)
 
 
-def late_kernel(theirs_own, sent_chip, low, high, energy, amp_ref, my_half, other_half, my_part, other_new):
+def late_kernel(theirs_own, sent_chip, long, short, energy, amp_ref, my_half, other_half, my_part, other_new):
     rows = amp_ref.shape[2]
 
     def body(core):
         my = my_kind()
+        low, high = halves_of(long[...], short[...])
         near, far = (low, high) if core == 0 else (high, low)
-        change = expand(rows_of((sent_chip,), core, rows), near[...]) + expand(
-            rows_of((theirs_own,), 0, rows), far[...]
+        change = expand(rows_of((sent_chip,), core, rows), near) + expand(
+            rows_of((theirs_own,), 0, rows), far
         )
         rate = energy[1 - my] * turned(other_half[...]) + change
         other_new[...] = (amp_ref[1 - my] + time_step * rate).T
@@ -360,13 +387,14 @@
     by_core(body)
 
 
-def last_kernel(mine_chip, theirs_chip, low, high, my_part, other_new, new_tgt, new_proj):
+def last_kernel(mine_chip, theirs_chip, long, short, my_part, other_new, new_tgt, new_proj):
     rows = my_part.shape[1]
 
     def body(core):
+        low, high = halves_of(long[...], short[...])
         near, far = (low, high) if core == 0 else (high, low)
-        change = expand(rows_of((mine_chip,), core, rows), near[...]) + expand(
-            rows_of((theirs_chip,), core, rows), far[...]
+        change = expand(rows_of((mine_chip,), core, rows), near) + expand(
+            rows_of((theirs_chip,), core, rows), far
         )
         my_new = (my_part[...] + time_step * change).T
         new_tgt[...], new_proj[0] = ordered(my_kind(), my_new, other_new[...])
@@ -409,32 +437,37 @@
     n_tgt, n_prj, n_core = sizes
     tgt_flips = [n_prj << bit for bit in range(n_tgt.bit_length() - 1)]
     prj_flips = [1 << bit for bit in range(n_prj.bit_length() - 1)]
-    far_first, near_first = tgt_flips[::-1], tgt_flips
-    flips = [(prj_flips + order, far_first + prj_flips) for order in (far_first, near_first)]
+    far_first = tgt_flips[::-1]
+    flips = (prj_flips + far_first, far_first + prj_flips)
     neighbours = (prj_flips[0], far_first[0] // n_prj)
     gate_levels = (len(prj_flips) - 1, len(tgt_flips) - 1)
     n_steps = len(tgt_flips) + len(prj_flips)
 
-    def exchanged(step, block, order=0, crossed=0):
+    def exchanged(step, block, crossed=0):
         pairs = []
         for place in range(n_tgt * n_prj):
             for kind in range(2):
-                there = place ^ flips[order][kind][step]
+                there = place ^ flips[kind][step]
                 to_core = kind ^ crossed ^ parity(there)
                 pairs.append((place * n_core + (kind ^ parity(place)), there * n_core + to_core))
         return lax.ppermute(block, DEVICES, pairs)
 
     in_vmem = pltpu.VMEM
-    sums = in_vmem((two_cols, points), jnp.bfloat16)
+    blocks = [in_vmem((two_cols, size), jnp.bfloat16) for size in (3 * points // 2, points // 2)]
     segment = in_vmem((two_cols, rows), jnp.float32)
 
-    def summed(halves, until, orders):
+    def summed(blocks, until):
         totals = []
-        for half, block in enumerate(halves):
+        first_point = 0
+        for block in blocks:
             for step in range(1, until):
-                other = exchanged(step, block, orders[half])
-                (block,) = run(functools.partial(add_kernel, step, half), [sums], gate, block, other)
+                other = exchanged(step, block)
+                kernel = functools.partial(add_kernel, step, first_point)
+                shape = in_vmem(block.shape, block.dtype)
+                cost = EVEN if first_point else None
+                (block,) = call(kernel, [shape], [VMEM] * 3, cost=cost)(gate, block, other)
             totals.append(block)
+            first_point += block.shape[1]
         return totals
 
     def swapped(fields):
@@ -489,7 +522,7 @@
         [
             pair,
             pair,
-            in_vmem((n_steps, 2, 1, points), jnp.float32),
+            in_vmem((n_steps, 1, 2 * points), jnp.float32),
         ],
         [HBM] * 4 + [VMEM],
         [
@@ -509,30 +542,30 @@
         chip_amp,
         weight,
     )
-    halves = run(first_kernel, [sums] * 2, mine_far, theirs_far, gate, weights, part, message)
-    parts = summed(halves, n_steps - 1, (0, 0))
-    low, high = [(other_core(block), exchanged(n_steps - 1, block, crossed=1)) for block in parts]
+    sums = run(first_kernel, blocks, mine_far, theirs_far, gate, weights, part, message)
+    parts = summed(sums, n_steps - 1)
+    long, short = [(other_core(block), exchanged(n_steps - 1, block, crossed=1)) for block in parts]
     (states,) = run(
-        low_kernel,
+        early_kernel,
         [in_vmem((4, two_cols, rows), jnp.float32)],
         *bases,
-        *low,
+        *long,
         chip_amp,
         energies,
         message,
     )
-    *halves, my_half, half_send = run(
+    *sums, my_half, half_send = run(
         second_kernel,
-        [sums, sums, segment, segment],
+        blocks + [segment, segment],
         *bases,
         states,
-        *high,
+        *long,
+        *short,
         gate,
         weights,
     )
     other_half = other_core(half_send)
-    fields = summed(halves, n_steps, (0, 1))
-    low, high = swapped(fields)
+    fields = summed(sums, n_steps)
     my_part, other_new = run(
         late_kernel,
         [segment, in_vmem((rows, two_cols), jnp.float32)],
@@ -552,8 +585,7 @@
         ],
         mine_chip,
         theirs_chip,
-        low,
-        high,
+        *swapped(fields),
         my_part,
         other_new,
     )

time: 36.9 us -> 38.8 us (1.051)
  waiting for transfers between devices: 10.8 us -> 12.9 us
    ppermute x9, waiting for transfers between devices: 8.91 us -> 12 us  [exchanged(): return lax.ppermute(block, DEVICES, pairs)]
    ppermute x12, waiting for transfers between devices: 1.92 us -> 0.91 us  [other_core(): return lax.ppermute(block, 'rep', [(0, 1), (1, 0)])]
    ppermute x9, starting transfers between devices: 13.9 us -> 13.3 us  [exchanged(): return lax.ppermute(block, DEVICES, pairs)]
    ppermute x12, starting transfers between devices: 3.71 us -> 4.1 us  [other_core(): return lax.ppermute(block, 'rep', [(0, 1), (1, 0)])]
    pallas_call x13 -> x7, Pallas kernels: 3.73 us -> 3.57 us  [run(): return call(kernel, out_shape, [VMEM] * len(blocks))(*blocks)]
  transfers between devices with their start and end apart: 21 -> 21, of which waited for: 10 -> 9; matrix products, arithmetic and copies ran while one was open for 0% -> 0% of each run, Pallas kernels for 16% -> 10%
where the time goes in v19:
time: 38.8 us; the launch traced here: 38.6 us
  starting transfers between devices  17.4 us (45%)
  waiting for transfers between devices  12.9 us (33%)
  Pallas kernels  7.44 us (19%)
  between operations  0.79 us (2%)
    ppermute x9, starting transfers between devices, exchanged(): return lax.ppermute(block, DEVICES, pairs)  13.3 us
    ppermute x9, waiting for transfers between devices, exchanged(): return lax.ppermute(block, DEVICES, pairs)  12 us
    ppermute x12, starting transfers between devices, other_core(): return lax.ppermute(block, 'rep', [(0, 1), (1, 0)])  4.1 us
    pallas_call x7, Pallas kernels, run(): return call(kernel, out_shape, [VMEM] * len(blocks))(*blocks)  3.57 us
    pallas_call x1, Pallas kernels, shards(): call(functools.partial(sent_kernel, neighbours), [in_vmem((2, 2 * rows +...  1.34 us
    pallas_call x1, Pallas kernels, shards(): call(functools.partial(side_kernel, gate_levels, neighbours), [pair, pair...  1.24 us
    pallas_call x1, Pallas kernels, shards(): call(load_kernel, [in_vmem((2, 1, rows), jnp.float32), in_vmem((2, two_co...  1.14 us
    ppermute x12, waiting for transfers between devices, other_core(): return lax.ppermute(block, 'rep', [(0, 1), (1, 0)])  0.91 us
  transfers between devices with their start and end apart: 21, of which 9 were waited for; matrix products, arithmetic and copies ran while one was open for 0% of the time, Pallas kernels for 10%

profile of v19, /device:TPU:0, one launch (start us, length us, event | category | flops | bytes accessed | tf_op | source)
XLA Modules:
  0.0 38.6 jit_solution(14372258651459280034)
XLA Ops:
  0.6 0.5 %collective-permute-start = (f32[256,128]{1,0:T(8,128)}, f32[256,128]{1,0:T(8,128)S(1)}, u32[]{:S(2)}, u32[]{:S(2)}) collective-permute-start(f32[256,128]{1,0:T(8,128)} %tgt_own_hbm.1), channel_id=1, source_target_pairs={{0,1},{1,0},{2,3},{3,2},{4,5},{5,4},{6,7},{7,6},{8,9},{9,8},{10,11... | collective-permute-start | bytes 393224 | tf_op jit(solution)/shard_map/ppermute | solution.py:435
  1.7 1.1 %shard_map.104 = (f32[2,1,256]{2,1,0:T(1,128)S(1)}, f32[2,128,256]{2,1,0:T(8,128)S(1)}) custom-call(f32[256]{0:T(256)} %tgt_energy_hbm.1, f32[1,256]{1,0:T(1,128)} %proj_energy_hbm.1, f32[256,128]{1,0:T(8,128)} %tgt_own_hbm.1, f32[1,256,128]{2,1,0:T(8,128)} %proj_own_hbm.1), custom_call_target="tpu_custom_call" | custom-call | flops 67108864 | bytes 4194304 | tf_op jit(solution)/shard_map/pallas_call | solution.py:480
  3.2 1.3 %shard_map.107 = (bf16[2,528,256]{2,1,0:T(8,128)(2,1)S(1)}, bf16[2,512,256]{2,1,0:T(8,128)(2,1)S(1)}, bf16[2,256,256]{2,1,0:T(8,128)(2,1)S(1)}, f32[1,1,256]{2,1,0:T(1,128)S(1)}) custom-call(f32[256]{0:T(256)} %weight_hbm.1, bf16[2,4,256,256]{3,2,1,0:T(8,128)(2,1)} %bitcast.3, bf16[2,8,256,256]{3,2,1,0:T(8,128)(2,1)} %proj_hbm.3, ...), custom_call_target="tpu_custom_call" | custom-call | tf_op jit(solution)/shard_map/pallas_call | solution.py:509
  5.1 2.6 %collective-permute-start.6 = (bf16[2,144,256]{2,1,0:T(8,128)(2,1)S(1)}, bf16[2,144,256]{2,1,0:T(8,128)(2,1)S(1)}, u32[]{:S(2)}, u32[]{:S(2)}) collective-permute-start(bf16[2,144,256]{2,1,0:T(8,128)(2,1)S(1)} %get-tuple-element.35), channel_id=1, source_target_pairs={{0,3},{1,8},{3,0},{2,11},{5,6},{4,13},{6,5},{7,14},{9,10},{8,1},{1... | collective-permute-start | bytes 442376 | tf_op jit(solution)/shard_map/ppermute | solution.py:453
  7.7 1.2 %shard_map.106 = (bf16[2,512,256]{2,1,0:T(8,128)(2,1)S(1)}, bf16[2,512,256]{2,1,0:T(8,128)(2,1)S(1)}, f32[3,1,512]{2,1,0:T(1,128)S(1)}) custom-call(s32[2,4]{1,0:T(2,128)} %bitcast.5, s32[2,4]{1,0:T(2,128)} %bitcast.6, bf16[2,4,256,256]{3,2,1,0:T(8,128)(2,1)} %bitcast.4, bf16[2,8,256,256]{3,2,1,0:T(8,128)(2,1)} %proj_hbm.3, ...), custom_call_target="tpu_custom_call" | custom-call | flops 34359738368 | bytes 65536 | tf_op jit(solution)/shard_map/pallas_call | solution.py:520
  9.3 1.2 %collective-permute-done.6.message = bf16[2,144,256]{2,1,0:T(8,128)(2,1)S(1)} collective-permute-done((bf16[2,144,256]{2,1,0:T(8,128)(2,1)S(1)}, bf16[2,144,256]{2,1,0:T(8,128)(2,1)S(1)}, u32[]{:S(2)}, u32[]{:S(2)}) %collective-permute-start.6) | collective-permute-done | bytes 147488 | tf_op jit(solution)/shard_map/ppermute | solution.py:453
  10.8 3.2 %collective-permute-start.7 = (bf16[128,384]{1,0:T(8,128)(2,1)S(1)}, bf16[128,384]{1,0:T(8,128)(2,1)S(1)}, u32[]{:S(2)}, u32[]{:S(2)}) collective-permute-start(bf16[128,384]{1,0:T(8,128)(2,1)S(1)} %get-tuple-element.36.own), channel_id=1, source_target_pairs={{0,9},{1,4},{3,10},{2,7},{5,12},{4,1},{6,15},{7,2},{9,0},{8,13},{1... | collective-permute-start | bytes 294920 | tf_op jit(solution)/shard_map/ppermute | solution.py:453
  14.1 3.1 %collective-permute-done.7.other = bf16[128,384]{1,0:T(8,128)(2,1)S(1)} collective-permute-done((bf16[128,384]{1,0:T(8,128)(2,1)S(1)}, bf16[128,384]{1,0:T(8,128)(2,1)S(1)}, u32[]{:S(2)}, u32[]{:S(2)}) %collective-permute-start.7) | collective-permute-done | bytes 98336 | tf_op jit(solution)/shard_map/ppermute | solution.py:453
  17.3 1.3 %collective-permute-start.8 = (bf16[128,384]{1,0:T(8,128)(2,1)S(1)}, bf16[128,384]{1,0:T(8,128)(2,1)S(1)}, u32[]{:S(2)}, u32[]{:S(2)}) collective-permute-start(bf16[128,384]{1,0:T(8,128)(2,1)S(1)} %shard_map.110), channel_id=1, source_target_pairs={{0,1},{1,0},{2,3},{3,2},{4,5},{5,4},{6,7},{7,6},{8,9},{9,8},{10,11... | collective-permute-start | bytes 294920 | tf_op jit(solution)/shard_map/ppermute | solution.py:435
  18.5 1.2 %collective-permute-start.9 = (bf16[128,384]{1,0:T(8,128)(2,1)S(1)}, bf16[128,384]{1,0:T(8,128)(2,1)S(1)}, u32[]{:S(2)}, u32[]{:S(2)}) collective-permute-start(bf16[128,384]{1,0:T(8,128)(2,1)S(1)} %shard_map.110), channel_id=1, source_target_pairs={{0,4},{1,3},{3,7},{2,0},{5,1},{4,6},{6,2},{7,5},{9,13},{8,10},{10,... | collective-permute-start | bytes 294920 | tf_op jit(solution)/shard_map/ppermute | solution.py:453
  19.7 1.0 %collective-permute-start.11 = (bf16[128,128]{1,0:T(8,128)(2,1)S(1)}, bf16[128,128]{1,0:T(8,128)(2,1)S(1)}, u32[]{:S(2)}, u32[]{:S(2)}) collective-permute-start(bf16[128,128]{1,0:T(8,128)(2,1)S(1)} %shard_map.112), channel_id=1, source_target_pairs={{0,1},{1,0},{2,3},{3,2},{4,5},{5,4},{6,7},{7,6},{8,9},{9,8},{10,11... | collective-permute-start | bytes 98312 | tf_op jit(solution)/shard_map/ppermute | solution.py:435
  21.0 2.2 %collective-permute-done.9.field_there = bf16[128,384]{1,0:T(8,128)(2,1)S(1)} collective-permute-done((bf16[128,384]{1,0:T(8,128)(2,1)S(1)}, bf16[128,384]{1,0:T(8,128)(2,1)S(1)}, u32[]{:S(2)}, u32[]{:S(2)}) %collective-permute-start.9) | collective-permute-done | bytes 98336 | tf_op jit(solution)/shard_map/ppermute | solution.py:453
  23.2 0.5 %shard_map.111.states_ref = f32[4,128,256]{2,1,0:T(8,128)S(1)} custom-call(bf16[2,512,256]{2,1,0:T(8,128)(2,1)S(1)} %get-tuple-element.27.mine_chip, bf16[2,512,256]{2,1,0:T(8,128)(2,1)S(1)} %get-tuple-element.30.mine_far, bf16[2,528,256]{2,1,0:T(8,128)(2,1)S(1)} %collective-permute-done.4.theirs_chip, ...), custom_call_target="tpu_custom_call" | custom-call | tf_op jit(solution)/shard_map/pallas_call | solution.py:432
  23.7 1.0 %collective-permute-done.12.short_there = bf16[128,128]{1,0:T(8,128)(2,1)S(1)} collective-permute-done((bf16[128,128]{1,0:T(8,128)(2,1)S(1)}, bf16[128,128]{1,0:T(8,128)(2,1)S(1)}, u32[]{:S(2)}, u32[]{:S(2)}) %collective-permute-start.12) | collective-permute-done | bytes 32800 | tf_op jit(solution)/shard_map/ppermute | solution.py:453
  24.7 0.8 %shard_map.113 = (bf16[128,384]{1,0:T(8,128)(2,1)S(1)}, bf16[128,128]{1,0:T(8,128)(2,1)S(1)}, f32[128,256]{1,0:T(8,128)S(1)}, f32[128,256]{1,0:T(8,128)S(1)}) custom-call(bf16[2,512,256]{2,1,0:T(8,128)(2,1)S(1)} %get-tuple-element.27.mine_chip, bf16[2,512,256]{2,1,0:T(8,128)(2,1)S(1)} %get-tuple-element.30.mine_far, ...), custom_call_target="tpu_custom_call" | custom-call | tf_op jit(solution)/shard_map/pallas_call | solution.py:432
  25.5 1.7 %collective-permute-start.13 = (bf16[128,384]{1,0:T(8,128)(2,1)S(1)}, bf16[128,384]{1,0:T(8,128)(2,1)S(1)}, u32[]{:S(2)}, u32[]{:S(2)}) collective-permute-start(bf16[128,384]{1,0:T(8,128)(2,1)S(1)} %get-tuple-element.39.own), channel_id=1, source_target_pairs={{0,9},{1,4},{3,10},{2,7},{5,12},{4,1},{6,15},{7,2},{9,0},{8,13},{1... | collective-permute-start | bytes 294920 | tf_op jit(solution)/shard_map/ppermute | solution.py:453
  27.2 1.0 %collective-permute-start.16 = (bf16[128,128]{1,0:T(8,128)(2,1)S(1)}, bf16[128,128]{1,0:T(8,128)(2,1)S(1)}, u32[]{:S(2)}, u32[]{:S(2)}) collective-permute-start(bf16[128,128]{1,0:T(8,128)(2,1)S(1)} %get-tuple-element.40.own), channel_id=1, source_target_pairs={{0,9},{1,4},{3,10},{2,7},{5,12},{4,1},{6,15},{7,2},{9,0},{8,13},{1... | collective-permute-start | bytes 98312 | tf_op jit(solution)/shard_map/ppermute | solution.py:453
  28.2 2.3 %collective-permute-done.13.other = bf16[128,384]{1,0:T(8,128)(2,1)S(1)} collective-permute-done((bf16[128,384]{1,0:T(8,128)(2,1)S(1)}, bf16[128,384]{1,0:T(8,128)(2,1)S(1)}, u32[]{:S(2)}, u32[]{:S(2)}) %collective-permute-start.13) | collective-permute-done | bytes 98336 | tf_op jit(solution)/shard_map/ppermute | solution.py:453
  30.5 2.3 %collective-permute-start.14 = (bf16[128,384]{1,0:T(8,128)(2,1)S(1)}, bf16[128,384]{1,0:T(8,128)(2,1)S(1)}, u32[]{:S(2)}, u32[]{:S(2)}) collective-permute-start(bf16[128,384]{1,0:T(8,128)(2,1)S(1)} %shard_map.114.own), channel_id=1, source_target_pairs={{0,5},{1,2},{3,6},{2,1},{5,0},{4,7},{6,3},{7,4},{9,12},{8,11},{10,... | collective-permute-start | bytes 294920 | tf_op jit(solution)/shard_map/ppermute | solution.py:453
  32.8 1.1 %collective-permute-start.17 = (bf16[128,128]{1,0:T(8,128)(2,1)S(1)}, bf16[128,128]{1,0:T(8,128)(2,1)S(1)}, u32[]{:S(2)}, u32[]{:S(2)}) collective-permute-start(bf16[128,128]{1,0:T(8,128)(2,1)S(1)} %shard_map.116.own), channel_id=1, source_target_pairs={{0,5},{1,2},{3,6},{2,1},{5,0},{4,7},{6,3},{7,4},{9,12},{8,11},{10,... | collective-permute-start | bytes 98312 | tf_op jit(solution)/shard_map/ppermute | solution.py:453
  33.9 1.2 %collective-permute-done.14.other = bf16[128,384]{1,0:T(8,128)(2,1)S(1)} collective-permute-done((bf16[128,384]{1,0:T(8,128)(2,1)S(1)}, bf16[128,384]{1,0:T(8,128)(2,1)S(1)}, u32[]{:S(2)}, u32[]{:S(2)}) %collective-permute-start.14) | collective-permute-done | bytes 98336 | tf_op jit(solution)/shard_map/ppermute | solution.py:453
  35.2 1.0 %collective-permute-done.17.other = bf16[128,128]{1,0:T(8,128)(2,1)S(1)} collective-permute-done((bf16[128,128]{1,0:T(8,128)(2,1)S(1)}, bf16[128,128]{1,0:T(8,128)(2,1)S(1)}, u32[]{:S(2)}, u32[]{:S(2)}) %collective-permute-start.17) | collective-permute-done | bytes 32800 | tf_op jit(solution)/shard_map/ppermute | solution.py:453
  36.7 0.8 %collective-permute-done.18.short = bf16[128,128]{1,0:T(8,128)(2,1)S(1)} collective-permute-done((bf16[128,128]{1,0:T(8,128)(2,1)S(1)}, bf16[128,128]{1,0:T(8,128)(2,1)S(1)}, u32[]{:S(2)}, u32[]{:S(2)}) %collective-permute-start.18) | collective-permute-done | bytes 32800 | tf_op jit(solution)/shard_map/ppermute | solution.py:435
  37.5 1.1 %shard_map.119 = (f32[256,128]{1,0:T(8,128)}, f32[1,256,128]{2,1,0:T(8,128)}) custom-call(bf16[2,512,256]{2,1,0:T(8,128)(2,1)S(1)} %get-tuple-element.27.mine_chip, bf16[2,528,256]{2,1,0:T(8,128)(2,1)S(1)} %collective-permute-done.4.theirs_chip, bf16[128,384]{1,0:T(8,128)(2,1)S(1)} %collective-permute-done.15.long, ...), custom_call_target="tpu_custom_call" | custom-call | tf_op jit(solution)/shard_map/pallas_call | solution.py:432
  (34 shorter events, 3.1 us)
Async XLA Ops:
  0.6 2.4 %collective-permute-start = (f32[256,128]{1,0:T(8,128)}, f32[256,128]{1,0:T(8,128)S(1)}, u32[]{:S(2)}, u32[]{:S(2)}) collective-permute-start(f32[256,128]{1,0:T(8,128)} %tgt_own_hbm.1), channel_id=1, source_target_pairs={{0,1},{1,0},{2,3},{3,2},{4,5},{5,4},{6,7},{7,6},{8,9},{9,8},{10,11... | collective-permute-start | bytes 393224 | tf_op jit(solution)/shard_map/ppermute | solution.py:435
  1.1 1.9 %collective-permute-start.1 = (f32[1,256,128]{2,1,0:T(8,128)}, f32[1,256,128]{2,1,0:T(8,128)S(1)}, u32[]{:S(2)}, u32[]{:S(2)}) collective-permute-start(f32[1,256,128]{2,1,0:T(8,128)} %proj_own_hbm.1), channel_id=1, source_target_pairs={{0,1},{1,0},{2,3},{3,2},{4,5},{5,4},{6,7},{7,6},{8,9},{9,8},{10,11... | collective-permute-start | bytes 393224 | tf_op jit(solution)/shard_map/ppermute | solution.py:435
  1.2 1.7 %collective-permute-start.2 = (f32[256]{0:T(256)}, f32[256]{0:T(256)S(1)}, u32[]{:S(2)}, u32[]{:S(2)}) collective-permute-start(f32[256]{0:T(256)} %tgt_energy_hbm.1), channel_id=1, source_target_pairs={{0,1},{1,0},{2,3},{3,2},{4,5},{5,4},{6,7},{7,6},{8,9},{9,8},{10,11... | collective-permute-start | bytes 3080 | tf_op jit(solution)/shard_map/ppermute | solution.py:435
  1.7 1.4 %collective-permute-start.3 = (f32[1,256]{1,0:T(1,128)}, f32[1,256]{1,0:T(1,128)S(1)}, u32[]{:S(2)}, u32[]{:S(2)}) collective-permute-start(f32[1,256]{1,0:T(1,128)} %proj_energy_hbm.1), channel_id=1, source_target_pairs={{0,1},{1,0},{2,3},{3,2},{4,5},{5,4},{6,7},{7,6},{8,9},{9,8},{10,11... | collective-permute-start | bytes 3080 | tf_op jit(solution)/shard_map/ppermute | solution.py:435
  4.5 4.4 %collective-permute-start.4 = (bf16[2,528,256]{2,1,0:T(8,128)(2,1)S(1)}, bf16[2,528,256]{2,1,0:T(8,128)(2,1)S(1)}, u32[]{:S(2)}, u32[]{:S(2)}) collective-permute-start(bf16[2,528,256]{2,1,0:T(8,128)(2,1)S(1)} %get-tuple-element.28.sent_chip), channel_id=1, source_target_pairs={{0,1},{1,0},{2,3},{3,2},{4,5},{5,4},{6,7},{7,6},{8,9},{9,8},{10,11... | collective-permute-start | bytes 1622024 | tf_op jit(solution)/shard_map/ppermute | solution.py:435
  4.9 5.6 %collective-permute-start.5 = (bf16[2,512,256]{2,1,0:T(8,128)(2,1)S(1)}, bf16[2,512,256]{2,1,0:T(8,128)(2,1)S(1)}, u32[]{:S(2)}, u32[]{:S(2)}) collective-permute-start(bf16[2,512,256]{2,1,0:T(8,128)(2,1)S(1)} %get-tuple-element.31), channel_id=1, source_target_pairs={{0,1},{1,0},{2,3},{3,2},{4,5},{5,4},{6,7},{7,6},{8,9},{9,8},{10,11... | collective-permute-start | bytes 1572872 | tf_op jit(solution)/shard_map/ppermute | solution.py:435
  5.1 5.4 %collective-permute-start.6 = (bf16[2,144,256]{2,1,0:T(8,128)(2,1)S(1)}, bf16[2,144,256]{2,1,0:T(8,128)(2,1)S(1)}, u32[]{:S(2)}, u32[]{:S(2)}) collective-permute-start(bf16[2,144,256]{2,1,0:T(8,128)(2,1)S(1)} %get-tuple-element.35), channel_id=1, source_target_pairs={{0,3},{1,8},{3,0},{2,11},{5,6},{4,13},{6,5},{7,14},{9,10},{8,1},{1... | collective-permute-start | bytes 442376 | tf_op jit(solution)/shard_map/ppermute | solution.py:453
  10.8 6.4 %collective-permute-start.7 = (bf16[128,384]{1,0:T(8,128)(2,1)S(1)}, bf16[128,384]{1,0:T(8,128)(2,1)S(1)}, u32[]{:S(2)}, u32[]{:S(2)}) collective-permute-start(bf16[128,384]{1,0:T(8,128)(2,1)S(1)} %get-tuple-element.36.own), channel_id=1, source_target_pairs={{0,9},{1,4},{3,10},{2,7},{5,12},{4,1},{6,15},{7,2},{9,0},{8,13},{1... | collective-permute-start | bytes 294920 | tf_op jit(solution)/shard_map/ppermute | solution.py:453
  14.0 5.7 %collective-permute-start.10 = (bf16[128,128]{1,0:T(8,128)(2,1)S(1)}, bf16[128,128]{1,0:T(8,128)(2,1)S(1)}, u32[]{:S(2)}, u32[]{:S(2)}) collective-permute-start(bf16[128,128]{1,0:T(8,128)(2,1)S(1)} %get-tuple-element.38.own), channel_id=1, source_target_pairs={{0,9},{1,4},{3,10},{2,7},{5,12},{4,1},{6,15},{7,2},{9,0},{8,13},{1... | collective-permute-start | bytes 98312 | tf_op jit(solution)/shard_map/ppermute | solution.py:453
  17.3 3.7 %collective-permute-start.8 = (bf16[128,384]{1,0:T(8,128)(2,1)S(1)}, bf16[128,384]{1,0:T(8,128)(2,1)S(1)}, u32[]{:S(2)}, u32[]{:S(2)}) collective-permute-start(bf16[128,384]{1,0:T(8,128)(2,1)S(1)} %shard_map.110), channel_id=1, source_target_pairs={{0,1},{1,0},{2,3},{3,2},{4,5},{5,4},{6,7},{7,6},{8,9},{9,8},{10,11... | collective-permute-start | bytes 294920 | tf_op jit(solution)/shard_map/ppermute | solution.py:435
  18.5 4.6 %collective-permute-start.9 = (bf16[128,384]{1,0:T(8,128)(2,1)S(1)}, bf16[128,384]{1,0:T(8,128)(2,1)S(1)}, u32[]{:S(2)}, u32[]{:S(2)}) collective-permute-start(bf16[128,384]{1,0:T(8,128)(2,1)S(1)} %shard_map.110), channel_id=1, source_target_pairs={{0,4},{1,3},{3,7},{2,0},{5,1},{4,6},{6,2},{7,5},{9,13},{8,10},{10,... | collective-permute-start | bytes 294920 | tf_op jit(solution)/shard_map/ppermute | solution.py:453
  19.7 3.9 %collective-permute-start.11 = (bf16[128,128]{1,0:T(8,128)(2,1)S(1)}, bf16[128,128]{1,0:T(8,128)(2,1)S(1)}, u32[]{:S(2)}, u32[]{:S(2)}) collective-permute-start(bf16[128,128]{1,0:T(8,128)(2,1)S(1)} %shard_map.112), channel_id=1, source_target_pairs={{0,1},{1,0},{2,3},{3,2},{4,5},{5,4},{6,7},{7,6},{8,9},{9,8},{10,11... | collective-permute-start | bytes 98312 | tf_op jit(solution)/shard_map/ppermute | solution.py:435
  20.7 3.9 %collective-permute-start.12 = (bf16[128,128]{1,0:T(8,128)(2,1)S(1)}, bf16[128,128]{1,0:T(8,128)(2,1)S(1)}, u32[]{:S(2)}, u32[]{:S(2)}) collective-permute-start(bf16[128,128]{1,0:T(8,128)(2,1)S(1)} %shard_map.112), channel_id=1, source_target_pairs={{0,4},{1,3},{3,7},{2,0},{5,1},{4,6},{6,2},{7,5},{9,13},{8,10},{10,... | collective-permute-start | bytes 98312 | tf_op jit(solution)/shard_map/ppermute | solution.py:453
  25.5 5.0 %collective-permute-start.13 = (bf16[128,384]{1,0:T(8,128)(2,1)S(1)}, bf16[128,384]{1,0:T(8,128)(2,1)S(1)}, u32[]{:S(2)}, u32[]{:S(2)}) collective-permute-start(bf16[128,384]{1,0:T(8,128)(2,1)S(1)} %get-tuple-element.39.own), channel_id=1, source_target_pairs={{0,9},{1,4},{3,10},{2,7},{5,12},{4,1},{6,15},{7,2},{9,0},{8,13},{1... | collective-permute-start | bytes 294920 | tf_op jit(solution)/shard_map/ppermute | solution.py:453
  27.2 5.6 %collective-permute-start.16 = (bf16[128,128]{1,0:T(8,128)(2,1)S(1)}, bf16[128,128]{1,0:T(8,128)(2,1)S(1)}, u32[]{:S(2)}, u32[]{:S(2)}) collective-permute-start(bf16[128,128]{1,0:T(8,128)(2,1)S(1)} %get-tuple-element.40.own), channel_id=1, source_target_pairs={{0,9},{1,4},{3,10},{2,7},{5,12},{4,1},{6,15},{7,2},{9,0},{8,13},{1... | collective-permute-start | bytes 98312 | tf_op jit(solution)/shard_map/ppermute | solution.py:453
  28.2 8.1 %collective-permute-start.19 = (bf16[2,256,256]{2,1,0:T(8,128)(2,1)S(1)}, bf16[2,256,256]{2,1,0:T(8,128)(2,1)S(1)}, u32[]{:S(2)}, u32[]{:S(2)}) collective-permute-start(bf16[2,256,256]{2,1,0:T(8,128)(2,1)S(1)} %get-tuple-element.41), channel_id=1, source_target_pairs={{0,1},{1,0},{2,3},{3,2},{4,5},{5,4},{6,7},{7,6},{8,9},{9,8},{10,11... | collective-permute-start | bytes 786440 | tf_op jit(solution)/shard_map/ppermute | solution.py:435
  30.5 4.6 %collective-permute-start.14 = (bf16[128,384]{1,0:T(8,128)(2,1)S(1)}, bf16[128,384]{1,0:T(8,128)(2,1)S(1)}, u32[]{:S(2)}, u32[]{:S(2)}) collective-permute-start(bf16[128,384]{1,0:T(8,128)(2,1)S(1)} %shard_map.114.own), channel_id=1, source_target_pairs={{0,5},{1,2},{3,6},{2,1},{5,0},{4,7},{6,3},{7,4},{9,12},{8,11},{10,... | collective-permute-start | bytes 294920 | tf_op jit(solution)/shard_map/ppermute | solution.py:453
  32.8 3.4 %collective-permute-start.17 = (bf16[128,128]{1,0:T(8,128)(2,1)S(1)}, bf16[128,128]{1,0:T(8,128)(2,1)S(1)}, u32[]{:S(2)}, u32[]{:S(2)}) collective-permute-start(bf16[128,128]{1,0:T(8,128)(2,1)S(1)} %shard_map.116.own), channel_id=1, source_target_pairs={{0,5},{1,2},{3,6},{2,1},{5,0},{4,7},{6,3},{7,4},{9,12},{8,11},{10,... | collective-permute-start | bytes 98312 | tf_op jit(solution)/shard_map/ppermute | solution.py:453
  33.9 2.4 %collective-permute-start.20 = (f32[128,256]{1,0:T(8,128)S(1)}, f32[128,256]{1,0:T(8,128)S(1)}, u32[]{:S(2)}, u32[]{:S(2)}) collective-permute-start(f32[128,256]{1,0:T(8,128)S(1)} %get-tuple-element.43), channel_id=1, source_target_pairs={{0,1},{1,0},{2,3},{3,2},{4,5},{5,4},{6,7},{7,6},{8,9},{9,8},{10,11... | collective-permute-start | bytes 393224 | tf_op jit(solution)/shard_map/ppermute | solution.py:435
  35.1 2.4 %collective-permute-start.15 = (bf16[128,384]{1,0:T(8,128)(2,1)S(1)}, bf16[128,384]{1,0:T(8,128)(2,1)S(1)}, u32[]{:S(2)}, u32[]{:S(2)}) collective-permute-start(bf16[128,384]{1,0:T(8,128)(2,1)S(1)} %shard_map.115.long), channel_id=1, source_target_pairs={{0,1},{1,0},{2,3},{3,2},{4,5},{5,4},{6,7},{7,6},{8,9},{9,8},{10,11... | collective-permute-start | bytes 294920 | tf_op jit(solution)/shard_map/ppermute | solution.py:435
  36.2 1.3 %collective-permute-start.18 = (bf16[128,128]{1,0:T(8,128)(2,1)S(1)}, bf16[128,128]{1,0:T(8,128)(2,1)S(1)}, u32[]{:S(2)}, u32[]{:S(2)}) collective-permute-start(bf16[128,128]{1,0:T(8,128)(2,1)S(1)} %shard_map.117.short), channel_id=1, source_target_pairs={{0,1},{1,0},{2,3},{3,2},{4,5},{5,4},{6,7},{7,6},{8,9},{9,8},{10,11... | collective-permute-start | bytes 98312 | tf_op jit(solution)/shard_map/ppermute | solution.py:435

commit v20 on v17

--- a/solution.py
+++ b/solution.py
@@ -138,33 +138,28 @@
     amp_ref[1] = proj_own[0].T
 
 
-def pack_kernel(
-    amp_ref,
-    energy,
-    tgt_other,
-    proj_other,
-    tgt_energy_other,
-    proj_energy_other,
-    chip_amp,
-    energies,
-    message,
-):
-    core = lax.axis_index("rep")
+def pack_kernel(amp_ref, tgt_other, proj_other, chip_amp, message):
     my = my_kind()
-    cols = chip_amp.shape[1]
     other_amp, _ = ordered(my, tgt_other[...].T, proj_other[0].T)
-    other_energy, _ = ordered(my, tgt_energy_other[...][None, :], proj_energy_other[...])
-    amps = ordered(core, amp_ref[my], other_amp)
-    rows = ordered(core, energy[my], other_energy)
+    amps = ordered(lax.axis_index("rep"), amp_ref[my], other_amp)
     for segment in range(2):
         chip_amp[segment] = amps[segment]
-        energies[segment] = rows[segment]
-        message[segment, :cols] = bf16(amps[segment])
-        message[segment, cols:] = split(rows[segment])
+        message[segment] = bf16(amps[segment])
 
 
 def sent_kernel(
-    neighbours, weight_hbm, tgt_hbm, proj_hbm, chip_amp, sent_chip, sent_far, sent_own, weight, flat_weight, sems
+    neighbours,
+    weight_hbm,
+    tgt_hbm,
+    proj_hbm,
+    chip_amp,
+    energy,
+    sent_chip,
+    sent_far,
+    sent_own,
+    weight,
+    flat_weight,
+    sems,
 ):
     my = my_kind()
     sources = (tgt_hbm, proj_hbm)
@@ -190,7 +185,8 @@
     weight_copy.wait()
     weight[0] = flat_weight[...][None, :]
     for part in range(2):
-        sent_chip[part, 2 * rows :] = split(weight[0])
+        sent_chip[part, 2 * rows : 2 * rows + PIECES] = split(weight[0])
+        sent_chip[part, 2 * rows + PIECES :, :rows] = split(energy[1 - my])
     for copy in copies_of(0):
         copy.wait()
 
@@ -245,7 +241,7 @@
         copy.wait()
 
 
-def chip_kernel(mine_chip, theirs_chip, chip_amp, weight, part_ref, weights):
+def chip_kernel(mine_chip, theirs_chip, chip_amp, weight, energy, part_ref, weights, energies):
     mine, theirs = (mine_chip,), (theirs_chip,)
     rows = chip_amp.shape[2]
 
@@ -255,7 +251,9 @@
                 project(rows_of(basis, segment, rows), chip_amp[segment]) for segment in range(2)
             )
         weights[core] = weight[0]
-        weights[1 - core] = joined(theirs_chip[0, 2 * rows :, :])
+        weights[1 - core] = joined(theirs_chip[0, 2 * rows : 2 * rows + PIECES, :])
+        energies[core] = energy[my_kind()]
+        energies[1 - core] = joined(theirs_chip[0, 2 * rows + PIECES :, :rows])
 
     by_core(body)
 
@@ -263,12 +261,11 @@
 def first_kernel(mine_far, theirs_far, gate, weights, part_ref, message, *outs):
     mine, theirs = (None, mine_far), (None, theirs_far)
     rows = message.shape[2]
-    cols = part_ref.shape[1]
 
     def body(core):
         for half, basis in enumerate((mine, theirs) if core == 0 else (theirs, mine)):
             total = part_ref[half] + sum(
-                project(rows_of(basis, 2 + segment, rows), f32(message[segment, :cols]))
+                project(rows_of(basis, 2 + segment, rows), f32(message[segment]))
                 for segment in range(2)
             )
             outs[half][...] = bf16(gate[0, half] * (weights[half] * total))
@@ -290,10 +287,11 @@
     chip_amp,
     energies,
     message,
+    neighbour_energies,
     states_ref,
 ):
     mine, theirs = (mine_chip, mine_far), (theirs_chip, theirs_far)
-    _, cols, rows = chip_amp.shape
+    rows = chip_amp.shape[2]
     field = bf16(f32(low[...]) + f32(low_there[...]))
 
     def body(core):
@@ -301,7 +299,7 @@
             if segment < 2:
                 amp, energy = chip_amp[segment], energies[segment]
             else:
-                amp, energy = f32(message[segment - 2, :cols]), joined(message[segment - 2, cols:])
+                amp, energy = f32(message[segment - 2]), neighbour_energies[segment - 2]
             change = expand(rows_of((mine, theirs)[core], segment, rows), field)
             states_ref[segment] = amp + half_step * (energy * turned(amp) + change)
 
@@ -409,17 +407,17 @@
     n_tgt, n_prj, n_core = sizes
     tgt_flips = [n_prj << bit for bit in range(n_tgt.bit_length() - 1)]
     prj_flips = [1 << bit for bit in range(n_prj.bit_length() - 1)]
-    far_first, near_first = tgt_flips[::-1], tgt_flips
-    flips = [(prj_flips + order, far_first + prj_flips) for order in (far_first, near_first)]
+    far_first = tgt_flips[::-1]
+    flips = (prj_flips + far_first, far_first + prj_flips)
     neighbours = (prj_flips[0], far_first[0] // n_prj)
     gate_levels = (len(prj_flips) - 1, len(tgt_flips) - 1)
     n_steps = len(tgt_flips) + len(prj_flips)
 
-    def exchanged(step, block, half=0, crossed=0):
+    def exchanged(step, block, crossed=0):
         pairs = []
         for place in range(n_tgt * n_prj):
             for kind in range(2):
-                there = place ^ flips[half][kind][step]
+                there = place ^ flips[kind][step]
                 to_core = kind ^ crossed ^ parity(there)
                 pairs.append((place * n_core + (kind ^ parity(place)), there * n_core + to_core))
         return lax.ppermute(block, DEVICES, pairs)
@@ -432,7 +430,7 @@
         totals = []
         for half, block in enumerate(halves):
             for step in range(1, until):
-                other = exchanged(step, block, half)
+                other = exchanged(step, block)
                 (block,) = run(functools.partial(add_kernel, step, half), [sums], gate, block, other)
             totals.append(block)
         return totals
@@ -443,7 +441,7 @@
     def in_hbm(*blocks):
         return [pltpu.with_memory_space_constraint(block, pltpu.HBM) for block in blocks]
 
-    others = swapped([tgt_amp, proj_amp, tgt_energy, proj_energy])
+    others = swapped([tgt_amp, proj_amp])
     energy, amp = call(
         load_kernel,
         [in_vmem((2, 1, rows), jnp.float32), in_vmem((2, two_cols, rows), jnp.float32)],
@@ -458,15 +456,10 @@
             flops=2 * 4 * rows * two_cols * points, bytes_accessed=4 * 1024 * 1024, transcendentals=0
         ),
     )(*in_hbm(tgt_energy, proj_energy, tgt_amp, proj_amp))
-    chip_amp, energies, message = run(
+    chip_amp, message = run(
         pack_kernel,
-        [
-            in_vmem((2, two_cols, rows), jnp.float32),
-            in_vmem((2, 1, rows), jnp.float32),
-            in_vmem((2, two_cols + PIECES, rows), jnp.bfloat16),
-        ],
+        [in_vmem((2, two_cols, rows), jnp.float32), in_vmem((2, two_cols, rows), jnp.bfloat16)],
         amp,
-        energy,
         *others,
     )
     message = exchanged(0, message)
@@ -476,14 +469,14 @@
     *sent, weight = call(
         functools.partial(sent_kernel, neighbours),
         [
-            in_vmem((2, 2 * rows + PIECES, points), jnp.bfloat16),
+            in_vmem((2, 2 * rows + 2 * PIECES, points), jnp.bfloat16),
             pair,
             in_vmem((2, rows, points), jnp.bfloat16),
             in_vmem((1, 1, points), jnp.float32),
         ],
-        [HBM] * 3 + [VMEM],
+        [HBM] * 3 + [VMEM] * 2,
         [pltpu.VMEM((points,), jnp.float32), pltpu.SemaphoreType.DMA((6,))],
-    )(*in_hbm(quad_weight), *bases, chip_amp)
+    )(*in_hbm(quad_weight), *bases, chip_amp, energy)
     mine_chip, mine_far, gate = call(
         functools.partial(side_kernel, gate_levels, neighbours),
         [
@@ -501,19 +494,25 @@
     )(*in_hbm(flags, counts), *bases, chip_amp)
     theirs_chip, theirs_far, theirs_own = swapped(sent)
     bases = (mine_chip, mine_far, theirs_chip, theirs_far)
-    part, weights = run(
+    part, weights, energies = run(
         chip_kernel,
-        [in_vmem((2, two_cols, points), jnp.float32), in_vmem((2, 1, points), jnp.float32)],
+        [
+            in_vmem((2, two_cols, points), jnp.float32),
+            in_vmem((2, 1, points), jnp.float32),
+            in_vmem((2, 1, rows), jnp.float32),
+        ],
         mine_chip,
         theirs_chip,
         chip_amp,
         weight,
+        energy,
     )
     halves = run(first_kernel, [sums] * 2, mine_far, theirs_far, gate, weights, part, message)
+    (low, high), energies = lax.optimization_barrier((halves, energies))
+    neighbour_energies = exchanged(0, energies)
+    halves = low, high
     parts = summed(halves, n_steps - 1)
-    low, high = [
-        (other_core(block), exchanged(n_steps - 1, block, half, 1)) for half, block in enumerate(parts)
-    ]
+    low, high = [(other_core(block), exchanged(n_steps - 1, block, crossed=1)) for block in parts]
     (states,) = run(
         low_kernel,
         [in_vmem((4, two_cols, rows), jnp.float32)],
@@ -522,6 +521,7 @@
         chip_amp,
         energies,
         message,
+        neighbour_energies,
     )
     *halves, my_half, half_send = run(
         second_kernel,

time: 36.8 us -> 35.8 us (0.973)
  starting transfers between devices: 18.9 us -> 18.3 us
  waiting for transfers between devices: 9.51 us -> 9.1 us
    ppermute x12 -> x10, starting transfers between devices: 4.76 us -> 3.36 us  [other_core(): return lax.ppermute(block, 'rep', [(0, 1), (1, 0)])]
    ppermute x9 -> x10, starting transfers between devices: 14.1 us -> 15 us  [exchanged(): return lax.ppermute(block, DEVICES, pairs)]
    ppermute x9 -> x10, waiting for transfers between devices: 7.67 us -> 7.03 us  [exchanged(): return lax.ppermute(block, DEVICES, pairs)]
    ppermute x12 -> x10, waiting for transfers between devices: 1.85 us -> 2.07 us  [other_core(): return lax.ppermute(block, 'rep', [(0, 1), (1, 0)])]
  transfers between devices with their start and end apart: 21 -> 20, of which waited for: 9 -> 10; matrix products, arithmetic and copies ran while one was open for 0% -> 0% of each run, Pallas kernels for 16% -> 17%
where the time goes in v20:
time: 35.8 us; the launch traced here: 35.6 us
  starting transfers between devices  18.3 us (51%)
  waiting for transfers between devices  9.1 us (25%)
  Pallas kernels  7.44 us (21%)
  between operations  0.78 us (2%)
    ppermute x10, starting transfers between devices, exchanged(): return lax.ppermute(block, DEVICES, pairs)  15 us
    ppermute x10, waiting for transfers between devices, exchanged(): return lax.ppermute(block, DEVICES, pairs)  7.03 us
    pallas_call x13, Pallas kernels, run(): return call(kernel, out_shape, [VMEM] * len(blocks))(*blocks)  3.73 us
    ppermute x10, starting transfers between devices, other_core(): return lax.ppermute(block, 'rep', [(0, 1), (1, 0)])  3.36 us
    ppermute x10, waiting for transfers between devices, other_core(): return lax.ppermute(block, 'rep', [(0, 1), (1, 0)])  2.07 us
    pallas_call x1, Pallas kernels, shards(): call(functools.partial(sent_kernel, neighbours), [in_vmem((2, 2 * rows +...  1.33 us
    pallas_call x1, Pallas kernels, shards(): call(functools.partial(side_kernel, gate_levels, neighbours), [pair, pair...  1.24 us
    pallas_call x1, Pallas kernels, shards(): call(load_kernel, [in_vmem((2, 1, rows), jnp.float32), in_vmem((2, two_co...  1.14 us
  transfers between devices with their start and end apart: 20, of which 10 were waited for; matrix products, arithmetic and copies ran while one was open for 0% of the time, Pallas kernels for 17%

profile of v20, /device:TPU:0, one launch (start us, length us, event | category | flops | bytes accessed | tf_op | source)
XLA Modules:
  0.0 35.6 jit_solution(267232327444302670)
XLA Ops:
  0.6 0.5 %collective-permute-start = (f32[256,128]{1,0:T(8,128)}, f32[256,128]{1,0:T(8,128)S(1)}, u32[]{:S(2)}, u32[]{:S(2)}) collective-permute-start(f32[256,128]{1,0:T(8,128)} %tgt_own_hbm.1), channel_id=1, source_target_pairs={{0,1},{1,0},{2,3},{3,2},{4,5},{5,4},{6,7},{7,6},{8,9},{9,8},{10,11... | collective-permute-start | bytes 393224 | tf_op jit(solution)/shard_map/ppermute | solution.py:405
  1.2 1.1 %shard_map.104 = (f32[2,1,256]{2,1,0:T(1,128)S(1)}, f32[2,128,256]{2,1,0:T(8,128)S(1)}) custom-call(f32[256]{0:T(256)} %tgt_energy_hbm.1, f32[1,256]{1,0:T(1,128)} %proj_energy_hbm.1, f32[256,128]{1,0:T(8,128)} %tgt_own_hbm.1, f32[1,256,128]{2,1,0:T(8,128)} %proj_own_hbm.1), custom_call_target="tpu_custom_call" | custom-call | flops 67108864 | bytes 4194304 | tf_op jit(solution)/shard_map/pallas_call | solution.py:445
  2.8 2.7 %collective-permute-start.4 = (bf16[2,128,256]{2,1,0:T(8,128)(2,1)S(1)}, bf16[2,128,256]{2,1,0:T(8,128)(2,1)S(1)}, u32[]{:S(2)}, u32[]{:S(2)}) collective-permute-start(bf16[2,128,256]{2,1,0:T(8,128)(2,1)S(1)} %get-tuple-element.38), channel_id=1, source_target_pairs={{0,3},{1,8},{3,0},{2,11},{5,6},{4,13},{6,5},{7,14},{9,10},{8,1},{1... | collective-permute-start | bytes 393224 | tf_op jit(solution)/shard_map/ppermute | solution.py:423
  5.5 1.3 %shard_map.107 = (bf16[2,544,256]{2,1,0:T(8,128)(2,1)S(1)}, bf16[2,512,256]{2,1,0:T(8,128)(2,1)S(1)}, bf16[2,256,256]{2,1,0:T(8,128)(2,1)S(1)}, f32[1,1,256]{2,1,0:T(1,128)S(1)}) custom-call(f32[256]{0:T(256)} %weight_hbm.1, bf16[2,4,256,256]{3,2,1,0:T(8,128)(2,1)} %bitcast.3, bf16[2,8,256,256]{3,2,1,0:T(8,128)(2,1)} %proj_hbm.3, ...), custom_call_target="tpu_custom_call" | custom-call | tf_op jit(solution)/shard_map/pallas_call | solution.py:469
  6.9 1.4 %collective-permute-start.3 = (bf16[2,512,256]{2,1,0:T(8,128)(2,1)S(1)}, bf16[2,512,256]{2,1,0:T(8,128)(2,1)S(1)}, u32[]{:S(2)}, u32[]{:S(2)}) collective-permute-start(bf16[2,512,256]{2,1,0:T(8,128)(2,1)S(1)} %get-tuple-element.34), channel_id=1, source_target_pairs={{0,1},{1,0},{2,3},{3,2},{4,5},{5,4},{6,7},{7,6},{8,9},{9,8},{10,11... | collective-permute-start | bytes 1572872 | tf_op jit(solution)/shard_map/ppermute | solution.py:405
  8.3 1.2 %shard_map.106 = (bf16[2,512,256]{2,1,0:T(8,128)(2,1)S(1)}, bf16[2,512,256]{2,1,0:T(8,128)(2,1)S(1)}, f32[3,2,1,256]{3,2,1,0:T(1,128)S(1)}) custom-call(s32[2,4]{1,0:T(2,128)} %bitcast.5, s32[2,4]{1,0:T(2,128)} %bitcast.6, bf16[2,4,256,256]{3,2,1,0:T(8,128)(2,1)} %bitcast.4, bf16[2,8,256,256]{3,2,1,0:T(8,128)(2,1)} %proj_hbm.3, ...), custom_call_target="tpu_custom_call" | custom-call | flops 34359738368 | bytes 65536 | tf_op jit(solution)/shard_map/pallas_call | solution.py:480
  9.5 1.0 %collective-permute-done.2.theirs_chip = bf16[2,544,256]{2,1,0:T(8,128)(2,1)S(1)} collective-permute-done((bf16[2,544,256]{2,1,0:T(8,128)(2,1)S(1)}, bf16[2,544,256]{2,1,0:T(8,128)(2,1)S(1)}, u32[]{:S(2)}, u32[]{:S(2)}) %collective-permute-start.2) | collective-permute-done | bytes 557088 | tf_op jit(solution)/shard_map/ppermute | solution.py:405
  11.2 1.5 %collective-permute-start.5 = (bf16[128,256]{1,0:T(8,128)(2,1)S(1)}, bf16[128,256]{1,0:T(8,128)(2,1)S(1)}, u32[]{:S(2)}, u32[]{:S(2)}) collective-permute-start(bf16[128,256]{1,0:T(8,128)(2,1)S(1)} %get-tuple-element.42.own), channel_id=1, source_target_pairs={{0,9},{1,4},{3,10},{2,7},{5,12},{4,1},{6,15},{7,2},{9,0},{8,13},{1... | collective-permute-start | bytes 196616 | tf_op jit(solution)/shard_map/ppermute | solution.py:423
  12.8 1.2 %collective-permute-start.9 = (bf16[128,256]{1,0:T(8,128)(2,1)S(1)}, bf16[128,256]{1,0:T(8,128)(2,1)S(1)}, u32[]{:S(2)}, u32[]{:S(2)}) collective-permute-start(bf16[128,256]{1,0:T(8,128)(2,1)S(1)} %get-tuple-element.44.own), channel_id=1, source_target_pairs={{0,9},{1,4},{3,10},{2,7},{5,12},{4,1},{6,15},{7,2},{9,0},{8,13},{1... | collective-permute-start | bytes 196616 | tf_op jit(solution)/shard_map/ppermute | solution.py:423
  13.9 1.4 %collective-permute-start.8 = (f32[2,1,256]{2,1,0:T(1,128)S(1)}, f32[2,1,256]{2,1,0:T(1,128)S(1)}, u32[]{:S(2)}, u32[]{:S(2)}) collective-permute-start(f32[2,1,256]{2,1,0:T(1,128)S(1)} %get-tuple-element.43.energies), channel_id=1, source_target_pairs={{0,3},{1,8},{3,0},{2,11},{5,6},{4,13},{6,5},{7,14},{9,10},{8,1},{1... | collective-permute-start | bytes 6152 | tf_op jit(solution)/shard_map/ppermute | solution.py:423
  15.4 0.6 %collective-permute-done.5.other = bf16[128,256]{1,0:T(8,128)(2,1)S(1)} collective-permute-done((bf16[128,256]{1,0:T(8,128)(2,1)S(1)}, bf16[128,256]{1,0:T(8,128)(2,1)S(1)}, u32[]{:S(2)}, u32[]{:S(2)}) %collective-permute-start.5) | collective-permute-done | bytes 65568 | tf_op jit(solution)/shard_map/ppermute | solution.py:423
  16.0 1.2 %collective-permute-start.7 = (bf16[128,256]{1,0:T(8,128)(2,1)S(1)}, bf16[128,256]{1,0:T(8,128)(2,1)S(1)}, u32[]{:S(2)}, u32[]{:S(2)}) collective-permute-start(bf16[128,256]{1,0:T(8,128)(2,1)S(1)} %shard_map.110), channel_id=1, source_target_pairs={{0,4},{1,3},{3,7},{2,0},{5,1},{4,6},{6,2},{7,5},{9,13},{8,10},{10,... | collective-permute-start | bytes 196616 | tf_op jit(solution)/shard_map/ppermute | solution.py:423
  17.2 0.6 %collective-permute-start.6 = (bf16[128,256]{1,0:T(8,128)(2,1)S(1)}, bf16[128,256]{1,0:T(8,128)(2,1)S(1)}, u32[]{:S(2)}, u32[]{:S(2)}) collective-permute-start(bf16[128,256]{1,0:T(8,128)(2,1)S(1)} %shard_map.110), channel_id=1, source_target_pairs={{0,1},{1,0},{2,3},{3,2},{4,5},{5,4},{6,7},{7,6},{8,9},{9,8},{10,11... | collective-permute-start | bytes 196616 | tf_op jit(solution)/shard_map/ppermute | solution.py:405
  18.1 1.6 %collective-permute-start.11 = (bf16[128,256]{1,0:T(8,128)(2,1)S(1)}, bf16[128,256]{1,0:T(8,128)(2,1)S(1)}, u32[]{:S(2)}, u32[]{:S(2)}) collective-permute-start(bf16[128,256]{1,0:T(8,128)(2,1)S(1)} %shard_map.112), channel_id=1, source_target_pairs={{0,4},{1,3},{3,7},{2,0},{5,1},{4,6},{6,2},{7,5},{9,13},{8,10},{10,... | collective-permute-start | bytes 196616 | tf_op jit(solution)/shard_map/ppermute | solution.py:423
  20.9 1.6 %collective-permute-done.11.high_there = bf16[128,256]{1,0:T(8,128)(2,1)S(1)} collective-permute-done((bf16[128,256]{1,0:T(8,128)(2,1)S(1)}, bf16[128,256]{1,0:T(8,128)(2,1)S(1)}, u32[]{:S(2)}, u32[]{:S(2)}) %collective-permute-start.11) | collective-permute-done | bytes 65568 | tf_op jit(solution)/shard_map/ppermute | solution.py:423
  22.4 0.8 %shard_map.113 = (bf16[128,256]{1,0:T(8,128)(2,1)S(1)}, bf16[128,256]{1,0:T(8,128)(2,1)S(1)}, f32[128,256]{1,0:T(8,128)S(1)}, f32[128,256]{1,0:T(8,128)S(1)}) custom-call(bf16[2,512,256]{2,1,0:T(8,128)(2,1)S(1)} %get-tuple-element.29.mine_chip, bf16[2,512,256]{2,1,0:T(8,128)(2,1)S(1)} %get-tuple-element.33.mine_far, ...), custom_call_target="tpu_custom_call" | custom-call | tf_op jit(solution)/shard_map/pallas_call | solution.py:402
  23.5 2.4 %collective-permute-start.15 = (bf16[128,256]{1,0:T(8,128)(2,1)S(1)}, bf16[128,256]{1,0:T(8,128)(2,1)S(1)}, u32[]{:S(2)}, u32[]{:S(2)}) collective-permute-start(bf16[128,256]{1,0:T(8,128)(2,1)S(1)} %get-tuple-element.46.own), channel_id=1, source_target_pairs={{0,9},{1,4},{3,10},{2,7},{5,12},{4,1},{6,15},{7,2},{9,0},{8,13},{1... | collective-permute-start | bytes 196616 | tf_op jit(solution)/shard_map/ppermute | solution.py:423
  26.0 1.9 %collective-permute-done.12.other = bf16[128,256]{1,0:T(8,128)(2,1)S(1)} collective-permute-done((bf16[128,256]{1,0:T(8,128)(2,1)S(1)}, bf16[128,256]{1,0:T(8,128)(2,1)S(1)}, u32[]{:S(2)}, u32[]{:S(2)}) %collective-permute-start.12) | collective-permute-done | bytes 65568 | tf_op jit(solution)/shard_map/ppermute | solution.py:423
  27.9 1.5 %collective-permute-start.13 = (bf16[128,256]{1,0:T(8,128)(2,1)S(1)}, bf16[128,256]{1,0:T(8,128)(2,1)S(1)}, u32[]{:S(2)}, u32[]{:S(2)}) collective-permute-start(bf16[128,256]{1,0:T(8,128)(2,1)S(1)} %shard_map.114.own), channel_id=1, source_target_pairs={{0,5},{1,2},{3,6},{2,1},{5,0},{4,7},{6,3},{7,4},{9,12},{8,11},{10,... | collective-permute-start | bytes 196616 | tf_op jit(solution)/shard_map/ppermute | solution.py:423
  29.5 1.2 %collective-permute-start.16 = (bf16[128,256]{1,0:T(8,128)(2,1)S(1)}, bf16[128,256]{1,0:T(8,128)(2,1)S(1)}, u32[]{:S(2)}, u32[]{:S(2)}) collective-permute-start(bf16[128,256]{1,0:T(8,128)(2,1)S(1)} %shard_map.116.own), channel_id=1, source_target_pairs={{0,5},{1,2},{3,6},{2,1},{5,0},{4,7},{6,3},{7,4},{9,12},{8,11},{10,... | collective-permute-start | bytes 196616 | tf_op jit(solution)/shard_map/ppermute | solution.py:423
  30.6 1.0 %collective-permute-done.13.other = bf16[128,256]{1,0:T(8,128)(2,1)S(1)} collective-permute-done((bf16[128,256]{1,0:T(8,128)(2,1)S(1)}, bf16[128,256]{1,0:T(8,128)(2,1)S(1)}, u32[]{:S(2)}, u32[]{:S(2)}) %collective-permute-start.13) | collective-permute-done | bytes 65568 | tf_op jit(solution)/shard_map/ppermute | solution.py:423
  31.8 1.4 %collective-permute-done.16.other = bf16[128,256]{1,0:T(8,128)(2,1)S(1)} collective-permute-done((bf16[128,256]{1,0:T(8,128)(2,1)S(1)}, bf16[128,256]{1,0:T(8,128)(2,1)S(1)}, u32[]{:S(2)}, u32[]{:S(2)}) %collective-permute-start.16) | collective-permute-done | bytes 65568 | tf_op jit(solution)/shard_map/ppermute | solution.py:423
  33.8 0.7 %collective-permute-done.17.high = bf16[128,256]{1,0:T(8,128)(2,1)S(1)} collective-permute-done((bf16[128,256]{1,0:T(8,128)(2,1)S(1)}, bf16[128,256]{1,0:T(8,128)(2,1)S(1)}, u32[]{:S(2)}, u32[]{:S(2)}) %collective-permute-start.17) | collective-permute-done | bytes 65568 | tf_op jit(solution)/shard_map/ppermute | solution.py:405
  34.6 1.1 %shard_map.119 = (f32[256,128]{1,0:T(8,128)}, f32[1,256,128]{2,1,0:T(8,128)}) custom-call(bf16[2,512,256]{2,1,0:T(8,128)(2,1)S(1)} %get-tuple-element.29.mine_chip, bf16[2,544,256]{2,1,0:T(8,128)(2,1)S(1)} %collective-permute-done.2.theirs_chip, bf16[128,256]{1,0:T(8,128)(2,1)S(1)} %collective-permute-done.14.low, ...), custom_call_target="tpu_custom_call" | custom-call | tf_op jit(solution)/shard_map/pallas_call | solution.py:402
  (32 shorter events, 3.8 us)
Async XLA Ops:
  0.6 1.7 %collective-permute-start = (f32[256,128]{1,0:T(8,128)}, f32[256,128]{1,0:T(8,128)S(1)}, u32[]{:S(2)}, u32[]{:S(2)}) collective-permute-start(f32[256,128]{1,0:T(8,128)} %tgt_own_hbm.1), channel_id=1, source_target_pairs={{0,1},{1,0},{2,3},{3,2},{4,5},{5,4},{6,7},{7,6},{8,9},{9,8},{10,11... | collective-permute-start | bytes 393224 | tf_op jit(solution)/shard_map/ppermute | solution.py:405
  1.1 1.6 %collective-permute-start.1 = (f32[1,256,128]{2,1,0:T(8,128)}, f32[1,256,128]{2,1,0:T(8,128)S(1)}, u32[]{:S(2)}, u32[]{:S(2)}) collective-permute-start(f32[1,256,128]{2,1,0:T(8,128)} %proj_own_hbm.1), channel_id=1, source_target_pairs={{0,1},{1,0},{2,3},{3,2},{4,5},{5,4},{6,7},{7,6},{8,9},{9,8},{10,11... | collective-permute-start | bytes 393224 | tf_op jit(solution)/shard_map/ppermute | solution.py:405
  2.8 8.0 %collective-permute-start.4 = (bf16[2,128,256]{2,1,0:T(8,128)(2,1)S(1)}, bf16[2,128,256]{2,1,0:T(8,128)(2,1)S(1)}, u32[]{:S(2)}, u32[]{:S(2)}) collective-permute-start(bf16[2,128,256]{2,1,0:T(8,128)(2,1)S(1)} %get-tuple-element.38), channel_id=1, source_target_pairs={{0,3},{1,8},{3,0},{2,11},{5,6},{4,13},{6,5},{7,14},{9,10},{8,1},{1... | collective-permute-start | bytes 393224 | tf_op jit(solution)/shard_map/ppermute | solution.py:423
  6.9 4.0 %collective-permute-start.3 = (bf16[2,512,256]{2,1,0:T(8,128)(2,1)S(1)}, bf16[2,512,256]{2,1,0:T(8,128)(2,1)S(1)}, u32[]{:S(2)}, u32[]{:S(2)}) collective-permute-start(bf16[2,512,256]{2,1,0:T(8,128)(2,1)S(1)} %get-tuple-element.34), channel_id=1, source_target_pairs={{0,1},{1,0},{2,3},{3,2},{4,5},{5,4},{6,7},{7,6},{8,9},{9,8},{10,11... | collective-permute-start | bytes 1572872 | tf_op jit(solution)/shard_map/ppermute | solution.py:405
  8.2 2.3 %collective-permute-start.2 = (bf16[2,544,256]{2,1,0:T(8,128)(2,1)S(1)}, bf16[2,544,256]{2,1,0:T(8,128)(2,1)S(1)}, u32[]{:S(2)}, u32[]{:S(2)}) collective-permute-start(bf16[2,544,256]{2,1,0:T(8,128)(2,1)S(1)} %get-tuple-element.31.sent_chip), channel_id=1, source_target_pairs={{0,1},{1,0},{2,3},{3,2},{4,5},{5,4},{6,7},{7,6},{8,9},{9,8},{10,11... | collective-permute-start | bytes 1671176 | tf_op jit(solution)/shard_map/ppermute | solution.py:405
  11.2 4.8 %collective-permute-start.5 = (bf16[128,256]{1,0:T(8,128)(2,1)S(1)}, bf16[128,256]{1,0:T(8,128)(2,1)S(1)}, u32[]{:S(2)}, u32[]{:S(2)}) collective-permute-start(bf16[128,256]{1,0:T(8,128)(2,1)S(1)} %get-tuple-element.42.own), channel_id=1, source_target_pairs={{0,9},{1,4},{3,10},{2,7},{5,12},{4,1},{6,15},{7,2},{9,0},{8,13},{1... | collective-permute-start | bytes 196616 | tf_op jit(solution)/shard_map/ppermute | solution.py:423
  12.8 5.3 %collective-permute-start.9 = (bf16[128,256]{1,0:T(8,128)(2,1)S(1)}, bf16[128,256]{1,0:T(8,128)(2,1)S(1)}, u32[]{:S(2)}, u32[]{:S(2)}) collective-permute-start(bf16[128,256]{1,0:T(8,128)(2,1)S(1)} %get-tuple-element.44.own), channel_id=1, source_target_pairs={{0,9},{1,4},{3,10},{2,7},{5,12},{4,1},{6,15},{7,2},{9,0},{8,13},{1... | collective-permute-start | bytes 196616 | tf_op jit(solution)/shard_map/ppermute | solution.py:423
  13.9 5.7 %collective-permute-start.8 = (f32[2,1,256]{2,1,0:T(1,128)S(1)}, f32[2,1,256]{2,1,0:T(1,128)S(1)}, u32[]{:S(2)}, u32[]{:S(2)}) collective-permute-start(f32[2,1,256]{2,1,0:T(1,128)S(1)} %get-tuple-element.43.energies), channel_id=1, source_target_pairs={{0,3},{1,8},{3,0},{2,11},{5,6},{4,13},{6,5},{7,14},{9,10},{8,1},{1... | collective-permute-start | bytes 6152 | tf_op jit(solution)/shard_map/ppermute | solution.py:423
  16.0 4.3 %collective-permute-start.7 = (bf16[128,256]{1,0:T(8,128)(2,1)S(1)}, bf16[128,256]{1,0:T(8,128)(2,1)S(1)}, u32[]{:S(2)}, u32[]{:S(2)}) collective-permute-start(bf16[128,256]{1,0:T(8,128)(2,1)S(1)} %shard_map.110), channel_id=1, source_target_pairs={{0,4},{1,3},{3,7},{2,0},{5,1},{4,6},{6,2},{7,5},{9,13},{8,10},{10,... | collective-permute-start | bytes 196616 | tf_op jit(solution)/shard_map/ppermute | solution.py:423
  17.2 3.1 %collective-permute-start.6 = (bf16[128,256]{1,0:T(8,128)(2,1)S(1)}, bf16[128,256]{1,0:T(8,128)(2,1)S(1)}, u32[]{:S(2)}, u32[]{:S(2)}) collective-permute-start(bf16[128,256]{1,0:T(8,128)(2,1)S(1)} %shard_map.110), channel_id=1, source_target_pairs={{0,1},{1,0},{2,3},{3,2},{4,5},{5,4},{6,7},{7,6},{8,9},{9,8},{10,11... | collective-permute-start | bytes 196616 | tf_op jit(solution)/shard_map/ppermute | solution.py:405
  18.1 4.3 %collective-permute-start.11 = (bf16[128,256]{1,0:T(8,128)(2,1)S(1)}, bf16[128,256]{1,0:T(8,128)(2,1)S(1)}, u32[]{:S(2)}, u32[]{:S(2)}) collective-permute-start(bf16[128,256]{1,0:T(8,128)(2,1)S(1)} %shard_map.112), channel_id=1, source_target_pairs={{0,4},{1,3},{3,7},{2,0},{5,1},{4,6},{6,2},{7,5},{9,13},{8,10},{10,... | collective-permute-start | bytes 196616 | tf_op jit(solution)/shard_map/ppermute | solution.py:423
  19.7 2.7 %collective-permute-start.10 = (bf16[128,256]{1,0:T(8,128)(2,1)S(1)}, bf16[128,256]{1,0:T(8,128)(2,1)S(1)}, u32[]{:S(2)}, u32[]{:S(2)}) collective-permute-start(bf16[128,256]{1,0:T(8,128)(2,1)S(1)} %shard_map.112), channel_id=1, source_target_pairs={{0,1},{1,0},{2,3},{3,2},{4,5},{5,4},{6,7},{7,6},{8,9},{9,8},{10,11... | collective-permute-start | bytes 196616 | tf_op jit(solution)/shard_map/ppermute | solution.py:405
  19.7 13.8 %collective-permute-start.18 = (bf16[2,256,256]{2,1,0:T(8,128)(2,1)S(1)}, bf16[2,256,256]{2,1,0:T(8,128)(2,1)S(1)}, u32[]{:S(2)}, u32[]{:S(2)}) collective-permute-start(bf16[2,256,256]{2,1,0:T(8,128)(2,1)S(1)} %get-tuple-element.47), channel_id=1, source_target_pairs={{0,1},{1,0},{2,3},{3,2},{4,5},{5,4},{6,7},{7,6},{8,9},{9,8},{10,11... | collective-permute-start | bytes 786440 | tf_op jit(solution)/shard_map/ppermute | solution.py:405
  23.2 4.7 %collective-permute-start.12 = (bf16[128,256]{1,0:T(8,128)(2,1)S(1)}, bf16[128,256]{1,0:T(8,128)(2,1)S(1)}, u32[]{:S(2)}, u32[]{:S(2)}) collective-permute-start(bf16[128,256]{1,0:T(8,128)(2,1)S(1)} %get-tuple-element.45.own), channel_id=1, source_target_pairs={{0,9},{1,4},{3,10},{2,7},{5,12},{4,1},{6,15},{7,2},{9,0},{8,13},{1... | collective-permute-start | bytes 196616 | tf_op jit(solution)/shard_map/ppermute | solution.py:423
  23.5 5.9 %collective-permute-start.15 = (bf16[128,256]{1,0:T(8,128)(2,1)S(1)}, bf16[128,256]{1,0:T(8,128)(2,1)S(1)}, u32[]{:S(2)}, u32[]{:S(2)}) collective-permute-start(bf16[128,256]{1,0:T(8,128)(2,1)S(1)} %get-tuple-element.46.own), channel_id=1, source_target_pairs={{0,9},{1,4},{3,10},{2,7},{5,12},{4,1},{6,15},{7,2},{9,0},{8,13},{1... | collective-permute-start | bytes 196616 | tf_op jit(solution)/shard_map/ppermute | solution.py:423
  26.0 7.5 %collective-permute-start.19 = (f32[128,256]{1,0:T(8,128)S(1)}, f32[128,256]{1,0:T(8,128)S(1)}, u32[]{:S(2)}, u32[]{:S(2)}) collective-permute-start(f32[128,256]{1,0:T(8,128)S(1)} %get-tuple-element.49), channel_id=1, source_target_pairs={{0,1},{1,0},{2,3},{3,2},{4,5},{5,4},{6,7},{7,6},{8,9},{9,8},{10,11... | collective-permute-start | bytes 393224 | tf_op jit(solution)/shard_map/ppermute | solution.py:405
  27.9 3.8 %collective-permute-start.13 = (bf16[128,256]{1,0:T(8,128)(2,1)S(1)}, bf16[128,256]{1,0:T(8,128)(2,1)S(1)}, u32[]{:S(2)}, u32[]{:S(2)}) collective-permute-start(bf16[128,256]{1,0:T(8,128)(2,1)S(1)} %shard_map.114.own), channel_id=1, source_target_pairs={{0,5},{1,2},{3,6},{2,1},{5,0},{4,7},{6,3},{7,4},{9,12},{8,11},{10,... | collective-permute-start | bytes 196616 | tf_op jit(solution)/shard_map/ppermute | solution.py:423
  29.5 3.8 %collective-permute-start.16 = (bf16[128,256]{1,0:T(8,128)(2,1)S(1)}, bf16[128,256]{1,0:T(8,128)(2,1)S(1)}, u32[]{:S(2)}, u32[]{:S(2)}) collective-permute-start(bf16[128,256]{1,0:T(8,128)(2,1)S(1)} %shard_map.116.own), channel_id=1, source_target_pairs={{0,5},{1,2},{3,6},{2,1},{5,0},{4,7},{6,3},{7,4},{9,12},{8,11},{10,... | collective-permute-start | bytes 196616 | tf_op jit(solution)/shard_map/ppermute | solution.py:423
  31.7 2.1 %collective-permute-start.14 = (bf16[128,256]{1,0:T(8,128)(2,1)S(1)}, bf16[128,256]{1,0:T(8,128)(2,1)S(1)}, u32[]{:S(2)}, u32[]{:S(2)}) collective-permute-start(bf16[128,256]{1,0:T(8,128)(2,1)S(1)} %shard_map.115.low), channel_id=1, source_target_pairs={{0,1},{1,0},{2,3},{3,2},{4,5},{5,4},{6,7},{7,6},{8,9},{9,8},{10,11... | collective-permute-start | bytes 196616 | tf_op jit(solution)/shard_map/ppermute | solution.py:405
  33.2 1.3 %collective-permute-start.17 = (bf16[128,256]{1,0:T(8,128)(2,1)S(1)}, bf16[128,256]{1,0:T(8,128)(2,1)S(1)}, u32[]{:S(2)}, u32[]{:S(2)}) collective-permute-start(bf16[128,256]{1,0:T(8,128)(2,1)S(1)} %shard_map.117.high), channel_id=1, source_target_pairs={{0,1},{1,0},{2,3},{3,2},{4,5},{5,4},{6,7},{7,6},{8,9},{9,8},{10,11... | collective-permute-start | bytes 196616 | tf_op jit(solution)/shard_map/ppermute | solution.py:405

commit v21 on v20

--- a/solution.py
+++ b/solution.py
@@ -342,7 +342,21 @@
     by_core(body)
 
 
-def late_kernel(theirs_own, sent_chip, low, high, energy, amp_ref, my_half, other_half, my_part, other_new):
+def late_kernel(
+    mine_chip,
+    theirs_chip,
+    theirs_own,
+    sent_chip,
+    low,
+    high,
+    my_low,
+    energy,
+    amp_ref,
+    my_half,
+    other_half,
+    my_part,
+    other_new,
+):
     rows = amp_ref.shape[2]
 
     def body(core):
@@ -353,23 +367,48 @@
         )
         rate = energy[1 - my] * turned(other_half[...]) + change
         other_new[...] = (amp_ref[1 - my] + time_step * rate).T
-        my_part[...] = amp_ref[my] + time_step * (energy[my] * turned(my_half[...]))
+        change = expand(rows_of(((mine_chip, theirs_chip)[core],), core, rows), my_low[...])
+        my_part[...] = amp_ref[my] + time_step * (energy[my] * turned(my_half[...]) + change)
 
     by_core(body)
 
 
-def last_kernel(mine_chip, theirs_chip, low, high, my_part, other_new, new_tgt, new_proj):
-    rows = my_part.shape[1]
+def last_kernel(
+    mine_chip, theirs_chip, high, my_part, other_new, new_tgt, new_proj, my_new, sems
+):
+    cols, rows = my_part.shape
+    my = my_kind()
+    parts = 2
+    size = rows // parts
+    outs = (new_tgt, new_proj.at[0])
+
+    def copies(kind):
+        return [pltpu.make_async_copy(other_new, outs[1 - kind], sems.at[parts])] + [
+            pltpu.make_async_copy(
+                my_new.at[pl.ds(part * size, size)], outs[kind].at[pl.ds(part * size, size)], sems.at[part]
+            )
+            for part in range(parts)
+        ]
+
+    def start(number):
+        for kind in range(2):
+
+            @pl.when(my == kind)
+            def _():
+                copies(kind)[number].start()
 
     def body(core):
-        near, far = (low, high) if core == 0 else (high, low)
-        change = expand(rows_of((mine_chip,), core, rows), near[...]) + expand(
-            rows_of((theirs_chip,), core, rows), far[...]
-        )
-        my_new = (my_part[...] + time_step * change).T
-        new_tgt[...], new_proj[0] = ordered(my_kind(), my_new, other_new[...])
-
+        basis = rows_of(((theirs_chip, mine_chip)[core],), core, rows)
+        for part in range(parts):
+            states = slice(part * size, (part + 1) * size)
+            change = expand([block[states] for block in basis], high[...])
+            my_new[states, :] = (my_part[:, states] + time_step * change).T
+            start(1 + part)
+
+    start(0)
     by_core(body)
+    for copy in copies(0):
+        copy.wait()
 
 
 def shards(
@@ -387,12 +426,12 @@
     rows, two_cols = tgt_amp.shape
     sizes = [lax.axis_size(axis) for axis in DEVICES]
 
-    def call(kernel, out_shape, in_specs, scratch_shapes=(), cost=None):
+    def call(kernel, out_shape, in_specs, scratch_shapes=(), cost=None, out_spec=VMEM):
         return pl.pallas_call(
             kernel,
             out_shape=out_shape,
             in_specs=in_specs,
-            out_specs=[VMEM] * len(out_shape),
+            out_specs=[out_spec] * len(out_shape),
             scratch_shapes=scratch_shapes,
             cost_estimate=cost,
             compiler_params=pltpu.CompilerParams(vmem_limit_bytes=VMEM_LIMIT),
@@ -535,30 +574,31 @@
     other_half = other_core(half_send)
     fields = summed(halves, n_steps)
     low, high = swapped(fields)
+    low, high = swapped(fields)
     my_part, other_new = run(
         late_kernel,
         [segment, in_vmem((rows, two_cols), jnp.float32)],
+        mine_chip,
+        theirs_chip,
         theirs_own,
         sent[0],
         *fields,
+        low,
         energy,
         amp,
         my_half,
         other_half,
     )
-    return run(
+    return call(
         last_kernel,
         [
             jax.ShapeDtypeStruct(tgt_amp.shape, jnp.float32),
             jax.ShapeDtypeStruct(proj_amp.shape, jnp.float32),
         ],
-        mine_chip,
-        theirs_chip,
-        low,
-        high,
-        my_part,
-        other_new,
-    )
+        [VMEM] * 5,
+        [pltpu.VMEM((rows, two_cols), jnp.float32), pltpu.SemaphoreType.DMA((3,))],
+        out_spec=HBM,
+    )(mine_chip, theirs_chip, high, my_part, other_new)
 
 
 def solution(mesh):

time: 35.8 us -> 35.7 us (level)
    pallas_call x13 -> x12, Pallas kernels: 3.73 us -> 2.73 us  [run(): return call(kernel, out_shape, [VMEM] * len(blocks))(*blocks)]
    pallas_call x0 -> x1, Pallas kernels: none -> 0.98 us  [shards(): call(last_kernel, [jax.ShapeDtypeStruct(tgt_amp.shape, jnp.float32), jax....]
where the time goes in v21:
time: 35.7 us; the launch traced here: 35.5 us
  starting transfers between devices  18.4 us (52%)
  waiting for transfers between devices  9 us (25%)
  Pallas kernels  7.42 us (21%)
  between operations  0.77 us (2%)
    ppermute x10, starting transfers between devices, exchanged(): return lax.ppermute(block, DEVICES, pairs)  15 us
    ppermute x10, waiting for transfers between devices, exchanged(): return lax.ppermute(block, DEVICES, pairs)  7.01 us
    ppermute x10, starting transfers between devices, other_core(): return lax.ppermute(block, 'rep', [(0, 1), (1, 0)])  3.36 us
    pallas_call x12, Pallas kernels, run(): return call(kernel, out_shape, [VMEM] * len(blocks))(*blocks)  2.73 us
    ppermute x10, waiting for transfers between devices, other_core(): return lax.ppermute(block, 'rep', [(0, 1), (1, 0)])  1.99 us
    pallas_call x1, Pallas kernels, shards(): call(functools.partial(sent_kernel, neighbours), [in_vmem((2, 2 * rows +...  1.33 us
    pallas_call x1, Pallas kernels, shards(): call(functools.partial(side_kernel, gate_levels, neighbours), [pair, pair...  1.24 us
    pallas_call x1, Pallas kernels, shards(): call(load_kernel, [in_vmem((2, 1, rows), jnp.float32), in_vmem((2, two_co...  1.14 us
  transfers between devices with their start and end apart: 20, of which 10 were waited for; matrix products, arithmetic and copies ran while one was open for 0% of the time, Pallas kernels for 17%

profile of v21, /device:TPU:0, one launch (start us, length us, event | category | flops | bytes accessed | tf_op | source)
XLA Modules:
  0.0 35.5 jit_solution(14951706060081434911)
XLA Ops:
  0.6 0.5 %collective-permute-start = (f32[256,128]{1,0:T(8,128)}, f32[256,128]{1,0:T(8,128)S(1)}, u32[]{:S(2)}, u32[]{:S(2)}) collective-permute-start(f32[256,128]{1,0:T(8,128)} %tgt_own_hbm.1), channel_id=1, source_target_pairs={{0,1},{1,0},{2,3},{3,2},{4,5},{5,4},{6,7},{7,6},{8,9},{9,8},{10,11... | collective-permute-start | bytes 393224 | tf_op jit(solution)/shard_map/ppermute | solution.py:444
  1.2 1.1 %shard_map.104 = (f32[2,1,256]{2,1,0:T(1,128)S(1)}, f32[2,128,256]{2,1,0:T(8,128)S(1)}) custom-call(f32[256]{0:T(256)} %tgt_energy_hbm.1, f32[1,256]{1,0:T(1,128)} %proj_energy_hbm.1, f32[256,128]{1,0:T(8,128)} %tgt_own_hbm.1, f32[1,256,128]{2,1,0:T(8,128)} %proj_own_hbm.1), custom_call_target="tpu_custom_call" | custom-call | flops 67108864 | bytes 4194304 | tf_op jit(solution)/shard_map/pallas_call | solution.py:484
  2.8 2.7 %collective-permute-start.4 = (bf16[2,128,256]{2,1,0:T(8,128)(2,1)S(1)}, bf16[2,128,256]{2,1,0:T(8,128)(2,1)S(1)}, u32[]{:S(2)}, u32[]{:S(2)}) collective-permute-start(bf16[2,128,256]{2,1,0:T(8,128)(2,1)S(1)} %get-tuple-element.38), channel_id=1, source_target_pairs={{0,3},{1,8},{3,0},{2,11},{5,6},{4,13},{6,5},{7,14},{9,10},{8,1},{1... | collective-permute-start | bytes 393224 | tf_op jit(solution)/shard_map/ppermute | solution.py:462
  5.5 1.3 %shard_map.107 = (bf16[2,544,256]{2,1,0:T(8,128)(2,1)S(1)}, bf16[2,512,256]{2,1,0:T(8,128)(2,1)S(1)}, bf16[2,256,256]{2,1,0:T(8,128)(2,1)S(1)}, f32[1,1,256]{2,1,0:T(1,128)S(1)}) custom-call(f32[256]{0:T(256)} %weight_hbm.1, bf16[2,4,256,256]{3,2,1,0:T(8,128)(2,1)} %bitcast.3, bf16[2,8,256,256]{3,2,1,0:T(8,128)(2,1)} %proj_hbm.3, ...), custom_call_target="tpu_custom_call" | custom-call | tf_op jit(solution)/shard_map/pallas_call | solution.py:508
  6.9 1.4 %collective-permute-start.3 = (bf16[2,512,256]{2,1,0:T(8,128)(2,1)S(1)}, bf16[2,512,256]{2,1,0:T(8,128)(2,1)S(1)}, u32[]{:S(2)}, u32[]{:S(2)}) collective-permute-start(bf16[2,512,256]{2,1,0:T(8,128)(2,1)S(1)} %get-tuple-element.34), channel_id=1, source_target_pairs={{0,1},{1,0},{2,3},{3,2},{4,5},{5,4},{6,7},{7,6},{8,9},{9,8},{10,11... | collective-permute-start | bytes 1572872 | tf_op jit(solution)/shard_map/ppermute | solution.py:444
  8.3 1.2 %shard_map.106 = (bf16[2,512,256]{2,1,0:T(8,128)(2,1)S(1)}, bf16[2,512,256]{2,1,0:T(8,128)(2,1)S(1)}, f32[3,2,1,256]{3,2,1,0:T(1,128)S(1)}) custom-call(s32[2,4]{1,0:T(2,128)} %bitcast.5, s32[2,4]{1,0:T(2,128)} %bitcast.6, bf16[2,4,256,256]{3,2,1,0:T(8,128)(2,1)} %bitcast.4, bf16[2,8,256,256]{3,2,1,0:T(8,128)(2,1)} %proj_hbm.3, ...), custom_call_target="tpu_custom_call" | custom-call | flops 34359738368 | bytes 65536 | tf_op jit(solution)/shard_map/pallas_call | solution.py:519
  9.5 1.0 %collective-permute-done.2.theirs_chip = bf16[2,544,256]{2,1,0:T(8,128)(2,1)S(1)} collective-permute-done((bf16[2,544,256]{2,1,0:T(8,128)(2,1)S(1)}, bf16[2,544,256]{2,1,0:T(8,128)(2,1)S(1)}, u32[]{:S(2)}, u32[]{:S(2)}) %collective-permute-start.2) | collective-permute-done | bytes 557088 | tf_op jit(solution)/shard_map/ppermute | solution.py:444
  11.2 1.5 %collective-permute-start.5 = (bf16[128,256]{1,0:T(8,128)(2,1)S(1)}, bf16[128,256]{1,0:T(8,128)(2,1)S(1)}, u32[]{:S(2)}, u32[]{:S(2)}) collective-permute-start(bf16[128,256]{1,0:T(8,128)(2,1)S(1)} %get-tuple-element.42.own), channel_id=1, source_target_pairs={{0,9},{1,4},{3,10},{2,7},{5,12},{4,1},{6,15},{7,2},{9,0},{8,13},{1... | collective-permute-start | bytes 196616 | tf_op jit(solution)/shard_map/ppermute | solution.py:462
  12.8 1.2 %collective-permute-start.9 = (bf16[128,256]{1,0:T(8,128)(2,1)S(1)}, bf16[128,256]{1,0:T(8,128)(2,1)S(1)}, u32[]{:S(2)}, u32[]{:S(2)}) collective-permute-start(bf16[128,256]{1,0:T(8,128)(2,1)S(1)} %get-tuple-element.44.own), channel_id=1, source_target_pairs={{0,9},{1,4},{3,10},{2,7},{5,12},{4,1},{6,15},{7,2},{9,0},{8,13},{1... | collective-permute-start | bytes 196616 | tf_op jit(solution)/shard_map/ppermute | solution.py:462
  13.9 1.4 %collective-permute-start.8 = (f32[2,1,256]{2,1,0:T(1,128)S(1)}, f32[2,1,256]{2,1,0:T(1,128)S(1)}, u32[]{:S(2)}, u32[]{:S(2)}) collective-permute-start(f32[2,1,256]{2,1,0:T(1,128)S(1)} %get-tuple-element.43.energies), channel_id=1, source_target_pairs={{0,3},{1,8},{3,0},{2,11},{5,6},{4,13},{6,5},{7,14},{9,10},{8,1},{1... | collective-permute-start | bytes 6152 | tf_op jit(solution)/shard_map/ppermute | solution.py:462
  15.4 0.6 %collective-permute-done.5.other = bf16[128,256]{1,0:T(8,128)(2,1)S(1)} collective-permute-done((bf16[128,256]{1,0:T(8,128)(2,1)S(1)}, bf16[128,256]{1,0:T(8,128)(2,1)S(1)}, u32[]{:S(2)}, u32[]{:S(2)}) %collective-permute-start.5) | collective-permute-done | bytes 65568 | tf_op jit(solution)/shard_map/ppermute | solution.py:462
  16.0 1.2 %collective-permute-start.7 = (bf16[128,256]{1,0:T(8,128)(2,1)S(1)}, bf16[128,256]{1,0:T(8,128)(2,1)S(1)}, u32[]{:S(2)}, u32[]{:S(2)}) collective-permute-start(bf16[128,256]{1,0:T(8,128)(2,1)S(1)} %shard_map.110), channel_id=1, source_target_pairs={{0,4},{1,3},{3,7},{2,0},{5,1},{4,6},{6,2},{7,5},{9,13},{8,10},{10,... | collective-permute-start | bytes 196616 | tf_op jit(solution)/shard_map/ppermute | solution.py:462
  17.2 0.6 %collective-permute-start.6 = (bf16[128,256]{1,0:T(8,128)(2,1)S(1)}, bf16[128,256]{1,0:T(8,128)(2,1)S(1)}, u32[]{:S(2)}, u32[]{:S(2)}) collective-permute-start(bf16[128,256]{1,0:T(8,128)(2,1)S(1)} %shard_map.110), channel_id=1, source_target_pairs={{0,1},{1,0},{2,3},{3,2},{4,5},{5,4},{6,7},{7,6},{8,9},{9,8},{10,11... | collective-permute-start | bytes 196616 | tf_op jit(solution)/shard_map/ppermute | solution.py:444
  18.1 1.6 %collective-permute-start.11 = (bf16[128,256]{1,0:T(8,128)(2,1)S(1)}, bf16[128,256]{1,0:T(8,128)(2,1)S(1)}, u32[]{:S(2)}, u32[]{:S(2)}) collective-permute-start(bf16[128,256]{1,0:T(8,128)(2,1)S(1)} %shard_map.112), channel_id=1, source_target_pairs={{0,4},{1,3},{3,7},{2,0},{5,1},{4,6},{6,2},{7,5},{9,13},{8,10},{10,... | collective-permute-start | bytes 196616 | tf_op jit(solution)/shard_map/ppermute | solution.py:462
  20.9 1.6 %collective-permute-done.11.high_there = bf16[128,256]{1,0:T(8,128)(2,1)S(1)} collective-permute-done((bf16[128,256]{1,0:T(8,128)(2,1)S(1)}, bf16[128,256]{1,0:T(8,128)(2,1)S(1)}, u32[]{:S(2)}, u32[]{:S(2)}) %collective-permute-start.11) | collective-permute-done | bytes 65568 | tf_op jit(solution)/shard_map/ppermute | solution.py:462
  22.4 0.8 %shard_map.113 = (bf16[128,256]{1,0:T(8,128)(2,1)S(1)}, bf16[128,256]{1,0:T(8,128)(2,1)S(1)}, f32[128,256]{1,0:T(8,128)S(1)}, f32[128,256]{1,0:T(8,128)S(1)}) custom-call(bf16[2,512,256]{2,1,0:T(8,128)(2,1)S(1)} %get-tuple-element.29.mine_chip, bf16[2,512,256]{2,1,0:T(8,128)(2,1)S(1)} %get-tuple-element.33.mine_far, ...), custom_call_target="tpu_custom_call" | custom-call | tf_op jit(solution)/shard_map/pallas_call | solution.py:441
  23.5 2.4 %collective-permute-start.12 = (bf16[128,256]{1,0:T(8,128)(2,1)S(1)}, bf16[128,256]{1,0:T(8,128)(2,1)S(1)}, u32[]{:S(2)}, u32[]{:S(2)}) collective-permute-start(bf16[128,256]{1,0:T(8,128)(2,1)S(1)} %get-tuple-element.45.own), channel_id=1, source_target_pairs={{0,9},{1,4},{3,10},{2,7},{5,12},{4,1},{6,15},{7,2},{9,0},{8,13},{1... | collective-permute-start | bytes 196616 | tf_op jit(solution)/shard_map/ppermute | solution.py:462
  25.9 1.9 %collective-permute-done.16.other = bf16[128,256]{1,0:T(8,128)(2,1)S(1)} collective-permute-done((bf16[128,256]{1,0:T(8,128)(2,1)S(1)}, bf16[128,256]{1,0:T(8,128)(2,1)S(1)}, u32[]{:S(2)}, u32[]{:S(2)}) %collective-permute-start.16) | collective-permute-done | bytes 65568 | tf_op jit(solution)/shard_map/ppermute | solution.py:462
  27.9 1.5 %collective-permute-start.17 = (bf16[128,256]{1,0:T(8,128)(2,1)S(1)}, bf16[128,256]{1,0:T(8,128)(2,1)S(1)}, u32[]{:S(2)}, u32[]{:S(2)}) collective-permute-start(bf16[128,256]{1,0:T(8,128)(2,1)S(1)} %shard_map.116.own), channel_id=1, source_target_pairs={{0,5},{1,2},{3,6},{2,1},{5,0},{4,7},{6,3},{7,4},{9,12},{8,11},{10,... | collective-permute-start | bytes 196616 | tf_op jit(solution)/shard_map/ppermute | solution.py:462
  29.5 1.2 %collective-permute-start.13 = (bf16[128,256]{1,0:T(8,128)(2,1)S(1)}, bf16[128,256]{1,0:T(8,128)(2,1)S(1)}, u32[]{:S(2)}, u32[]{:S(2)}) collective-permute-start(bf16[128,256]{1,0:T(8,128)(2,1)S(1)} %shard_map.114.own), channel_id=1, source_target_pairs={{0,5},{1,2},{3,6},{2,1},{5,0},{4,7},{6,3},{7,4},{9,12},{8,11},{10,... | collective-permute-start | bytes 196616 | tf_op jit(solution)/shard_map/ppermute | solution.py:462
  30.6 1.0 %collective-permute-done.17.other = bf16[128,256]{1,0:T(8,128)(2,1)S(1)} collective-permute-done((bf16[128,256]{1,0:T(8,128)(2,1)S(1)}, bf16[128,256]{1,0:T(8,128)(2,1)S(1)}, u32[]{:S(2)}, u32[]{:S(2)}) %collective-permute-start.17) | collective-permute-done | bytes 65568 | tf_op jit(solution)/shard_map/ppermute | solution.py:462
  31.8 1.4 %collective-permute-done.13.other = bf16[128,256]{1,0:T(8,128)(2,1)S(1)} collective-permute-done((bf16[128,256]{1,0:T(8,128)(2,1)S(1)}, bf16[128,256]{1,0:T(8,128)(2,1)S(1)}, u32[]{:S(2)}, u32[]{:S(2)}) %collective-permute-start.13) | collective-permute-done | bytes 65568 | tf_op jit(solution)/shard_map/ppermute | solution.py:462
  33.9 0.6 %collective-permute-done.14.high = bf16[128,256]{1,0:T(8,128)(2,1)S(1)} collective-permute-done((bf16[128,256]{1,0:T(8,128)(2,1)S(1)}, bf16[128,256]{1,0:T(8,128)(2,1)S(1)}, u32[]{:S(2)}, u32[]{:S(2)}) %collective-permute-start.14) | collective-permute-done | bytes 65568 | tf_op jit(solution)/shard_map/ppermute | solution.py:444
  34.6 1.0 %shard_map.119 = (f32[256,128]{1,0:T(8,128)}, f32[1,256,128]{2,1,0:T(8,128)}) custom-call(bf16[2,512,256]{2,1,0:T(8,128)(2,1)S(1)} %get-tuple-element.29.mine_chip, bf16[2,544,256]{2,1,0:T(8,128)(2,1)S(1)} %collective-permute-done.2.theirs_chip, bf16[128,256]{1,0:T(8,128)(2,1)S(1)} %collective-permute-done.14.high, ...), custom_call_target="tpu_custom_call" | custom-call | tf_op jit(solution)/shard_map/pallas_call | solution.py:592
  (32 shorter events, 3.9 us)
Async XLA Ops:
  0.6 1.7 %collective-permute-start = (f32[256,128]{1,0:T(8,128)}, f32[256,128]{1,0:T(8,128)S(1)}, u32[]{:S(2)}, u32[]{:S(2)}) collective-permute-start(f32[256,128]{1,0:T(8,128)} %tgt_own_hbm.1), channel_id=1, source_target_pairs={{0,1},{1,0},{2,3},{3,2},{4,5},{5,4},{6,7},{7,6},{8,9},{9,8},{10,11... | collective-permute-start | bytes 393224 | tf_op jit(solution)/shard_map/ppermute | solution.py:444
  1.1 1.6 %collective-permute-start.1 = (f32[1,256,128]{2,1,0:T(8,128)}, f32[1,256,128]{2,1,0:T(8,128)S(1)}, u32[]{:S(2)}, u32[]{:S(2)}) collective-permute-start(f32[1,256,128]{2,1,0:T(8,128)} %proj_own_hbm.1), channel_id=1, source_target_pairs={{0,1},{1,0},{2,3},{3,2},{4,5},{5,4},{6,7},{7,6},{8,9},{9,8},{10,11... | collective-permute-start | bytes 393224 | tf_op jit(solution)/shard_map/ppermute | solution.py:444
  2.8 8.0 %collective-permute-start.4 = (bf16[2,128,256]{2,1,0:T(8,128)(2,1)S(1)}, bf16[2,128,256]{2,1,0:T(8,128)(2,1)S(1)}, u32[]{:S(2)}, u32[]{:S(2)}) collective-permute-start(bf16[2,128,256]{2,1,0:T(8,128)(2,1)S(1)} %get-tuple-element.38), channel_id=1, source_target_pairs={{0,3},{1,8},{3,0},{2,11},{5,6},{4,13},{6,5},{7,14},{9,10},{8,1},{1... | collective-permute-start | bytes 393224 | tf_op jit(solution)/shard_map/ppermute | solution.py:462
  6.9 4.0 %collective-permute-start.3 = (bf16[2,512,256]{2,1,0:T(8,128)(2,1)S(1)}, bf16[2,512,256]{2,1,0:T(8,128)(2,1)S(1)}, u32[]{:S(2)}, u32[]{:S(2)}) collective-permute-start(bf16[2,512,256]{2,1,0:T(8,128)(2,1)S(1)} %get-tuple-element.34), channel_id=1, source_target_pairs={{0,1},{1,0},{2,3},{3,2},{4,5},{5,4},{6,7},{7,6},{8,9},{9,8},{10,11... | collective-permute-start | bytes 1572872 | tf_op jit(solution)/shard_map/ppermute | solution.py:444
  8.2 2.3 %collective-permute-start.2 = (bf16[2,544,256]{2,1,0:T(8,128)(2,1)S(1)}, bf16[2,544,256]{2,1,0:T(8,128)(2,1)S(1)}, u32[]{:S(2)}, u32[]{:S(2)}) collective-permute-start(bf16[2,544,256]{2,1,0:T(8,128)(2,1)S(1)} %get-tuple-element.31.sent_chip), channel_id=1, source_target_pairs={{0,1},{1,0},{2,3},{3,2},{4,5},{5,4},{6,7},{7,6},{8,9},{9,8},{10,11... | collective-permute-start | bytes 1671176 | tf_op jit(solution)/shard_map/ppermute | solution.py:444
  11.2 4.8 %collective-permute-start.5 = (bf16[128,256]{1,0:T(8,128)(2,1)S(1)}, bf16[128,256]{1,0:T(8,128)(2,1)S(1)}, u32[]{:S(2)}, u32[]{:S(2)}) collective-permute-start(bf16[128,256]{1,0:T(8,128)(2,1)S(1)} %get-tuple-element.42.own), channel_id=1, source_target_pairs={{0,9},{1,4},{3,10},{2,7},{5,12},{4,1},{6,15},{7,2},{9,0},{8,13},{1... | collective-permute-start | bytes 196616 | tf_op jit(solution)/shard_map/ppermute | solution.py:462
  12.8 5.3 %collective-permute-start.9 = (bf16[128,256]{1,0:T(8,128)(2,1)S(1)}, bf16[128,256]{1,0:T(8,128)(2,1)S(1)}, u32[]{:S(2)}, u32[]{:S(2)}) collective-permute-start(bf16[128,256]{1,0:T(8,128)(2,1)S(1)} %get-tuple-element.44.own), channel_id=1, source_target_pairs={{0,9},{1,4},{3,10},{2,7},{5,12},{4,1},{6,15},{7,2},{9,0},{8,13},{1... | collective-permute-start | bytes 196616 | tf_op jit(solution)/shard_map/ppermute | solution.py:462
  13.9 5.7 %collective-permute-start.8 = (f32[2,1,256]{2,1,0:T(1,128)S(1)}, f32[2,1,256]{2,1,0:T(1,128)S(1)}, u32[]{:S(2)}, u32[]{:S(2)}) collective-permute-start(f32[2,1,256]{2,1,0:T(1,128)S(1)} %get-tuple-element.43.energies), channel_id=1, source_target_pairs={{0,3},{1,8},{3,0},{2,11},{5,6},{4,13},{6,5},{7,14},{9,10},{8,1},{1... | collective-permute-start | bytes 6152 | tf_op jit(solution)/shard_map/ppermute | solution.py:462
  16.0 4.3 %collective-permute-start.7 = (bf16[128,256]{1,0:T(8,128)(2,1)S(1)}, bf16[128,256]{1,0:T(8,128)(2,1)S(1)}, u32[]{:S(2)}, u32[]{:S(2)}) collective-permute-start(bf16[128,256]{1,0:T(8,128)(2,1)S(1)} %shard_map.110), channel_id=1, source_target_pairs={{0,4},{1,3},{3,7},{2,0},{5,1},{4,6},{6,2},{7,5},{9,13},{8,10},{10,... | collective-permute-start | bytes 196616 | tf_op jit(solution)/shard_map/ppermute | solution.py:462
  17.2 3.1 %collective-permute-start.6 = (bf16[128,256]{1,0:T(8,128)(2,1)S(1)}, bf16[128,256]{1,0:T(8,128)(2,1)S(1)}, u32[]{:S(2)}, u32[]{:S(2)}) collective-permute-start(bf16[128,256]{1,0:T(8,128)(2,1)S(1)} %shard_map.110), channel_id=1, source_target_pairs={{0,1},{1,0},{2,3},{3,2},{4,5},{5,4},{6,7},{7,6},{8,9},{9,8},{10,11... | collective-permute-start | bytes 196616 | tf_op jit(solution)/shard_map/ppermute | solution.py:444
  18.1 4.3 %collective-permute-start.11 = (bf16[128,256]{1,0:T(8,128)(2,1)S(1)}, bf16[128,256]{1,0:T(8,128)(2,1)S(1)}, u32[]{:S(2)}, u32[]{:S(2)}) collective-permute-start(bf16[128,256]{1,0:T(8,128)(2,1)S(1)} %shard_map.112), channel_id=1, source_target_pairs={{0,4},{1,3},{3,7},{2,0},{5,1},{4,6},{6,2},{7,5},{9,13},{8,10},{10,... | collective-permute-start | bytes 196616 | tf_op jit(solution)/shard_map/ppermute | solution.py:462
  19.7 2.7 %collective-permute-start.10 = (bf16[128,256]{1,0:T(8,128)(2,1)S(1)}, bf16[128,256]{1,0:T(8,128)(2,1)S(1)}, u32[]{:S(2)}, u32[]{:S(2)}) collective-permute-start(bf16[128,256]{1,0:T(8,128)(2,1)S(1)} %shard_map.112), channel_id=1, source_target_pairs={{0,1},{1,0},{2,3},{3,2},{4,5},{5,4},{6,7},{7,6},{8,9},{9,8},{10,11... | collective-permute-start | bytes 196616 | tf_op jit(solution)/shard_map/ppermute | solution.py:444
  19.7 13.7 %collective-permute-start.15 = (bf16[2,256,256]{2,1,0:T(8,128)(2,1)S(1)}, bf16[2,256,256]{2,1,0:T(8,128)(2,1)S(1)}, u32[]{:S(2)}, u32[]{:S(2)}) collective-permute-start(bf16[2,256,256]{2,1,0:T(8,128)(2,1)S(1)} %get-tuple-element.46), channel_id=1, source_target_pairs={{0,1},{1,0},{2,3},{3,2},{4,5},{5,4},{6,7},{7,6},{8,9},{9,8},{10,11... | collective-permute-start | bytes 786440 | tf_op jit(solution)/shard_map/ppermute | solution.py:444
  23.2 4.7 %collective-permute-start.16 = (bf16[128,256]{1,0:T(8,128)(2,1)S(1)}, bf16[128,256]{1,0:T(8,128)(2,1)S(1)}, u32[]{:S(2)}, u32[]{:S(2)}) collective-permute-start(bf16[128,256]{1,0:T(8,128)(2,1)S(1)} %get-tuple-element.47.own), channel_id=1, source_target_pairs={{0,9},{1,4},{3,10},{2,7},{5,12},{4,1},{6,15},{7,2},{9,0},{8,13},{1... | collective-permute-start | bytes 196616 | tf_op jit(solution)/shard_map/ppermute | solution.py:462
  23.5 5.9 %collective-permute-start.12 = (bf16[128,256]{1,0:T(8,128)(2,1)S(1)}, bf16[128,256]{1,0:T(8,128)(2,1)S(1)}, u32[]{:S(2)}, u32[]{:S(2)}) collective-permute-start(bf16[128,256]{1,0:T(8,128)(2,1)S(1)} %get-tuple-element.45.own), channel_id=1, source_target_pairs={{0,9},{1,4},{3,10},{2,7},{5,12},{4,1},{6,15},{7,2},{9,0},{8,13},{1... | collective-permute-start | bytes 196616 | tf_op jit(solution)/shard_map/ppermute | solution.py:462
  25.9 7.5 %collective-permute-start.19 = (f32[128,256]{1,0:T(8,128)S(1)}, f32[128,256]{1,0:T(8,128)S(1)}, u32[]{:S(2)}, u32[]{:S(2)}) collective-permute-start(f32[128,256]{1,0:T(8,128)S(1)} %get-tuple-element.49), channel_id=1, source_target_pairs={{0,1},{1,0},{2,3},{3,2},{4,5},{5,4},{6,7},{7,6},{8,9},{9,8},{10,11... | collective-permute-start | bytes 393224 | tf_op jit(solution)/shard_map/ppermute | solution.py:444
  27.9 3.8 %collective-permute-start.17 = (bf16[128,256]{1,0:T(8,128)(2,1)S(1)}, bf16[128,256]{1,0:T(8,128)(2,1)S(1)}, u32[]{:S(2)}, u32[]{:S(2)}) collective-permute-start(bf16[128,256]{1,0:T(8,128)(2,1)S(1)} %shard_map.116.own), channel_id=1, source_target_pairs={{0,5},{1,2},{3,6},{2,1},{5,0},{4,7},{6,3},{7,4},{9,12},{8,11},{10,... | collective-permute-start | bytes 196616 | tf_op jit(solution)/shard_map/ppermute | solution.py:462
  29.5 3.8 %collective-permute-start.13 = (bf16[128,256]{1,0:T(8,128)(2,1)S(1)}, bf16[128,256]{1,0:T(8,128)(2,1)S(1)}, u32[]{:S(2)}, u32[]{:S(2)}) collective-permute-start(bf16[128,256]{1,0:T(8,128)(2,1)S(1)} %shard_map.114.own), channel_id=1, source_target_pairs={{0,5},{1,2},{3,6},{2,1},{5,0},{4,7},{6,3},{7,4},{9,12},{8,11},{10,... | collective-permute-start | bytes 196616 | tf_op jit(solution)/shard_map/ppermute | solution.py:462
  31.7 1.7 %collective-permute-start.18 = (bf16[128,256]{1,0:T(8,128)(2,1)S(1)}, bf16[128,256]{1,0:T(8,128)(2,1)S(1)}, u32[]{:S(2)}, u32[]{:S(2)}) collective-permute-start(bf16[128,256]{1,0:T(8,128)(2,1)S(1)} %shard_map.117.low), channel_id=1, source_target_pairs={{0,1},{1,0},{2,3},{3,2},{4,5},{5,4},{6,7},{7,6},{8,9},{9,8},{10,11... | collective-permute-start | bytes 196616 | tf_op jit(solution)/shard_map/ppermute | solution.py:444
  33.2 1.3 %collective-permute-start.14 = (bf16[128,256]{1,0:T(8,128)(2,1)S(1)}, bf16[128,256]{1,0:T(8,128)(2,1)S(1)}, u32[]{:S(2)}, u32[]{:S(2)}) collective-permute-start(bf16[128,256]{1,0:T(8,128)(2,1)S(1)} %shard_map.115.high), channel_id=1, source_target_pairs={{0,1},{1,0},{2,3},{3,2},{4,5},{5,4},{6,7},{7,6},{8,9},{9,8},{10,11... | collective-permute-start | bytes 196616 | tf_op jit(solution)/shard_map/ppermute | solution.py:444

commit v22 on v21

--- a/solution.py
+++ b/solution.py
@@ -480,7 +480,14 @@
     def in_hbm(*blocks):
         return [pltpu.with_memory_space_constraint(block, pltpu.HBM) for block in blocks]
 
-    others = swapped([tgt_amp, proj_amp])
+    def handed(kind, block):
+        pairs = []
+        for place in range(n_tgt * n_prj):
+            to_core = kind ^ parity(place)
+            pairs.append((place * n_core + 1 - to_core, place * n_core + to_core))
+        return lax.ppermute(block, DEVICES, pairs)
+
+    others = handed(0, tgt_amp), handed(1, proj_amp)
     energy, amp = call(
         load_kernel,
         [in_vmem((2, 1, rows), jnp.float32), in_vmem((2, two_cols, rows), jnp.float32)],

time: 35.7 us -> 39.5 us (1.11)
  starting transfers between devices: 18.4 us -> 21.5 us
  waiting for transfers between devices: 9 us -> 9.57 us
    ppermute x0 -> x2, starting transfers between devices: none -> 4.33 us  [handed(): return lax.ppermute(block, DEVICES, pairs)]
    ppermute x10, starting transfers between devices: 15 us -> 14 us  [exchanged(): return lax.ppermute(block, DEVICES, pairs)]
    ppermute x10, waiting for transfers between devices: 7.01 us -> 7.79 us  [exchanged(): return lax.ppermute(block, DEVICES, pairs)]
    ppermute x10 -> x8, starting transfers between devices: 3.36 us -> 3.13 us  [other_core(): return lax.ppermute(block, 'rep', [(0, 1), (1, 0)])]
    ppermute x10 -> x8, waiting for transfers between devices: 1.99 us -> 1.76 us  [other_core(): return lax.ppermute(block, 'rep', [(0, 1), (1, 0)])]
  transfers between devices with their start and end apart: 20 -> 20, of which waited for: 10 -> 10; matrix products, arithmetic and copies ran while one was open for 0% -> 0% of each run, Pallas kernels for 17% -> 15%
where the time goes in v22:
time: 39.5 us; the launch traced here: 39.3 us
  starting transfers between devices  21.5 us (54%)
  waiting for transfers between devices  9.57 us (24%)
  Pallas kernels  7.42 us (19%)
  between operations  0.81 us (2%)
    ppermute x10, starting transfers between devices, exchanged(): return lax.ppermute(block, DEVICES, pairs)  14 us
    ppermute x10, waiting for transfers between devices, exchanged(): return lax.ppermute(block, DEVICES, pairs)  7.79 us
    ppermute x2, starting transfers between devices, handed(): return lax.ppermute(block, DEVICES, pairs)  4.33 us
    ppermute x8, starting transfers between devices, other_core(): return lax.ppermute(block, 'rep', [(0, 1), (1, 0)])  3.13 us
    pallas_call x12, Pallas kernels, run(): return call(kernel, out_shape, [VMEM] * len(blocks))(*blocks)  2.73 us
    ppermute x8, waiting for transfers between devices, other_core(): return lax.ppermute(block, 'rep', [(0, 1), (1, 0)])  1.76 us
    pallas_call x1, Pallas kernels, shards(): call(functools.partial(sent_kernel, neighbours), [in_vmem((2, 2 * rows +...  1.33 us
    pallas_call x1, Pallas kernels, shards(): call(functools.partial(side_kernel, gate_levels, neighbours), [pair, pair...  1.24 us
  transfers between devices with their start and end apart: 20, of which 10 were waited for; matrix products, arithmetic and copies ran while one was open for 0% of the time, Pallas kernels for 15%

profile of v22, /device:TPU:0, one launch (start us, length us, event | category | flops | bytes accessed | tf_op | source)
XLA Modules:
  0.0 39.3 jit_solution(885971688721700973)
XLA Ops:
  0.6 1.3 %collective-permute-start = (f32[256,128]{1,0:T(8,128)}, f32[256,128]{1,0:T(8,128)S(1)}, u32[]{:S(2)}, u32[]{:S(2)}) collective-permute-start(f32[256,128]{1,0:T(8,128)} %tgt_own_hbm.1), channel_id=1, source_target_pairs={{1,0},{2,3},{4,5},{7,6},{8,9},{11,10},{13,12},{14,15},{17,16},{18,... | collective-permute-start | bytes 393224 | tf_op jit(solution)/shard_map/ppermute | solution.py:488
  1.9 3.0 %collective-permute-start.1 = (f32[1,256,128]{2,1,0:T(8,128)}, f32[1,256,128]{2,1,0:T(8,128)S(1)}, u32[]{:S(2)}, u32[]{:S(2)}) collective-permute-start(f32[1,256,128]{2,1,0:T(8,128)} %proj_own_hbm.1), channel_id=1, source_target_pairs={{0,1},{3,2},{5,4},{6,7},{9,8},{10,11},{12,13},{15,14},{16,17},{19,... | collective-permute-start | bytes 393224 | tf_op jit(solution)/shard_map/ppermute | solution.py:488
  5.0 1.1 %shard_map.104 = (f32[2,1,256]{2,1,0:T(1,128)S(1)}, f32[2,128,256]{2,1,0:T(8,128)S(1)}) custom-call(f32[256]{0:T(256)} %tgt_energy_hbm.1, f32[1,256]{1,0:T(1,128)} %proj_energy_hbm.1, f32[256,128]{1,0:T(8,128)} %tgt_own_hbm.1, f32[1,256,128]{2,1,0:T(8,128)} %proj_own_hbm.1), custom_call_target="tpu_custom_call" | custom-call | flops 67108864 | bytes 4194304 | tf_op jit(solution)/shard_map/pallas_call | solution.py:491
  6.3 2.4 %collective-permute-start.4 = (bf16[2,128,256]{2,1,0:T(8,128)(2,1)S(1)}, bf16[2,128,256]{2,1,0:T(8,128)(2,1)S(1)}, u32[]{:S(2)}, u32[]{:S(2)}) collective-permute-start(bf16[2,128,256]{2,1,0:T(8,128)(2,1)S(1)} %get-tuple-element.38), channel_id=1, source_target_pairs={{0,3},{1,8},{3,0},{2,11},{5,6},{4,13},{6,5},{7,14},{9,10},{8,1},{1... | collective-permute-start | bytes 393224 | tf_op jit(solution)/shard_map/ppermute | solution.py:462
  8.7 1.3 %shard_map.107 = (bf16[2,544,256]{2,1,0:T(8,128)(2,1)S(1)}, bf16[2,512,256]{2,1,0:T(8,128)(2,1)S(1)}, bf16[2,256,256]{2,1,0:T(8,128)(2,1)S(1)}, f32[1,1,256]{2,1,0:T(1,128)S(1)}) custom-call(f32[256]{0:T(256)} %weight_hbm.1, bf16[2,4,256,256]{3,2,1,0:T(8,128)(2,1)} %bitcast.3, bf16[2,8,256,256]{3,2,1,0:T(8,128)(2,1)} %proj_hbm.3, ...), custom_call_target="tpu_custom_call" | custom-call | tf_op jit(solution)/shard_map/pallas_call | solution.py:515
  10.1 1.5 %collective-permute-start.3 = (bf16[2,512,256]{2,1,0:T(8,128)(2,1)S(1)}, bf16[2,512,256]{2,1,0:T(8,128)(2,1)S(1)}, u32[]{:S(2)}, u32[]{:S(2)}) collective-permute-start(bf16[2,512,256]{2,1,0:T(8,128)(2,1)S(1)} %get-tuple-element.34), channel_id=1, source_target_pairs={{0,1},{1,0},{2,3},{3,2},{4,5},{5,4},{6,7},{7,6},{8,9},{9,8},{10,11... | collective-permute-start | bytes 1572872 | tf_op jit(solution)/shard_map/ppermute | solution.py:444
  11.7 1.2 %shard_map.106 = (bf16[2,512,256]{2,1,0:T(8,128)(2,1)S(1)}, bf16[2,512,256]{2,1,0:T(8,128)(2,1)S(1)}, f32[3,2,1,256]{3,2,1,0:T(1,128)S(1)}) custom-call(s32[2,4]{1,0:T(2,128)} %bitcast.5, s32[2,4]{1,0:T(2,128)} %bitcast.6, bf16[2,4,256,256]{3,2,1,0:T(8,128)(2,1)} %bitcast.4, bf16[2,8,256,256]{3,2,1,0:T(8,128)(2,1)} %proj_hbm.3, ...), custom_call_target="tpu_custom_call" | custom-call | flops 34359738368 | bytes 65536 | tf_op jit(solution)/shard_map/pallas_call | solution.py:526
  12.9 1.0 %collective-permute-done.2.theirs_chip = bf16[2,544,256]{2,1,0:T(8,128)(2,1)S(1)} collective-permute-done((bf16[2,544,256]{2,1,0:T(8,128)(2,1)S(1)}, bf16[2,544,256]{2,1,0:T(8,128)(2,1)S(1)}, u32[]{:S(2)}, u32[]{:S(2)}) %collective-permute-start.2) | collective-permute-done | bytes 557088 | tf_op jit(solution)/shard_map/ppermute | solution.py:444
  14.6 1.8 %collective-permute-start.5 = (bf16[128,256]{1,0:T(8,128)(2,1)S(1)}, bf16[128,256]{1,0:T(8,128)(2,1)S(1)}, u32[]{:S(2)}, u32[]{:S(2)}) collective-permute-start(bf16[128,256]{1,0:T(8,128)(2,1)S(1)} %get-tuple-element.42.own), channel_id=1, source_target_pairs={{0,9},{1,4},{3,10},{2,7},{5,12},{4,1},{6,15},{7,2},{9,0},{8,13},{1... | collective-permute-start | bytes 196616 | tf_op jit(solution)/shard_map/ppermute | solution.py:462
  16.5 0.9 %collective-permute-start.9 = (bf16[128,256]{1,0:T(8,128)(2,1)S(1)}, bf16[128,256]{1,0:T(8,128)(2,1)S(1)}, u32[]{:S(2)}, u32[]{:S(2)}) collective-permute-start(bf16[128,256]{1,0:T(8,128)(2,1)S(1)} %get-tuple-element.44.own), channel_id=1, source_target_pairs={{0,9},{1,4},{3,10},{2,7},{5,12},{4,1},{6,15},{7,2},{9,0},{8,13},{1... | collective-permute-start | bytes 196616 | tf_op jit(solution)/shard_map/ppermute | solution.py:462
  17.3 1.8 %collective-permute-start.8 = (f32[2,1,256]{2,1,0:T(1,128)S(1)}, f32[2,1,256]{2,1,0:T(1,128)S(1)}, u32[]{:S(2)}, u32[]{:S(2)}) collective-permute-start(f32[2,1,256]{2,1,0:T(1,128)S(1)} %get-tuple-element.43.energies), channel_id=1, source_target_pairs={{0,3},{1,8},{3,0},{2,11},{5,6},{4,13},{6,5},{7,14},{9,10},{8,1},{1... | collective-permute-start | bytes 6152 | tf_op jit(solution)/shard_map/ppermute | solution.py:462
  19.4 1.6 %collective-permute-start.7 = (bf16[128,256]{1,0:T(8,128)(2,1)S(1)}, bf16[128,256]{1,0:T(8,128)(2,1)S(1)}, u32[]{:S(2)}, u32[]{:S(2)}) collective-permute-start(bf16[128,256]{1,0:T(8,128)(2,1)S(1)} %shard_map.110), channel_id=1, source_target_pairs={{0,4},{1,3},{3,7},{2,0},{5,1},{4,6},{6,2},{7,5},{9,13},{8,10},{10,... | collective-permute-start | bytes 196616 | tf_op jit(solution)/shard_map/ppermute | solution.py:462
  21.0 0.9 %collective-permute-start.6 = (bf16[128,256]{1,0:T(8,128)(2,1)S(1)}, bf16[128,256]{1,0:T(8,128)(2,1)S(1)}, u32[]{:S(2)}, u32[]{:S(2)}) collective-permute-start(bf16[128,256]{1,0:T(8,128)(2,1)S(1)} %shard_map.110), channel_id=1, source_target_pairs={{0,1},{1,0},{2,3},{3,2},{4,5},{5,4},{6,7},{7,6},{8,9},{9,8},{10,11... | collective-permute-start | bytes 196616 | tf_op jit(solution)/shard_map/ppermute | solution.py:444
  21.9 1.1 %collective-permute-start.11 = (bf16[128,256]{1,0:T(8,128)(2,1)S(1)}, bf16[128,256]{1,0:T(8,128)(2,1)S(1)}, u32[]{:S(2)}, u32[]{:S(2)}) collective-permute-start(bf16[128,256]{1,0:T(8,128)(2,1)S(1)} %shard_map.112), channel_id=1, source_target_pairs={{0,4},{1,3},{3,7},{2,0},{5,1},{4,6},{6,2},{7,5},{9,13},{8,10},{10,... | collective-permute-start | bytes 196616 | tf_op jit(solution)/shard_map/ppermute | solution.py:462
  24.3 2.0 %collective-permute-done.11.high_there = bf16[128,256]{1,0:T(8,128)(2,1)S(1)} collective-permute-done((bf16[128,256]{1,0:T(8,128)(2,1)S(1)}, bf16[128,256]{1,0:T(8,128)(2,1)S(1)}, u32[]{:S(2)}, u32[]{:S(2)}) %collective-permute-start.11) | collective-permute-done | bytes 65568 | tf_op jit(solution)/shard_map/ppermute | solution.py:462
  26.3 0.8 %shard_map.113 = (bf16[128,256]{1,0:T(8,128)(2,1)S(1)}, bf16[128,256]{1,0:T(8,128)(2,1)S(1)}, f32[128,256]{1,0:T(8,128)S(1)}, f32[128,256]{1,0:T(8,128)S(1)}) custom-call(bf16[2,512,256]{2,1,0:T(8,128)(2,1)S(1)} %get-tuple-element.29.mine_chip, bf16[2,512,256]{2,1,0:T(8,128)(2,1)S(1)} %get-tuple-element.33.mine_far, ...), custom_call_target="tpu_custom_call" | custom-call | tf_op jit(solution)/shard_map/pallas_call | solution.py:441
  27.4 2.4 %collective-permute-start.12 = (bf16[128,256]{1,0:T(8,128)(2,1)S(1)}, bf16[128,256]{1,0:T(8,128)(2,1)S(1)}, u32[]{:S(2)}, u32[]{:S(2)}) collective-permute-start(bf16[128,256]{1,0:T(8,128)(2,1)S(1)} %get-tuple-element.45.own), channel_id=1, source_target_pairs={{0,9},{1,4},{3,10},{2,7},{5,12},{4,1},{6,15},{7,2},{9,0},{8,13},{1... | collective-permute-start | bytes 196616 | tf_op jit(solution)/shard_map/ppermute | solution.py:462
  29.8 2.3 %collective-permute-done.16.other = bf16[128,256]{1,0:T(8,128)(2,1)S(1)} collective-permute-done((bf16[128,256]{1,0:T(8,128)(2,1)S(1)}, bf16[128,256]{1,0:T(8,128)(2,1)S(1)}, u32[]{:S(2)}, u32[]{:S(2)}) %collective-permute-start.16) | collective-permute-done | bytes 65568 | tf_op jit(solution)/shard_map/ppermute | solution.py:462
  32.6 0.6 %collective-permute-done.12.other = bf16[128,256]{1,0:T(8,128)(2,1)S(1)} collective-permute-done((bf16[128,256]{1,0:T(8,128)(2,1)S(1)}, bf16[128,256]{1,0:T(8,128)(2,1)S(1)}, u32[]{:S(2)}, u32[]{:S(2)}) %collective-permute-start.12) | collective-permute-done | bytes 65568 | tf_op jit(solution)/shard_map/ppermute | solution.py:462
  33.2 1.2 %collective-permute-start.13 = (bf16[128,256]{1,0:T(8,128)(2,1)S(1)}, bf16[128,256]{1,0:T(8,128)(2,1)S(1)}, u32[]{:S(2)}, u32[]{:S(2)}) collective-permute-start(bf16[128,256]{1,0:T(8,128)(2,1)S(1)} %shard_map.114.own), channel_id=1, source_target_pairs={{0,5},{1,2},{3,6},{2,1},{5,0},{4,7},{6,3},{7,4},{9,12},{8,11},{10,... | collective-permute-start | bytes 196616 | tf_op jit(solution)/shard_map/ppermute | solution.py:462
  34.4 1.5 %collective-permute-done.17.other = bf16[128,256]{1,0:T(8,128)(2,1)S(1)} collective-permute-done((bf16[128,256]{1,0:T(8,128)(2,1)S(1)}, bf16[128,256]{1,0:T(8,128)(2,1)S(1)}, u32[]{:S(2)}, u32[]{:S(2)}) %collective-permute-start.17) | collective-permute-done | bytes 65568 | tf_op jit(solution)/shard_map/ppermute | solution.py:462
  36.0 1.0 %collective-permute-done.13.other = bf16[128,256]{1,0:T(8,128)(2,1)S(1)} collective-permute-done((bf16[128,256]{1,0:T(8,128)(2,1)S(1)}, bf16[128,256]{1,0:T(8,128)(2,1)S(1)}, u32[]{:S(2)}, u32[]{:S(2)}) %collective-permute-start.13) | collective-permute-done | bytes 65568 | tf_op jit(solution)/shard_map/ppermute | solution.py:462
  37.7 0.6 %collective-permute-done.14.high = bf16[128,256]{1,0:T(8,128)(2,1)S(1)} collective-permute-done((bf16[128,256]{1,0:T(8,128)(2,1)S(1)}, bf16[128,256]{1,0:T(8,128)(2,1)S(1)}, u32[]{:S(2)}, u32[]{:S(2)}) %collective-permute-start.14) | collective-permute-done | bytes 65568 | tf_op jit(solution)/shard_map/ppermute | solution.py:444
  38.3 1.0 %shard_map.119 = (f32[256,128]{1,0:T(8,128)}, f32[1,256,128]{2,1,0:T(8,128)}) custom-call(bf16[2,512,256]{2,1,0:T(8,128)(2,1)S(1)} %get-tuple-element.29.mine_chip, bf16[2,544,256]{2,1,0:T(8,128)(2,1)S(1)} %collective-permute-done.2.theirs_chip, bf16[128,256]{1,0:T(8,128)(2,1)S(1)} %collective-permute-done.14.high, ...), custom_call_target="tpu_custom_call" | custom-call | tf_op jit(solution)/shard_map/pallas_call | solution.py:599
  (32 shorter events, 4.0 us)
Async XLA Ops:
  0.6 5.5 %collective-permute-start = (f32[256,128]{1,0:T(8,128)}, f32[256,128]{1,0:T(8,128)S(1)}, u32[]{:S(2)}, u32[]{:S(2)}) collective-permute-start(f32[256,128]{1,0:T(8,128)} %tgt_own_hbm.1), channel_id=1, source_target_pairs={{1,0},{2,3},{4,5},{7,6},{8,9},{11,10},{13,12},{14,15},{17,16},{18,... | collective-permute-start | bytes 393224 | tf_op jit(solution)/shard_map/ppermute | solution.py:488
  1.9 4.2 %collective-permute-start.1 = (f32[1,256,128]{2,1,0:T(8,128)}, f32[1,256,128]{2,1,0:T(8,128)S(1)}, u32[]{:S(2)}, u32[]{:S(2)}) collective-permute-start(f32[1,256,128]{2,1,0:T(8,128)} %proj_own_hbm.1), channel_id=1, source_target_pairs={{0,1},{3,2},{5,4},{6,7},{9,8},{10,11},{12,13},{15,14},{16,17},{19,... | collective-permute-start | bytes 393224 | tf_op jit(solution)/shard_map/ppermute | solution.py:488
  6.3 8.0 %collective-permute-start.4 = (bf16[2,128,256]{2,1,0:T(8,128)(2,1)S(1)}, bf16[2,128,256]{2,1,0:T(8,128)(2,1)S(1)}, u32[]{:S(2)}, u32[]{:S(2)}) collective-permute-start(bf16[2,128,256]{2,1,0:T(8,128)(2,1)S(1)} %get-tuple-element.38), channel_id=1, source_target_pairs={{0,3},{1,8},{3,0},{2,11},{5,6},{4,13},{6,5},{7,14},{9,10},{8,1},{1... | collective-permute-start | bytes 393224 | tf_op jit(solution)/shard_map/ppermute | solution.py:462
  10.1 4.2 %collective-permute-start.3 = (bf16[2,512,256]{2,1,0:T(8,128)(2,1)S(1)}, bf16[2,512,256]{2,1,0:T(8,128)(2,1)S(1)}, u32[]{:S(2)}, u32[]{:S(2)}) collective-permute-start(bf16[2,512,256]{2,1,0:T(8,128)(2,1)S(1)} %get-tuple-element.34), channel_id=1, source_target_pairs={{0,1},{1,0},{2,3},{3,2},{4,5},{5,4},{6,7},{7,6},{8,9},{9,8},{10,11... | collective-permute-start | bytes 1572872 | tf_op jit(solution)/shard_map/ppermute | solution.py:444
  11.6 2.3 %collective-permute-start.2 = (bf16[2,544,256]{2,1,0:T(8,128)(2,1)S(1)}, bf16[2,544,256]{2,1,0:T(8,128)(2,1)S(1)}, u32[]{:S(2)}, u32[]{:S(2)}) collective-permute-start(bf16[2,544,256]{2,1,0:T(8,128)(2,1)S(1)} %get-tuple-element.31.sent_chip), channel_id=1, source_target_pairs={{0,1},{1,0},{2,3},{3,2},{4,5},{5,4},{6,7},{7,6},{8,9},{9,8},{10,11... | collective-permute-start | bytes 1671176 | tf_op jit(solution)/shard_map/ppermute | solution.py:444
  14.6 4.8 %collective-permute-start.5 = (bf16[128,256]{1,0:T(8,128)(2,1)S(1)}, bf16[128,256]{1,0:T(8,128)(2,1)S(1)}, u32[]{:S(2)}, u32[]{:S(2)}) collective-permute-start(bf16[128,256]{1,0:T(8,128)(2,1)S(1)} %get-tuple-element.42.own), channel_id=1, source_target_pairs={{0,9},{1,4},{3,10},{2,7},{5,12},{4,1},{6,15},{7,2},{9,0},{8,13},{1... | collective-permute-start | bytes 196616 | tf_op jit(solution)/shard_map/ppermute | solution.py:462
  16.5 5.5 %collective-permute-start.9 = (bf16[128,256]{1,0:T(8,128)(2,1)S(1)}, bf16[128,256]{1,0:T(8,128)(2,1)S(1)}, u32[]{:S(2)}, u32[]{:S(2)}) collective-permute-start(bf16[128,256]{1,0:T(8,128)(2,1)S(1)} %get-tuple-element.44.own), channel_id=1, source_target_pairs={{0,9},{1,4},{3,10},{2,7},{5,12},{4,1},{6,15},{7,2},{9,0},{8,13},{1... | collective-permute-start | bytes 196616 | tf_op jit(solution)/shard_map/ppermute | solution.py:462
  17.3 6.0 %collective-permute-start.8 = (f32[2,1,256]{2,1,0:T(1,128)S(1)}, f32[2,1,256]{2,1,0:T(1,128)S(1)}, u32[]{:S(2)}, u32[]{:S(2)}) collective-permute-start(f32[2,1,256]{2,1,0:T(1,128)S(1)} %get-tuple-element.43.energies), channel_id=1, source_target_pairs={{0,3},{1,8},{3,0},{2,11},{5,6},{4,13},{6,5},{7,14},{9,10},{8,1},{1... | collective-permute-start | bytes 6152 | tf_op jit(solution)/shard_map/ppermute | solution.py:462
  19.4 4.3 %collective-permute-start.7 = (bf16[128,256]{1,0:T(8,128)(2,1)S(1)}, bf16[128,256]{1,0:T(8,128)(2,1)S(1)}, u32[]{:S(2)}, u32[]{:S(2)}) collective-permute-start(bf16[128,256]{1,0:T(8,128)(2,1)S(1)} %shard_map.110), channel_id=1, source_target_pairs={{0,4},{1,3},{3,7},{2,0},{5,1},{4,6},{6,2},{7,5},{9,13},{8,10},{10,... | collective-permute-start | bytes 196616 | tf_op jit(solution)/shard_map/ppermute | solution.py:462
  21.0 2.7 %collective-permute-start.6 = (bf16[128,256]{1,0:T(8,128)(2,1)S(1)}, bf16[128,256]{1,0:T(8,128)(2,1)S(1)}, u32[]{:S(2)}, u32[]{:S(2)}) collective-permute-start(bf16[128,256]{1,0:T(8,128)(2,1)S(1)} %shard_map.110), channel_id=1, source_target_pairs={{0,1},{1,0},{2,3},{3,2},{4,5},{5,4},{6,7},{7,6},{8,9},{9,8},{10,11... | collective-permute-start | bytes 196616 | tf_op jit(solution)/shard_map/ppermute | solution.py:444
  21.9 4.3 %collective-permute-start.11 = (bf16[128,256]{1,0:T(8,128)(2,1)S(1)}, bf16[128,256]{1,0:T(8,128)(2,1)S(1)}, u32[]{:S(2)}, u32[]{:S(2)}) collective-permute-start(bf16[128,256]{1,0:T(8,128)(2,1)S(1)} %shard_map.112), channel_id=1, source_target_pairs={{0,4},{1,3},{3,7},{2,0},{5,1},{4,6},{6,2},{7,5},{9,13},{8,10},{10,... | collective-permute-start | bytes 196616 | tf_op jit(solution)/shard_map/ppermute | solution.py:462
  23.1 3.2 %collective-permute-start.10 = (bf16[128,256]{1,0:T(8,128)(2,1)S(1)}, bf16[128,256]{1,0:T(8,128)(2,1)S(1)}, u32[]{:S(2)}, u32[]{:S(2)}) collective-permute-start(bf16[128,256]{1,0:T(8,128)(2,1)S(1)} %shard_map.112), channel_id=1, source_target_pairs={{0,1},{1,0},{2,3},{3,2},{4,5},{5,4},{6,7},{7,6},{8,9},{9,8},{10,11... | collective-permute-start | bytes 196616 | tf_op jit(solution)/shard_map/ppermute | solution.py:444
  23.4 13.7 %collective-permute-start.15 = (bf16[2,256,256]{2,1,0:T(8,128)(2,1)S(1)}, bf16[2,256,256]{2,1,0:T(8,128)(2,1)S(1)}, u32[]{:S(2)}, u32[]{:S(2)}) collective-permute-start(bf16[2,256,256]{2,1,0:T(8,128)(2,1)S(1)} %get-tuple-element.46), channel_id=1, source_target_pairs={{0,1},{1,0},{2,3},{3,2},{4,5},{5,4},{6,7},{7,6},{8,9},{9,8},{10,11... | collective-permute-start | bytes 786440 | tf_op jit(solution)/shard_map/ppermute | solution.py:444
  27.1 5.0 %collective-permute-start.16 = (bf16[128,256]{1,0:T(8,128)(2,1)S(1)}, bf16[128,256]{1,0:T(8,128)(2,1)S(1)}, u32[]{:S(2)}, u32[]{:S(2)}) collective-permute-start(bf16[128,256]{1,0:T(8,128)(2,1)S(1)} %get-tuple-element.47.own), channel_id=1, source_target_pairs={{0,9},{1,4},{3,10},{2,7},{5,12},{4,1},{6,15},{7,2},{9,0},{8,13},{1... | collective-permute-start | bytes 196616 | tf_op jit(solution)/shard_map/ppermute | solution.py:462
  27.4 5.8 %collective-permute-start.12 = (bf16[128,256]{1,0:T(8,128)(2,1)S(1)}, bf16[128,256]{1,0:T(8,128)(2,1)S(1)}, u32[]{:S(2)}, u32[]{:S(2)}) collective-permute-start(bf16[128,256]{1,0:T(8,128)(2,1)S(1)} %get-tuple-element.45.own), channel_id=1, source_target_pairs={{0,9},{1,4},{3,10},{2,7},{5,12},{4,1},{6,15},{7,2},{9,0},{8,13},{1... | collective-permute-start | bytes 196616 | tf_op jit(solution)/shard_map/ppermute | solution.py:462
  29.8 7.3 %collective-permute-start.19 = (f32[128,256]{1,0:T(8,128)S(1)}, f32[128,256]{1,0:T(8,128)S(1)}, u32[]{:S(2)}, u32[]{:S(2)}) collective-permute-start(f32[128,256]{1,0:T(8,128)S(1)} %get-tuple-element.49), channel_id=1, source_target_pairs={{0,1},{1,0},{2,3},{3,2},{4,5},{5,4},{6,7},{7,6},{8,9},{9,8},{10,11... | collective-permute-start | bytes 393224 | tf_op jit(solution)/shard_map/ppermute | solution.py:444
  32.1 3.8 %collective-permute-start.17 = (bf16[128,256]{1,0:T(8,128)(2,1)S(1)}, bf16[128,256]{1,0:T(8,128)(2,1)S(1)}, u32[]{:S(2)}, u32[]{:S(2)}) collective-permute-start(bf16[128,256]{1,0:T(8,128)(2,1)S(1)} %shard_map.116.own), channel_id=1, source_target_pairs={{0,5},{1,2},{3,6},{2,1},{5,0},{4,7},{6,3},{7,4},{9,12},{8,11},{10,... | collective-permute-start | bytes 196616 | tf_op jit(solution)/shard_map/ppermute | solution.py:462
  33.2 3.8 %collective-permute-start.13 = (bf16[128,256]{1,0:T(8,128)(2,1)S(1)}, bf16[128,256]{1,0:T(8,128)(2,1)S(1)}, u32[]{:S(2)}, u32[]{:S(2)}) collective-permute-start(bf16[128,256]{1,0:T(8,128)(2,1)S(1)} %shard_map.114.own), channel_id=1, source_target_pairs={{0,5},{1,2},{3,6},{2,1},{5,0},{4,7},{6,3},{7,4},{9,12},{8,11},{10,... | collective-permute-start | bytes 196616 | tf_op jit(solution)/shard_map/ppermute | solution.py:462
  35.9 1.3 %collective-permute-start.18 = (bf16[128,256]{1,0:T(8,128)(2,1)S(1)}, bf16[128,256]{1,0:T(8,128)(2,1)S(1)}, u32[]{:S(2)}, u32[]{:S(2)}) collective-permute-start(bf16[128,256]{1,0:T(8,128)(2,1)S(1)} %shard_map.117.low), channel_id=1, source_target_pairs={{0,1},{1,0},{2,3},{3,2},{4,5},{5,4},{6,7},{7,6},{8,9},{9,8},{10,11... | collective-permute-start | bytes 196616 | tf_op jit(solution)/shard_map/ppermute | solution.py:444
  37.0 1.3 %collective-permute-start.14 = (bf16[128,256]{1,0:T(8,128)(2,1)S(1)}, bf16[128,256]{1,0:T(8,128)(2,1)S(1)}, u32[]{:S(2)}, u32[]{:S(2)}) collective-permute-start(bf16[128,256]{1,0:T(8,128)(2,1)S(1)} %shard_map.115.high), channel_id=1, source_target_pairs={{0,1},{1,0},{2,3},{3,2},{4,5},{5,4},{6,7},{7,6},{8,9},{9,8},{10,11... | collective-permute-start | bytes 196616 | tf_op jit(solution)/shard_map/ppermute | solution.py:444

commit v23 on v21

--- a/solution.py
+++ b/solution.py
@@ -16,16 +16,16 @@
 
 
 def parity(place):
-    odd = 0
+    even = 1
     while place:
-        odd, place = odd ^ (place & 1), place >> 1
-    return odd
+        even, place = even ^ (place & 1), place >> 1
+    return even
 
 
 def my_kind():
     n_tgt, n_prj = lax.axis_size("tgt"), lax.axis_size("prj")
     place = lax.axis_index("tgt") * n_prj + lax.axis_index("prj")
-    kind = lax.axis_index("rep")
+    kind = 1 - lax.axis_index("rep")
     for bit in range((n_tgt * n_prj).bit_length() - 1):
         kind = jnp.bitwise_xor(kind, jnp.bitwise_and(lax.shift_right_logical(place, bit), 1))
     return kind

time: 35.7 us -> 35.9 us (level)
  starting transfers between devices: 18.4 us -> 21.9 us
  waiting for transfers between devices: 9 us -> 5.64 us
    ppermute x10, waiting for transfers between devices: 7.01 us -> 3.95 us  [exchanged(): return lax.ppermute(block, DEVICES, pairs)]
    ppermute x10, starting transfers between devices: 3.36 us -> 6.2 us  [other_core(): return lax.ppermute(block, 'rep', [(0, 1), (1, 0)])]
    ppermute x10, starting transfers between devices: 15 us -> 15.7 us  [exchanged(): return lax.ppermute(block, DEVICES, pairs)]
  transfers between devices with their start and end apart: 20 -> 20, of which waited for: 10 -> 8; matrix products, arithmetic and copies ran while one was open for 0% -> 0% of each run, Pallas kernels for 17% -> 17%
where the time goes in v23:
time: 35.9 us; the launch traced here: 35.7 us
  starting transfers between devices  21.9 us (61%)
  Pallas kernels  7.44 us (21%)
  waiting for transfers between devices  5.64 us (16%)
  between operations  0.77 us (2%)
    ppermute x10, starting transfers between devices, exchanged(): return lax.ppermute(block, DEVICES, pairs)  15.7 us
    ppermute x10, starting transfers between devices, other_core(): return lax.ppermute(block, 'rep', [(0, 1), (1, 0)])  6.2 us
    ppermute x10, waiting for transfers between devices, exchanged(): return lax.ppermute(block, DEVICES, pairs)  3.95 us
    pallas_call x12, Pallas kernels, run(): return call(kernel, out_shape, [VMEM] * len(blocks))(*blocks)  2.76 us
    ppermute x10, waiting for transfers between devices, other_core(): return lax.ppermute(block, 'rep', [(0, 1), (1, 0)])  1.69 us
    pallas_call x1, Pallas kernels, shards(): call(functools.partial(sent_kernel, neighbours), [in_vmem((2, 2 * rows +...  1.33 us
    pallas_call x1, Pallas kernels, shards(): call(functools.partial(side_kernel, gate_levels, neighbours), [pair, pair...  1.24 us
    pallas_call x1, Pallas kernels, shards(): call(load_kernel, [in_vmem((2, 1, rows), jnp.float32), in_vmem((2, two_co...  1.14 us
  transfers between devices with their start and end apart: 20, of which 8 were waited for; matrix products, arithmetic and copies ran while one was open for 0% of the time, Pallas kernels for 17%

profile of v23, /device:TPU:0, one launch (start us, length us, event | category | flops | bytes accessed | tf_op | source)
XLA Modules:
  0.0 35.7 jit_solution(14948068132891008850)
XLA Ops:
  0.6 0.5 %collective-permute-start = (f32[256,128]{1,0:T(8,128)}, f32[256,128]{1,0:T(8,128)S(1)}, u32[]{:S(2)}, u32[]{:S(2)}) collective-permute-start(f32[256,128]{1,0:T(8,128)} %tgt_own_hbm.1), channel_id=1, source_target_pairs={{0,1},{1,0},{2,3},{3,2},{4,5},{5,4},{6,7},{7,6},{8,9},{9,8},{10,11... | collective-permute-start | bytes 393224 | tf_op jit(solution)/shard_map/ppermute | solution.py:444
  1.2 1.1 %shard_map.104 = (f32[2,1,256]{2,1,0:T(1,128)S(1)}, f32[2,128,256]{2,1,0:T(8,128)S(1)}) custom-call(f32[256]{0:T(256)} %tgt_energy_hbm.1, f32[1,256]{1,0:T(1,128)} %proj_energy_hbm.1, f32[256,128]{1,0:T(8,128)} %tgt_own_hbm.1, f32[1,256,128]{2,1,0:T(8,128)} %proj_own_hbm.1), custom_call_target="tpu_custom_call" | custom-call | flops 67108864 | bytes 4194304 | tf_op jit(solution)/shard_map/pallas_call | solution.py:484
  2.8 3.8 %collective-permute-start.4 = (bf16[2,128,256]{2,1,0:T(8,128)(2,1)S(1)}, bf16[2,128,256]{2,1,0:T(8,128)(2,1)S(1)}, u32[]{:S(2)}, u32[]{:S(2)}) collective-permute-start(bf16[2,128,256]{2,1,0:T(8,128)(2,1)S(1)} %get-tuple-element.38), channel_id=1, source_target_pairs={{1,2},{0,9},{2,1},{3,10},{4,7},{5,12},{7,4},{6,15},{8,11},{9,0},{1... | collective-permute-start | bytes 393224 | tf_op jit(solution)/shard_map/ppermute | solution.py:462
  6.6 1.3 %shard_map.107 = (bf16[2,544,256]{2,1,0:T(8,128)(2,1)S(1)}, bf16[2,512,256]{2,1,0:T(8,128)(2,1)S(1)}, bf16[2,256,256]{2,1,0:T(8,128)(2,1)S(1)}, f32[1,1,256]{2,1,0:T(1,128)S(1)}) custom-call(f32[256]{0:T(256)} %weight_hbm.1, bf16[2,4,256,256]{3,2,1,0:T(8,128)(2,1)} %bitcast.3, bf16[2,8,256,256]{3,2,1,0:T(8,128)(2,1)} %proj_hbm.3, ...), custom_call_target="tpu_custom_call" | custom-call | tf_op jit(solution)/shard_map/pallas_call | solution.py:508
  8.0 0.5 %collective-permute-start.2 = (bf16[2,544,256]{2,1,0:T(8,128)(2,1)S(1)}, bf16[2,544,256]{2,1,0:T(8,128)(2,1)S(1)}, u32[]{:S(2)}, u32[]{:S(2)}) collective-permute-start(bf16[2,544,256]{2,1,0:T(8,128)(2,1)S(1)} %get-tuple-element.31.sent_chip), channel_id=1, source_target_pairs={{0,1},{1,0},{2,3},{3,2},{4,5},{5,4},{6,7},{7,6},{8,9},{9,8},{10,11... | collective-permute-start | bytes 1671176 | tf_op jit(solution)/shard_map/ppermute | solution.py:444
  8.5 1.2 %shard_map.106 = (bf16[2,512,256]{2,1,0:T(8,128)(2,1)S(1)}, bf16[2,512,256]{2,1,0:T(8,128)(2,1)S(1)}, f32[3,2,1,256]{3,2,1,0:T(1,128)S(1)}) custom-call(s32[2,4]{1,0:T(2,128)} %bitcast.5, s32[2,4]{1,0:T(2,128)} %bitcast.6, bf16[2,4,256,256]{3,2,1,0:T(8,128)(2,1)} %bitcast.4, bf16[2,8,256,256]{3,2,1,0:T(8,128)(2,1)} %proj_hbm.3, ...), custom_call_target="tpu_custom_call" | custom-call | flops 34359738368 | bytes 65536 | tf_op jit(solution)/shard_map/pallas_call | solution.py:519
  9.8 0.9 %collective-permute-done.2.theirs_chip = bf16[2,544,256]{2,1,0:T(8,128)(2,1)S(1)} collective-permute-done((bf16[2,544,256]{2,1,0:T(8,128)(2,1)S(1)}, bf16[2,544,256]{2,1,0:T(8,128)(2,1)S(1)}, u32[]{:S(2)}, u32[]{:S(2)}) %collective-permute-start.2) | collective-permute-done | bytes 557088 | tf_op jit(solution)/shard_map/ppermute | solution.py:444
  11.4 1.4 %collective-permute-start.5 = (bf16[128,256]{1,0:T(8,128)(2,1)S(1)}, bf16[128,256]{1,0:T(8,128)(2,1)S(1)}, u32[]{:S(2)}, u32[]{:S(2)}) collective-permute-start(bf16[128,256]{1,0:T(8,128)(2,1)S(1)} %get-tuple-element.42.own), channel_id=1, source_target_pairs={{1,8},{0,5},{2,11},{3,6},{4,13},{5,0},{7,14},{6,3},{8,1},{9,12},{1... | collective-permute-start | bytes 196616 | tf_op jit(solution)/shard_map/ppermute | solution.py:462
  13.2 1.9 %collective-permute-start.8 = (f32[2,1,256]{2,1,0:T(1,128)S(1)}, f32[2,1,256]{2,1,0:T(1,128)S(1)}, u32[]{:S(2)}, u32[]{:S(2)}) collective-permute-start(f32[2,1,256]{2,1,0:T(1,128)S(1)} %get-tuple-element.43.energies), channel_id=1, source_target_pairs={{1,2},{0,9},{2,1},{3,10},{4,7},{5,12},{7,4},{6,15},{8,11},{9,0},{1... | collective-permute-start | bytes 6152 | tf_op jit(solution)/shard_map/ppermute | solution.py:462
  15.2 2.4 %collective-permute-start.7 = (bf16[128,256]{1,0:T(8,128)(2,1)S(1)}, bf16[128,256]{1,0:T(8,128)(2,1)S(1)}, u32[]{:S(2)}, u32[]{:S(2)}) collective-permute-start(bf16[128,256]{1,0:T(8,128)(2,1)S(1)} %shard_map.110), channel_id=1, source_target_pairs={{1,5},{0,2},{2,6},{3,1},{4,0},{5,7},{7,3},{6,4},{8,12},{9,11},{11,... | collective-permute-start | bytes 196616 | tf_op jit(solution)/shard_map/ppermute | solution.py:462
  17.6 1.2 %collective-permute-start.11 = (bf16[128,256]{1,0:T(8,128)(2,1)S(1)}, bf16[128,256]{1,0:T(8,128)(2,1)S(1)}, u32[]{:S(2)}, u32[]{:S(2)}) collective-permute-start(bf16[128,256]{1,0:T(8,128)(2,1)S(1)} %shard_map.112), channel_id=1, source_target_pairs={{1,5},{0,2},{2,6},{3,1},{4,0},{5,7},{7,3},{6,4},{8,12},{9,11},{11,... | collective-permute-start | bytes 196616 | tf_op jit(solution)/shard_map/ppermute | solution.py:462
  19.3 1.0 %collective-permute-done.7.low_there = bf16[128,256]{1,0:T(8,128)(2,1)S(1)} collective-permute-done((bf16[128,256]{1,0:T(8,128)(2,1)S(1)}, bf16[128,256]{1,0:T(8,128)(2,1)S(1)}, u32[]{:S(2)}, u32[]{:S(2)}) %collective-permute-start.7) | collective-permute-done | bytes 65568 | tf_op jit(solution)/shard_map/ppermute | solution.py:462
  20.3 0.5 %shard_map.111.states_ref = f32[4,128,256]{2,1,0:T(8,128)S(1)} custom-call(bf16[2,512,256]{2,1,0:T(8,128)(2,1)S(1)} %get-tuple-element.29.mine_chip, bf16[2,512,256]{2,1,0:T(8,128)(2,1)S(1)} %get-tuple-element.33.mine_far, bf16[2,544,256]{2,1,0:T(8,128)(2,1)S(1)} %collective-permute-done.2.theirs_chip, ...), custom_call_target="tpu_custom_call" | custom-call | tf_op jit(solution)/shard_map/pallas_call | solution.py:441
  20.9 1.0 %collective-permute-done.11.high_there = bf16[128,256]{1,0:T(8,128)(2,1)S(1)} collective-permute-done((bf16[128,256]{1,0:T(8,128)(2,1)S(1)}, bf16[128,256]{1,0:T(8,128)(2,1)S(1)}, u32[]{:S(2)}, u32[]{:S(2)}) %collective-permute-start.11) | collective-permute-done | bytes 65568 | tf_op jit(solution)/shard_map/ppermute | solution.py:462
  21.9 0.8 %shard_map.113 = (bf16[128,256]{1,0:T(8,128)(2,1)S(1)}, bf16[128,256]{1,0:T(8,128)(2,1)S(1)}, f32[128,256]{1,0:T(8,128)S(1)}, f32[128,256]{1,0:T(8,128)S(1)}) custom-call(bf16[2,512,256]{2,1,0:T(8,128)(2,1)S(1)} %get-tuple-element.29.mine_chip, bf16[2,512,256]{2,1,0:T(8,128)(2,1)S(1)} %get-tuple-element.33.mine_far, ...), custom_call_target="tpu_custom_call" | custom-call | tf_op jit(solution)/shard_map/pallas_call | solution.py:441
  23.2 1.4 %collective-permute-start.12 = (bf16[128,256]{1,0:T(8,128)(2,1)S(1)}, bf16[128,256]{1,0:T(8,128)(2,1)S(1)}, u32[]{:S(2)}, u32[]{:S(2)}) collective-permute-start(bf16[128,256]{1,0:T(8,128)(2,1)S(1)} %get-tuple-element.45.own), channel_id=1, source_target_pairs={{1,8},{0,5},{2,11},{3,6},{4,13},{5,0},{7,14},{6,3},{8,1},{9,12},{1... | collective-permute-start | bytes 196616 | tf_op jit(solution)/shard_map/ppermute | solution.py:462
  24.5 1.0 %collective-permute-start.19 = (f32[128,256]{1,0:T(8,128)S(1)}, f32[128,256]{1,0:T(8,128)S(1)}, u32[]{:S(2)}, u32[]{:S(2)}) collective-permute-start(f32[128,256]{1,0:T(8,128)S(1)} %get-tuple-element.49), channel_id=1, source_target_pairs={{0,1},{1,0},{2,3},{3,2},{4,5},{5,4},{6,7},{7,6},{8,9},{9,8},{10,11... | collective-permute-start | bytes 393224 | tf_op jit(solution)/shard_map/ppermute | solution.py:444
  25.5 1.0 %collective-permute-done.16.other = bf16[128,256]{1,0:T(8,128)(2,1)S(1)} collective-permute-done((bf16[128,256]{1,0:T(8,128)(2,1)S(1)}, bf16[128,256]{1,0:T(8,128)(2,1)S(1)}, u32[]{:S(2)}, u32[]{:S(2)}) %collective-permute-start.16) | collective-permute-done | bytes 65568 | tf_op jit(solution)/shard_map/ppermute | solution.py:462
  26.5 1.2 %collective-permute-start.17 = (bf16[128,256]{1,0:T(8,128)(2,1)S(1)}, bf16[128,256]{1,0:T(8,128)(2,1)S(1)}, u32[]{:S(2)}, u32[]{:S(2)}) collective-permute-start(bf16[128,256]{1,0:T(8,128)(2,1)S(1)} %shard_map.116.own), channel_id=1, source_target_pairs={{1,4},{0,3},{2,7},{3,0},{4,1},{5,6},{7,2},{6,5},{8,13},{9,10},{11,... | collective-permute-start | bytes 196616 | tf_op jit(solution)/shard_map/ppermute | solution.py:462
  27.9 1.7 %collective-permute-start.13 = (bf16[128,256]{1,0:T(8,128)(2,1)S(1)}, bf16[128,256]{1,0:T(8,128)(2,1)S(1)}, u32[]{:S(2)}, u32[]{:S(2)}) collective-permute-start(bf16[128,256]{1,0:T(8,128)(2,1)S(1)} %shard_map.114.own), channel_id=1, source_target_pairs={{1,4},{0,3},{2,7},{3,0},{4,1},{5,6},{7,2},{6,5},{8,13},{9,10},{11,... | collective-permute-start | bytes 196616 | tf_op jit(solution)/shard_map/ppermute | solution.py:462
  29.6 0.7 %collective-permute-done.17.other = bf16[128,256]{1,0:T(8,128)(2,1)S(1)} collective-permute-done((bf16[128,256]{1,0:T(8,128)(2,1)S(1)}, bf16[128,256]{1,0:T(8,128)(2,1)S(1)}, u32[]{:S(2)}, u32[]{:S(2)}) %collective-permute-start.17) | collective-permute-done | bytes 65568 | tf_op jit(solution)/shard_map/ppermute | solution.py:462
  30.3 1.5 %collective-permute-start.18 = (bf16[128,256]{1,0:T(8,128)(2,1)S(1)}, bf16[128,256]{1,0:T(8,128)(2,1)S(1)}, u32[]{:S(2)}, u32[]{:S(2)}) collective-permute-start(bf16[128,256]{1,0:T(8,128)(2,1)S(1)} %shard_map.117.low), channel_id=1, source_target_pairs={{0,1},{1,0},{2,3},{3,2},{4,5},{5,4},{6,7},{7,6},{8,9},{9,8},{10,11... | collective-permute-start | bytes 196616 | tf_op jit(solution)/shard_map/ppermute | solution.py:444
  31.9 2.0 %collective-permute-start.14 = (bf16[128,256]{1,0:T(8,128)(2,1)S(1)}, bf16[128,256]{1,0:T(8,128)(2,1)S(1)}, u32[]{:S(2)}, u32[]{:S(2)}) collective-permute-start(bf16[128,256]{1,0:T(8,128)(2,1)S(1)} %shard_map.115.high), channel_id=1, source_target_pairs={{0,1},{1,0},{2,3},{3,2},{4,5},{5,4},{6,7},{7,6},{8,9},{9,8},{10,11... | collective-permute-start | bytes 196616 | tf_op jit(solution)/shard_map/ppermute | solution.py:444
  34.8 1.0 %shard_map.119 = (f32[256,128]{1,0:T(8,128)}, f32[1,256,128]{2,1,0:T(8,128)}) custom-call(bf16[2,512,256]{2,1,0:T(8,128)(2,1)S(1)} %get-tuple-element.29.mine_chip, bf16[2,544,256]{2,1,0:T(8,128)(2,1)S(1)} %collective-permute-done.2.theirs_chip, bf16[128,256]{1,0:T(8,128)(2,1)S(1)} %collective-permute-done.14.high, ...), custom_call_target="tpu_custom_call" | custom-call | tf_op jit(solution)/shard_map/pallas_call | solution.py:592
  (32 shorter events, 3.9 us)
Async XLA Ops:
  0.6 1.7 %collective-permute-start = (f32[256,128]{1,0:T(8,128)}, f32[256,128]{1,0:T(8,128)S(1)}, u32[]{:S(2)}, u32[]{:S(2)}) collective-permute-start(f32[256,128]{1,0:T(8,128)} %tgt_own_hbm.1), channel_id=1, source_target_pairs={{0,1},{1,0},{2,3},{3,2},{4,5},{5,4},{6,7},{7,6},{8,9},{9,8},{10,11... | collective-permute-start | bytes 393224 | tf_op jit(solution)/shard_map/ppermute | solution.py:444
  1.1 1.6 %collective-permute-start.1 = (f32[1,256,128]{2,1,0:T(8,128)}, f32[1,256,128]{2,1,0:T(8,128)S(1)}, u32[]{:S(2)}, u32[]{:S(2)}) collective-permute-start(f32[1,256,128]{2,1,0:T(8,128)} %proj_own_hbm.1), channel_id=1, source_target_pairs={{0,1},{1,0},{2,3},{3,2},{4,5},{5,4},{6,7},{7,6},{8,9},{9,8},{10,11... | collective-permute-start | bytes 393224 | tf_op jit(solution)/shard_map/ppermute | solution.py:444
  2.8 8.2 %collective-permute-start.4 = (bf16[2,128,256]{2,1,0:T(8,128)(2,1)S(1)}, bf16[2,128,256]{2,1,0:T(8,128)(2,1)S(1)}, u32[]{:S(2)}, u32[]{:S(2)}) collective-permute-start(bf16[2,128,256]{2,1,0:T(8,128)(2,1)S(1)} %get-tuple-element.38), channel_id=1, source_target_pairs={{1,2},{0,9},{2,1},{3,10},{4,7},{5,12},{7,4},{6,15},{8,11},{9,0},{1... | collective-permute-start | bytes 393224 | tf_op jit(solution)/shard_map/ppermute | solution.py:462
  8.0 3.1 %collective-permute-start.3 = (bf16[2,512,256]{2,1,0:T(8,128)(2,1)S(1)}, bf16[2,512,256]{2,1,0:T(8,128)(2,1)S(1)}, u32[]{:S(2)}, u32[]{:S(2)}) collective-permute-start(bf16[2,512,256]{2,1,0:T(8,128)(2,1)S(1)} %get-tuple-element.34), channel_id=1, source_target_pairs={{0,1},{1,0},{2,3},{3,2},{4,5},{5,4},{6,7},{7,6},{8,9},{9,8},{10,11... | collective-permute-start | bytes 1572872 | tf_op jit(solution)/shard_map/ppermute | solution.py:444
  8.0 2.7 %collective-permute-start.2 = (bf16[2,544,256]{2,1,0:T(8,128)(2,1)S(1)}, bf16[2,544,256]{2,1,0:T(8,128)(2,1)S(1)}, u32[]{:S(2)}, u32[]{:S(2)}) collective-permute-start(bf16[2,544,256]{2,1,0:T(8,128)(2,1)S(1)} %get-tuple-element.31.sent_chip), channel_id=1, source_target_pairs={{0,1},{1,0},{2,3},{3,2},{4,5},{5,4},{6,7},{7,6},{8,9},{9,8},{10,11... | collective-permute-start | bytes 1671176 | tf_op jit(solution)/shard_map/ppermute | solution.py:444
  11.4 3.8 %collective-permute-start.5 = (bf16[128,256]{1,0:T(8,128)(2,1)S(1)}, bf16[128,256]{1,0:T(8,128)(2,1)S(1)}, u32[]{:S(2)}, u32[]{:S(2)}) collective-permute-start(bf16[128,256]{1,0:T(8,128)(2,1)S(1)} %get-tuple-element.42.own), channel_id=1, source_target_pairs={{1,8},{0,5},{2,11},{3,6},{4,13},{5,0},{7,14},{6,3},{8,1},{9,12},{1... | collective-permute-start | bytes 196616 | tf_op jit(solution)/shard_map/ppermute | solution.py:462
  12.8 4.7 %collective-permute-start.9 = (bf16[128,256]{1,0:T(8,128)(2,1)S(1)}, bf16[128,256]{1,0:T(8,128)(2,1)S(1)}, u32[]{:S(2)}, u32[]{:S(2)}) collective-permute-start(bf16[128,256]{1,0:T(8,128)(2,1)S(1)} %get-tuple-element.44.own), channel_id=1, source_target_pairs={{1,8},{0,5},{2,11},{3,6},{4,13},{5,0},{7,14},{6,3},{8,1},{9,12},{1... | collective-permute-start | bytes 196616 | tf_op jit(solution)/shard_map/ppermute | solution.py:462
  13.2 6.0 %collective-permute-start.8 = (f32[2,1,256]{2,1,0:T(1,128)S(1)}, f32[2,1,256]{2,1,0:T(1,128)S(1)}, u32[]{:S(2)}, u32[]{:S(2)}) collective-permute-start(f32[2,1,256]{2,1,0:T(1,128)S(1)} %get-tuple-element.43.energies), channel_id=1, source_target_pairs={{1,2},{0,9},{2,1},{3,10},{4,7},{5,12},{7,4},{6,15},{8,11},{9,0},{1... | collective-permute-start | bytes 6152 | tf_op jit(solution)/shard_map/ppermute | solution.py:462
  15.2 5.1 %collective-permute-start.7 = (bf16[128,256]{1,0:T(8,128)(2,1)S(1)}, bf16[128,256]{1,0:T(8,128)(2,1)S(1)}, u32[]{:S(2)}, u32[]{:S(2)}) collective-permute-start(bf16[128,256]{1,0:T(8,128)(2,1)S(1)} %shard_map.110), channel_id=1, source_target_pairs={{1,5},{0,2},{2,6},{3,1},{4,0},{5,7},{7,3},{6,4},{8,12},{9,11},{11,... | collective-permute-start | bytes 196616 | tf_op jit(solution)/shard_map/ppermute | solution.py:462
  17.6 2.8 %collective-permute-start.6 = (bf16[128,256]{1,0:T(8,128)(2,1)S(1)}, bf16[128,256]{1,0:T(8,128)(2,1)S(1)}, u32[]{:S(2)}, u32[]{:S(2)}) collective-permute-start(bf16[128,256]{1,0:T(8,128)(2,1)S(1)} %shard_map.110), channel_id=1, source_target_pairs={{0,1},{1,0},{2,3},{3,2},{4,5},{5,4},{6,7},{7,6},{8,9},{9,8},{10,11... | collective-permute-start | bytes 196616 | tf_op jit(solution)/shard_map/ppermute | solution.py:444
  17.6 4.3 %collective-permute-start.11 = (bf16[128,256]{1,0:T(8,128)(2,1)S(1)}, bf16[128,256]{1,0:T(8,128)(2,1)S(1)}, u32[]{:S(2)}, u32[]{:S(2)}) collective-permute-start(bf16[128,256]{1,0:T(8,128)(2,1)S(1)} %shard_map.112), channel_id=1, source_target_pairs={{1,5},{0,2},{2,6},{3,1},{4,0},{5,7},{7,3},{6,4},{8,12},{9,11},{11,... | collective-permute-start | bytes 196616 | tf_op jit(solution)/shard_map/ppermute | solution.py:462
  18.8 3.1 %collective-permute-start.10 = (bf16[128,256]{1,0:T(8,128)(2,1)S(1)}, bf16[128,256]{1,0:T(8,128)(2,1)S(1)}, u32[]{:S(2)}, u32[]{:S(2)}) collective-permute-start(bf16[128,256]{1,0:T(8,128)(2,1)S(1)} %shard_map.112), channel_id=1, source_target_pairs={{0,1},{1,0},{2,3},{3,2},{4,5},{5,4},{6,7},{7,6},{8,9},{9,8},{10,11... | collective-permute-start | bytes 196616 | tf_op jit(solution)/shard_map/ppermute | solution.py:444
  19.3 14.6 %collective-permute-start.15 = (bf16[2,256,256]{2,1,0:T(8,128)(2,1)S(1)}, bf16[2,256,256]{2,1,0:T(8,128)(2,1)S(1)}, u32[]{:S(2)}, u32[]{:S(2)}) collective-permute-start(bf16[2,256,256]{2,1,0:T(8,128)(2,1)S(1)} %get-tuple-element.46), channel_id=1, source_target_pairs={{0,1},{1,0},{2,3},{3,2},{4,5},{5,4},{6,7},{7,6},{8,9},{9,8},{10,11... | collective-permute-start | bytes 786440 | tf_op jit(solution)/shard_map/ppermute | solution.py:444
  22.7 3.8 %collective-permute-start.16 = (bf16[128,256]{1,0:T(8,128)(2,1)S(1)}, bf16[128,256]{1,0:T(8,128)(2,1)S(1)}, u32[]{:S(2)}, u32[]{:S(2)}) collective-permute-start(bf16[128,256]{1,0:T(8,128)(2,1)S(1)} %get-tuple-element.47.own), channel_id=1, source_target_pairs={{1,8},{0,5},{2,11},{3,6},{4,13},{5,0},{7,14},{6,3},{8,1},{9,12},{1... | collective-permute-start | bytes 196616 | tf_op jit(solution)/shard_map/ppermute | solution.py:462
  23.2 4.7 %collective-permute-start.12 = (bf16[128,256]{1,0:T(8,128)(2,1)S(1)}, bf16[128,256]{1,0:T(8,128)(2,1)S(1)}, u32[]{:S(2)}, u32[]{:S(2)}) collective-permute-start(bf16[128,256]{1,0:T(8,128)(2,1)S(1)} %get-tuple-element.45.own), channel_id=1, source_target_pairs={{1,8},{0,5},{2,11},{3,6},{4,13},{5,0},{7,14},{6,3},{8,1},{9,12},{1... | collective-permute-start | bytes 196616 | tf_op jit(solution)/shard_map/ppermute | solution.py:462
  24.5 9.3 %collective-permute-start.19 = (f32[128,256]{1,0:T(8,128)S(1)}, f32[128,256]{1,0:T(8,128)S(1)}, u32[]{:S(2)}, u32[]{:S(2)}) collective-permute-start(f32[128,256]{1,0:T(8,128)S(1)} %get-tuple-element.49), channel_id=1, source_target_pairs={{0,1},{1,0},{2,3},{3,2},{4,5},{5,4},{6,7},{7,6},{8,9},{9,8},{10,11... | collective-permute-start | bytes 393224 | tf_op jit(solution)/shard_map/ppermute | solution.py:444
  26.5 3.8 %collective-permute-start.17 = (bf16[128,256]{1,0:T(8,128)(2,1)S(1)}, bf16[128,256]{1,0:T(8,128)(2,1)S(1)}, u32[]{:S(2)}, u32[]{:S(2)}) collective-permute-start(bf16[128,256]{1,0:T(8,128)(2,1)S(1)} %shard_map.116.own), channel_id=1, source_target_pairs={{1,4},{0,3},{2,7},{3,0},{4,1},{5,6},{7,2},{6,5},{8,13},{9,10},{11,... | collective-permute-start | bytes 196616 | tf_op jit(solution)/shard_map/ppermute | solution.py:462
  27.9 3.9 %collective-permute-start.13 = (bf16[128,256]{1,0:T(8,128)(2,1)S(1)}, bf16[128,256]{1,0:T(8,128)(2,1)S(1)}, u32[]{:S(2)}, u32[]{:S(2)}) collective-permute-start(bf16[128,256]{1,0:T(8,128)(2,1)S(1)} %shard_map.114.own), channel_id=1, source_target_pairs={{1,4},{0,3},{2,7},{3,0},{4,1},{5,6},{7,2},{6,5},{8,13},{9,10},{11,... | collective-permute-start | bytes 196616 | tf_op jit(solution)/shard_map/ppermute | solution.py:462
  30.3 3.6 %collective-permute-start.18 = (bf16[128,256]{1,0:T(8,128)(2,1)S(1)}, bf16[128,256]{1,0:T(8,128)(2,1)S(1)}, u32[]{:S(2)}, u32[]{:S(2)}) collective-permute-start(bf16[128,256]{1,0:T(8,128)(2,1)S(1)} %shard_map.117.low), channel_id=1, source_target_pairs={{0,1},{1,0},{2,3},{3,2},{4,5},{5,4},{6,7},{7,6},{8,9},{9,8},{10,11... | collective-permute-start | bytes 196616 | tf_op jit(solution)/shard_map/ppermute | solution.py:444
  31.9 2.9 %collective-permute-start.14 = (bf16[128,256]{1,0:T(8,128)(2,1)S(1)}, bf16[128,256]{1,0:T(8,128)(2,1)S(1)}, u32[]{:S(2)}, u32[]{:S(2)}) collective-permute-start(bf16[128,256]{1,0:T(8,128)(2,1)S(1)} %shard_map.115.high), channel_id=1, source_target_pairs={{0,1},{1,0},{2,3},{3,2},{4,5},{5,4},{6,7},{7,6},{8,9},{9,8},{10,11... | collective-permute-start | bytes 196616 | tf_op jit(solution)/shard_map/ppermute | solution.py:444

commit v24 on v21

--- a/solution.py
+++ b/solution.py
@@ -92,6 +92,10 @@
 def joined(block):
     pieces = f32(block)
     return pieces[0:1] + pieces[1:2] + pieces[2:3]
+
+
+def both(basis, rows):
+    return basis.at[:, : 2 * rows], basis.at[:, 2 * rows : 4 * rows]
 
 
 def basis_copies(bases, sem, my, neighbours, sources):
@@ -147,33 +151,15 @@
         message[segment] = bf16(amps[segment])
 
 
-def sent_kernel(
-    neighbours,
-    weight_hbm,
-    tgt_hbm,
-    proj_hbm,
-    chip_amp,
-    energy,
-    sent_chip,
-    sent_far,
-    sent_own,
-    weight,
-    flat_weight,
-    sems,
-):
+def sent_kernel(neighbours, weight_hbm, tgt_hbm, proj_hbm, chip_amp, energy, sent, weight, flat_weight, sems):
     my = my_kind()
     sources = (tgt_hbm, proj_hbm)
     rows = chip_amp.shape[2]
 
     def copies_of(kind):
-        own = pltpu.make_async_copy(
-            sources[kind].at[:, 2 * lax.axis_index(("prj", "tgt")[kind]) + 1 - lax.axis_index("rep")],
-            sent_own,
-            sems.at[4],
-        )
-        return basis_copies((sent_chip, sent_far), sems, 1 - kind, neighbours, sources) + [own]
-
-    weight_copy = pltpu.make_async_copy(weight_hbm, flat_weight, sems.at[5])
+        return basis_copies(both(sent, rows), sems, 1 - kind, neighbours, sources)
+
+    weight_copy = pltpu.make_async_copy(weight_hbm, flat_weight, sems.at[4])
     weight_copy.start()
     for kind in range(2):
 
@@ -185,8 +171,8 @@
     weight_copy.wait()
     weight[0] = flat_weight[...][None, :]
     for part in range(2):
-        sent_chip[part, 2 * rows : 2 * rows + PIECES] = split(weight[0])
-        sent_chip[part, 2 * rows + PIECES :, :rows] = split(energy[1 - my])
+        sent[part, 4 * rows : 4 * rows + PIECES] = split(weight[0])
+        sent[part, 4 * rows + PIECES :, :rows] = split(energy[1 - my])
     for copy in copies_of(0):
         copy.wait()
 
@@ -201,6 +187,7 @@
     chip_amp,
     mine_chip,
     mine_far,
+    send_own,
     gate,
     flags,
     counts,
@@ -239,31 +226,35 @@
                 )
     for copy in basis_copies((mine_chip, mine_far), sems, 0, neighbours, sources):
         copy.wait()
-
-
-def chip_kernel(mine_chip, theirs_chip, chip_amp, weight, energy, part_ref, weights, energies):
-    mine, theirs = (mine_chip,), (theirs_chip,)
+    core = lax.axis_index("rep")
+    rows = send_own.shape[1]
+    for part in range(2):
+        send_own[part] = mine_chip[part, pl.ds(pl.multiple_of((1 - core) * rows, rows), rows), :]
+
+
+def chip_kernel(mine_chip, theirs, chip_amp, weight, energy, part_ref, weights, energies):
     rows = chip_amp.shape[2]
+    near, far = (mine_chip,), both(theirs, rows)
 
     def body(core):
-        for half, basis in enumerate((mine, theirs) if core == 0 else (theirs, mine)):
+        for half, basis in enumerate((near, far) if core == 0 else (far, near)):
             part_ref[half] = sum(
                 project(rows_of(basis, segment, rows), chip_amp[segment]) for segment in range(2)
             )
         weights[core] = weight[0]
-        weights[1 - core] = joined(theirs_chip[0, 2 * rows : 2 * rows + PIECES, :])
+        weights[1 - core] = joined(theirs[0, 4 * rows : 4 * rows + PIECES, :])
         energies[core] = energy[my_kind()]
-        energies[1 - core] = joined(theirs_chip[0, 2 * rows + PIECES :, :rows])
+        energies[1 - core] = joined(theirs[0, 4 * rows + PIECES :, :rows])
 
     by_core(body)
 
 
-def first_kernel(mine_far, theirs_far, gate, weights, part_ref, message, *outs):
-    mine, theirs = (None, mine_far), (None, theirs_far)
+def first_kernel(mine_far, theirs, gate, weights, part_ref, message, *outs):
     rows = message.shape[2]
+    near, far = (None, mine_far), both(theirs, rows)
 
     def body(core):
-        for half, basis in enumerate((mine, theirs) if core == 0 else (theirs, mine)):
+        for half, basis in enumerate((near, far) if core == 0 else (far, near)):
             total = part_ref[half] + sum(
                 project(rows_of(basis, 2 + segment, rows), f32(message[segment]))
                 for segment in range(2)
@@ -280,8 +271,7 @@
 def low_kernel(
     mine_chip,
     mine_far,
-    theirs_chip,
-    theirs_far,
+    theirs,
     low,
     low_there,
     chip_amp,
@@ -290,8 +280,8 @@
     neighbour_energies,
     states_ref,
 ):
-    mine, theirs = (mine_chip, mine_far), (theirs_chip, theirs_far)
     rows = chip_amp.shape[2]
+    mine, theirs = (mine_chip, mine_far), both(theirs, rows)
     field = bf16(f32(low[...]) + f32(low_there[...]))
 
     def body(core):
@@ -309,8 +299,7 @@
 def second_kernel(
     mine_chip,
     mine_far,
-    theirs_chip,
-    theirs_far,
+    theirs,
     states_ref,
     high,
     high_there,
@@ -321,8 +310,8 @@
     half_ref,
     send_ref,
 ):
-    mine, theirs = (mine_chip, mine_far), (theirs_chip, theirs_far)
     rows = states_ref.shape[2]
+    mine, theirs = (mine_chip, mine_far), both(theirs, rows)
     field = bf16(f32(high[...]) + f32(high_there[...]))
 
     def body(core):
@@ -344,9 +333,9 @@
 
 def late_kernel(
     mine_chip,
-    theirs_chip,
+    theirs,
     theirs_own,
-    sent_chip,
+    sent,
     low,
     high,
     my_low,
@@ -362,19 +351,19 @@
     def body(core):
         my = my_kind()
         near, far = (low, high) if core == 0 else (high, low)
-        change = expand(rows_of((sent_chip,), core, rows), near[...]) + expand(
+        change = expand(rows_of(both(sent, rows), core, rows), near[...]) + expand(
             rows_of((theirs_own,), 0, rows), far[...]
         )
         rate = energy[1 - my] * turned(other_half[...]) + change
         other_new[...] = (amp_ref[1 - my] + time_step * rate).T
-        change = expand(rows_of(((mine_chip, theirs_chip)[core],), core, rows), my_low[...])
+        change = expand(rows_of(((mine_chip,), both(theirs, rows))[core], core, rows), my_low[...])
         my_part[...] = amp_ref[my] + time_step * (energy[my] * turned(my_half[...]) + change)
 
     by_core(body)
 
 
 def last_kernel(
-    mine_chip, theirs_chip, high, my_part, other_new, new_tgt, new_proj, my_new, sems
+    mine_chip, theirs, high, my_part, other_new, new_tgt, new_proj, my_new, sems
 ):
     cols, rows = my_part.shape
     my = my_kind()
@@ -398,7 +387,7 @@
                 copies(kind)[number].start()
 
     def body(core):
-        basis = rows_of(((theirs_chip, mine_chip)[core],), core, rows)
+        basis = rows_of((both(theirs, rows), (mine_chip,))[core], core, rows)
         for part in range(parts):
             states = slice(part * size, (part + 1) * size)
             change = expand([block[states] for block in basis], high[...])
@@ -505,22 +494,21 @@
     flags, counts = pair_flags.T, tile_counts.T
     bases = in_hbm(tgt_basis.reshape(2, -1, rows, points), proj_basis)
     pair = in_vmem((2, 2 * rows, points), jnp.bfloat16)
-    *sent, weight = call(
+    sent, weight = call(
         functools.partial(sent_kernel, neighbours),
         [
-            in_vmem((2, 2 * rows + 2 * PIECES, points), jnp.bfloat16),
-            pair,
-            in_vmem((2, rows, points), jnp.bfloat16),
+            in_vmem((2, 4 * rows + 2 * PIECES, points), jnp.bfloat16),
             in_vmem((1, 1, points), jnp.float32),
         ],
         [HBM] * 3 + [VMEM] * 2,
-        [pltpu.VMEM((points,), jnp.float32), pltpu.SemaphoreType.DMA((6,))],
+        [pltpu.VMEM((points,), jnp.float32), pltpu.SemaphoreType.DMA((5,))],
     )(*in_hbm(quad_weight), *bases, chip_amp, energy)
-    mine_chip, mine_far, gate = call(
+    mine_chip, mine_far, send_own, gate = call(
         functools.partial(side_kernel, gate_levels, neighbours),
         [
             pair,
             pair,
+            in_vmem((2, rows, points), jnp.bfloat16),
             in_vmem((n_steps, 2, 1, points), jnp.float32),
         ],
         [HBM] * 4 + [VMEM],
@@ -531,8 +519,8 @@
         ],
         BEHIND,
     )(*in_hbm(flags, counts), *bases, chip_amp)
-    theirs_chip, theirs_far, theirs_own = swapped(sent)
-    bases = (mine_chip, mine_far, theirs_chip, theirs_far)
+    theirs, theirs_own = swapped([sent, send_own])
+    bases = (mine_chip, mine_far, theirs)
     part, weights, energies = run(
         chip_kernel,
         [
@@ -541,12 +529,12 @@
             in_vmem((2, 1, rows), jnp.float32),
         ],
         mine_chip,
-        theirs_chip,
+        theirs,
         chip_amp,
         weight,
         energy,
     )
-    halves = run(first_kernel, [sums] * 2, mine_far, theirs_far, gate, weights, part, message)
+    halves = run(first_kernel, [sums] * 2, mine_far, theirs, gate, weights, part, message)
     (low, high), energies = lax.optimization_barrier((halves, energies))
     neighbour_energies = exchanged(0, energies)
     halves = low, high
@@ -579,9 +567,9 @@
         late_kernel,
         [segment, in_vmem((rows, two_cols), jnp.float32)],
         mine_chip,
-        theirs_chip,
+        theirs,
         theirs_own,
-        sent[0],
+        sent,
         *fields,
         low,
         energy,
@@ -598,7 +586,7 @@
         [VMEM] * 5,
         [pltpu.VMEM((rows, two_cols), jnp.float32), pltpu.SemaphoreType.DMA((3,))],
         out_spec=HBM,
-    )(mine_chip, theirs_chip, high, my_part, other_new)
+    )(mine_chip, theirs, high, my_part, other_new)
 
 
 def solution(mesh):

time: 35.7 us -> 35.5 us (level)
    ppermute x10 -> x9, waiting for transfers between devices: 1.99 us -> 2.05 us  [other_core(): return lax.ppermute(block, 'rep', [(0, 1), (1, 0)])]
    ppermute x10 -> x9, starting transfers between devices: 3.36 us -> 3.42 us  [other_core(): return lax.ppermute(block, 'rep', [(0, 1), (1, 0)])]
  transfers between devices with their start and end apart: 20 -> 19, of which waited for: 10 -> 11; matrix products, arithmetic and copies ran while one was open for 0% -> 0% of each run, Pallas kernels for 17% -> 17%
where the time goes in v24:
time: 35.5 us; the launch traced here: 35.4 us
  starting transfers between devices  18.2 us (51%)
  waiting for transfers between devices  9.06 us (26%)
  Pallas kernels  7.36 us (21%)
  between operations  0.76 us (2%)
    ppermute x10, starting transfers between devices, exchanged(): return lax.ppermute(block, DEVICES, pairs)  14.8 us
    ppermute x10, waiting for transfers between devices, exchanged(): return lax.ppermute(block, DEVICES, pairs)  7.01 us
    ppermute x9, starting transfers between devices, other_core(): return lax.ppermute(block, 'rep', [(0, 1), (1, 0)])  3.42 us
    pallas_call x12, Pallas kernels, run(): return call(kernel, out_shape, [VMEM] * len(blocks))(*blocks)  2.75 us
    ppermute x9, waiting for transfers between devices, other_core(): return lax.ppermute(block, 'rep', [(0, 1), (1, 0)])  2.05 us
    pallas_call x1, Pallas kernels, shards(): call(functools.partial(side_kernel, gate_levels, neighbours), [pair, pair...  1.26 us
    pallas_call x1, Pallas kernels, shards(): call(functools.partial(sent_kernel, neighbours), [in_vmem((2, 4 * rows +...  1.24 us
    pallas_call x1, Pallas kernels, shards(): call(load_kernel, [in_vmem((2, 1, rows), jnp.float32), in_vmem((2, two_co...  1.14 us
  transfers between devices with their start and end apart: 19, of which 11 were waited for; matrix products, arithmetic and copies ran while one was open for 0% of the time, Pallas kernels for 17%

profile of v24, /device:TPU:0, one launch (start us, length us, event | category | flops | bytes accessed | tf_op | source)
XLA Modules:
  0.0 35.4 jit_solution(10342129934693725307)
XLA Ops:
  0.6 0.5 %collective-permute-start = (f32[256,128]{1,0:T(8,128)}, f32[256,128]{1,0:T(8,128)S(1)}, u32[]{:S(2)}, u32[]{:S(2)}) collective-permute-start(f32[256,128]{1,0:T(8,128)} %tgt_own_hbm.1), channel_id=1, source_target_pairs={{0,1},{1,0},{2,3},{3,2},{4,5},{5,4},{6,7},{7,6},{8,9},{9,8},{10,11... | collective-permute-start | bytes 393224 | tf_op jit(solution)/shard_map/ppermute | solution.py:433
  1.2 1.1 %shard_map.104 = (f32[2,1,256]{2,1,0:T(1,128)S(1)}, f32[2,128,256]{2,1,0:T(8,128)S(1)}) custom-call(f32[256]{0:T(256)} %tgt_energy_hbm.1, f32[1,256]{1,0:T(1,128)} %proj_energy_hbm.1, f32[256,128]{1,0:T(8,128)} %tgt_own_hbm.1, f32[1,256,128]{2,1,0:T(8,128)} %proj_own_hbm.1), custom_call_target="tpu_custom_call" | custom-call | flops 67108864 | bytes 4194304 | tf_op jit(solution)/shard_map/pallas_call | solution.py:473
  2.8 2.7 %collective-permute-start.3 = (bf16[2,128,256]{2,1,0:T(8,128)(2,1)S(1)}, bf16[2,128,256]{2,1,0:T(8,128)(2,1)S(1)}, u32[]{:S(2)}, u32[]{:S(2)}) collective-permute-start(bf16[2,128,256]{2,1,0:T(8,128)(2,1)S(1)} %get-tuple-element.36), channel_id=1, source_target_pairs={{0,3},{1,8},{3,0},{2,11},{5,6},{4,13},{6,5},{7,14},{9,10},{8,1},{1... | collective-permute-start | bytes 393224 | tf_op jit(solution)/shard_map/ppermute | solution.py:451
  5.5 1.2 %shard_map.107 = (bf16[2,1056,256]{2,1,0:T(8,128)(2,1)S(1)}, f32[1,1,256]{2,1,0:T(1,128)S(1)}) custom-call(f32[256]{0:T(256)} %weight_hbm.1, bf16[2,4,256,256]{3,2,1,0:T(8,128)(2,1)} %bitcast.3, bf16[2,8,256,256]{3,2,1,0:T(8,128)(2,1)} %proj_hbm.3, f32[2,128,256]{2,1,0:T(8,128)S(1)} %get-tuple-element.27.chip_amp, f32[2,1,256]{2,1,0:T(1,128)S(1)} %get-tuple-element.29.energy), custom_call_target="tpu_custom_call" | custom-call | tf_op jit(solution)/shard_map/pallas_call | solution.py:497
  6.8 1.4 %collective-permute-start.2 = (bf16[2,1056,256]{2,1,0:T(8,128)(2,1)S(1)}, bf16[2,1056,256]{2,1,0:T(8,128)(2,1)S(1)}, u32[]{:S(2)}, u32[]{:S(2)}) collective-permute-start(bf16[2,1056,256]{2,1,0:T(8,128)(2,1)S(1)} %get-tuple-element.30.sent), channel_id=1, source_target_pairs={{0,1},{1,0},{2,3},{3,2},{4,5},{5,4},{6,7},{7,6},{8,9},{9,8},{10,11... | collective-permute-start | bytes 3244040 | tf_op jit(solution)/shard_map/ppermute | solution.py:433
  8.1 1.3 %shard_map.106 = (bf16[2,512,256]{2,1,0:T(8,128)(2,1)S(1)}, bf16[2,512,256]{2,1,0:T(8,128)(2,1)S(1)}, bf16[2,256,256]{2,1,0:T(8,128)(2,1)S(1)}, f32[3,2,1,256]{3,2,1,0:T(1,128)S(1)}) custom-call(s32[2,4]{1,0:T(2,128)} %bitcast.5, s32[2,4]{1,0:T(2,128)} %bitcast.6, bf16[2,4,256,256]{3,2,1,0:T(8,128)(2,1)} %bitcast.4, bf16[2,8,256,256]{3,2,1,0:T(8,128)(2,1)} %proj_hbm.3, ...), custom_call_target="tpu_custom_call" | custom-call | flops 34359738368 | bytes 65536 | tf_op jit(solution)/shard_map/pallas_call | solution.py:506
  9.4 1.1 %collective-permute-done.2.theirs = bf16[2,1056,256]{2,1,0:T(8,128)(2,1)S(1)} collective-permute-done((bf16[2,1056,256]{2,1,0:T(8,128)(2,1)S(1)}, bf16[2,1056,256]{2,1,0:T(8,128)(2,1)S(1)}, u32[]{:S(2)}, u32[]{:S(2)}) %collective-permute-start.2) | collective-permute-done | bytes 1081376 | tf_op jit(solution)/shard_map/ppermute | solution.py:433
  11.1 1.5 %collective-permute-start.4 = (bf16[128,256]{1,0:T(8,128)(2,1)S(1)}, bf16[128,256]{1,0:T(8,128)(2,1)S(1)}, u32[]{:S(2)}, u32[]{:S(2)}) collective-permute-start(bf16[128,256]{1,0:T(8,128)(2,1)S(1)} %get-tuple-element.40.own), channel_id=1, source_target_pairs={{0,9},{1,4},{3,10},{2,7},{5,12},{4,1},{6,15},{7,2},{9,0},{8,13},{1... | collective-permute-start | bytes 196616 | tf_op jit(solution)/shard_map/ppermute | solution.py:451
  12.7 1.2 %collective-permute-start.8 = (bf16[128,256]{1,0:T(8,128)(2,1)S(1)}, bf16[128,256]{1,0:T(8,128)(2,1)S(1)}, u32[]{:S(2)}, u32[]{:S(2)}) collective-permute-start(bf16[128,256]{1,0:T(8,128)(2,1)S(1)} %get-tuple-element.42.own), channel_id=1, source_target_pairs={{0,9},{1,4},{3,10},{2,7},{5,12},{4,1},{6,15},{7,2},{9,0},{8,13},{1... | collective-permute-start | bytes 196616 | tf_op jit(solution)/shard_map/ppermute | solution.py:451
  13.8 1.4 %collective-permute-start.7 = (f32[2,1,256]{2,1,0:T(1,128)S(1)}, f32[2,1,256]{2,1,0:T(1,128)S(1)}, u32[]{:S(2)}, u32[]{:S(2)}) collective-permute-start(f32[2,1,256]{2,1,0:T(1,128)S(1)} %get-tuple-element.41.energies), channel_id=1, source_target_pairs={{0,3},{1,8},{3,0},{2,11},{5,6},{4,13},{6,5},{7,14},{9,10},{8,1},{1... | collective-permute-start | bytes 6152 | tf_op jit(solution)/shard_map/ppermute | solution.py:451
  15.3 0.6 %collective-permute-done.4.other = bf16[128,256]{1,0:T(8,128)(2,1)S(1)} collective-permute-done((bf16[128,256]{1,0:T(8,128)(2,1)S(1)}, bf16[128,256]{1,0:T(8,128)(2,1)S(1)}, u32[]{:S(2)}, u32[]{:S(2)}) %collective-permute-start.4) | collective-permute-done | bytes 65568 | tf_op jit(solution)/shard_map/ppermute | solution.py:451
  15.9 1.2 %collective-permute-start.6 = (bf16[128,256]{1,0:T(8,128)(2,1)S(1)}, bf16[128,256]{1,0:T(8,128)(2,1)S(1)}, u32[]{:S(2)}, u32[]{:S(2)}) collective-permute-start(bf16[128,256]{1,0:T(8,128)(2,1)S(1)} %shard_map.110), channel_id=1, source_target_pairs={{0,4},{1,3},{3,7},{2,0},{5,1},{4,6},{6,2},{7,5},{9,13},{8,10},{10,... | collective-permute-start | bytes 196616 | tf_op jit(solution)/shard_map/ppermute | solution.py:451
  17.1 0.7 %collective-permute-start.5 = (bf16[128,256]{1,0:T(8,128)(2,1)S(1)}, bf16[128,256]{1,0:T(8,128)(2,1)S(1)}, u32[]{:S(2)}, u32[]{:S(2)}) collective-permute-start(bf16[128,256]{1,0:T(8,128)(2,1)S(1)} %shard_map.110), channel_id=1, source_target_pairs={{0,1},{1,0},{2,3},{3,2},{4,5},{5,4},{6,7},{7,6},{8,9},{9,8},{10,11... | collective-permute-start | bytes 196616 | tf_op jit(solution)/shard_map/ppermute | solution.py:433
  18.0 1.5 %collective-permute-start.10 = (bf16[128,256]{1,0:T(8,128)(2,1)S(1)}, bf16[128,256]{1,0:T(8,128)(2,1)S(1)}, u32[]{:S(2)}, u32[]{:S(2)}) collective-permute-start(bf16[128,256]{1,0:T(8,128)(2,1)S(1)} %shard_map.112), channel_id=1, source_target_pairs={{0,4},{1,3},{3,7},{2,0},{5,1},{4,6},{6,2},{7,5},{9,13},{8,10},{10,... | collective-permute-start | bytes 196616 | tf_op jit(solution)/shard_map/ppermute | solution.py:451
  20.8 1.6 %collective-permute-done.10.high_there = bf16[128,256]{1,0:T(8,128)(2,1)S(1)} collective-permute-done((bf16[128,256]{1,0:T(8,128)(2,1)S(1)}, bf16[128,256]{1,0:T(8,128)(2,1)S(1)}, u32[]{:S(2)}, u32[]{:S(2)}) %collective-permute-start.10) | collective-permute-done | bytes 65568 | tf_op jit(solution)/shard_map/ppermute | solution.py:451
  22.3 0.8 %shard_map.113 = (bf16[128,256]{1,0:T(8,128)(2,1)S(1)}, bf16[128,256]{1,0:T(8,128)(2,1)S(1)}, f32[128,256]{1,0:T(8,128)S(1)}, f32[128,256]{1,0:T(8,128)S(1)}) custom-call(bf16[2,512,256]{2,1,0:T(8,128)(2,1)S(1)} %get-tuple-element.28.mine_chip, bf16[2,512,256]{2,1,0:T(8,128)(2,1)S(1)} %get-tuple-element.32.mine_far, ...), custom_call_target="tpu_custom_call" | custom-call | tf_op jit(solution)/shard_map/pallas_call | solution.py:430
  23.4 2.5 %collective-permute-start.11 = (bf16[128,256]{1,0:T(8,128)(2,1)S(1)}, bf16[128,256]{1,0:T(8,128)(2,1)S(1)}, u32[]{:S(2)}, u32[]{:S(2)}) collective-permute-start(bf16[128,256]{1,0:T(8,128)(2,1)S(1)} %get-tuple-element.43.own), channel_id=1, source_target_pairs={{0,9},{1,4},{3,10},{2,7},{5,12},{4,1},{6,15},{7,2},{9,0},{8,13},{1... | collective-permute-start | bytes 196616 | tf_op jit(solution)/shard_map/ppermute | solution.py:451
  25.9 2.0 %collective-permute-done.15.other = bf16[128,256]{1,0:T(8,128)(2,1)S(1)} collective-permute-done((bf16[128,256]{1,0:T(8,128)(2,1)S(1)}, bf16[128,256]{1,0:T(8,128)(2,1)S(1)}, u32[]{:S(2)}, u32[]{:S(2)}) %collective-permute-start.15) | collective-permute-done | bytes 65568 | tf_op jit(solution)/shard_map/ppermute | solution.py:451
  27.8 1.3 %collective-permute-start.16 = (bf16[128,256]{1,0:T(8,128)(2,1)S(1)}, bf16[128,256]{1,0:T(8,128)(2,1)S(1)}, u32[]{:S(2)}, u32[]{:S(2)}) collective-permute-start(bf16[128,256]{1,0:T(8,128)(2,1)S(1)} %shard_map.116.own), channel_id=1, source_target_pairs={{0,5},{1,2},{3,6},{2,1},{5,0},{4,7},{6,3},{7,4},{9,12},{8,11},{10,... | collective-permute-start | bytes 196616 | tf_op jit(solution)/shard_map/ppermute | solution.py:451
  29.3 1.3 %collective-permute-start.12 = (bf16[128,256]{1,0:T(8,128)(2,1)S(1)}, bf16[128,256]{1,0:T(8,128)(2,1)S(1)}, u32[]{:S(2)}, u32[]{:S(2)}) collective-permute-start(bf16[128,256]{1,0:T(8,128)(2,1)S(1)} %shard_map.114.own), channel_id=1, source_target_pairs={{0,5},{1,2},{3,6},{2,1},{5,0},{4,7},{6,3},{7,4},{9,12},{8,11},{10,... | collective-permute-start | bytes 196616 | tf_op jit(solution)/shard_map/ppermute | solution.py:451
  30.5 1.1 %collective-permute-done.16.other = bf16[128,256]{1,0:T(8,128)(2,1)S(1)} collective-permute-done((bf16[128,256]{1,0:T(8,128)(2,1)S(1)}, bf16[128,256]{1,0:T(8,128)(2,1)S(1)}, u32[]{:S(2)}, u32[]{:S(2)}) %collective-permute-start.16) | collective-permute-done | bytes 65568 | tf_op jit(solution)/shard_map/ppermute | solution.py:451
  31.7 1.3 %collective-permute-done.12.other = bf16[128,256]{1,0:T(8,128)(2,1)S(1)} collective-permute-done((bf16[128,256]{1,0:T(8,128)(2,1)S(1)}, bf16[128,256]{1,0:T(8,128)(2,1)S(1)}, u32[]{:S(2)}, u32[]{:S(2)}) %collective-permute-start.12) | collective-permute-done | bytes 65568 | tf_op jit(solution)/shard_map/ppermute | solution.py:451
  33.7 0.6 %collective-permute-done.13.high = bf16[128,256]{1,0:T(8,128)(2,1)S(1)} collective-permute-done((bf16[128,256]{1,0:T(8,128)(2,1)S(1)}, bf16[128,256]{1,0:T(8,128)(2,1)S(1)}, u32[]{:S(2)}, u32[]{:S(2)}) %collective-permute-start.13) | collective-permute-done | bytes 65568 | tf_op jit(solution)/shard_map/ppermute | solution.py:433
  34.4 1.0 %shard_map.119 = (f32[256,128]{1,0:T(8,128)}, f32[1,256,128]{2,1,0:T(8,128)}) custom-call(bf16[2,512,256]{2,1,0:T(8,128)(2,1)S(1)} %get-tuple-element.28.mine_chip, bf16[2,1056,256]{2,1,0:T(8,128)(2,1)S(1)} %collective-permute-done.2.theirs, bf16[128,256]{1,0:T(8,128)(2,1)S(1)} %collective-permute-done.13.high, f32[128,256]{1,0:T(8,128)S(1)} %get-tuple-element.48.my_part, ...), custom_call_target="tpu_custom_call" | custom-call | tf_op jit(solution)/shard_map/pallas_call | solution.py:580
  (30 shorter events, 3.8 us)
Async XLA Ops:
  0.6 1.7 %collective-permute-start = (f32[256,128]{1,0:T(8,128)}, f32[256,128]{1,0:T(8,128)S(1)}, u32[]{:S(2)}, u32[]{:S(2)}) collective-permute-start(f32[256,128]{1,0:T(8,128)} %tgt_own_hbm.1), channel_id=1, source_target_pairs={{0,1},{1,0},{2,3},{3,2},{4,5},{5,4},{6,7},{7,6},{8,9},{9,8},{10,11... | collective-permute-start | bytes 393224 | tf_op jit(solution)/shard_map/ppermute | solution.py:433
  1.1 1.6 %collective-permute-start.1 = (f32[1,256,128]{2,1,0:T(8,128)}, f32[1,256,128]{2,1,0:T(8,128)S(1)}, u32[]{:S(2)}, u32[]{:S(2)}) collective-permute-start(f32[1,256,128]{2,1,0:T(8,128)} %proj_own_hbm.1), channel_id=1, source_target_pairs={{0,1},{1,0},{2,3},{3,2},{4,5},{5,4},{6,7},{7,6},{8,9},{9,8},{10,11... | collective-permute-start | bytes 393224 | tf_op jit(solution)/shard_map/ppermute | solution.py:433
  2.8 7.9 %collective-permute-start.3 = (bf16[2,128,256]{2,1,0:T(8,128)(2,1)S(1)}, bf16[2,128,256]{2,1,0:T(8,128)(2,1)S(1)}, u32[]{:S(2)}, u32[]{:S(2)}) collective-permute-start(bf16[2,128,256]{2,1,0:T(8,128)(2,1)S(1)} %get-tuple-element.36), channel_id=1, source_target_pairs={{0,3},{1,8},{3,0},{2,11},{5,6},{4,13},{6,5},{7,14},{9,10},{8,1},{1... | collective-permute-start | bytes 393224 | tf_op jit(solution)/shard_map/ppermute | solution.py:451
  6.8 3.7 %collective-permute-start.2 = (bf16[2,1056,256]{2,1,0:T(8,128)(2,1)S(1)}, bf16[2,1056,256]{2,1,0:T(8,128)(2,1)S(1)}, u32[]{:S(2)}, u32[]{:S(2)}) collective-permute-start(bf16[2,1056,256]{2,1,0:T(8,128)(2,1)S(1)} %get-tuple-element.30.sent), channel_id=1, source_target_pairs={{0,1},{1,0},{2,3},{3,2},{4,5},{5,4},{6,7},{7,6},{8,9},{9,8},{10,11... | collective-permute-start | bytes 3244040 | tf_op jit(solution)/shard_map/ppermute | solution.py:433
  11.1 4.8 %collective-permute-start.4 = (bf16[128,256]{1,0:T(8,128)(2,1)S(1)}, bf16[128,256]{1,0:T(8,128)(2,1)S(1)}, u32[]{:S(2)}, u32[]{:S(2)}) collective-permute-start(bf16[128,256]{1,0:T(8,128)(2,1)S(1)} %get-tuple-element.40.own), channel_id=1, source_target_pairs={{0,9},{1,4},{3,10},{2,7},{5,12},{4,1},{6,15},{7,2},{9,0},{8,13},{1... | collective-permute-start | bytes 196616 | tf_op jit(solution)/shard_map/ppermute | solution.py:451
  12.7 5.3 %collective-permute-start.8 = (bf16[128,256]{1,0:T(8,128)(2,1)S(1)}, bf16[128,256]{1,0:T(8,128)(2,1)S(1)}, u32[]{:S(2)}, u32[]{:S(2)}) collective-permute-start(bf16[128,256]{1,0:T(8,128)(2,1)S(1)} %get-tuple-element.42.own), channel_id=1, source_target_pairs={{0,9},{1,4},{3,10},{2,7},{5,12},{4,1},{6,15},{7,2},{9,0},{8,13},{1... | collective-permute-start | bytes 196616 | tf_op jit(solution)/shard_map/ppermute | solution.py:451
  13.8 5.7 %collective-permute-start.7 = (f32[2,1,256]{2,1,0:T(1,128)S(1)}, f32[2,1,256]{2,1,0:T(1,128)S(1)}, u32[]{:S(2)}, u32[]{:S(2)}) collective-permute-start(f32[2,1,256]{2,1,0:T(1,128)S(1)} %get-tuple-element.41.energies), channel_id=1, source_target_pairs={{0,3},{1,8},{3,0},{2,11},{5,6},{4,13},{6,5},{7,14},{9,10},{8,1},{1... | collective-permute-start | bytes 6152 | tf_op jit(solution)/shard_map/ppermute | solution.py:451
  15.9 4.3 %collective-permute-start.6 = (bf16[128,256]{1,0:T(8,128)(2,1)S(1)}, bf16[128,256]{1,0:T(8,128)(2,1)S(1)}, u32[]{:S(2)}, u32[]{:S(2)}) collective-permute-start(bf16[128,256]{1,0:T(8,128)(2,1)S(1)} %shard_map.110), channel_id=1, source_target_pairs={{0,4},{1,3},{3,7},{2,0},{5,1},{4,6},{6,2},{7,5},{9,13},{8,10},{10,... | collective-permute-start | bytes 196616 | tf_op jit(solution)/shard_map/ppermute | solution.py:451
  17.1 3.1 %collective-permute-start.5 = (bf16[128,256]{1,0:T(8,128)(2,1)S(1)}, bf16[128,256]{1,0:T(8,128)(2,1)S(1)}, u32[]{:S(2)}, u32[]{:S(2)}) collective-permute-start(bf16[128,256]{1,0:T(8,128)(2,1)S(1)} %shard_map.110), channel_id=1, source_target_pairs={{0,1},{1,0},{2,3},{3,2},{4,5},{5,4},{6,7},{7,6},{8,9},{9,8},{10,11... | collective-permute-start | bytes 196616 | tf_op jit(solution)/shard_map/ppermute | solution.py:433
  18.0 4.3 %collective-permute-start.10 = (bf16[128,256]{1,0:T(8,128)(2,1)S(1)}, bf16[128,256]{1,0:T(8,128)(2,1)S(1)}, u32[]{:S(2)}, u32[]{:S(2)}) collective-permute-start(bf16[128,256]{1,0:T(8,128)(2,1)S(1)} %shard_map.112), channel_id=1, source_target_pairs={{0,4},{1,3},{3,7},{2,0},{5,1},{4,6},{6,2},{7,5},{9,13},{8,10},{10,... | collective-permute-start | bytes 196616 | tf_op jit(solution)/shard_map/ppermute | solution.py:451
  19.5 2.9 %collective-permute-start.9 = (bf16[128,256]{1,0:T(8,128)(2,1)S(1)}, bf16[128,256]{1,0:T(8,128)(2,1)S(1)}, u32[]{:S(2)}, u32[]{:S(2)}) collective-permute-start(bf16[128,256]{1,0:T(8,128)(2,1)S(1)} %shard_map.112), channel_id=1, source_target_pairs={{0,1},{1,0},{2,3},{3,2},{4,5},{5,4},{6,7},{7,6},{8,9},{9,8},{10,11... | collective-permute-start | bytes 196616 | tf_op jit(solution)/shard_map/ppermute | solution.py:433
  19.5 13.7 %collective-permute-start.14 = (bf16[2,256,256]{2,1,0:T(8,128)(2,1)S(1)}, bf16[2,256,256]{2,1,0:T(8,128)(2,1)S(1)}, u32[]{:S(2)}, u32[]{:S(2)}) collective-permute-start(bf16[2,256,256]{2,1,0:T(8,128)(2,1)S(1)} %get-tuple-element.44), channel_id=1, source_target_pairs={{0,1},{1,0},{2,3},{3,2},{4,5},{5,4},{6,7},{7,6},{8,9},{9,8},{10,11... | collective-permute-start | bytes 786440 | tf_op jit(solution)/shard_map/ppermute | solution.py:433
  23.2 4.7 %collective-permute-start.15 = (bf16[128,256]{1,0:T(8,128)(2,1)S(1)}, bf16[128,256]{1,0:T(8,128)(2,1)S(1)}, u32[]{:S(2)}, u32[]{:S(2)}) collective-permute-start(bf16[128,256]{1,0:T(8,128)(2,1)S(1)} %get-tuple-element.45.own), channel_id=1, source_target_pairs={{0,9},{1,4},{3,10},{2,7},{5,12},{4,1},{6,15},{7,2},{9,0},{8,13},{1... | collective-permute-start | bytes 196616 | tf_op jit(solution)/shard_map/ppermute | solution.py:451
  23.4 5.9 %collective-permute-start.11 = (bf16[128,256]{1,0:T(8,128)(2,1)S(1)}, bf16[128,256]{1,0:T(8,128)(2,1)S(1)}, u32[]{:S(2)}, u32[]{:S(2)}) collective-permute-start(bf16[128,256]{1,0:T(8,128)(2,1)S(1)} %get-tuple-element.43.own), channel_id=1, source_target_pairs={{0,9},{1,4},{3,10},{2,7},{5,12},{4,1},{6,15},{7,2},{9,0},{8,13},{1... | collective-permute-start | bytes 196616 | tf_op jit(solution)/shard_map/ppermute | solution.py:451
  25.9 7.4 %collective-permute-start.18 = (f32[128,256]{1,0:T(8,128)S(1)}, f32[128,256]{1,0:T(8,128)S(1)}, u32[]{:S(2)}, u32[]{:S(2)}) collective-permute-start(f32[128,256]{1,0:T(8,128)S(1)} %get-tuple-element.47), channel_id=1, source_target_pairs={{0,1},{1,0},{2,3},{3,2},{4,5},{5,4},{6,7},{7,6},{8,9},{9,8},{10,11... | collective-permute-start | bytes 393224 | tf_op jit(solution)/shard_map/ppermute | solution.py:433
  27.8 3.8 %collective-permute-start.16 = (bf16[128,256]{1,0:T(8,128)(2,1)S(1)}, bf16[128,256]{1,0:T(8,128)(2,1)S(1)}, u32[]{:S(2)}, u32[]{:S(2)}) collective-permute-start(bf16[128,256]{1,0:T(8,128)(2,1)S(1)} %shard_map.116.own), channel_id=1, source_target_pairs={{0,5},{1,2},{3,6},{2,1},{5,0},{4,7},{6,3},{7,4},{9,12},{8,11},{10,... | collective-permute-start | bytes 196616 | tf_op jit(solution)/shard_map/ppermute | solution.py:451
  29.3 3.8 %collective-permute-start.12 = (bf16[128,256]{1,0:T(8,128)(2,1)S(1)}, bf16[128,256]{1,0:T(8,128)(2,1)S(1)}, u32[]{:S(2)}, u32[]{:S(2)}) collective-permute-start(bf16[128,256]{1,0:T(8,128)(2,1)S(1)} %shard_map.114.own), channel_id=1, source_target_pairs={{0,5},{1,2},{3,6},{2,1},{5,0},{4,7},{6,3},{7,4},{9,12},{8,11},{10,... | collective-permute-start | bytes 196616 | tf_op jit(solution)/shard_map/ppermute | solution.py:451
  31.6 1.6 %collective-permute-start.17 = (bf16[128,256]{1,0:T(8,128)(2,1)S(1)}, bf16[128,256]{1,0:T(8,128)(2,1)S(1)}, u32[]{:S(2)}, u32[]{:S(2)}) collective-permute-start(bf16[128,256]{1,0:T(8,128)(2,1)S(1)} %shard_map.117.low), channel_id=1, source_target_pairs={{0,1},{1,0},{2,3},{3,2},{4,5},{5,4},{6,7},{7,6},{8,9},{9,8},{10,11... | collective-permute-start | bytes 196616 | tf_op jit(solution)/shard_map/ppermute | solution.py:433
  33.1 1.3 %collective-permute-start.13 = (bf16[128,256]{1,0:T(8,128)(2,1)S(1)}, bf16[128,256]{1,0:T(8,128)(2,1)S(1)}, u32[]{:S(2)}, u32[]{:S(2)}) collective-permute-start(bf16[128,256]{1,0:T(8,128)(2,1)S(1)} %shard_map.115.high), channel_id=1, source_target_pairs={{0,1},{1,0},{2,3},{3,2},{4,5},{5,4},{6,7},{7,6},{8,9},{9,8},{10,11... | collective-permute-start | bytes 196616 | tf_op jit(solution)/shard_map/ppermute | solution.py:433

commit v25 on v24

--- a/solution.py
+++ b/solution.py
@@ -249,17 +249,16 @@
     by_core(body)
 
 
-def first_kernel(mine_far, theirs, gate, weights, part_ref, message, *outs):
+def first_kernel(half, mine_far, theirs, gate, weights, part_ref, message, out_ref):
     rows = message.shape[2]
-    near, far = (None, mine_far), both(theirs, rows)
+    near, far = (None, mine_far), (None, both(theirs, rows)[1])
 
     def body(core):
-        for half, basis in enumerate((near, far) if core == 0 else (far, near)):
-            total = part_ref[half] + sum(
-                project(rows_of(basis, 2 + segment, rows), f32(message[segment]))
-                for segment in range(2)
-            )
-            outs[half][...] = bf16(gate[0, half] * (weights[half] * total))
+        basis = near if core == half else far
+        total = part_ref[half] + sum(
+            project(rows_of(basis, 2 + segment, rows), f32(message[segment])) for segment in range(2)
+        )
+        out_ref[...] = bf16(gate[0, half] * (weights[half] * total))
 
     by_core(body)
 
@@ -306,7 +305,7 @@
     gate,
     weights,
     low_ref,
-    high_ref,
+    halves_ref,
     half_ref,
     send_ref,
 ):
@@ -320,13 +319,28 @@
             states_ref[segment] + half_step * expand(rows_of(bases[1], segment, rows), field)
             for segment in range(4)
         ]
+        total = sum(
+            project(rows_of(bases[0], segment, rows), halves[segment]) for segment in range(4)
+        )
+        low_ref[...] = bf16(gate[0, 0] * (weights[0] * total))
+        for segment in range(4):
+            halves_ref[segment] = halves[segment]
         half_ref[...] = halves[core]
         send_ref[...] = halves[1 - core]
-        for half, out_ref in enumerate((low_ref, high_ref)):
-            total = sum(
-                project(rows_of(bases[half], segment, rows), halves[segment]) for segment in range(4)
-            )
-            out_ref[...] = bf16(gate[0, half] * (weights[half] * total))
+
+    by_core(body)
+
+
+def high_kernel(mine_chip, mine_far, theirs, gate, weights, halves_ref, high_ref):
+    rows = halves_ref.shape[2]
+    mine, theirs = (mine_chip, mine_far), both(theirs, rows)
+
+    def body(core):
+        basis = (theirs, mine)[core]
+        total = sum(
+            project(rows_of(basis, segment, rows), halves_ref[segment]) for segment in range(4)
+        )
+        high_ref[...] = bf16(gate[0, 1] * (weights[1] * total))
 
     by_core(body)
 
@@ -534,10 +548,11 @@
         weight,
         energy,
     )
-    halves = run(first_kernel, [sums] * 2, mine_far, theirs, gate, weights, part, message)
-    (low, high), energies = lax.optimization_barrier((halves, energies))
+    halves = [
+        run(functools.partial(first_kernel, half), [sums], mine_far, theirs, gate, weights, part, message)[0]
+        for half in range(2)
+    ]
     neighbour_energies = exchanged(0, energies)
-    halves = low, high
     parts = summed(halves, n_steps - 1)
     low, high = [(other_core(block), exchanged(n_steps - 1, block, crossed=1)) for block in parts]
     (states,) = run(
@@ -550,17 +565,18 @@
         message,
         neighbour_energies,
     )
-    *halves, my_half, half_send = run(
+    low, states, my_half, half_send = run(
         second_kernel,
-        [sums, sums, segment, segment],
+        [sums, in_vmem((4, two_cols, rows), jnp.float32), segment, segment],
         *bases,
         states,
         *high,
         gate,
         weights,
     )
+    (high,) = run(high_kernel, [sums], *bases, gate, weights, states)
     other_half = other_core(half_send)
-    fields = summed(halves, n_steps)
+    fields = summed((low, high), n_steps)
     low, high = swapped(fields)
     low, high = swapped(fields)
     my_part, other_new = run(

time: 35.5 us -> 35.8 us (level)
  waiting for transfers between devices: 9.06 us -> 7.97 us
  starting transfers between devices: 18.2 us -> 19 us
  Pallas kernels: 7.36 us -> 7.83 us
    ppermute x10, waiting for transfers between devices: 7.01 us -> 5.93 us  [exchanged(): return lax.ppermute(block, DEVICES, pairs)]
    ppermute x10, starting transfers between devices: 14.8 us -> 15.6 us  [exchanged(): return lax.ppermute(block, DEVICES, pairs)]
    pallas_call x12 -> x14, Pallas kernels: 2.75 us -> 3.22 us  [run(): return call(kernel, out_shape, [VMEM] * len(blocks))(*blocks)]
  transfers between devices with their start and end apart: 19 -> 19, of which waited for: 11 -> 11; matrix products, arithmetic and copies ran while one was open for 0% -> 0% of each run, Pallas kernels for 17% -> 18%
where the time goes in v25:
time: 35.8 us; the launch traced here: 35.6 us
  starting transfers between devices  19 us (53%)
  waiting for transfers between devices  7.97 us (22%)
  Pallas kernels  7.83 us (22%)
  between operations  0.78 us (2%)
    ppermute x10, starting transfers between devices, exchanged(): return lax.ppermute(block, DEVICES, pairs)  15.6 us
    ppermute x10, waiting for transfers between devices, exchanged(): return lax.ppermute(block, DEVICES, pairs)  5.93 us
    ppermute x9, starting transfers between devices, other_core(): return lax.ppermute(block, 'rep', [(0, 1), (1, 0)])  3.38 us
    pallas_call x14, Pallas kernels, run(): return call(kernel, out_shape, [VMEM] * len(blocks))(*blocks)  3.22 us
    ppermute x9, waiting for transfers between devices, other_core(): return lax.ppermute(block, 'rep', [(0, 1), (1, 0)])  2.05 us
    pallas_call x1, Pallas kernels, shards(): call(functools.partial(side_kernel, gate_levels, neighbours), [pair, pair...  1.26 us
    pallas_call x1, Pallas kernels, shards(): call(functools.partial(sent_kernel, neighbours), [in_vmem((2, 4 * rows +...  1.24 us
    pallas_call x1, Pallas kernels, shards(): call(load_kernel, [in_vmem((2, 1, rows), jnp.float32), in_vmem((2, two_co...  1.14 us
  transfers between devices with their start and end apart: 19, of which 11 were waited for; matrix products, arithmetic and copies ran while one was open for 0% of the time, Pallas kernels for 18%

profile of v25, /device:TPU:0, one launch (start us, length us, event | category | flops | bytes accessed | tf_op | source)
XLA Modules:
  0.0 35.6 jit_solution(8090984111196980778)
XLA Ops:
  0.6 0.5 %collective-permute-start = (f32[256,128]{1,0:T(8,128)}, f32[256,128]{1,0:T(8,128)S(1)}, u32[]{:S(2)}, u32[]{:S(2)}) collective-permute-start(f32[256,128]{1,0:T(8,128)} %tgt_own_hbm.1), channel_id=1, source_target_pairs={{0,1},{1,0},{2,3},{3,2},{4,5},{5,4},{6,7},{7,6},{8,9},{9,8},{10,11... | collective-permute-start | bytes 393224 | tf_op jit(solution)/shard_map/ppermute | solution.py:447
  1.2 1.1 %shard_map.104 = (f32[2,1,256]{2,1,0:T(1,128)S(1)}, f32[2,128,256]{2,1,0:T(8,128)S(1)}) custom-call(f32[256]{0:T(256)} %tgt_energy_hbm.1, f32[1,256]{1,0:T(1,128)} %proj_energy_hbm.1, f32[256,128]{1,0:T(8,128)} %tgt_own_hbm.1, f32[1,256,128]{2,1,0:T(8,128)} %proj_own_hbm.1), custom_call_target="tpu_custom_call" | custom-call | flops 67108864 | bytes 4194304 | tf_op jit(solution)/shard_map/pallas_call | solution.py:487
  2.8 2.7 %collective-permute-start.3 = (bf16[2,128,256]{2,1,0:T(8,128)(2,1)S(1)}, bf16[2,128,256]{2,1,0:T(8,128)(2,1)S(1)}, u32[]{:S(2)}, u32[]{:S(2)}) collective-permute-start(bf16[2,128,256]{2,1,0:T(8,128)(2,1)S(1)} %get-tuple-element.31), channel_id=1, source_target_pairs={{0,3},{1,8},{3,0},{2,11},{5,6},{4,13},{6,5},{7,14},{9,10},{8,1},{1... | collective-permute-start | bytes 393224 | tf_op jit(solution)/shard_map/ppermute | solution.py:465
  5.5 1.2 %shard_map.107 = (bf16[2,1056,256]{2,1,0:T(8,128)(2,1)S(1)}, f32[1,1,256]{2,1,0:T(1,128)S(1)}) custom-call(f32[256]{0:T(256)} %weight_hbm.1, bf16[2,4,256,256]{3,2,1,0:T(8,128)(2,1)} %bitcast.3, bf16[2,8,256,256]{3,2,1,0:T(8,128)(2,1)} %proj_hbm.3, f32[2,128,256]{2,1,0:T(8,128)S(1)} %get-tuple-element.22.chip_amp, f32[2,1,256]{2,1,0:T(1,128)S(1)} %get-tuple-element.24.energy), custom_call_target="tpu_custom_call" | custom-call | tf_op jit(solution)/shard_map/pallas_call | solution.py:511
  6.8 1.4 %collective-permute-start.2 = (bf16[2,1056,256]{2,1,0:T(8,128)(2,1)S(1)}, bf16[2,1056,256]{2,1,0:T(8,128)(2,1)S(1)}, u32[]{:S(2)}, u32[]{:S(2)}) collective-permute-start(bf16[2,1056,256]{2,1,0:T(8,128)(2,1)S(1)} %get-tuple-element.25.sent), channel_id=1, source_target_pairs={{0,1},{1,0},{2,3},{3,2},{4,5},{5,4},{6,7},{7,6},{8,9},{9,8},{10,11... | collective-permute-start | bytes 3244040 | tf_op jit(solution)/shard_map/ppermute | solution.py:447
  8.1 1.3 %shard_map.106 = (bf16[2,512,256]{2,1,0:T(8,128)(2,1)S(1)}, bf16[2,512,256]{2,1,0:T(8,128)(2,1)S(1)}, bf16[2,256,256]{2,1,0:T(8,128)(2,1)S(1)}, f32[3,2,1,256]{3,2,1,0:T(1,128)S(1)}) custom-call(s32[2,4]{1,0:T(2,128)} %bitcast.5, s32[2,4]{1,0:T(2,128)} %bitcast.6, bf16[2,4,256,256]{3,2,1,0:T(8,128)(2,1)} %bitcast.4, bf16[2,8,256,256]{3,2,1,0:T(8,128)(2,1)} %proj_hbm.3, ...), custom_call_target="tpu_custom_call" | custom-call | flops 34359738368 | bytes 65536 | tf_op jit(solution)/shard_map/pallas_call | solution.py:520
  9.4 1.1 %collective-permute-done.2.theirs = bf16[2,1056,256]{2,1,0:T(8,128)(2,1)S(1)} collective-permute-done((bf16[2,1056,256]{2,1,0:T(8,128)(2,1)S(1)}, bf16[2,1056,256]{2,1,0:T(8,128)(2,1)S(1)}, u32[]{:S(2)}, u32[]{:S(2)}) %collective-permute-start.2) | collective-permute-done | bytes 1081376 | tf_op jit(solution)/shard_map/ppermute | solution.py:447
  11.0 1.5 %collective-permute-start.4 = (bf16[128,256]{1,0:T(8,128)(2,1)S(1)}, bf16[128,256]{1,0:T(8,128)(2,1)S(1)}, u32[]{:S(2)}, u32[]{:S(2)}) collective-permute-start(bf16[128,256]{1,0:T(8,128)(2,1)S(1)} %shard_map.109.own), channel_id=1, source_target_pairs={{0,9},{1,4},{3,10},{2,7},{5,12},{4,1},{6,15},{7,2},{9,0},{8,13},{1... | collective-permute-start | bytes 196616 | tf_op jit(solution)/shard_map/ppermute | solution.py:465
  12.8 1.2 %collective-permute-start.8 = (bf16[128,256]{1,0:T(8,128)(2,1)S(1)}, bf16[128,256]{1,0:T(8,128)(2,1)S(1)}, u32[]{:S(2)}, u32[]{:S(2)}) collective-permute-start(bf16[128,256]{1,0:T(8,128)(2,1)S(1)} %shard_map.112.own), channel_id=1, source_target_pairs={{0,9},{1,4},{3,10},{2,7},{5,12},{4,1},{6,15},{7,2},{9,0},{8,13},{1... | collective-permute-start | bytes 196616 | tf_op jit(solution)/shard_map/ppermute | solution.py:465
  14.1 1.4 %collective-permute-start.7 = (f32[2,1,256]{2,1,0:T(1,128)S(1)}, f32[2,1,256]{2,1,0:T(1,128)S(1)}, u32[]{:S(2)}, u32[]{:S(2)}) collective-permute-start(f32[2,1,256]{2,1,0:T(1,128)S(1)} %get-tuple-element.32.energies), channel_id=1, source_target_pairs={{0,3},{1,8},{3,0},{2,11},{5,6},{4,13},{6,5},{7,14},{9,10},{8,1},{1... | collective-permute-start | bytes 6152 | tf_op jit(solution)/shard_map/ppermute | solution.py:465
  15.8 1.2 %collective-permute-start.6 = (bf16[128,256]{1,0:T(8,128)(2,1)S(1)}, bf16[128,256]{1,0:T(8,128)(2,1)S(1)}, u32[]{:S(2)}, u32[]{:S(2)}) collective-permute-start(bf16[128,256]{1,0:T(8,128)(2,1)S(1)} %shard_map.110), channel_id=1, source_target_pairs={{0,4},{1,3},{3,7},{2,0},{5,1},{4,6},{6,2},{7,5},{9,13},{8,10},{10,... | collective-permute-start | bytes 196616 | tf_op jit(solution)/shard_map/ppermute | solution.py:465
  17.1 0.7 %collective-permute-start.5 = (bf16[128,256]{1,0:T(8,128)(2,1)S(1)}, bf16[128,256]{1,0:T(8,128)(2,1)S(1)}, u32[]{:S(2)}, u32[]{:S(2)}) collective-permute-start(bf16[128,256]{1,0:T(8,128)(2,1)S(1)} %shard_map.110), channel_id=1, source_target_pairs={{0,1},{1,0},{2,3},{3,2},{4,5},{5,4},{6,7},{7,6},{8,9},{9,8},{10,11... | collective-permute-start | bytes 196616 | tf_op jit(solution)/shard_map/ppermute | solution.py:447
  18.0 1.4 %collective-permute-start.10 = (bf16[128,256]{1,0:T(8,128)(2,1)S(1)}, bf16[128,256]{1,0:T(8,128)(2,1)S(1)}, u32[]{:S(2)}, u32[]{:S(2)}) collective-permute-start(bf16[128,256]{1,0:T(8,128)(2,1)S(1)} %shard_map.113), channel_id=1, source_target_pairs={{0,4},{1,3},{3,7},{2,0},{5,1},{4,6},{6,2},{7,5},{9,13},{8,10},{10,... | collective-permute-start | bytes 196616 | tf_op jit(solution)/shard_map/ppermute | solution.py:465
  20.2 0.5 %shard_map.111.states_ref = f32[4,128,256]{2,1,0:T(8,128)S(1)} custom-call(bf16[2,512,256]{2,1,0:T(8,128)(2,1)S(1)} %get-tuple-element.23.mine_chip, bf16[2,512,256]{2,1,0:T(8,128)(2,1)S(1)} %get-tuple-element.27.mine_far, bf16[2,1056,256]{2,1,0:T(8,128)(2,1)S(1)} %collective-permute-done.2.theirs, bf16[128,256]{1,0:T(8,128)(2,1)S(1)} %collective-permute-done.5.low, ...), custom_call_target="tpu_custom_call" | custom-call | tf_op jit(solution)/shard_map/pallas_call | solution.py:444
  20.7 1.6 %collective-permute-done.10.high_there = bf16[128,256]{1,0:T(8,128)(2,1)S(1)} collective-permute-done((bf16[128,256]{1,0:T(8,128)(2,1)S(1)}, bf16[128,256]{1,0:T(8,128)(2,1)S(1)}, u32[]{:S(2)}, u32[]{:S(2)}) %collective-permute-start.10) | collective-permute-done | bytes 65568 | tf_op jit(solution)/shard_map/ppermute | solution.py:465
  22.3 0.8 %shard_map.114 = (bf16[128,256]{1,0:T(8,128)(2,1)S(1)}, f32[4,128,256]{2,1,0:T(8,128)S(1)}, f32[128,256]{1,0:T(8,128)S(1)}, f32[128,256]{1,0:T(8,128)S(1)}) custom-call(bf16[2,512,256]{2,1,0:T(8,128)(2,1)S(1)} %get-tuple-element.23.mine_chip, bf16[2,512,256]{2,1,0:T(8,128)(2,1)S(1)} %get-tuple-element.27.mine_far, ...), custom_call_target="tpu_custom_call" | custom-call | tf_op jit(solution)/shard_map/pallas_call | solution.py:444
  23.1 0.5 %collective-permute-start.15 = (bf16[128,256]{1,0:T(8,128)(2,1)S(1)}, bf16[128,256]{1,0:T(8,128)(2,1)S(1)}, u32[]{:S(2)}, u32[]{:S(2)}) collective-permute-start(bf16[128,256]{1,0:T(8,128)(2,1)S(1)} %get-tuple-element.35.own), channel_id=1, source_target_pairs={{0,9},{1,4},{3,10},{2,7},{5,12},{4,1},{6,15},{7,2},{9,0},{8,13},{1... | collective-permute-start | bytes 196616 | tf_op jit(solution)/shard_map/ppermute | solution.py:465
  24.0 2.3 %collective-permute-start.11 = (bf16[128,256]{1,0:T(8,128)(2,1)S(1)}, bf16[128,256]{1,0:T(8,128)(2,1)S(1)}, u32[]{:S(2)}, u32[]{:S(2)}) collective-permute-start(bf16[128,256]{1,0:T(8,128)(2,1)S(1)} %shard_map.115.own), channel_id=1, source_target_pairs={{0,9},{1,4},{3,10},{2,7},{5,12},{4,1},{6,15},{7,2},{9,0},{8,13},{1... | collective-permute-start | bytes 196616 | tf_op jit(solution)/shard_map/ppermute | solution.py:465
  26.2 1.6 %collective-permute-done.15.other = bf16[128,256]{1,0:T(8,128)(2,1)S(1)} collective-permute-done((bf16[128,256]{1,0:T(8,128)(2,1)S(1)}, bf16[128,256]{1,0:T(8,128)(2,1)S(1)}, u32[]{:S(2)}, u32[]{:S(2)}) %collective-permute-start.15) | collective-permute-done | bytes 65568 | tf_op jit(solution)/shard_map/ppermute | solution.py:465
  27.8 1.3 %collective-permute-start.16 = (bf16[128,256]{1,0:T(8,128)(2,1)S(1)}, bf16[128,256]{1,0:T(8,128)(2,1)S(1)}, u32[]{:S(2)}, u32[]{:S(2)}) collective-permute-start(bf16[128,256]{1,0:T(8,128)(2,1)S(1)} %shard_map.118.own), channel_id=1, source_target_pairs={{0,5},{1,2},{3,6},{2,1},{5,0},{4,7},{6,3},{7,4},{9,12},{8,11},{10,... | collective-permute-start | bytes 196616 | tf_op jit(solution)/shard_map/ppermute | solution.py:465
  29.3 2.0 %collective-permute-start.12 = (bf16[128,256]{1,0:T(8,128)(2,1)S(1)}, bf16[128,256]{1,0:T(8,128)(2,1)S(1)}, u32[]{:S(2)}, u32[]{:S(2)}) collective-permute-start(bf16[128,256]{1,0:T(8,128)(2,1)S(1)} %shard_map.116.own), channel_id=1, source_target_pairs={{0,5},{1,2},{3,6},{2,1},{5,0},{4,7},{6,3},{7,4},{9,12},{8,11},{10,... | collective-permute-start | bytes 196616 | tf_op jit(solution)/shard_map/ppermute | solution.py:465
  31.7 1.6 %collective-permute-done.12.other = bf16[128,256]{1,0:T(8,128)(2,1)S(1)} collective-permute-done((bf16[128,256]{1,0:T(8,128)(2,1)S(1)}, bf16[128,256]{1,0:T(8,128)(2,1)S(1)}, u32[]{:S(2)}, u32[]{:S(2)}) %collective-permute-start.12) | collective-permute-done | bytes 65568 | tf_op jit(solution)/shard_map/ppermute | solution.py:465
  34.0 0.6 %collective-permute-done.13.high = bf16[128,256]{1,0:T(8,128)(2,1)S(1)} collective-permute-done((bf16[128,256]{1,0:T(8,128)(2,1)S(1)}, bf16[128,256]{1,0:T(8,128)(2,1)S(1)}, u32[]{:S(2)}, u32[]{:S(2)}) %collective-permute-start.13) | collective-permute-done | bytes 65568 | tf_op jit(solution)/shard_map/ppermute | solution.py:447
  34.6 1.0 %shard_map.121 = (f32[256,128]{1,0:T(8,128)}, f32[1,256,128]{2,1,0:T(8,128)}) custom-call(bf16[2,512,256]{2,1,0:T(8,128)(2,1)S(1)} %get-tuple-element.23.mine_chip, bf16[2,1056,256]{2,1,0:T(8,128)(2,1)S(1)} %collective-permute-done.2.theirs, bf16[128,256]{1,0:T(8,128)(2,1)S(1)} %collective-permute-done.13.high, f32[128,256]{1,0:T(8,128)S(1)} %get-tuple-element.38.my_part, ...), custom_call_target="tpu_custom_call" | custom-call | tf_op jit(solution)/shard_map/pallas_call | solution.py:596
  (32 shorter events, 4.2 us)
Async XLA Ops:
  0.6 1.7 %collective-permute-start = (f32[256,128]{1,0:T(8,128)}, f32[256,128]{1,0:T(8,128)S(1)}, u32[]{:S(2)}, u32[]{:S(2)}) collective-permute-start(f32[256,128]{1,0:T(8,128)} %tgt_own_hbm.1), channel_id=1, source_target_pairs={{0,1},{1,0},{2,3},{3,2},{4,5},{5,4},{6,7},{7,6},{8,9},{9,8},{10,11... | collective-permute-start | bytes 393224 | tf_op jit(solution)/shard_map/ppermute | solution.py:447
  1.1 1.6 %collective-permute-start.1 = (f32[1,256,128]{2,1,0:T(8,128)}, f32[1,256,128]{2,1,0:T(8,128)S(1)}, u32[]{:S(2)}, u32[]{:S(2)}) collective-permute-start(f32[1,256,128]{2,1,0:T(8,128)} %proj_own_hbm.1), channel_id=1, source_target_pairs={{0,1},{1,0},{2,3},{3,2},{4,5},{5,4},{6,7},{7,6},{8,9},{9,8},{10,11... | collective-permute-start | bytes 393224 | tf_op jit(solution)/shard_map/ppermute | solution.py:447
  2.8 7.9 %collective-permute-start.3 = (bf16[2,128,256]{2,1,0:T(8,128)(2,1)S(1)}, bf16[2,128,256]{2,1,0:T(8,128)(2,1)S(1)}, u32[]{:S(2)}, u32[]{:S(2)}) collective-permute-start(bf16[2,128,256]{2,1,0:T(8,128)(2,1)S(1)} %get-tuple-element.31), channel_id=1, source_target_pairs={{0,3},{1,8},{3,0},{2,11},{5,6},{4,13},{6,5},{7,14},{9,10},{8,1},{1... | collective-permute-start | bytes 393224 | tf_op jit(solution)/shard_map/ppermute | solution.py:465
  6.8 3.7 %collective-permute-start.2 = (bf16[2,1056,256]{2,1,0:T(8,128)(2,1)S(1)}, bf16[2,1056,256]{2,1,0:T(8,128)(2,1)S(1)}, u32[]{:S(2)}, u32[]{:S(2)}) collective-permute-start(bf16[2,1056,256]{2,1,0:T(8,128)(2,1)S(1)} %get-tuple-element.25.sent), channel_id=1, source_target_pairs={{0,1},{1,0},{2,3},{3,2},{4,5},{5,4},{6,7},{7,6},{8,9},{9,8},{10,11... | collective-permute-start | bytes 3244040 | tf_op jit(solution)/shard_map/ppermute | solution.py:447
  11.0 4.8 %collective-permute-start.4 = (bf16[128,256]{1,0:T(8,128)(2,1)S(1)}, bf16[128,256]{1,0:T(8,128)(2,1)S(1)}, u32[]{:S(2)}, u32[]{:S(2)}) collective-permute-start(bf16[128,256]{1,0:T(8,128)(2,1)S(1)} %shard_map.109.own), channel_id=1, source_target_pairs={{0,9},{1,4},{3,10},{2,7},{5,12},{4,1},{6,15},{7,2},{9,0},{8,13},{1... | collective-permute-start | bytes 196616 | tf_op jit(solution)/shard_map/ppermute | solution.py:465
  12.8 5.1 %collective-permute-start.8 = (bf16[128,256]{1,0:T(8,128)(2,1)S(1)}, bf16[128,256]{1,0:T(8,128)(2,1)S(1)}, u32[]{:S(2)}, u32[]{:S(2)}) collective-permute-start(bf16[128,256]{1,0:T(8,128)(2,1)S(1)} %shard_map.112.own), channel_id=1, source_target_pairs={{0,9},{1,4},{3,10},{2,7},{5,12},{4,1},{6,15},{7,2},{9,0},{8,13},{1... | collective-permute-start | bytes 196616 | tf_op jit(solution)/shard_map/ppermute | solution.py:465
  14.1 5.4 %collective-permute-start.7 = (f32[2,1,256]{2,1,0:T(1,128)S(1)}, f32[2,1,256]{2,1,0:T(1,128)S(1)}, u32[]{:S(2)}, u32[]{:S(2)}) collective-permute-start(f32[2,1,256]{2,1,0:T(1,128)S(1)} %get-tuple-element.32.energies), channel_id=1, source_target_pairs={{0,3},{1,8},{3,0},{2,11},{5,6},{4,13},{6,5},{7,14},{9,10},{8,1},{1... | collective-permute-start | bytes 6152 | tf_op jit(solution)/shard_map/ppermute | solution.py:465
  15.8 4.3 %collective-permute-start.6 = (bf16[128,256]{1,0:T(8,128)(2,1)S(1)}, bf16[128,256]{1,0:T(8,128)(2,1)S(1)}, u32[]{:S(2)}, u32[]{:S(2)}) collective-permute-start(bf16[128,256]{1,0:T(8,128)(2,1)S(1)} %shard_map.110), channel_id=1, source_target_pairs={{0,4},{1,3},{3,7},{2,0},{5,1},{4,6},{6,2},{7,5},{9,13},{8,10},{10,... | collective-permute-start | bytes 196616 | tf_op jit(solution)/shard_map/ppermute | solution.py:465
  17.1 3.1 %collective-permute-start.5 = (bf16[128,256]{1,0:T(8,128)(2,1)S(1)}, bf16[128,256]{1,0:T(8,128)(2,1)S(1)}, u32[]{:S(2)}, u32[]{:S(2)}) collective-permute-start(bf16[128,256]{1,0:T(8,128)(2,1)S(1)} %shard_map.110), channel_id=1, source_target_pairs={{0,1},{1,0},{2,3},{3,2},{4,5},{5,4},{6,7},{7,6},{8,9},{9,8},{10,11... | collective-permute-start | bytes 196616 | tf_op jit(solution)/shard_map/ppermute | solution.py:447
  18.0 4.3 %collective-permute-start.10 = (bf16[128,256]{1,0:T(8,128)(2,1)S(1)}, bf16[128,256]{1,0:T(8,128)(2,1)S(1)}, u32[]{:S(2)}, u32[]{:S(2)}) collective-permute-start(bf16[128,256]{1,0:T(8,128)(2,1)S(1)} %shard_map.113), channel_id=1, source_target_pairs={{0,4},{1,3},{3,7},{2,0},{5,1},{4,6},{6,2},{7,5},{9,13},{8,10},{10,... | collective-permute-start | bytes 196616 | tf_op jit(solution)/shard_map/ppermute | solution.py:465
  19.4 2.9 %collective-permute-start.9 = (bf16[128,256]{1,0:T(8,128)(2,1)S(1)}, bf16[128,256]{1,0:T(8,128)(2,1)S(1)}, u32[]{:S(2)}, u32[]{:S(2)}) collective-permute-start(bf16[128,256]{1,0:T(8,128)(2,1)S(1)} %shard_map.113), channel_id=1, source_target_pairs={{0,1},{1,0},{2,3},{3,2},{4,5},{5,4},{6,7},{7,6},{8,9},{9,8},{10,11... | collective-permute-start | bytes 196616 | tf_op jit(solution)/shard_map/ppermute | solution.py:447
  19.4 14.0 %collective-permute-start.14 = (bf16[2,256,256]{2,1,0:T(8,128)(2,1)S(1)}, bf16[2,256,256]{2,1,0:T(8,128)(2,1)S(1)}, u32[]{:S(2)}, u32[]{:S(2)}) collective-permute-start(bf16[2,256,256]{2,1,0:T(8,128)(2,1)S(1)} %get-tuple-element.34), channel_id=1, source_target_pairs={{0,1},{1,0},{2,3},{3,2},{4,5},{5,4},{6,7},{7,6},{8,9},{9,8},{10,11... | collective-permute-start | bytes 786440 | tf_op jit(solution)/shard_map/ppermute | solution.py:447
  23.1 4.7 %collective-permute-start.15 = (bf16[128,256]{1,0:T(8,128)(2,1)S(1)}, bf16[128,256]{1,0:T(8,128)(2,1)S(1)}, u32[]{:S(2)}, u32[]{:S(2)}) collective-permute-start(bf16[128,256]{1,0:T(8,128)(2,1)S(1)} %get-tuple-element.35.own), channel_id=1, source_target_pairs={{0,9},{1,4},{3,10},{2,7},{5,12},{4,1},{6,15},{7,2},{9,0},{8,13},{1... | collective-permute-start | bytes 196616 | tf_op jit(solution)/shard_map/ppermute | solution.py:465
  24.0 5.3 %collective-permute-start.11 = (bf16[128,256]{1,0:T(8,128)(2,1)S(1)}, bf16[128,256]{1,0:T(8,128)(2,1)S(1)}, u32[]{:S(2)}, u32[]{:S(2)}) collective-permute-start(bf16[128,256]{1,0:T(8,128)(2,1)S(1)} %shard_map.115.own), channel_id=1, source_target_pairs={{0,9},{1,4},{3,10},{2,7},{5,12},{4,1},{6,15},{7,2},{9,0},{8,13},{1... | collective-permute-start | bytes 196616 | tf_op jit(solution)/shard_map/ppermute | solution.py:465
  26.2 7.3 %collective-permute-start.18 = (f32[128,256]{1,0:T(8,128)S(1)}, f32[128,256]{1,0:T(8,128)S(1)}, u32[]{:S(2)}, u32[]{:S(2)}) collective-permute-start(f32[128,256]{1,0:T(8,128)S(1)} %get-tuple-element.37), channel_id=1, source_target_pairs={{0,1},{1,0},{2,3},{3,2},{4,5},{5,4},{6,7},{7,6},{8,9},{9,8},{10,11... | collective-permute-start | bytes 393224 | tf_op jit(solution)/shard_map/ppermute | solution.py:447
  27.8 3.8 %collective-permute-start.16 = (bf16[128,256]{1,0:T(8,128)(2,1)S(1)}, bf16[128,256]{1,0:T(8,128)(2,1)S(1)}, u32[]{:S(2)}, u32[]{:S(2)}) collective-permute-start(bf16[128,256]{1,0:T(8,128)(2,1)S(1)} %shard_map.118.own), channel_id=1, source_target_pairs={{0,5},{1,2},{3,6},{2,1},{5,0},{4,7},{6,3},{7,4},{9,12},{8,11},{10,... | collective-permute-start | bytes 196616 | tf_op jit(solution)/shard_map/ppermute | solution.py:465
  29.3 3.9 %collective-permute-start.12 = (bf16[128,256]{1,0:T(8,128)(2,1)S(1)}, bf16[128,256]{1,0:T(8,128)(2,1)S(1)}, u32[]{:S(2)}, u32[]{:S(2)}) collective-permute-start(bf16[128,256]{1,0:T(8,128)(2,1)S(1)} %shard_map.116.own), channel_id=1, source_target_pairs={{0,5},{1,2},{3,6},{2,1},{5,0},{4,7},{6,3},{7,4},{9,12},{8,11},{10,... | collective-permute-start | bytes 196616 | tf_op jit(solution)/shard_map/ppermute | solution.py:465
  31.6 1.9 %collective-permute-start.17 = (bf16[128,256]{1,0:T(8,128)(2,1)S(1)}, bf16[128,256]{1,0:T(8,128)(2,1)S(1)}, u32[]{:S(2)}, u32[]{:S(2)}) collective-permute-start(bf16[128,256]{1,0:T(8,128)(2,1)S(1)} %shard_map.119.low), channel_id=1, source_target_pairs={{0,1},{1,0},{2,3},{3,2},{4,5},{5,4},{6,7},{7,6},{8,9},{9,8},{10,11... | collective-permute-start | bytes 196616 | tf_op jit(solution)/shard_map/ppermute | solution.py:447
  33.3 1.3 %collective-permute-start.13 = (bf16[128,256]{1,0:T(8,128)(2,1)S(1)}, bf16[128,256]{1,0:T(8,128)(2,1)S(1)}, u32[]{:S(2)}, u32[]{:S(2)}) collective-permute-start(bf16[128,256]{1,0:T(8,128)(2,1)S(1)} %shard_map.117.high), channel_id=1, source_target_pairs={{0,1},{1,0},{2,3},{3,2},{4,5},{5,4},{6,7},{7,6},{8,9},{9,8},{10,11... | collective-permute-start | bytes 196616 | tf_op jit(solution)/shard_map/ppermute | solution.py:447

commit v26 on v24

--- a/solution.py
+++ b/solution.py
@@ -436,16 +436,16 @@
     tgt_flips = [n_prj << bit for bit in range(n_tgt.bit_length() - 1)]
     prj_flips = [1 << bit for bit in range(n_prj.bit_length() - 1)]
     far_first = tgt_flips[::-1]
-    flips = (prj_flips + far_first, far_first + prj_flips)
+    flips = [(prj_flips + order, far_first + prj_flips) for order in (far_first, tgt_flips)]
     neighbours = (prj_flips[0], far_first[0] // n_prj)
     gate_levels = (len(prj_flips) - 1, len(tgt_flips) - 1)
     n_steps = len(tgt_flips) + len(prj_flips)
 
-    def exchanged(step, block, crossed=0):
+    def exchanged(step, block, rate=0, crossed=0):
         pairs = []
         for place in range(n_tgt * n_prj):
             for kind in range(2):
-                there = place ^ flips[kind][step]
+                there = place ^ flips[rate][kind][step]
                 to_core = kind ^ crossed ^ parity(there)
                 pairs.append((place * n_core + (kind ^ parity(place)), there * n_core + to_core))
         return lax.ppermute(block, DEVICES, pairs)
@@ -454,11 +454,11 @@
     sums = in_vmem((two_cols, points), jnp.bfloat16)
     segment = in_vmem((two_cols, rows), jnp.float32)
 
-    def summed(halves, until):
+    def summed(halves, until, rate):
         totals = []
         for half, block in enumerate(halves):
             for step in range(1, until):
-                other = exchanged(step, block)
+                other = exchanged(step, block, rate)
                 (block,) = run(functools.partial(add_kernel, step, half), [sums], gate, block, other)
             totals.append(block)
         return totals
@@ -538,7 +538,7 @@
     (low, high), energies = lax.optimization_barrier((halves, energies))
     neighbour_energies = exchanged(0, energies)
     halves = low, high
-    parts = summed(halves, n_steps - 1)
+    parts = summed(halves, n_steps - 1, 0)
     low, high = [(other_core(block), exchanged(n_steps - 1, block, crossed=1)) for block in parts]
     (states,) = run(
         low_kernel,
@@ -560,7 +560,7 @@
         weights,
     )
     other_half = other_core(half_send)
-    fields = summed(halves, n_steps)
+    fields = summed(halves, n_steps, 1)
     low, high = swapped(fields)
     low, high = swapped(fields)
     my_part, other_new = run(

time: 35.5 us -> 36.3 us (1.023)
  waiting for transfers between devices: 9.06 us -> 10.6 us
  starting transfers between devices: 18.2 us -> 17.4 us
    ppermute x10, waiting for transfers between devices: 7.01 us -> 8.44 us  [exchanged(): return lax.ppermute(block, DEVICES, pairs)]
    ppermute x10, starting transfers between devices: 14.8 us -> 14.1 us  [exchanged(): return lax.ppermute(block, DEVICES, pairs)]
  transfers between devices with their start and end apart: 19 -> 19, of which waited for: 11 -> 10; matrix products, arithmetic and copies ran while one was open for 0% -> 0% of each run, Pallas kernels for 17% -> 16%
where the time goes in v26:
time: 36.3 us; the launch traced here: 36.1 us
  starting transfers between devices  17.4 us (48%)
  waiting for transfers between devices  10.6 us (29%)
  Pallas kernels  7.36 us (20%)
  between operations  0.79 us (2%)
    ppermute x10, starting transfers between devices, exchanged(): return lax.ppermute(block, DEVICES, pairs)  14.1 us
    ppermute x10, waiting for transfers between devices, exchanged(): return lax.ppermute(block, DEVICES, pairs)  8.44 us
    ppermute x9, starting transfers between devices, other_core(): return lax.ppermute(block, 'rep', [(0, 1), (1, 0)])  3.31 us
    pallas_call x12, Pallas kernels, run(): return call(kernel, out_shape, [VMEM] * len(blocks))(*blocks)  2.75 us
    ppermute x9, waiting for transfers between devices, other_core(): return lax.ppermute(block, 'rep', [(0, 1), (1, 0)])  2.13 us
    pallas_call x1, Pallas kernels, shards(): call(functools.partial(side_kernel, gate_levels, neighbours), [pair, pair...  1.26 us
    pallas_call x1, Pallas kernels, shards(): call(functools.partial(sent_kernel, neighbours), [in_vmem((2, 4 * rows +...  1.24 us
    pallas_call x1, Pallas kernels, shards(): call(load_kernel, [in_vmem((2, 1, rows), jnp.float32), in_vmem((2, two_co...  1.14 us
  transfers between devices with their start and end apart: 19, of which 10 were waited for; matrix products, arithmetic and copies ran while one was open for 0% of the time, Pallas kernels for 16%

profile of v26, /device:TPU:0, one launch (start us, length us, event | category | flops | bytes accessed | tf_op | source)
XLA Modules:
  0.0 36.1 jit_solution(9909687210963817195)
XLA Ops:
  1.2 1.1 %shard_map.104 = (f32[2,1,256]{2,1,0:T(1,128)S(1)}, f32[2,128,256]{2,1,0:T(8,128)S(1)}) custom-call(f32[256]{0:T(256)} %tgt_energy_hbm.1, f32[1,256]{1,0:T(1,128)} %proj_energy_hbm.1, f32[256,128]{1,0:T(8,128)} %tgt_own_hbm.1, f32[1,256,128]{2,1,0:T(8,128)} %proj_own_hbm.1), custom_call_target="tpu_custom_call" | custom-call | flops 67108864 | bytes 4194304 | tf_op jit(solution)/shard_map/pallas_call | solution.py:473
  2.8 2.7 %collective-permute-start.3 = (bf16[2,128,256]{2,1,0:T(8,128)(2,1)S(1)}, bf16[2,128,256]{2,1,0:T(8,128)(2,1)S(1)}, u32[]{:S(2)}, u32[]{:S(2)}) collective-permute-start(bf16[2,128,256]{2,1,0:T(8,128)(2,1)S(1)} %get-tuple-element.36), channel_id=1, source_target_pairs={{0,3},{1,8},{3,0},{2,11},{5,6},{4,13},{6,5},{7,14},{9,10},{8,1},{1... | collective-permute-start | bytes 393224 | tf_op jit(solution)/shard_map/ppermute | solution.py:451
  5.5 1.2 %shard_map.107 = (bf16[2,1056,256]{2,1,0:T(8,128)(2,1)S(1)}, f32[1,1,256]{2,1,0:T(1,128)S(1)}) custom-call(f32[256]{0:T(256)} %weight_hbm.1, bf16[2,4,256,256]{3,2,1,0:T(8,128)(2,1)} %bitcast.3, bf16[2,8,256,256]{3,2,1,0:T(8,128)(2,1)} %proj_hbm.3, f32[2,128,256]{2,1,0:T(8,128)S(1)} %get-tuple-element.27.chip_amp, f32[2,1,256]{2,1,0:T(1,128)S(1)} %get-tuple-element.29.energy), custom_call_target="tpu_custom_call" | custom-call | tf_op jit(solution)/shard_map/pallas_call | solution.py:497
  6.8 1.4 %collective-permute-start.2 = (bf16[2,1056,256]{2,1,0:T(8,128)(2,1)S(1)}, bf16[2,1056,256]{2,1,0:T(8,128)(2,1)S(1)}, u32[]{:S(2)}, u32[]{:S(2)}) collective-permute-start(bf16[2,1056,256]{2,1,0:T(8,128)(2,1)S(1)} %get-tuple-element.30.sent), channel_id=1, source_target_pairs={{0,1},{1,0},{2,3},{3,2},{4,5},{5,4},{6,7},{7,6},{8,9},{9,8},{10,11... | collective-permute-start | bytes 3244040 | tf_op jit(solution)/shard_map/ppermute | solution.py:433
  8.1 1.3 %shard_map.106 = (bf16[2,512,256]{2,1,0:T(8,128)(2,1)S(1)}, bf16[2,512,256]{2,1,0:T(8,128)(2,1)S(1)}, bf16[2,256,256]{2,1,0:T(8,128)(2,1)S(1)}, f32[3,2,1,256]{3,2,1,0:T(1,128)S(1)}) custom-call(s32[2,4]{1,0:T(2,128)} %bitcast.5, s32[2,4]{1,0:T(2,128)} %bitcast.6, bf16[2,4,256,256]{3,2,1,0:T(8,128)(2,1)} %bitcast.4, bf16[2,8,256,256]{3,2,1,0:T(8,128)(2,1)} %proj_hbm.3, ...), custom_call_target="tpu_custom_call" | custom-call | flops 34359738368 | bytes 65536 | tf_op jit(solution)/shard_map/pallas_call | solution.py:506
  9.4 1.1 %collective-permute-done.2.theirs = bf16[2,1056,256]{2,1,0:T(8,128)(2,1)S(1)} collective-permute-done((bf16[2,1056,256]{2,1,0:T(8,128)(2,1)S(1)}, bf16[2,1056,256]{2,1,0:T(8,128)(2,1)S(1)}, u32[]{:S(2)}, u32[]{:S(2)}) %collective-permute-start.2) | collective-permute-done | bytes 1081376 | tf_op jit(solution)/shard_map/ppermute | solution.py:433
  11.1 1.5 %collective-permute-start.4 = (bf16[128,256]{1,0:T(8,128)(2,1)S(1)}, bf16[128,256]{1,0:T(8,128)(2,1)S(1)}, u32[]{:S(2)}, u32[]{:S(2)}) collective-permute-start(bf16[128,256]{1,0:T(8,128)(2,1)S(1)} %get-tuple-element.40.own), channel_id=1, source_target_pairs={{0,9},{1,4},{3,10},{2,7},{5,12},{4,1},{6,15},{7,2},{9,0},{8,13},{1... | collective-permute-start | bytes 196616 | tf_op jit(solution)/shard_map/ppermute | solution.py:451
  12.7 1.2 %collective-permute-start.8 = (bf16[128,256]{1,0:T(8,128)(2,1)S(1)}, bf16[128,256]{1,0:T(8,128)(2,1)S(1)}, u32[]{:S(2)}, u32[]{:S(2)}) collective-permute-start(bf16[128,256]{1,0:T(8,128)(2,1)S(1)} %get-tuple-element.42.own), channel_id=1, source_target_pairs={{0,9},{1,4},{3,10},{2,7},{5,12},{4,1},{6,15},{7,2},{9,0},{8,13},{1... | collective-permute-start | bytes 196616 | tf_op jit(solution)/shard_map/ppermute | solution.py:451
  13.8 1.4 %collective-permute-start.7 = (f32[2,1,256]{2,1,0:T(1,128)S(1)}, f32[2,1,256]{2,1,0:T(1,128)S(1)}, u32[]{:S(2)}, u32[]{:S(2)}) collective-permute-start(f32[2,1,256]{2,1,0:T(1,128)S(1)} %get-tuple-element.41.energies), channel_id=1, source_target_pairs={{0,3},{1,8},{3,0},{2,11},{5,6},{4,13},{6,5},{7,14},{9,10},{8,1},{1... | collective-permute-start | bytes 6152 | tf_op jit(solution)/shard_map/ppermute | solution.py:451
  15.3 0.6 %collective-permute-done.4.other = bf16[128,256]{1,0:T(8,128)(2,1)S(1)} collective-permute-done((bf16[128,256]{1,0:T(8,128)(2,1)S(1)}, bf16[128,256]{1,0:T(8,128)(2,1)S(1)}, u32[]{:S(2)}, u32[]{:S(2)}) %collective-permute-start.4) | collective-permute-done | bytes 65568 | tf_op jit(solution)/shard_map/ppermute | solution.py:451
  15.9 1.2 %collective-permute-start.6 = (bf16[128,256]{1,0:T(8,128)(2,1)S(1)}, bf16[128,256]{1,0:T(8,128)(2,1)S(1)}, u32[]{:S(2)}, u32[]{:S(2)}) collective-permute-start(bf16[128,256]{1,0:T(8,128)(2,1)S(1)} %shard_map.110), channel_id=1, source_target_pairs={{0,4},{1,3},{3,7},{2,0},{5,1},{4,6},{6,2},{7,5},{9,13},{8,10},{10,... | collective-permute-start | bytes 196616 | tf_op jit(solution)/shard_map/ppermute | solution.py:451
  17.1 0.7 %collective-permute-start.5 = (bf16[128,256]{1,0:T(8,128)(2,1)S(1)}, bf16[128,256]{1,0:T(8,128)(2,1)S(1)}, u32[]{:S(2)}, u32[]{:S(2)}) collective-permute-start(bf16[128,256]{1,0:T(8,128)(2,1)S(1)} %shard_map.110), channel_id=1, source_target_pairs={{0,1},{1,0},{2,3},{3,2},{4,5},{5,4},{6,7},{7,6},{8,9},{9,8},{10,11... | collective-permute-start | bytes 196616 | tf_op jit(solution)/shard_map/ppermute | solution.py:433
  18.0 1.5 %collective-permute-start.10 = (bf16[128,256]{1,0:T(8,128)(2,1)S(1)}, bf16[128,256]{1,0:T(8,128)(2,1)S(1)}, u32[]{:S(2)}, u32[]{:S(2)}) collective-permute-start(bf16[128,256]{1,0:T(8,128)(2,1)S(1)} %shard_map.112), channel_id=1, source_target_pairs={{0,4},{1,3},{3,7},{2,0},{5,1},{4,6},{6,2},{7,5},{9,13},{8,10},{10,... | collective-permute-start | bytes 196616 | tf_op jit(solution)/shard_map/ppermute | solution.py:451
  20.8 1.6 %collective-permute-done.10.high_there = bf16[128,256]{1,0:T(8,128)(2,1)S(1)} collective-permute-done((bf16[128,256]{1,0:T(8,128)(2,1)S(1)}, bf16[128,256]{1,0:T(8,128)(2,1)S(1)}, u32[]{:S(2)}, u32[]{:S(2)}) %collective-permute-start.10) | collective-permute-done | bytes 65568 | tf_op jit(solution)/shard_map/ppermute | solution.py:451
  22.3 0.8 %shard_map.113 = (bf16[128,256]{1,0:T(8,128)(2,1)S(1)}, bf16[128,256]{1,0:T(8,128)(2,1)S(1)}, f32[128,256]{1,0:T(8,128)S(1)}, f32[128,256]{1,0:T(8,128)S(1)}) custom-call(bf16[2,512,256]{2,1,0:T(8,128)(2,1)S(1)} %get-tuple-element.28.mine_chip, bf16[2,512,256]{2,1,0:T(8,128)(2,1)S(1)} %get-tuple-element.32.mine_far, ...), custom_call_target="tpu_custom_call" | custom-call | tf_op jit(solution)/shard_map/pallas_call | solution.py:430
  23.2 0.7 %collective-permute-start.15 = (bf16[128,256]{1,0:T(8,128)(2,1)S(1)}, bf16[128,256]{1,0:T(8,128)(2,1)S(1)}, u32[]{:S(2)}, u32[]{:S(2)}) collective-permute-start(bf16[128,256]{1,0:T(8,128)(2,1)S(1)} %get-tuple-element.45.own), channel_id=1, source_target_pairs={{0,5},{1,4},{3,6},{2,7},{5,0},{4,1},{6,3},{7,2},{9,12},{8,13},{10,... | collective-permute-start | bytes 196616 | tf_op jit(solution)/shard_map/ppermute | solution.py:451
  23.9 1.1 %collective-permute-start.11 = (bf16[128,256]{1,0:T(8,128)(2,1)S(1)}, bf16[128,256]{1,0:T(8,128)(2,1)S(1)}, u32[]{:S(2)}, u32[]{:S(2)}) collective-permute-start(bf16[128,256]{1,0:T(8,128)(2,1)S(1)} %get-tuple-element.43.own), channel_id=1, source_target_pairs={{0,5},{1,4},{3,6},{2,7},{5,0},{4,1},{6,3},{7,2},{9,12},{8,13},{10,... | collective-permute-start | bytes 196616 | tf_op jit(solution)/shard_map/ppermute | solution.py:451
  25.0 2.6 %collective-permute-done.15.other = bf16[128,256]{1,0:T(8,128)(2,1)S(1)} collective-permute-done((bf16[128,256]{1,0:T(8,128)(2,1)S(1)}, bf16[128,256]{1,0:T(8,128)(2,1)S(1)}, u32[]{:S(2)}, u32[]{:S(2)}) %collective-permute-start.15) | collective-permute-done | bytes 65568 | tf_op jit(solution)/shard_map/ppermute | solution.py:451
  27.6 1.0 %collective-permute-start.16 = (bf16[128,256]{1,0:T(8,128)(2,1)S(1)}, bf16[128,256]{1,0:T(8,128)(2,1)S(1)}, u32[]{:S(2)}, u32[]{:S(2)}) collective-permute-start(bf16[128,256]{1,0:T(8,128)(2,1)S(1)} %shard_map.116.own), channel_id=1, source_target_pairs={{0,9},{1,2},{3,10},{2,1},{5,12},{4,7},{6,15},{7,4},{9,0},{8,11},{1... | collective-permute-start | bytes 196616 | tf_op jit(solution)/shard_map/ppermute | solution.py:451
  28.7 1.7 %collective-permute-start.12 = (bf16[128,256]{1,0:T(8,128)(2,1)S(1)}, bf16[128,256]{1,0:T(8,128)(2,1)S(1)}, u32[]{:S(2)}, u32[]{:S(2)}) collective-permute-start(bf16[128,256]{1,0:T(8,128)(2,1)S(1)} %shard_map.114.own), channel_id=1, source_target_pairs={{0,9},{1,2},{3,10},{2,1},{5,12},{4,7},{6,15},{7,4},{9,0},{8,11},{1... | collective-permute-start | bytes 196616 | tf_op jit(solution)/shard_map/ppermute | solution.py:451
  30.4 1.8 %collective-permute-done.16.other = bf16[128,256]{1,0:T(8,128)(2,1)S(1)} collective-permute-done((bf16[128,256]{1,0:T(8,128)(2,1)S(1)}, bf16[128,256]{1,0:T(8,128)(2,1)S(1)}, u32[]{:S(2)}, u32[]{:S(2)}) %collective-permute-start.16) | collective-permute-done | bytes 65568 | tf_op jit(solution)/shard_map/ppermute | solution.py:451
  32.4 1.4 %collective-permute-done.12.other = bf16[128,256]{1,0:T(8,128)(2,1)S(1)} collective-permute-done((bf16[128,256]{1,0:T(8,128)(2,1)S(1)}, bf16[128,256]{1,0:T(8,128)(2,1)S(1)}, u32[]{:S(2)}, u32[]{:S(2)}) %collective-permute-start.12) | collective-permute-done | bytes 65568 | tf_op jit(solution)/shard_map/ppermute | solution.py:451
  34.4 0.7 %collective-permute-done.13.high = bf16[128,256]{1,0:T(8,128)(2,1)S(1)} collective-permute-done((bf16[128,256]{1,0:T(8,128)(2,1)S(1)}, bf16[128,256]{1,0:T(8,128)(2,1)S(1)}, u32[]{:S(2)}, u32[]{:S(2)}) %collective-permute-start.13) | collective-permute-done | bytes 65568 | tf_op jit(solution)/shard_map/ppermute | solution.py:433
  35.1 1.0 %shard_map.119 = (f32[256,128]{1,0:T(8,128)}, f32[1,256,128]{2,1,0:T(8,128)}) custom-call(bf16[2,512,256]{2,1,0:T(8,128)(2,1)S(1)} %get-tuple-element.28.mine_chip, bf16[2,1056,256]{2,1,0:T(8,128)(2,1)S(1)} %collective-permute-done.2.theirs, bf16[128,256]{1,0:T(8,128)(2,1)S(1)} %collective-permute-done.13.high, f32[128,256]{1,0:T(8,128)S(1)} %get-tuple-element.48.my_part, ...), custom_call_target="tpu_custom_call" | custom-call | tf_op jit(solution)/shard_map/pallas_call | solution.py:580
  (30 shorter events, 3.9 us)
Async XLA Ops:
  0.6 1.7 %collective-permute-start = (f32[256,128]{1,0:T(8,128)}, f32[256,128]{1,0:T(8,128)S(1)}, u32[]{:S(2)}, u32[]{:S(2)}) collective-permute-start(f32[256,128]{1,0:T(8,128)} %tgt_own_hbm.1), channel_id=1, source_target_pairs={{0,1},{1,0},{2,3},{3,2},{4,5},{5,4},{6,7},{7,6},{8,9},{9,8},{10,11... | collective-permute-start | bytes 393224 | tf_op jit(solution)/shard_map/ppermute | solution.py:433
  1.1 1.6 %collective-permute-start.1 = (f32[1,256,128]{2,1,0:T(8,128)}, f32[1,256,128]{2,1,0:T(8,128)S(1)}, u32[]{:S(2)}, u32[]{:S(2)}) collective-permute-start(f32[1,256,128]{2,1,0:T(8,128)} %proj_own_hbm.1), channel_id=1, source_target_pairs={{0,1},{1,0},{2,3},{3,2},{4,5},{5,4},{6,7},{7,6},{8,9},{9,8},{10,11... | collective-permute-start | bytes 393224 | tf_op jit(solution)/shard_map/ppermute | solution.py:433
  2.8 7.9 %collective-permute-start.3 = (bf16[2,128,256]{2,1,0:T(8,128)(2,1)S(1)}, bf16[2,128,256]{2,1,0:T(8,128)(2,1)S(1)}, u32[]{:S(2)}, u32[]{:S(2)}) collective-permute-start(bf16[2,128,256]{2,1,0:T(8,128)(2,1)S(1)} %get-tuple-element.36), channel_id=1, source_target_pairs={{0,3},{1,8},{3,0},{2,11},{5,6},{4,13},{6,5},{7,14},{9,10},{8,1},{1... | collective-permute-start | bytes 393224 | tf_op jit(solution)/shard_map/ppermute | solution.py:451
  6.8 3.7 %collective-permute-start.2 = (bf16[2,1056,256]{2,1,0:T(8,128)(2,1)S(1)}, bf16[2,1056,256]{2,1,0:T(8,128)(2,1)S(1)}, u32[]{:S(2)}, u32[]{:S(2)}) collective-permute-start(bf16[2,1056,256]{2,1,0:T(8,128)(2,1)S(1)} %get-tuple-element.30.sent), channel_id=1, source_target_pairs={{0,1},{1,0},{2,3},{3,2},{4,5},{5,4},{6,7},{7,6},{8,9},{9,8},{10,11... | collective-permute-start | bytes 3244040 | tf_op jit(solution)/shard_map/ppermute | solution.py:433
  11.1 4.8 %collective-permute-start.4 = (bf16[128,256]{1,0:T(8,128)(2,1)S(1)}, bf16[128,256]{1,0:T(8,128)(2,1)S(1)}, u32[]{:S(2)}, u32[]{:S(2)}) collective-permute-start(bf16[128,256]{1,0:T(8,128)(2,1)S(1)} %get-tuple-element.40.own), channel_id=1, source_target_pairs={{0,9},{1,4},{3,10},{2,7},{5,12},{4,1},{6,15},{7,2},{9,0},{8,13},{1... | collective-permute-start | bytes 196616 | tf_op jit(solution)/shard_map/ppermute | solution.py:451
  12.7 5.3 %collective-permute-start.8 = (bf16[128,256]{1,0:T(8,128)(2,1)S(1)}, bf16[128,256]{1,0:T(8,128)(2,1)S(1)}, u32[]{:S(2)}, u32[]{:S(2)}) collective-permute-start(bf16[128,256]{1,0:T(8,128)(2,1)S(1)} %get-tuple-element.42.own), channel_id=1, source_target_pairs={{0,9},{1,4},{3,10},{2,7},{5,12},{4,1},{6,15},{7,2},{9,0},{8,13},{1... | collective-permute-start | bytes 196616 | tf_op jit(solution)/shard_map/ppermute | solution.py:451
  13.8 5.7 %collective-permute-start.7 = (f32[2,1,256]{2,1,0:T(1,128)S(1)}, f32[2,1,256]{2,1,0:T(1,128)S(1)}, u32[]{:S(2)}, u32[]{:S(2)}) collective-permute-start(f32[2,1,256]{2,1,0:T(1,128)S(1)} %get-tuple-element.41.energies), channel_id=1, source_target_pairs={{0,3},{1,8},{3,0},{2,11},{5,6},{4,13},{6,5},{7,14},{9,10},{8,1},{1... | collective-permute-start | bytes 6152 | tf_op jit(solution)/shard_map/ppermute | solution.py:451
  15.9 4.3 %collective-permute-start.6 = (bf16[128,256]{1,0:T(8,128)(2,1)S(1)}, bf16[128,256]{1,0:T(8,128)(2,1)S(1)}, u32[]{:S(2)}, u32[]{:S(2)}) collective-permute-start(bf16[128,256]{1,0:T(8,128)(2,1)S(1)} %shard_map.110), channel_id=1, source_target_pairs={{0,4},{1,3},{3,7},{2,0},{5,1},{4,6},{6,2},{7,5},{9,13},{8,10},{10,... | collective-permute-start | bytes 196616 | tf_op jit(solution)/shard_map/ppermute | solution.py:451
  17.1 3.1 %collective-permute-start.5 = (bf16[128,256]{1,0:T(8,128)(2,1)S(1)}, bf16[128,256]{1,0:T(8,128)(2,1)S(1)}, u32[]{:S(2)}, u32[]{:S(2)}) collective-permute-start(bf16[128,256]{1,0:T(8,128)(2,1)S(1)} %shard_map.110), channel_id=1, source_target_pairs={{0,1},{1,0},{2,3},{3,2},{4,5},{5,4},{6,7},{7,6},{8,9},{9,8},{10,11... | collective-permute-start | bytes 196616 | tf_op jit(solution)/shard_map/ppermute | solution.py:433
  18.0 4.3 %collective-permute-start.10 = (bf16[128,256]{1,0:T(8,128)(2,1)S(1)}, bf16[128,256]{1,0:T(8,128)(2,1)S(1)}, u32[]{:S(2)}, u32[]{:S(2)}) collective-permute-start(bf16[128,256]{1,0:T(8,128)(2,1)S(1)} %shard_map.112), channel_id=1, source_target_pairs={{0,4},{1,3},{3,7},{2,0},{5,1},{4,6},{6,2},{7,5},{9,13},{8,10},{10,... | collective-permute-start | bytes 196616 | tf_op jit(solution)/shard_map/ppermute | solution.py:451
  19.5 2.9 %collective-permute-start.9 = (bf16[128,256]{1,0:T(8,128)(2,1)S(1)}, bf16[128,256]{1,0:T(8,128)(2,1)S(1)}, u32[]{:S(2)}, u32[]{:S(2)}) collective-permute-start(bf16[128,256]{1,0:T(8,128)(2,1)S(1)} %shard_map.112), channel_id=1, source_target_pairs={{0,1},{1,0},{2,3},{3,2},{4,5},{5,4},{6,7},{7,6},{8,9},{9,8},{10,11... | collective-permute-start | bytes 196616 | tf_op jit(solution)/shard_map/ppermute | solution.py:433
  19.5 14.3 %collective-permute-start.14 = (bf16[2,256,256]{2,1,0:T(8,128)(2,1)S(1)}, bf16[2,256,256]{2,1,0:T(8,128)(2,1)S(1)}, u32[]{:S(2)}, u32[]{:S(2)}) collective-permute-start(bf16[2,256,256]{2,1,0:T(8,128)(2,1)S(1)} %get-tuple-element.44), channel_id=1, source_target_pairs={{0,1},{1,0},{2,3},{3,2},{4,5},{5,4},{6,7},{7,6},{8,9},{9,8},{10,11... | collective-permute-start | bytes 786440 | tf_op jit(solution)/shard_map/ppermute | solution.py:433
  23.2 4.4 %collective-permute-start.15 = (bf16[128,256]{1,0:T(8,128)(2,1)S(1)}, bf16[128,256]{1,0:T(8,128)(2,1)S(1)}, u32[]{:S(2)}, u32[]{:S(2)}) collective-permute-start(bf16[128,256]{1,0:T(8,128)(2,1)S(1)} %get-tuple-element.45.own), channel_id=1, source_target_pairs={{0,5},{1,4},{3,6},{2,7},{5,0},{4,1},{6,3},{7,2},{9,12},{8,13},{10,... | collective-permute-start | bytes 196616 | tf_op jit(solution)/shard_map/ppermute | solution.py:451
  23.9 4.8 %collective-permute-start.11 = (bf16[128,256]{1,0:T(8,128)(2,1)S(1)}, bf16[128,256]{1,0:T(8,128)(2,1)S(1)}, u32[]{:S(2)}, u32[]{:S(2)}) collective-permute-start(bf16[128,256]{1,0:T(8,128)(2,1)S(1)} %get-tuple-element.43.own), channel_id=1, source_target_pairs={{0,5},{1,4},{3,6},{2,7},{5,0},{4,1},{6,3},{7,2},{9,12},{8,13},{10,... | collective-permute-start | bytes 196616 | tf_op jit(solution)/shard_map/ppermute | solution.py:451
  25.0 8.9 %collective-permute-start.18 = (f32[128,256]{1,0:T(8,128)S(1)}, f32[128,256]{1,0:T(8,128)S(1)}, u32[]{:S(2)}, u32[]{:S(2)}) collective-permute-start(f32[128,256]{1,0:T(8,128)S(1)} %get-tuple-element.47), channel_id=1, source_target_pairs={{0,1},{1,0},{2,3},{3,2},{4,5},{5,4},{6,7},{7,6},{8,9},{9,8},{10,11... | collective-permute-start | bytes 393224 | tf_op jit(solution)/shard_map/ppermute | solution.py:433
  27.6 4.7 %collective-permute-start.16 = (bf16[128,256]{1,0:T(8,128)(2,1)S(1)}, bf16[128,256]{1,0:T(8,128)(2,1)S(1)}, u32[]{:S(2)}, u32[]{:S(2)}) collective-permute-start(bf16[128,256]{1,0:T(8,128)(2,1)S(1)} %shard_map.116.own), channel_id=1, source_target_pairs={{0,9},{1,2},{3,10},{2,1},{5,12},{4,7},{6,15},{7,4},{9,0},{8,11},{1... | collective-permute-start | bytes 196616 | tf_op jit(solution)/shard_map/ppermute | solution.py:451
  28.7 5.1 %collective-permute-start.12 = (bf16[128,256]{1,0:T(8,128)(2,1)S(1)}, bf16[128,256]{1,0:T(8,128)(2,1)S(1)}, u32[]{:S(2)}, u32[]{:S(2)}) collective-permute-start(bf16[128,256]{1,0:T(8,128)(2,1)S(1)} %shard_map.114.own), channel_id=1, source_target_pairs={{0,9},{1,2},{3,10},{2,1},{5,12},{4,7},{6,15},{7,4},{9,0},{8,11},{1... | collective-permute-start | bytes 196616 | tf_op jit(solution)/shard_map/ppermute | solution.py:451
  32.3 1.6 %collective-permute-start.17 = (bf16[128,256]{1,0:T(8,128)(2,1)S(1)}, bf16[128,256]{1,0:T(8,128)(2,1)S(1)}, u32[]{:S(2)}, u32[]{:S(2)}) collective-permute-start(bf16[128,256]{1,0:T(8,128)(2,1)S(1)} %shard_map.117.low), channel_id=1, source_target_pairs={{0,1},{1,0},{2,3},{3,2},{4,5},{5,4},{6,7},{7,6},{8,9},{9,8},{10,11... | collective-permute-start | bytes 196616 | tf_op jit(solution)/shard_map/ppermute | solution.py:433
  33.8 1.3 %collective-permute-start.13 = (bf16[128,256]{1,0:T(8,128)(2,1)S(1)}, bf16[128,256]{1,0:T(8,128)(2,1)S(1)}, u32[]{:S(2)}, u32[]{:S(2)}) collective-permute-start(bf16[128,256]{1,0:T(8,128)(2,1)S(1)} %shard_map.115.high), channel_id=1, source_target_pairs={{0,1},{1,0},{2,3},{3,2},{4,5},{5,4},{6,7},{7,6},{8,9},{9,8},{10,11... | collective-permute-start | bytes 196616 | tf_op jit(solution)/shard_map/ppermute | solution.py:433

commit v27 on v24

--- a/solution.py
+++ b/solution.py
@@ -76,6 +76,7 @@
 
 PIECES = 16
 
+EVEN = pl.CostEstimate(flops=1 << 32, bytes_accessed=1 << 16, transcendentals=0)
 BEHIND = pl.CostEstimate(flops=1 << 35, bytes_accessed=1 << 16, transcendentals=0)
 
 
@@ -264,7 +265,8 @@
     by_core(body)
 
 
-def add_kernel(level, half, gate, own, other, out_ref):
+def add_kernel(level, half, gate, own, other, *rest):
+    out_ref = rest[-1]
     out_ref[...] = bf16(gate[level, half] * (f32(own[...]) + f32(other[...])))
 
 
@@ -454,12 +456,15 @@
     sums = in_vmem((two_cols, points), jnp.bfloat16)
     segment = in_vmem((two_cols, rows), jnp.float32)
 
-    def summed(halves, until):
+    def summed(halves, until, *ahead):
         totals = []
         for half, block in enumerate(halves):
             for step in range(1, until):
                 other = exchanged(step, block)
-                (block,) = run(functools.partial(add_kernel, step, half), [sums], gate, block, other)
+                kernel = functools.partial(add_kernel, step, half)
+                blocks = [gate, block, other] + (list(ahead) if half and step == 1 else [])
+                cost = EVEN if half else None
+                (block,) = call(kernel, [sums], [VMEM] * len(blocks), cost=cost)(*blocks)
             totals.append(block)
         return totals
 
@@ -538,7 +543,7 @@
     (low, high), energies = lax.optimization_barrier((halves, energies))
     neighbour_energies = exchanged(0, energies)
     halves = low, high
-    parts = summed(halves, n_steps - 1)
+    parts = summed(halves, n_steps - 1, neighbour_energies)
     low, high = [(other_core(block), exchanged(n_steps - 1, block, crossed=1)) for block in parts]
     (states,) = run(
         low_kernel,
@@ -559,8 +564,9 @@
         gate,
         weights,
     )
+    fields = summed(halves, n_steps)
+    fields[0], half_send = lax.optimization_barrier((fields[0], half_send))
     other_half = other_core(half_send)
-    fields = summed(halves, n_steps)
     low, high = swapped(fields)
     low, high = swapped(fields)
     my_part, other_new = run(

time: 35.5 us -> 35.5 us (level)
    pallas_call x12 -> x6, Pallas kernels: 2.75 us -> 2.6 us  [run(): return call(kernel, out_shape, [VMEM] * len(blocks))(*blocks)]
  transfers between devices with their start and end apart: 19 -> 19, of which waited for: 11 -> 11; matrix products, arithmetic and copies ran while one was open for 0% -> 0% of each run, Pallas kernels for 17% -> 14%
where the time goes in v27:
time: 35.5 us; the launch traced here: 35.4 us
  starting transfers between devices  18.2 us (51%)
  waiting for transfers between devices  9.02 us (25%)
  Pallas kernels  7.35 us (21%)
  between operations  0.76 us (2%)
    ppermute x10, starting transfers between devices, exchanged(): return lax.ppermute(block, DEVICES, pairs)  14.8 us
    ppermute x10, waiting for transfers between devices, exchanged(): return lax.ppermute(block, DEVICES, pairs)  6.98 us
    ppermute x9, starting transfers between devices, other_core(): return lax.ppermute(block, 'rep', [(0, 1), (1, 0)])  3.45 us
    pallas_call x6, Pallas kernels, run(): return call(kernel, out_shape, [VMEM] * len(blocks))(*blocks)  2.6 us
    ppermute x9, waiting for transfers between devices, other_core(): return lax.ppermute(block, 'rep', [(0, 1), (1, 0)])  2.04 us
    pallas_call x1, Pallas kernels, shards(): call(functools.partial(side_kernel, gate_levels, neighbours), [pair, pair...  1.26 us
    pallas_call x1, Pallas kernels, shards(): call(functools.partial(sent_kernel, neighbours), [in_vmem((2, 4 * rows +...  1.24 us
    pallas_call x1, Pallas kernels, shards(): call(load_kernel, [in_vmem((2, 1, rows), jnp.float32), in_vmem((2, two_co...  1.14 us
  transfers between devices with their start and end apart: 19, of which 11 were waited for; matrix products, arithmetic and copies ran while one was open for 0% of the time, Pallas kernels for 14%

profile of v27, /device:TPU:0, one launch (start us, length us, event | category | flops | bytes accessed | tf_op | source)
XLA Modules:
  0.0 35.4 jit_solution(1103388320746089257)
XLA Ops:
  1.2 1.1 %shard_map.104 = (f32[2,1,256]{2,1,0:T(1,128)S(1)}, f32[2,128,256]{2,1,0:T(8,128)S(1)}) custom-call(f32[256]{0:T(256)} %tgt_energy_hbm.1, f32[1,256]{1,0:T(1,128)} %proj_energy_hbm.1, f32[256,128]{1,0:T(8,128)} %tgt_own_hbm.1, f32[1,256,128]{2,1,0:T(8,128)} %proj_own_hbm.1), custom_call_target="tpu_custom_call" | custom-call | flops 67108864 | bytes 4194304 | tf_op jit(solution)/shard_map/pallas_call | solution.py:478
  2.8 2.7 %collective-permute-start.3 = (bf16[2,128,256]{2,1,0:T(8,128)(2,1)S(1)}, bf16[2,128,256]{2,1,0:T(8,128)(2,1)S(1)}, u32[]{:S(2)}, u32[]{:S(2)}) collective-permute-start(bf16[2,128,256]{2,1,0:T(8,128)(2,1)S(1)} %get-tuple-element.38), channel_id=1, source_target_pairs={{0,3},{1,8},{3,0},{2,11},{5,6},{4,13},{6,5},{7,14},{9,10},{8,1},{1... | collective-permute-start | bytes 393224 | tf_op jit(solution)/shard_map/ppermute | solution.py:453
  5.5 1.2 %shard_map.107 = (bf16[2,1056,256]{2,1,0:T(8,128)(2,1)S(1)}, f32[1,1,256]{2,1,0:T(1,128)S(1)}) custom-call(f32[256]{0:T(256)} %weight_hbm.1, bf16[2,4,256,256]{3,2,1,0:T(8,128)(2,1)} %bitcast.3, bf16[2,8,256,256]{3,2,1,0:T(8,128)(2,1)} %proj_hbm.3, f32[2,128,256]{2,1,0:T(8,128)S(1)} %get-tuple-element.29.chip_amp, f32[2,1,256]{2,1,0:T(1,128)S(1)} %get-tuple-element.31.energy), custom_call_target="tpu_custom_call" | custom-call | tf_op jit(solution)/shard_map/pallas_call | solution.py:502
  6.8 1.4 %collective-permute-start.2 = (bf16[2,1056,256]{2,1,0:T(8,128)(2,1)S(1)}, bf16[2,1056,256]{2,1,0:T(8,128)(2,1)S(1)}, u32[]{:S(2)}, u32[]{:S(2)}) collective-permute-start(bf16[2,1056,256]{2,1,0:T(8,128)(2,1)S(1)} %get-tuple-element.32.sent), channel_id=1, source_target_pairs={{0,1},{1,0},{2,3},{3,2},{4,5},{5,4},{6,7},{7,6},{8,9},{9,8},{10,11... | collective-permute-start | bytes 3244040 | tf_op jit(solution)/shard_map/ppermute | solution.py:435
  8.1 1.3 %shard_map.106 = (bf16[2,512,256]{2,1,0:T(8,128)(2,1)S(1)}, bf16[2,512,256]{2,1,0:T(8,128)(2,1)S(1)}, bf16[2,256,256]{2,1,0:T(8,128)(2,1)S(1)}, f32[3,2,1,256]{3,2,1,0:T(1,128)S(1)}) custom-call(s32[2,4]{1,0:T(2,128)} %bitcast.5, s32[2,4]{1,0:T(2,128)} %bitcast.6, bf16[2,4,256,256]{3,2,1,0:T(8,128)(2,1)} %bitcast.4, bf16[2,8,256,256]{3,2,1,0:T(8,128)(2,1)} %proj_hbm.3, ...), custom_call_target="tpu_custom_call" | custom-call | flops 34359738368 | bytes 65536 | tf_op jit(solution)/shard_map/pallas_call | solution.py:511
  9.4 1.1 %collective-permute-done.2.theirs = bf16[2,1056,256]{2,1,0:T(8,128)(2,1)S(1)} collective-permute-done((bf16[2,1056,256]{2,1,0:T(8,128)(2,1)S(1)}, bf16[2,1056,256]{2,1,0:T(8,128)(2,1)S(1)}, u32[]{:S(2)}, u32[]{:S(2)}) %collective-permute-start.2) | collective-permute-done | bytes 1081376 | tf_op jit(solution)/shard_map/ppermute | solution.py:435
  11.1 1.5 %collective-permute-start.4 = (bf16[128,256]{1,0:T(8,128)(2,1)S(1)}, bf16[128,256]{1,0:T(8,128)(2,1)S(1)}, u32[]{:S(2)}, u32[]{:S(2)}) collective-permute-start(bf16[128,256]{1,0:T(8,128)(2,1)S(1)} %get-tuple-element.42.own), channel_id=1, source_target_pairs={{0,9},{1,4},{3,10},{2,7},{5,12},{4,1},{6,15},{7,2},{9,0},{8,13},{1... | collective-permute-start | bytes 196616 | tf_op jit(solution)/shard_map/ppermute | solution.py:453
  12.7 1.2 %collective-permute-start.8 = (bf16[128,256]{1,0:T(8,128)(2,1)S(1)}, bf16[128,256]{1,0:T(8,128)(2,1)S(1)}, u32[]{:S(2)}, u32[]{:S(2)}) collective-permute-start(bf16[128,256]{1,0:T(8,128)(2,1)S(1)} %get-tuple-element.44.own), channel_id=1, source_target_pairs={{0,9},{1,4},{3,10},{2,7},{5,12},{4,1},{6,15},{7,2},{9,0},{8,13},{1... | collective-permute-start | bytes 196616 | tf_op jit(solution)/shard_map/ppermute | solution.py:453
  13.8 1.4 %collective-permute-start.7 = (f32[2,1,256]{2,1,0:T(1,128)S(1)}, f32[2,1,256]{2,1,0:T(1,128)S(1)}, u32[]{:S(2)}, u32[]{:S(2)}) collective-permute-start(f32[2,1,256]{2,1,0:T(1,128)S(1)} %get-tuple-element.43.energies), channel_id=1, source_target_pairs={{0,3},{1,8},{3,0},{2,11},{5,6},{4,13},{6,5},{7,14},{9,10},{8,1},{1... | collective-permute-start | bytes 6152 | tf_op jit(solution)/shard_map/ppermute | solution.py:453
  15.3 0.6 %collective-permute-done.4.other = bf16[128,256]{1,0:T(8,128)(2,1)S(1)} collective-permute-done((bf16[128,256]{1,0:T(8,128)(2,1)S(1)}, bf16[128,256]{1,0:T(8,128)(2,1)S(1)}, u32[]{:S(2)}, u32[]{:S(2)}) %collective-permute-start.4) | collective-permute-done | bytes 65568 | tf_op jit(solution)/shard_map/ppermute | solution.py:453
  15.9 1.2 %collective-permute-start.6 = (bf16[128,256]{1,0:T(8,128)(2,1)S(1)}, bf16[128,256]{1,0:T(8,128)(2,1)S(1)}, u32[]{:S(2)}, u32[]{:S(2)}) collective-permute-start(bf16[128,256]{1,0:T(8,128)(2,1)S(1)} %shard_map.110), channel_id=1, source_target_pairs={{0,4},{1,3},{3,7},{2,0},{5,1},{4,6},{6,2},{7,5},{9,13},{8,10},{10,... | collective-permute-start | bytes 196616 | tf_op jit(solution)/shard_map/ppermute | solution.py:453
  17.1 0.7 %collective-permute-start.5 = (bf16[128,256]{1,0:T(8,128)(2,1)S(1)}, bf16[128,256]{1,0:T(8,128)(2,1)S(1)}, u32[]{:S(2)}, u32[]{:S(2)}) collective-permute-start(bf16[128,256]{1,0:T(8,128)(2,1)S(1)} %shard_map.110), channel_id=1, source_target_pairs={{0,1},{1,0},{2,3},{3,2},{4,5},{5,4},{6,7},{7,6},{8,9},{9,8},{10,11... | collective-permute-start | bytes 196616 | tf_op jit(solution)/shard_map/ppermute | solution.py:435
  18.0 1.5 %collective-permute-start.10 = (bf16[128,256]{1,0:T(8,128)(2,1)S(1)}, bf16[128,256]{1,0:T(8,128)(2,1)S(1)}, u32[]{:S(2)}, u32[]{:S(2)}) collective-permute-start(bf16[128,256]{1,0:T(8,128)(2,1)S(1)} %shard_map.112), channel_id=1, source_target_pairs={{0,4},{1,3},{3,7},{2,0},{5,1},{4,6},{6,2},{7,5},{9,13},{8,10},{10,... | collective-permute-start | bytes 196616 | tf_op jit(solution)/shard_map/ppermute | solution.py:453
  19.5 0.7 %collective-permute-done.6.low_there = bf16[128,256]{1,0:T(8,128)(2,1)S(1)} collective-permute-done((bf16[128,256]{1,0:T(8,128)(2,1)S(1)}, bf16[128,256]{1,0:T(8,128)(2,1)S(1)}, u32[]{:S(2)}, u32[]{:S(2)}) %collective-permute-start.6) | collective-permute-done | bytes 65568 | tf_op jit(solution)/shard_map/ppermute | solution.py:453
  20.7 1.6 %collective-permute-done.10.high_there = bf16[128,256]{1,0:T(8,128)(2,1)S(1)} collective-permute-done((bf16[128,256]{1,0:T(8,128)(2,1)S(1)}, bf16[128,256]{1,0:T(8,128)(2,1)S(1)}, u32[]{:S(2)}, u32[]{:S(2)}) %collective-permute-start.10) | collective-permute-done | bytes 65568 | tf_op jit(solution)/shard_map/ppermute | solution.py:453
  22.3 0.8 %shard_map.113 = (bf16[128,256]{1,0:T(8,128)(2,1)S(1)}, bf16[128,256]{1,0:T(8,128)(2,1)S(1)}, f32[128,256]{1,0:T(8,128)S(1)}, f32[128,256]{1,0:T(8,128)S(1)}) custom-call(bf16[2,512,256]{2,1,0:T(8,128)(2,1)S(1)} %get-tuple-element.30.mine_chip, bf16[2,512,256]{2,1,0:T(8,128)(2,1)S(1)} %get-tuple-element.34.mine_far, ...), custom_call_target="tpu_custom_call" | custom-call | tf_op jit(solution)/shard_map/pallas_call | solution.py:432
  23.4 2.5 %collective-permute-start.11 = (bf16[128,256]{1,0:T(8,128)(2,1)S(1)}, bf16[128,256]{1,0:T(8,128)(2,1)S(1)}, u32[]{:S(2)}, u32[]{:S(2)}) collective-permute-start(bf16[128,256]{1,0:T(8,128)(2,1)S(1)} %get-tuple-element.45.own), channel_id=1, source_target_pairs={{0,9},{1,4},{3,10},{2,7},{5,12},{4,1},{6,15},{7,2},{9,0},{8,13},{1... | collective-permute-start | bytes 196616 | tf_op jit(solution)/shard_map/ppermute | solution.py:453
  25.9 2.0 %collective-permute-done.15.other = bf16[128,256]{1,0:T(8,128)(2,1)S(1)} collective-permute-done((bf16[128,256]{1,0:T(8,128)(2,1)S(1)}, bf16[128,256]{1,0:T(8,128)(2,1)S(1)}, u32[]{:S(2)}, u32[]{:S(2)}) %collective-permute-start.15) | collective-permute-done | bytes 65568 | tf_op jit(solution)/shard_map/ppermute | solution.py:453
  27.8 1.3 %collective-permute-start.16 = (bf16[128,256]{1,0:T(8,128)(2,1)S(1)}, bf16[128,256]{1,0:T(8,128)(2,1)S(1)}, u32[]{:S(2)}, u32[]{:S(2)}) collective-permute-start(bf16[128,256]{1,0:T(8,128)(2,1)S(1)} %shard_map.116.own), channel_id=1, source_target_pairs={{0,5},{1,2},{3,6},{2,1},{5,0},{4,7},{6,3},{7,4},{9,12},{8,11},{10,... | collective-permute-start | bytes 196616 | tf_op jit(solution)/shard_map/ppermute | solution.py:453
  29.3 1.2 %collective-permute-start.12 = (bf16[128,256]{1,0:T(8,128)(2,1)S(1)}, bf16[128,256]{1,0:T(8,128)(2,1)S(1)}, u32[]{:S(2)}, u32[]{:S(2)}) collective-permute-start(bf16[128,256]{1,0:T(8,128)(2,1)S(1)} %shard_map.114.own), channel_id=1, source_target_pairs={{0,5},{1,2},{3,6},{2,1},{5,0},{4,7},{6,3},{7,4},{9,12},{8,11},{10,... | collective-permute-start | bytes 196616 | tf_op jit(solution)/shard_map/ppermute | solution.py:453
  30.5 1.1 %collective-permute-done.16.other = bf16[128,256]{1,0:T(8,128)(2,1)S(1)} collective-permute-done((bf16[128,256]{1,0:T(8,128)(2,1)S(1)}, bf16[128,256]{1,0:T(8,128)(2,1)S(1)}, u32[]{:S(2)}, u32[]{:S(2)}) %collective-permute-start.16) | collective-permute-done | bytes 65568 | tf_op jit(solution)/shard_map/ppermute | solution.py:453
  32.2 0.8 %collective-permute-done.12.other = bf16[128,256]{1,0:T(8,128)(2,1)S(1)} collective-permute-done((bf16[128,256]{1,0:T(8,128)(2,1)S(1)}, bf16[128,256]{1,0:T(8,128)(2,1)S(1)}, u32[]{:S(2)}, u32[]{:S(2)}) %collective-permute-start.12) | collective-permute-done | bytes 65568 | tf_op jit(solution)/shard_map/ppermute | solution.py:453
  33.8 0.6 %collective-permute-done.13.high = bf16[128,256]{1,0:T(8,128)(2,1)S(1)} collective-permute-done((bf16[128,256]{1,0:T(8,128)(2,1)S(1)}, bf16[128,256]{1,0:T(8,128)(2,1)S(1)}, u32[]{:S(2)}, u32[]{:S(2)}) %collective-permute-start.13) | collective-permute-done | bytes 65568 | tf_op jit(solution)/shard_map/ppermute | solution.py:435
  34.4 1.0 %shard_map.119 = (f32[256,128]{1,0:T(8,128)}, f32[1,256,128]{2,1,0:T(8,128)}) custom-call(bf16[2,512,256]{2,1,0:T(8,128)(2,1)S(1)} %get-tuple-element.30.mine_chip, bf16[2,1056,256]{2,1,0:T(8,128)(2,1)S(1)} %collective-permute-done.2.theirs, bf16[128,256]{1,0:T(8,128)(2,1)S(1)} %collective-permute-done.13.high, f32[128,256]{1,0:T(8,128)S(1)} %get-tuple-element.52.my_part, ...), custom_call_target="tpu_custom_call" | custom-call | tf_op jit(solution)/shard_map/pallas_call | solution.py:586
  (30 shorter events, 4.1 us)
Async XLA Ops:
  0.6 1.7 %collective-permute-start = (f32[256,128]{1,0:T(8,128)}, f32[256,128]{1,0:T(8,128)S(1)}, u32[]{:S(2)}, u32[]{:S(2)}) collective-permute-start(f32[256,128]{1,0:T(8,128)} %tgt_own_hbm.1), channel_id=1, source_target_pairs={{0,1},{1,0},{2,3},{3,2},{4,5},{5,4},{6,7},{7,6},{8,9},{9,8},{10,11... | collective-permute-start | bytes 393224 | tf_op jit(solution)/shard_map/ppermute | solution.py:435
  1.1 1.6 %collective-permute-start.1 = (f32[1,256,128]{2,1,0:T(8,128)}, f32[1,256,128]{2,1,0:T(8,128)S(1)}, u32[]{:S(2)}, u32[]{:S(2)}) collective-permute-start(f32[1,256,128]{2,1,0:T(8,128)} %proj_own_hbm.1), channel_id=1, source_target_pairs={{0,1},{1,0},{2,3},{3,2},{4,5},{5,4},{6,7},{7,6},{8,9},{9,8},{10,11... | collective-permute-start | bytes 393224 | tf_op jit(solution)/shard_map/ppermute | solution.py:435
  2.8 7.9 %collective-permute-start.3 = (bf16[2,128,256]{2,1,0:T(8,128)(2,1)S(1)}, bf16[2,128,256]{2,1,0:T(8,128)(2,1)S(1)}, u32[]{:S(2)}, u32[]{:S(2)}) collective-permute-start(bf16[2,128,256]{2,1,0:T(8,128)(2,1)S(1)} %get-tuple-element.38), channel_id=1, source_target_pairs={{0,3},{1,8},{3,0},{2,11},{5,6},{4,13},{6,5},{7,14},{9,10},{8,1},{1... | collective-permute-start | bytes 393224 | tf_op jit(solution)/shard_map/ppermute | solution.py:453
  6.8 3.7 %collective-permute-start.2 = (bf16[2,1056,256]{2,1,0:T(8,128)(2,1)S(1)}, bf16[2,1056,256]{2,1,0:T(8,128)(2,1)S(1)}, u32[]{:S(2)}, u32[]{:S(2)}) collective-permute-start(bf16[2,1056,256]{2,1,0:T(8,128)(2,1)S(1)} %get-tuple-element.32.sent), channel_id=1, source_target_pairs={{0,1},{1,0},{2,3},{3,2},{4,5},{5,4},{6,7},{7,6},{8,9},{9,8},{10,11... | collective-permute-start | bytes 3244040 | tf_op jit(solution)/shard_map/ppermute | solution.py:435
  11.1 4.8 %collective-permute-start.4 = (bf16[128,256]{1,0:T(8,128)(2,1)S(1)}, bf16[128,256]{1,0:T(8,128)(2,1)S(1)}, u32[]{:S(2)}, u32[]{:S(2)}) collective-permute-start(bf16[128,256]{1,0:T(8,128)(2,1)S(1)} %get-tuple-element.42.own), channel_id=1, source_target_pairs={{0,9},{1,4},{3,10},{2,7},{5,12},{4,1},{6,15},{7,2},{9,0},{8,13},{1... | collective-permute-start | bytes 196616 | tf_op jit(solution)/shard_map/ppermute | solution.py:453
  12.7 5.3 %collective-permute-start.8 = (bf16[128,256]{1,0:T(8,128)(2,1)S(1)}, bf16[128,256]{1,0:T(8,128)(2,1)S(1)}, u32[]{:S(2)}, u32[]{:S(2)}) collective-permute-start(bf16[128,256]{1,0:T(8,128)(2,1)S(1)} %get-tuple-element.44.own), channel_id=1, source_target_pairs={{0,9},{1,4},{3,10},{2,7},{5,12},{4,1},{6,15},{7,2},{9,0},{8,13},{1... | collective-permute-start | bytes 196616 | tf_op jit(solution)/shard_map/ppermute | solution.py:453
  13.8 4.0 %collective-permute-start.7 = (f32[2,1,256]{2,1,0:T(1,128)S(1)}, f32[2,1,256]{2,1,0:T(1,128)S(1)}, u32[]{:S(2)}, u32[]{:S(2)}) collective-permute-start(f32[2,1,256]{2,1,0:T(1,128)S(1)} %get-tuple-element.43.energies), channel_id=1, source_target_pairs={{0,3},{1,8},{3,0},{2,11},{5,6},{4,13},{6,5},{7,14},{9,10},{8,1},{1... | collective-permute-start | bytes 6152 | tf_op jit(solution)/shard_map/ppermute | solution.py:453
  15.9 4.3 %collective-permute-start.6 = (bf16[128,256]{1,0:T(8,128)(2,1)S(1)}, bf16[128,256]{1,0:T(8,128)(2,1)S(1)}, u32[]{:S(2)}, u32[]{:S(2)}) collective-permute-start(bf16[128,256]{1,0:T(8,128)(2,1)S(1)} %shard_map.110), channel_id=1, source_target_pairs={{0,4},{1,3},{3,7},{2,0},{5,1},{4,6},{6,2},{7,5},{9,13},{8,10},{10,... | collective-permute-start | bytes 196616 | tf_op jit(solution)/shard_map/ppermute | solution.py:453
  17.1 3.1 %collective-permute-start.5 = (bf16[128,256]{1,0:T(8,128)(2,1)S(1)}, bf16[128,256]{1,0:T(8,128)(2,1)S(1)}, u32[]{:S(2)}, u32[]{:S(2)}) collective-permute-start(bf16[128,256]{1,0:T(8,128)(2,1)S(1)} %shard_map.110), channel_id=1, source_target_pairs={{0,1},{1,0},{2,3},{3,2},{4,5},{5,4},{6,7},{7,6},{8,9},{9,8},{10,11... | collective-permute-start | bytes 196616 | tf_op jit(solution)/shard_map/ppermute | solution.py:435
  18.0 4.3 %collective-permute-start.10 = (bf16[128,256]{1,0:T(8,128)(2,1)S(1)}, bf16[128,256]{1,0:T(8,128)(2,1)S(1)}, u32[]{:S(2)}, u32[]{:S(2)}) collective-permute-start(bf16[128,256]{1,0:T(8,128)(2,1)S(1)} %shard_map.112), channel_id=1, source_target_pairs={{0,4},{1,3},{3,7},{2,0},{5,1},{4,6},{6,2},{7,5},{9,13},{8,10},{10,... | collective-permute-start | bytes 196616 | tf_op jit(solution)/shard_map/ppermute | solution.py:453
  19.5 2.9 %collective-permute-start.9 = (bf16[128,256]{1,0:T(8,128)(2,1)S(1)}, bf16[128,256]{1,0:T(8,128)(2,1)S(1)}, u32[]{:S(2)}, u32[]{:S(2)}) collective-permute-start(bf16[128,256]{1,0:T(8,128)(2,1)S(1)} %shard_map.112), channel_id=1, source_target_pairs={{0,1},{1,0},{2,3},{3,2},{4,5},{5,4},{6,7},{7,6},{8,9},{9,8},{10,11... | collective-permute-start | bytes 196616 | tf_op jit(solution)/shard_map/ppermute | solution.py:435
  23.2 4.7 %collective-permute-start.15 = (bf16[128,256]{1,0:T(8,128)(2,1)S(1)}, bf16[128,256]{1,0:T(8,128)(2,1)S(1)}, u32[]{:S(2)}, u32[]{:S(2)}) collective-permute-start(bf16[128,256]{1,0:T(8,128)(2,1)S(1)} %get-tuple-element.47.own), channel_id=1, source_target_pairs={{0,9},{1,4},{3,10},{2,7},{5,12},{4,1},{6,15},{7,2},{9,0},{8,13},{1... | collective-permute-start | bytes 196616 | tf_op jit(solution)/shard_map/ppermute | solution.py:453
  23.4 5.9 %collective-permute-start.11 = (bf16[128,256]{1,0:T(8,128)(2,1)S(1)}, bf16[128,256]{1,0:T(8,128)(2,1)S(1)}, u32[]{:S(2)}, u32[]{:S(2)}) collective-permute-start(bf16[128,256]{1,0:T(8,128)(2,1)S(1)} %get-tuple-element.45.own), channel_id=1, source_target_pairs={{0,9},{1,4},{3,10},{2,7},{5,12},{4,1},{6,15},{7,2},{9,0},{8,13},{1... | collective-permute-start | bytes 196616 | tf_op jit(solution)/shard_map/ppermute | solution.py:453
  27.8 3.8 %collective-permute-start.16 = (bf16[128,256]{1,0:T(8,128)(2,1)S(1)}, bf16[128,256]{1,0:T(8,128)(2,1)S(1)}, u32[]{:S(2)}, u32[]{:S(2)}) collective-permute-start(bf16[128,256]{1,0:T(8,128)(2,1)S(1)} %shard_map.116.own), channel_id=1, source_target_pairs={{0,5},{1,2},{3,6},{2,1},{5,0},{4,7},{6,3},{7,4},{9,12},{8,11},{10,... | collective-permute-start | bytes 196616 | tf_op jit(solution)/shard_map/ppermute | solution.py:453
  29.3 3.8 %collective-permute-start.12 = (bf16[128,256]{1,0:T(8,128)(2,1)S(1)}, bf16[128,256]{1,0:T(8,128)(2,1)S(1)}, u32[]{:S(2)}, u32[]{:S(2)}) collective-permute-start(bf16[128,256]{1,0:T(8,128)(2,1)S(1)} %shard_map.114.own), channel_id=1, source_target_pairs={{0,5},{1,2},{3,6},{2,1},{5,0},{4,7},{6,3},{7,4},{9,12},{8,11},{10,... | collective-permute-start | bytes 196616 | tf_op jit(solution)/shard_map/ppermute | solution.py:453
  30.5 2.7 %collective-permute-start.14 = (bf16[2,256,256]{2,1,0:T(8,128)(2,1)S(1)}, bf16[2,256,256]{2,1,0:T(8,128)(2,1)S(1)}, u32[]{:S(2)}, u32[]{:S(2)}) collective-permute-start(bf16[2,256,256]{2,1,0:T(8,128)(2,1)S(1)} %get-tuple-element.46), channel_id=1, source_target_pairs={{0,1},{1,0},{2,3},{3,2},{4,5},{5,4},{6,7},{7,6},{8,9},{9,8},{10,11... | collective-permute-start | bytes 786440 | tf_op jit(solution)/shard_map/ppermute | solution.py:435
  31.6 1.6 %collective-permute-start.17 = (bf16[128,256]{1,0:T(8,128)(2,1)S(1)}, bf16[128,256]{1,0:T(8,128)(2,1)S(1)}, u32[]{:S(2)}, u32[]{:S(2)}) collective-permute-start(bf16[128,256]{1,0:T(8,128)(2,1)S(1)} %shard_map.117.low), channel_id=1, source_target_pairs={{0,1},{1,0},{2,3},{3,2},{4,5},{5,4},{6,7},{7,6},{8,9},{9,8},{10,11... | collective-permute-start | bytes 196616 | tf_op jit(solution)/shard_map/ppermute | solution.py:435
  31.7 1.5 %collective-permute-start.18 = (f32[128,256]{1,0:T(8,128)S(1)}, f32[128,256]{1,0:T(8,128)S(1)}, u32[]{:S(2)}, u32[]{:S(2)}) collective-permute-start(f32[128,256]{1,0:T(8,128)S(1)} %get-tuple-element.51), channel_id=1, source_target_pairs={{0,1},{1,0},{2,3},{3,2},{4,5},{5,4},{6,7},{7,6},{8,9},{9,8},{10,11... | collective-permute-start | bytes 393224 | tf_op jit(solution)/shard_map/ppermute | solution.py:435
  33.1 1.3 %collective-permute-start.13 = (bf16[128,256]{1,0:T(8,128)(2,1)S(1)}, bf16[128,256]{1,0:T(8,128)(2,1)S(1)}, u32[]{:S(2)}, u32[]{:S(2)}) collective-permute-start(bf16[128,256]{1,0:T(8,128)(2,1)S(1)} %shard_map.115.high), channel_id=1, source_target_pairs={{0,1},{1,0},{2,3},{3,2},{4,5},{5,4},{6,7},{7,6},{8,9},{9,8},{10,11... | collective-permute-start | bytes 196616 | tf_op jit(solution)/shard_map/ppermute | solution.py:435

commit v28 on v27

--- a/solution.py
+++ b/solution.py
@@ -524,7 +524,7 @@
         ],
         BEHIND,
     )(*in_hbm(flags, counts), *bases, chip_amp)
-    theirs, theirs_own = swapped([sent, send_own])
+    theirs = other_core(sent)
     bases = (mine_chip, mine_far, theirs)
     part, weights, energies = run(
         chip_kernel,
@@ -565,8 +565,8 @@
         weights,
     )
     fields = summed(halves, n_steps)
-    fields[0], half_send = lax.optimization_barrier((fields[0], half_send))
-    other_half = other_core(half_send)
+    fields[0], send_own, half_send = lax.optimization_barrier((fields[0], send_own, half_send))
+    theirs_own, other_half = swapped([send_own, half_send])
     low, high = swapped(fields)
     low, high = swapped(fields)
     my_part, other_new = run(

time: 35.5 us -> 35.5 us (level)
  transfers between devices with their start and end apart: 19 -> 19, of which waited for: 11 -> 12; matrix products, arithmetic and copies ran while one was open for 0% -> 0% of each run, Pallas kernels for 14% -> 14%
where the time goes in v28:
time: 35.5 us; the launch traced here: 35.4 us
  starting transfers between devices  18.3 us (52%)
  waiting for transfers between devices  8.97 us (25%)
  Pallas kernels  7.34 us (21%)
  between operations  0.76 us (2%)
    ppermute x10, starting transfers between devices, exchanged(): return lax.ppermute(block, DEVICES, pairs)  14.8 us
    ppermute x10, waiting for transfers between devices, exchanged(): return lax.ppermute(block, DEVICES, pairs)  6.9 us
    ppermute x9, starting transfers between devices, other_core(): return lax.ppermute(block, 'rep', [(0, 1), (1, 0)])  3.53 us
    pallas_call x6, Pallas kernels, run(): return call(kernel, out_shape, [VMEM] * len(blocks))(*blocks)  2.58 us
    ppermute x9, waiting for transfers between devices, other_core(): return lax.ppermute(block, 'rep', [(0, 1), (1, 0)])  2.06 us
    pallas_call x1, Pallas kernels, shards(): call(functools.partial(side_kernel, gate_levels, neighbours), [pair, pair...  1.26 us
    pallas_call x1, Pallas kernels, shards(): call(functools.partial(sent_kernel, neighbours), [in_vmem((2, 4 * rows +...  1.24 us
    pallas_call x1, Pallas kernels, shards(): call(load_kernel, [in_vmem((2, 1, rows), jnp.float32), in_vmem((2, two_co...  1.14 us
  transfers between devices with their start and end apart: 19, of which 12 were waited for; matrix products, arithmetic and copies ran while one was open for 0% of the time, Pallas kernels for 14%

profile of v28, /device:TPU:0, one launch (start us, length us, event | category | flops | bytes accessed | tf_op | source)
XLA Modules:
  0.0 35.4 jit_solution(4388899740886772748)
XLA Ops:
  0.6 0.5 %collective-permute-start = (f32[256,128]{1,0:T(8,128)}, f32[256,128]{1,0:T(8,128)S(1)}, u32[]{:S(2)}, u32[]{:S(2)}) collective-permute-start(f32[256,128]{1,0:T(8,128)} %tgt_own_hbm.1), channel_id=1, source_target_pairs={{0,1},{1,0},{2,3},{3,2},{4,5},{5,4},{6,7},{7,6},{8,9},{9,8},{10,11... | collective-permute-start | bytes 393224 | tf_op jit(solution)/shard_map/ppermute | solution.py:435
  1.2 1.1 %shard_map.104 = (f32[2,1,256]{2,1,0:T(1,128)S(1)}, f32[2,128,256]{2,1,0:T(8,128)S(1)}) custom-call(f32[256]{0:T(256)} %tgt_energy_hbm.1, f32[1,256]{1,0:T(1,128)} %proj_energy_hbm.1, f32[256,128]{1,0:T(8,128)} %tgt_own_hbm.1, f32[1,256,128]{2,1,0:T(8,128)} %proj_own_hbm.1), custom_call_target="tpu_custom_call" | custom-call | flops 67108864 | bytes 4194304 | tf_op jit(solution)/shard_map/pallas_call | solution.py:478
  2.8 2.7 %collective-permute-start.3 = (bf16[2,128,256]{2,1,0:T(8,128)(2,1)S(1)}, bf16[2,128,256]{2,1,0:T(8,128)(2,1)S(1)}, u32[]{:S(2)}, u32[]{:S(2)}) collective-permute-start(bf16[2,128,256]{2,1,0:T(8,128)(2,1)S(1)} %get-tuple-element.39), channel_id=1, source_target_pairs={{0,3},{1,8},{3,0},{2,11},{5,6},{4,13},{6,5},{7,14},{9,10},{8,1},{1... | collective-permute-start | bytes 393224 | tf_op jit(solution)/shard_map/ppermute | solution.py:453
  5.5 1.2 %shard_map.107 = (bf16[2,1056,256]{2,1,0:T(8,128)(2,1)S(1)}, f32[1,1,256]{2,1,0:T(1,128)S(1)}) custom-call(f32[256]{0:T(256)} %weight_hbm.1, bf16[2,4,256,256]{3,2,1,0:T(8,128)(2,1)} %bitcast.3, bf16[2,8,256,256]{3,2,1,0:T(8,128)(2,1)} %proj_hbm.3, f32[2,128,256]{2,1,0:T(8,128)S(1)} %get-tuple-element.30.chip_amp, f32[2,1,256]{2,1,0:T(1,128)S(1)} %get-tuple-element.32.energy), custom_call_target="tpu_custom_call" | custom-call | tf_op jit(solution)/shard_map/pallas_call | solution.py:502
  6.8 1.4 %collective-permute-start.2 = (bf16[2,1056,256]{2,1,0:T(8,128)(2,1)S(1)}, bf16[2,1056,256]{2,1,0:T(8,128)(2,1)S(1)}, u32[]{:S(2)}, u32[]{:S(2)}) collective-permute-start(bf16[2,1056,256]{2,1,0:T(8,128)(2,1)S(1)} %get-tuple-element.33.sent), channel_id=1, source_target_pairs={{0,1},{1,0},{2,3},{3,2},{4,5},{5,4},{6,7},{7,6},{8,9},{9,8},{10,11... | collective-permute-start | bytes 3244040 | tf_op jit(solution)/shard_map/ppermute | solution.py:435
  8.1 1.3 %shard_map.106 = (bf16[2,512,256]{2,1,0:T(8,128)(2,1)S(1)}, bf16[2,512,256]{2,1,0:T(8,128)(2,1)S(1)}, bf16[2,256,256]{2,1,0:T(8,128)(2,1)S(1)}, f32[3,2,1,256]{3,2,1,0:T(1,128)S(1)}) custom-call(s32[2,4]{1,0:T(2,128)} %bitcast.5, s32[2,4]{1,0:T(2,128)} %bitcast.6, bf16[2,4,256,256]{3,2,1,0:T(8,128)(2,1)} %bitcast.4, bf16[2,8,256,256]{3,2,1,0:T(8,128)(2,1)} %proj_hbm.3, ...), custom_call_target="tpu_custom_call" | custom-call | flops 34359738368 | bytes 65536 | tf_op jit(solution)/shard_map/pallas_call | solution.py:511
  9.4 1.1 %collective-permute-done.2.theirs = bf16[2,1056,256]{2,1,0:T(8,128)(2,1)S(1)} collective-permute-done((bf16[2,1056,256]{2,1,0:T(8,128)(2,1)S(1)}, bf16[2,1056,256]{2,1,0:T(8,128)(2,1)S(1)}, u32[]{:S(2)}, u32[]{:S(2)}) %collective-permute-start.2) | collective-permute-done | bytes 1081376 | tf_op jit(solution)/shard_map/ppermute | solution.py:435
  11.1 1.5 %collective-permute-start.4 = (bf16[128,256]{1,0:T(8,128)(2,1)S(1)}, bf16[128,256]{1,0:T(8,128)(2,1)S(1)}, u32[]{:S(2)}, u32[]{:S(2)}) collective-permute-start(bf16[128,256]{1,0:T(8,128)(2,1)S(1)} %get-tuple-element.43.own), channel_id=1, source_target_pairs={{0,9},{1,4},{3,10},{2,7},{5,12},{4,1},{6,15},{7,2},{9,0},{8,13},{1... | collective-permute-start | bytes 196616 | tf_op jit(solution)/shard_map/ppermute | solution.py:453
  12.7 1.2 %collective-permute-start.8 = (bf16[128,256]{1,0:T(8,128)(2,1)S(1)}, bf16[128,256]{1,0:T(8,128)(2,1)S(1)}, u32[]{:S(2)}, u32[]{:S(2)}) collective-permute-start(bf16[128,256]{1,0:T(8,128)(2,1)S(1)} %get-tuple-element.45.own), channel_id=1, source_target_pairs={{0,9},{1,4},{3,10},{2,7},{5,12},{4,1},{6,15},{7,2},{9,0},{8,13},{1... | collective-permute-start | bytes 196616 | tf_op jit(solution)/shard_map/ppermute | solution.py:453
  13.8 1.4 %collective-permute-start.7 = (f32[2,1,256]{2,1,0:T(1,128)S(1)}, f32[2,1,256]{2,1,0:T(1,128)S(1)}, u32[]{:S(2)}, u32[]{:S(2)}) collective-permute-start(f32[2,1,256]{2,1,0:T(1,128)S(1)} %get-tuple-element.44.energies), channel_id=1, source_target_pairs={{0,3},{1,8},{3,0},{2,11},{5,6},{4,13},{6,5},{7,14},{9,10},{8,1},{1... | collective-permute-start | bytes 6152 | tf_op jit(solution)/shard_map/ppermute | solution.py:453
  15.3 0.6 %collective-permute-done.4.other = bf16[128,256]{1,0:T(8,128)(2,1)S(1)} collective-permute-done((bf16[128,256]{1,0:T(8,128)(2,1)S(1)}, bf16[128,256]{1,0:T(8,128)(2,1)S(1)}, u32[]{:S(2)}, u32[]{:S(2)}) %collective-permute-start.4) | collective-permute-done | bytes 65568 | tf_op jit(solution)/shard_map/ppermute | solution.py:453
  15.9 1.2 %collective-permute-start.6 = (bf16[128,256]{1,0:T(8,128)(2,1)S(1)}, bf16[128,256]{1,0:T(8,128)(2,1)S(1)}, u32[]{:S(2)}, u32[]{:S(2)}) collective-permute-start(bf16[128,256]{1,0:T(8,128)(2,1)S(1)} %shard_map.110), channel_id=1, source_target_pairs={{0,4},{1,3},{3,7},{2,0},{5,1},{4,6},{6,2},{7,5},{9,13},{8,10},{10,... | collective-permute-start | bytes 196616 | tf_op jit(solution)/shard_map/ppermute | solution.py:453
  17.1 0.7 %collective-permute-start.5 = (bf16[128,256]{1,0:T(8,128)(2,1)S(1)}, bf16[128,256]{1,0:T(8,128)(2,1)S(1)}, u32[]{:S(2)}, u32[]{:S(2)}) collective-permute-start(bf16[128,256]{1,0:T(8,128)(2,1)S(1)} %shard_map.110), channel_id=1, source_target_pairs={{0,1},{1,0},{2,3},{3,2},{4,5},{5,4},{6,7},{7,6},{8,9},{9,8},{10,11... | collective-permute-start | bytes 196616 | tf_op jit(solution)/shard_map/ppermute | solution.py:435
  18.0 1.5 %collective-permute-start.10 = (bf16[128,256]{1,0:T(8,128)(2,1)S(1)}, bf16[128,256]{1,0:T(8,128)(2,1)S(1)}, u32[]{:S(2)}, u32[]{:S(2)}) collective-permute-start(bf16[128,256]{1,0:T(8,128)(2,1)S(1)} %shard_map.112), channel_id=1, source_target_pairs={{0,4},{1,3},{3,7},{2,0},{5,1},{4,6},{6,2},{7,5},{9,13},{8,10},{10,... | collective-permute-start | bytes 196616 | tf_op jit(solution)/shard_map/ppermute | solution.py:453
  19.5 0.7 %collective-permute-done.6.low_there = bf16[128,256]{1,0:T(8,128)(2,1)S(1)} collective-permute-done((bf16[128,256]{1,0:T(8,128)(2,1)S(1)}, bf16[128,256]{1,0:T(8,128)(2,1)S(1)}, u32[]{:S(2)}, u32[]{:S(2)}) %collective-permute-start.6) | collective-permute-done | bytes 65568 | tf_op jit(solution)/shard_map/ppermute | solution.py:453
  20.7 1.6 %collective-permute-done.10.high_there = bf16[128,256]{1,0:T(8,128)(2,1)S(1)} collective-permute-done((bf16[128,256]{1,0:T(8,128)(2,1)S(1)}, bf16[128,256]{1,0:T(8,128)(2,1)S(1)}, u32[]{:S(2)}, u32[]{:S(2)}) %collective-permute-start.10) | collective-permute-done | bytes 65568 | tf_op jit(solution)/shard_map/ppermute | solution.py:453
  22.3 0.8 %shard_map.113 = (bf16[128,256]{1,0:T(8,128)(2,1)S(1)}, bf16[128,256]{1,0:T(8,128)(2,1)S(1)}, f32[128,256]{1,0:T(8,128)S(1)}, f32[128,256]{1,0:T(8,128)S(1)}) custom-call(bf16[2,512,256]{2,1,0:T(8,128)(2,1)S(1)} %get-tuple-element.31.mine_chip, bf16[2,512,256]{2,1,0:T(8,128)(2,1)S(1)} %get-tuple-element.35.mine_far, ...), custom_call_target="tpu_custom_call" | custom-call | tf_op jit(solution)/shard_map/pallas_call | solution.py:432
  23.4 2.5 %collective-permute-start.11 = (bf16[128,256]{1,0:T(8,128)(2,1)S(1)}, bf16[128,256]{1,0:T(8,128)(2,1)S(1)}, u32[]{:S(2)}, u32[]{:S(2)}) collective-permute-start(bf16[128,256]{1,0:T(8,128)(2,1)S(1)} %get-tuple-element.46.own), channel_id=1, source_target_pairs={{0,9},{1,4},{3,10},{2,7},{5,12},{4,1},{6,15},{7,2},{9,0},{8,13},{1... | collective-permute-start | bytes 196616 | tf_op jit(solution)/shard_map/ppermute | solution.py:453
  25.9 2.0 %collective-permute-done.14.other = bf16[128,256]{1,0:T(8,128)(2,1)S(1)} collective-permute-done((bf16[128,256]{1,0:T(8,128)(2,1)S(1)}, bf16[128,256]{1,0:T(8,128)(2,1)S(1)}, u32[]{:S(2)}, u32[]{:S(2)}) %collective-permute-start.14) | collective-permute-done | bytes 65568 | tf_op jit(solution)/shard_map/ppermute | solution.py:453
  27.8 1.3 %collective-permute-start.15 = (bf16[128,256]{1,0:T(8,128)(2,1)S(1)}, bf16[128,256]{1,0:T(8,128)(2,1)S(1)}, u32[]{:S(2)}, u32[]{:S(2)}) collective-permute-start(bf16[128,256]{1,0:T(8,128)(2,1)S(1)} %shard_map.116.own), channel_id=1, source_target_pairs={{0,5},{1,2},{3,6},{2,1},{5,0},{4,7},{6,3},{7,4},{9,12},{8,11},{10,... | collective-permute-start | bytes 196616 | tf_op jit(solution)/shard_map/ppermute | solution.py:453
  29.3 1.2 %collective-permute-start.12 = (bf16[128,256]{1,0:T(8,128)(2,1)S(1)}, bf16[128,256]{1,0:T(8,128)(2,1)S(1)}, u32[]{:S(2)}, u32[]{:S(2)}) collective-permute-start(bf16[128,256]{1,0:T(8,128)(2,1)S(1)} %shard_map.114.own), channel_id=1, source_target_pairs={{0,5},{1,2},{3,6},{2,1},{5,0},{4,7},{6,3},{7,4},{9,12},{8,11},{10,... | collective-permute-start | bytes 196616 | tf_op jit(solution)/shard_map/ppermute | solution.py:453
  30.5 1.1 %collective-permute-done.15.other = bf16[128,256]{1,0:T(8,128)(2,1)S(1)} collective-permute-done((bf16[128,256]{1,0:T(8,128)(2,1)S(1)}, bf16[128,256]{1,0:T(8,128)(2,1)S(1)}, u32[]{:S(2)}, u32[]{:S(2)}) %collective-permute-start.15) | collective-permute-done | bytes 65568 | tf_op jit(solution)/shard_map/ppermute | solution.py:453
  32.3 0.7 %collective-permute-done.12.other = bf16[128,256]{1,0:T(8,128)(2,1)S(1)} collective-permute-done((bf16[128,256]{1,0:T(8,128)(2,1)S(1)}, bf16[128,256]{1,0:T(8,128)(2,1)S(1)}, u32[]{:S(2)}, u32[]{:S(2)}) %collective-permute-start.12) | collective-permute-done | bytes 65568 | tf_op jit(solution)/shard_map/ppermute | solution.py:453
  34.4 1.0 %shard_map.119 = (f32[256,128]{1,0:T(8,128)}, f32[1,256,128]{2,1,0:T(8,128)}) custom-call(bf16[2,512,256]{2,1,0:T(8,128)(2,1)S(1)} %get-tuple-element.31.mine_chip, bf16[2,1056,256]{2,1,0:T(8,128)(2,1)S(1)} %collective-permute-done.2.theirs, bf16[128,256]{1,0:T(8,128)(2,1)S(1)} %collective-permute-done.13.high, f32[128,256]{1,0:T(8,128)S(1)} %get-tuple-element.54.my_part, ...), custom_call_target="tpu_custom_call" | custom-call | tf_op jit(solution)/shard_map/pallas_call | solution.py:586
  (30 shorter events, 4.3 us)
Async XLA Ops:
  0.6 1.7 %collective-permute-start = (f32[256,128]{1,0:T(8,128)}, f32[256,128]{1,0:T(8,128)S(1)}, u32[]{:S(2)}, u32[]{:S(2)}) collective-permute-start(f32[256,128]{1,0:T(8,128)} %tgt_own_hbm.1), channel_id=1, source_target_pairs={{0,1},{1,0},{2,3},{3,2},{4,5},{5,4},{6,7},{7,6},{8,9},{9,8},{10,11... | collective-permute-start | bytes 393224 | tf_op jit(solution)/shard_map/ppermute | solution.py:435
  1.1 1.6 %collective-permute-start.1 = (f32[1,256,128]{2,1,0:T(8,128)}, f32[1,256,128]{2,1,0:T(8,128)S(1)}, u32[]{:S(2)}, u32[]{:S(2)}) collective-permute-start(f32[1,256,128]{2,1,0:T(8,128)} %proj_own_hbm.1), channel_id=1, source_target_pairs={{0,1},{1,0},{2,3},{3,2},{4,5},{5,4},{6,7},{7,6},{8,9},{9,8},{10,11... | collective-permute-start | bytes 393224 | tf_op jit(solution)/shard_map/ppermute | solution.py:435
  2.8 7.9 %collective-permute-start.3 = (bf16[2,128,256]{2,1,0:T(8,128)(2,1)S(1)}, bf16[2,128,256]{2,1,0:T(8,128)(2,1)S(1)}, u32[]{:S(2)}, u32[]{:S(2)}) collective-permute-start(bf16[2,128,256]{2,1,0:T(8,128)(2,1)S(1)} %get-tuple-element.39), channel_id=1, source_target_pairs={{0,3},{1,8},{3,0},{2,11},{5,6},{4,13},{6,5},{7,14},{9,10},{8,1},{1... | collective-permute-start | bytes 393224 | tf_op jit(solution)/shard_map/ppermute | solution.py:453
  6.8 3.7 %collective-permute-start.2 = (bf16[2,1056,256]{2,1,0:T(8,128)(2,1)S(1)}, bf16[2,1056,256]{2,1,0:T(8,128)(2,1)S(1)}, u32[]{:S(2)}, u32[]{:S(2)}) collective-permute-start(bf16[2,1056,256]{2,1,0:T(8,128)(2,1)S(1)} %get-tuple-element.33.sent), channel_id=1, source_target_pairs={{0,1},{1,0},{2,3},{3,2},{4,5},{5,4},{6,7},{7,6},{8,9},{9,8},{10,11... | collective-permute-start | bytes 3244040 | tf_op jit(solution)/shard_map/ppermute | solution.py:435
  11.1 4.8 %collective-permute-start.4 = (bf16[128,256]{1,0:T(8,128)(2,1)S(1)}, bf16[128,256]{1,0:T(8,128)(2,1)S(1)}, u32[]{:S(2)}, u32[]{:S(2)}) collective-permute-start(bf16[128,256]{1,0:T(8,128)(2,1)S(1)} %get-tuple-element.43.own), channel_id=1, source_target_pairs={{0,9},{1,4},{3,10},{2,7},{5,12},{4,1},{6,15},{7,2},{9,0},{8,13},{1... | collective-permute-start | bytes 196616 | tf_op jit(solution)/shard_map/ppermute | solution.py:453
  12.7 5.3 %collective-permute-start.8 = (bf16[128,256]{1,0:T(8,128)(2,1)S(1)}, bf16[128,256]{1,0:T(8,128)(2,1)S(1)}, u32[]{:S(2)}, u32[]{:S(2)}) collective-permute-start(bf16[128,256]{1,0:T(8,128)(2,1)S(1)} %get-tuple-element.45.own), channel_id=1, source_target_pairs={{0,9},{1,4},{3,10},{2,7},{5,12},{4,1},{6,15},{7,2},{9,0},{8,13},{1... | collective-permute-start | bytes 196616 | tf_op jit(solution)/shard_map/ppermute | solution.py:453
  13.8 4.0 %collective-permute-start.7 = (f32[2,1,256]{2,1,0:T(1,128)S(1)}, f32[2,1,256]{2,1,0:T(1,128)S(1)}, u32[]{:S(2)}, u32[]{:S(2)}) collective-permute-start(f32[2,1,256]{2,1,0:T(1,128)S(1)} %get-tuple-element.44.energies), channel_id=1, source_target_pairs={{0,3},{1,8},{3,0},{2,11},{5,6},{4,13},{6,5},{7,14},{9,10},{8,1},{1... | collective-permute-start | bytes 6152 | tf_op jit(solution)/shard_map/ppermute | solution.py:453
  15.9 4.3 %collective-permute-start.6 = (bf16[128,256]{1,0:T(8,128)(2,1)S(1)}, bf16[128,256]{1,0:T(8,128)(2,1)S(1)}, u32[]{:S(2)}, u32[]{:S(2)}) collective-permute-start(bf16[128,256]{1,0:T(8,128)(2,1)S(1)} %shard_map.110), channel_id=1, source_target_pairs={{0,4},{1,3},{3,7},{2,0},{5,1},{4,6},{6,2},{7,5},{9,13},{8,10},{10,... | collective-permute-start | bytes 196616 | tf_op jit(solution)/shard_map/ppermute | solution.py:453
  17.1 3.1 %collective-permute-start.5 = (bf16[128,256]{1,0:T(8,128)(2,1)S(1)}, bf16[128,256]{1,0:T(8,128)(2,1)S(1)}, u32[]{:S(2)}, u32[]{:S(2)}) collective-permute-start(bf16[128,256]{1,0:T(8,128)(2,1)S(1)} %shard_map.110), channel_id=1, source_target_pairs={{0,1},{1,0},{2,3},{3,2},{4,5},{5,4},{6,7},{7,6},{8,9},{9,8},{10,11... | collective-permute-start | bytes 196616 | tf_op jit(solution)/shard_map/ppermute | solution.py:435
  18.0 4.3 %collective-permute-start.10 = (bf16[128,256]{1,0:T(8,128)(2,1)S(1)}, bf16[128,256]{1,0:T(8,128)(2,1)S(1)}, u32[]{:S(2)}, u32[]{:S(2)}) collective-permute-start(bf16[128,256]{1,0:T(8,128)(2,1)S(1)} %shard_map.112), channel_id=1, source_target_pairs={{0,4},{1,3},{3,7},{2,0},{5,1},{4,6},{6,2},{7,5},{9,13},{8,10},{10,... | collective-permute-start | bytes 196616 | tf_op jit(solution)/shard_map/ppermute | solution.py:453
  19.5 2.9 %collective-permute-start.9 = (bf16[128,256]{1,0:T(8,128)(2,1)S(1)}, bf16[128,256]{1,0:T(8,128)(2,1)S(1)}, u32[]{:S(2)}, u32[]{:S(2)}) collective-permute-start(bf16[128,256]{1,0:T(8,128)(2,1)S(1)} %shard_map.112), channel_id=1, source_target_pairs={{0,1},{1,0},{2,3},{3,2},{4,5},{5,4},{6,7},{7,6},{8,9},{9,8},{10,11... | collective-permute-start | bytes 196616 | tf_op jit(solution)/shard_map/ppermute | solution.py:435
  23.2 4.7 %collective-permute-start.14 = (bf16[128,256]{1,0:T(8,128)(2,1)S(1)}, bf16[128,256]{1,0:T(8,128)(2,1)S(1)}, u32[]{:S(2)}, u32[]{:S(2)}) collective-permute-start(bf16[128,256]{1,0:T(8,128)(2,1)S(1)} %get-tuple-element.47.own), channel_id=1, source_target_pairs={{0,9},{1,4},{3,10},{2,7},{5,12},{4,1},{6,15},{7,2},{9,0},{8,13},{1... | collective-permute-start | bytes 196616 | tf_op jit(solution)/shard_map/ppermute | solution.py:453
  23.4 5.9 %collective-permute-start.11 = (bf16[128,256]{1,0:T(8,128)(2,1)S(1)}, bf16[128,256]{1,0:T(8,128)(2,1)S(1)}, u32[]{:S(2)}, u32[]{:S(2)}) collective-permute-start(bf16[128,256]{1,0:T(8,128)(2,1)S(1)} %get-tuple-element.46.own), channel_id=1, source_target_pairs={{0,9},{1,4},{3,10},{2,7},{5,12},{4,1},{6,15},{7,2},{9,0},{8,13},{1... | collective-permute-start | bytes 196616 | tf_op jit(solution)/shard_map/ppermute | solution.py:453
  27.8 3.8 %collective-permute-start.15 = (bf16[128,256]{1,0:T(8,128)(2,1)S(1)}, bf16[128,256]{1,0:T(8,128)(2,1)S(1)}, u32[]{:S(2)}, u32[]{:S(2)}) collective-permute-start(bf16[128,256]{1,0:T(8,128)(2,1)S(1)} %shard_map.116.own), channel_id=1, source_target_pairs={{0,5},{1,2},{3,6},{2,1},{5,0},{4,7},{6,3},{7,4},{9,12},{8,11},{10,... | collective-permute-start | bytes 196616 | tf_op jit(solution)/shard_map/ppermute | solution.py:453
  29.3 3.8 %collective-permute-start.12 = (bf16[128,256]{1,0:T(8,128)(2,1)S(1)}, bf16[128,256]{1,0:T(8,128)(2,1)S(1)}, u32[]{:S(2)}, u32[]{:S(2)}) collective-permute-start(bf16[128,256]{1,0:T(8,128)(2,1)S(1)} %shard_map.114.own), channel_id=1, source_target_pairs={{0,5},{1,2},{3,6},{2,1},{5,0},{4,7},{6,3},{7,4},{9,12},{8,11},{10,... | collective-permute-start | bytes 196616 | tf_op jit(solution)/shard_map/ppermute | solution.py:453
  31.6 1.6 %collective-permute-start.17 = (bf16[128,256]{1,0:T(8,128)(2,1)S(1)}, bf16[128,256]{1,0:T(8,128)(2,1)S(1)}, u32[]{:S(2)}, u32[]{:S(2)}) collective-permute-start(bf16[128,256]{1,0:T(8,128)(2,1)S(1)} %shard_map.117.low), channel_id=1, source_target_pairs={{0,1},{1,0},{2,3},{3,2},{4,5},{5,4},{6,7},{7,6},{8,9},{9,8},{10,11... | collective-permute-start | bytes 196616 | tf_op jit(solution)/shard_map/ppermute | solution.py:435
  31.7 1.5 %collective-permute-start.18 = (f32[128,256]{1,0:T(8,128)S(1)}, f32[128,256]{1,0:T(8,128)S(1)}, u32[]{:S(2)}, u32[]{:S(2)}) collective-permute-start(f32[128,256]{1,0:T(8,128)S(1)} %get-tuple-element.53), channel_id=1, source_target_pairs={{0,1},{1,0},{2,3},{3,2},{4,5},{5,4},{6,7},{7,6},{8,9},{9,8},{10,11... | collective-permute-start | bytes 393224 | tf_op jit(solution)/shard_map/ppermute | solution.py:435
  32.2 1.5 %collective-permute-start.16 = (bf16[2,256,256]{2,1,0:T(8,128)(2,1)S(1)}, bf16[2,256,256]{2,1,0:T(8,128)(2,1)S(1)}, u32[]{:S(2)}, u32[]{:S(2)}) collective-permute-start(bf16[2,256,256]{2,1,0:T(8,128)(2,1)S(1)} %get-tuple-element.50), channel_id=1, source_target_pairs={{0,1},{1,0},{2,3},{3,2},{4,5},{5,4},{6,7},{7,6},{8,9},{9,8},{10,11... | collective-permute-start | bytes 786440 | tf_op jit(solution)/shard_map/ppermute | solution.py:435
  33.1 1.3 %collective-permute-start.13 = (bf16[128,256]{1,0:T(8,128)(2,1)S(1)}, bf16[128,256]{1,0:T(8,128)(2,1)S(1)}, u32[]{:S(2)}, u32[]{:S(2)}) collective-permute-start(bf16[128,256]{1,0:T(8,128)(2,1)S(1)} %shard_map.115.high), channel_id=1, source_target_pairs={{0,1},{1,0},{2,3},{3,2},{4,5},{5,4},{6,7},{7,6},{8,9},{9,8},{10,11... | collective-permute-start | bytes 196616 | tf_op jit(solution)/shard_map/ppermute | solution.py:435

commit v29 on v27

--- a/solution.py
+++ b/solution.py
@@ -438,16 +438,16 @@
     tgt_flips = [n_prj << bit for bit in range(n_tgt.bit_length() - 1)]
     prj_flips = [1 << bit for bit in range(n_prj.bit_length() - 1)]
     far_first = tgt_flips[::-1]
-    flips = (prj_flips + far_first, far_first + prj_flips)
+    flips = [(prj_flips + order, far_first + prj_flips) for order in (far_first, tgt_flips)]
     neighbours = (prj_flips[0], far_first[0] // n_prj)
     gate_levels = (len(prj_flips) - 1, len(tgt_flips) - 1)
     n_steps = len(tgt_flips) + len(prj_flips)
 
-    def exchanged(step, block, crossed=0):
+    def exchanged(step, block, order=0, crossed=0):
         pairs = []
         for place in range(n_tgt * n_prj):
             for kind in range(2):
-                there = place ^ flips[kind][step]
+                there = place ^ flips[order][kind][step]
                 to_core = kind ^ crossed ^ parity(there)
                 pairs.append((place * n_core + (kind ^ parity(place)), there * n_core + to_core))
         return lax.ppermute(block, DEVICES, pairs)
@@ -456,11 +456,11 @@
     sums = in_vmem((two_cols, points), jnp.bfloat16)
     segment = in_vmem((two_cols, rows), jnp.float32)
 
-    def summed(halves, until, *ahead):
+    def summed(halves, until, orders, *ahead):
         totals = []
         for half, block in enumerate(halves):
             for step in range(1, until):
-                other = exchanged(step, block)
+                other = exchanged(step, block, orders[half])
                 kernel = functools.partial(add_kernel, step, half)
                 blocks = [gate, block, other] + (list(ahead) if half and step == 1 else [])
                 cost = EVEN if half else None
@@ -543,7 +543,7 @@
     (low, high), energies = lax.optimization_barrier((halves, energies))
     neighbour_energies = exchanged(0, energies)
     halves = low, high
-    parts = summed(halves, n_steps - 1, neighbour_energies)
+    parts = summed(halves, n_steps - 1, (0, 0), neighbour_energies)
     low, high = [(other_core(block), exchanged(n_steps - 1, block, crossed=1)) for block in parts]
     (states,) = run(
         low_kernel,
@@ -564,7 +564,7 @@
         gate,
         weights,
     )
-    fields = summed(halves, n_steps)
+    fields = summed(halves, n_steps, (0, 1))
     fields[0], half_send = lax.optimization_barrier((fields[0], half_send))
     other_half = other_core(half_send)
     low, high = swapped(fields)

time: 35.5 us -> 36.4 us (1.025)
  waiting for transfers between devices: 9.02 us -> 9.77 us
    ppermute x10, waiting for transfers between devices: 6.98 us -> 7.63 us  [exchanged(): return lax.ppermute(block, DEVICES, pairs)]
  transfers between devices with their start and end apart: 19 -> 19, of which waited for: 11 -> 10; matrix products, arithmetic and copies ran while one was open for 0% -> 0% of each run, Pallas kernels for 14% -> 14%
where the time goes in v29:
time: 36.4 us; the launch traced here: 36.2 us
  starting transfers between devices  18.3 us (50%)
  waiting for transfers between devices  9.77 us (27%)
  Pallas kernels  7.35 us (20%)
  between operations  0.79 us (2%)
    ppermute x10, starting transfers between devices, exchanged(): return lax.ppermute(block, DEVICES, pairs)  14.9 us
    ppermute x10, waiting for transfers between devices, exchanged(): return lax.ppermute(block, DEVICES, pairs)  7.63 us
    ppermute x9, starting transfers between devices, other_core(): return lax.ppermute(block, 'rep', [(0, 1), (1, 0)])  3.34 us
    pallas_call x6, Pallas kernels, run(): return call(kernel, out_shape, [VMEM] * len(blocks))(*blocks)  2.59 us
    ppermute x9, waiting for transfers between devices, other_core(): return lax.ppermute(block, 'rep', [(0, 1), (1, 0)])  2.13 us
    pallas_call x1, Pallas kernels, shards(): call(functools.partial(side_kernel, gate_levels, neighbours), [pair, pair...  1.26 us
    pallas_call x1, Pallas kernels, shards(): call(functools.partial(sent_kernel, neighbours), [in_vmem((2, 4 * rows +...  1.24 us
    pallas_call x1, Pallas kernels, shards(): call(load_kernel, [in_vmem((2, 1, rows), jnp.float32), in_vmem((2, two_co...  1.14 us
  transfers between devices with their start and end apart: 19, of which 10 were waited for; matrix products, arithmetic and copies ran while one was open for 0% of the time, Pallas kernels for 14%

profile of v29, /device:TPU:0, one launch (start us, length us, event | category | flops | bytes accessed | tf_op | source)
XLA Modules:
  0.0 36.2 jit_solution(5589462823218134438)
XLA Ops:
  1.2 1.1 %shard_map.104 = (f32[2,1,256]{2,1,0:T(1,128)S(1)}, f32[2,128,256]{2,1,0:T(8,128)S(1)}) custom-call(f32[256]{0:T(256)} %tgt_energy_hbm.1, f32[1,256]{1,0:T(1,128)} %proj_energy_hbm.1, f32[256,128]{1,0:T(8,128)} %tgt_own_hbm.1, f32[1,256,128]{2,1,0:T(8,128)} %proj_own_hbm.1), custom_call_target="tpu_custom_call" | custom-call | flops 67108864 | bytes 4194304 | tf_op jit(solution)/shard_map/pallas_call | solution.py:478
  2.8 2.7 %collective-permute-start.3 = (bf16[2,128,256]{2,1,0:T(8,128)(2,1)S(1)}, bf16[2,128,256]{2,1,0:T(8,128)(2,1)S(1)}, u32[]{:S(2)}, u32[]{:S(2)}) collective-permute-start(bf16[2,128,256]{2,1,0:T(8,128)(2,1)S(1)} %get-tuple-element.38), channel_id=1, source_target_pairs={{0,3},{1,8},{3,0},{2,11},{5,6},{4,13},{6,5},{7,14},{9,10},{8,1},{1... | collective-permute-start | bytes 393224 | tf_op jit(solution)/shard_map/ppermute | solution.py:453
  5.5 1.2 %shard_map.107 = (bf16[2,1056,256]{2,1,0:T(8,128)(2,1)S(1)}, f32[1,1,256]{2,1,0:T(1,128)S(1)}) custom-call(f32[256]{0:T(256)} %weight_hbm.1, bf16[2,4,256,256]{3,2,1,0:T(8,128)(2,1)} %bitcast.3, bf16[2,8,256,256]{3,2,1,0:T(8,128)(2,1)} %proj_hbm.3, f32[2,128,256]{2,1,0:T(8,128)S(1)} %get-tuple-element.29.chip_amp, f32[2,1,256]{2,1,0:T(1,128)S(1)} %get-tuple-element.31.energy), custom_call_target="tpu_custom_call" | custom-call | tf_op jit(solution)/shard_map/pallas_call | solution.py:502
  6.8 1.4 %collective-permute-start.2 = (bf16[2,1056,256]{2,1,0:T(8,128)(2,1)S(1)}, bf16[2,1056,256]{2,1,0:T(8,128)(2,1)S(1)}, u32[]{:S(2)}, u32[]{:S(2)}) collective-permute-start(bf16[2,1056,256]{2,1,0:T(8,128)(2,1)S(1)} %get-tuple-element.32.sent), channel_id=1, source_target_pairs={{0,1},{1,0},{2,3},{3,2},{4,5},{5,4},{6,7},{7,6},{8,9},{9,8},{10,11... | collective-permute-start | bytes 3244040 | tf_op jit(solution)/shard_map/ppermute | solution.py:435
  8.1 1.3 %shard_map.106 = (bf16[2,512,256]{2,1,0:T(8,128)(2,1)S(1)}, bf16[2,512,256]{2,1,0:T(8,128)(2,1)S(1)}, bf16[2,256,256]{2,1,0:T(8,128)(2,1)S(1)}, f32[3,2,1,256]{3,2,1,0:T(1,128)S(1)}) custom-call(s32[2,4]{1,0:T(2,128)} %bitcast.5, s32[2,4]{1,0:T(2,128)} %bitcast.6, bf16[2,4,256,256]{3,2,1,0:T(8,128)(2,1)} %bitcast.4, bf16[2,8,256,256]{3,2,1,0:T(8,128)(2,1)} %proj_hbm.3, ...), custom_call_target="tpu_custom_call" | custom-call | flops 34359738368 | bytes 65536 | tf_op jit(solution)/shard_map/pallas_call | solution.py:511
  9.4 1.1 %collective-permute-done.2.theirs = bf16[2,1056,256]{2,1,0:T(8,128)(2,1)S(1)} collective-permute-done((bf16[2,1056,256]{2,1,0:T(8,128)(2,1)S(1)}, bf16[2,1056,256]{2,1,0:T(8,128)(2,1)S(1)}, u32[]{:S(2)}, u32[]{:S(2)}) %collective-permute-start.2) | collective-permute-done | bytes 1081376 | tf_op jit(solution)/shard_map/ppermute | solution.py:435
  11.1 1.5 %collective-permute-start.4 = (bf16[128,256]{1,0:T(8,128)(2,1)S(1)}, bf16[128,256]{1,0:T(8,128)(2,1)S(1)}, u32[]{:S(2)}, u32[]{:S(2)}) collective-permute-start(bf16[128,256]{1,0:T(8,128)(2,1)S(1)} %get-tuple-element.42.own), channel_id=1, source_target_pairs={{0,9},{1,4},{3,10},{2,7},{5,12},{4,1},{6,15},{7,2},{9,0},{8,13},{1... | collective-permute-start | bytes 196616 | tf_op jit(solution)/shard_map/ppermute | solution.py:453
  12.7 1.2 %collective-permute-start.8 = (bf16[128,256]{1,0:T(8,128)(2,1)S(1)}, bf16[128,256]{1,0:T(8,128)(2,1)S(1)}, u32[]{:S(2)}, u32[]{:S(2)}) collective-permute-start(bf16[128,256]{1,0:T(8,128)(2,1)S(1)} %get-tuple-element.44.own), channel_id=1, source_target_pairs={{0,9},{1,4},{3,10},{2,7},{5,12},{4,1},{6,15},{7,2},{9,0},{8,13},{1... | collective-permute-start | bytes 196616 | tf_op jit(solution)/shard_map/ppermute | solution.py:453
  13.8 1.4 %collective-permute-start.7 = (f32[2,1,256]{2,1,0:T(1,128)S(1)}, f32[2,1,256]{2,1,0:T(1,128)S(1)}, u32[]{:S(2)}, u32[]{:S(2)}) collective-permute-start(f32[2,1,256]{2,1,0:T(1,128)S(1)} %get-tuple-element.43.energies), channel_id=1, source_target_pairs={{0,3},{1,8},{3,0},{2,11},{5,6},{4,13},{6,5},{7,14},{9,10},{8,1},{1... | collective-permute-start | bytes 6152 | tf_op jit(solution)/shard_map/ppermute | solution.py:453
  15.3 0.6 %collective-permute-done.4.other = bf16[128,256]{1,0:T(8,128)(2,1)S(1)} collective-permute-done((bf16[128,256]{1,0:T(8,128)(2,1)S(1)}, bf16[128,256]{1,0:T(8,128)(2,1)S(1)}, u32[]{:S(2)}, u32[]{:S(2)}) %collective-permute-start.4) | collective-permute-done | bytes 65568 | tf_op jit(solution)/shard_map/ppermute | solution.py:453
  15.9 1.2 %collective-permute-start.6 = (bf16[128,256]{1,0:T(8,128)(2,1)S(1)}, bf16[128,256]{1,0:T(8,128)(2,1)S(1)}, u32[]{:S(2)}, u32[]{:S(2)}) collective-permute-start(bf16[128,256]{1,0:T(8,128)(2,1)S(1)} %shard_map.110), channel_id=1, source_target_pairs={{0,4},{1,3},{3,7},{2,0},{5,1},{4,6},{6,2},{7,5},{9,13},{8,10},{10,... | collective-permute-start | bytes 196616 | tf_op jit(solution)/shard_map/ppermute | solution.py:453
  17.1 0.7 %collective-permute-start.5 = (bf16[128,256]{1,0:T(8,128)(2,1)S(1)}, bf16[128,256]{1,0:T(8,128)(2,1)S(1)}, u32[]{:S(2)}, u32[]{:S(2)}) collective-permute-start(bf16[128,256]{1,0:T(8,128)(2,1)S(1)} %shard_map.110), channel_id=1, source_target_pairs={{0,1},{1,0},{2,3},{3,2},{4,5},{5,4},{6,7},{7,6},{8,9},{9,8},{10,11... | collective-permute-start | bytes 196616 | tf_op jit(solution)/shard_map/ppermute | solution.py:435
  18.0 1.5 %collective-permute-start.10 = (bf16[128,256]{1,0:T(8,128)(2,1)S(1)}, bf16[128,256]{1,0:T(8,128)(2,1)S(1)}, u32[]{:S(2)}, u32[]{:S(2)}) collective-permute-start(bf16[128,256]{1,0:T(8,128)(2,1)S(1)} %shard_map.112), channel_id=1, source_target_pairs={{0,4},{1,3},{3,7},{2,0},{5,1},{4,6},{6,2},{7,5},{9,13},{8,10},{10,... | collective-permute-start | bytes 196616 | tf_op jit(solution)/shard_map/ppermute | solution.py:453
  19.5 0.7 %collective-permute-done.6.low_there = bf16[128,256]{1,0:T(8,128)(2,1)S(1)} collective-permute-done((bf16[128,256]{1,0:T(8,128)(2,1)S(1)}, bf16[128,256]{1,0:T(8,128)(2,1)S(1)}, u32[]{:S(2)}, u32[]{:S(2)}) %collective-permute-start.6) | collective-permute-done | bytes 65568 | tf_op jit(solution)/shard_map/ppermute | solution.py:453
  20.7 1.6 %collective-permute-done.10.high_there = bf16[128,256]{1,0:T(8,128)(2,1)S(1)} collective-permute-done((bf16[128,256]{1,0:T(8,128)(2,1)S(1)}, bf16[128,256]{1,0:T(8,128)(2,1)S(1)}, u32[]{:S(2)}, u32[]{:S(2)}) %collective-permute-start.10) | collective-permute-done | bytes 65568 | tf_op jit(solution)/shard_map/ppermute | solution.py:453
  22.3 0.8 %shard_map.113 = (bf16[128,256]{1,0:T(8,128)(2,1)S(1)}, bf16[128,256]{1,0:T(8,128)(2,1)S(1)}, f32[128,256]{1,0:T(8,128)S(1)}, f32[128,256]{1,0:T(8,128)S(1)}) custom-call(bf16[2,512,256]{2,1,0:T(8,128)(2,1)S(1)} %get-tuple-element.30.mine_chip, bf16[2,512,256]{2,1,0:T(8,128)(2,1)S(1)} %get-tuple-element.34.mine_far, ...), custom_call_target="tpu_custom_call" | custom-call | tf_op jit(solution)/shard_map/pallas_call | solution.py:432
  23.4 2.5 %collective-permute-start.11 = (bf16[128,256]{1,0:T(8,128)(2,1)S(1)}, bf16[128,256]{1,0:T(8,128)(2,1)S(1)}, u32[]{:S(2)}, u32[]{:S(2)}) collective-permute-start(bf16[128,256]{1,0:T(8,128)(2,1)S(1)} %get-tuple-element.45.own), channel_id=1, source_target_pairs={{0,5},{1,4},{3,6},{2,7},{5,0},{4,1},{6,3},{7,2},{9,12},{8,13},{10,... | collective-permute-start | bytes 196616 | tf_op jit(solution)/shard_map/ppermute | solution.py:453
  25.8 2.1 %collective-permute-done.15.other = bf16[128,256]{1,0:T(8,128)(2,1)S(1)} collective-permute-done((bf16[128,256]{1,0:T(8,128)(2,1)S(1)}, bf16[128,256]{1,0:T(8,128)(2,1)S(1)}, u32[]{:S(2)}, u32[]{:S(2)}) %collective-permute-start.15) | collective-permute-done | bytes 65568 | tf_op jit(solution)/shard_map/ppermute | solution.py:453
  27.9 1.2 %collective-permute-start.16 = (bf16[128,256]{1,0:T(8,128)(2,1)S(1)}, bf16[128,256]{1,0:T(8,128)(2,1)S(1)}, u32[]{:S(2)}, u32[]{:S(2)}) collective-permute-start(bf16[128,256]{1,0:T(8,128)(2,1)S(1)} %shard_map.116.own), channel_id=1, source_target_pairs={{0,5},{1,2},{3,6},{2,1},{5,0},{4,7},{6,3},{7,4},{9,12},{8,11},{10,... | collective-permute-start | bytes 196616 | tf_op jit(solution)/shard_map/ppermute | solution.py:453
  29.2 1.5 %collective-permute-start.12 = (bf16[128,256]{1,0:T(8,128)(2,1)S(1)}, bf16[128,256]{1,0:T(8,128)(2,1)S(1)}, u32[]{:S(2)}, u32[]{:S(2)}) collective-permute-start(bf16[128,256]{1,0:T(8,128)(2,1)S(1)} %shard_map.114.own), channel_id=1, source_target_pairs={{0,9},{1,2},{3,10},{2,1},{5,12},{4,7},{6,15},{7,4},{9,0},{8,11},{1... | collective-permute-start | bytes 196616 | tf_op jit(solution)/shard_map/ppermute | solution.py:453
  30.7 1.0 %collective-permute-done.16.other = bf16[128,256]{1,0:T(8,128)(2,1)S(1)} collective-permute-done((bf16[128,256]{1,0:T(8,128)(2,1)S(1)}, bf16[128,256]{1,0:T(8,128)(2,1)S(1)}, u32[]{:S(2)}, u32[]{:S(2)}) %collective-permute-start.16) | collective-permute-done | bytes 65568 | tf_op jit(solution)/shard_map/ppermute | solution.py:453
  32.3 1.6 %collective-permute-done.12.other = bf16[128,256]{1,0:T(8,128)(2,1)S(1)} collective-permute-done((bf16[128,256]{1,0:T(8,128)(2,1)S(1)}, bf16[128,256]{1,0:T(8,128)(2,1)S(1)}, u32[]{:S(2)}, u32[]{:S(2)}) %collective-permute-start.12) | collective-permute-done | bytes 65568 | tf_op jit(solution)/shard_map/ppermute | solution.py:453
  34.5 0.7 %collective-permute-done.13.high = bf16[128,256]{1,0:T(8,128)(2,1)S(1)} collective-permute-done((bf16[128,256]{1,0:T(8,128)(2,1)S(1)}, bf16[128,256]{1,0:T(8,128)(2,1)S(1)}, u32[]{:S(2)}, u32[]{:S(2)}) %collective-permute-start.13) | collective-permute-done | bytes 65568 | tf_op jit(solution)/shard_map/ppermute | solution.py:435
  35.2 1.0 %shard_map.119 = (f32[256,128]{1,0:T(8,128)}, f32[1,256,128]{2,1,0:T(8,128)}) custom-call(bf16[2,512,256]{2,1,0:T(8,128)(2,1)S(1)} %get-tuple-element.30.mine_chip, bf16[2,1056,256]{2,1,0:T(8,128)(2,1)S(1)} %collective-permute-done.2.theirs, bf16[128,256]{1,0:T(8,128)(2,1)S(1)} %collective-permute-done.13.high, f32[128,256]{1,0:T(8,128)S(1)} %get-tuple-element.52.my_part, ...), custom_call_target="tpu_custom_call" | custom-call | tf_op jit(solution)/shard_map/pallas_call | solution.py:586
  (30 shorter events, 3.9 us)
Async XLA Ops:
  0.6 1.7 %collective-permute-start = (f32[256,128]{1,0:T(8,128)}, f32[256,128]{1,0:T(8,128)S(1)}, u32[]{:S(2)}, u32[]{:S(2)}) collective-permute-start(f32[256,128]{1,0:T(8,128)} %tgt_own_hbm.1), channel_id=1, source_target_pairs={{0,1},{1,0},{2,3},{3,2},{4,5},{5,4},{6,7},{7,6},{8,9},{9,8},{10,11... | collective-permute-start | bytes 393224 | tf_op jit(solution)/shard_map/ppermute | solution.py:435
  1.1 1.6 %collective-permute-start.1 = (f32[1,256,128]{2,1,0:T(8,128)}, f32[1,256,128]{2,1,0:T(8,128)S(1)}, u32[]{:S(2)}, u32[]{:S(2)}) collective-permute-start(f32[1,256,128]{2,1,0:T(8,128)} %proj_own_hbm.1), channel_id=1, source_target_pairs={{0,1},{1,0},{2,3},{3,2},{4,5},{5,4},{6,7},{7,6},{8,9},{9,8},{10,11... | collective-permute-start | bytes 393224 | tf_op jit(solution)/shard_map/ppermute | solution.py:435
  2.8 7.9 %collective-permute-start.3 = (bf16[2,128,256]{2,1,0:T(8,128)(2,1)S(1)}, bf16[2,128,256]{2,1,0:T(8,128)(2,1)S(1)}, u32[]{:S(2)}, u32[]{:S(2)}) collective-permute-start(bf16[2,128,256]{2,1,0:T(8,128)(2,1)S(1)} %get-tuple-element.38), channel_id=1, source_target_pairs={{0,3},{1,8},{3,0},{2,11},{5,6},{4,13},{6,5},{7,14},{9,10},{8,1},{1... | collective-permute-start | bytes 393224 | tf_op jit(solution)/shard_map/ppermute | solution.py:453
  6.8 3.7 %collective-permute-start.2 = (bf16[2,1056,256]{2,1,0:T(8,128)(2,1)S(1)}, bf16[2,1056,256]{2,1,0:T(8,128)(2,1)S(1)}, u32[]{:S(2)}, u32[]{:S(2)}) collective-permute-start(bf16[2,1056,256]{2,1,0:T(8,128)(2,1)S(1)} %get-tuple-element.32.sent), channel_id=1, source_target_pairs={{0,1},{1,0},{2,3},{3,2},{4,5},{5,4},{6,7},{7,6},{8,9},{9,8},{10,11... | collective-permute-start | bytes 3244040 | tf_op jit(solution)/shard_map/ppermute | solution.py:435
  11.1 4.8 %collective-permute-start.4 = (bf16[128,256]{1,0:T(8,128)(2,1)S(1)}, bf16[128,256]{1,0:T(8,128)(2,1)S(1)}, u32[]{:S(2)}, u32[]{:S(2)}) collective-permute-start(bf16[128,256]{1,0:T(8,128)(2,1)S(1)} %get-tuple-element.42.own), channel_id=1, source_target_pairs={{0,9},{1,4},{3,10},{2,7},{5,12},{4,1},{6,15},{7,2},{9,0},{8,13},{1... | collective-permute-start | bytes 196616 | tf_op jit(solution)/shard_map/ppermute | solution.py:453
  12.7 5.3 %collective-permute-start.8 = (bf16[128,256]{1,0:T(8,128)(2,1)S(1)}, bf16[128,256]{1,0:T(8,128)(2,1)S(1)}, u32[]{:S(2)}, u32[]{:S(2)}) collective-permute-start(bf16[128,256]{1,0:T(8,128)(2,1)S(1)} %get-tuple-element.44.own), channel_id=1, source_target_pairs={{0,9},{1,4},{3,10},{2,7},{5,12},{4,1},{6,15},{7,2},{9,0},{8,13},{1... | collective-permute-start | bytes 196616 | tf_op jit(solution)/shard_map/ppermute | solution.py:453
  13.8 4.0 %collective-permute-start.7 = (f32[2,1,256]{2,1,0:T(1,128)S(1)}, f32[2,1,256]{2,1,0:T(1,128)S(1)}, u32[]{:S(2)}, u32[]{:S(2)}) collective-permute-start(f32[2,1,256]{2,1,0:T(1,128)S(1)} %get-tuple-element.43.energies), channel_id=1, source_target_pairs={{0,3},{1,8},{3,0},{2,11},{5,6},{4,13},{6,5},{7,14},{9,10},{8,1},{1... | collective-permute-start | bytes 6152 | tf_op jit(solution)/shard_map/ppermute | solution.py:453
  15.9 4.3 %collective-permute-start.6 = (bf16[128,256]{1,0:T(8,128)(2,1)S(1)}, bf16[128,256]{1,0:T(8,128)(2,1)S(1)}, u32[]{:S(2)}, u32[]{:S(2)}) collective-permute-start(bf16[128,256]{1,0:T(8,128)(2,1)S(1)} %shard_map.110), channel_id=1, source_target_pairs={{0,4},{1,3},{3,7},{2,0},{5,1},{4,6},{6,2},{7,5},{9,13},{8,10},{10,... | collective-permute-start | bytes 196616 | tf_op jit(solution)/shard_map/ppermute | solution.py:453
  17.1 3.1 %collective-permute-start.5 = (bf16[128,256]{1,0:T(8,128)(2,1)S(1)}, bf16[128,256]{1,0:T(8,128)(2,1)S(1)}, u32[]{:S(2)}, u32[]{:S(2)}) collective-permute-start(bf16[128,256]{1,0:T(8,128)(2,1)S(1)} %shard_map.110), channel_id=1, source_target_pairs={{0,1},{1,0},{2,3},{3,2},{4,5},{5,4},{6,7},{7,6},{8,9},{9,8},{10,11... | collective-permute-start | bytes 196616 | tf_op jit(solution)/shard_map/ppermute | solution.py:435
  18.0 4.3 %collective-permute-start.10 = (bf16[128,256]{1,0:T(8,128)(2,1)S(1)}, bf16[128,256]{1,0:T(8,128)(2,1)S(1)}, u32[]{:S(2)}, u32[]{:S(2)}) collective-permute-start(bf16[128,256]{1,0:T(8,128)(2,1)S(1)} %shard_map.112), channel_id=1, source_target_pairs={{0,4},{1,3},{3,7},{2,0},{5,1},{4,6},{6,2},{7,5},{9,13},{8,10},{10,... | collective-permute-start | bytes 196616 | tf_op jit(solution)/shard_map/ppermute | solution.py:453
  19.5 2.9 %collective-permute-start.9 = (bf16[128,256]{1,0:T(8,128)(2,1)S(1)}, bf16[128,256]{1,0:T(8,128)(2,1)S(1)}, u32[]{:S(2)}, u32[]{:S(2)}) collective-permute-start(bf16[128,256]{1,0:T(8,128)(2,1)S(1)} %shard_map.112), channel_id=1, source_target_pairs={{0,1},{1,0},{2,3},{3,2},{4,5},{5,4},{6,7},{7,6},{8,9},{9,8},{10,11... | collective-permute-start | bytes 196616 | tf_op jit(solution)/shard_map/ppermute | solution.py:435
  23.2 4.8 %collective-permute-start.15 = (bf16[128,256]{1,0:T(8,128)(2,1)S(1)}, bf16[128,256]{1,0:T(8,128)(2,1)S(1)}, u32[]{:S(2)}, u32[]{:S(2)}) collective-permute-start(bf16[128,256]{1,0:T(8,128)(2,1)S(1)} %get-tuple-element.47.own), channel_id=1, source_target_pairs={{0,9},{1,4},{3,10},{2,7},{5,12},{4,1},{6,15},{7,2},{9,0},{8,13},{1... | collective-permute-start | bytes 196616 | tf_op jit(solution)/shard_map/ppermute | solution.py:453
  23.4 5.8 %collective-permute-start.11 = (bf16[128,256]{1,0:T(8,128)(2,1)S(1)}, bf16[128,256]{1,0:T(8,128)(2,1)S(1)}, u32[]{:S(2)}, u32[]{:S(2)}) collective-permute-start(bf16[128,256]{1,0:T(8,128)(2,1)S(1)} %get-tuple-element.45.own), channel_id=1, source_target_pairs={{0,5},{1,4},{3,6},{2,7},{5,0},{4,1},{6,3},{7,2},{9,12},{8,13},{10,... | collective-permute-start | bytes 196616 | tf_op jit(solution)/shard_map/ppermute | solution.py:453
  27.9 3.8 %collective-permute-start.16 = (bf16[128,256]{1,0:T(8,128)(2,1)S(1)}, bf16[128,256]{1,0:T(8,128)(2,1)S(1)}, u32[]{:S(2)}, u32[]{:S(2)}) collective-permute-start(bf16[128,256]{1,0:T(8,128)(2,1)S(1)} %shard_map.116.own), channel_id=1, source_target_pairs={{0,5},{1,2},{3,6},{2,1},{5,0},{4,7},{6,3},{7,4},{9,12},{8,11},{10,... | collective-permute-start | bytes 196616 | tf_op jit(solution)/shard_map/ppermute | solution.py:453
  29.2 4.7 %collective-permute-start.12 = (bf16[128,256]{1,0:T(8,128)(2,1)S(1)}, bf16[128,256]{1,0:T(8,128)(2,1)S(1)}, u32[]{:S(2)}, u32[]{:S(2)}) collective-permute-start(bf16[128,256]{1,0:T(8,128)(2,1)S(1)} %shard_map.114.own), channel_id=1, source_target_pairs={{0,9},{1,2},{3,10},{2,1},{5,12},{4,7},{6,15},{7,4},{9,0},{8,11},{1... | collective-permute-start | bytes 196616 | tf_op jit(solution)/shard_map/ppermute | solution.py:453
  30.7 3.2 %collective-permute-start.14 = (bf16[2,256,256]{2,1,0:T(8,128)(2,1)S(1)}, bf16[2,256,256]{2,1,0:T(8,128)(2,1)S(1)}, u32[]{:S(2)}, u32[]{:S(2)}) collective-permute-start(bf16[2,256,256]{2,1,0:T(8,128)(2,1)S(1)} %get-tuple-element.46), channel_id=1, source_target_pairs={{0,1},{1,0},{2,3},{3,2},{4,5},{5,4},{6,7},{7,6},{8,9},{9,8},{10,11... | collective-permute-start | bytes 786440 | tf_op jit(solution)/shard_map/ppermute | solution.py:435
  31.7 2.3 %collective-permute-start.17 = (bf16[128,256]{1,0:T(8,128)(2,1)S(1)}, bf16[128,256]{1,0:T(8,128)(2,1)S(1)}, u32[]{:S(2)}, u32[]{:S(2)}) collective-permute-start(bf16[128,256]{1,0:T(8,128)(2,1)S(1)} %shard_map.117.low), channel_id=1, source_target_pairs={{0,1},{1,0},{2,3},{3,2},{4,5},{5,4},{6,7},{7,6},{8,9},{9,8},{10,11... | collective-permute-start | bytes 196616 | tf_op jit(solution)/shard_map/ppermute | solution.py:435
  31.8 2.2 %collective-permute-start.18 = (f32[128,256]{1,0:T(8,128)S(1)}, f32[128,256]{1,0:T(8,128)S(1)}, u32[]{:S(2)}, u32[]{:S(2)}) collective-permute-start(f32[128,256]{1,0:T(8,128)S(1)} %get-tuple-element.51), channel_id=1, source_target_pairs={{0,1},{1,0},{2,3},{3,2},{4,5},{5,4},{6,7},{7,6},{8,9},{9,8},{10,11... | collective-permute-start | bytes 393224 | tf_op jit(solution)/shard_map/ppermute | solution.py:435
  33.9 1.3 %collective-permute-start.13 = (bf16[128,256]{1,0:T(8,128)(2,1)S(1)}, bf16[128,256]{1,0:T(8,128)(2,1)S(1)}, u32[]{:S(2)}, u32[]{:S(2)}) collective-permute-start(bf16[128,256]{1,0:T(8,128)(2,1)S(1)} %shard_map.115.high), channel_id=1, source_target_pairs={{0,1},{1,0},{2,3},{3,2},{4,5},{5,4},{6,7},{7,6},{8,9},{9,8},{10,11... | collective-permute-start | bytes 196616 | tf_op jit(solution)/shard_map/ppermute | solution.py:435

commit v30 on v24

--- a/solution.py
+++ b/solution.py
@@ -16,16 +16,16 @@
 
 
 def parity(place):
-    odd = 0
+    even = 1
     while place:
-        odd, place = odd ^ (place & 1), place >> 1
-    return odd
+        even, place = even ^ (place & 1), place >> 1
+    return even
 
 
 def my_kind():
     n_tgt, n_prj = lax.axis_size("tgt"), lax.axis_size("prj")
     place = lax.axis_index("tgt") * n_prj + lax.axis_index("prj")
-    kind = lax.axis_index("rep")
+    kind = 1 - lax.axis_index("rep")
     for bit in range((n_tgt * n_prj).bit_length() - 1):
         kind = jnp.bitwise_xor(kind, jnp.bitwise_and(lax.shift_right_logical(place, bit), 1))
     return kind

time: 35.5 us -> 36 us (1.014)
  starting transfers between devices: 18.2 us -> 21.6 us
  waiting for transfers between devices: 9.06 us -> 6.08 us
    ppermute x10, waiting for transfers between devices: 7.01 us -> 3.94 us  [exchanged(): return lax.ppermute(block, DEVICES, pairs)]
    ppermute x9, starting transfers between devices: 3.42 us -> 5.8 us  [other_core(): return lax.ppermute(block, 'rep', [(0, 1), (1, 0)])]
    ppermute x10, starting transfers between devices: 14.8 us -> 15.8 us  [exchanged(): return lax.ppermute(block, DEVICES, pairs)]
  transfers between devices with their start and end apart: 19 -> 19, of which waited for: 11 -> 8; matrix products, arithmetic and copies ran while one was open for 0% -> 0% of each run, Pallas kernels for 17% -> 17%
where the time goes in v30:
time: 36 us; the launch traced here: 35.8 us
  starting transfers between devices  21.6 us (60%)
  Pallas kernels  7.39 us (21%)
  waiting for transfers between devices  6.08 us (17%)
  between operations  0.77 us (2%)
    ppermute x10, starting transfers between devices, exchanged(): return lax.ppermute(block, DEVICES, pairs)  15.8 us
    ppermute x9, starting transfers between devices, other_core(): return lax.ppermute(block, 'rep', [(0, 1), (1, 0)])  5.8 us
    ppermute x10, waiting for transfers between devices, exchanged(): return lax.ppermute(block, DEVICES, pairs)  3.94 us
    pallas_call x12, Pallas kernels, run(): return call(kernel, out_shape, [VMEM] * len(blocks))(*blocks)  2.75 us
    ppermute x9, waiting for transfers between devices, other_core(): return lax.ppermute(block, 'rep', [(0, 1), (1, 0)])  2.14 us
    pallas_call x1, Pallas kernels, shards(): call(functools.partial(side_kernel, gate_levels, neighbours), [pair, pair...  1.28 us
    pallas_call x1, Pallas kernels, shards(): call(functools.partial(sent_kernel, neighbours), [in_vmem((2, 4 * rows +...  1.24 us
    pallas_call x1, Pallas kernels, shards(): call(load_kernel, [in_vmem((2, 1, rows), jnp.float32), in_vmem((2, two_co...  1.14 us
  transfers between devices with their start and end apart: 19, of which 8 were waited for; matrix products, arithmetic and copies ran while one was open for 0% of the time, Pallas kernels for 17%

profile of v30, /device:TPU:0, one launch (start us, length us, event | category | flops | bytes accessed | tf_op | source)
XLA Modules:
  0.0 35.8 jit_solution(15255403653444574763)
XLA Ops:
  0.6 0.5 %collective-permute-start = (f32[256,128]{1,0:T(8,128)}, f32[256,128]{1,0:T(8,128)S(1)}, u32[]{:S(2)}, u32[]{:S(2)}) collective-permute-start(f32[256,128]{1,0:T(8,128)} %tgt_own_hbm.1), channel_id=1, source_target_pairs={{0,1},{1,0},{2,3},{3,2},{4,5},{5,4},{6,7},{7,6},{8,9},{9,8},{10,11... | collective-permute-start | bytes 393224 | tf_op jit(solution)/shard_map/ppermute | solution.py:433
  1.2 1.1 %shard_map.104 = (f32[2,1,256]{2,1,0:T(1,128)S(1)}, f32[2,128,256]{2,1,0:T(8,128)S(1)}) custom-call(f32[256]{0:T(256)} %tgt_energy_hbm.1, f32[1,256]{1,0:T(1,128)} %proj_energy_hbm.1, f32[256,128]{1,0:T(8,128)} %tgt_own_hbm.1, f32[1,256,128]{2,1,0:T(8,128)} %proj_own_hbm.1), custom_call_target="tpu_custom_call" | custom-call | flops 67108864 | bytes 4194304 | tf_op jit(solution)/shard_map/pallas_call | solution.py:473
  2.8 3.8 %collective-permute-start.3 = (bf16[2,128,256]{2,1,0:T(8,128)(2,1)S(1)}, bf16[2,128,256]{2,1,0:T(8,128)(2,1)S(1)}, u32[]{:S(2)}, u32[]{:S(2)}) collective-permute-start(bf16[2,128,256]{2,1,0:T(8,128)(2,1)S(1)} %get-tuple-element.36), channel_id=1, source_target_pairs={{1,2},{0,9},{2,1},{3,10},{4,7},{5,12},{7,4},{6,15},{8,11},{9,0},{1... | collective-permute-start | bytes 393224 | tf_op jit(solution)/shard_map/ppermute | solution.py:451
  6.6 1.2 %shard_map.107 = (bf16[2,1056,256]{2,1,0:T(8,128)(2,1)S(1)}, f32[1,1,256]{2,1,0:T(1,128)S(1)}) custom-call(f32[256]{0:T(256)} %weight_hbm.1, bf16[2,4,256,256]{3,2,1,0:T(8,128)(2,1)} %bitcast.3, bf16[2,8,256,256]{3,2,1,0:T(8,128)(2,1)} %proj_hbm.3, f32[2,128,256]{2,1,0:T(8,128)S(1)} %get-tuple-element.27.chip_amp, f32[2,1,256]{2,1,0:T(1,128)S(1)} %get-tuple-element.29.energy), custom_call_target="tpu_custom_call" | custom-call | tf_op jit(solution)/shard_map/pallas_call | solution.py:497
  7.9 1.3 %shard_map.106 = (bf16[2,512,256]{2,1,0:T(8,128)(2,1)S(1)}, bf16[2,512,256]{2,1,0:T(8,128)(2,1)S(1)}, bf16[2,256,256]{2,1,0:T(8,128)(2,1)S(1)}, f32[3,2,1,256]{3,2,1,0:T(1,128)S(1)}) custom-call(s32[2,4]{1,0:T(2,128)} %bitcast.5, s32[2,4]{1,0:T(2,128)} %bitcast.6, bf16[2,4,256,256]{3,2,1,0:T(8,128)(2,1)} %bitcast.4, bf16[2,8,256,256]{3,2,1,0:T(8,128)(2,1)} %proj_hbm.3, ...), custom_call_target="tpu_custom_call" | custom-call | flops 34359738368 | bytes 65536 | tf_op jit(solution)/shard_map/pallas_call | solution.py:506
  9.2 1.4 %collective-permute-done.2.theirs = bf16[2,1056,256]{2,1,0:T(8,128)(2,1)S(1)} collective-permute-done((bf16[2,1056,256]{2,1,0:T(8,128)(2,1)S(1)}, bf16[2,1056,256]{2,1,0:T(8,128)(2,1)S(1)}, u32[]{:S(2)}, u32[]{:S(2)}) %collective-permute-start.2) | collective-permute-done | bytes 1081376 | tf_op jit(solution)/shard_map/ppermute | solution.py:433
  11.3 1.4 %collective-permute-start.4 = (bf16[128,256]{1,0:T(8,128)(2,1)S(1)}, bf16[128,256]{1,0:T(8,128)(2,1)S(1)}, u32[]{:S(2)}, u32[]{:S(2)}) collective-permute-start(bf16[128,256]{1,0:T(8,128)(2,1)S(1)} %get-tuple-element.40.own), channel_id=1, source_target_pairs={{1,8},{0,5},{2,11},{3,6},{4,13},{5,0},{7,14},{6,3},{8,1},{9,12},{1... | collective-permute-start | bytes 196616 | tf_op jit(solution)/shard_map/ppermute | solution.py:451
  13.1 2.0 %collective-permute-start.7 = (f32[2,1,256]{2,1,0:T(1,128)S(1)}, f32[2,1,256]{2,1,0:T(1,128)S(1)}, u32[]{:S(2)}, u32[]{:S(2)}) collective-permute-start(f32[2,1,256]{2,1,0:T(1,128)S(1)} %get-tuple-element.41.energies), channel_id=1, source_target_pairs={{1,2},{0,9},{2,1},{3,10},{4,7},{5,12},{7,4},{6,15},{8,11},{9,0},{1... | collective-permute-start | bytes 6152 | tf_op jit(solution)/shard_map/ppermute | solution.py:451
  15.2 2.3 %collective-permute-start.6 = (bf16[128,256]{1,0:T(8,128)(2,1)S(1)}, bf16[128,256]{1,0:T(8,128)(2,1)S(1)}, u32[]{:S(2)}, u32[]{:S(2)}) collective-permute-start(bf16[128,256]{1,0:T(8,128)(2,1)S(1)} %shard_map.110), channel_id=1, source_target_pairs={{1,5},{0,2},{2,6},{3,1},{4,0},{5,7},{7,3},{6,4},{8,12},{9,11},{11,... | collective-permute-start | bytes 196616 | tf_op jit(solution)/shard_map/ppermute | solution.py:451
  17.5 1.2 %collective-permute-start.10 = (bf16[128,256]{1,0:T(8,128)(2,1)S(1)}, bf16[128,256]{1,0:T(8,128)(2,1)S(1)}, u32[]{:S(2)}, u32[]{:S(2)}) collective-permute-start(bf16[128,256]{1,0:T(8,128)(2,1)S(1)} %shard_map.112), channel_id=1, source_target_pairs={{1,5},{0,2},{2,6},{3,1},{4,0},{5,7},{7,3},{6,4},{8,12},{9,11},{11,... | collective-permute-start | bytes 196616 | tf_op jit(solution)/shard_map/ppermute | solution.py:451
  19.2 0.9 %collective-permute-done.6.low_there = bf16[128,256]{1,0:T(8,128)(2,1)S(1)} collective-permute-done((bf16[128,256]{1,0:T(8,128)(2,1)S(1)}, bf16[128,256]{1,0:T(8,128)(2,1)S(1)}, u32[]{:S(2)}, u32[]{:S(2)}) %collective-permute-start.6) | collective-permute-done | bytes 65568 | tf_op jit(solution)/shard_map/ppermute | solution.py:451
  20.1 0.5 %shard_map.111.states_ref = f32[4,128,256]{2,1,0:T(8,128)S(1)} custom-call(bf16[2,512,256]{2,1,0:T(8,128)(2,1)S(1)} %get-tuple-element.28.mine_chip, bf16[2,512,256]{2,1,0:T(8,128)(2,1)S(1)} %get-tuple-element.32.mine_far, bf16[2,1056,256]{2,1,0:T(8,128)(2,1)S(1)} %collective-permute-done.2.theirs, bf16[128,256]{1,0:T(8,128)(2,1)S(1)} %collective-permute-done.5.low, ...), custom_call_target="tpu_custom_call" | custom-call | tf_op jit(solution)/shard_map/pallas_call | solution.py:430
  20.7 1.1 %collective-permute-done.10.high_there = bf16[128,256]{1,0:T(8,128)(2,1)S(1)} collective-permute-done((bf16[128,256]{1,0:T(8,128)(2,1)S(1)}, bf16[128,256]{1,0:T(8,128)(2,1)S(1)}, u32[]{:S(2)}, u32[]{:S(2)}) %collective-permute-start.10) | collective-permute-done | bytes 65568 | tf_op jit(solution)/shard_map/ppermute | solution.py:451
  21.8 0.8 %shard_map.113 = (bf16[128,256]{1,0:T(8,128)(2,1)S(1)}, bf16[128,256]{1,0:T(8,128)(2,1)S(1)}, f32[128,256]{1,0:T(8,128)S(1)}, f32[128,256]{1,0:T(8,128)S(1)}) custom-call(bf16[2,512,256]{2,1,0:T(8,128)(2,1)S(1)} %get-tuple-element.28.mine_chip, bf16[2,512,256]{2,1,0:T(8,128)(2,1)S(1)} %get-tuple-element.32.mine_far, ...), custom_call_target="tpu_custom_call" | custom-call | tf_op jit(solution)/shard_map/pallas_call | solution.py:430
  22.9 1.5 %collective-permute-start.11 = (bf16[128,256]{1,0:T(8,128)(2,1)S(1)}, bf16[128,256]{1,0:T(8,128)(2,1)S(1)}, u32[]{:S(2)}, u32[]{:S(2)}) collective-permute-start(bf16[128,256]{1,0:T(8,128)(2,1)S(1)} %get-tuple-element.43.own), channel_id=1, source_target_pairs={{1,8},{0,5},{2,11},{3,6},{4,13},{5,0},{7,14},{6,3},{8,1},{9,12},{1... | collective-permute-start | bytes 196616 | tf_op jit(solution)/shard_map/ppermute | solution.py:451
  24.5 0.9 %collective-permute-start.18 = (f32[128,256]{1,0:T(8,128)S(1)}, f32[128,256]{1,0:T(8,128)S(1)}, u32[]{:S(2)}, u32[]{:S(2)}) collective-permute-start(f32[128,256]{1,0:T(8,128)S(1)} %get-tuple-element.47), channel_id=1, source_target_pairs={{0,1},{1,0},{2,3},{3,2},{4,5},{5,4},{6,7},{7,6},{8,9},{9,8},{10,11... | collective-permute-start | bytes 393224 | tf_op jit(solution)/shard_map/ppermute | solution.py:433
  25.4 1.0 %collective-permute-done.15.other = bf16[128,256]{1,0:T(8,128)(2,1)S(1)} collective-permute-done((bf16[128,256]{1,0:T(8,128)(2,1)S(1)}, bf16[128,256]{1,0:T(8,128)(2,1)S(1)}, u32[]{:S(2)}, u32[]{:S(2)}) %collective-permute-start.15) | collective-permute-done | bytes 65568 | tf_op jit(solution)/shard_map/ppermute | solution.py:451
  26.4 1.2 %collective-permute-start.16 = (bf16[128,256]{1,0:T(8,128)(2,1)S(1)}, bf16[128,256]{1,0:T(8,128)(2,1)S(1)}, u32[]{:S(2)}, u32[]{:S(2)}) collective-permute-start(bf16[128,256]{1,0:T(8,128)(2,1)S(1)} %shard_map.116.own), channel_id=1, source_target_pairs={{1,4},{0,3},{2,7},{3,0},{4,1},{5,6},{7,2},{6,5},{8,13},{9,10},{11,... | collective-permute-start | bytes 196616 | tf_op jit(solution)/shard_map/ppermute | solution.py:451
  27.8 1.7 %collective-permute-start.12 = (bf16[128,256]{1,0:T(8,128)(2,1)S(1)}, bf16[128,256]{1,0:T(8,128)(2,1)S(1)}, u32[]{:S(2)}, u32[]{:S(2)}) collective-permute-start(bf16[128,256]{1,0:T(8,128)(2,1)S(1)} %shard_map.114.own), channel_id=1, source_target_pairs={{1,4},{0,3},{2,7},{3,0},{4,1},{5,6},{7,2},{6,5},{8,13},{9,10},{11,... | collective-permute-start | bytes 196616 | tf_op jit(solution)/shard_map/ppermute | solution.py:451
  29.5 0.6 %collective-permute-done.16.other = bf16[128,256]{1,0:T(8,128)(2,1)S(1)} collective-permute-done((bf16[128,256]{1,0:T(8,128)(2,1)S(1)}, bf16[128,256]{1,0:T(8,128)(2,1)S(1)}, u32[]{:S(2)}, u32[]{:S(2)}) %collective-permute-start.16) | collective-permute-done | bytes 65568 | tf_op jit(solution)/shard_map/ppermute | solution.py:451
  30.2 1.6 %collective-permute-start.17 = (bf16[128,256]{1,0:T(8,128)(2,1)S(1)}, bf16[128,256]{1,0:T(8,128)(2,1)S(1)}, u32[]{:S(2)}, u32[]{:S(2)}) collective-permute-start(bf16[128,256]{1,0:T(8,128)(2,1)S(1)} %shard_map.117.low), channel_id=1, source_target_pairs={{0,1},{1,0},{2,3},{3,2},{4,5},{5,4},{6,7},{7,6},{8,9},{9,8},{10,11... | collective-permute-start | bytes 196616 | tf_op jit(solution)/shard_map/ppermute | solution.py:433
  31.8 2.1 %collective-permute-start.13 = (bf16[128,256]{1,0:T(8,128)(2,1)S(1)}, bf16[128,256]{1,0:T(8,128)(2,1)S(1)}, u32[]{:S(2)}, u32[]{:S(2)}) collective-permute-start(bf16[128,256]{1,0:T(8,128)(2,1)S(1)} %shard_map.115.high), channel_id=1, source_target_pairs={{0,1},{1,0},{2,3},{3,2},{4,5},{5,4},{6,7},{7,6},{8,9},{9,8},{10,11... | collective-permute-start | bytes 196616 | tf_op jit(solution)/shard_map/ppermute | solution.py:433
  33.9 0.5 %shard_map.118 = (f32[128,256]{1,0:T(8,128)S(1)}, f32[256,128]{1,0:T(8,128)S(1)}) custom-call(bf16[2,512,256]{2,1,0:T(8,128)(2,1)S(1)} %get-tuple-element.28.mine_chip, bf16[2,1056,256]{2,1,0:T(8,128)(2,1)S(1)} %collective-permute-done.2.theirs, bf16[2,256,256]{2,1,0:T(8,128)(2,1)S(1)} %collective-permute-done.14.theirs_own, ...), custom_call_target="tpu_custom_call" | custom-call | tf_op jit(solution)/shard_map/pallas_call | solution.py:430
  34.8 1.0 %shard_map.119 = (f32[256,128]{1,0:T(8,128)}, f32[1,256,128]{2,1,0:T(8,128)}) custom-call(bf16[2,512,256]{2,1,0:T(8,128)(2,1)S(1)} %get-tuple-element.28.mine_chip, bf16[2,1056,256]{2,1,0:T(8,128)(2,1)S(1)} %collective-permute-done.2.theirs, bf16[128,256]{1,0:T(8,128)(2,1)S(1)} %collective-permute-done.13.high, f32[128,256]{1,0:T(8,128)S(1)} %get-tuple-element.48.my_part, ...), custom_call_target="tpu_custom_call" | custom-call | tf_op jit(solution)/shard_map/pallas_call | solution.py:580
  (30 shorter events, 3.2 us)
Async XLA Ops:
  0.6 1.7 %collective-permute-start = (f32[256,128]{1,0:T(8,128)}, f32[256,128]{1,0:T(8,128)S(1)}, u32[]{:S(2)}, u32[]{:S(2)}) collective-permute-start(f32[256,128]{1,0:T(8,128)} %tgt_own_hbm.1), channel_id=1, source_target_pairs={{0,1},{1,0},{2,3},{3,2},{4,5},{5,4},{6,7},{7,6},{8,9},{9,8},{10,11... | collective-permute-start | bytes 393224 | tf_op jit(solution)/shard_map/ppermute | solution.py:433
  1.1 1.6 %collective-permute-start.1 = (f32[1,256,128]{2,1,0:T(8,128)}, f32[1,256,128]{2,1,0:T(8,128)S(1)}, u32[]{:S(2)}, u32[]{:S(2)}) collective-permute-start(f32[1,256,128]{2,1,0:T(8,128)} %proj_own_hbm.1), channel_id=1, source_target_pairs={{0,1},{1,0},{2,3},{3,2},{4,5},{5,4},{6,7},{7,6},{8,9},{9,8},{10,11... | collective-permute-start | bytes 393224 | tf_op jit(solution)/shard_map/ppermute | solution.py:433
  2.8 8.1 %collective-permute-start.3 = (bf16[2,128,256]{2,1,0:T(8,128)(2,1)S(1)}, bf16[2,128,256]{2,1,0:T(8,128)(2,1)S(1)}, u32[]{:S(2)}, u32[]{:S(2)}) collective-permute-start(bf16[2,128,256]{2,1,0:T(8,128)(2,1)S(1)} %get-tuple-element.36), channel_id=1, source_target_pairs={{1,2},{0,9},{2,1},{3,10},{4,7},{5,12},{7,4},{6,15},{8,11},{9,0},{1... | collective-permute-start | bytes 393224 | tf_op jit(solution)/shard_map/ppermute | solution.py:451
  7.9 2.8 %collective-permute-start.2 = (bf16[2,1056,256]{2,1,0:T(8,128)(2,1)S(1)}, bf16[2,1056,256]{2,1,0:T(8,128)(2,1)S(1)}, u32[]{:S(2)}, u32[]{:S(2)}) collective-permute-start(bf16[2,1056,256]{2,1,0:T(8,128)(2,1)S(1)} %get-tuple-element.30.sent), channel_id=1, source_target_pairs={{0,1},{1,0},{2,3},{3,2},{4,5},{5,4},{6,7},{7,6},{8,9},{9,8},{10,11... | collective-permute-start | bytes 3244040 | tf_op jit(solution)/shard_map/ppermute | solution.py:433
  11.3 3.9 %collective-permute-start.4 = (bf16[128,256]{1,0:T(8,128)(2,1)S(1)}, bf16[128,256]{1,0:T(8,128)(2,1)S(1)}, u32[]{:S(2)}, u32[]{:S(2)}) collective-permute-start(bf16[128,256]{1,0:T(8,128)(2,1)S(1)} %get-tuple-element.40.own), channel_id=1, source_target_pairs={{1,8},{0,5},{2,11},{3,6},{4,13},{5,0},{7,14},{6,3},{8,1},{9,12},{1... | collective-permute-start | bytes 196616 | tf_op jit(solution)/shard_map/ppermute | solution.py:451
  12.7 4.7 %collective-permute-start.8 = (bf16[128,256]{1,0:T(8,128)(2,1)S(1)}, bf16[128,256]{1,0:T(8,128)(2,1)S(1)}, u32[]{:S(2)}, u32[]{:S(2)}) collective-permute-start(bf16[128,256]{1,0:T(8,128)(2,1)S(1)} %get-tuple-element.42.own), channel_id=1, source_target_pairs={{1,8},{0,5},{2,11},{3,6},{4,13},{5,0},{7,14},{6,3},{8,1},{9,12},{1... | collective-permute-start | bytes 196616 | tf_op jit(solution)/shard_map/ppermute | solution.py:451
  13.1 5.9 %collective-permute-start.7 = (f32[2,1,256]{2,1,0:T(1,128)S(1)}, f32[2,1,256]{2,1,0:T(1,128)S(1)}, u32[]{:S(2)}, u32[]{:S(2)}) collective-permute-start(f32[2,1,256]{2,1,0:T(1,128)S(1)} %get-tuple-element.41.energies), channel_id=1, source_target_pairs={{1,2},{0,9},{2,1},{3,10},{4,7},{5,12},{7,4},{6,15},{8,11},{9,0},{1... | collective-permute-start | bytes 6152 | tf_op jit(solution)/shard_map/ppermute | solution.py:451
  15.2 4.9 %collective-permute-start.6 = (bf16[128,256]{1,0:T(8,128)(2,1)S(1)}, bf16[128,256]{1,0:T(8,128)(2,1)S(1)}, u32[]{:S(2)}, u32[]{:S(2)}) collective-permute-start(bf16[128,256]{1,0:T(8,128)(2,1)S(1)} %shard_map.110), channel_id=1, source_target_pairs={{1,5},{0,2},{2,6},{3,1},{4,0},{5,7},{7,3},{6,4},{8,12},{9,11},{11,... | collective-permute-start | bytes 196616 | tf_op jit(solution)/shard_map/ppermute | solution.py:451
  17.4 2.7 %collective-permute-start.5 = (bf16[128,256]{1,0:T(8,128)(2,1)S(1)}, bf16[128,256]{1,0:T(8,128)(2,1)S(1)}, u32[]{:S(2)}, u32[]{:S(2)}) collective-permute-start(bf16[128,256]{1,0:T(8,128)(2,1)S(1)} %shard_map.110), channel_id=1, source_target_pairs={{0,1},{1,0},{2,3},{3,2},{4,5},{5,4},{6,7},{7,6},{8,9},{9,8},{10,11... | collective-permute-start | bytes 196616 | tf_op jit(solution)/shard_map/ppermute | solution.py:433
  17.5 4.3 %collective-permute-start.10 = (bf16[128,256]{1,0:T(8,128)(2,1)S(1)}, bf16[128,256]{1,0:T(8,128)(2,1)S(1)}, u32[]{:S(2)}, u32[]{:S(2)}) collective-permute-start(bf16[128,256]{1,0:T(8,128)(2,1)S(1)} %shard_map.112), channel_id=1, source_target_pairs={{1,5},{0,2},{2,6},{3,1},{4,0},{5,7},{7,3},{6,4},{8,12},{9,11},{11,... | collective-permute-start | bytes 196616 | tf_op jit(solution)/shard_map/ppermute | solution.py:451
  18.7 3.1 %collective-permute-start.9 = (bf16[128,256]{1,0:T(8,128)(2,1)S(1)}, bf16[128,256]{1,0:T(8,128)(2,1)S(1)}, u32[]{:S(2)}, u32[]{:S(2)}) collective-permute-start(bf16[128,256]{1,0:T(8,128)(2,1)S(1)} %shard_map.112), channel_id=1, source_target_pairs={{0,1},{1,0},{2,3},{3,2},{4,5},{5,4},{6,7},{7,6},{8,9},{9,8},{10,11... | collective-permute-start | bytes 196616 | tf_op jit(solution)/shard_map/ppermute | solution.py:433
  19.1 14.9 %collective-permute-start.14 = (bf16[2,256,256]{2,1,0:T(8,128)(2,1)S(1)}, bf16[2,256,256]{2,1,0:T(8,128)(2,1)S(1)}, u32[]{:S(2)}, u32[]{:S(2)}) collective-permute-start(bf16[2,256,256]{2,1,0:T(8,128)(2,1)S(1)} %get-tuple-element.44), channel_id=1, source_target_pairs={{0,1},{1,0},{2,3},{3,2},{4,5},{5,4},{6,7},{7,6},{8,9},{9,8},{10,11... | collective-permute-start | bytes 786440 | tf_op jit(solution)/shard_map/ppermute | solution.py:433
  22.6 3.8 %collective-permute-start.15 = (bf16[128,256]{1,0:T(8,128)(2,1)S(1)}, bf16[128,256]{1,0:T(8,128)(2,1)S(1)}, u32[]{:S(2)}, u32[]{:S(2)}) collective-permute-start(bf16[128,256]{1,0:T(8,128)(2,1)S(1)} %get-tuple-element.45.own), channel_id=1, source_target_pairs={{1,8},{0,5},{2,11},{3,6},{4,13},{5,0},{7,14},{6,3},{8,1},{9,12},{1... | collective-permute-start | bytes 196616 | tf_op jit(solution)/shard_map/ppermute | solution.py:451
  22.9 4.9 %collective-permute-start.11 = (bf16[128,256]{1,0:T(8,128)(2,1)S(1)}, bf16[128,256]{1,0:T(8,128)(2,1)S(1)}, u32[]{:S(2)}, u32[]{:S(2)}) collective-permute-start(bf16[128,256]{1,0:T(8,128)(2,1)S(1)} %get-tuple-element.43.own), channel_id=1, source_target_pairs={{1,8},{0,5},{2,11},{3,6},{4,13},{5,0},{7,14},{6,3},{8,1},{9,12},{1... | collective-permute-start | bytes 196616 | tf_op jit(solution)/shard_map/ppermute | solution.py:451
  24.5 9.5 %collective-permute-start.18 = (f32[128,256]{1,0:T(8,128)S(1)}, f32[128,256]{1,0:T(8,128)S(1)}, u32[]{:S(2)}, u32[]{:S(2)}) collective-permute-start(f32[128,256]{1,0:T(8,128)S(1)} %get-tuple-element.47), channel_id=1, source_target_pairs={{0,1},{1,0},{2,3},{3,2},{4,5},{5,4},{6,7},{7,6},{8,9},{9,8},{10,11... | collective-permute-start | bytes 393224 | tf_op jit(solution)/shard_map/ppermute | solution.py:433
  26.4 3.8 %collective-permute-start.16 = (bf16[128,256]{1,0:T(8,128)(2,1)S(1)}, bf16[128,256]{1,0:T(8,128)(2,1)S(1)}, u32[]{:S(2)}, u32[]{:S(2)}) collective-permute-start(bf16[128,256]{1,0:T(8,128)(2,1)S(1)} %shard_map.116.own), channel_id=1, source_target_pairs={{1,4},{0,3},{2,7},{3,0},{4,1},{5,6},{7,2},{6,5},{8,13},{9,10},{11,... | collective-permute-start | bytes 196616 | tf_op jit(solution)/shard_map/ppermute | solution.py:451
  27.8 4.0 %collective-permute-start.12 = (bf16[128,256]{1,0:T(8,128)(2,1)S(1)}, bf16[128,256]{1,0:T(8,128)(2,1)S(1)}, u32[]{:S(2)}, u32[]{:S(2)}) collective-permute-start(bf16[128,256]{1,0:T(8,128)(2,1)S(1)} %shard_map.114.own), channel_id=1, source_target_pairs={{1,4},{0,3},{2,7},{3,0},{4,1},{5,6},{7,2},{6,5},{8,13},{9,10},{11,... | collective-permute-start | bytes 196616 | tf_op jit(solution)/shard_map/ppermute | solution.py:451
  30.2 3.7 %collective-permute-start.17 = (bf16[128,256]{1,0:T(8,128)(2,1)S(1)}, bf16[128,256]{1,0:T(8,128)(2,1)S(1)}, u32[]{:S(2)}, u32[]{:S(2)}) collective-permute-start(bf16[128,256]{1,0:T(8,128)(2,1)S(1)} %shard_map.117.low), channel_id=1, source_target_pairs={{0,1},{1,0},{2,3},{3,2},{4,5},{5,4},{6,7},{7,6},{8,9},{9,8},{10,11... | collective-permute-start | bytes 196616 | tf_op jit(solution)/shard_map/ppermute | solution.py:433
  31.8 3.0 %collective-permute-start.13 = (bf16[128,256]{1,0:T(8,128)(2,1)S(1)}, bf16[128,256]{1,0:T(8,128)(2,1)S(1)}, u32[]{:S(2)}, u32[]{:S(2)}) collective-permute-start(bf16[128,256]{1,0:T(8,128)(2,1)S(1)} %shard_map.115.high), channel_id=1, source_target_pairs={{0,1},{1,0},{2,3},{3,2},{4,5},{5,4},{6,7},{7,6},{8,9},{9,8},{10,11... | collective-permute-start | bytes 196616 | tf_op jit(solution)/shard_map/ppermute | solution.py:433

commit v31 on v24

--- a/solution.py
+++ b/solution.py
@@ -114,44 +114,41 @@
     return copies
 
 
-def load_kernel(
-    tgt_energy_hbm,
-    proj_energy_hbm,
-    tgt_own_hbm,
-    proj_own_hbm,
-    energy,
-    amp_ref,
-    flat_energy,
-    tgt_own,
-    proj_own,
-    sems,
-):
-    pairs = [
-        (tgt_own_hbm, tgt_own),
-        (proj_own_hbm, proj_own),
-        (tgt_energy_hbm, flat_energy),
-        (proj_energy_hbm, energy.at[1]),
-    ]
+def load_kernel(tgt_own_hbm, proj_own_hbm, amp_ref, tgt_own, proj_own, sems):
+    pairs = [(tgt_own_hbm, tgt_own), (proj_own_hbm, proj_own)]
     copies = [pltpu.make_async_copy(src, dst, sems.at[k]) for k, (src, dst) in enumerate(pairs)]
     for copy in copies:
         copy.start()
     for copy in copies:
         copy.wait()
-    energy[0] = flat_energy[...][None, :]
     amp_ref[0] = tgt_own[...].T
     amp_ref[1] = proj_own[0].T
 
 
 def pack_kernel(amp_ref, tgt_other, proj_other, chip_amp, message):
     my = my_kind()
-    other_amp, _ = ordered(my, tgt_other[...].T, proj_other[0].T)
+    other_amp = jnp.where(my == 0, tgt_other[...], proj_other[0]).T
     amps = ordered(lax.axis_index("rep"), amp_ref[my], other_amp)
     for segment in range(2):
         chip_amp[segment] = amps[segment]
         message[segment] = bf16(amps[segment])
 
 
-def sent_kernel(neighbours, weight_hbm, tgt_hbm, proj_hbm, chip_amp, energy, sent, weight, flat_weight, sems):
+def sent_kernel(
+    neighbours,
+    weight_hbm,
+    tgt_energy_hbm,
+    proj_energy_hbm,
+    tgt_hbm,
+    proj_hbm,
+    chip_amp,
+    sent,
+    weight,
+    energy,
+    flat_weight,
+    flat_energy,
+    sems,
+):
     my = my_kind()
     sources = (tgt_hbm, proj_hbm)
     rows = chip_amp.shape[2]
@@ -159,8 +156,10 @@
     def copies_of(kind):
         return basis_copies(both(sent, rows), sems, 1 - kind, neighbours, sources)
 
-    weight_copy = pltpu.make_async_copy(weight_hbm, flat_weight, sems.at[4])
-    weight_copy.start()
+    pairs = [(weight_hbm, flat_weight), (tgt_energy_hbm, flat_energy), (proj_energy_hbm, energy.at[1])]
+    rows_copies = [pltpu.make_async_copy(src, dst, sems.at[4 + k]) for k, (src, dst) in enumerate(pairs)]
+    for copy in rows_copies:
+        copy.start()
     for kind in range(2):
 
         @pl.when(my == kind)
@@ -168,8 +167,10 @@
             for copy in copies_of(kind):
                 copy.start()
 
-    weight_copy.wait()
+    for copy in rows_copies:
+        copy.wait()
     weight[0] = flat_weight[...][None, :]
+    energy[0] = flat_energy[...][None, :]
     for part in range(2):
         sent[part, 4 * rows : 4 * rows + PIECES] = split(weight[0])
         sent[part, 4 * rows + PIECES :, :rows] = split(energy[1 - my])
@@ -470,20 +471,19 @@
         return [pltpu.with_memory_space_constraint(block, pltpu.HBM) for block in blocks]
 
     others = swapped([tgt_amp, proj_amp])
-    energy, amp = call(
+    (amp,) = call(
         load_kernel,
-        [in_vmem((2, 1, rows), jnp.float32), in_vmem((2, two_cols, rows), jnp.float32)],
-        [HBM] * 4,
+        [in_vmem((2, two_cols, rows), jnp.float32)],
+        [HBM] * 2,
         [
-            pltpu.VMEM((rows,), jnp.float32),
             pltpu.VMEM(tgt_amp.shape, jnp.float32),
             pltpu.VMEM(proj_amp.shape, jnp.float32),
-            pltpu.SemaphoreType.DMA((4,)),
+            pltpu.SemaphoreType.DMA((2,)),
         ],
         pl.CostEstimate(
             flops=2 * 4 * rows * two_cols * points, bytes_accessed=4 * 1024 * 1024, transcendentals=0
         ),
-    )(*in_hbm(tgt_energy, proj_energy, tgt_amp, proj_amp))
+    )(*in_hbm(tgt_amp, proj_amp))
     chip_amp, message = run(
         pack_kernel,
         [in_vmem((2, two_cols, rows), jnp.float32), in_vmem((2, two_cols, rows), jnp.bfloat16)],
@@ -494,15 +494,20 @@
     flags, counts = pair_flags.T, tile_counts.T
     bases = in_hbm(tgt_basis.reshape(2, -1, rows, points), proj_basis)
     pair = in_vmem((2, 2 * rows, points), jnp.bfloat16)
-    sent, weight = call(
+    sent, weight, energy = call(
         functools.partial(sent_kernel, neighbours),
         [
             in_vmem((2, 4 * rows + 2 * PIECES, points), jnp.bfloat16),
             in_vmem((1, 1, points), jnp.float32),
+            in_vmem((2, 1, rows), jnp.float32),
         ],
-        [HBM] * 3 + [VMEM] * 2,
-        [pltpu.VMEM((points,), jnp.float32), pltpu.SemaphoreType.DMA((5,))],
-    )(*in_hbm(quad_weight), *bases, chip_amp, energy)
+        [HBM] * 5 + [VMEM],
+        [
+            pltpu.VMEM((points,), jnp.float32),
+            pltpu.VMEM((rows,), jnp.float32),
+            pltpu.SemaphoreType.DMA((7,)),
+        ],
+    )(*in_hbm(quad_weight, tgt_energy, proj_energy), *bases, chip_amp)
     mine_chip, mine_far, send_own, gate = call(
         functools.partial(side_kernel, gate_levels, neighbours),
         [

time: 35.5 us -> 35.6 us (level)
  transfers between devices with their start and end apart: 19 -> 19, of which waited for: 11 -> 10; matrix products, arithmetic and copies ran while one was open for 0% -> 0% of each run, Pallas kernels for 17% -> 17%
where the time goes in v31:
time: 35.6 us; the launch traced here: 35.4 us
  starting transfers between devices  18.2 us (51%)
  waiting for transfers between devices  9.05 us (25%)
  Pallas kernels  7.36 us (21%)
  between operations  0.76 us (2%)
    ppermute x10, starting transfers between devices, exchanged(): return lax.ppermute(block, DEVICES, pairs)  14.9 us
    ppermute x10, waiting for transfers between devices, exchanged(): return lax.ppermute(block, DEVICES, pairs)  6.98 us
    ppermute x9, starting transfers between devices, other_core(): return lax.ppermute(block, 'rep', [(0, 1), (1, 0)])  3.36 us
    pallas_call x12, Pallas kernels, run(): return call(kernel, out_shape, [VMEM] * len(blocks))(*blocks)  2.72 us
    ppermute x9, waiting for transfers between devices, other_core(): return lax.ppermute(block, 'rep', [(0, 1), (1, 0)])  2.07 us
    pallas_call x1, Pallas kernels, shards(): call(functools.partial(sent_kernel, neighbours), [in_vmem((2, 4 * rows +...  1.29 us
    pallas_call x1, Pallas kernels, shards(): call(functools.partial(side_kernel, gate_levels, neighbours), [pair, pair...  1.26 us
    pallas_call x1, Pallas kernels, shards(): call(load_kernel, [in_vmem((2, two_cols, rows), jnp.float32)], [HBM] * 2,...  1.12 us
  transfers between devices with their start and end apart: 19, of which 10 were waited for; matrix products, arithmetic and copies ran while one was open for 0% of the time, Pallas kernels for 17%

profile of v31, /device:TPU:0, one launch (start us, length us, event | category | flops | bytes accessed | tf_op | source)
XLA Modules:
  0.0 35.4 jit_solution(14312373335543059455)
XLA Ops:
  0.6 0.5 %collective-permute-start = (f32[256,128]{1,0:T(8,128)}, f32[256,128]{1,0:T(8,128)S(1)}, u32[]{:S(2)}, u32[]{:S(2)}) collective-permute-start(f32[256,128]{1,0:T(8,128)} %tgt_own_hbm.1), channel_id=1, source_target_pairs={{0,1},{1,0},{2,3},{3,2},{4,5},{5,4},{6,7},{7,6},{8,9},{9,8},{10,11... | collective-permute-start | bytes 393224 | tf_op jit(solution)/shard_map/ppermute | solution.py:434
  1.2 1.1 %shard_map.104.amp_ref = f32[2,128,256]{2,1,0:T(8,128)S(1)} custom-call(f32[256,128]{1,0:T(8,128)} %tgt_own_hbm.1, f32[1,256,128]{2,1,0:T(8,128)} %proj_own_hbm.1), custom_call_target="tpu_custom_call" | custom-call | flops 67108864 | bytes 4194304 | tf_op jit(solution)/shard_map/pallas_call | solution.py:474
  2.8 2.7 %collective-permute-start.3 = (bf16[2,128,256]{2,1,0:T(8,128)(2,1)S(1)}, bf16[2,128,256]{2,1,0:T(8,128)(2,1)S(1)}, u32[]{:S(2)}, u32[]{:S(2)}) collective-permute-start(bf16[2,128,256]{2,1,0:T(8,128)(2,1)S(1)} %get-tuple-element.34), channel_id=1, source_target_pairs={{0,3},{1,8},{3,0},{2,11},{5,6},{4,13},{6,5},{7,14},{9,10},{8,1},{1... | collective-permute-start | bytes 393224 | tf_op jit(solution)/shard_map/ppermute | solution.py:452
  5.5 1.3 %shard_map.107 = (bf16[2,1056,256]{2,1,0:T(8,128)(2,1)S(1)}, f32[1,1,256]{2,1,0:T(1,128)S(1)}, f32[2,1,256]{2,1,0:T(1,128)S(1)}) custom-call(f32[256]{0:T(256)} %weight_hbm.1, f32[256]{0:T(256)} %tgt_energy_hbm.1, f32[1,256]{1,0:T(1,128)} %proj_energy_hbm.1, bf16[2,4,256,256]{3,2,1,0:T(8,128)(2,1)} %bitcast.3, bf16[2,8,256,256]{3,2,1,0:T(8,128)(2,1)} %proj_hbm.3, ...), custom_call_target="tpu_custom_call" | custom-call | tf_op jit(solution)/shard_map/pallas_call | solution.py:497
  6.8 1.4 %collective-permute-start.2 = (bf16[2,1056,256]{2,1,0:T(8,128)(2,1)S(1)}, bf16[2,1056,256]{2,1,0:T(8,128)(2,1)S(1)}, u32[]{:S(2)}, u32[]{:S(2)}) collective-permute-start(bf16[2,1056,256]{2,1,0:T(8,128)(2,1)S(1)} %get-tuple-element.27.sent), channel_id=1, source_target_pairs={{0,1},{1,0},{2,3},{3,2},{4,5},{5,4},{6,7},{7,6},{8,9},{9,8},{10,11... | collective-permute-start | bytes 3244040 | tf_op jit(solution)/shard_map/ppermute | solution.py:434
  8.1 1.3 %shard_map.106 = (bf16[2,512,256]{2,1,0:T(8,128)(2,1)S(1)}, bf16[2,512,256]{2,1,0:T(8,128)(2,1)S(1)}, bf16[2,256,256]{2,1,0:T(8,128)(2,1)S(1)}, f32[3,2,1,256]{3,2,1,0:T(1,128)S(1)}) custom-call(s32[2,4]{1,0:T(2,128)} %bitcast.5, s32[2,4]{1,0:T(2,128)} %bitcast.6, bf16[2,4,256,256]{3,2,1,0:T(8,128)(2,1)} %bitcast.4, bf16[2,8,256,256]{3,2,1,0:T(8,128)(2,1)} %proj_hbm.3, ...), custom_call_target="tpu_custom_call" | custom-call | flops 34359738368 | bytes 65536 | tf_op jit(solution)/shard_map/pallas_call | solution.py:511
  9.4 1.1 %collective-permute-done.2.theirs = bf16[2,1056,256]{2,1,0:T(8,128)(2,1)S(1)} collective-permute-done((bf16[2,1056,256]{2,1,0:T(8,128)(2,1)S(1)}, bf16[2,1056,256]{2,1,0:T(8,128)(2,1)S(1)}, u32[]{:S(2)}, u32[]{:S(2)}) %collective-permute-start.2) | collective-permute-done | bytes 1081376 | tf_op jit(solution)/shard_map/ppermute | solution.py:434
  11.1 1.5 %collective-permute-start.4 = (bf16[128,256]{1,0:T(8,128)(2,1)S(1)}, bf16[128,256]{1,0:T(8,128)(2,1)S(1)}, u32[]{:S(2)}, u32[]{:S(2)}) collective-permute-start(bf16[128,256]{1,0:T(8,128)(2,1)S(1)} %get-tuple-element.38.own), channel_id=1, source_target_pairs={{0,9},{1,4},{3,10},{2,7},{5,12},{4,1},{6,15},{7,2},{9,0},{8,13},{1... | collective-permute-start | bytes 196616 | tf_op jit(solution)/shard_map/ppermute | solution.py:452
  12.7 1.2 %collective-permute-start.8 = (bf16[128,256]{1,0:T(8,128)(2,1)S(1)}, bf16[128,256]{1,0:T(8,128)(2,1)S(1)}, u32[]{:S(2)}, u32[]{:S(2)}) collective-permute-start(bf16[128,256]{1,0:T(8,128)(2,1)S(1)} %get-tuple-element.40.own), channel_id=1, source_target_pairs={{0,9},{1,4},{3,10},{2,7},{5,12},{4,1},{6,15},{7,2},{9,0},{8,13},{1... | collective-permute-start | bytes 196616 | tf_op jit(solution)/shard_map/ppermute | solution.py:452
  13.9 1.4 %collective-permute-start.7 = (f32[2,1,256]{2,1,0:T(1,128)S(1)}, f32[2,1,256]{2,1,0:T(1,128)S(1)}, u32[]{:S(2)}, u32[]{:S(2)}) collective-permute-start(f32[2,1,256]{2,1,0:T(1,128)S(1)} %get-tuple-element.39.energies), channel_id=1, source_target_pairs={{0,3},{1,8},{3,0},{2,11},{5,6},{4,13},{6,5},{7,14},{9,10},{8,1},{1... | collective-permute-start | bytes 6152 | tf_op jit(solution)/shard_map/ppermute | solution.py:452
  15.3 0.6 %collective-permute-done.4.other = bf16[128,256]{1,0:T(8,128)(2,1)S(1)} collective-permute-done((bf16[128,256]{1,0:T(8,128)(2,1)S(1)}, bf16[128,256]{1,0:T(8,128)(2,1)S(1)}, u32[]{:S(2)}, u32[]{:S(2)}) %collective-permute-start.4) | collective-permute-done | bytes 65568 | tf_op jit(solution)/shard_map/ppermute | solution.py:452
  15.9 1.2 %collective-permute-start.6 = (bf16[128,256]{1,0:T(8,128)(2,1)S(1)}, bf16[128,256]{1,0:T(8,128)(2,1)S(1)}, u32[]{:S(2)}, u32[]{:S(2)}) collective-permute-start(bf16[128,256]{1,0:T(8,128)(2,1)S(1)} %shard_map.110), channel_id=1, source_target_pairs={{0,4},{1,3},{3,7},{2,0},{5,1},{4,6},{6,2},{7,5},{9,13},{8,10},{10,... | collective-permute-start | bytes 196616 | tf_op jit(solution)/shard_map/ppermute | solution.py:452
  17.2 0.6 %collective-permute-start.5 = (bf16[128,256]{1,0:T(8,128)(2,1)S(1)}, bf16[128,256]{1,0:T(8,128)(2,1)S(1)}, u32[]{:S(2)}, u32[]{:S(2)}) collective-permute-start(bf16[128,256]{1,0:T(8,128)(2,1)S(1)} %shard_map.110), channel_id=1, source_target_pairs={{0,1},{1,0},{2,3},{3,2},{4,5},{5,4},{6,7},{7,6},{8,9},{9,8},{10,11... | collective-permute-start | bytes 196616 | tf_op jit(solution)/shard_map/ppermute | solution.py:434
  18.0 1.5 %collective-permute-start.10 = (bf16[128,256]{1,0:T(8,128)(2,1)S(1)}, bf16[128,256]{1,0:T(8,128)(2,1)S(1)}, u32[]{:S(2)}, u32[]{:S(2)}) collective-permute-start(bf16[128,256]{1,0:T(8,128)(2,1)S(1)} %shard_map.112), channel_id=1, source_target_pairs={{0,4},{1,3},{3,7},{2,0},{5,1},{4,6},{6,2},{7,5},{9,13},{8,10},{10,... | collective-permute-start | bytes 196616 | tf_op jit(solution)/shard_map/ppermute | solution.py:452
  20.8 1.6 %collective-permute-done.10.high_there = bf16[128,256]{1,0:T(8,128)(2,1)S(1)} collective-permute-done((bf16[128,256]{1,0:T(8,128)(2,1)S(1)}, bf16[128,256]{1,0:T(8,128)(2,1)S(1)}, u32[]{:S(2)}, u32[]{:S(2)}) %collective-permute-start.10) | collective-permute-done | bytes 65568 | tf_op jit(solution)/shard_map/ppermute | solution.py:452
  22.3 0.8 %shard_map.113 = (bf16[128,256]{1,0:T(8,128)(2,1)S(1)}, bf16[128,256]{1,0:T(8,128)(2,1)S(1)}, f32[128,256]{1,0:T(8,128)S(1)}, f32[128,256]{1,0:T(8,128)S(1)}) custom-call(bf16[2,512,256]{2,1,0:T(8,128)(2,1)S(1)} %get-tuple-element.26.mine_chip, bf16[2,512,256]{2,1,0:T(8,128)(2,1)S(1)} %get-tuple-element.29.mine_far, ...), custom_call_target="tpu_custom_call" | custom-call | tf_op jit(solution)/shard_map/pallas_call | solution.py:431
  23.4 2.5 %collective-permute-start.11 = (bf16[128,256]{1,0:T(8,128)(2,1)S(1)}, bf16[128,256]{1,0:T(8,128)(2,1)S(1)}, u32[]{:S(2)}, u32[]{:S(2)}) collective-permute-start(bf16[128,256]{1,0:T(8,128)(2,1)S(1)} %get-tuple-element.41.own), channel_id=1, source_target_pairs={{0,9},{1,4},{3,10},{2,7},{5,12},{4,1},{6,15},{7,2},{9,0},{8,13},{1... | collective-permute-start | bytes 196616 | tf_op jit(solution)/shard_map/ppermute | solution.py:452
  25.9 1.9 %collective-permute-done.15.other = bf16[128,256]{1,0:T(8,128)(2,1)S(1)} collective-permute-done((bf16[128,256]{1,0:T(8,128)(2,1)S(1)}, bf16[128,256]{1,0:T(8,128)(2,1)S(1)}, u32[]{:S(2)}, u32[]{:S(2)}) %collective-permute-start.15) | collective-permute-done | bytes 65568 | tf_op jit(solution)/shard_map/ppermute | solution.py:452
  27.9 1.4 %collective-permute-start.16 = (bf16[128,256]{1,0:T(8,128)(2,1)S(1)}, bf16[128,256]{1,0:T(8,128)(2,1)S(1)}, u32[]{:S(2)}, u32[]{:S(2)}) collective-permute-start(bf16[128,256]{1,0:T(8,128)(2,1)S(1)} %shard_map.116.own), channel_id=1, source_target_pairs={{0,5},{1,2},{3,6},{2,1},{5,0},{4,7},{6,3},{7,4},{9,12},{8,11},{10,... | collective-permute-start | bytes 196616 | tf_op jit(solution)/shard_map/ppermute | solution.py:452
  29.3 1.2 %collective-permute-start.12 = (bf16[128,256]{1,0:T(8,128)(2,1)S(1)}, bf16[128,256]{1,0:T(8,128)(2,1)S(1)}, u32[]{:S(2)}, u32[]{:S(2)}) collective-permute-start(bf16[128,256]{1,0:T(8,128)(2,1)S(1)} %shard_map.114.own), channel_id=1, source_target_pairs={{0,5},{1,2},{3,6},{2,1},{5,0},{4,7},{6,3},{7,4},{9,12},{8,11},{10,... | collective-permute-start | bytes 196616 | tf_op jit(solution)/shard_map/ppermute | solution.py:452
  30.6 1.1 %collective-permute-done.16.other = bf16[128,256]{1,0:T(8,128)(2,1)S(1)} collective-permute-done((bf16[128,256]{1,0:T(8,128)(2,1)S(1)}, bf16[128,256]{1,0:T(8,128)(2,1)S(1)}, u32[]{:S(2)}, u32[]{:S(2)}) %collective-permute-start.16) | collective-permute-done | bytes 65568 | tf_op jit(solution)/shard_map/ppermute | solution.py:452
  31.7 1.3 %collective-permute-done.12.other = bf16[128,256]{1,0:T(8,128)(2,1)S(1)} collective-permute-done((bf16[128,256]{1,0:T(8,128)(2,1)S(1)}, bf16[128,256]{1,0:T(8,128)(2,1)S(1)}, u32[]{:S(2)}, u32[]{:S(2)}) %collective-permute-start.12) | collective-permute-done | bytes 65568 | tf_op jit(solution)/shard_map/ppermute | solution.py:452
  33.8 0.6 %collective-permute-done.13.high = bf16[128,256]{1,0:T(8,128)(2,1)S(1)} collective-permute-done((bf16[128,256]{1,0:T(8,128)(2,1)S(1)}, bf16[128,256]{1,0:T(8,128)(2,1)S(1)}, u32[]{:S(2)}, u32[]{:S(2)}) %collective-permute-start.13) | collective-permute-done | bytes 65568 | tf_op jit(solution)/shard_map/ppermute | solution.py:434
  34.4 1.0 %shard_map.119 = (f32[256,128]{1,0:T(8,128)}, f32[1,256,128]{2,1,0:T(8,128)}) custom-call(bf16[2,512,256]{2,1,0:T(8,128)(2,1)S(1)} %get-tuple-element.26.mine_chip, bf16[2,1056,256]{2,1,0:T(8,128)(2,1)S(1)} %collective-permute-done.2.theirs, bf16[128,256]{1,0:T(8,128)(2,1)S(1)} %collective-permute-done.13.high, f32[128,256]{1,0:T(8,128)S(1)} %get-tuple-element.46.my_part, ...), custom_call_target="tpu_custom_call" | custom-call | tf_op jit(solution)/shard_map/pallas_call | solution.py:585
  (30 shorter events, 3.8 us)
Async XLA Ops:
  0.6 1.7 %collective-permute-start = (f32[256,128]{1,0:T(8,128)}, f32[256,128]{1,0:T(8,128)S(1)}, u32[]{:S(2)}, u32[]{:S(2)}) collective-permute-start(f32[256,128]{1,0:T(8,128)} %tgt_own_hbm.1), channel_id=1, source_target_pairs={{0,1},{1,0},{2,3},{3,2},{4,5},{5,4},{6,7},{7,6},{8,9},{9,8},{10,11... | collective-permute-start | bytes 393224 | tf_op jit(solution)/shard_map/ppermute | solution.py:434
  1.1 1.6 %collective-permute-start.1 = (f32[1,256,128]{2,1,0:T(8,128)}, f32[1,256,128]{2,1,0:T(8,128)S(1)}, u32[]{:S(2)}, u32[]{:S(2)}) collective-permute-start(f32[1,256,128]{2,1,0:T(8,128)} %proj_own_hbm.1), channel_id=1, source_target_pairs={{0,1},{1,0},{2,3},{3,2},{4,5},{5,4},{6,7},{7,6},{8,9},{9,8},{10,11... | collective-permute-start | bytes 393224 | tf_op jit(solution)/shard_map/ppermute | solution.py:434
  2.8 8.0 %collective-permute-start.3 = (bf16[2,128,256]{2,1,0:T(8,128)(2,1)S(1)}, bf16[2,128,256]{2,1,0:T(8,128)(2,1)S(1)}, u32[]{:S(2)}, u32[]{:S(2)}) collective-permute-start(bf16[2,128,256]{2,1,0:T(8,128)(2,1)S(1)} %get-tuple-element.34), channel_id=1, source_target_pairs={{0,3},{1,8},{3,0},{2,11},{5,6},{4,13},{6,5},{7,14},{9,10},{8,1},{1... | collective-permute-start | bytes 393224 | tf_op jit(solution)/shard_map/ppermute | solution.py:452
  6.8 3.7 %collective-permute-start.2 = (bf16[2,1056,256]{2,1,0:T(8,128)(2,1)S(1)}, bf16[2,1056,256]{2,1,0:T(8,128)(2,1)S(1)}, u32[]{:S(2)}, u32[]{:S(2)}) collective-permute-start(bf16[2,1056,256]{2,1,0:T(8,128)(2,1)S(1)} %get-tuple-element.27.sent), channel_id=1, source_target_pairs={{0,1},{1,0},{2,3},{3,2},{4,5},{5,4},{6,7},{7,6},{8,9},{9,8},{10,11... | collective-permute-start | bytes 3244040 | tf_op jit(solution)/shard_map/ppermute | solution.py:434
  11.1 4.8 %collective-permute-start.4 = (bf16[128,256]{1,0:T(8,128)(2,1)S(1)}, bf16[128,256]{1,0:T(8,128)(2,1)S(1)}, u32[]{:S(2)}, u32[]{:S(2)}) collective-permute-start(bf16[128,256]{1,0:T(8,128)(2,1)S(1)} %get-tuple-element.38.own), channel_id=1, source_target_pairs={{0,9},{1,4},{3,10},{2,7},{5,12},{4,1},{6,15},{7,2},{9,0},{8,13},{1... | collective-permute-start | bytes 196616 | tf_op jit(solution)/shard_map/ppermute | solution.py:452
  12.7 5.3 %collective-permute-start.8 = (bf16[128,256]{1,0:T(8,128)(2,1)S(1)}, bf16[128,256]{1,0:T(8,128)(2,1)S(1)}, u32[]{:S(2)}, u32[]{:S(2)}) collective-permute-start(bf16[128,256]{1,0:T(8,128)(2,1)S(1)} %get-tuple-element.40.own), channel_id=1, source_target_pairs={{0,9},{1,4},{3,10},{2,7},{5,12},{4,1},{6,15},{7,2},{9,0},{8,13},{1... | collective-permute-start | bytes 196616 | tf_op jit(solution)/shard_map/ppermute | solution.py:452
  13.9 5.7 %collective-permute-start.7 = (f32[2,1,256]{2,1,0:T(1,128)S(1)}, f32[2,1,256]{2,1,0:T(1,128)S(1)}, u32[]{:S(2)}, u32[]{:S(2)}) collective-permute-start(f32[2,1,256]{2,1,0:T(1,128)S(1)} %get-tuple-element.39.energies), channel_id=1, source_target_pairs={{0,3},{1,8},{3,0},{2,11},{5,6},{4,13},{6,5},{7,14},{9,10},{8,1},{1... | collective-permute-start | bytes 6152 | tf_op jit(solution)/shard_map/ppermute | solution.py:452
  15.9 4.3 %collective-permute-start.6 = (bf16[128,256]{1,0:T(8,128)(2,1)S(1)}, bf16[128,256]{1,0:T(8,128)(2,1)S(1)}, u32[]{:S(2)}, u32[]{:S(2)}) collective-permute-start(bf16[128,256]{1,0:T(8,128)(2,1)S(1)} %shard_map.110), channel_id=1, source_target_pairs={{0,4},{1,3},{3,7},{2,0},{5,1},{4,6},{6,2},{7,5},{9,13},{8,10},{10,... | collective-permute-start | bytes 196616 | tf_op jit(solution)/shard_map/ppermute | solution.py:452
  17.2 3.1 %collective-permute-start.5 = (bf16[128,256]{1,0:T(8,128)(2,1)S(1)}, bf16[128,256]{1,0:T(8,128)(2,1)S(1)}, u32[]{:S(2)}, u32[]{:S(2)}) collective-permute-start(bf16[128,256]{1,0:T(8,128)(2,1)S(1)} %shard_map.110), channel_id=1, source_target_pairs={{0,1},{1,0},{2,3},{3,2},{4,5},{5,4},{6,7},{7,6},{8,9},{9,8},{10,11... | collective-permute-start | bytes 196616 | tf_op jit(solution)/shard_map/ppermute | solution.py:434
  18.0 4.3 %collective-permute-start.10 = (bf16[128,256]{1,0:T(8,128)(2,1)S(1)}, bf16[128,256]{1,0:T(8,128)(2,1)S(1)}, u32[]{:S(2)}, u32[]{:S(2)}) collective-permute-start(bf16[128,256]{1,0:T(8,128)(2,1)S(1)} %shard_map.112), channel_id=1, source_target_pairs={{0,4},{1,3},{3,7},{2,0},{5,1},{4,6},{6,2},{7,5},{9,13},{8,10},{10,... | collective-permute-start | bytes 196616 | tf_op jit(solution)/shard_map/ppermute | solution.py:452
  19.5 2.8 %collective-permute-start.9 = (bf16[128,256]{1,0:T(8,128)(2,1)S(1)}, bf16[128,256]{1,0:T(8,128)(2,1)S(1)}, u32[]{:S(2)}, u32[]{:S(2)}) collective-permute-start(bf16[128,256]{1,0:T(8,128)(2,1)S(1)} %shard_map.112), channel_id=1, source_target_pairs={{0,1},{1,0},{2,3},{3,2},{4,5},{5,4},{6,7},{7,6},{8,9},{9,8},{10,11... | collective-permute-start | bytes 196616 | tf_op jit(solution)/shard_map/ppermute | solution.py:434
  19.6 13.7 %collective-permute-start.14 = (bf16[2,256,256]{2,1,0:T(8,128)(2,1)S(1)}, bf16[2,256,256]{2,1,0:T(8,128)(2,1)S(1)}, u32[]{:S(2)}, u32[]{:S(2)}) collective-permute-start(bf16[2,256,256]{2,1,0:T(8,128)(2,1)S(1)} %get-tuple-element.42), channel_id=1, source_target_pairs={{0,1},{1,0},{2,3},{3,2},{4,5},{5,4},{6,7},{7,6},{8,9},{9,8},{10,11... | collective-permute-start | bytes 786440 | tf_op jit(solution)/shard_map/ppermute | solution.py:434
  23.2 4.7 %collective-permute-start.15 = (bf16[128,256]{1,0:T(8,128)(2,1)S(1)}, bf16[128,256]{1,0:T(8,128)(2,1)S(1)}, u32[]{:S(2)}, u32[]{:S(2)}) collective-permute-start(bf16[128,256]{1,0:T(8,128)(2,1)S(1)} %get-tuple-element.43.own), channel_id=1, source_target_pairs={{0,9},{1,4},{3,10},{2,7},{5,12},{4,1},{6,15},{7,2},{9,0},{8,13},{1... | collective-permute-start | bytes 196616 | tf_op jit(solution)/shard_map/ppermute | solution.py:452
  23.4 5.9 %collective-permute-start.11 = (bf16[128,256]{1,0:T(8,128)(2,1)S(1)}, bf16[128,256]{1,0:T(8,128)(2,1)S(1)}, u32[]{:S(2)}, u32[]{:S(2)}) collective-permute-start(bf16[128,256]{1,0:T(8,128)(2,1)S(1)} %get-tuple-element.41.own), channel_id=1, source_target_pairs={{0,9},{1,4},{3,10},{2,7},{5,12},{4,1},{6,15},{7,2},{9,0},{8,13},{1... | collective-permute-start | bytes 196616 | tf_op jit(solution)/shard_map/ppermute | solution.py:452
  25.9 7.4 %collective-permute-start.18 = (f32[128,256]{1,0:T(8,128)S(1)}, f32[128,256]{1,0:T(8,128)S(1)}, u32[]{:S(2)}, u32[]{:S(2)}) collective-permute-start(f32[128,256]{1,0:T(8,128)S(1)} %get-tuple-element.45), channel_id=1, source_target_pairs={{0,1},{1,0},{2,3},{3,2},{4,5},{5,4},{6,7},{7,6},{8,9},{9,8},{10,11... | collective-permute-start | bytes 393224 | tf_op jit(solution)/shard_map/ppermute | solution.py:434
  27.9 3.8 %collective-permute-start.16 = (bf16[128,256]{1,0:T(8,128)(2,1)S(1)}, bf16[128,256]{1,0:T(8,128)(2,1)S(1)}, u32[]{:S(2)}, u32[]{:S(2)}) collective-permute-start(bf16[128,256]{1,0:T(8,128)(2,1)S(1)} %shard_map.116.own), channel_id=1, source_target_pairs={{0,5},{1,2},{3,6},{2,1},{5,0},{4,7},{6,3},{7,4},{9,12},{8,11},{10,... | collective-permute-start | bytes 196616 | tf_op jit(solution)/shard_map/ppermute | solution.py:452
  29.3 3.8 %collective-permute-start.12 = (bf16[128,256]{1,0:T(8,128)(2,1)S(1)}, bf16[128,256]{1,0:T(8,128)(2,1)S(1)}, u32[]{:S(2)}, u32[]{:S(2)}) collective-permute-start(bf16[128,256]{1,0:T(8,128)(2,1)S(1)} %shard_map.114.own), channel_id=1, source_target_pairs={{0,5},{1,2},{3,6},{2,1},{5,0},{4,7},{6,3},{7,4},{9,12},{8,11},{10,... | collective-permute-start | bytes 196616 | tf_op jit(solution)/shard_map/ppermute | solution.py:452
  31.6 1.6 %collective-permute-start.17 = (bf16[128,256]{1,0:T(8,128)(2,1)S(1)}, bf16[128,256]{1,0:T(8,128)(2,1)S(1)}, u32[]{:S(2)}, u32[]{:S(2)}) collective-permute-start(bf16[128,256]{1,0:T(8,128)(2,1)S(1)} %shard_map.117.low), channel_id=1, source_target_pairs={{0,1},{1,0},{2,3},{3,2},{4,5},{5,4},{6,7},{7,6},{8,9},{9,8},{10,11... | collective-permute-start | bytes 196616 | tf_op jit(solution)/shard_map/ppermute | solution.py:434
  33.1 1.3 %collective-permute-start.13 = (bf16[128,256]{1,0:T(8,128)(2,1)S(1)}, bf16[128,256]{1,0:T(8,128)(2,1)S(1)}, u32[]{:S(2)}, u32[]{:S(2)}) collective-permute-start(bf16[128,256]{1,0:T(8,128)(2,1)S(1)} %shard_map.115.high), channel_id=1, source_target_pairs={{0,1},{1,0},{2,3},{3,2},{4,5},{5,4},{6,7},{7,6},{8,9},{9,8},{10,11... | collective-permute-start | bytes 196616 | tf_op jit(solution)/shard_map/ppermute | solution.py:434

commit v32 on v31

--- a/solution.py
+++ b/solution.py
@@ -76,6 +76,7 @@
 
 PIECES = 16
 
+EVEN = pl.CostEstimate(flops=1 << 32, bytes_accessed=1 << 16, transcendentals=0)
 BEHIND = pl.CostEstimate(flops=1 << 35, bytes_accessed=1 << 16, transcendentals=0)
 
 
@@ -265,7 +266,8 @@
     by_core(body)
 
 
-def add_kernel(level, half, gate, own, other, out_ref):
+def add_kernel(level, half, gate, own, other, *rest):
+    out_ref = rest[-1]
     out_ref[...] = bf16(gate[level, half] * (f32(own[...]) + f32(other[...])))
 
 
@@ -455,12 +457,15 @@
     sums = in_vmem((two_cols, points), jnp.bfloat16)
     segment = in_vmem((two_cols, rows), jnp.float32)
 
-    def summed(halves, until):
+    def summed(halves, until, *ahead):
         totals = []
         for half, block in enumerate(halves):
             for step in range(1, until):
                 other = exchanged(step, block)
-                (block,) = run(functools.partial(add_kernel, step, half), [sums], gate, block, other)
+                kernel = functools.partial(add_kernel, step, half)
+                blocks = [gate, block, other] + (list(ahead) if half and step == 1 else [])
+                cost = EVEN if half else None
+                (block,) = call(kernel, [sums], [VMEM] * len(blocks), cost=cost)(*blocks)
             totals.append(block)
         return totals
 
@@ -543,7 +548,7 @@
     (low, high), energies = lax.optimization_barrier((halves, energies))
     neighbour_energies = exchanged(0, energies)
     halves = low, high
-    parts = summed(halves, n_steps - 1)
+    parts = summed(halves, n_steps - 1, neighbour_energies)
     low, high = [(other_core(block), exchanged(n_steps - 1, block, crossed=1)) for block in parts]
     (states,) = run(
         low_kernel,
@@ -564,8 +569,9 @@
         gate,
         weights,
     )
+    fields = summed(halves, n_steps)
+    fields[0], half_send = lax.optimization_barrier((fields[0], half_send))
     other_half = other_core(half_send)
-    fields = summed(halves, n_steps)
     low, high = swapped(fields)
     low, high = swapped(fields)
     my_part, other_new = run(

time: 35.6 us -> 35.6 us (level)
    pallas_call x12 -> x6, Pallas kernels: 2.72 us -> 2.58 us  [run(): return call(kernel, out_shape, [VMEM] * len(blocks))(*blocks)]
  transfers between devices with their start and end apart: 19 -> 19, of which waited for: 10 -> 10; matrix products, arithmetic and copies ran while one was open for 0% -> 0% of each run, Pallas kernels for 17% -> 14%
where the time goes in v32:
time: 35.6 us; the launch traced here: 35.4 us
  starting transfers between devices  18.3 us (51%)
  waiting for transfers between devices  9 us (25%)
  Pallas kernels  7.37 us (21%)
  between operations  0.76 us (2%)
    ppermute x10, starting transfers between devices, exchanged(): return lax.ppermute(block, DEVICES, pairs)  14.9 us
    ppermute x10, waiting for transfers between devices, exchanged(): return lax.ppermute(block, DEVICES, pairs)  6.94 us
    ppermute x9, starting transfers between devices, other_core(): return lax.ppermute(block, 'rep', [(0, 1), (1, 0)])  3.35 us
    pallas_call x6, Pallas kernels, run(): return call(kernel, out_shape, [VMEM] * len(blocks))(*blocks)  2.58 us
    ppermute x9, waiting for transfers between devices, other_core(): return lax.ppermute(block, 'rep', [(0, 1), (1, 0)])  2.07 us
    pallas_call x1, Pallas kernels, shards(): call(functools.partial(sent_kernel, neighbours), [in_vmem((2, 4 * rows +...  1.29 us
    pallas_call x1, Pallas kernels, shards(): call(functools.partial(side_kernel, gate_levels, neighbours), [pair, pair...  1.26 us
    pallas_call x1, Pallas kernels, shards(): call(load_kernel, [in_vmem((2, two_cols, rows), jnp.float32)], [HBM] * 2,...  1.12 us
  transfers between devices with their start and end apart: 19, of which 10 were waited for; matrix products, arithmetic and copies ran while one was open for 0% of the time, Pallas kernels for 14%

profile of v32, /device:TPU:0, one launch (start us, length us, event | category | flops | bytes accessed | tf_op | source)
XLA Modules:
  0.0 35.4 jit_solution(15201614513942294267)
XLA Ops:
  1.2 1.1 %shard_map.104.amp_ref = f32[2,128,256]{2,1,0:T(8,128)S(1)} custom-call(f32[256,128]{1,0:T(8,128)} %tgt_own_hbm.1, f32[1,256,128]{2,1,0:T(8,128)} %proj_own_hbm.1), custom_call_target="tpu_custom_call" | custom-call | flops 67108864 | bytes 4194304 | tf_op jit(solution)/shard_map/pallas_call | solution.py:479
  2.8 2.7 %collective-permute-start.3 = (bf16[2,128,256]{2,1,0:T(8,128)(2,1)S(1)}, bf16[2,128,256]{2,1,0:T(8,128)(2,1)S(1)}, u32[]{:S(2)}, u32[]{:S(2)}) collective-permute-start(bf16[2,128,256]{2,1,0:T(8,128)(2,1)S(1)} %get-tuple-element.36), channel_id=1, source_target_pairs={{0,3},{1,8},{3,0},{2,11},{5,6},{4,13},{6,5},{7,14},{9,10},{8,1},{1... | collective-permute-start | bytes 393224 | tf_op jit(solution)/shard_map/ppermute | solution.py:454
  5.5 1.3 %shard_map.107 = (bf16[2,1056,256]{2,1,0:T(8,128)(2,1)S(1)}, f32[1,1,256]{2,1,0:T(1,128)S(1)}, f32[2,1,256]{2,1,0:T(1,128)S(1)}) custom-call(f32[256]{0:T(256)} %weight_hbm.1, f32[256]{0:T(256)} %tgt_energy_hbm.1, f32[1,256]{1,0:T(1,128)} %proj_energy_hbm.1, bf16[2,4,256,256]{3,2,1,0:T(8,128)(2,1)} %bitcast.3, bf16[2,8,256,256]{3,2,1,0:T(8,128)(2,1)} %proj_hbm.3, ...), custom_call_target="tpu_custom_call" | custom-call | tf_op jit(solution)/shard_map/pallas_call | solution.py:502
  6.8 1.4 %collective-permute-start.2 = (bf16[2,1056,256]{2,1,0:T(8,128)(2,1)S(1)}, bf16[2,1056,256]{2,1,0:T(8,128)(2,1)S(1)}, u32[]{:S(2)}, u32[]{:S(2)}) collective-permute-start(bf16[2,1056,256]{2,1,0:T(8,128)(2,1)S(1)} %get-tuple-element.29.sent), channel_id=1, source_target_pairs={{0,1},{1,0},{2,3},{3,2},{4,5},{5,4},{6,7},{7,6},{8,9},{9,8},{10,11... | collective-permute-start | bytes 3244040 | tf_op jit(solution)/shard_map/ppermute | solution.py:436
  8.1 1.3 %shard_map.106 = (bf16[2,512,256]{2,1,0:T(8,128)(2,1)S(1)}, bf16[2,512,256]{2,1,0:T(8,128)(2,1)S(1)}, bf16[2,256,256]{2,1,0:T(8,128)(2,1)S(1)}, f32[3,2,1,256]{3,2,1,0:T(1,128)S(1)}) custom-call(s32[2,4]{1,0:T(2,128)} %bitcast.5, s32[2,4]{1,0:T(2,128)} %bitcast.6, bf16[2,4,256,256]{3,2,1,0:T(8,128)(2,1)} %bitcast.4, bf16[2,8,256,256]{3,2,1,0:T(8,128)(2,1)} %proj_hbm.3, ...), custom_call_target="tpu_custom_call" | custom-call | flops 34359738368 | bytes 65536 | tf_op jit(solution)/shard_map/pallas_call | solution.py:516
  9.4 1.1 %collective-permute-done.2.theirs = bf16[2,1056,256]{2,1,0:T(8,128)(2,1)S(1)} collective-permute-done((bf16[2,1056,256]{2,1,0:T(8,128)(2,1)S(1)}, bf16[2,1056,256]{2,1,0:T(8,128)(2,1)S(1)}, u32[]{:S(2)}, u32[]{:S(2)}) %collective-permute-start.2) | collective-permute-done | bytes 1081376 | tf_op jit(solution)/shard_map/ppermute | solution.py:436
  11.1 1.5 %collective-permute-start.4 = (bf16[128,256]{1,0:T(8,128)(2,1)S(1)}, bf16[128,256]{1,0:T(8,128)(2,1)S(1)}, u32[]{:S(2)}, u32[]{:S(2)}) collective-permute-start(bf16[128,256]{1,0:T(8,128)(2,1)S(1)} %get-tuple-element.40.own), channel_id=1, source_target_pairs={{0,9},{1,4},{3,10},{2,7},{5,12},{4,1},{6,15},{7,2},{9,0},{8,13},{1... | collective-permute-start | bytes 196616 | tf_op jit(solution)/shard_map/ppermute | solution.py:454
  12.7 1.2 %collective-permute-start.8 = (bf16[128,256]{1,0:T(8,128)(2,1)S(1)}, bf16[128,256]{1,0:T(8,128)(2,1)S(1)}, u32[]{:S(2)}, u32[]{:S(2)}) collective-permute-start(bf16[128,256]{1,0:T(8,128)(2,1)S(1)} %get-tuple-element.42.own), channel_id=1, source_target_pairs={{0,9},{1,4},{3,10},{2,7},{5,12},{4,1},{6,15},{7,2},{9,0},{8,13},{1... | collective-permute-start | bytes 196616 | tf_op jit(solution)/shard_map/ppermute | solution.py:454
  13.9 1.4 %collective-permute-start.7 = (f32[2,1,256]{2,1,0:T(1,128)S(1)}, f32[2,1,256]{2,1,0:T(1,128)S(1)}, u32[]{:S(2)}, u32[]{:S(2)}) collective-permute-start(f32[2,1,256]{2,1,0:T(1,128)S(1)} %get-tuple-element.41.energies), channel_id=1, source_target_pairs={{0,3},{1,8},{3,0},{2,11},{5,6},{4,13},{6,5},{7,14},{9,10},{8,1},{1... | collective-permute-start | bytes 6152 | tf_op jit(solution)/shard_map/ppermute | solution.py:454
  15.3 0.6 %collective-permute-done.4.other = bf16[128,256]{1,0:T(8,128)(2,1)S(1)} collective-permute-done((bf16[128,256]{1,0:T(8,128)(2,1)S(1)}, bf16[128,256]{1,0:T(8,128)(2,1)S(1)}, u32[]{:S(2)}, u32[]{:S(2)}) %collective-permute-start.4) | collective-permute-done | bytes 65568 | tf_op jit(solution)/shard_map/ppermute | solution.py:454
  15.9 1.2 %collective-permute-start.6 = (bf16[128,256]{1,0:T(8,128)(2,1)S(1)}, bf16[128,256]{1,0:T(8,128)(2,1)S(1)}, u32[]{:S(2)}, u32[]{:S(2)}) collective-permute-start(bf16[128,256]{1,0:T(8,128)(2,1)S(1)} %shard_map.110), channel_id=1, source_target_pairs={{0,4},{1,3},{3,7},{2,0},{5,1},{4,6},{6,2},{7,5},{9,13},{8,10},{10,... | collective-permute-start | bytes 196616 | tf_op jit(solution)/shard_map/ppermute | solution.py:454
  17.2 0.6 %collective-permute-start.5 = (bf16[128,256]{1,0:T(8,128)(2,1)S(1)}, bf16[128,256]{1,0:T(8,128)(2,1)S(1)}, u32[]{:S(2)}, u32[]{:S(2)}) collective-permute-start(bf16[128,256]{1,0:T(8,128)(2,1)S(1)} %shard_map.110), channel_id=1, source_target_pairs={{0,1},{1,0},{2,3},{3,2},{4,5},{5,4},{6,7},{7,6},{8,9},{9,8},{10,11... | collective-permute-start | bytes 196616 | tf_op jit(solution)/shard_map/ppermute | solution.py:436
  18.0 1.5 %collective-permute-start.10 = (bf16[128,256]{1,0:T(8,128)(2,1)S(1)}, bf16[128,256]{1,0:T(8,128)(2,1)S(1)}, u32[]{:S(2)}, u32[]{:S(2)}) collective-permute-start(bf16[128,256]{1,0:T(8,128)(2,1)S(1)} %shard_map.112), channel_id=1, source_target_pairs={{0,4},{1,3},{3,7},{2,0},{5,1},{4,6},{6,2},{7,5},{9,13},{8,10},{10,... | collective-permute-start | bytes 196616 | tf_op jit(solution)/shard_map/ppermute | solution.py:454
  19.5 0.7 %collective-permute-done.6.low_there = bf16[128,256]{1,0:T(8,128)(2,1)S(1)} collective-permute-done((bf16[128,256]{1,0:T(8,128)(2,1)S(1)}, bf16[128,256]{1,0:T(8,128)(2,1)S(1)}, u32[]{:S(2)}, u32[]{:S(2)}) %collective-permute-start.6) | collective-permute-done | bytes 65568 | tf_op jit(solution)/shard_map/ppermute | solution.py:454
  20.8 1.6 %collective-permute-done.10.high_there = bf16[128,256]{1,0:T(8,128)(2,1)S(1)} collective-permute-done((bf16[128,256]{1,0:T(8,128)(2,1)S(1)}, bf16[128,256]{1,0:T(8,128)(2,1)S(1)}, u32[]{:S(2)}, u32[]{:S(2)}) %collective-permute-start.10) | collective-permute-done | bytes 65568 | tf_op jit(solution)/shard_map/ppermute | solution.py:454
  22.3 0.8 %shard_map.113 = (bf16[128,256]{1,0:T(8,128)(2,1)S(1)}, bf16[128,256]{1,0:T(8,128)(2,1)S(1)}, f32[128,256]{1,0:T(8,128)S(1)}, f32[128,256]{1,0:T(8,128)S(1)}) custom-call(bf16[2,512,256]{2,1,0:T(8,128)(2,1)S(1)} %get-tuple-element.28.mine_chip, bf16[2,512,256]{2,1,0:T(8,128)(2,1)S(1)} %get-tuple-element.31.mine_far, ...), custom_call_target="tpu_custom_call" | custom-call | tf_op jit(solution)/shard_map/pallas_call | solution.py:433
  23.4 2.5 %collective-permute-start.11 = (bf16[128,256]{1,0:T(8,128)(2,1)S(1)}, bf16[128,256]{1,0:T(8,128)(2,1)S(1)}, u32[]{:S(2)}, u32[]{:S(2)}) collective-permute-start(bf16[128,256]{1,0:T(8,128)(2,1)S(1)} %get-tuple-element.43.own), channel_id=1, source_target_pairs={{0,9},{1,4},{3,10},{2,7},{5,12},{4,1},{6,15},{7,2},{9,0},{8,13},{1... | collective-permute-start | bytes 196616 | tf_op jit(solution)/shard_map/ppermute | solution.py:454
  25.9 1.9 %collective-permute-done.15.other = bf16[128,256]{1,0:T(8,128)(2,1)S(1)} collective-permute-done((bf16[128,256]{1,0:T(8,128)(2,1)S(1)}, bf16[128,256]{1,0:T(8,128)(2,1)S(1)}, u32[]{:S(2)}, u32[]{:S(2)}) %collective-permute-start.15) | collective-permute-done | bytes 65568 | tf_op jit(solution)/shard_map/ppermute | solution.py:454
  27.9 1.4 %collective-permute-start.16 = (bf16[128,256]{1,0:T(8,128)(2,1)S(1)}, bf16[128,256]{1,0:T(8,128)(2,1)S(1)}, u32[]{:S(2)}, u32[]{:S(2)}) collective-permute-start(bf16[128,256]{1,0:T(8,128)(2,1)S(1)} %shard_map.116.own), channel_id=1, source_target_pairs={{0,5},{1,2},{3,6},{2,1},{5,0},{4,7},{6,3},{7,4},{9,12},{8,11},{10,... | collective-permute-start | bytes 196616 | tf_op jit(solution)/shard_map/ppermute | solution.py:454
  29.3 1.2 %collective-permute-start.12 = (bf16[128,256]{1,0:T(8,128)(2,1)S(1)}, bf16[128,256]{1,0:T(8,128)(2,1)S(1)}, u32[]{:S(2)}, u32[]{:S(2)}) collective-permute-start(bf16[128,256]{1,0:T(8,128)(2,1)S(1)} %shard_map.114.own), channel_id=1, source_target_pairs={{0,5},{1,2},{3,6},{2,1},{5,0},{4,7},{6,3},{7,4},{9,12},{8,11},{10,... | collective-permute-start | bytes 196616 | tf_op jit(solution)/shard_map/ppermute | solution.py:454
  30.6 1.1 %collective-permute-done.16.other = bf16[128,256]{1,0:T(8,128)(2,1)S(1)} collective-permute-done((bf16[128,256]{1,0:T(8,128)(2,1)S(1)}, bf16[128,256]{1,0:T(8,128)(2,1)S(1)}, u32[]{:S(2)}, u32[]{:S(2)}) %collective-permute-start.16) | collective-permute-done | bytes 65568 | tf_op jit(solution)/shard_map/ppermute | solution.py:454
  32.2 0.8 %collective-permute-done.12.other = bf16[128,256]{1,0:T(8,128)(2,1)S(1)} collective-permute-done((bf16[128,256]{1,0:T(8,128)(2,1)S(1)}, bf16[128,256]{1,0:T(8,128)(2,1)S(1)}, u32[]{:S(2)}, u32[]{:S(2)}) %collective-permute-start.12) | collective-permute-done | bytes 65568 | tf_op jit(solution)/shard_map/ppermute | solution.py:454
  33.8 0.6 %collective-permute-done.13.high = bf16[128,256]{1,0:T(8,128)(2,1)S(1)} collective-permute-done((bf16[128,256]{1,0:T(8,128)(2,1)S(1)}, bf16[128,256]{1,0:T(8,128)(2,1)S(1)}, u32[]{:S(2)}, u32[]{:S(2)}) %collective-permute-start.13) | collective-permute-done | bytes 65568 | tf_op jit(solution)/shard_map/ppermute | solution.py:436
  34.4 1.0 %shard_map.119 = (f32[256,128]{1,0:T(8,128)}, f32[1,256,128]{2,1,0:T(8,128)}) custom-call(bf16[2,512,256]{2,1,0:T(8,128)(2,1)S(1)} %get-tuple-element.28.mine_chip, bf16[2,1056,256]{2,1,0:T(8,128)(2,1)S(1)} %collective-permute-done.2.theirs, bf16[128,256]{1,0:T(8,128)(2,1)S(1)} %collective-permute-done.13.high, f32[128,256]{1,0:T(8,128)S(1)} %get-tuple-element.50.my_part, ...), custom_call_target="tpu_custom_call" | custom-call | tf_op jit(solution)/shard_map/pallas_call | solution.py:591
  (30 shorter events, 4.0 us)
Async XLA Ops:
  0.6 1.7 %collective-permute-start = (f32[256,128]{1,0:T(8,128)}, f32[256,128]{1,0:T(8,128)S(1)}, u32[]{:S(2)}, u32[]{:S(2)}) collective-permute-start(f32[256,128]{1,0:T(8,128)} %tgt_own_hbm.1), channel_id=1, source_target_pairs={{0,1},{1,0},{2,3},{3,2},{4,5},{5,4},{6,7},{7,6},{8,9},{9,8},{10,11... | collective-permute-start | bytes 393224 | tf_op jit(solution)/shard_map/ppermute | solution.py:436
  1.1 1.6 %collective-permute-start.1 = (f32[1,256,128]{2,1,0:T(8,128)}, f32[1,256,128]{2,1,0:T(8,128)S(1)}, u32[]{:S(2)}, u32[]{:S(2)}) collective-permute-start(f32[1,256,128]{2,1,0:T(8,128)} %proj_own_hbm.1), channel_id=1, source_target_pairs={{0,1},{1,0},{2,3},{3,2},{4,5},{5,4},{6,7},{7,6},{8,9},{9,8},{10,11... | collective-permute-start | bytes 393224 | tf_op jit(solution)/shard_map/ppermute | solution.py:436
  2.8 8.0 %collective-permute-start.3 = (bf16[2,128,256]{2,1,0:T(8,128)(2,1)S(1)}, bf16[2,128,256]{2,1,0:T(8,128)(2,1)S(1)}, u32[]{:S(2)}, u32[]{:S(2)}) collective-permute-start(bf16[2,128,256]{2,1,0:T(8,128)(2,1)S(1)} %get-tuple-element.36), channel_id=1, source_target_pairs={{0,3},{1,8},{3,0},{2,11},{5,6},{4,13},{6,5},{7,14},{9,10},{8,1},{1... | collective-permute-start | bytes 393224 | tf_op jit(solution)/shard_map/ppermute | solution.py:454
  6.8 3.7 %collective-permute-start.2 = (bf16[2,1056,256]{2,1,0:T(8,128)(2,1)S(1)}, bf16[2,1056,256]{2,1,0:T(8,128)(2,1)S(1)}, u32[]{:S(2)}, u32[]{:S(2)}) collective-permute-start(bf16[2,1056,256]{2,1,0:T(8,128)(2,1)S(1)} %get-tuple-element.29.sent), channel_id=1, source_target_pairs={{0,1},{1,0},{2,3},{3,2},{4,5},{5,4},{6,7},{7,6},{8,9},{9,8},{10,11... | collective-permute-start | bytes 3244040 | tf_op jit(solution)/shard_map/ppermute | solution.py:436
  11.1 4.8 %collective-permute-start.4 = (bf16[128,256]{1,0:T(8,128)(2,1)S(1)}, bf16[128,256]{1,0:T(8,128)(2,1)S(1)}, u32[]{:S(2)}, u32[]{:S(2)}) collective-permute-start(bf16[128,256]{1,0:T(8,128)(2,1)S(1)} %get-tuple-element.40.own), channel_id=1, source_target_pairs={{0,9},{1,4},{3,10},{2,7},{5,12},{4,1},{6,15},{7,2},{9,0},{8,13},{1... | collective-permute-start | bytes 196616 | tf_op jit(solution)/shard_map/ppermute | solution.py:454
  12.7 5.3 %collective-permute-start.8 = (bf16[128,256]{1,0:T(8,128)(2,1)S(1)}, bf16[128,256]{1,0:T(8,128)(2,1)S(1)}, u32[]{:S(2)}, u32[]{:S(2)}) collective-permute-start(bf16[128,256]{1,0:T(8,128)(2,1)S(1)} %get-tuple-element.42.own), channel_id=1, source_target_pairs={{0,9},{1,4},{3,10},{2,7},{5,12},{4,1},{6,15},{7,2},{9,0},{8,13},{1... | collective-permute-start | bytes 196616 | tf_op jit(solution)/shard_map/ppermute | solution.py:454
  13.9 4.0 %collective-permute-start.7 = (f32[2,1,256]{2,1,0:T(1,128)S(1)}, f32[2,1,256]{2,1,0:T(1,128)S(1)}, u32[]{:S(2)}, u32[]{:S(2)}) collective-permute-start(f32[2,1,256]{2,1,0:T(1,128)S(1)} %get-tuple-element.41.energies), channel_id=1, source_target_pairs={{0,3},{1,8},{3,0},{2,11},{5,6},{4,13},{6,5},{7,14},{9,10},{8,1},{1... | collective-permute-start | bytes 6152 | tf_op jit(solution)/shard_map/ppermute | solution.py:454
  15.9 4.3 %collective-permute-start.6 = (bf16[128,256]{1,0:T(8,128)(2,1)S(1)}, bf16[128,256]{1,0:T(8,128)(2,1)S(1)}, u32[]{:S(2)}, u32[]{:S(2)}) collective-permute-start(bf16[128,256]{1,0:T(8,128)(2,1)S(1)} %shard_map.110), channel_id=1, source_target_pairs={{0,4},{1,3},{3,7},{2,0},{5,1},{4,6},{6,2},{7,5},{9,13},{8,10},{10,... | collective-permute-start | bytes 196616 | tf_op jit(solution)/shard_map/ppermute | solution.py:454
  17.2 3.1 %collective-permute-start.5 = (bf16[128,256]{1,0:T(8,128)(2,1)S(1)}, bf16[128,256]{1,0:T(8,128)(2,1)S(1)}, u32[]{:S(2)}, u32[]{:S(2)}) collective-permute-start(bf16[128,256]{1,0:T(8,128)(2,1)S(1)} %shard_map.110), channel_id=1, source_target_pairs={{0,1},{1,0},{2,3},{3,2},{4,5},{5,4},{6,7},{7,6},{8,9},{9,8},{10,11... | collective-permute-start | bytes 196616 | tf_op jit(solution)/shard_map/ppermute | solution.py:436
  18.0 4.3 %collective-permute-start.10 = (bf16[128,256]{1,0:T(8,128)(2,1)S(1)}, bf16[128,256]{1,0:T(8,128)(2,1)S(1)}, u32[]{:S(2)}, u32[]{:S(2)}) collective-permute-start(bf16[128,256]{1,0:T(8,128)(2,1)S(1)} %shard_map.112), channel_id=1, source_target_pairs={{0,4},{1,3},{3,7},{2,0},{5,1},{4,6},{6,2},{7,5},{9,13},{8,10},{10,... | collective-permute-start | bytes 196616 | tf_op jit(solution)/shard_map/ppermute | solution.py:454
  19.5 2.8 %collective-permute-start.9 = (bf16[128,256]{1,0:T(8,128)(2,1)S(1)}, bf16[128,256]{1,0:T(8,128)(2,1)S(1)}, u32[]{:S(2)}, u32[]{:S(2)}) collective-permute-start(bf16[128,256]{1,0:T(8,128)(2,1)S(1)} %shard_map.112), channel_id=1, source_target_pairs={{0,1},{1,0},{2,3},{3,2},{4,5},{5,4},{6,7},{7,6},{8,9},{9,8},{10,11... | collective-permute-start | bytes 196616 | tf_op jit(solution)/shard_map/ppermute | solution.py:436
  23.2 4.7 %collective-permute-start.15 = (bf16[128,256]{1,0:T(8,128)(2,1)S(1)}, bf16[128,256]{1,0:T(8,128)(2,1)S(1)}, u32[]{:S(2)}, u32[]{:S(2)}) collective-permute-start(bf16[128,256]{1,0:T(8,128)(2,1)S(1)} %get-tuple-element.45.own), channel_id=1, source_target_pairs={{0,9},{1,4},{3,10},{2,7},{5,12},{4,1},{6,15},{7,2},{9,0},{8,13},{1... | collective-permute-start | bytes 196616 | tf_op jit(solution)/shard_map/ppermute | solution.py:454
  23.4 5.9 %collective-permute-start.11 = (bf16[128,256]{1,0:T(8,128)(2,1)S(1)}, bf16[128,256]{1,0:T(8,128)(2,1)S(1)}, u32[]{:S(2)}, u32[]{:S(2)}) collective-permute-start(bf16[128,256]{1,0:T(8,128)(2,1)S(1)} %get-tuple-element.43.own), channel_id=1, source_target_pairs={{0,9},{1,4},{3,10},{2,7},{5,12},{4,1},{6,15},{7,2},{9,0},{8,13},{1... | collective-permute-start | bytes 196616 | tf_op jit(solution)/shard_map/ppermute | solution.py:454
  27.9 3.8 %collective-permute-start.16 = (bf16[128,256]{1,0:T(8,128)(2,1)S(1)}, bf16[128,256]{1,0:T(8,128)(2,1)S(1)}, u32[]{:S(2)}, u32[]{:S(2)}) collective-permute-start(bf16[128,256]{1,0:T(8,128)(2,1)S(1)} %shard_map.116.own), channel_id=1, source_target_pairs={{0,5},{1,2},{3,6},{2,1},{5,0},{4,7},{6,3},{7,4},{9,12},{8,11},{10,... | collective-permute-start | bytes 196616 | tf_op jit(solution)/shard_map/ppermute | solution.py:454
  29.3 3.8 %collective-permute-start.12 = (bf16[128,256]{1,0:T(8,128)(2,1)S(1)}, bf16[128,256]{1,0:T(8,128)(2,1)S(1)}, u32[]{:S(2)}, u32[]{:S(2)}) collective-permute-start(bf16[128,256]{1,0:T(8,128)(2,1)S(1)} %shard_map.114.own), channel_id=1, source_target_pairs={{0,5},{1,2},{3,6},{2,1},{5,0},{4,7},{6,3},{7,4},{9,12},{8,11},{10,... | collective-permute-start | bytes 196616 | tf_op jit(solution)/shard_map/ppermute | solution.py:454
  30.6 2.7 %collective-permute-start.14 = (bf16[2,256,256]{2,1,0:T(8,128)(2,1)S(1)}, bf16[2,256,256]{2,1,0:T(8,128)(2,1)S(1)}, u32[]{:S(2)}, u32[]{:S(2)}) collective-permute-start(bf16[2,256,256]{2,1,0:T(8,128)(2,1)S(1)} %get-tuple-element.44), channel_id=1, source_target_pairs={{0,1},{1,0},{2,3},{3,2},{4,5},{5,4},{6,7},{7,6},{8,9},{9,8},{10,11... | collective-permute-start | bytes 786440 | tf_op jit(solution)/shard_map/ppermute | solution.py:436
  31.6 1.6 %collective-permute-start.17 = (bf16[128,256]{1,0:T(8,128)(2,1)S(1)}, bf16[128,256]{1,0:T(8,128)(2,1)S(1)}, u32[]{:S(2)}, u32[]{:S(2)}) collective-permute-start(bf16[128,256]{1,0:T(8,128)(2,1)S(1)} %shard_map.117.low), channel_id=1, source_target_pairs={{0,1},{1,0},{2,3},{3,2},{4,5},{5,4},{6,7},{7,6},{8,9},{9,8},{10,11... | collective-permute-start | bytes 196616 | tf_op jit(solution)/shard_map/ppermute | solution.py:436
  31.7 1.6 %collective-permute-start.18 = (f32[128,256]{1,0:T(8,128)S(1)}, f32[128,256]{1,0:T(8,128)S(1)}, u32[]{:S(2)}, u32[]{:S(2)}) collective-permute-start(f32[128,256]{1,0:T(8,128)S(1)} %get-tuple-element.49), channel_id=1, source_target_pairs={{0,1},{1,0},{2,3},{3,2},{4,5},{5,4},{6,7},{7,6},{8,9},{9,8},{10,11... | collective-permute-start | bytes 393224 | tf_op jit(solution)/shard_map/ppermute | solution.py:436
  33.1 1.3 %collective-permute-start.13 = (bf16[128,256]{1,0:T(8,128)(2,1)S(1)}, bf16[128,256]{1,0:T(8,128)(2,1)S(1)}, u32[]{:S(2)}, u32[]{:S(2)}) collective-permute-start(bf16[128,256]{1,0:T(8,128)(2,1)S(1)} %shard_map.115.high), channel_id=1, source_target_pairs={{0,1},{1,0},{2,3},{3,2},{4,5},{5,4},{6,7},{7,6},{8,9},{9,8},{10,11... | collective-permute-start | bytes 196616 | tf_op jit(solution)/shard_map/ppermute | solution.py:436
